TPU v7x, 32 devices: a whole 2x2x4 slice. The times are simulated.
32 devices in a mesh: stream: 2 (over x), dp: 16 (over z, y, core).
Axes of the slice: x: 2, y: 2, z: 4, core: 2. Of those that a mesh axis runs over, the one named last changes fastest.
Arguments:
- tokens: bfloat16 [2, 4096, 512], P('stream', 'dp'), may hold values from -6 to 6
- qkv_weight: bfloat16 [2, 512, 1536], P('stream'), may hold values from -0.25 to 0.25
- qkv_bias: bfloat16 [2, 1536], P('stream'), may hold values from -1.5 to 1.5
- out_weight: bfloat16 [2, 512, 512], P('stream'), may hold values from -1.5 to 1.5
- out_bias: bfloat16 [2, 512], P('stream'), may hold values from -1.5 to 1.5
- first_gain: bfloat16 [2, 512], P('stream'), may hold values from 0.25 to 1.75
- first_shift: bfloat16 [2, 512], P('stream'), may hold values from -1.5 to 1.5
- up_weight: bfloat16 [2, 512, 2048], P('stream'), may hold values from -0.25 to 0.25
- up_bias: bfloat16 [2, 2048], P('stream'), may hold values from -1.5 to 1.5
- down_weight: bfloat16 [2, 2048, 512], P('stream'), may hold values from -0.25 to 0.25
- down_bias: bfloat16 [2, 512], P('stream'), may hold values from -1.5 to 1.5
- second_gain: bfloat16 [2, 512], P('stream'), may hold values from 0.25 to 1.75
- second_shift: bfloat16 [2, 512], P('stream'), may hold values from -1.5 to 1.5
- proj_weight: bfloat16 [2, 512, 128], P('stream'), may hold values from -0.25 to 0.25
- log_scale: float32 [], replicated, may hold values from 2.5 to 3.5
- doc_lengths: int32 [16, 5], replicated, may hold values from 1 to 128, 256 in all within a row
- labels: int32 [128], P('dp'), may hold values from 0 to 63
Outputs:
- loss: float32 [], replicated
- tokens_grad: float32 [2, 4096, 512], P('stream', 'dp')
- qkv_weight_grad: float32 [2, 512, 1536], P('stream')
- qkv_bias_grad: float32 [2, 1536], P('stream')
- out_weight_grad: float32 [2, 512, 512], P('stream')
- out_bias_grad: float32 [2, 512], P('stream')
- first_gain_grad: float32 [2, 512], P('stream')
- first_shift_grad: float32 [2, 512], P('stream')
- up_weight_grad: float32 [2, 512, 2048], P('stream')
- up_bias_grad: float32 [2, 2048], P('stream')
- down_weight_grad: float32 [2, 2048, 512], P('stream')
- down_bias_grad: float32 [2, 512], P('stream')
- second_gain_grad: float32 [2, 512], P('stream')
- second_shift_grad: float32 [2, 512], P('stream')
- proj_weight_grad: float32 [2, 512, 128], P('stream')
- log_scale_grad: float32 [], replicated
Inputs may be any that keep to these rules, and one draw needn't show every extreme that they name: Each row of doc_lengths sums to 256; its last entry is the padding; its largest entry is 128.
All inputs are finite; a program needn't handle non-finite values.
Results may differ from a plain program's by a relative error of at most 0.023.
Values may be sent and summed in bfloat16 or wider, within the bound.
No kernel may reach another device: no remote copies, remote signals or barrier semaphores. Data moves between devices by JAX's collectives and lax.ppermute only.
A program may use at most 128 MiB of HBM per device.

v0:
```python
from functools import partial
import math

import jax
import jax.numpy as jnp
from jax import lax
from jax.sharding import PartitionSpec as P

D = 512
HEADS = 8
HD = 64
PROJ = 128
QLEN = 32
DOCS_ROW = 4


sharpness = 8.0
eps_norm = 1e-06
eps_layer = 1e-05


def swapped(value, axis, stride):
    mask = 2**stride
    pairs = [(source, source ^ mask) for source in range(lax.axis_size(axis))]
    return lax.ppermute(value, axis, pairs)


def layer_norm(values, gain_vec, shift_vec):
    centred = values - jnp.mean(values, axis=-1, keepdims=True)
    spread = jnp.mean(centred * centred, axis=-1, keepdims=True)
    return centred * lax.rsqrt(spread + eps_layer) * gain_vec + shift_vec


def angles(position):
    half_len = HD // 2
    freqs = 10000.0 ** (-jnp.arange(half_len, dtype=jnp.float32) / half_len)
    turned = position.astype(jnp.float32)[..., None] * freqs
    return (jnp.cos(turned)[..., None, :], jnp.sin(turned)[..., None, :])


def rotate(values, cosine, sine):
    half_len = HD // 2
    first_half = values[..., :half_len]
    second_half = values[..., half_len:]
    return jnp.concatenate(
        [first_half * cosine - second_half * sine, second_half * cosine + first_half * sine],
        axis=-1,
    )


def rotate_back(values, cosine, sine):
    half_len = HD // 2
    first_half = values[..., :half_len]
    second_half = values[..., half_len:]
    return jnp.concatenate(
        [first_half * cosine + second_half * sine, second_half * cosine - first_half * sine],
        axis=-1,
    )


def inverse_norms(values):
    cut_a = PROJ // 2
    cut_b = 3 * PROJ // 4
    squared = values * values
    part_a = jnp.sum(squared[:, :cut_a], axis=1)
    part_b = part_a + jnp.sum(squared[:, cut_a:cut_b], axis=1)
    part_c = part_b + jnp.sum(squared[:, cut_b:], axis=1)
    return lax.rsqrt(jnp.stack([part_a, part_b, part_c]) + eps_norm)


def norms_back(values, inverse, d_inverse):
    cut_a = PROJ // 2
    cut_b = 3 * PROJ // 4
    coeff = -d_inverse * inverse * inverse * inverse
    weight_c = coeff[2]
    weight_b = coeff[1] + weight_c
    weight_a = coeff[0] + weight_b
    return jnp.concatenate(
        [
            values[:, :cut_a] * weight_a[:, None],
            values[:, cut_a:cut_b] * weight_b[:, None],
            values[:, cut_b:] * weight_c[:, None],
        ],
        axis=1,
    )


def row_layout(doc_lengths, row_len):
    ends = jnp.cumsum(doc_lengths, axis=1)
    spots = jnp.arange(row_len, dtype=jnp.int32)
    finished = (spots[None, :, None] >= ends[:, None, :DOCS_ROW]).astype(jnp.int32)
    doc_table = jnp.sum(finished, axis=2)
    offsets = jnp.sum(finished * doc_lengths[:, None, :DOCS_ROW], axis=2)
    return (doc_table, spots[None, :] - offsets)


def inner_rows(left_op, right_op):
    return lax.dot_general(
        left_op, right_op, (((1,), (1,)), ((), ())), preferred_element_type=jnp.float32
    )


def outer_rows(left_op, right_op):
    return lax.dot_general(
        left_op, right_op, (((0,), (0,)), ((), ())), preferred_element_type=jnp.float32
    )


def similarities(queries, query_inv, documents):
    cut_a = PROJ // 2
    cut_b = 3 * PROJ // 4
    doc_inv = inverse_norms(documents.astype(jnp.float32))
    part_a = inner_rows(queries[:, :cut_a], documents[:, :cut_a])
    part_b = inner_rows(queries[:, cut_a:cut_b], documents[:, cut_a:cut_b])
    part_c = inner_rows(queries[:, cut_b:], documents[:, cut_b:])
    sums = jnp.stack([part_a, part_a + part_b, part_a + part_b + part_c])
    scaled = sums * query_inv[:, :, None] * doc_inv[:, None, :]
    return (sums, scaled, doc_inv)


def piece_onehot(doc_flat, start, count, row_len):
    table = lax.dynamic_slice_in_dim(doc_flat, start, count).reshape(count // row_len, row_len)
    return (table[..., None] == jnp.arange(DOCS_ROW, dtype=jnp.int32)).astype(jnp.float32)


def sweep(step_fn, carry, pieces, start, row_len):
    shards = pieces.shape[0] // row_len
    block = row_len * math.gcd(shards, 8)

    def turn(index, state):
        offset = index * block
        return step_fn(state, lax.dynamic_slice_in_dim(pieces, offset, block, 0), start + offset)

    return lax.fori_loop(0, pieces.shape[0] // block, turn, carry)


def per_device(
    tokens,
    qkv_weight,
    qkv_bias,
    out_weight,
    out_bias,
    first_gain,
    first_shift,
    up_weight,
    up_bias,
    down_weight,
    down_bias,
    second_gain,
    second_shift,
    proj_weight,
    log_scale,
    doc_lengths,
    labels,
):
    inputs = tokens[0]
    row_len = inputs.shape[0]
    half_len = row_len // 2
    num_rows = doc_lengths.shape[0]
    documents = num_rows * DOCS_ROW
    query_count = half_len // QLEN
    queries_all = row_len // QLEN * num_rows
    cut_a = PROJ // 2
    cut_b = 3 * PROJ // 4
    stream_idx = lax.axis_index("stream")
    is_query = stream_idx == 0
    dp_index = lax.axis_index("dp")
    doc_table, doc_position = row_layout(doc_lengths, row_len)
    doc_flat = doc_table.reshape(-1)
    log_length = jnp.log(doc_lengths[:, :DOCS_ROW].astype(jnp.float32)).reshape(-1)
    spots = jnp.arange(row_len, dtype=jnp.int32)
    segment = jnp.where(
        is_query, spots // QLEN, lax.dynamic_index_in_dim(doc_table, dp_index, 0, False)
    )
    position = jnp.where(
        is_query, spots % QLEN, lax.dynamic_index_in_dim(doc_position, dp_index, 0, False)
    )
    weight_qkv = qkv_weight[0]
    weight_out = out_weight[0]
    weight_up = up_weight[0]
    weight_down = down_weight[0]
    weight_proj = proj_weight[0]
    bias_qkv = qkv_bias[0].astype(jnp.float32)
    bias_out = out_bias[0].astype(jnp.float32)
    bias_up = up_bias[0].astype(jnp.float32)
    bias_down = down_bias[0].astype(jnp.float32)
    gain_one = first_gain[0].astype(jnp.float32)
    shift_one = first_shift[0].astype(jnp.float32)
    gain_two = second_gain[0].astype(jnp.float32)
    shift_two = second_shift[0].astype(jnp.float32)
    att_scale = 1.0 / math.sqrt(HD)
    inputs_f = inputs.astype(jnp.float32)
    joined = jnp.dot(inputs, weight_qkv, preferred_element_type=jnp.float32) + bias_qkv
    cosine, sine = angles(position)
    query_rot = rotate(joined[:, :D].reshape(row_len, HEADS, HD), cosine, sine).astype(jnp.bfloat16)
    key_rot = rotate(joined[:, D : 2 * D].reshape(row_len, HEADS, HD), cosine, sine).astype(
        jnp.bfloat16
    )
    value_low = joined[:, 2 * D :].reshape(row_len, HEADS, HD).astype(jnp.bfloat16)
    same_seg = segment[:, None] == segment[None, :]
    raw_scores = (
        jnp.einsum("qhd,khd->hqk", query_rot, key_rot, preferred_element_type=jnp.float32)
        * att_scale
    )
    masked = jnp.where(same_seg[None], raw_scores, -1e30)
    row_top = jnp.max(masked, axis=2, keepdims=True)
    exp_scores = jnp.exp(masked - row_top)
    probs_f = exp_scores / jnp.sum(exp_scores, axis=2, keepdims=True)
    probs_low = probs_f.astype(jnp.bfloat16)
    mixed_low = (
        jnp.einsum("hqk,khd->qhd", probs_low, value_low, preferred_element_type=jnp.float32)
        .reshape(row_len, D)
        .astype(jnp.bfloat16)
    )
    attended = jnp.dot(mixed_low, weight_out, preferred_element_type=jnp.float32) + bias_out
    first_out, first_back = jax.vjp(layer_norm, inputs_f + attended, gain_one, shift_one)
    first_low = first_out.astype(jnp.bfloat16)
    inner_pre = jnp.dot(first_low, weight_up, preferred_element_type=jnp.float32) + bias_up
    activ_out, gelu_back = jax.vjp(partial(jax.nn.gelu, approximate=False), inner_pre)
    activ_low = activ_out.astype(jnp.bfloat16)
    branch = jnp.dot(activ_low, weight_down, preferred_element_type=jnp.float32) + bias_down
    second, second_back = jax.vjp(layer_norm, first_out + branch, gain_two, shift_two)
    second_low = second.astype(jnp.bfloat16)
    own_vectors = jnp.dot(second_low, weight_proj, preferred_element_type=jnp.float32).astype(
        jnp.bfloat16
    )
    partner = swapped(own_vectors, "stream", 0)
    docs_here = jnp.where(is_query, partner, own_vectors)
    queries = jnp.where(is_query, own_vectors[:half_len], partner[half_len:])
    query_inv = inverse_norms(queries.astype(jnp.float32))

    def sum_block(totals, piece, start):
        count = piece.shape[0]
        blocks = count // row_len
        sums, scaled, doc_inv = similarities(queries, query_inv, piece)
        exp_sims = jnp.exp(sharpness * scaled).reshape(3, half_len, blocks, row_len)
        onehot = piece_onehot(doc_flat, start, count, row_len)
        part = jnp.einsum(
            "mqnr,nrd->mqnd", exp_sims, onehot, precision=lax.Precision.HIGHEST
        ).reshape(3, half_len, blocks * DOCS_ROW)
        first_doc = start // row_len * DOCS_ROW
        current = lax.dynamic_slice_in_dim(totals, first_doc, blocks * DOCS_ROW, 2)
        return lax.dynamic_update_slice_in_dim(totals, current + part, first_doc, 2)

    empty_totals = jnp.zeros((3, half_len, documents), jnp.float32)
    all_docs = lax.all_gather(docs_here, "dp", axis=0, tiled=True)
    totals = sweep(sum_block, empty_totals, all_docs, 0, row_len)
    scale_value = jnp.exp(log_scale)
    matched = (jnp.log(totals) - log_length[None, None, :]) / sharpness
    per_query = jnp.sum(matched.reshape(3, query_count, QLEN, documents), axis=2)
    logits = scale_value * per_query / QLEN
    log_totals = jax.nn.logsumexp(logits, axis=2)
    own_labels = jnp.where(is_query, labels[:query_count], labels[query_count:])
    label_hot = (
        jnp.arange(documents, dtype=jnp.int32)[None, None, :] == own_labels[None, :, None]
    ).astype(jnp.float32)
    picked = jnp.sum(logits * label_hot, axis=2)
    loss_part = jnp.sum(log_totals - picked) / queries_all
    d_logits = (jnp.exp(logits - log_totals[..., None]) - label_hot) / queries_all
    scale_part = jnp.sum(d_logits * logits)
    loss, log_scale_grad = lax.psum((loss_part, scale_part), ("stream", "dp"))
    token_terms = jnp.broadcast_to(
        (d_logits * scale_value / QLEN)[:, :, None, :], (3, query_count, QLEN, documents)
    ).reshape(3, half_len, documents)
    ratio = token_terms / totals

    def grad_block(carry, piece, start):
        dq_acc, dq_inv, dd_all = carry
        count = piece.shape[0]
        blocks = count // row_len
        sums, scaled, doc_inv = similarities(queries, query_inv, piece)
        exp_sims = jnp.exp(sharpness * scaled)
        onehot = piece_onehot(doc_flat, start, count, row_len)
        first_doc = start // row_len * DOCS_ROW
        coeff = lax.dynamic_slice_in_dim(ratio, first_doc, blocks * DOCS_ROW, 2).reshape(
            3, half_len, blocks, DOCS_ROW
        )
        spread = jnp.einsum(
            "mqnd,nrd->mqnr", coeff, onehot, precision=lax.Precision.HIGHEST
        ).reshape(3, half_len, count)
        d_scaled = exp_sims * spread
        d_sums = d_scaled * query_inv[:, :, None] * doc_inv[:, None, :]
        dq_inv = dq_inv + jnp.sum(d_scaled * sums * doc_inv[:, None, :], axis=2)
        d_doc_inv = jnp.sum(d_scaled * sums * query_inv[:, :, None], axis=1)
        grad_c = d_sums[2]
        grad_b = d_sums[1] + grad_c
        grad_a = d_sums[0] + grad_b
        grad_a = grad_a.astype(jnp.bfloat16)
        grad_b = grad_b.astype(jnp.bfloat16)
        grad_c = grad_c.astype(jnp.bfloat16)
        dq_acc = dq_acc + jnp.concatenate(
            [
                jnp.dot(grad_a, piece[:, :cut_a], preferred_element_type=jnp.float32),
                jnp.dot(grad_b, piece[:, cut_a:cut_b], preferred_element_type=jnp.float32),
                jnp.dot(grad_c, piece[:, cut_b:], preferred_element_type=jnp.float32),
            ],
            axis=1,
        )
        d_docs = jnp.concatenate(
            [
                outer_rows(grad_a, queries[:, :cut_a]),
                outer_rows(grad_b, queries[:, cut_a:cut_b]),
                outer_rows(grad_c, queries[:, cut_b:]),
            ],
            axis=1,
        )
        d_docs = d_docs + norms_back(piece.astype(jnp.float32), doc_inv, d_doc_inv)
        dd_all = lax.dynamic_update_slice_in_dim(dd_all, d_docs, start, 0)
        return (dq_acc, dq_inv, dd_all)

    empty_grads = (
        jnp.zeros((half_len, PROJ), jnp.float32),
        jnp.zeros((3, half_len), jnp.float32),
        jnp.zeros((num_rows * row_len, PROJ), jnp.float32),
    )
    dq_acc, dq_inv, dd_all = sweep(grad_block, empty_grads, all_docs, 0, row_len)
    dq_total = dq_acc + norms_back(queries.astype(jnp.float32), query_inv, dq_inv)
    doc_share = lax.psum_scatter(dd_all, "dp", scatter_dimension=0, tiled=True)
    other_docs, other_queries = (
        swapped(doc_share.astype(jnp.bfloat16), "stream", 0).astype(doc_share.dtype),
        swapped(dq_total.astype(jnp.bfloat16), "stream", 0).astype(dq_total.dtype),
    )
    d_vectors = jnp.where(
        is_query, jnp.concatenate([dq_total, other_queries], axis=0), doc_share + other_docs
    )
    d_proj_low = d_vectors.astype(jnp.bfloat16)
    grad_proj = outer_rows(second_low, d_proj_low)
    d_second = inner_rows(d_proj_low, weight_proj)
    d_sum2, grad_gain2, grad_shift2 = second_back(d_second)
    d_branch = d_sum2.astype(jnp.bfloat16)
    grad_down = outer_rows(activ_low, d_branch)
    grad_bdown = jnp.sum(d_branch.astype(jnp.float32), axis=0)
    d_activ = inner_rows(d_branch, weight_down)
    (d_inner_f,) = gelu_back(d_activ)
    d_inner = d_inner_f.astype(jnp.bfloat16)
    grad_up = outer_rows(first_low, d_inner)
    grad_bup = jnp.sum(d_inner.astype(jnp.float32), axis=0)
    d_first = d_sum2 + inner_rows(d_inner, weight_up)
    d_sum1, grad_gain1, grad_shift1 = first_back(d_first)
    d_att = d_sum1.astype(jnp.bfloat16)
    grad_out = outer_rows(mixed_low, d_att)
    grad_bout = jnp.sum(d_att.astype(jnp.float32), axis=0)
    d_mixed = inner_rows(d_att, weight_out).astype(jnp.bfloat16).reshape(row_len, HEADS, HD)
    d_probs = jnp.einsum("qhd,khd->hqk", d_mixed, value_low, preferred_element_type=jnp.float32)
    d_value = jnp.einsum("hqk,qhd->khd", probs_low, d_mixed, preferred_element_type=jnp.float32)
    d_scores = (probs_f * (d_probs - jnp.sum(d_probs * probs_f, axis=2, keepdims=True))).astype(
        jnp.bfloat16
    )
    d_query = (
        jnp.einsum("hqk,khd->qhd", d_scores, key_rot, preferred_element_type=jnp.float32)
        * att_scale
    )
    d_key = (
        jnp.einsum("hqk,qhd->khd", d_scores, query_rot, preferred_element_type=jnp.float32)
        * att_scale
    )
    d_joined = jnp.concatenate(
        [
            rotate_back(d_query, cosine, sine).reshape(row_len, D),
            rotate_back(d_key, cosine, sine).reshape(row_len, D),
            d_value.reshape(row_len, D),
        ],
        axis=1,
    ).astype(jnp.bfloat16)
    grad_qkv = outer_rows(inputs, d_joined)
    grad_bqkv = jnp.sum(d_joined.astype(jnp.float32), axis=0)
    tokens_grad = d_sum1 + inner_rows(d_joined, weight_qkv)
    summed = lax.psum(
        (
            grad_qkv,
            grad_bqkv,
            grad_out,
            grad_bout,
            grad_gain1,
            grad_shift1,
            grad_up,
            grad_bup,
            grad_down,
            grad_bdown,
            grad_gain2,
            grad_shift2,
            grad_proj,
        ),
        "dp",
    )
    return (
        loss,
        tokens_grad[None],
        summed[0][None],
        summed[1][None],
        summed[2][None],
        summed[3][None],
        summed[4][None],
        summed[5][None],
        summed[6][None],
        summed[7][None],
        summed[8][None],
        summed[9][None],
        summed[10][None],
        summed[11][None],
        summed[12][None],
        log_scale_grad,
    )


def solution(mesh):
    return jax.shard_map(
        per_device,
        mesh=mesh,
        in_specs=(
            P("stream", "dp", None),
            P("stream", None, None),
            P("stream", None),
            P("stream", None, None),
            P("stream", None),
            P("stream", None),
            P("stream", None),
            P("stream", None, None),
            P("stream", None),
            P("stream", None, None),
            P("stream", None),
            P("stream", None),
            P("stream", None),
            P("stream", None, None),
            P(),
            P(),
            P("dp"),
        ),
        out_specs=(
            P(),
            P("stream", "dp", None),
            P("stream", None, None),
            P("stream", None),
            P("stream", None, None),
            P("stream", None),
            P("stream", None),
            P("stream", None),
            P("stream", None, None),
            P("stream", None),
            P("stream", None, None),
            P("stream", None),
            P("stream", None),
            P("stream", None),
            P("stream", None, None),
            P(),
        ),
        check_vma=False,
    )
```

profile of v0, /device:TPU:0, one launch (start us, length us, event | category | flops | bytes accessed | tf_op | source)
XLA Modules:
  0.0 500.8 jit_solution(15288307676167278738)
XLA Ops:
  8.1 2.1 convolution_add_fusion
  14.9 1.2 copy.148
  17.9 3.2 fusion.160
  21.2 2.0 convolution_convert_fusion.2
  24.5 6.6 %multiply_convert_fusion.1 = (bf16[256,2048]{1,0:T(8,128)(2,1)S(1)}, f32[256,2048]{1,0:T(8,128)}, f32[256,2048]{1,0:T(8,128)}) fusion(f32[2048]{0:T(1024)S(1)} %bitcast.413, bf16[1,512,2048]{2,1,0:T(8,128)(2,1)S(1)} %copy-done, f32[256,512]{1,0:T(8,128)S(1)} %get-tuple-element.704, f32[512]{0:T(512)S(1)} %bitcast.398, f32[512]{0:T(512)S(1)} %bitcast.392, ...), kind=kOutput, calls=%fused_computation.124 | convolution fusion | flops 572129280 | bytes 7878656 | tf_op jit(solution)/shard_map/dot_general | solution.py:218
  33.3 3.0 collective-permute-start
  36.3 2.2 collective-permute-done
  43.7 34.3 %all-gather.2.cloned.1.call-done = bf16[4096,128]{0,1:T(8,128)(2,1)} async-done(((bf16[256,128]{0,1:T(8,128)(2,1)}), bf16[4096,128]{0,1:T(8,128)(2,1)}) %all-gather.2.cloned.1.call-update) | async-done | bytes 1048592 | tf_op jit(solution)/shard_map/all_gather | solution.py:246
  78.6 34.3 %while.35 = (s32[]{:T(128)}, f32[3,128,64]{1,2,0:T(8,128)}, s32[4096]{0:T(1024)S(1)}, bf16[4096,128]{0,1:T(8,128)(2,1)}, bf16[128,128]{1,0:T(8,128)(2,1)S(1)}, /...) while((s32[]{:T(128)}, f32[3,128,64]{1,2,0:T(8,128)}, ...), condition=%wide.region_16.17_spmd, body=%wide.region_12.16_spmd.sunk | while | flops 110137344 | bytes 35014664 | solution.py:134
  81.0 1.2 slice_reduce_fusion.13
  83.0 1.4 fusion.245
  84.3 2.6 copy.182
  87.0 2.5 copy.183
  89.5 1.3 copy.184
  90.8 4.0 fusion.248
  100.1 1.4 fusion.245
  101.5 2.6 copy.182
  104.1 2.5 copy.183
  106.6 1.3 copy.184
  108.0 4.0 fusion.248
  112.9 1.8 copy.152
  115.9 1.4 multiply_reduce_fusion.9
  117.3 1.6 bitcast_divide_fusion
  119.0 1.7 copy.156
  120.6 1.6 broadcast_in_dim.149
  122.2 26.2 %while.36 = (s32[]{:T(128)}, f32[128,128]{0,1:T(8,128)S(1)}, f32[3,128]{1,0:T(4,128)S(1)}, f32[4096,128]{0,1:T(8,128)}, bf16[4096,128]{0,1:T(8,128)(2,1)S(1)}, /...) while((s32[]{:T(128)}, f32[128,128]{0,1:T(8,128)S(1)}, ...), condition=%wide.region_29.30_spmd.clone, body=%wide.region_23.29_spmd.clone.sunk | while | flops 258347392 | bytes 64063032 | solution.py:134
  124.9 4.2 multiply_reduce_fusion.12
  129.5 1.4 fusion.274
  134.1 1.3 copy-done.8
  137.8 4.2 multiply_reduce_fusion.12
  142.5 1.4 fusion.274
  147.1 1.3 copy-done.8
  149.2 60.5 %reduce-scatter.2.cloned.1.call-done = f32[256,128]{0,1:T(8,128)} async-done(((f32[4096,128]{0,1:T(8,128)}), f32[256,128]{0,1:T(8,128)}) %reduce-scatter.2.cloned.1.call-update) | async-done | bytes 131088 | tf_op jit(solution)/shard_map/reduce_scatter | solution.py:318
  210.6 1.5 collective-permute-start.2
  212.8 3.3 collective-permute-done.1
  219.4 3.0 convert_reduce_fusion
  224.9 1.3 convolution_bitcast_fusion.8
  227.0 2.3 convolution_convert_fusion
  232.1 2.9 convolution_bitcast_fusion.7
  235.0 2.8 convolution_bitcast_fusion.6
  238.7 2.2 convolution_bitcast_fusion.5
  242.2 41.5 %all-reduce = (f32[]{:T(128)}, f32[]{:T(128)}) all-reduce(f32[]{:T(128)S(6)} %div.120, f32[]{:T(128)} %get-tuple-element.597), channel_id=1, replica_groups=mesh['stream'=2,'dp'=16] {'stream','dp'}, use_global_device_ids=true, to_apply=%region_22.23 | all-reduce | flops 2 | bytes 16 | tf_op jit(solution)/shard_map/psum | solution.py:261
  284.0 62.5 %all-reduce.1 = (f32[1,1536]{1,0:T(1,128)}, f32[1,512]{1,0:T(1,128)}, f32[1,512]{1,0:T(1,128)}, f32[1,512]{1,0:T(1,128)}, f32[1,2048]{1,0:T(1,128)}, /*index=5*/...) all-reduce(f32[1,1536]{1,0:T(1,128)S(1)} %broadcast_in_dim.157, ...), channel_id=1, replica_groups=mesh['stream'=2,'dp'=16] {'dp'}, use_global_device_ids=true, to_apply=%region_38.39 | all-reduce | flops 6656 | bytes 53248 | tf_op jit(solution)/shard_map/psum | solution.py:368
  346.6 2.8 fusion.109
  349.4 132.7 %all-reduce.5.cloned.1.call-done = (f32[1,512,1536]{1,2,0:T(8,128)}, f32[1,512,512]{2,1,0:T(8,128)}, f32[1,512,2048]{2,1,0:T(8,128)}, f32[1,2048,512]{2,1,0:T(8,128)}, f32[1,512,128]{2,1,0:T(8,128)}) async-done(((f32[1,512,1536]{1,2,0:T(8,128)}, f32[1,512,512]{2,1,0:T(8,128)}, f32[1,512,2048]{2,1,0:T(8,128)}, f32[1,2048,512]{2,1,0:T(8,128)}, f32[1,512,128]{2,1,0:T(8,128)}), (f32[1,512,1536]{1,2,0:T(8,128)}, ...) | async-done | bytes 12845072 | tf_op jit(solution)/shard_map/psum | solution.py:368
  482.1 3.6 copy.161
  486.7 4.8 copy.215
  491.6 2.0 copy.216
  (381 shorter events, 52.6 us)
Async XLA Ops:
  7.2 17.3 %copy-start = (bf16[1,512,2048]{2,1,0:T(8,128)(2,1)S(1)}, bf16[1,512,2048]{2,1,0:T(8,128)(2,1)}, u32[]{:S(2)}) copy-start(bf16[1,512,2048]{2,1,0:T(8,128)(2,1)} %param.28) | copy-start | bytes 6291460
  7.2 70.7 %all-gather.2.cloned.1.call-start = ((), (), s32[]{:S(2)}) async-start(), calls=%async_computation.1 | async-start | bytes 1114112 | tf_op jit(solution)/shard_map/all_gather | solution.py:246
  10.3 3.4 slice-start
  11.8 19.2 %copy-start.46 = (f32[1,512]{1,0:T(1,128)}, f32[1,512]{1,0:T(1,128)S(1)}, u32[]{:S(2)}) copy-start(f32[1,512]{1,0:T(1,128)S(1)} %mul.894) | copy-start | bytes 6148
  11.9 19.2 %copy-start.52 = (f32[1,512]{1,0:T(1,128)}, f32[1,512]{1,0:T(1,128)S(1)}, u32[]{:S(2)}) copy-start(f32[1,512]{1,0:T(1,128)S(1)} %add.681) | copy-start | bytes 6148
  12.5 19.8 %copy-start.54 = (f32[1,512]{1,0:T(1,128)}, f32[1,512]{1,0:T(1,128)S(1)}, u32[]{:S(2)}) copy-start(f32[1,512]{1,0:T(1,128)S(1)} %mul.895) | copy-start | bytes 6148
  13.8 3.3 copy-start.50
  17.9 3.3 copy-start.28
  17.9 3.3 copy-start.30
  17.9 3.3 copy-start.32
  17.9 3.3 copy-start.41
  23.6 7.4 %copy-start.5 = (f32[256,512]{1,0:T(8,128)}, f32[256,512]{1,0:T(8,128)S(1)}, u32[]{:S(2)}) copy-start(f32[256,512]{1,0:T(8,128)S(1)} %get-tuple-element.704) | copy-start | bytes 1572868
  23.7 7.4 %copy-start.56 = (f32[256]{0:T(256)}, f32[256]{0:T(256)S(1)}, u32[]{:S(2)}) copy-start(f32[256]{0:T(256)S(1)} %broadcast_multiply_fusion.1) | copy-start | bytes 3076
  23.9 7.2 %copy-start.60 = (f32[256]{0:T(256)}, f32[256]{0:T(256)S(1)}, u32[]{:S(2)}) copy-start(f32[256]{0:T(256)S(1)} %fusion.139) | copy-start | bytes 3076
  24.5 6.6 %copy-start.87 = (f32[1,512]{1,0:T(1,128)S(1)}, f32[1,512]{1,0:T(1,128)}, u32[]{:S(2)}) copy-start(f32[1,512]{1,0:T(1,128)} %add.683) | copy-start | bytes 6148
  24.5 6.6 %copy-start.89 = (bf16[1,2048,512]{2,1,0:T(8,128)(2,1)S(1)}, bf16[1,2048,512]{2,1,0:T(8,128)(2,1)}, u32[]{:S(2)}) copy-start(bf16[1,2048,512]{2,1,0:T(8,128)(2,1)} %param.30) | copy-start | bytes 6291460
  32.0 8.8 %copy-start.51 = (s32[16,256]{1,0:T(8,128)S(1)}, s32[16,256]{1,0:T(8,128)}, u32[]{:S(2)}) copy-start(s32[16,256]{1,0:T(8,128)} %copy-done.50) | copy-start | bytes 49156
  32.0 8.8 %copy-start.88 = (s32[8]{0:T(128)S(1)}, s32[8]{0:T(128)}, u32[]{:S(2)}) copy-start(s32[8]{0:T(128)} %param.37) | copy-start | bytes 100
  32.0 9.5 %copy-start.58 = (f32[256]{0:T(256)}, f32[256]{0:T(256)S(1)}, u32[]{:S(2)}) copy-start(f32[256]{0:T(256)S(1)} %broadcast_multiply_fusion) | copy-start | bytes 3076
  32.3 9.3 %copy-start.67 = (f32[256]{0:T(256)}, f32[256]{0:T(256)S(1)}, u32[]{:S(2)}) copy-start(f32[256]{0:T(256)S(1)} %multiply_reduce_fusion.7) | copy-start | bytes 3076
  32.3 9.3 %copy-start.63 = (f32[256]{0:T(256)}, f32[256]{0:T(256)S(1)}, u32[]{:S(2)}) copy-start(f32[256]{0:T(256)S(1)} %fusion.140) | copy-start | bytes 3076
  33.3 5.2 %collective-permute-start = (bf16[256,128]{0,1:T(8,128)(2,1)S(1)}, bf16[256,128]{0,1:T(8,128)(2,1)S(1)}, u32[]{:S(2)}, u32[]{:S(2)}) collective-permute-start(bf16[256,128]{0,1:T(8,128)(2,1)S(1)} %convolution_convert_fusion.3), channel_id=1, source_target_pairs={{0,16},{16,0},{1,17},{17,1},{2,18},{18,2},{3,19},{19,3},{4,20},{20... | collective-permute-start | bytes 196616 | tf_op jit(solution)/shard_map/ppermute | solution.py:25
  39.2 170.5 %reduce-scatter.2.cloned.1.call-start = ((), (), s32[]{:S(2)}) async-start(), calls=%async_computation.2 | async-start | bytes 2228224 | tf_op jit(solution)/shard_map/reduce_scatter | solution.py:318
  43.0 35.5 %copy-start.73 = (f32[128]{0:T(128)}, f32[128]{0:T(128)S(1)}, u32[]{:S(2)}) copy-start(f32[128]{0:T(128)S(1)} %slice_reduce_fusion.6) | copy-start | bytes 1540
  43.1 35.5 %copy-start.77 = (f32[1,128]{1,0:T(1,128)}, f32[1,128]{1,0:T(1,128)S(1)}, u32[]{:S(2)}) copy-start(f32[1,128]{1,0:T(1,128)S(1)} %get-tuple-element.666) | copy-start | bytes 1540
  43.1 35.5 %copy-start.79 = (f32[1,128]{1,0:T(1,128)}, f32[1,128]{1,0:T(1,128)S(1)}, u32[]{:S(2)}) copy-start(f32[1,128]{1,0:T(1,128)S(1)} %get-tuple-element.667) | copy-start | bytes 1540
  84.3 5.2 %copy-start.2 = (f32[2048,128]{1,0:T(8,128)S(1)}, f32[2048,128]{1,0:T(8,128)}, u32[]{:S(2)}) copy-start(f32[2048,128]{1,0:T(8,128)} %copy-done.1) | copy-start | bytes 3145732 | tf_op jit(solution)/shard_map/while
  90.8 4.0 copy-start.19
  101.5 5.2 %copy-start.2 = (f32[2048,128]{1,0:T(8,128)S(1)}, f32[2048,128]{1,0:T(8,128)}, u32[]{:S(2)}) copy-start(f32[2048,128]{1,0:T(8,128)} %copy-done.1) | copy-start | bytes 3145732 | tf_op jit(solution)/shard_map/while
  108.0 4.0 copy-start.19
  112.9 9.3 %copy-start.4 = (bf16[4096,128]{0,1:T(8,128)(2,1)S(1)}, bf16[4096,128]{0,1:T(8,128)(2,1)}, u32[]{:S(2)}) copy-start(bf16[4096,128]{0,1:T(8,128)(2,1)} %get-tuple-element.997) | copy-start | bytes 3145732
  112.9 9.3 %copy-start.48 = (f32[3,128]{1,0:T(4,128)S(1)}, f32[3,128]{1,0:T(4,128)}, u32[]{:S(2)}) copy-start(f32[3,128]{1,0:T(4,128)} %custom-call.1) | copy-start | bytes 4612
  112.9 9.3 %copy-start.49 = (f32[3,128]{1,0:T(4,128)S(1)}, f32[3,128]{1,0:T(4,128)}, u32[]{:S(2)}) copy-start(f32[3,128]{1,0:T(4,128)} %get-tuple-element.1020) | copy-start | bytes 4612
  148.4 69.7 %copy-start.10 = (f32[256,512]{1,0:T(8,128)S(1)}, f32[256,512]{1,0:T(8,128)}, u32[]{:S(2)}) copy-start(f32[256,512]{1,0:T(8,128)} %copy-done.9) | copy-start | bytes 1572868
  148.4 69.7 %copy-start.36 = (bf16[1,512,128]{2,1,0:T(8,128)(2,1)S(1)}, bf16[1,512,128]{2,1,0:T(8,128)(2,1)}, u32[]{:S(2)}) copy-start(bf16[1,512,128]{2,1,0:T(8,128)(2,1)} %param.34) | copy-start | bytes 393220
  148.4 69.6 %copy-start.55 = (f32[1,512]{1,0:T(1,128)S(1)}, f32[1,512]{1,0:T(1,128)}, u32[]{:S(2)}) copy-start(f32[1,512]{1,0:T(1,128)} %copy-done.54) | copy-start | bytes 6148
  148.4 69.6 %copy-start.59 = (f32[256]{0:T(256)S(1)}, f32[256]{0:T(256)}, u32[]{:S(2)}) copy-start(f32[256]{0:T(256)} %copy-done.58) | copy-start | bytes 3076
  148.4 69.6 %copy-start.64 = (f32[256]{0:T(256)S(1)}, f32[256]{0:T(256)}, u32[]{:S(2)}) copy-start(f32[256]{0:T(256)} %copy-done.63) | copy-start | bytes 3076
  148.4 70.0 %copy-start.68 = (f32[256]{0:T(256)S(1)}, f32[256]{0:T(256)}, u32[]{:S(2)}) copy-start(f32[256]{0:T(256)} %copy-done.67) | copy-start | bytes 3076
  148.5 333.7 %all-reduce.5.cloned.1.call-start = ((), (), s32[]{:S(2)}) async-start(), calls=%async_computation.3 | async-start | bytes 25690112 | tf_op jit(solution)/shard_map/psum | solution.py:368
  210.6 5.5 %collective-permute-start.2 = (bf16[256,128]{0,1:T(8,128)(2,1)S(1)}, bf16[256,128]{0,1:T(8,128)(2,1)S(1)}, u32[]{:S(2)}, u32[]{:S(2)}) collective-permute-start(bf16[256,128]{0,1:T(8,128)(2,1)S(1)} %convert_element_type.202), channel_id=1, source_target_pairs={{0,16},{16,0},{1,17},{17,1},{2,18},{18,2},{3,19},{19,3},{4,20},{20... | collective-permute-start | bytes 196616 | tf_op jit(solution)/shard_map/ppermute | solution.py:25
  212.1 4.0 collective-permute-start.1
  218.9 3.5 copy-start.23
  219.4 3.0 copy-start.57
  219.4 3.0 copy-start.61
  223.8 3.2 copy-start.70
  482.1 3.6 copy-start.25
  486.7 4.9 copy-start.11
  (58 other events, 91.5 us)
Sparse Core Ops, SparseCore 0:
  39.3 38.5 all-gather.1
  148.6 61.0 reduce-scatter.1
  241.1 240.9 all-reduce.4
where the time goes:
time: 502 us; the launch traced here: 501 us
  waiting for transfers between devices  233 us (46%)
  blocking collectives  104 us (21%)
  matrix products  62.8 us (13%)
  local copies, waits for them, and re-layouts  53 us (11%)
  other arithmetic  25.3 us (5%)
  between operations  16.1 us (3%)
  starting transfers between devices  5.71 us (1%)
    psum x1, waiting for transfers between devices, per_device(): lax.psum((grad_qkv, grad_bqkv, grad_out, grad_bout, grad_gain1, grad_shif...  133 us
    psum x1, blocking collectives, per_device(): lax.psum((grad_qkv, grad_bqkv, grad_out, grad_bout, grad_gain1, grad_shif...  62.5 us
    reduce_scatter x1, waiting for transfers between devices, per_device(): doc_share = lax.psum_scatter(dd_all, 'dp', scatter_dimension=0, tiled=True)  60.5 us
    psum x1, blocking collectives, per_device(): loss, log_scale_grad = lax.psum((loss_part, scale_part), ('stream', 'dp'))  41.5 us
    all_gather x1, waiting for transfers between devices, per_device(): all_docs = lax.all_gather(docs_here, 'dp', axis=0, tiled=True)  34.3 us
    unnamed x177, local copies, waits for them, and re-layouts  18.7 us
    dot_general x17, matrix products, inner_rows(): lax.dot_general(left_op, right_op, (((1,), (1,)), ((), ())), preferred_el...  13.9 us
    another operation x6, local copies, waits for them, and re-layouts, similarities(): sums = jnp.stack([part_a, part_a + part_b, part_a + part_b + part_c])  13 us
  transfers between devices with their start and end apart: 6, of which 5 were waited for; matrix products, arithmetic and copies ran while one was open for 1% of the time, Pallas kernels for 0%

commit v1 on v0

v1 whole, which is shorter than its diff:
```python
from functools import partial
import math

import jax
import jax.numpy as jnp
import numpy as np
from jax import lax
from jax.experimental import pallas as pl
from jax.experimental.pallas import tpu as pltpu
from jax.sharding import PartitionSpec as P

D = 512
HEADS = 8
HD = 64
FF = 2048
PROJ = 128
QLEN = 32
DOCS_ROW = 4
ROW = 256
EXT = 16
RANGES = (64, 96, 128)

SHARPNESS = 8.0
EPS_NORM = 1e-06
EPS_LAYER = 1e-05
LOG2E = 1.4426950408889634

F32 = jnp.float32
BF16 = jnp.bfloat16
REST = 2304
VLIMIT = 56 * 1024 * 1024

VMEM = pl.BlockSpec(memory_space=pltpu.VMEM)
SMEM = pl.BlockSpec(memory_space=pltpu.SMEM)


def mm(a, b):
    return lax.dot_general(a, b, (((1,), (0,)), ((), ())), preferred_element_type=F32)


def mm_nt(a, b):
    return lax.dot_general(a, b, (((1,), (1,)), ((), ())), preferred_element_type=F32)


def mm_tn(a, b):
    return lax.dot_general(a, b, (((0,), (0,)), ((), ())), preferred_element_type=F32)


def iota(shape, axis):
    return lax.broadcasted_iota(jnp.int32, shape, axis)


def rope_table():
    half = HD // 2
    freqs = (10000.0 ** (-np.arange(half, dtype=np.float32) / np.float32(half))).astype(np.float32)
    turned = np.arange(ROW, dtype=np.float32)[:, None] * freqs[None, :]
    cosine = np.cos(turned.astype(np.float64))
    sine = np.sin(turned.astype(np.float64))
    cosine = np.concatenate([cosine, cosine, cosine, cosine], axis=1).astype(np.float32)
    sine = np.concatenate([-sine, sine, -sine, sine], axis=1).astype(np.float32)
    parts = []
    for table in (cosine, sine):
        high = table.astype(jnp.bfloat16)
        low = (table - high.astype(np.float32)).astype(jnp.bfloat16)
        parts += [high, low]
    return np.concatenate(parts, axis=1)


def swap_halves(block):
    lane = iota(block.shape, 1)
    return jnp.where(lane % HD < HD // 2, pltpu.roll(block, 96, 1), pltpu.roll(block, 32, 1))


def bounds_of(lens_ref, row):
    ends, total = [], jnp.int32(0)
    for k in range(DOCS_ROW):
        total = total + lens_ref[row, k]
        ends.append(total)
    return ends


def segment_of(spot, ends):
    seg = jnp.zeros_like(spot)
    for end in ends:
        seg = seg + (spot >= end).astype(jnp.int32)
    return seg


def norm_rows(values):
    mean = jnp.mean(values, axis=1, keepdims=True)
    centred = values - mean
    spread = jnp.mean(centred * centred, axis=1, keepdims=True)
    rstd = lax.rsqrt(spread + EPS_LAYER)
    return centred * rstd, rstd


def norm_back(d_out, xhat, rstd, gain):
    scaled = d_out * gain
    first = jnp.mean(scaled, axis=1, keepdims=True)
    second = jnp.mean(scaled * xhat, axis=1, keepdims=True)
    return rstd * (scaled - first - xhat * second)


def col_sum(values):
    return jnp.sum(values, axis=0, keepdims=True)


def encoder_forward(
    where_ref, lens_ref, labels_ref, table_ref, x_ref, wqkv_ref, bqkv_ref, wout_ref, bout_ref,
    g1_ref, s1_ref, wup_ref, bup_ref, wdown_ref, bdown_ref, g2_ref, s2_ref, wproj_ref,
    vec_ref, qkv_ref, rope_ref, probs_ref, mixed_ref, xh1_ref, rs1_ref, act_ref, slope_ref,
    xh2_ref, rs2_ref,
):
    me, is_query = where_ref[0], where_ref[1] == 0
    ends = bounds_of(lens_ref, me)

    def layout(spot):
        seg_doc = segment_of(spot, ends)
        start_doc = jnp.zeros_like(spot)
        for k in range(DOCS_ROW):
            start_doc = jnp.where(seg_doc == k + 1, ends[k], start_doc)
        seg_query = spot // QLEN
        seg = jnp.where(is_query, seg_query, seg_doc)
        start = jnp.where(is_query, seg_query * QLEN, start_doc)
        return seg, start

    shape = (ROW, ROW)
    seg_q, start_q = layout(iota(shape, 0))
    seg_k, _ = layout(iota(shape, 1))
    same = seg_q == seg_k
    onehot = (iota(shape, 1) == iota(shape, 0) - start_q).astype(F32).astype(BF16)
    turned = mm(onehot, table_ref[...])
    cosine = turned[:, :128] + turned[:, 128:256]
    sine = turned[:, 256:384] + turned[:, 384:]
    rope_ref[:, :128] = cosine
    rope_ref[:, 128:] = sine

    x = x_ref[...]
    joined = mm(x, wqkv_ref[...]) + bqkv_ref[...].astype(F32)
    for g in range(2 * D // 128):
        block = joined[:, g * 128 : (g + 1) * 128]
        qkv_ref[:, g * 128 : (g + 1) * 128] = (
            block * cosine + swap_halves(block) * sine
        ).astype(BF16)
    qkv_ref[:, 2 * D :] = joined[:, 2 * D :].astype(BF16)

    low_half = iota((ROW, 128), 1) < HD
    for g in range(HEADS // 2):
        q_g = qkv_ref[:, g * 128 : (g + 1) * 128]
        k_g = qkv_ref[:, D + g * 128 : D + (g + 1) * 128]
        v_g = qkv_ref[:, 2 * D + g * 128 : 2 * D + (g + 1) * 128]
        outs = []
        for h in range(2):
            pick = low_half if h == 0 else jnp.logical_not(low_half)
            scores = mm_nt(jnp.where(pick, q_g, jnp.zeros_like(q_g)), k_g) * (1.0 / math.sqrt(HD))
            scores = jnp.where(same, scores, -1e30)
            top = jnp.max(scores, axis=1, keepdims=True)
            exps = jnp.exp(scores - top)
            probs = (exps / jnp.sum(exps, axis=1, keepdims=True)).astype(BF16)
            probs_ref[2 * g + h] = probs
            outs.append(mm(probs, v_g))
        mixed_ref[:, g * 128 : (g + 1) * 128] = jnp.where(low_half, outs[0], outs[1]).astype(BF16)

    attended = mm(mixed_ref[...], wout_ref[...]) + bout_ref[...].astype(F32)
    xhat, rstd = norm_rows(x.astype(F32) + attended)
    xh1_ref[...] = xhat
    rs1_ref[...] = jnp.broadcast_to(rstd, (ROW, 128))
    first = xhat * g1_ref[...].astype(F32) + s1_ref[...].astype(F32)
    first_low = first.astype(BF16)
    branch = bdown_ref[...].astype(F32) + first
    step = 512
    for c in range(FF // step):
        cols = slice(c * step, (c + 1) * step)
        inner = mm(first_low, wup_ref[:, cols]) + bup_ref[:, cols].astype(F32)
        gate = 0.5 + 0.5 * lax.erf(inner * math.sqrt(0.5))
        bell = jnp.exp(inner * inner * -0.5) * (1.0 / math.sqrt(2.0 * math.pi))
        act = (inner * gate).astype(BF16)
        act_ref[:, cols] = act
        slope_ref[:, cols] = (gate + inner * bell).astype(BF16)
        branch = branch + mm(act, wdown_ref[cols, :])
    xhat, rstd = norm_rows(branch)
    xh2_ref[...] = xhat
    rs2_ref[...] = jnp.broadcast_to(rstd, (ROW, 128))
    second = xhat * g2_ref[...].astype(F32) + s2_ref[...].astype(F32)
    vec_ref[:ROW, :] = mm(second.astype(BF16), wproj_ref[...]).astype(BF16)
    line = iota((EXT, PROJ), 0)
    tag = jnp.zeros((EXT, PROJ), jnp.int32)
    for k in range(labels_ref.shape[0]):
        label = labels_ref[k]
        tag = jnp.where(line == k, label >> 6, tag)
        tag = jnp.where(line == k + 8, label & 63, tag)
    vec_ref[ROW:, :] = tag.astype(F32).astype(BF16)


def prefix_norms(values, axis):
    place = iota(values.shape, axis)
    squared = values * values
    sums = [
        jnp.sum(jnp.where(place < cut, squared, 0.0), axis=axis, keepdims=True) for cut in RANGES
    ]
    return [lax.rsqrt(s + EPS_NORM) for s in sums]


def load_queries(near_ref, far_ref):
    span = ROW + EXT
    rows = []
    for ref in (near_ref, far_ref):
        for k in range(ref.shape[0] // span):
            rows.append(ref[k * span : k * span + ROW, :])
    return jnp.concatenate(rows, axis=0).astype(F32)


def unit_queries(queries, scale):
    lane = iota(queries.shape, 1)
    inverse = prefix_norms(queries, 1)
    unit = [
        jnp.where(lane < cut, queries * (inv * scale), 0.0) for cut, inv in zip(RANGES, inverse)
    ]
    return unit, inverse


def unit_docs(doc_refs, scratch_ref):
    at = 0
    for ref in doc_refs:
        for k in range(ref.shape[0] // ROW):
            scratch_ref[:, at * ROW : (at + 1) * ROW] = ref[
                k * ROW : (k + 1) * ROW, :
            ].astype(F32).T
            at += 1
    turned = scratch_ref[...]
    inverse = prefix_norms(turned, 0)
    place = iota(turned.shape, 0)
    unit = [jnp.where(place < cut, turned * inv, 0.0) for cut, inv in zip(RANGES, inverse)]
    return unit, inverse


def row_ids(base, masks, doc_rows):
    ids = []
    for p in range(doc_rows):
        offset = 0
        for k, mask in enumerate(masks):
            if (p >> k) & 1:
                offset ^= mask
        ids.append(base ^ offset)
    return ids


def doc_marks(lens_ref, ids, lanes, transposed):
    docs = len(ids) * DOCS_ROW
    shape = (lanes, ROW) if transposed else (ROW, lanes)
    spot, lane = (iota(shape, 1), iota(shape, 0)) if transposed else (iota(shape, 0), iota(shape, 1))
    marks = []
    for p, row in enumerate(ids):
        seg = segment_of(spot, bounds_of(lens_ref, row))
        local = jnp.where(seg < DOCS_ROW, seg + p * DOCS_ROW, -1 - lanes)
        marks.append(
            [(lane == local + m * docs).astype(F32).astype(BF16) for m in range(len(RANGES))]
        )
    return marks


def matching_stats(
    masks, lanes, where_ref, scale_ref, lens_ref, near_ref, far_ref, *refs
):
    doc_refs = refs[:-6]
    totals_ref, el_ref, hot_ref, stats_ref, turn_ref, unit_ref = refs[-6:]
    base, near_at = where_ref[2], where_ref[3]
    span = ROW + EXT
    queries = load_queries(near_ref, far_ref)
    count = queries.shape[0]
    unit_q, _ = unit_queries(queries, SHARPNESS * LOG2E)
    unit_q = [u.astype(BF16) for u in unit_q]
    unit_d, _ = unit_docs(doc_refs, turn_ref)
    for m in range(len(RANGES)):
        unit_ref[m] = unit_d[m].astype(BF16)
    doc_rows = turn_ref.shape[1] // ROW
    docs = doc_rows * DOCS_ROW
    ids = row_ids(base, masks, doc_rows)
    marks = doc_marks(lens_ref, ids, lanes, False)
    totals = jnp.zeros((count, lanes), F32)
    for p in range(doc_rows):
        for m in range(len(RANGES)):
            sims = mm(unit_q[m], unit_ref[m, :, p * ROW : (p + 1) * ROW])
            totals = totals + mm(jnp.exp2(sims).astype(BF16), marks[p][m])
    lane_t = iota((count, lanes), 1)
    totals = jnp.where(lane_t < len(RANGES) * docs, totals, 1.0)
    totals_ref[...] = totals
    shape = (8, lanes)
    lane = iota(shape, 1)
    length = jnp.ones(shape, jnp.int32)
    name = jnp.full(shape, -1, jnp.int32)
    for p in range(doc_rows):
        for k in range(DOCS_ROW):
            own = jnp.zeros(shape, jnp.bool_)
            for m in range(len(RANGES)):
                own = jnp.logical_or(own, lane == m * docs + p * DOCS_ROW + k)
            length = jnp.where(own, lens_ref[ids[p], k], length)
            name = jnp.where(own, ids[p] * DOCS_ROW + k, name)
    log_length = jnp.log(length.astype(F32))
    matched = (jnp.log(totals) - log_length[:1]) * (1.0 / SHARPNESS)
    per_query = jnp.sum(matched.reshape(count // QLEN, QLEN, lanes), axis=1)
    scale = jnp.exp(jnp.full(shape, scale_ref[0], F32))[:1]
    logits = per_query * (scale * (1.0 / QLEN))
    groups = count // ROW
    tags = []
    for ref in (near_ref, far_ref):
        for k in range(ref.shape[0] // span):
            high = ref[k * span + ROW : k * span + ROW + 8, :].astype(F32).astype(jnp.int32)
            low = ref[k * span + ROW + 8 : k * span + ROW + 16, :].astype(F32).astype(jnp.int32)
            tag = high * 64 + low
            tags.append(jnp.concatenate([tag] * (lanes // 128), axis=1))
    tag = jnp.concatenate(tags, axis=0)
    lane_q = iota(logits.shape, 1)
    valid = lane_q < len(RANGES) * docs
    el = jnp.where(valid, jnp.exp(logits), 0.0)
    hot = jnp.where(jnp.logical_and(valid, jnp.concatenate([name] * groups, axis=0) == tag), 1.0, 0.0)
    el_ref[...] = el
    hot_ref[...] = hot
    place = iota((groups * 8, 128), 1)
    stats = jnp.zeros((groups * 8, 128), F32)
    for k, values in enumerate((el, el * logits, hot * logits)):
        for m in range(len(RANGES)):
            inside = jnp.logical_and(lane_q >= m * docs, lane_q < (m + 1) * docs)
            one = jnp.sum(jnp.where(inside, values, 0.0), axis=1, keepdims=True)
            stats = jnp.where(place == k * 3 + m, one, stats)
    for a in range(groups):
        at = pl.multiple_of((near_at ^ a) * 8, 8)
        stats_ref[pl.ds(at, 8), :] = stats[a * 8 : (a + 1) * 8, :]


def matching_back(
    masks, lanes, total_queries, where_ref, scale_ref, lens_ref, near_ref, far_ref, totals_ref,
    el_ref, hot_ref, stats_ref, *refs
):
    doc_refs = refs[:-8]
    dq_ref, dd_ref, loss_ref, turn_ref, unit_ref, qt_ref, dot_ref, dt_ref = refs[-8:]
    base, near_at = where_ref[2], where_ref[3]
    temper = SHARPNESS * LOG2E
    queries = load_queries(near_ref, far_ref)
    count = queries.shape[0]
    unit_q, inv_q = unit_queries(queries, temper)
    unit_q = [u.astype(BF16) for u in unit_q]
    unit_d, inv_d = unit_docs(doc_refs, turn_ref)
    for m in range(len(RANGES)):
        unit_ref[m] = unit_d[m].astype(BF16)
        qt_ref[m] = unit_q[m].astype(F32).T.astype(BF16)
    doc_rows = turn_ref.shape[1] // ROW
    docs = doc_rows * DOCS_ROW
    ids = row_ids(base, masks, doc_rows)
    marks = doc_marks(lens_ref, ids, lanes, True)
    groups = count // ROW
    rows = []
    for a in range(groups):
        at = pl.multiple_of((near_at ^ a) * 8, 8)
        rows.append(stats_ref[pl.ds(at, 8), :])
    stats = jnp.concatenate(rows, axis=0)
    place = iota(stats.shape, 1)

    def column(k):
        return jnp.sum(jnp.where(place == k, stats, 0.0), axis=1, keepdims=True)

    shape = (groups * 8, lanes)
    lane_q = iota(shape, 1)
    sums = jnp.ones(shape, F32)
    loss = jnp.zeros((groups * 8, 1), F32)
    moved = jnp.zeros((groups * 8, 1), F32)
    for m in range(len(RANGES)):
        whole, weighted, picked = column(m), column(3 + m), column(6 + m)
        inside = jnp.logical_and(lane_q >= m * docs, lane_q < (m + 1) * docs)
        sums = jnp.where(inside, whole, sums)
        loss = loss + (jnp.log(whole) - picked)
        moved = moved + (weighted / whole - picked)
    line = iota((8, 128), 0)
    loss_ref[...] = jnp.where(
        line == 0,
        jnp.sum(loss, axis=0, keepdims=True) * (1.0 / total_queries),
        jnp.where(line == 1, jnp.sum(moved, axis=0, keepdims=True) * (1.0 / total_queries), 0.0),
    )
    scale = jnp.exp(jnp.full((8, lanes), scale_ref[0], F32))[:1]
    coeff = (el_ref[...] / sums - hot_ref[...]) * (scale * (1.0 / (QLEN * total_queries)))
    coeff = jnp.broadcast_to(coeff[:, None, :], (groups * 8, QLEN, lanes)).reshape(count, lanes)
    ratio = coeff / totals_ref[...]
    ratio_high = ratio.astype(BF16)
    ratio_low = (ratio - ratio_high.astype(F32)).astype(BF16)
    ratio = jnp.concatenate([ratio_high, ratio_low], axis=1)
    for m in range(len(RANGES)):
        grad = jnp.zeros((count, PROJ), F32)
        for p in range(doc_rows):
            block = unit_ref[m, :, p * ROW : (p + 1) * ROW]
            mark = marks[p][m]
            exps = jnp.exp2(mm(unit_q[m], block))
            d_sims = (exps * mm(ratio, jnp.concatenate([mark, mark], axis=0))).astype(BF16)
            grad = grad + mm_nt(d_sims, block)
            dt_ref[m, :, p * ROW : (p + 1) * ROW] = mm(qt_ref[m], d_sims)
        unit = unit_q[m].astype(F32) * (1.0 / temper)
        along = jnp.sum(grad * unit, axis=1, keepdims=True)
        part = inv_q[m] * (grad - unit * along)
        if m == 0:
            dot_ref[...] = part
        else:
            dot_ref[...] += part
    dq_ref[...] = dot_ref[...].astype(BF16)
    total = jnp.zeros(turn_ref.shape, F32)
    for m in range(len(RANGES)):
        grad = dt_ref[m] * (1.0 / temper)
        unit = unit_ref[m].astype(F32)
        along = jnp.sum(grad * unit, axis=0, keepdims=True)
        total = total + inv_d[m] * (grad - unit * along)
    for p in range(doc_rows):
        dd_ref[p * ROW : (p + 1) * ROW, :] = total[:, p * ROW : (p + 1) * ROW].T.astype(BF16)


def store_block(refs, at, value):
    keep_ref, send_ref = refs
    half = keep_ref.shape[0]

    @pl.when(at < half)
    def _():
        keep_ref[at] = value

    @pl.when(at >= half)
    def _():
        send_ref[at - half] = value


def feed_back(
    where_ref, dq_ref, dd_ref, got_ref, xh2_ref, rs2_ref, g2_ref, s2_ref, xh1_ref, g1_ref, s1_ref,
    act_ref, slope_ref, wproj_ref, wdown_ref, wup_ref,
    down_keep, down_send, up_keep, up_send, dfirst_ref, gproj_ref, small_ref, dinner_ref,
):
    is_query, docs_there = where_ref[1] == 0, where_ref[4] == 0
    down_at, up_at = where_ref[5], where_ref[6]
    got = got_ref[...].astype(F32)
    d_vec = jnp.where(
        is_query,
        dq_ref[...].astype(F32) + got,
        jnp.where(docs_there, got, dd_ref[...].astype(F32)),
    )
    d_proj = d_vec.astype(BF16)
    xhat = xh2_ref[...]
    gain = g2_ref[...].astype(F32)
    second = (xhat * gain + s2_ref[...].astype(F32)).astype(BF16)
    gproj_ref[...] = mm_tn(second, d_proj)
    d_second = mm_nt(d_proj, wproj_ref[...])
    small_ref[...] = jnp.zeros_like(small_ref)
    small_ref[5:6, :] = col_sum(d_second * xhat)
    small_ref[6:7, :] = col_sum(d_second)
    d_sum = norm_back(d_second, xhat, rs2_ref[:, :1], gain)
    d_branch = d_sum.astype(BF16)
    small_ref[4:5, :] = col_sum(d_branch.astype(F32))
    step = 512
    blocks = 2 * down_keep.shape[0]
    size = down_keep.shape[1]
    d_first = d_sum
    for c in range(FF // step):
        cols = slice(c * step, (c + 1) * step)
        d_act = mm_nt(d_branch, wdown_ref[cols, :])
        d_inner = (d_act * slope_ref[:, cols].astype(F32)).astype(BF16)
        dinner_ref[:, cols] = d_inner
        small_ref[c : c + 1, :] = col_sum(d_inner.astype(F32))
        grad = mm_tn(act_ref[:, cols], d_branch).astype(BF16)
        for k in range(step // size):
            store_block(
                (down_keep, down_send),
                (c * (step // size) + k) ^ down_at,
                grad[k * size : (k + 1) * size, :],
            )
        d_first = d_first + mm_nt(d_inner, wup_ref[:, cols])
    dfirst_ref[...] = d_first
    first = (xh1_ref[...] * g1_ref[...].astype(F32) + s1_ref[...].astype(F32)).astype(BF16)
    for c in range(FF // step):
        cols = slice(c * step, (c + 1) * step)
        grad = mm_tn(first, dinner_ref[:, cols]).astype(BF16)
        for k in range(D // size):
            store_block(
                (up_keep, up_send),
                (c * (D // size) + k) ^ up_at,
                grad[k * size : (k + 1) * size, :],
            )


def attend_back(
    where_ref, dfirst_ref, xh1_ref, rs1_ref, g1_ref, mixed_ref, wout_ref, qkv_ref, probs_ref,
    rope_ref, x_ref, wqkv_ref, gproj_ref, small_ref,
    keep_ref, send_ref, tokens_ref, djoined_ref, rest_ref,
):
    at = where_ref[7]
    d_first = dfirst_ref[...]
    xhat = xh1_ref[...]
    gain = g1_ref[...].astype(F32)
    gain_grad = col_sum(d_first * xhat)
    shift_grad = col_sum(d_first)
    d_sum = norm_back(d_first, xhat, rs1_ref[:, :1], gain)
    d_att = d_sum.astype(BF16)
    bias_out = col_sum(d_att.astype(F32))
    rest_ref[3 * D : 4 * D, :] = mm_tn(mixed_ref[...], d_att).astype(BF16)
    d_mixed = mm_nt(d_att, wout_ref[...]).astype(BF16)
    cosine, sine = rope_ref[:, :128], rope_ref[:, 128:]
    low_half = iota((ROW, 128), 1) < HD

    def unrotate(values):
        values = values * (1.0 / math.sqrt(HD))
        return (values * cosine - swap_halves(values) * sine).astype(BF16)

    for g in range(HEADS // 2):
        span = slice(g * 128, (g + 1) * 128)
        q_g = qkv_ref[:, g * 128 : (g + 1) * 128]
        k_g = qkv_ref[:, D + g * 128 : D + (g + 1) * 128]
        v_g = qkv_ref[:, 2 * D + g * 128 : 2 * D + (g + 1) * 128]
        m_g = d_mixed[:, span]
        d_q = jnp.zeros((ROW, 128), F32)
        d_k = jnp.zeros((ROW, 128), F32)
        d_v = jnp.zeros((ROW, 128), F32)
        zero = jnp.zeros((ROW, 128), BF16)
        for h in range(2):
            pick = low_half if h == 0 else jnp.logical_not(low_half)
            probs_low = probs_ref[2 * g + h]
            probs = probs_low.astype(F32)
            m_h = jnp.where(pick, m_g, zero)
            d_probs = mm_nt(m_h, v_g)
            d_v = d_v + mm_tn(probs_low, m_h)
            inner = jnp.sum(d_probs * probs, axis=1, keepdims=True)
            d_scores = (probs * (d_probs - inner)).astype(BF16)
            d_q = d_q + mm(d_scores, jnp.where(pick, k_g, zero))
            d_k = d_k + mm_tn(d_scores, jnp.where(pick, q_g, zero))
        djoined_ref[:, g * 128 : (g + 1) * 128] = unrotate(d_q)
        djoined_ref[:, D + g * 128 : D + (g + 1) * 128] = unrotate(d_k)
        djoined_ref[:, 2 * D + g * 128 : 2 * D + (g + 1) * 128] = d_v.astype(BF16)
    x = x_ref[...]
    tokens = d_sum
    rest_ref[4 * D + 128 :, :] = jnp.zeros((REST - 4 * D - 128, D), BF16)
    smalls = []
    for c in range(3):
        cols = slice(c * D, (c + 1) * D)
        d_part = djoined_ref[:, cols]
        rest_ref[c * D : (c + 1) * D, :] = mm_tn(x, d_part).astype(BF16)
        smalls.append(col_sum(d_part.astype(F32)))
        tokens = tokens + mm_nt(d_part, wqkv_ref[:, cols])
    tokens_ref[...] = tokens
    for k in range(4):
        rest_ref[4 * D : 4 * D + 128, k * 128 : (k + 1) * 128] = gproj_ref[
            k * 128 : (k + 1) * 128, :
        ].astype(BF16)
    smalls += [bias_out, gain_grad, shift_grad] + [small_ref[k : k + 1, :] for k in range(7)]
    smalls += [jnp.zeros((EXT - len(smalls), D), F32)]
    rest_ref[4 * D + 128 : 4 * D + 128 + EXT, :] = jnp.concatenate(smalls, axis=0).astype(BF16)
    half, size = keep_ref.shape[0], keep_ref.shape[1]
    for p in range(half):
        for ref, offset in ((keep_ref, p), (send_ref, p + half)):
            start = pl.multiple_of((offset ^ at) * size, 16)
            ref[p] = rest_ref[pl.ds(start, size), :]


def spread_out(at_index, order, where_ref, near_ref, far_ref, out_ref):
    p = pl.program_id(0)
    half = pl.num_programs(0) // 2

    @pl.when(p < half)
    def _():
        out_ref[...] = near_ref[0].astype(F32)

    @pl.when(p >= half)
    def _():
        out_ref[...] = far_ref[0].astype(F32)


def spread_call(near, far, where, at_index, columns):
    half, size, width = near.shape
    blocks = 2 * half
    per_column = blocks // columns

    def out_index(p, where_ref):
        b = p ^ where_ref[at_index]
        return (b % per_column, b // per_column)

    return pl.pallas_call(
        partial(spread_out, at_index, None),
        out_shape=jax.ShapeDtypeStruct((blocks * size // columns, width * columns), F32),
        grid_spec=pltpu.PrefetchScalarGridSpec(
            num_scalar_prefetch=1,
            grid=(blocks,),
            in_specs=[
                pl.BlockSpec((1, size, width), lambda p, w: (jnp.minimum(p, half - 1), 0, 0)),
                pl.BlockSpec((1, size, width), lambda p, w: (jnp.maximum(p - half, 0), 0, 0)),
            ],
            out_specs=pl.BlockSpec((size, width), out_index),
        ),
    )(where, near, far)


def spread_rest(
    where_ref, near_ref, far_ref, qkv_ref, out_ref, proj_ref, bqkv_ref, bout_ref, g1_ref, s1_ref,
    bup_ref, bdown_ref, g2_ref, s2_ref, rest_ref,
):
    at = where_ref[7]
    half, size = near_ref.shape[0], near_ref.shape[1]
    for p in range(half):
        for ref, offset in ((near_ref, p), (far_ref, p + half)):
            start = pl.multiple_of((offset ^ at) * size, 16)
            rest_ref[pl.ds(start, size), :] = ref[p]
    for c in range(3):
        qkv_ref[:, c * D : (c + 1) * D] = rest_ref[c * D : (c + 1) * D, :].astype(F32)
    out_ref[...] = rest_ref[3 * D : 4 * D, :].astype(F32)
    for k in range(4):
        proj_ref[k * 128 : (k + 1) * 128, :] = rest_ref[
            4 * D : 4 * D + 128, k * 128 : (k + 1) * 128
        ].astype(F32)
    small = rest_ref[4 * D + 128 : 4 * D + 128 + EXT, :].astype(F32)
    row = [small[k : k + 1, :] for k in range(13)]
    for c in range(3):
        bqkv_ref[:, c * D : (c + 1) * D] = row[c]
    bout_ref[...] = row[3]
    g1_ref[...] = row[4]
    s1_ref[...] = row[5]
    for c in range(4):
        bup_ref[:, c * D : (c + 1) * D] = row[6 + c]
    bdown_ref[...] = row[10]
    g2_ref[...] = row[11]
    s2_ref[...] = row[12]


def shape_of(shape, dtype=F32):
    return jax.ShapeDtypeStruct(tuple(shape), dtype)


def call(kernel, args, specs, outs, scratch=(), flops=0):
    return pl.pallas_call(
        kernel,
        out_shape=outs,
        in_specs=specs,
        out_specs=[VMEM] * len(outs),
        scratch_shapes=list(scratch),
        compiler_params=pltpu.CompilerParams(vmem_limit_bytes=VLIMIT),
        cost_estimate=pl.CostEstimate(flops=flops, bytes_accessed=10**6, transcendentals=0),
    )(*args)


def swapped(value, mask, axis="dp"):
    size = lax.axis_size(axis)
    return lax.ppermute(value, axis, [(k, k ^ mask) for k in range(size)])


def added(a, b):
    return (a.astype(F32) + b.astype(F32)).astype(BF16)


def block_place(me, order):
    place = jnp.int32(0)
    for k, mask in enumerate(order):
        place = place | jnp.where((me & mask) != 0, 1 << (len(order) - 1 - k), 0)
    return place


def reduce_gather(keep, send, order, others):
    got = swapped(send, order[0])
    for mask in order[1:]:
        half = keep.shape[0] // 2
        send = added(keep[half:], got[half:])
        keep = added(keep[:half], got[:half])
        got = swapped(send, mask)
    own = added(keep, got)
    for mask in others:
        own = added(own, swapped(own, mask))
    for mask in reversed(order[1:]):
        own = jnp.concatenate([own, swapped(own, mask)], axis=0)
    return own, swapped(own, order[0])


def per_device(
    tokens, qkv_weight, qkv_bias, out_weight, out_bias, first_gain, first_shift, up_weight,
    up_bias, down_weight, down_bias, second_gain, second_shift, proj_weight, log_scale,
    doc_lengths, labels,
):
    size = lax.axis_size("dp")
    bits = [1 << k for k in range(size.bit_length() - 1)]
    near_masks, doc_masks = bits[:2], bits[2:]
    top_mask, doc_masks = doc_masks[-1], doc_masks[:-1]
    orders = [
        (bits[0], bits[1], bits[2], bits[3]),
        (bits[0], bits[2], bits[1], bits[3]),
        (bits[0], bits[1], bits[2], bits[3]),
    ]
    others = bits[4:]
    blocks = 16
    me = lax.axis_index("dp")
    stream = lax.axis_index("stream")
    is_query = stream == 0
    has_top = (me & top_mask) != 0
    base = jnp.where(is_query, me & ~top_mask, me | top_mask)
    near_at = jnp.where((me & near_masks[1]) != 0, 1, 0) + jnp.where((me & near_masks[0]) != 0, 2, 0)
    where = jnp.stack(
        [me, stream, base, near_at, has_top.astype(jnp.int32)]
        + [block_place(me, order) for order in orders]
    ).astype(jnp.int32)
    scale = log_scale.reshape(1)

    vec, qkv, rope, probs, mixed, xh1, rs1, act, slope, xh2, rs2 = call(
        encoder_forward,
        (
            where, doc_lengths, labels, jnp.asarray(rope_table()), tokens[0], qkv_weight[0], qkv_bias,
            out_weight[0], out_bias, first_gain, first_shift, up_weight[0], up_bias,
            down_weight[0], down_bias, second_gain, second_shift, proj_weight[0],
        ),
        [SMEM] * 3 + [VMEM] * 15,
        [
            shape_of((ROW + EXT, PROJ), BF16),
            shape_of((ROW, 3 * D), BF16),
            shape_of((ROW, 256)),
            shape_of((HEADS, ROW, ROW), BF16),
            shape_of((ROW, D), BF16),
            shape_of((ROW, D)),
            shape_of((ROW, 128)),
            shape_of((ROW, FF), BF16),
            shape_of((ROW, FF), BF16),
            shape_of((ROW, D)),
            shape_of((ROW, 128)),
        ],
    )

    other = swapped(vec, 1, "stream")
    near = jnp.where(is_query, vec, other)
    rows = jnp.where(is_query, other, vec)[:ROW]
    moved = swapped(rows, top_mask)
    near = jnp.concatenate([near, swapped(near, near_masks[1])], axis=0)
    rows = jnp.where(has_top == is_query, moved, rows)
    far = swapped(near, near_masks[0])
    pieces = []
    for k, mask in enumerate(doc_masks):
        pieces.append(rows)
        got = swapped(rows, mask)
        if k + 1 < len(doc_masks):
            rows = jnp.concatenate([rows, got], axis=0)
        else:
            pieces = [rows, got]
    doc_rows = sum(p.shape[0] for p in pieces) // ROW
    tokens_d = doc_rows * ROW
    tokens_q = 4 * ROW
    lanes = -(-3 * doc_rows * DOCS_ROW // 128) * 128
    total_queries = size * (ROW // QLEN)
    totals, el, hot, stats = call(
        partial(matching_stats, doc_masks, lanes),
        (where, scale, doc_lengths, near, far, *pieces),
        [SMEM] * 3 + [VMEM] * (2 + len(pieces)),
        [
            shape_of((tokens_q, lanes)),
            shape_of((tokens_q // QLEN, lanes)),
            shape_of((tokens_q // QLEN, lanes)),
            shape_of((tokens_q // QLEN, 128)),
        ],
        [pltpu.VMEM((PROJ, tokens_d), F32), pltpu.VMEM((3, PROJ, tokens_d), BF16)],
    )
    stats = stats + swapped(stats, near_masks[0])
    stats = stats + swapped(stats, near_masks[1])
    stats = stats + swapped(stats, 1, "stream")
    dq, dd, loss = call(
        partial(matching_back, doc_masks, lanes, total_queries),
        (where, scale, doc_lengths, near, far, totals, el, hot, stats, *pieces),
        [SMEM] * 3 + [VMEM] * (6 + len(pieces)),
        [shape_of((tokens_q, PROJ), BF16), shape_of((tokens_d, PROJ), BF16), shape_of((8, 128))],
        [
            pltpu.VMEM((PROJ, tokens_d), F32),
            pltpu.VMEM((3, PROJ, tokens_d), BF16),
            pltpu.VMEM((3, PROJ, tokens_q), BF16),
            pltpu.VMEM((tokens_q, PROJ), F32),
            pltpu.VMEM((3, PROJ, tokens_d), F32),
        ],
    )
    for mask in reversed(doc_masks):
        half = dd.shape[0] // 2
        dd = added(dd[:half], swapped(dd[half:], mask))
    for mask in near_masks:
        half = dq.shape[0] // 2
        dq = added(dq[:half], swapped(dq[half:], mask))
    dd = added(dd, swapped(dd, top_mask))
    got = swapped(jnp.where(is_query, dd, dq), 1, "stream")

    down_keep, down_send, up_keep, up_send, d_first, gproj, small = call(
        feed_back,
        (
            where, dq, dd, got, xh2, rs2, second_gain, second_shift, xh1, first_gain, first_shift,
            act, slope, proj_weight[0], down_weight[0], up_weight[0],
        ),
        [SMEM] + [VMEM] * 15,
        [shape_of((blocks // 2, FF // blocks, D), BF16)] * 4
        + [shape_of((ROW, D)), shape_of((D, PROJ)), shape_of((8, D))],
        [pltpu.VMEM((ROW, FF), BF16)],
    )
    rest_keep, rest_send, tokens_grad = call(
        attend_back,
        (
            where, d_first, xh1, rs1, first_gain, mixed, out_weight[0], qkv, probs, rope,
            tokens[0], qkv_weight[0], gproj, small,
        ),
        [SMEM] + [VMEM] * 13,
        [shape_of((blocks // 2, REST // blocks, D), BF16)] * 2 + [shape_of((ROW, D))],
        [pltpu.VMEM((ROW, 3 * D), BF16), pltpu.VMEM((REST, D), BF16)],
    )
    down_near, down_far = reduce_gather(down_keep, down_send, orders[0], others)
    up_near, up_far = reduce_gather(up_keep, up_send, orders[1], others)
    rest_near, rest_far = reduce_gather(rest_keep, rest_send, orders[2], others)
    for mask in doc_masks + [top_mask]:
        loss = loss + swapped(loss, mask)
    grad_down = spread_call(down_near, down_far, where, 5, 1)
    grad_up = spread_call(up_near, up_far, where, 6, 4)
    (
        grad_qkv, grad_out, grad_proj, grad_bqkv, grad_bout, grad_g1, grad_s1, grad_bup,
        grad_bdown, grad_g2, grad_s2,
    ) = call(
        spread_rest,
        (where, rest_near, rest_far),
        [SMEM, VMEM, VMEM],
        [
            shape_of((D, 3 * D)), shape_of((D, D)), shape_of((D, PROJ)), shape_of((1, 3 * D)),
            shape_of((1, D)), shape_of((1, D)), shape_of((1, D)), shape_of((1, FF)),
            shape_of((1, D)), shape_of((1, D)), shape_of((1, D)),
        ],
        [pltpu.VMEM((REST, D), BF16)],
    )
    return (
        loss[0, 0],
        tokens_grad[None],
        grad_qkv[None],
        grad_bqkv,
        grad_out[None],
        grad_bout,
        grad_g1,
        grad_s1,
        grad_up[None],
        grad_bup,
        grad_down[None],
        grad_bdown,
        grad_g2,
        grad_s2,
        grad_proj[None],
        loss[1, 0],
    )


def solution(mesh):
    return jax.shard_map(
        per_device,
        mesh=mesh,
        in_specs=(
            P("stream", "dp", None),
            P("stream", None, None),
            P("stream", None),
            P("stream", None, None),
            P("stream", None),
            P("stream", None),
            P("stream", None),
            P("stream", None, None),
            P("stream", None),
            P("stream", None, None),
            P("stream", None),
            P("stream", None),
            P("stream", None),
            P("stream", None, None),
            P(),
            P(),
            P("dp"),
        ),
        out_specs=(
            P(),
            P("stream", "dp", None),
            P("stream", None, None),
            P("stream", None),
            P("stream", None, None),
            P("stream", None),
            P("stream", None),
            P("stream", None),
            P("stream", None, None),
            P("stream", None),
            P("stream", None, None),
            P("stream", None),
            P("stream", None),
            P("stream", None),
            P("stream", None, None),
            P(),
        ),
        check_vma=False,
    )
```

time: 502 us -> 232 us (0.46)
  waiting for transfers between devices: 233 us -> 118 us
  blocking collectives: 104 us -> 0 us
  Pallas kernels: 0 us -> 64.4 us
  matrix products: 62.8 us -> 0 us
  local copies, waits for them, and re-layouts: 53 us -> 6.03 us
  starting transfers between devices: 5.71 us -> 32.1 us
  other arithmetic: 25.3 us -> 7.87 us
  between operations: 16.1 us -> 1.85 us
    psum x1 -> x0, waiting for transfers between devices: 133 us -> none  [per_device(): lax.psum((grad_qkv, grad_bqkv, grad_out, grad_bout, grad_gain1, grad_shif...]
    ppermute x3 -> x39, waiting for transfers between devices: 5.58 us -> 118 us  [swapped(): return lax.ppermute(value, axis, [(k, k ^ mask) for k in range(size)])]
    psum x2 -> x0, blocking collectives: 104 us -> none  [the longest x1 62.5 us: per_device(): lax.psum((grad_qkv, grad_bqkv, grad_out, grad_bout, grad_gain1, grad_shif...]
    pallas_call x0 -> x8, Pallas kernels: none -> 64.4 us  [the longest x6 43.1 us: call(): pl.pallas_call(kernel, out_shape=outs, in_specs=specs, out_specs=[VMEM] *...]
    reduce_scatter x1 -> x0, waiting for transfers between devices: 60.5 us -> none  [per_device(): doc_share = lax.psum_scatter(dd_all, 'dp', scatter_dimension=0, tiled=True)]
    dot_general x48 -> x0, matrix products: 59.5 us -> none  [the longest x17 13.9 us: inner_rows(): lax.dot_general(left_op, right_op, (((1,), (1,)), ((), ())), preferred_el...]
    all_gather x1 -> x0, waiting for transfers between devices: 34.3 us -> none  [per_device(): all_docs = lax.all_gather(docs_here, 'dp', axis=0, tiled=True)]
    ppermute x3 -> x39, starting transfers between devices: 5.14 us -> 32.1 us  [swapped(): return lax.ppermute(value, axis, [(k, k ^ mask) for k in range(size)])]
  transfers between devices with their start and end apart: 6 -> 39, of which waited for: 5 -> 28; matrix products, arithmetic and copies ran while one was open for 1% -> 3% of each run, Pallas kernels for 0% -> 13%
where the time goes in v1:
time: 232 us; the launch traced here: 231 us
  waiting for transfers between devices  118 us (51%)
  Pallas kernels  64.4 us (28%)
  starting transfers between devices  32.1 us (14%)
  other arithmetic  7.87 us (3%)
  local copies, waits for them, and re-layouts  6.03 us (3%)
    ppermute x39, waiting for transfers between devices, swapped(): return lax.ppermute(value, axis, [(k, k ^ mask) for k in range(size)])  118 us
    pallas_call x6, Pallas kernels, call(): pl.pallas_call(kernel, out_shape=outs, in_specs=specs, out_specs=[VMEM] *...  43.1 us
    ppermute x39, starting transfers between devices, swapped(): return lax.ppermute(value, axis, [(k, k ^ mask) for k in range(size)])  32.1 us
    pallas_call x2, Pallas kernels, spread_call(): pl.pallas_call(partial(spread_out, at_index, None), out_shape=jax.ShapeDt...  21.3 us
  transfers between devices with their start and end apart: 39, of which 28 were waited for; matrix products, arithmetic and copies ran while one was open for 3% of the time, Pallas kernels for 13%

profile of v1, /device:TPU:0, one launch (start us, length us, event | category | flops | bytes accessed | tf_op | source)
XLA Modules:
  0.0 230.5 jit_solution(6564020485303321916)
XLA Ops:
  0.7 1.4 copy.36.lens_ref
  2.7 10.4 %shard_map.297 = (bf16[272,128]{1,0:T(8,128)(2,1)}, bf16[256,1536]{1,0:T(8,128)(2,1)}, f32[256,256]{1,0:T(8,128)}, bf16[8,256,256]{2,1,0:T(8,128)(2,1)}, bf16[25...) custom-call(s32[8]{0:T(128)} %stack.36.where_ref, ...), custom_call_target="tpu_custom_call" | custom-call | bytes 1000000 | tf_op jit(solution)/shard_map/pallas_call | solution.py:627
  13.1 3.0 %collective-permute-start = (bf16[272,128]{1,0:T(8,128)(2,1)}, bf16[272,128]{1,0:T(8,128)(2,1)S(1)}, u32[]{:S(2)}, u32[]{:S(2)}) collective-permute-start(bf16[272,128]{1,0:T(8,128)(2,1)} %get-tuple-element.55), channel_id=1, source_target_pairs={{0,16},{16,0},{1,17},{17,1},{2,18},{18,2},{3,19},{19,3},{4,20},{20... | collective-permute-start | bytes 208904 | tf_op jit(solution)/shard_map/ppermute | solution.py:640
  16.1 2.5 %collective-permute-done = bf16[272,128]{1,0:T(8,128)(2,1)S(1)} collective-permute-done((bf16[272,128]{1,0:T(8,128)(2,1)}, bf16[272,128]{1,0:T(8,128)(2,1)S(1)}, u32[]{:S(2)}, u32[]{:S(2)}) %collective-permute-start) | collective-permute-done | bytes 69664 | tf_op jit(solution)/shard_map/ppermute | solution.py:640
  18.6 0.9 broadcast_select_fusion
  19.5 2.1 collective-permute-start.1
  22.5 2.7 %collective-permute-start.3 = (bf16[256,128]{1,0:T(8,128)(2,1)S(1)}, bf16[256,128]{1,0:T(8,128)(2,1)S(1)}, u32[]{:S(2)}, u32[]{:S(2)}) collective-permute-start(bf16[256,128]{1,0:T(8,128)(2,1)S(1)} %slice_select_fusion), channel_id=1, source_target_pairs={{0,8},{1,9},{2,10},{3,11},{4,12},{5,13},{6,14},{7,15},{8,0},{9,1},... | collective-permute-start | bytes 196616 | tf_op jit(solution)/shard_map/ppermute | solution.py:640
  25.2 2.5 %collective-permute-done.3 = bf16[256,128]{1,0:T(8,128)(2,1)S(1)} collective-permute-done((bf16[256,128]{1,0:T(8,128)(2,1)S(1)}, bf16[256,128]{1,0:T(8,128)(2,1)S(1)}, u32[]{:S(2)}, u32[]{:S(2)}) %collective-permute-start.3) | collective-permute-done | bytes 65568 | tf_op jit(solution)/shard_map/ppermute | solution.py:640
  27.7 1.7 collective-permute-start.4
  30.0 2.0 collective-permute-done.4.refs_1_
  32.7 3.9 %shard_map.298 = (f32[1024,128]{1,0:T(8,128)}, f32[32,128]{1,0:T(8,128)}, f32[32,128]{1,0:T(8,128)}, f32[32,128]{1,0:T(8,128)}) custom-call(s32[8]{0:T(128)} %stack.36.where_ref, f32[1]{0:T(128)} %bitcast.22.scale_ref, s32[16,5]{1,0:T(8,128)} %copy.36.lens_ref, bf16[544,128]{1,0:T(8,128)(2,1)} %copy-done.3, bf16[544,128]{1,0:T(8,128)(2,1)} %copy-done.8, ...), custom_call_target="tpu_custom_call" | custom-call | bytes 1000000 | tf_op jit(solution)/shard_map/pallas_call | solution.py:627
  36.6 1.4 collective-permute-done.5
  38.9 3.6 %collective-permute-done.6 = f32[32,128]{1,0:T(8,128)S(1)} collective-permute-done((f32[32,128]{1,0:T(8,128)S(1)}, f32[32,128]{1,0:T(8,128)S(1)}, u32[]{:S(2)}, u32[]{:S(2)}) %collective-permute-start.6) | collective-permute-done | bytes 16416 | tf_op jit(solution)/shard_map/ppermute | solution.py:640
  43.1 3.1 %collective-permute-done.7 = f32[32,128]{1,0:T(8,128)S(1)} collective-permute-done((f32[32,128]{1,0:T(8,128)S(1)}, f32[32,128]{1,0:T(8,128)S(1)}, u32[]{:S(2)}, u32[]{:S(2)}) %collective-permute-start.7) | collective-permute-done | bytes 16416 | tf_op jit(solution)/shard_map/ppermute | solution.py:640
  46.8 6.5 %shard_map.299 = (bf16[1024,128]{1,0:T(8,128)(2,1)}, bf16[512,128]{1,0:T(8,128)(2,1)}, f32[8,128]{1,0:T(8,128)}) custom-call(s32[8]{0:T(128)} %stack.36.where_ref, f32[1]{0:T(128)} %bitcast.23.scale_ref, s32[16,5]{1,0:T(8,128)} %copy.36.lens_ref, bf16[544,128]{1,0:T(8,128)(2,1)} %copy-done.3, bf16[544,128]{1,0:T(8,128)(2,1)} %copy-done.8, ...), custom_call_target="tpu_custom_call" | custom-call | bytes 1000000 | tf_op jit(solution)/shard_map/pallas_call | solution.py:627
  54.1 1.6 collective-permute-start.12
  55.7 0.9 slice.138
  56.7 1.7 collective-permute-done.12
  59.3 2.8 %collective-permute-start.13 = (bf16[256,128]{1,0:T(8,128)(2,1)S(1)}, bf16[256,128]{1,0:T(8,128)(2,1)S(1)}, u32[]{:S(2)}, u32[]{:S(2)}) collective-permute-start(bf16[256,128]{1,0:T(8,128)(2,1)S(1)} %add_convert_fusion.23), channel_id=1, source_target_pairs={{0,8},{1,9},{2,10},{3,11},{4,12},{5,13},{6,14},{7,15},{8,0},{9,1},... | collective-permute-start | bytes 196616 | tf_op jit(solution)/shard_map/ppermute | solution.py:640
  62.1 0.9 add_convert_fusion.21
  64.5 2.9 %collective-permute-done.11 = bf16[256,128]{1,0:T(8,128)(2,1)S(1)} collective-permute-done((bf16[256,128]{1,0:T(8,128)(2,1)S(1)}, bf16[256,128]{1,0:T(8,128)(2,1)S(1)}, u32[]{:S(2)}, u32[]{:S(2)}) %collective-permute-start.11) | collective-permute-done | bytes 65568 | tf_op jit(solution)/shard_map/ppermute | solution.py:640
  68.7 3.7 %collective-permute-done.14.got_ref = bf16[256,128]{1,0:T(8,128)(2,1)S(1)} collective-permute-done((bf16[256,128]{1,0:T(8,128)(2,1)S(1)}, bf16[256,128]{1,0:T(8,128)(2,1)S(1)}, u32[]{:S(2)}, u32[]{:S(2)}) %collective-permute-start.14) | collective-permute-done | bytes 65568 | tf_op jit(solution)/shard_map/ppermute | solution.py:640
  73.0 10.3 %shard_map.300 = (bf16[8,128,512]{2,1,0:T(8,128)(2,1)}, bf16[8,128,512]{2,1,0:T(8,128)(2,1)}, bf16[8,128,512]{2,1,0:T(8,128)(2,1)}, bf16[8,128,512]{2,1,0:T(8,12...) custom-call(s32[8]{0:T(128)} %stack.36.where_ref, bf16[256,128]{1,0:T(8,128)(2,1)} %get-tuple-element.96.dq_ref, ...), custom_call_target="tpu_custom_call" | custom-call | bytes 1000000 | tf_op jit(solution)/shard_map/pallas_call | solution.py:627
  83.8 8.0 %shard_map.301 = (bf16[8,144,512]{2,1,0:T(8,128)(2,1)}, bf16[8,144,512]{2,1,0:T(8,128)(2,1)}, f32[256,512]{1,0:T(8,128)}) custom-call(s32[8]{0:T(128)} %stack.36.where_ref, f32[256,512]{1,0:T(8,128)} %get-tuple-element.68.dfirst_ref, f32[256,512]{1,0:T(8,128)} %get-tuple-element.65.xh1_ref, f32[256,128]{1,0:T(8,128)} %get-tuple-element.69.rs1_ref, ...), custom_call_target="tpu_custom_call" | custom-call | bytes 1000000 | tf_op jit(solution)/shard_map/pallas_call | solution.py:627
  92.3 2.1 collective-permute-start.24
  96.0 1.2 collective-permute-start.16
  97.2 9.7 %collective-permute-done.24 = bf16[4,128,512]{2,1,0:T(8,128)(2,1)S(1)} collective-permute-done((bf16[4,128,512]{2,1,0:T(8,128)(2,1)S(1)}, bf16[4,128,512]{2,1,0:T(8,128)(2,1)S(1)}, u32[]{:S(2)}, u32[]{:S(2)}) %collective-permute-start.24) | collective-permute-done | bytes 524320 | tf_op jit(solution)/shard_map/ppermute | solution.py:640
  107.6 1.9 collective-permute-done.32
  110.5 11.6 %collective-permute-done.16 = bf16[4,144,512]{2,1,0:T(8,128)(2,1)S(1)} collective-permute-done((bf16[4,144,512]{2,1,0:T(8,128)(2,1)S(1)}, bf16[4,144,512]{2,1,0:T(8,128)(2,1)S(1)}, u32[]{:S(2)}, u32[]{:S(2)}) %collective-permute-start.16) | collective-permute-done | bytes 589856 | tf_op jit(solution)/shard_map/ppermute | solution.py:640
  123.2 3.8 %collective-permute-done.25 = bf16[2,128,512]{2,1,0:T(8,128)(2,1)S(1)} collective-permute-done((bf16[2,128,512]{2,1,0:T(8,128)(2,1)S(1)}, bf16[2,128,512]{2,1,0:T(8,128)(2,1)S(1)}, u32[]{:S(2)}, u32[]{:S(2)}) %collective-permute-start.25) | collective-permute-done | bytes 262176 | tf_op jit(solution)/shard_map/ppermute | solution.py:640
  127.2 3.0 %collective-permute-start.34 = (bf16[1,128,512]{2,1,0:T(8,128)(2,1)S(1)}, bf16[1,128,512]{2,1,0:T(8,128)(2,1)S(1)}, u32[]{:S(2)}, u32[]{:S(2)}) collective-permute-start(bf16[1,128,512]{2,1,0:T(8,128)(2,1)S(1)} %add_convert_fusion.16), channel_id=1, source_target_pairs={{0,8},{1,9},{2,10},{3,11},{4,12},{5,13},{6,14},{7,15},{8,0},{9,1},... | collective-permute-start | bytes 393224 | tf_op jit(solution)/shard_map/ppermute | solution.py:640
  130.8 11.8 %collective-permute-done.26 = bf16[1,128,512]{2,1,0:T(8,128)(2,1)S(1)} collective-permute-done((bf16[1,128,512]{2,1,0:T(8,128)(2,1)S(1)}, bf16[1,128,512]{2,1,0:T(8,128)(2,1)S(1)}, u32[]{:S(2)}, u32[]{:S(2)}) %collective-permute-start.26) | collective-permute-done | bytes 131104 | tf_op jit(solution)/shard_map/ppermute | solution.py:640
  142.7 8.6 %collective-permute-done.18 = bf16[1,144,512]{2,1,0:T(8,128)(2,1)S(1)} collective-permute-done((bf16[1,144,512]{2,1,0:T(8,128)(2,1)S(1)}, bf16[1,144,512]{2,1,0:T(8,128)(2,1)S(1)}, u32[]{:S(2)}, u32[]{:S(2)}) %collective-permute-start.18) | collective-permute-done | bytes 147488 | tf_op jit(solution)/shard_map/ppermute | solution.py:640
  151.5 3.0 %collective-permute-start.35 = (bf16[1,128,512]{2,1,0:T(8,128)(2,1)S(1)}, bf16[1,128,512]{2,1,0:T(8,128)(2,1)S(1)}, u32[]{:S(2)}, u32[]{:S(2)}) collective-permute-start(bf16[1,128,512]{2,1,0:T(8,128)(2,1)S(1)} %add_convert_fusion.15), channel_id=1, source_target_pairs={{0,8},{1,9},{2,10},{3,11},{4,12},{5,13},{6,14},{7,15},{8,0},{9,1},... | collective-permute-start | bytes 393224 | tf_op jit(solution)/shard_map/ppermute | solution.py:640
  154.5 5.5 %collective-permute-done.27 = bf16[1,128,512]{2,1,0:T(8,128)(2,1)S(1)} collective-permute-done((bf16[1,128,512]{2,1,0:T(8,128)(2,1)S(1)}, bf16[1,128,512]{2,1,0:T(8,128)(2,1)S(1)}, u32[]{:S(2)}, u32[]{:S(2)}) %collective-permute-start.27) | collective-permute-done | bytes 131104 | tf_op jit(solution)/shard_map/ppermute | solution.py:640
  160.6 2.6 %collective-permute-done.19 = bf16[1,144,512]{2,1,0:T(8,128)(2,1)S(1)} collective-permute-done((bf16[1,144,512]{2,1,0:T(8,128)(2,1)S(1)}, bf16[1,144,512]{2,1,0:T(8,128)(2,1)S(1)}, u32[]{:S(2)}, u32[]{:S(2)}) %collective-permute-start.19) | collective-permute-done | bytes 147488 | tf_op jit(solution)/shard_map/ppermute | solution.py:640
  163.3 1.8 collective-permute-done.35
  165.4 1.1 collective-permute-done.28
  167.4 5.9 %collective-permute-done.20 = bf16[2,144,512]{2,1,0:T(8,128)(2,1)S(1)} collective-permute-done((bf16[2,144,512]{2,1,0:T(8,128)(2,1)S(1)}, bf16[2,144,512]{2,1,0:T(8,128)(2,1)S(1)}, u32[]{:S(2)}, u32[]{:S(2)}) %collective-permute-start.20) | collective-permute-done | bytes 294944 | tf_op jit(solution)/shard_map/ppermute | solution.py:640
  173.9 5.0 %collective-permute-done.36 = bf16[2,128,512]{2,1,0:T(8,128)(2,1)S(1)} collective-permute-done((bf16[2,128,512]{2,1,0:T(8,128)(2,1)S(1)}, bf16[2,128,512]{2,1,0:T(8,128)(2,1)S(1)}, u32[]{:S(2)}, u32[]{:S(2)}) %collective-permute-start.36) | collective-permute-done | bytes 262176 | tf_op jit(solution)/shard_map/ppermute | solution.py:640
  179.5 8.7 %collective-permute-done.29 = bf16[4,128,512]{2,1,0:T(8,128)(2,1)S(1)} collective-permute-done((bf16[4,128,512]{2,1,0:T(8,128)(2,1)S(1)}, bf16[4,128,512]{2,1,0:T(8,128)(2,1)S(1)}, u32[]{:S(2)}, u32[]{:S(2)}) %collective-permute-start.29) | collective-permute-done | bytes 524320 | tf_op jit(solution)/shard_map/ppermute | solution.py:640
  188.4 1.2 collective-permute-done.21
  189.9 6.3 %collective-permute-done.37 = bf16[4,128,512]{2,1,0:T(8,128)(2,1)S(1)} collective-permute-done((bf16[4,128,512]{2,1,0:T(8,128)(2,1)S(1)}, bf16[4,128,512]{2,1,0:T(8,128)(2,1)S(1)}, u32[]{:S(2)}, u32[]{:S(2)}) %collective-permute-start.37) | collective-permute-done | bytes 524320 | tf_op jit(solution)/shard_map/ppermute | solution.py:640
  196.4 3.6 %collective-permute-done.8 = f32[8,128]{1,0:T(8,128)S(1)} collective-permute-done((f32[8,128]{1,0:T(8,128)S(1)}, f32[8,128]{1,0:T(8,128)S(1)}, u32[]{:S(2)}, u32[]{:S(2)}) %collective-permute-start.8) | collective-permute-done | bytes 4128 | tf_op jit(solution)/shard_map/ppermute | solution.py:640
  200.0 4.5 %collective-permute-done.9 = f32[8,128]{1,0:T(8,128)S(1)} collective-permute-done((f32[8,128]{1,0:T(8,128)S(1)}, f32[8,128]{1,0:T(8,128)S(1)}, u32[]{:S(2)}, u32[]{:S(2)}) %collective-permute-start.9) | collective-permute-done | bytes 4128 | tf_op jit(solution)/shard_map/ppermute | solution.py:640
  205.1 10.7 %shard_map.303 = f32[512,2048]{1,0:T(8,128)} custom-call(s32[8]{0:T(128)} %stack.36.where_ref, bf16[8,128,512]{2,1,0:T(8,128)(2,1)} %copy-done.1, bf16[8,128,512]{2,1,0:T(8,128)(2,1)} %collective-permute-done.30.far_ref), custom_call_target="tpu_custom_call" | custom-call | tf_op jit(solution)/shard_map/pallas_call | solution.py:576
  215.7 10.7 %shard_map.304 = f32[2048,512]{1,0:T(8,128)} custom-call(s32[8]{0:T(128)} %stack.36.where_ref, bf16[8,128,512]{2,1,0:T(8,128)(2,1)} %copy-done.2, bf16[8,128,512]{2,1,0:T(8,128)(2,1)} %collective-permute-done.38.far_ref), custom_call_target="tpu_custom_call" | custom-call | tf_op jit(solution)/shard_map/pallas_call | solution.py:576
  226.4 4.0 %shard_map.302 = (f32[512,1536]{1,0:T(8,128)}, f32[512,512]{1,0:T(8,128)}, f32[512,128]{1,0:T(8,128)}, f32[1,1536]{1,0:T(1,128)}, f32[1,512]{1,0:T(1,128)}, /*in...) custom-call(s32[8]{0:T(128)} %stack.36.where_ref, ...), custom_call_target="tpu_custom_call" | custom-call | bytes 1000000 | tf_op jit(solution)/shard_map/pallas_call | solution.py:627
  (101 shorter events, 20.3 us)
Async XLA Ops:
  13.1 5.5 %collective-permute-start = (bf16[272,128]{1,0:T(8,128)(2,1)}, bf16[272,128]{1,0:T(8,128)(2,1)S(1)}, u32[]{:S(2)}, u32[]{:S(2)}) collective-permute-start(bf16[272,128]{1,0:T(8,128)(2,1)} %get-tuple-element.55), channel_id=1, source_target_pairs={{0,16},{16,0},{1,17},{17,1},{2,18},{18,2},{3,19},{19,3},{4,20},{20... | collective-permute-start | bytes 208904 | tf_op jit(solution)/shard_map/ppermute | solution.py:640
  19.5 5.6 %collective-permute-start.1 = (bf16[272,128]{1,0:T(8,128)(2,1)S(1)}, bf16[272,128]{1,0:T(8,128)(2,1)S(1)}, u32[]{:S(2)}, u32[]{:S(2)}) collective-permute-start(bf16[272,128]{1,0:T(8,128)(2,1)S(1)} %broadcast_select_fusion), channel_id=1, source_target_pairs={{0,2},{1,3},{2,0},{3,1},{4,6},{5,7},{6,4},{7,5},{8,10},{9,11},{10,... | collective-permute-start | bytes 208904 | tf_op jit(solution)/shard_map/ppermute | solution.py:640
  22.5 5.2 %collective-permute-start.3 = (bf16[256,128]{1,0:T(8,128)(2,1)S(1)}, bf16[256,128]{1,0:T(8,128)(2,1)S(1)}, u32[]{:S(2)}, u32[]{:S(2)}) collective-permute-start(bf16[256,128]{1,0:T(8,128)(2,1)S(1)} %slice_select_fusion), channel_id=1, source_target_pairs={{0,8},{1,9},{2,10},{3,11},{4,12},{5,13},{6,14},{7,15},{8,0},{9,1},... | collective-permute-start | bytes 196616 | tf_op jit(solution)/shard_map/ppermute | solution.py:640
  25.1 6.9 %copy-start.3 = (bf16[544,128]{1,0:T(8,128)(2,1)}, bf16[544,128]{1,0:T(8,128)(2,1)S(1)}, u32[]{:S(2)}) copy-start(bf16[544,128]{1,0:T(8,128)(2,1)S(1)} %pad_maximum_fusion.9.near_ref) | copy-start | bytes 417796
  25.1 6.9 %collective-permute-start.2 = (bf16[544,128]{1,0:T(8,128)(2,1)S(1)}, bf16[544,128]{1,0:T(8,128)(2,1)S(1)}, u32[]{:S(2)}, u32[]{:S(2)}) collective-permute-start(bf16[544,128]{1,0:T(8,128)(2,1)S(1)} %pad_maximum_fusion.9.near_ref), channel_id=1, source_target_pairs={{0,1},{1,0},{2,3},{3,2},{4,5},{5,4},{6,7},{7,6},{8,9},{9,8},{10,11... | collective-permute-start | bytes 417800 | tf_op jit(solution)/shard_map/ppermute | solution.py:640
  27.7 4.4 %copy-start.7 = (bf16[256,128]{1,0:T(8,128)(2,1)}, bf16[256,128]{1,0:T(8,128)(2,1)S(1)}, u32[]{:S(2)}) copy-start(bf16[256,128]{1,0:T(8,128)(2,1)S(1)} %broadcast_select_fusion.2.refs_0_) | copy-start | bytes 196612
  27.7 4.3 %collective-permute-start.4 = (bf16[256,128]{1,0:T(8,128)(2,1)S(1)}, bf16[256,128]{1,0:T(8,128)(2,1)S(1)}, u32[]{:S(2)}, u32[]{:S(2)}) collective-permute-start(bf16[256,128]{1,0:T(8,128)(2,1)S(1)} %broadcast_select_fusion.2.refs_0_), channel_id=1, source_target_pairs={{0,4},{1,5},{2,6},{3,7},{4,0},{5,1},{6,2},{7,3},{8,12},{9,13},{10,... | collective-permute-start | bytes 196616 | tf_op jit(solution)/shard_map/ppermute | solution.py:640
  36.6 1.4 collective-permute-start.5
  38.7 3.7 %collective-permute-start.6 = (f32[32,128]{1,0:T(8,128)S(1)}, f32[32,128]{1,0:T(8,128)S(1)}, u32[]{:S(2)}, u32[]{:S(2)}) collective-permute-start(f32[32,128]{1,0:T(8,128)S(1)} %add.94), channel_id=1, source_target_pairs={{0,2},{1,3},{2,0},{3,1},{4,6},{5,7},{6,4},{7,5},{8,10},{9,11},{10,... | collective-permute-start | bytes 49160 | tf_op jit(solution)/shard_map/ppermute | solution.py:640
  42.5 3.7 %collective-permute-start.7 = (f32[32,128]{1,0:T(8,128)S(1)}, f32[32,128]{1,0:T(8,128)S(1)}, u32[]{:S(2)}, u32[]{:S(2)}) collective-permute-start(f32[32,128]{1,0:T(8,128)S(1)} %add.95), channel_id=1, source_target_pairs={{0,16},{16,0},{1,17},{17,1},{2,18},{18,2},{3,19},{19,3},{4,20},{20... | collective-permute-start | bytes 49160 | tf_op jit(solution)/shard_map/ppermute | solution.py:640
  54.1 4.3 %collective-permute-start.12 = (bf16[256,128]{1,0:T(8,128)(2,1)S(1)}, bf16[256,128]{1,0:T(8,128)(2,1)S(1)}, u32[]{:S(2)}, u32[]{:S(2)}) collective-permute-start(bf16[256,128]{1,0:T(8,128)(2,1)S(1)} %slice.142), channel_id=1, source_target_pairs={{0,4},{1,5},{2,6},{3,7},{4,0},{5,1},{6,2},{7,3},{8,12},{9,13},{10,... | collective-permute-start | bytes 196616 | tf_op jit(solution)/shard_map/ppermute | solution.py:640
  56.6 5.4 %collective-permute-start.10 = (bf16[512,128]{1,0:T(8,128)(2,1)S(1)}, bf16[512,128]{1,0:T(8,128)(2,1)S(1)}, u32[]{:S(2)}, u32[]{:S(2)}) collective-permute-start(bf16[512,128]{1,0:T(8,128)(2,1)S(1)} %slice.138), channel_id=1, source_target_pairs={{0,1},{1,0},{2,3},{3,2},{4,5},{5,4},{6,7},{7,6},{8,9},{9,8},{10,11... | collective-permute-start | bytes 393224 | tf_op jit(solution)/shard_map/ppermute | solution.py:640
  59.3 5.2 %collective-permute-start.13 = (bf16[256,128]{1,0:T(8,128)(2,1)S(1)}, bf16[256,128]{1,0:T(8,128)(2,1)S(1)}, u32[]{:S(2)}, u32[]{:S(2)}) collective-permute-start(bf16[256,128]{1,0:T(8,128)(2,1)S(1)} %add_convert_fusion.23), channel_id=1, source_target_pairs={{0,8},{1,9},{2,10},{3,11},{4,12},{5,13},{6,14},{7,15},{8,0},{9,1},... | collective-permute-start | bytes 196616 | tf_op jit(solution)/shard_map/ppermute | solution.py:640
  63.0 4.3 %collective-permute-start.11 = (bf16[256,128]{1,0:T(8,128)(2,1)S(1)}, bf16[256,128]{1,0:T(8,128)(2,1)S(1)}, u32[]{:S(2)}, u32[]{:S(2)}) collective-permute-start(bf16[256,128]{1,0:T(8,128)(2,1)S(1)} %slice.183), channel_id=1, source_target_pairs={{0,2},{1,3},{2,0},{3,1},{4,6},{5,7},{6,4},{7,5},{8,10},{9,11},{10,... | collective-permute-start | bytes 196616 | tf_op jit(solution)/shard_map/ppermute | solution.py:640
  68.1 4.3 %collective-permute-start.14 = (bf16[256,128]{1,0:T(8,128)(2,1)S(1)}, bf16[256,128]{1,0:T(8,128)(2,1)S(1)}, u32[]{:S(2)}, u32[]{:S(2)}) collective-permute-start(bf16[256,128]{1,0:T(8,128)(2,1)S(1)} %get-tuple-element.94), channel_id=1, source_target_pairs={{0,16},{16,0},{1,17},{17,1},{2,18},{18,2},{3,19},{19,3},{4,20},{20... | collective-permute-start | bytes 196616 | tf_op jit(solution)/shard_map/ppermute | solution.py:640
  83.3 8.7 %collective-permute-start.23 = (bf16[8,128,512]{2,1,0:T(8,128)(2,1)}, bf16[8,128,512]{2,1,0:T(8,128)(2,1)S(1)}, u32[]{:S(2)}, u32[]{:S(2)}) collective-permute-start(bf16[8,128,512]{2,1,0:T(8,128)(2,1)} %get-tuple-element.86), channel_id=1, source_target_pairs={{0,1},{1,0},{2,3},{3,2},{4,5},{5,4},{6,7},{7,6},{8,9},{9,8},{10,11... | collective-permute-start | bytes 3145736 | tf_op jit(solution)/shard_map/ppermute | solution.py:640
  83.3 11.0 %collective-permute-start.31 = (bf16[8,128,512]{2,1,0:T(8,128)(2,1)}, bf16[8,128,512]{2,1,0:T(8,128)(2,1)S(1)}, u32[]{:S(2)}, u32[]{:S(2)}) collective-permute-start(bf16[8,128,512]{2,1,0:T(8,128)(2,1)} %get-tuple-element.89), channel_id=1, source_target_pairs={{0,1},{1,0},{2,3},{3,2},{4,5},{5,4},{6,7},{7,6},{8,9},{9,8},{10,11... | collective-permute-start | bytes 3145736 | tf_op jit(solution)/shard_map/ppermute | solution.py:640
  83.8 8.1 %copy-start.6 = (bf16[8,128,512]{2,1,0:T(8,128)(2,1)S(1)}, bf16[8,128,512]{2,1,0:T(8,128)(2,1)}, u32[]{:S(2)}) copy-start(bf16[8,128,512]{2,1,0:T(8,128)(2,1)} %get-tuple-element.85) | copy-start | bytes 3145732
  91.9 3.4 %collective-permute-start.15 = (bf16[8,144,512]{2,1,0:T(8,128)(2,1)}, bf16[8,144,512]{2,1,0:T(8,128)(2,1)S(1)}, u32[]{:S(2)}, u32[]{:S(2)}) collective-permute-start(bf16[8,144,512]{2,1,0:T(8,128)(2,1)} %get-tuple-element.78), channel_id=1, source_target_pairs={{0,1},{1,0},{2,3},{3,2},{4,5},{5,4},{6,7},{7,6},{8,9},{9,8},{10,11... | collective-permute-start | bytes 3538952 | tf_op jit(solution)/shard_map/ppermute | solution.py:640
  92.0 2.4 %copy-start.5 = (bf16[8,128,512]{2,1,0:T(8,128)(2,1)S(1)}, bf16[8,128,512]{2,1,0:T(8,128)(2,1)}, u32[]{:S(2)}) copy-start(bf16[8,128,512]{2,1,0:T(8,128)(2,1)} %get-tuple-element.88) | copy-start | bytes 3145732
  92.3 14.6 %collective-permute-start.24 = (bf16[4,128,512]{2,1,0:T(8,128)(2,1)S(1)}, bf16[4,128,512]{2,1,0:T(8,128)(2,1)S(1)}, u32[]{:S(2)}, u32[]{:S(2)}) collective-permute-start(bf16[4,128,512]{2,1,0:T(8,128)(2,1)S(1)} %get-tuple-element.102), channel_id=1, source_target_pairs={{0,4},{1,5},{2,6},{3,7},{4,0},{5,1},{6,2},{7,3},{8,12},{9,13},{10,... | collective-permute-start | bytes 1572872 | tf_op jit(solution)/shard_map/ppermute | solution.py:640
  94.4 1.3 copy-start.4
  94.7 14.8 %collective-permute-start.32 = (bf16[4,128,512]{2,1,0:T(8,128)(2,1)S(1)}, bf16[4,128,512]{2,1,0:T(8,128)(2,1)S(1)}, u32[]{:S(2)}, u32[]{:S(2)}) collective-permute-start(bf16[4,128,512]{2,1,0:T(8,128)(2,1)S(1)} %get-tuple-element.100), channel_id=1, source_target_pairs={{0,2},{1,3},{2,0},{3,1},{4,6},{5,7},{6,4},{7,5},{8,10},{9,11},{10,... | collective-permute-start | bytes 1572872 | tf_op jit(solution)/shard_map/ppermute | solution.py:640
  96.0 26.1 %collective-permute-start.16 = (bf16[4,144,512]{2,1,0:T(8,128)(2,1)S(1)}, bf16[4,144,512]{2,1,0:T(8,128)(2,1)S(1)}, u32[]{:S(2)}, u32[]{:S(2)}) collective-permute-start(bf16[4,144,512]{2,1,0:T(8,128)(2,1)S(1)} %get-tuple-element.98), channel_id=1, source_target_pairs={{0,2},{1,3},{2,0},{3,1},{4,6},{5,7},{6,4},{7,5},{8,10},{9,11},{10,... | collective-permute-start | bytes 1769480 | tf_op jit(solution)/shard_map/ppermute | solution.py:640
  107.0 20.0 %collective-permute-start.25 = (bf16[2,128,512]{2,1,0:T(8,128)(2,1)S(1)}, bf16[2,128,512]{2,1,0:T(8,128)(2,1)S(1)}, u32[]{:S(2)}, u32[]{:S(2)}) collective-permute-start(bf16[2,128,512]{2,1,0:T(8,128)(2,1)S(1)} %get-tuple-element.108), channel_id=1, source_target_pairs={{0,2},{1,3},{2,0},{3,1},{4,6},{5,7},{6,4},{7,5},{8,10},{9,11},{10,... | collective-permute-start | bytes 786440 | tf_op jit(solution)/shard_map/ppermute | solution.py:640
  109.6 17.5 %collective-permute-start.33 = (bf16[2,128,512]{2,1,0:T(8,128)(2,1)S(1)}, bf16[2,128,512]{2,1,0:T(8,128)(2,1)S(1)}, u32[]{:S(2)}, u32[]{:S(2)}) collective-permute-start(bf16[2,128,512]{2,1,0:T(8,128)(2,1)S(1)} %get-tuple-element.106), channel_id=1, source_target_pairs={{0,4},{1,5},{2,6},{3,7},{4,0},{5,1},{6,2},{7,3},{8,12},{9,13},{10,... | collective-permute-start | bytes 786440 | tf_op jit(solution)/shard_map/ppermute | solution.py:640
  122.3 8.3 %collective-permute-start.17 = (bf16[2,144,512]{2,1,0:T(8,128)(2,1)S(1)}, bf16[2,144,512]{2,1,0:T(8,128)(2,1)S(1)}, u32[]{:S(2)}, u32[]{:S(2)}) collective-permute-start(bf16[2,144,512]{2,1,0:T(8,128)(2,1)S(1)} %get-tuple-element.104), channel_id=1, source_target_pairs={{0,4},{1,5},{2,6},{3,7},{4,0},{5,1},{6,2},{7,3},{8,12},{9,13},{10,... | collective-permute-start | bytes 884744 | tf_op jit(solution)/shard_map/ppermute | solution.py:640
  127.0 15.5 %collective-permute-start.26 = (bf16[1,128,512]{2,1,0:T(8,128)(2,1)S(1)}, bf16[1,128,512]{2,1,0:T(8,128)(2,1)S(1)}, u32[]{:S(2)}, u32[]{:S(2)}) collective-permute-start(bf16[1,128,512]{2,1,0:T(8,128)(2,1)S(1)} %add_convert_fusion.19), channel_id=1, source_target_pairs={{0,8},{1,9},{2,10},{3,11},{4,12},{5,13},{6,14},{7,15},{8,0},{9,1},... | collective-permute-start | bytes 393224 | tf_op jit(solution)/shard_map/ppermute | solution.py:640
  127.2 24.3 %collective-permute-start.34 = (bf16[1,128,512]{2,1,0:T(8,128)(2,1)S(1)}, bf16[1,128,512]{2,1,0:T(8,128)(2,1)S(1)}, u32[]{:S(2)}, u32[]{:S(2)}) collective-permute-start(bf16[1,128,512]{2,1,0:T(8,128)(2,1)S(1)} %add_convert_fusion.16), channel_id=1, source_target_pairs={{0,8},{1,9},{2,10},{3,11},{4,12},{5,13},{6,14},{7,15},{8,0},{9,1},... | collective-permute-start | bytes 393224 | tf_op jit(solution)/shard_map/ppermute | solution.py:640
  130.7 20.6 %collective-permute-start.18 = (bf16[1,144,512]{2,1,0:T(8,128)(2,1)S(1)}, bf16[1,144,512]{2,1,0:T(8,128)(2,1)S(1)}, u32[]{:S(2)}, u32[]{:S(2)}) collective-permute-start(bf16[1,144,512]{2,1,0:T(8,128)(2,1)S(1)} %add_convert_fusion.13), channel_id=1, source_target_pairs={{0,8},{1,9},{2,10},{3,11},{4,12},{5,13},{6,14},{7,15},{8,0},{9,1},... | collective-permute-start | bytes 442376 | tf_op jit(solution)/shard_map/ppermute | solution.py:640
  142.6 17.4 %collective-permute-start.27 = (bf16[1,128,512]{2,1,0:T(8,128)(2,1)S(1)}, bf16[1,128,512]{2,1,0:T(8,128)(2,1)S(1)}, u32[]{:S(2)}, u32[]{:S(2)}) collective-permute-start(bf16[1,128,512]{2,1,0:T(8,128)(2,1)S(1)} %add_convert_fusion.18), channel_id=1, source_target_pairs={{0,8},{1,9},{2,10},{3,11},{4,12},{5,13},{6,14},{7,15},{8,0},{9,1},... | collective-permute-start | bytes 393224 | tf_op jit(solution)/shard_map/ppermute | solution.py:640
  151.4 11.8 %collective-permute-start.19 = (bf16[1,144,512]{2,1,0:T(8,128)(2,1)S(1)}, bf16[1,144,512]{2,1,0:T(8,128)(2,1)S(1)}, u32[]{:S(2)}, u32[]{:S(2)}) collective-permute-start(bf16[1,144,512]{2,1,0:T(8,128)(2,1)S(1)} %add_convert_fusion.12), channel_id=1, source_target_pairs={{0,8},{1,9},{2,10},{3,11},{4,12},{5,13},{6,14},{7,15},{8,0},{9,1},... | collective-permute-start | bytes 442376 | tf_op jit(solution)/shard_map/ppermute | solution.py:640
  151.5 13.6 %collective-permute-start.35 = (bf16[1,128,512]{2,1,0:T(8,128)(2,1)S(1)}, bf16[1,128,512]{2,1,0:T(8,128)(2,1)S(1)}, u32[]{:S(2)}, u32[]{:S(2)}) collective-permute-start(bf16[1,128,512]{2,1,0:T(8,128)(2,1)S(1)} %add_convert_fusion.15), channel_id=1, source_target_pairs={{0,8},{1,9},{2,10},{3,11},{4,12},{5,13},{6,14},{7,15},{8,0},{9,1},... | collective-permute-start | bytes 393224 | tf_op jit(solution)/shard_map/ppermute | solution.py:640
  160.1 6.4 %collective-permute-start.28 = (bf16[2,128,512]{2,1,0:T(8,128)(2,1)S(1)}, bf16[2,128,512]{2,1,0:T(8,128)(2,1)S(1)}, u32[]{:S(2)}, u32[]{:S(2)}) collective-permute-start(bf16[2,128,512]{2,1,0:T(8,128)(2,1)S(1)} %pad_maximum_fusion.7), channel_id=1, source_target_pairs={{0,2},{1,3},{2,0},{3,1},{4,6},{5,7},{6,4},{7,5},{8,10},{9,11},{10,... | collective-permute-start | bytes 786440 | tf_op jit(solution)/shard_map/ppermute | solution.py:640
  163.2 10.0 %collective-permute-start.20 = (bf16[2,144,512]{2,1,0:T(8,128)(2,1)S(1)}, bf16[2,144,512]{2,1,0:T(8,128)(2,1)S(1)}, u32[]{:S(2)}, u32[]{:S(2)}) collective-permute-start(bf16[2,144,512]{2,1,0:T(8,128)(2,1)S(1)} %pad_maximum_fusion.6), channel_id=1, source_target_pairs={{0,4},{1,5},{2,6},{3,7},{4,0},{5,1},{6,2},{7,3},{8,12},{9,13},{10,... | collective-permute-start | bytes 884744 | tf_op jit(solution)/shard_map/ppermute | solution.py:640
  165.2 13.7 %collective-permute-start.36 = (bf16[2,128,512]{2,1,0:T(8,128)(2,1)S(1)}, bf16[2,128,512]{2,1,0:T(8,128)(2,1)S(1)}, u32[]{:S(2)}, u32[]{:S(2)}) collective-permute-start(bf16[2,128,512]{2,1,0:T(8,128)(2,1)S(1)} %pad_maximum_fusion.8), channel_id=1, source_target_pairs={{0,4},{1,5},{2,6},{3,7},{4,0},{5,1},{6,2},{7,3},{8,12},{9,13},{10,... | collective-permute-start | bytes 786440 | tf_op jit(solution)/shard_map/ppermute | solution.py:640
  166.6 21.6 %collective-permute-start.29 = (bf16[4,128,512]{2,1,0:T(8,128)(2,1)S(1)}, bf16[4,128,512]{2,1,0:T(8,128)(2,1)S(1)}, u32[]{:S(2)}, u32[]{:S(2)}) collective-permute-start(bf16[4,128,512]{2,1,0:T(8,128)(2,1)S(1)} %pad_maximum_fusion.4), channel_id=1, source_target_pairs={{0,4},{1,5},{2,6},{3,7},{4,0},{5,1},{6,2},{7,3},{8,12},{9,13},{10,... | collective-permute-start | bytes 1572872 | tf_op jit(solution)/shard_map/ppermute | solution.py:640
  173.3 16.3 %collective-permute-start.21 = (bf16[4,144,512]{2,1,0:T(8,128)(2,1)S(1)}, bf16[4,144,512]{2,1,0:T(8,128)(2,1)S(1)}, u32[]{:S(2)}, u32[]{:S(2)}) collective-permute-start(bf16[4,144,512]{2,1,0:T(8,128)(2,1)S(1)} %pad_maximum_fusion.3), channel_id=1, source_target_pairs={{0,2},{1,3},{2,0},{3,1},{4,6},{5,7},{6,4},{7,5},{8,10},{9,11},{10,... | collective-permute-start | bytes 1769480 | tf_op jit(solution)/shard_map/ppermute | solution.py:640
  178.9 17.2 %collective-permute-start.37 = (bf16[4,128,512]{2,1,0:T(8,128)(2,1)S(1)}, bf16[4,128,512]{2,1,0:T(8,128)(2,1)S(1)}, u32[]{:S(2)}, u32[]{:S(2)}) collective-permute-start(bf16[4,128,512]{2,1,0:T(8,128)(2,1)S(1)} %pad_maximum_fusion.5), channel_id=1, source_target_pairs={{0,2},{1,3},{2,0},{3,1},{4,6},{5,7},{6,4},{7,5},{8,10},{9,11},{10,... | collective-permute-start | bytes 1572872 | tf_op jit(solution)/shard_map/ppermute | solution.py:640
  188.3 1.5 copy-start.1
  188.3 16.7 %collective-permute-start.30 = (bf16[8,128,512]{2,1,0:T(8,128)(2,1)S(1)}, bf16[8,128,512]{2,1,0:T(8,128)(2,1)}, u32[]{:S(2)}, u32[]{:S(2)}) collective-permute-start(bf16[8,128,512]{2,1,0:T(8,128)(2,1)S(1)} %pad_maximum_fusion.1.near_ref), channel_id=1, source_target_pairs={{0,1},{1,0},{2,3},{3,2},{4,5},{5,4},{6,7},{7,6},{8,9},{9,8},{10,11... | collective-permute-start | bytes 3145736 | tf_op jit(solution)/shard_map/ppermute | solution.py:640
  189.8 26.0 %copy-start = (bf16[8,144,512]{2,1,0:T(8,128)(2,1)}, bf16[8,144,512]{2,1,0:T(8,128)(2,1)S(1)}, u32[]{:S(2)}) copy-start(bf16[8,144,512]{2,1,0:T(8,128)(2,1)S(1)} %pad_maximum_fusion.near_ref) | copy-start | bytes 3538948
  189.8 6.6 %copy-start.11 = (f32[8,128]{1,0:T(8,128)S(1)}, f32[8,128]{1,0:T(8,128)}, u32[]{:S(2)}) copy-start(f32[8,128]{1,0:T(8,128)} %get-tuple-element.60) | copy-start | bytes 12292
  189.8 36.6 %collective-permute-start.22 = (bf16[8,144,512]{2,1,0:T(8,128)(2,1)S(1)}, bf16[8,144,512]{2,1,0:T(8,128)(2,1)}, u32[]{:S(2)}, u32[]{:S(2)}) collective-permute-start(bf16[8,144,512]{2,1,0:T(8,128)(2,1)S(1)} %pad_maximum_fusion.near_ref), channel_id=1, source_target_pairs={{0,1},{1,0},{2,3},{3,2},{4,5},{5,4},{6,7},{7,6},{8,9},{9,8},{10,11... | collective-permute-start | bytes 3538952 | tf_op jit(solution)/shard_map/ppermute | solution.py:640
  196.3 19.5 %copy-start.2 = (bf16[8,128,512]{2,1,0:T(8,128)(2,1)}, bf16[8,128,512]{2,1,0:T(8,128)(2,1)S(1)}, u32[]{:S(2)}) copy-start(bf16[8,128,512]{2,1,0:T(8,128)(2,1)S(1)} %pad_maximum_fusion.2.near_ref) | copy-start | bytes 3145732
  196.3 19.5 %collective-permute-start.38 = (bf16[8,128,512]{2,1,0:T(8,128)(2,1)S(1)}, bf16[8,128,512]{2,1,0:T(8,128)(2,1)}, u32[]{:S(2)}, u32[]{:S(2)}) collective-permute-start(bf16[8,128,512]{2,1,0:T(8,128)(2,1)S(1)} %pad_maximum_fusion.2.near_ref), channel_id=1, source_target_pairs={{0,1},{1,0},{2,3},{3,2},{4,5},{5,4},{6,7},{7,6},{8,9},{9,8},{10,11... | collective-permute-start | bytes 3145736 | tf_op jit(solution)/shard_map/ppermute | solution.py:640
  196.4 3.7 %collective-permute-start.8 = (f32[8,128]{1,0:T(8,128)S(1)}, f32[8,128]{1,0:T(8,128)S(1)}, u32[]{:S(2)}, u32[]{:S(2)}) collective-permute-start(f32[8,128]{1,0:T(8,128)S(1)} %copy-done.11), channel_id=1, source_target_pairs={{0,4},{1,5},{2,6},{3,7},{4,0},{5,1},{6,2},{7,3},{8,12},{9,13},{10,... | collective-permute-start | bytes 12296 | tf_op jit(solution)/shard_map/ppermute | solution.py:640
  200.0 4.5 %collective-permute-start.9 = (f32[8,128]{1,0:T(8,128)S(1)}, f32[8,128]{1,0:T(8,128)S(1)}, u32[]{:S(2)}, u32[]{:S(2)}) collective-permute-start(f32[8,128]{1,0:T(8,128)S(1)} %add.97), channel_id=1, source_target_pairs={{0,8},{1,9},{2,10},{3,11},{4,12},{5,13},{6,14},{7,15},{8,0},{9,1},... | collective-permute-start | bytes 12296 | tf_op jit(solution)/shard_map/ppermute | solution.py:640
  (3 other events, 1.9 us)

commit v2 on v1

--- a/solution.py
+++ b/solution.py
@@ -28,7 +28,9 @@
 F32 = jnp.float32
 BF16 = jnp.bfloat16
 REST = 2304
-VLIMIT = 56 * 1024 * 1024
+FINAL = ((0,), (1,), (2, 3))
+ORDER = [4, 2, 3, 0, 1, 2, 3, 2, 4, 3, 0, 2, 1, 3, 0, 2, 1, 3, 4, 2, 0, 3, 1, 2, 0, 2, 1, 3, 0, 3, 12, 1, 0, 1, 0, 10, 1, 11]
+MIB = 1024 * 1024
 
 VMEM = pl.BlockSpec(memory_space=pltpu.VMEM)
 SMEM = pl.BlockSpec(memory_space=pltpu.SMEM)
@@ -410,17 +412,19 @@
         dd_ref[p * ROW : (p + 1) * ROW, :] = total[:, p * ROW : (p + 1) * ROW].T.astype(BF16)
 
 
-def store_block(refs, at, value):
+def store_block(refs, block, places, value):
     keep_ref, send_ref = refs
+    core, near_place, far_place = places
     half = keep_ref.shape[0]
-
-    @pl.when(at < half)
+    mine = core == block // half
+
+    @pl.when(mine)
     def _():
-        keep_ref[at] = value
-
-    @pl.when(at >= half)
+        keep_ref[(block % half) ^ near_place] = value
+
+    @pl.when(jnp.logical_not(mine))
     def _():
-        send_ref[at - half] = value
+        send_ref[(block % half) ^ far_place] = value
 
 
 def feed_back(
@@ -429,7 +433,7 @@
     down_keep, down_send, up_keep, up_send, dfirst_ref, gproj_ref, small_ref, dinner_ref,
 ):
     is_query, docs_there = where_ref[1] == 0, where_ref[4] == 0
-    down_at, up_at = where_ref[5], where_ref[6]
+    places = (where_ref[5], where_ref[6], where_ref[7])
     got = got_ref[...].astype(F32)
     d_vec = jnp.where(
         is_query,
@@ -462,7 +466,8 @@
         for k in range(step // size):
             store_block(
                 (down_keep, down_send),
-                (c * (step // size) + k) ^ down_at,
+                c * (step // size) + k,
+                places,
                 grad[k * size : (k + 1) * size, :],
             )
         d_first = d_first + mm_nt(d_inner, wup_ref[:, cols])
@@ -474,7 +479,8 @@
         for k in range(D // size):
             store_block(
                 (up_keep, up_send),
-                (c * (D // size) + k) ^ up_at,
+                c * (D // size) + k,
+                places,
                 grad[k * size : (k + 1) * size, :],
             )
 
@@ -482,9 +488,9 @@
 def attend_back(
     where_ref, dfirst_ref, xh1_ref, rs1_ref, g1_ref, mixed_ref, wout_ref, qkv_ref, probs_ref,
     rope_ref, x_ref, wqkv_ref, gproj_ref, small_ref,
-    keep_ref, send_ref, tokens_ref, djoined_ref, rest_ref,
+    keep_one, send_one, keep_two, send_two, tokens_ref, djoined_ref, rest_ref,
 ):
-    at = where_ref[7]
+    core, near_place, far_place = where_ref[5], where_ref[6], where_ref[7]
     d_first = dfirst_ref[...]
     xhat = xh1_ref[...]
     gain = g1_ref[...].astype(F32)
@@ -493,7 +499,7 @@
     d_sum = norm_back(d_first, xhat, rs1_ref[:, :1], gain)
     d_att = d_sum.astype(BF16)
     bias_out = col_sum(d_att.astype(F32))
-    rest_ref[3 * D : 4 * D, :] = mm_tn(mixed_ref[...], d_att).astype(BF16)
+    rest_ref[3 * D : 4 * D, :] = mm_tn(mixed_ref[...], d_att)
     d_mixed = mm_nt(d_att, wout_ref[...]).astype(BF16)
     cosine, sine = rope_ref[:, :128], rope_ref[:, 128:]
     low_half = iota((ROW, 128), 1) < HD
@@ -528,84 +534,67 @@
         djoined_ref[:, 2 * D + g * 128 : 2 * D + (g + 1) * 128] = d_v.astype(BF16)
     x = x_ref[...]
     tokens = d_sum
-    rest_ref[4 * D + 128 :, :] = jnp.zeros((REST - 4 * D - 128, D), BF16)
+    rest_ref[4 * D + 128 :, :] = jnp.zeros((REST - 4 * D - 128, D), F32)
     smalls = []
     for c in range(3):
         cols = slice(c * D, (c + 1) * D)
         d_part = djoined_ref[:, cols]
-        rest_ref[c * D : (c + 1) * D, :] = mm_tn(x, d_part).astype(BF16)
+        rest_ref[c * D : (c + 1) * D, :] = mm_tn(x, d_part)
         smalls.append(col_sum(d_part.astype(F32)))
         tokens = tokens + mm_nt(d_part, wqkv_ref[:, cols])
     tokens_ref[...] = tokens
     for k in range(4):
         rest_ref[4 * D : 4 * D + 128, k * 128 : (k + 1) * 128] = gproj_ref[
             k * 128 : (k + 1) * 128, :
-        ].astype(BF16)
+        ]
     smalls += [bias_out, gain_grad, shift_grad] + [small_ref[k : k + 1, :] for k in range(7)]
     smalls += [jnp.zeros((EXT - len(smalls), D), F32)]
-    rest_ref[4 * D + 128 : 4 * D + 128 + EXT, :] = jnp.concatenate(smalls, axis=0).astype(BF16)
-    half, size = keep_ref.shape[0], keep_ref.shape[1]
+    rest_ref[4 * D + 128 : 4 * D + 128 + EXT, :] = jnp.concatenate(smalls, axis=0)
+    first = 0
+    for keep_ref, send_ref in ((keep_one, send_one), (keep_two, send_two)):
+        half, size = keep_ref.shape[0], keep_ref.shape[1]
+        for p in range(half):
+            for ref, owner, place in ((keep_ref, core, near_place), (send_ref, 1 - core, far_place)):
+                block = owner * half + (p ^ place)
+                start = pl.multiple_of(first + block * size, 8)
+                ref[p] = rest_ref[pl.ds(start, size), :].astype(BF16)
+        first += 2 * half * size
+
+
+def spread_out(columns, where_ref, near_ref, far_ref, out_ref):
+    core, near_place, far_place = where_ref[5], where_ref[6], where_ref[7]
+    half, size, width = near_ref.shape
+    per_column = 2 * half // columns
     for p in range(half):
-        for ref, offset in ((keep_ref, p), (send_ref, p + half)):
-            start = pl.multiple_of((offset ^ at) * size, 16)
-            ref[p] = rest_ref[pl.ds(start, size), :]
-
-
-def spread_out(at_index, order, where_ref, near_ref, far_ref, out_ref):
-    p = pl.program_id(0)
-    half = pl.num_programs(0) // 2
-
-    @pl.when(p < half)
-    def _():
-        out_ref[...] = near_ref[0].astype(F32)
-
-    @pl.when(p >= half)
-    def _():
-        out_ref[...] = far_ref[0].astype(F32)
-
-
-def spread_call(near, far, where, at_index, columns):
-    half, size, width = near.shape
-    blocks = 2 * half
-    per_column = blocks // columns
-
-    def out_index(p, where_ref):
-        b = p ^ where_ref[at_index]
-        return (b % per_column, b // per_column)
-
-    return pl.pallas_call(
-        partial(spread_out, at_index, None),
-        out_shape=jax.ShapeDtypeStruct((blocks * size // columns, width * columns), F32),
-        grid_spec=pltpu.PrefetchScalarGridSpec(
-            num_scalar_prefetch=1,
-            grid=(blocks,),
-            in_specs=[
-                pl.BlockSpec((1, size, width), lambda p, w: (jnp.minimum(p, half - 1), 0, 0)),
-                pl.BlockSpec((1, size, width), lambda p, w: (jnp.maximum(p - half, 0), 0, 0)),
-            ],
-            out_specs=pl.BlockSpec((size, width), out_index),
-        ),
-    )(where, near, far)
+        for ref, owner, place in ((near_ref, core, near_place), (far_ref, 1 - core, far_place)):
+            block = owner * half + (p ^ place)
+            start = pl.multiple_of((block % per_column) * size, 8)
+            left = pl.multiple_of((block // per_column) * width, 128)
+            out_ref[pl.ds(start, size), pl.ds(left, width)] = ref[p].astype(F32)
 
 
 def spread_rest(
-    where_ref, near_ref, far_ref, qkv_ref, out_ref, proj_ref, bqkv_ref, bout_ref, g1_ref, s1_ref,
-    bup_ref, bdown_ref, g2_ref, s2_ref, rest_ref,
+    where_ref, near_one, far_one, near_two, far_two, qkv_ref, out_ref, proj_ref, bqkv_ref, bout_ref,
+    g1_ref, s1_ref, bup_ref, bdown_ref, g2_ref, s2_ref, rest_ref,
 ):
-    at = where_ref[7]
-    half, size = near_ref.shape[0], near_ref.shape[1]
-    for p in range(half):
-        for ref, offset in ((near_ref, p), (far_ref, p + half)):
-            start = pl.multiple_of((offset ^ at) * size, 16)
-            rest_ref[pl.ds(start, size), :] = ref[p]
+    core, near_place, far_place = where_ref[5], where_ref[6], where_ref[7]
+    first = 0
+    for near_ref, far_ref in ((near_one, far_one), (near_two, far_two)):
+        half, size = near_ref.shape[0], near_ref.shape[1]
+        for p in range(half):
+            for ref, owner, place in ((near_ref, core, near_place), (far_ref, 1 - core, far_place)):
+                block = owner * half + (p ^ place)
+                start = pl.multiple_of(first + block * size, 8)
+                rest_ref[pl.ds(start, size), :] = ref[p].astype(F32)
+        first += 2 * half * size
     for c in range(3):
-        qkv_ref[:, c * D : (c + 1) * D] = rest_ref[c * D : (c + 1) * D, :].astype(F32)
-    out_ref[...] = rest_ref[3 * D : 4 * D, :].astype(F32)
+        qkv_ref[:, c * D : (c + 1) * D] = rest_ref[c * D : (c + 1) * D, :]
+    out_ref[...] = rest_ref[3 * D : 4 * D, :]
     for k in range(4):
         proj_ref[k * 128 : (k + 1) * 128, :] = rest_ref[
             4 * D : 4 * D + 128, k * 128 : (k + 1) * 128
-        ].astype(F32)
-    small = rest_ref[4 * D + 128 : 4 * D + 128 + EXT, :].astype(F32)
+        ]
+    small = rest_ref[4 * D + 128 : 4 * D + 128 + EXT, :]
     row = [small[k : k + 1, :] for k in range(13)]
     for c in range(3):
         bqkv_ref[:, c * D : (c + 1) * D] = row[c]
@@ -623,16 +612,32 @@
     return jax.ShapeDtypeStruct(tuple(shape), dtype)
 
 
-def call(kernel, args, specs, outs, scratch=(), flops=0):
+def call(kernel, args, specs, outs, scratch=(), room=24):
     return pl.pallas_call(
         kernel,
         out_shape=outs,
         in_specs=specs,
         out_specs=[VMEM] * len(outs),
         scratch_shapes=list(scratch),
-        compiler_params=pltpu.CompilerParams(vmem_limit_bytes=VLIMIT),
-        cost_estimate=pl.CostEstimate(flops=flops, bytes_accessed=10**6, transcendentals=0),
+        compiler_params=pltpu.CompilerParams(vmem_limit_bytes=room * MIB),
+        cost_estimate=pl.CostEstimate(flops=10**9, bytes_accessed=10**7, transcendentals=0),
     )(*args)
+
+
+def spread_call(kind, where, halves):
+    if kind < 2:
+        columns = (1, 4)[kind]
+        kernel, outs, scratch = (
+            partial(spread_out, columns), [shape_of((FF // columns, D * columns))], []
+        )
+    else:
+        kernel, scratch = spread_rest, [pltpu.VMEM((REST, D), F32)]
+        outs = [
+            shape_of((D, 3 * D)), shape_of((D, D)), shape_of((D, PROJ)), shape_of((1, 3 * D)),
+            shape_of((1, D)), shape_of((1, D)), shape_of((1, D)), shape_of((1, FF)),
+            shape_of((1, D)), shape_of((1, D)), shape_of((1, D)),
+        ]
+    return call(kernel, (where, *halves), [SMEM] + [VMEM] * len(halves), outs, scratch)
 
 
 def swapped(value, mask, axis="dp"):
@@ -651,19 +656,56 @@
     return place
 
 
-def reduce_gather(keep, send, order, others):
-    got = swapped(send, order[0])
-    for mask in order[1:]:
-        half = keep.shape[0] // 2
-        send = added(keep[half:], got[half:])
-        keep = added(keep[:half], got[:half])
-        got = swapped(send, mask)
-    own = added(keep, got)
-    for mask in others:
-        own = added(own, swapped(own, mask))
-    for mask in reversed(order[1:]):
-        own = jnp.concatenate([own, swapped(own, mask)], axis=0)
-    return own, swapped(own, order[0])
+def swapped_by_core(value, masks):
+    size = lax.axis_size("dp")
+    return lax.ppermute(value, "dp", [(k, k ^ masks[k & 1]) for k in range(size)])
+
+
+class Summed:
+    def __init__(self, keep, send, masks, others):
+        self.keep, self.masks, self.others, self.at = keep, masks, others, 0
+        self.got = swapped_by_core(send, masks[0])
+
+    def step(self, after):
+        keep, got = self.keep, self.got
+        if after is not None:
+            keep, got, _ = lax.optimization_barrier((keep, got, after))
+        self.at += 1
+        last = len(self.masks)
+        if self.at < last:
+            half = keep.shape[0] // 2
+            send = added(keep[half:], got[half:])
+            self.keep = added(keep[:half], got[:half])
+            self.got = swapped_by_core(send, self.masks[self.at])
+            return send
+        if self.at == last:
+            keep = added(keep, got)
+            for mask in self.others:
+                keep = added(keep, swapped(keep, mask))
+        elif self.at < 2 * last:
+            keep = jnp.concatenate([keep, got], axis=0)
+        else:
+            self.keep, self.got = keep, got
+            return got
+        self.keep = keep
+        self.got = swapped_by_core(keep, self.masks[2 * last - 1 - self.at])
+        return keep
+
+
+class Doubled:
+    def __init__(self, value, masks):
+        self.value, self.masks, self.got = value, list(masks), None
+
+    def step(self, after):
+        value, got = self.value, self.got
+        if after is not None:
+            value, _ = lax.optimization_barrier((value, after))
+        if got is not None:
+            value = value + got
+        self.value, self.got = value, None
+        if self.masks:
+            self.got = swapped(value, self.masks.pop(0))
+        return value
 
 
 def per_device(
@@ -675,11 +717,7 @@
     bits = [1 << k for k in range(size.bit_length() - 1)]
     near_masks, doc_masks = bits[:2], bits[2:]
     top_mask, doc_masks = doc_masks[-1], doc_masks[:-1]
-    orders = [
-        (bits[0], bits[1], bits[2], bits[3]),
-        (bits[0], bits[2], bits[1], bits[3]),
-        (bits[0], bits[1], bits[2], bits[3]),
-    ]
+    masks = [(bits[0], bits[0]), (bits[1], bits[2]), (bits[2], bits[1]), (bits[3], bits[3])]
     others = bits[4:]
     blocks = 16
     me = lax.axis_index("dp")
@@ -688,9 +726,11 @@
     has_top = (me & top_mask) != 0
     base = jnp.where(is_query, me & ~top_mask, me | top_mask)
     near_at = jnp.where((me & near_masks[1]) != 0, 1, 0) + jnp.where((me & near_masks[0]) != 0, 2, 0)
+    core = me & 1
+    places = [block_place(me, [pair[k] for pair in masks[1:]]) for k in range(2)]
     where = jnp.stack(
-        [me, stream, base, near_at, has_top.astype(jnp.int32)]
-        + [block_place(me, order) for order in orders]
+        [me, stream, base, near_at, has_top.astype(jnp.int32), core]
+        + [jnp.where(core == 0, *places), jnp.where(core == 0, *places[::-1])]
     ).astype(jnp.int32)
     scale = log_scale.reshape(1)
 
@@ -737,6 +777,7 @@
     tokens_q = 4 * ROW
     lanes = -(-3 * doc_rows * DOCS_ROW // 128) * 128
     total_queries = size * (ROW // QLEN)
+    room = 20 if doc_rows <= 4 else 56
     totals, el, hot, stats = call(
         partial(matching_stats, doc_masks, lanes),
         (where, scale, doc_lengths, near, far, *pieces),
@@ -748,6 +789,7 @@
             shape_of((tokens_q // QLEN, 128)),
         ],
         [pltpu.VMEM((PROJ, tokens_d), F32), pltpu.VMEM((3, PROJ, tokens_d), BF16)],
+        room=room,
     )
     stats = stats + swapped(stats, near_masks[0])
     stats = stats + swapped(stats, near_masks[1])
@@ -764,6 +806,7 @@
             pltpu.VMEM((tokens_q, PROJ), F32),
             pltpu.VMEM((3, PROJ, tokens_d), F32),
         ],
+        room=room,
     )
     for mask in reversed(doc_masks):
         half = dd.shape[0] // 2
@@ -785,37 +828,42 @@
         + [shape_of((ROW, D)), shape_of((D, PROJ)), shape_of((8, D))],
         [pltpu.VMEM((ROW, FF), BF16)],
     )
-    rest_keep, rest_send, tokens_grad = call(
+    keep_one, send_one, keep_two, send_two, tokens_grad = call(
         attend_back,
         (
             where, d_first, xh1, rs1, first_gain, mixed, out_weight[0], qkv, probs, rope,
             tokens[0], qkv_weight[0], gproj, small,
         ),
         [SMEM] + [VMEM] * 13,
-        [shape_of((blocks // 2, REST // blocks, D), BF16)] * 2 + [shape_of((ROW, D))],
-        [pltpu.VMEM((ROW, 3 * D), BF16), pltpu.VMEM((REST, D), BF16)],
+        [shape_of((blocks // 2, 3 * D // blocks, D), BF16)] * 2
+        + [shape_of((blocks // 2, (REST - 3 * D) // blocks, D), BF16)] * 2
+        + [shape_of((ROW, D))],
+        [pltpu.VMEM((ROW, 3 * D), BF16), pltpu.VMEM((REST, D), F32)],
     )
-    down_near, down_far = reduce_gather(down_keep, down_send, orders[0], others)
-    up_near, up_far = reduce_gather(up_keep, up_send, orders[1], others)
-    rest_near, rest_far = reduce_gather(rest_keep, rest_send, orders[2], others)
-    for mask in doc_masks + [top_mask]:
-        loss = loss + swapped(loss, mask)
-    grad_down = spread_call(down_near, down_far, where, 5, 1)
-    grad_up = spread_call(up_near, up_far, where, 6, 4)
+    pieces = [
+        Summed(keep, send, masks, others)
+        for keep, send in (
+            (down_keep, down_send), (up_keep, up_send), (keep_one, send_one), (keep_two, send_two)
+        )
+    ] + [Doubled(loss, doc_masks + [top_mask])]
+    token, spread = None, {}
+    for k in ORDER:
+        if k >= 10:
+            ready = [pieces[j] for j in FINAL[k - 10]]
+            halves = [half for piece in ready for half in (piece.keep, piece.got)]
+            *halves, _ = lax.optimization_barrier((*halves, token))
+            spread[k - 10] = spread_call(k - 10, where, halves)
+            token = spread[k - 10][0]
+        else:
+            token = pieces[k].step(token)
+    grad_down, grad_up = spread[0][0], spread[1][0]
     (
         grad_qkv, grad_out, grad_proj, grad_bqkv, grad_bout, grad_g1, grad_s1, grad_bup,
         grad_bdown, grad_g2, grad_s2,
-    ) = call(
-        spread_rest,
-        (where, rest_near, rest_far),
-        [SMEM, VMEM, VMEM],
-        [
-            shape_of((D, 3 * D)), shape_of((D, D)), shape_of((D, PROJ)), shape_of((1, 3 * D)),
-            shape_of((1, D)), shape_of((1, D)), shape_of((1, D)), shape_of((1, FF)),
-            shape_of((1, D)), shape_of((1, D)), shape_of((1, D)),
-        ],
-        [pltpu.VMEM((REST, D), BF16)],
-    )
+    ) = spread[2]
+    while pieces[-1].got is not None:
+        pieces[-1].step(None)
+    loss = pieces[-1].value
     return (
         loss[0, 0],
         tokens_grad[None],

time: 232 us -> 185 us (0.80)
  waiting for transfers between devices: 118 us -> 74.4 us
  Pallas kernels: 64.4 us -> 34.5 us
  starting transfers between devices: 32.1 us -> 48.9 us
  local copies, waits for them, and re-layouts: 6.03 us -> 21.6 us
  other arithmetic: 7.87 us -> 2.53 us
    ppermute x39 -> x15, waiting for transfers between devices: 118 us -> 23.3 us  [swapped(): return lax.ppermute(value, axis, [(k, k ^ mask) for k in range(size)])]
    ppermute x0 -> x32, waiting for transfers between devices: none -> 51.2 us  [swapped_by_core(): lax.ppermute(value, 'dp', [(k, k ^ masks[k & 1]) for k in range(size)])]
    ppermute x0 -> x32, starting transfers between devices: none -> 27.6 us  [swapped_by_core(): lax.ppermute(value, 'dp', [(k, k ^ masks[k & 1]) for k in range(size)])]
    pallas_call x2 -> x0, Pallas kernels: 21.3 us -> none  [spread_call(): pl.pallas_call(partial(spread_out, at_index, None), out_shape=jax.ShapeDt...]
    unnamed x25 -> x95, local copies, waits for them, and re-layouts: 3.09 us -> 20.8 us
    ppermute x39 -> x15, starting transfers between devices: 32.1 us -> 21.3 us  [swapped(): return lax.ppermute(value, axis, [(k, k ^ mask) for k in range(size)])]
    pallas_call x6 -> x8, Pallas kernels: 43.1 us -> 34.5 us  [call(): pl.pallas_call(kernel, out_shape=outs, in_specs=specs, out_specs=[VMEM] *...]
  transfers between devices with their start and end apart: 39 -> 47, of which waited for: 28 -> 25; matrix products, arithmetic and copies ran while one was open for 3% -> 2% of each run, Pallas kernels for 13% -> 3%
where the time goes in v2:
time: 185 us; the launch traced here: 184 us
  waiting for transfers between devices  74.4 us (40%)
  starting transfers between devices  48.9 us (26%)
  Pallas kernels  34.5 us (19%)
  local copies, waits for them, and re-layouts  21.6 us (12%)
  other arithmetic  2.53 us (1%)
  between operations  2.13 us (1%)
    ppermute x32, waiting for transfers between devices, swapped_by_core(): lax.ppermute(value, 'dp', [(k, k ^ masks[k & 1]) for k in range(size)])  51.2 us
    pallas_call x8, Pallas kernels, call(): pl.pallas_call(kernel, out_shape=outs, in_specs=specs, out_specs=[VMEM] *...  34.5 us
    ppermute x32, starting transfers between devices, swapped_by_core(): lax.ppermute(value, 'dp', [(k, k ^ masks[k & 1]) for k in range(size)])  27.6 us
    ppermute x15, waiting for transfers between devices, swapped(): return lax.ppermute(value, axis, [(k, k ^ mask) for k in range(size)])  23.3 us
    ppermute x15, starting transfers between devices, swapped(): return lax.ppermute(value, axis, [(k, k ^ mask) for k in range(size)])  21.3 us
    unnamed x95, local copies, waits for them, and re-layouts  20.8 us
  transfers between devices with their start and end apart: 47, of which 25 were waited for; matrix products, arithmetic and copies ran while one was open for 2% of the time, Pallas kernels for 3%

profile of v2, /device:TPU:0, one launch (start us, length us, event | category | flops | bytes accessed | tf_op | source)
XLA Modules:
  0.0 184.2 jit_solution(9576560731838806292)
XLA Ops:
  1.5 1.6 copy-done
  3.1 1.6 copy-done.2
  4.7 1.4 copy-done.4
  16.1 6.8 %shard_map.297 = (bf16[272,128]{1,0:T(8,128)(2,1)S(1)}, bf16[256,1536]{1,0:T(8,128)(2,1)S(1)}, f32[256,256]{1,0:T(8,128)S(1)}, bf16[8,256,256]{2,1,0:T(8,128)(2,...) custom-call(s32[8]{0:T(128)S(1)} %stack.39.where_ref, ...), custom_call_target="tpu_custom_call" | custom-call | flops 1000000000 | bytes 10000000 | tf_op jit(solution)/shard_map/pallas_call | solution.py:616
  27.4 2.9 %collective-permute-start = (bf16[272,128]{1,0:T(8,128)(2,1)S(1)}, bf16[272,128]{1,0:T(8,128)(2,1)S(1)}, u32[]{:S(2)}, u32[]{:S(2)}) collective-permute-start(bf16[272,128]{1,0:T(8,128)(2,1)S(1)} %get-tuple-element.131), channel_id=1, source_target_pairs={{0,16},{16,0},{1,17},{17,1},{2,18},{18,2},{3,19},{19,3},{4,20},{20... | collective-permute-start | bytes 208904 | tf_op jit(solution)/shard_map/ppermute | solution.py:645
  30.3 2.3 %collective-permute-done = bf16[272,128]{1,0:T(8,128)(2,1)S(1)} collective-permute-done((bf16[272,128]{1,0:T(8,128)(2,1)S(1)}, bf16[272,128]{1,0:T(8,128)(2,1)S(1)}, u32[]{:S(2)}, u32[]{:S(2)}) %collective-permute-start) | collective-permute-done | bytes 69664 | tf_op jit(solution)/shard_map/ppermute | solution.py:645
  32.6 2.1 %collective-permute-start.1 = (bf16[272,128]{1,0:T(8,128)(2,1)S(1)}, bf16[272,128]{1,0:T(8,128)(2,1)S(1)}, u32[]{:S(2)}, u32[]{:S(2)}) collective-permute-start(bf16[272,128]{1,0:T(8,128)(2,1)S(1)} %broadcast_select_fusion), channel_id=1, source_target_pairs={{0,2},{1,3},{2,0},{3,1},{4,6},{5,7},{6,4},{7,5},{8,10},{9,11},{10,... | collective-permute-start | bytes 208904 | tf_op jit(solution)/shard_map/ppermute | solution.py:645
  34.7 2.7 %collective-permute-start.3 = (bf16[256,128]{1,0:T(8,128)(2,1)S(1)}, bf16[256,128]{1,0:T(8,128)(2,1)S(1)}, u32[]{:S(2)}, u32[]{:S(2)}) collective-permute-start(bf16[256,128]{1,0:T(8,128)(2,1)S(1)} %slice_select_fusion), channel_id=1, source_target_pairs={{0,8},{1,9},{2,10},{3,11},{4,12},{5,13},{6,14},{7,15},{8,0},{9,1},... | collective-permute-start | bytes 196616 | tf_op jit(solution)/shard_map/ppermute | solution.py:645
  37.5 2.5 %collective-permute-done.3 = bf16[256,128]{1,0:T(8,128)(2,1)S(1)} collective-permute-done((bf16[256,128]{1,0:T(8,128)(2,1)S(1)}, bf16[256,128]{1,0:T(8,128)(2,1)S(1)}, u32[]{:S(2)}, u32[]{:S(2)}) %collective-permute-start.3) | collective-permute-done | bytes 65568 | tf_op jit(solution)/shard_map/ppermute | solution.py:645
  40.6 1.6 collective-permute-start.4
  42.8 2.4 %collective-permute-done.4.refs_1_ = bf16[256,128]{1,0:T(8,128)(2,1)} collective-permute-done((bf16[256,128]{1,0:T(8,128)(2,1)}, bf16[256,128]{1,0:T(8,128)(2,1)}, u32[]{:S(2)}, u32[]{:S(2)}) %collective-permute-start.4) | collective-permute-done | bytes 65568 | tf_op jit(solution)/shard_map/ppermute | solution.py:645
  45.9 3.1 %shard_map.298 = (f32[1024,128]{1,0:T(8,128)S(1)}, f32[32,128]{1,0:T(8,128)S(1)}, f32[32,128]{1,0:T(8,128)S(1)}, f32[32,128]{1,0:T(8,128)S(1)}) custom-call(s32[8]{0:T(128)S(1)} %copy-done.28, f32[1]{0:T(128)} %bitcast.23.scale_ref, s32[16,5]{1,0:T(8,128)S(1)} %copy.36.lens_ref, bf16[544,128]{1,0:T(8,128)(2,1)S(1)} %pad_maximum_fusion.near_ref, ...), custom_call_target="tpu_custom_call" | custom-call | flops 1000000000 | bytes 10000000 | tf_op jit(solution)/shard_map/pallas_call | solution.py:616
  50.6 3.6 %collective-permute-done.6 = f32[32,128]{1,0:T(8,128)S(1)} collective-permute-done((f32[32,128]{1,0:T(8,128)S(1)}, f32[32,128]{1,0:T(8,128)S(1)}, u32[]{:S(2)}, u32[]{:S(2)}) %collective-permute-start.6) | collective-permute-done | bytes 16416 | tf_op jit(solution)/shard_map/ppermute | solution.py:645
  54.1 1.5 collective-permute-start.7
  55.6 2.2 %collective-permute-done.7 = f32[32,128]{1,0:T(8,128)S(1)} collective-permute-done((f32[32,128]{1,0:T(8,128)S(1)}, f32[32,128]{1,0:T(8,128)S(1)}, u32[]{:S(2)}, u32[]{:S(2)}) %collective-permute-start.7) | collective-permute-done | bytes 16416 | tf_op jit(solution)/shard_map/ppermute | solution.py:645
  57.9 5.5 %shard_map.299 = (bf16[1024,128]{1,0:T(8,128)(2,1)S(1)}, bf16[512,128]{1,0:T(8,128)(2,1)S(1)}, f32[8,128]{1,0:T(8,128)S(1)}) custom-call(s32[8]{0:T(128)S(1)} %copy-done.28, f32[1]{0:T(128)} %bitcast.24.scale_ref, s32[16,5]{1,0:T(8,128)S(1)} %copy.36.lens_ref, bf16[544,128]{1,0:T(8,128)(2,1)S(1)} %pad_maximum_fusion.near_ref, ...), custom_call_target="tpu_custom_call" | custom-call | flops 1000000000 | bytes 10000000 | tf_op jit(solution)/shard_map/pallas_call | solution.py:616
  63.4 1.6 collective-permute-start.10
  65.1 2.6 %collective-permute-done.10 = bf16[256,128]{1,0:T(8,128)(2,1)S(1)} collective-permute-done((bf16[256,128]{1,0:T(8,128)(2,1)S(1)}, bf16[256,128]{1,0:T(8,128)(2,1)S(1)}, u32[]{:S(2)}, u32[]{:S(2)}) %collective-permute-start.10) | collective-permute-done | bytes 65568 | tf_op jit(solution)/shard_map/ppermute | solution.py:645
  67.7 3.2 %collective-permute-start.11 = (bf16[256,128]{1,0:T(8,128)(2,1)S(1)}, bf16[256,128]{1,0:T(8,128)(2,1)S(1)}, u32[]{:S(2)}, u32[]{:S(2)}) collective-permute-start(bf16[256,128]{1,0:T(8,128)(2,1)S(1)} %add_convert_fusion.27), channel_id=1, source_target_pairs={{0,8},{1,9},{2,10},{3,11},{4,12},{5,13},{6,14},{7,15},{8,0},{9,1},... | collective-permute-start | bytes 196616 | tf_op jit(solution)/shard_map/ppermute | solution.py:645
  71.6 1.6 collective-permute-done.11
  73.2 2.1 %collective-permute-done.9 = bf16[256,128]{1,0:T(8,128)(2,1)S(1)} collective-permute-done((bf16[256,128]{1,0:T(8,128)(2,1)S(1)}, bf16[256,128]{1,0:T(8,128)(2,1)S(1)}, u32[]{:S(2)}, u32[]{:S(2)}) %collective-permute-start.9) | collective-permute-done | bytes 65568 | tf_op jit(solution)/shard_map/ppermute | solution.py:645
  75.4 1.6 collective-permute-start.12
  76.9 2.8 %collective-permute-done.12.got_ref = bf16[256,128]{1,0:T(8,128)(2,1)S(1)} collective-permute-done((bf16[256,128]{1,0:T(8,128)(2,1)S(1)}, bf16[256,128]{1,0:T(8,128)(2,1)S(1)}, u32[]{:S(2)}, u32[]{:S(2)}) %collective-permute-start.12) | collective-permute-done | bytes 65568 | tf_op jit(solution)/shard_map/ppermute | solution.py:645
  79.9 5.1 %shard_map.300 = (bf16[8,128,512]{2,1,0:T(8,128)(2,1)S(1)}, bf16[8,128,512]{2,1,0:T(8,128)(2,1)S(1)}, bf16[8,128,512]{2,1,0:T(8,128)(2,1)S(1)}, bf16[8,128,512]{...) custom-call(s32[8]{0:T(128)S(1)} %copy-done.29, ...), custom_call_target="tpu_custom_call" | custom-call | flops 1000000000 | bytes 10000000 | tf_op jit(solution)/shard_map/pallas_call | solution.py:616
  85.1 5.2 %shard_map.301 = (bf16[8,96,512]{2,1,0:T(8,128)(2,1)S(1)}, bf16[8,96,512]{2,1,0:T(8,128)(2,1)S(1)}, bf16[8,48,512]{2,1,0:T(8,128)(2,1)S(1)}, bf16[8,48,512]{2,1,0:T(8,128)(2,1)S(1)}, f32[256,512]{1,0:T(8,128)}) custom-call(s32[8]{0:T(128)S(1)} %copy-done.29, f32[256,512]{1,0:T(8,128)S(1)} %get-tuple-element.144.dfirst_ref, ...), custom_call_target="tpu_custom_call" | custom-call | flops 1000000000 | bytes 10000000 | tf_op jit(solution)/shard_map/pallas_call | solution.py:616
  91.3 1.6 collective-permute-start.20
  93.7 2.4 %collective-permute-done.17 = bf16[8,48,512]{2,1,0:T(8,128)(2,1)S(1)} collective-permute-done((bf16[8,48,512]{2,1,0:T(8,128)(2,1)S(1)}, bf16[8,48,512]{2,1,0:T(8,128)(2,1)S(1)}, u32[]{:S(2)}, u32[]{:S(2)}) %collective-permute-start.17) | collective-permute-done | bytes 393248 | tf_op jit(solution)/shard_map/ppermute | solution.py:661
  97.1 1.6 collective-permute-start.25
  104.5 4.5 %collective-permute-done.18 = bf16[2,96,512]{2,1,0:T(8,128)(2,1)S(1)} collective-permute-done((bf16[2,96,512]{2,1,0:T(8,128)(2,1)S(1)}, bf16[2,96,512]{2,1,0:T(8,128)(2,1)S(1)}, u32[]{:S(2)}, u32[]{:S(2)}) %collective-permute-start.18) | collective-permute-done | bytes 196640 | tf_op jit(solution)/shard_map/ppermute | solution.py:661
  109.1 1.4 collective-permute-start.24
  110.5 1.6 collective-permute-start.30
  115.5 1.7 collective-permute-start.28
  117.2 3.1 %collective-permute-done.23 = bf16[4,128,512]{2,1,0:T(8,128)(2,1)S(1)} collective-permute-done((bf16[4,128,512]{2,1,0:T(8,128)(2,1)S(1)}, bf16[4,128,512]{2,1,0:T(8,128)(2,1)S(1)}, u32[]{:S(2)}, u32[]{:S(2)}) %collective-permute-start.23) | collective-permute-done | bytes 524320 | tf_op jit(solution)/shard_map/ppermute | solution.py:661
  121.8 1.4 collective-permute-start.26
  124.8 4.2 %collective-permute-done.27 = bf16[2,128,512]{2,1,0:T(8,128)(2,1)S(1)} collective-permute-done((bf16[2,128,512]{2,1,0:T(8,128)(2,1)S(1)}, bf16[2,128,512]{2,1,0:T(8,128)(2,1)S(1)}, u32[]{:S(2)}, u32[]{:S(2)}) %collective-permute-start.27) | collective-permute-done | bytes 262176 | tf_op jit(solution)/shard_map/ppermute | solution.py:661
  129.9 1.5 collective-permute-start.33
  131.4 1.4 collective-permute-start.35
  133.5 10.9 %collective-permute-done.35 = bf16[1,128,512]{2,1,0:T(8,128)(2,1)S(1)} collective-permute-done((bf16[1,128,512]{2,1,0:T(8,128)(2,1)S(1)}, bf16[1,128,512]{2,1,0:T(8,128)(2,1)S(1)}, u32[]{:S(2)}, u32[]{:S(2)}) %collective-permute-start.35) | collective-permute-done | bytes 131104 | tf_op jit(solution)/shard_map/ppermute | solution.py:661
  144.8 2.9 %collective-permute-start.39 = (bf16[1,128,512]{2,1,0:T(8,128)(2,1)S(1)}, bf16[1,128,512]{2,1,0:T(8,128)(2,1)S(1)}, u32[]{:S(2)}, u32[]{:S(2)}) collective-permute-start(bf16[1,128,512]{2,1,0:T(8,128)(2,1)S(1)} %add_convert_fusion.14), channel_id=1, source_target_pairs={{0,8},{1,9},{2,10},{3,11},{4,12},{5,13},{6,14},{7,15},{8,0},{9,1},... | collective-permute-start | bytes 393224 | tf_op jit(solution)/shard_map/ppermute | solution.py:661
  148.8 7.5 %collective-permute-done.37 = bf16[1,128,512]{2,1,0:T(8,128)(2,1)S(1)} collective-permute-done((bf16[1,128,512]{2,1,0:T(8,128)(2,1)S(1)}, bf16[1,128,512]{2,1,0:T(8,128)(2,1)S(1)}, u32[]{:S(2)}, u32[]{:S(2)}) %collective-permute-start.37) | collective-permute-done | bytes 131104 | tf_op jit(solution)/shard_map/ppermute | solution.py:661
  156.4 2.6 %collective-permute-done.39 = bf16[1,128,512]{2,1,0:T(8,128)(2,1)S(1)} collective-permute-done((bf16[1,128,512]{2,1,0:T(8,128)(2,1)S(1)}, bf16[1,128,512]{2,1,0:T(8,128)(2,1)S(1)}, u32[]{:S(2)}, u32[]{:S(2)}) %collective-permute-start.39) | collective-permute-done | bytes 131104 | tf_op jit(solution)/shard_map/ppermute | solution.py:661
  159.3 3.5 %collective-permute-done.41 = bf16[2,128,512]{2,1,0:T(8,128)(2,1)S(1)} collective-permute-done((bf16[2,128,512]{2,1,0:T(8,128)(2,1)S(1)}, bf16[2,128,512]{2,1,0:T(8,128)(2,1)S(1)}, u32[]{:S(2)}, u32[]{:S(2)}) %collective-permute-start.41) | collective-permute-done | bytes 262176 | tf_op jit(solution)/shard_map/ppermute | solution.py:661
  162.8 1.7 collective-permute-start.44
  164.5 3.0 %shard_map.302 = (f32[512,1536]{1,0:T(8,128)}, f32[512,512]{1,0:T(8,128)}, f32[512,128]{1,0:T(8,128)}, f32[1,1536]{1,0:T(1,128)}, f32[1,512]{1,0:T(1,128)}, /*in...) custom-call(s32[8]{0:T(128)S(1)} %copy-done.29, ...), custom_call_target="tpu_custom_call" | custom-call | flops 1000000000 | bytes 10000000 | tf_op jit(solution)/shard_map/pallas_call | solution.py:616
  168.4 3.7 %collective-permute-done.44 = bf16[4,128,512]{2,1,0:T(8,128)(2,1)S(1)} collective-permute-done((bf16[4,128,512]{2,1,0:T(8,128)(2,1)S(1)}, bf16[4,128,512]{2,1,0:T(8,128)(2,1)S(1)}, u32[]{:S(2)}, u32[]{:S(2)}) %collective-permute-start.44) | collective-permute-done | bytes 524320 | tf_op jit(solution)/shard_map/ppermute | solution.py:661
  172.2 5.5 %collective-permute-done.43 = bf16[4,128,512]{2,1,0:T(8,128)(2,1)S(1)} collective-permute-done((bf16[4,128,512]{2,1,0:T(8,128)(2,1)S(1)}, bf16[4,128,512]{2,1,0:T(8,128)(2,1)S(1)}, u32[]{:S(2)}, u32[]{:S(2)}) %collective-permute-start.43) | collective-permute-done | bytes 524320 | tf_op jit(solution)/shard_map/ppermute | solution.py:661
  178.4 2.9 %shard_map.303 = f32[2048,512]{1,0:T(8,128)} custom-call(s32[8]{0:T(128)S(1)} %copy-done.29, bf16[8,128,512]{2,1,0:T(8,128)(2,1)S(1)} %constant_dynamic-update-slice_fusion.20.near_ref, bf16[8,128,512]{2,1,0:T(8,128)(2,1)S(1)} %collective-permute-done.46.far_ref), custom_call_target="tpu_custom_call" | custom-call | flops 1000000000 | bytes 10000000 | tf_op jit(solution)/shard_map/pallas_call | solution.py:616
  181.3 2.9 %shard_map.304 = f32[512,2048]{1,0:T(8,128)} custom-call(s32[8]{0:T(128)S(1)} %copy-done.29, bf16[8,128,512]{2,1,0:T(8,128)(2,1)S(1)} %constant_dynamic-update-slice_fusion.22.near_ref, bf16[8,128,512]{2,1,0:T(8,128)(2,1)S(1)} %collective-permute-done.45.far_ref), custom_call_target="tpu_custom_call" | custom-call | flops 1000000000 | bytes 10000000 | tf_op jit(solution)/shard_map/pallas_call | solution.py:616
  (194 shorter events, 38.9 us)
Async XLA Ops:
  27.4 5.2 %collective-permute-start = (bf16[272,128]{1,0:T(8,128)(2,1)S(1)}, bf16[272,128]{1,0:T(8,128)(2,1)S(1)}, u32[]{:S(2)}, u32[]{:S(2)}) collective-permute-start(bf16[272,128]{1,0:T(8,128)(2,1)S(1)} %get-tuple-element.131), channel_id=1, source_target_pairs={{0,16},{16,0},{1,17},{17,1},{2,18},{18,2},{3,19},{19,3},{4,20},{20... | collective-permute-start | bytes 208904 | tf_op jit(solution)/shard_map/ppermute | solution.py:645
  32.6 4.8 %collective-permute-start.1 = (bf16[272,128]{1,0:T(8,128)(2,1)S(1)}, bf16[272,128]{1,0:T(8,128)(2,1)S(1)}, u32[]{:S(2)}, u32[]{:S(2)}) collective-permute-start(bf16[272,128]{1,0:T(8,128)(2,1)S(1)} %broadcast_select_fusion), channel_id=1, source_target_pairs={{0,2},{1,3},{2,0},{3,1},{4,6},{5,7},{6,4},{7,5},{8,10},{9,11},{10,... | collective-permute-start | bytes 208904 | tf_op jit(solution)/shard_map/ppermute | solution.py:645
  34.7 5.2 %collective-permute-start.3 = (bf16[256,128]{1,0:T(8,128)(2,1)S(1)}, bf16[256,128]{1,0:T(8,128)(2,1)S(1)}, u32[]{:S(2)}, u32[]{:S(2)}) collective-permute-start(bf16[256,128]{1,0:T(8,128)(2,1)S(1)} %slice_select_fusion), channel_id=1, source_target_pairs={{0,8},{1,9},{2,10},{3,11},{4,12},{5,13},{6,14},{7,15},{8,0},{9,1},... | collective-permute-start | bytes 196616 | tf_op jit(solution)/shard_map/ppermute | solution.py:645
  37.4 7.8 %collective-permute-start.2 = (bf16[544,128]{1,0:T(8,128)(2,1)S(1)}, bf16[544,128]{1,0:T(8,128)(2,1)}, u32[]{:S(2)}, u32[]{:S(2)}) collective-permute-start(bf16[544,128]{1,0:T(8,128)(2,1)S(1)} %pad_maximum_fusion.near_ref), channel_id=1, source_target_pairs={{0,1},{1,0},{2,3},{3,2},{4,5},{5,4},{6,7},{7,6},{8,9},{9,8},{10,11... | collective-permute-start | bytes 417800 | tf_op jit(solution)/shard_map/ppermute | solution.py:645
  40.6 4.6 %collective-permute-start.4 = (bf16[256,128]{1,0:T(8,128)(2,1)}, bf16[256,128]{1,0:T(8,128)(2,1)}, u32[]{:S(2)}, u32[]{:S(2)}) collective-permute-start(bf16[256,128]{1,0:T(8,128)(2,1)} %broadcast_select_fusion.2.refs_0_), channel_id=1, source_target_pairs={{0,4},{1,5},{2,6},{3,7},{4,0},{5,1},{6,2},{7,3},{8,12},{9,13},{10,... | collective-permute-start | bytes 196616 | tf_op jit(solution)/shard_map/ppermute | solution.py:645
  49.0 30.7 %copy-start.1 = (bf16[1,512,2048]{2,1,0:T(8,128)(2,1)S(1)}, bf16[1,512,2048]{2,1,0:T(8,128)(2,1)}, u32[]{:S(2)}) copy-start(bf16[1,512,2048]{2,1,0:T(8,128)(2,1)} %param.25) | copy-start | bytes 6291460
  49.1 1.2 collective-permute-start.5
  50.4 3.7 %collective-permute-start.6 = (f32[32,128]{1,0:T(8,128)S(1)}, f32[32,128]{1,0:T(8,128)S(1)}, u32[]{:S(2)}, u32[]{:S(2)}) collective-permute-start(f32[32,128]{1,0:T(8,128)S(1)} %add.115), channel_id=1, source_target_pairs={{0,2},{1,3},{2,0},{3,1},{4,6},{5,7},{6,4},{7,5},{8,10},{9,11},{10,... | collective-permute-start | bytes 49160 | tf_op jit(solution)/shard_map/ppermute | solution.py:645
  54.1 3.7 %collective-permute-start.7 = (f32[32,128]{1,0:T(8,128)S(1)}, f32[32,128]{1,0:T(8,128)S(1)}, u32[]{:S(2)}, u32[]{:S(2)}) collective-permute-start(f32[32,128]{1,0:T(8,128)S(1)} %add.116), channel_id=1, source_target_pairs={{0,16},{16,0},{1,17},{17,1},{2,18},{18,2},{3,19},{19,3},{4,20},{20... | collective-permute-start | bytes 49160 | tf_op jit(solution)/shard_map/ppermute | solution.py:645
  63.4 4.3 %collective-permute-start.10 = (bf16[256,128]{1,0:T(8,128)(2,1)S(1)}, bf16[256,128]{1,0:T(8,128)(2,1)S(1)}, u32[]{:S(2)}, u32[]{:S(2)}) collective-permute-start(bf16[256,128]{1,0:T(8,128)(2,1)S(1)} %slice.177), channel_id=1, source_target_pairs={{0,4},{1,5},{2,6},{3,7},{4,0},{5,1},{6,2},{7,3},{8,12},{9,13},{10,... | collective-permute-start | bytes 196616 | tf_op jit(solution)/shard_map/ppermute | solution.py:645
  65.0 5.9 %collective-permute-start.8 = (bf16[512,128]{1,0:T(8,128)(2,1)S(1)}, bf16[512,128]{1,0:T(8,128)(2,1)S(1)}, u32[]{:S(2)}, u32[]{:S(2)}) collective-permute-start(bf16[512,128]{1,0:T(8,128)(2,1)S(1)} %slice.173), channel_id=1, source_target_pairs={{0,1},{1,0},{2,3},{3,2},{4,5},{5,4},{6,7},{7,6},{8,9},{9,8},{10,11... | collective-permute-start | bytes 393224 | tf_op jit(solution)/shard_map/ppermute | solution.py:645
  67.7 5.5 %collective-permute-start.11 = (bf16[256,128]{1,0:T(8,128)(2,1)S(1)}, bf16[256,128]{1,0:T(8,128)(2,1)S(1)}, u32[]{:S(2)}, u32[]{:S(2)}) collective-permute-start(bf16[256,128]{1,0:T(8,128)(2,1)S(1)} %add_convert_fusion.27), channel_id=1, source_target_pairs={{0,8},{1,9},{2,10},{3,11},{4,12},{5,13},{6,14},{7,15},{8,0},{9,1},... | collective-permute-start | bytes 196616 | tf_op jit(solution)/shard_map/ppermute | solution.py:645
  71.0 4.3 %collective-permute-start.9 = (bf16[256,128]{1,0:T(8,128)(2,1)S(1)}, bf16[256,128]{1,0:T(8,128)(2,1)S(1)}, u32[]{:S(2)}, u32[]{:S(2)}) collective-permute-start(bf16[256,128]{1,0:T(8,128)(2,1)S(1)} %slice.231), channel_id=1, source_target_pairs={{0,2},{1,3},{2,0},{3,1},{4,6},{5,7},{6,4},{7,5},{8,10},{9,11},{10,... | collective-permute-start | bytes 196616 | tf_op jit(solution)/shard_map/ppermute | solution.py:645
  75.4 4.3 %collective-permute-start.12 = (bf16[256,128]{1,0:T(8,128)(2,1)S(1)}, bf16[256,128]{1,0:T(8,128)(2,1)S(1)}, u32[]{:S(2)}, u32[]{:S(2)}) collective-permute-start(bf16[256,128]{1,0:T(8,128)(2,1)S(1)} %get-tuple-element.246), channel_id=1, source_target_pairs={{0,16},{16,0},{1,17},{17,1},{2,18},{18,2},{3,19},{19,3},{4,20},{20... | collective-permute-start | bytes 196616 | tf_op jit(solution)/shard_map/ppermute | solution.py:645
  90.3 2.6 %collective-permute-start.13 = (bf16[8,96,512]{2,1,0:T(8,128)(2,1)S(1)}, bf16[8,96,512]{2,1,0:T(8,128)(2,1)S(1)}, u32[]{:S(2)}, u32[]{:S(2)}) collective-permute-start(bf16[8,96,512]{2,1,0:T(8,128)(2,1)S(1)} %get-tuple-element.153), channel_id=1, source_target_pairs={{0,1},{1,0},{2,3},{3,2},{4,5},{5,4},{6,7},{7,6},{8,9},{9,8},{10,11... | collective-permute-start | bytes 2359304 | tf_op jit(solution)/shard_map/ppermute | solution.py:661
  90.3 6.5 %collective-permute-start.16 = (bf16[8,128,512]{2,1,0:T(8,128)(2,1)S(1)}, bf16[8,128,512]{2,1,0:T(8,128)(2,1)S(1)}, u32[]{:S(2)}, u32[]{:S(2)}) collective-permute-start(bf16[8,128,512]{2,1,0:T(8,128)(2,1)S(1)} %get-tuple-element.159), channel_id=1, source_target_pairs={{0,1},{1,0},{2,3},{3,2},{4,5},{5,4},{6,7},{7,6},{8,9},{9,8},{10,11... | collective-permute-start | bytes 3145736 | tf_op jit(solution)/shard_map/ppermute | solution.py:661
  90.8 7.9 %collective-permute-start.15 = (bf16[8,128,512]{2,1,0:T(8,128)(2,1)S(1)}, bf16[8,128,512]{2,1,0:T(8,128)(2,1)S(1)}, u32[]{:S(2)}, u32[]{:S(2)}) collective-permute-start(bf16[8,128,512]{2,1,0:T(8,128)(2,1)S(1)} %get-tuple-element.157), channel_id=1, source_target_pairs={{0,1},{1,0},{2,3},{3,2},{4,5},{5,4},{6,7},{7,6},{8,9},{9,8},{10,11... | collective-permute-start | bytes 3145736 | tf_op jit(solution)/shard_map/ppermute | solution.py:661
  90.8 5.3 %collective-permute-start.17 = (bf16[8,48,512]{2,1,0:T(8,128)(2,1)S(1)}, bf16[8,48,512]{2,1,0:T(8,128)(2,1)S(1)}, u32[]{:S(2)}, u32[]{:S(2)}) collective-permute-start(bf16[8,48,512]{2,1,0:T(8,128)(2,1)S(1)} %get-tuple-element.161), channel_id=1, source_target_pairs={{0,1},{1,0},{2,3},{3,2},{4,5},{5,4},{6,7},{7,6},{8,9},{9,8},{10,11... | collective-permute-start | bytes 1179656 | tf_op jit(solution)/shard_map/ppermute | solution.py:661
  91.3 19.2 %collective-permute-start.20 = (f32[8,128]{1,0:T(8,128)S(1)}, f32[8,128]{1,0:T(8,128)S(1)}, u32[]{:S(2)}, u32[]{:S(2)}) collective-permute-start(f32[8,128]{1,0:T(8,128)S(1)} %get-tuple-element.174), channel_id=1, source_target_pairs={{0,4},{1,5},{2,6},{3,7},{4,0},{5,1},{6,2},{7,3},{8,12},{9,13},{10,... | collective-permute-start | bytes 12296 | tf_op jit(solution)/shard_map/ppermute | solution.py:645
  93.2 7.8 %collective-permute-start.14 = (bf16[4,96,512]{2,1,0:T(8,128)(2,1)S(1)}, bf16[4,96,512]{2,1,0:T(8,128)(2,1)S(1)}, u32[]{:S(2)}, u32[]{:S(2)}) collective-permute-start(bf16[4,96,512]{2,1,0:T(8,128)(2,1)S(1)} %get-tuple-element.253), channel_id=1, source_target_pairs={{0,2},{1,5},{2,0},{3,7},{4,6},{5,1},{6,4},{7,3},{8,10},{9,13},{10,... | collective-permute-start | bytes 1179656 | tf_op jit(solution)/shard_map/ppermute | solution.py:661
  96.2 7.1 %collective-permute-start.19 = (bf16[4,48,512]{2,1,0:T(8,128)(2,1)S(1)}, bf16[4,48,512]{2,1,0:T(8,128)(2,1)S(1)}, u32[]{:S(2)}, u32[]{:S(2)}) collective-permute-start(bf16[4,48,512]{2,1,0:T(8,128)(2,1)S(1)} %get-tuple-element.260), channel_id=1, source_target_pairs={{0,2},{1,5},{2,0},{3,7},{4,6},{5,1},{6,4},{7,3},{8,10},{9,13},{10,... | collective-permute-start | bytes 589832 | tf_op jit(solution)/shard_map/ppermute | solution.py:661
  97.1 16.4 %collective-permute-start.25 = (bf16[4,128,512]{2,1,0:T(8,128)(2,1)S(1)}, bf16[4,128,512]{2,1,0:T(8,128)(2,1)S(1)}, u32[]{:S(2)}, u32[]{:S(2)}) collective-permute-start(bf16[4,128,512]{2,1,0:T(8,128)(2,1)S(1)} %get-tuple-element.250), channel_id=1, source_target_pairs={{0,2},{1,5},{2,0},{3,7},{4,6},{5,1},{6,4},{7,3},{8,10},{9,13},{10,... | collective-permute-start | bytes 1572872 | tf_op jit(solution)/shard_map/ppermute | solution.py:661
  99.1 21.2 %collective-permute-start.23 = (bf16[4,128,512]{2,1,0:T(8,128)(2,1)S(1)}, bf16[4,128,512]{2,1,0:T(8,128)(2,1)S(1)}, u32[]{:S(2)}, u32[]{:S(2)}) collective-permute-start(bf16[4,128,512]{2,1,0:T(8,128)(2,1)S(1)} %get-tuple-element.252), channel_id=1, source_target_pairs={{0,2},{1,5},{2,0},{3,7},{4,6},{5,1},{6,4},{7,3},{8,10},{9,13},{10,... | collective-permute-start | bytes 1572872 | tf_op jit(solution)/shard_map/ppermute | solution.py:661
  101.1 7.9 %collective-permute-start.18 = (bf16[2,96,512]{2,1,0:T(8,128)(2,1)S(1)}, bf16[2,96,512]{2,1,0:T(8,128)(2,1)S(1)}, u32[]{:S(2)}, u32[]{:S(2)}) collective-permute-start(bf16[2,96,512]{2,1,0:T(8,128)(2,1)S(1)} %get-tuple-element.261), channel_id=1, source_target_pairs={{0,4},{1,3},{2,6},{3,1},{4,0},{5,7},{6,2},{7,5},{8,12},{9,11},{10,... | collective-permute-start | bytes 589832 | tf_op jit(solution)/shard_map/ppermute | solution.py:661
  103.4 8.8 %collective-permute-start.21 = (bf16[2,48,512]{2,1,0:T(8,128)(2,1)S(1)}, bf16[2,48,512]{2,1,0:T(8,128)(2,1)S(1)}, u32[]{:S(2)}, u32[]{:S(2)}) collective-permute-start(bf16[2,48,512]{2,1,0:T(8,128)(2,1)S(1)} %get-tuple-element.270), channel_id=1, source_target_pairs={{0,4},{1,3},{2,6},{3,1},{4,0},{5,7},{6,2},{7,5},{8,12},{9,11},{10,... | collective-permute-start | bytes 294920 | tf_op jit(solution)/shard_map/ppermute | solution.py:661
  109.1 6.4 %collective-permute-start.24 = (bf16[1,96,512]{2,1,0:T(8,128)(2,1)S(1)}, bf16[1,96,512]{2,1,0:T(8,128)(2,1)S(1)}, u32[]{:S(2)}, u32[]{:S(2)}) collective-permute-start(bf16[1,96,512]{2,1,0:T(8,128)(2,1)S(1)} %get-tuple-element.268), channel_id=1, source_target_pairs={{0,8},{1,9},{2,10},{3,11},{4,12},{5,13},{6,14},{7,15},{8,0},{9,1},... | collective-permute-start | bytes 294920 | tf_op jit(solution)/shard_map/ppermute | solution.py:661
  110.5 22.4 %collective-permute-start.30 = (f32[8,128]{1,0:T(8,128)S(1)}, f32[8,128]{1,0:T(8,128)S(1)}, u32[]{:S(2)}, u32[]{:S(2)}) collective-permute-start(f32[8,128]{1,0:T(8,128)S(1)} %add.132), channel_id=1, source_target_pairs={{0,8},{1,9},{2,10},{3,11},{4,12},{5,13},{6,14},{7,15},{8,0},{9,1},... | collective-permute-start | bytes 12296 | tf_op jit(solution)/shard_map/ppermute | solution.py:645
  112.3 9.5 %collective-permute-start.22 = (bf16[1,48,512]{2,1,0:T(8,128)(2,1)S(1)}, bf16[1,48,512]{2,1,0:T(8,128)(2,1)S(1)}, u32[]{:S(2)}, u32[]{:S(2)}) collective-permute-start(bf16[1,48,512]{2,1,0:T(8,128)(2,1)S(1)} %get-tuple-element.271), channel_id=1, source_target_pairs={{0,8},{1,9},{2,10},{3,11},{4,12},{5,13},{6,14},{7,15},{8,0},{9,1},... | collective-permute-start | bytes 147464 | tf_op jit(solution)/shard_map/ppermute | solution.py:661
  113.6 9.8 %collective-permute-start.29 = (bf16[2,128,512]{2,1,0:T(8,128)(2,1)S(1)}, bf16[2,128,512]{2,1,0:T(8,128)(2,1)S(1)}, u32[]{:S(2)}, u32[]{:S(2)}) collective-permute-start(bf16[2,128,512]{2,1,0:T(8,128)(2,1)S(1)} %get-tuple-element.256), channel_id=1, source_target_pairs={{0,4},{1,3},{2,6},{3,1},{4,0},{5,7},{6,2},{7,5},{8,12},{9,11},{10,... | collective-permute-start | bytes 786440 | tf_op jit(solution)/shard_map/ppermute | solution.py:661
  115.5 8.0 %collective-permute-start.28 = (bf16[1,96,512]{2,1,0:T(8,128)(2,1)S(1)}, bf16[1,96,512]{2,1,0:T(8,128)(2,1)S(1)}, u32[]{:S(2)}, u32[]{:S(2)}) collective-permute-start(bf16[1,96,512]{2,1,0:T(8,128)(2,1)S(1)} %add_convert_fusion.21), channel_id=1, source_target_pairs={{0,8},{1,9},{2,10},{3,11},{4,12},{5,13},{6,14},{7,15},{8,0},{9,1},... | collective-permute-start | bytes 294920 | tf_op jit(solution)/shard_map/ppermute | solution.py:661
  120.5 8.5 %collective-permute-start.27 = (bf16[2,128,512]{2,1,0:T(8,128)(2,1)S(1)}, bf16[2,128,512]{2,1,0:T(8,128)(2,1)S(1)}, u32[]{:S(2)}, u32[]{:S(2)}) collective-permute-start(bf16[2,128,512]{2,1,0:T(8,128)(2,1)S(1)} %get-tuple-element.258), channel_id=1, source_target_pairs={{0,4},{1,3},{2,6},{3,1},{4,0},{5,7},{6,2},{7,5},{8,12},{9,11},{10,... | collective-permute-start | bytes 786440 | tf_op jit(solution)/shard_map/ppermute | solution.py:661
  121.8 7.3 %collective-permute-start.26 = (bf16[1,48,512]{2,1,0:T(8,128)(2,1)S(1)}, bf16[1,48,512]{2,1,0:T(8,128)(2,1)S(1)}, u32[]{:S(2)}, u32[]{:S(2)}) collective-permute-start(bf16[1,48,512]{2,1,0:T(8,128)(2,1)S(1)} %add_convert_fusion.29), channel_id=1, source_target_pairs={{0,8},{1,9},{2,10},{3,11},{4,12},{5,13},{6,14},{7,15},{8,0},{9,1},... | collective-permute-start | bytes 147464 | tf_op jit(solution)/shard_map/ppermute | solution.py:661
  123.5 9.3 %collective-permute-start.31 = (bf16[2,96,512]{2,1,0:T(8,128)(2,1)S(1)}, bf16[2,96,512]{2,1,0:T(8,128)(2,1)S(1)}, u32[]{:S(2)}, u32[]{:S(2)}) collective-permute-start(bf16[2,96,512]{2,1,0:T(8,128)(2,1)S(1)} %constant_dynamic-update-slice_fusion), channel_id=1, source_target_pairs={{0,4},{1,3},{2,6},{3,1},{4,0},{5,7},{6,2},{7,5},{8,12},{9,11},{10,... | collective-permute-start | bytes 589832 | tf_op jit(solution)/shard_map/ppermute | solution.py:661
  129.1 15.4 %collective-permute-start.34 = (bf16[2,48,512]{2,1,0:T(8,128)(2,1)S(1)}, bf16[2,48,512]{2,1,0:T(8,128)(2,1)S(1)}, u32[]{:S(2)}, u32[]{:S(2)}) collective-permute-start(bf16[2,48,512]{2,1,0:T(8,128)(2,1)S(1)} %constant_dynamic-update-slice_fusion.2), channel_id=1, source_target_pairs={{0,4},{1,3},{2,6},{3,1},{4,0},{5,7},{6,2},{7,5},{8,12},{9,11},{10,... | collective-permute-start | bytes 294920 | tf_op jit(solution)/shard_map/ppermute | solution.py:661
  129.9 14.6 %collective-permute-start.33 = (bf16[1,128,512]{2,1,0:T(8,128)(2,1)S(1)}, bf16[1,128,512]{2,1,0:T(8,128)(2,1)S(1)}, u32[]{:S(2)}, u32[]{:S(2)}) collective-permute-start(bf16[1,128,512]{2,1,0:T(8,128)(2,1)S(1)} %get-tuple-element.266), channel_id=1, source_target_pairs={{0,8},{1,9},{2,10},{3,11},{4,12},{5,13},{6,14},{7,15},{8,0},{9,1},... | collective-permute-start | bytes 393224 | tf_op jit(solution)/shard_map/ppermute | solution.py:661
  131.4 13.0 %collective-permute-start.35 = (bf16[1,128,512]{2,1,0:T(8,128)(2,1)S(1)}, bf16[1,128,512]{2,1,0:T(8,128)(2,1)S(1)}, u32[]{:S(2)}, u32[]{:S(2)}) collective-permute-start(bf16[1,128,512]{2,1,0:T(8,128)(2,1)S(1)} %get-tuple-element.264), channel_id=1, source_target_pairs={{0,8},{1,9},{2,10},{3,11},{4,12},{5,13},{6,14},{7,15},{8,0},{9,1},... | collective-permute-start | bytes 393224 | tf_op jit(solution)/shard_map/ppermute | solution.py:661
  132.9 11.7 %collective-permute-start.32 = (bf16[4,96,512]{2,1,0:T(8,128)(2,1)S(1)}, bf16[4,96,512]{2,1,0:T(8,128)(2,1)S(1)}, u32[]{:S(2)}, u32[]{:S(2)}) collective-permute-start(bf16[4,96,512]{2,1,0:T(8,128)(2,1)S(1)} %constant_dynamic-update-slice_fusion.4), channel_id=1, source_target_pairs={{0,2},{1,5},{2,0},{3,7},{4,6},{5,1},{6,4},{7,3},{8,10},{9,13},{10,... | collective-permute-start | bytes 1179656 | tf_op jit(solution)/shard_map/ppermute | solution.py:661
  144.7 11.8 %collective-permute-start.36 = (bf16[8,96,512]{2,1,0:T(8,128)(2,1)S(1)}, bf16[8,96,512]{2,1,0:T(8,128)(2,1)S(1)}, u32[]{:S(2)}, u32[]{:S(2)}) collective-permute-start(bf16[8,96,512]{2,1,0:T(8,128)(2,1)S(1)} %constant_dynamic-update-slice_fusion.8.near_one), channel_id=1, source_target_pairs={{0,1},{1,0},{2,3},{3,2},{4,5},{5,4},{6,7},{7,6},{8,9},{9,8},{10,11... | collective-permute-start | bytes 2359304 | tf_op jit(solution)/shard_map/ppermute | solution.py:661
  144.7 11.6 %collective-permute-start.37 = (bf16[1,128,512]{2,1,0:T(8,128)(2,1)S(1)}, bf16[1,128,512]{2,1,0:T(8,128)(2,1)S(1)}, u32[]{:S(2)}, u32[]{:S(2)}) collective-permute-start(bf16[1,128,512]{2,1,0:T(8,128)(2,1)S(1)} %add_convert_fusion.15), channel_id=1, source_target_pairs={{0,8},{1,9},{2,10},{3,11},{4,12},{5,13},{6,14},{7,15},{8,0},{9,1},... | collective-permute-start | bytes 393224 | tf_op jit(solution)/shard_map/ppermute | solution.py:661
  144.8 14.3 %collective-permute-start.39 = (bf16[1,128,512]{2,1,0:T(8,128)(2,1)S(1)}, bf16[1,128,512]{2,1,0:T(8,128)(2,1)S(1)}, u32[]{:S(2)}, u32[]{:S(2)}) collective-permute-start(bf16[1,128,512]{2,1,0:T(8,128)(2,1)S(1)} %add_convert_fusion.14), channel_id=1, source_target_pairs={{0,8},{1,9},{2,10},{3,11},{4,12},{5,13},{6,14},{7,15},{8,0},{9,1},... | collective-permute-start | bytes 393224 | tf_op jit(solution)/shard_map/ppermute | solution.py:661
  147.7 11.4 %collective-permute-start.38 = (bf16[4,48,512]{2,1,0:T(8,128)(2,1)S(1)}, bf16[4,48,512]{2,1,0:T(8,128)(2,1)S(1)}, u32[]{:S(2)}, u32[]{:S(2)}) collective-permute-start(bf16[4,48,512]{2,1,0:T(8,128)(2,1)S(1)} %constant_dynamic-update-slice_fusion.6), channel_id=1, source_target_pairs={{0,2},{1,5},{2,0},{3,7},{4,6},{5,1},{6,4},{7,3},{8,10},{9,13},{10,... | collective-permute-start | bytes 589832 | tf_op jit(solution)/shard_map/ppermute | solution.py:661
  156.3 6.4 %collective-permute-start.41 = (bf16[2,128,512]{2,1,0:T(8,128)(2,1)S(1)}, bf16[2,128,512]{2,1,0:T(8,128)(2,1)S(1)}, u32[]{:S(2)}, u32[]{:S(2)}) collective-permute-start(bf16[2,128,512]{2,1,0:T(8,128)(2,1)S(1)} %constant_dynamic-update-slice_fusion.10), channel_id=1, source_target_pairs={{0,4},{1,3},{2,6},{3,1},{4,0},{5,7},{6,2},{7,5},{8,12},{9,11},{10,... | collective-permute-start | bytes 786440 | tf_op jit(solution)/shard_map/ppermute | solution.py:661
  159.2 5.4 %collective-permute-start.40 = (bf16[8,48,512]{2,1,0:T(8,128)(2,1)S(1)}, bf16[8,48,512]{2,1,0:T(8,128)(2,1)S(1)}, u32[]{:S(2)}, u32[]{:S(2)}) collective-permute-start(bf16[8,48,512]{2,1,0:T(8,128)(2,1)S(1)} %constant_dynamic-update-slice_fusion.14.near_two), channel_id=1, source_target_pairs={{0,1},{1,0},{2,3},{3,2},{4,5},{5,4},{6,7},{7,6},{8,9},{9,8},{10,11... | collective-permute-start | bytes 1179656 | tf_op jit(solution)/shard_map/ppermute | solution.py:661
  159.3 8.3 %collective-permute-start.42 = (bf16[2,128,512]{2,1,0:T(8,128)(2,1)S(1)}, bf16[2,128,512]{2,1,0:T(8,128)(2,1)S(1)}, u32[]{:S(2)}, u32[]{:S(2)}) collective-permute-start(bf16[2,128,512]{2,1,0:T(8,128)(2,1)S(1)} %constant_dynamic-update-slice_fusion.12), channel_id=1, source_target_pairs={{0,4},{1,3},{2,6},{3,1},{4,0},{5,7},{6,2},{7,5},{8,12},{9,11},{10,... | collective-permute-start | bytes 786440 | tf_op jit(solution)/shard_map/ppermute | solution.py:661
  162.8 9.2 %collective-permute-start.44 = (bf16[4,128,512]{2,1,0:T(8,128)(2,1)S(1)}, bf16[4,128,512]{2,1,0:T(8,128)(2,1)S(1)}, u32[]{:S(2)}, u32[]{:S(2)}) collective-permute-start(bf16[4,128,512]{2,1,0:T(8,128)(2,1)S(1)} %constant_dynamic-update-slice_fusion.16), channel_id=1, source_target_pairs={{0,2},{1,5},{2,0},{3,7},{4,6},{5,1},{6,4},{7,3},{8,10},{9,13},{10,... | collective-permute-start | bytes 1572872 | tf_op jit(solution)/shard_map/ppermute | solution.py:661
  167.6 10.1 %collective-permute-start.43 = (bf16[4,128,512]{2,1,0:T(8,128)(2,1)S(1)}, bf16[4,128,512]{2,1,0:T(8,128)(2,1)S(1)}, u32[]{:S(2)}, u32[]{:S(2)}) collective-permute-start(bf16[4,128,512]{2,1,0:T(8,128)(2,1)S(1)} %constant_dynamic-update-slice_fusion.18), channel_id=1, source_target_pairs={{0,2},{1,5},{2,0},{3,7},{4,6},{5,1},{6,4},{7,3},{8,10},{9,13},{10,... | collective-permute-start | bytes 1572872 | tf_op jit(solution)/shard_map/ppermute | solution.py:661
  172.2 6.2 %collective-permute-start.46 = (bf16[8,128,512]{2,1,0:T(8,128)(2,1)S(1)}, bf16[8,128,512]{2,1,0:T(8,128)(2,1)S(1)}, u32[]{:S(2)}, u32[]{:S(2)}) collective-permute-start(bf16[8,128,512]{2,1,0:T(8,128)(2,1)S(1)} %constant_dynamic-update-slice_fusion.20.near_ref), channel_id=1, source_target_pairs={{0,1},{1,0},{2,3},{3,2},{4,5},{5,4},{6,7},{7,6},{8,9},{9,8},{10,11... | collective-permute-start | bytes 3145736 | tf_op jit(solution)/shard_map/ppermute | solution.py:661
  177.8 3.5 %collective-permute-start.45 = (bf16[8,128,512]{2,1,0:T(8,128)(2,1)S(1)}, bf16[8,128,512]{2,1,0:T(8,128)(2,1)S(1)}, u32[]{:S(2)}, u32[]{:S(2)}) collective-permute-start(bf16[8,128,512]{2,1,0:T(8,128)(2,1)S(1)} %constant_dynamic-update-slice_fusion.22.near_ref), channel_id=1, source_target_pairs={{0,1},{1,0},{2,3},{3,2},{4,5},{5,4},{6,7},{7,6},{8,9},{9,8},{10,11... | collective-permute-start | bytes 3145736 | tf_op jit(solution)/shard_map/ppermute | solution.py:661
  (40 other events, 353.8 us)

commit v3 on v2

--- a/solution.py
+++ b/solution.py
@@ -34,6 +34,8 @@
 
 VMEM = pl.BlockSpec(memory_space=pltpu.VMEM)
 SMEM = pl.BlockSpec(memory_space=pltpu.SMEM)
+HBM = pl.BlockSpec(memory_space=pltpu.HBM)
+HELD = pl.BlockSpec(memory_space=pltpu.VMEM)
 
 
 def mm(a, b):
@@ -107,12 +109,54 @@
     return jnp.sum(values, axis=0, keepdims=True)
 
 
+def fetch(pairs, sems):
+    copies = [pltpu.make_async_copy(src, dst, sems.at[k]) for k, (src, dst) in enumerate(pairs)]
+    for copy in copies:
+        copy.start()
+    return copies
+
+
+KEPT = (
+    ((ROW, 3 * D), BF16),
+    ((ROW, 256), F32),
+    ((HEADS, ROW, ROW), BF16),
+    ((ROW, D), BF16),
+    ((ROW, D), F32),
+    ((ROW, 128), F32),
+    ((ROW, FF), BF16),
+    ((ROW, FF), BF16),
+    ((ROW, D), F32),
+    ((ROW, 128), F32),
+    ((8, D), F32),
+)
+
+
 def encoder_forward(
-    where_ref, lens_ref, labels_ref, table_ref, x_ref, wqkv_ref, bqkv_ref, wout_ref, bout_ref,
-    g1_ref, s1_ref, wup_ref, bup_ref, wdown_ref, bdown_ref, g2_ref, s2_ref, wproj_ref,
-    vec_ref, qkv_ref, rope_ref, probs_ref, mixed_ref, xh1_ref, rs1_ref, act_ref, slope_ref,
-    xh2_ref, rs2_ref,
+    where_ref, lens_ref, labels_ref, table_hbm, x_hbm, wqkv_hbm, bqkv_hbm, wout_hbm, bout_hbm,
+    g1_hbm, s1_hbm, wup_hbm, bup_hbm, wdown_hbm, bdown_hbm, g2_hbm, s2_hbm, wproj_hbm,
+    vec_ref, qkv_hbm, rope_hbm, probs_hbm, mixed_hbm, xh1_hbm, rs1_hbm, act_hbm, slope_hbm,
+    xh2_hbm, rs2_hbm, affine_hbm,
+    qkv_ref, rope_ref, probs_ref, mixed_ref, xh1_ref, rs1_ref, act_ref, slope_ref,
+    xh2_ref, rs2_ref, affine_ref, out_sems,
+    table_ref, x_ref, wqkv_ref, bqkv_ref, wout_ref, bout_ref, g1_ref, s1_ref, wup_ref, bup_ref,
+    wdown_ref, bdown_ref, g2_ref, s2_ref, wproj_ref, sems,
 ):
+    copies = fetch(
+        (
+            (table_hbm, table_ref), (x_hbm, x_ref), (wqkv_hbm, wqkv_ref), (bqkv_hbm, bqkv_ref),
+            (wout_hbm, wout_ref), (bout_hbm, bout_ref), (g1_hbm, g1_ref), (s1_hbm, s1_ref),
+            (bup_hbm, bup_ref), (bdown_hbm, bdown_ref), (g2_hbm, g2_ref), (s2_hbm, s2_ref),
+            (wup_hbm, wup_ref), (wdown_hbm, wdown_ref), (wproj_hbm, wproj_ref),
+        ),
+        sems,
+    )
+    kept = []
+
+    def keep(src, dst):
+        copy = pltpu.make_async_copy(src, dst, out_sems.at[len(kept)])
+        copy.start()
+        kept.append(copy)
+
     me, is_query = where_ref[0], where_ref[1] == 0
     ends = bounds_of(lens_ref, me)
 
@@ -131,11 +175,14 @@
     seg_k, _ = layout(iota(shape, 1))
     same = seg_q == seg_k
     onehot = (iota(shape, 1) == iota(shape, 0) - start_q).astype(F32).astype(BF16)
+    for copy in copies[:4]:
+        copy.wait()
     turned = mm(onehot, table_ref[...])
     cosine = turned[:, :128] + turned[:, 128:256]
     sine = turned[:, 256:384] + turned[:, 384:]
     rope_ref[:, :128] = cosine
     rope_ref[:, 128:] = sine
+    keep(rope_ref, rope_hbm)
 
     x = x_ref[...]
     joined = mm(x, wqkv_ref[...]) + bqkv_ref[...].astype(F32)
@@ -145,6 +192,7 @@
             block * cosine + swap_halves(block) * sine
         ).astype(BF16)
     qkv_ref[:, 2 * D :] = joined[:, 2 * D :].astype(BF16)
+    keep(qkv_ref, qkv_hbm)
 
     low_half = iota((ROW, 128), 1) < HD
     for g in range(HEADS // 2):
@@ -163,14 +211,26 @@
             outs.append(mm(probs, v_g))
         mixed_ref[:, g * 128 : (g + 1) * 128] = jnp.where(low_half, outs[0], outs[1]).astype(BF16)
 
+    keep(probs_ref, probs_hbm)
+    keep(mixed_ref, mixed_hbm)
+    for copy in copies[4:12]:
+        copy.wait()
+    for k, ref in enumerate((g1_ref, s1_ref, g2_ref, s2_ref)):
+        affine_ref[k : k + 1, :] = ref[...].astype(F32)
+    affine_ref[4:, :] = jnp.zeros((4, D), F32)
+    keep(affine_ref, affine_hbm)
     attended = mm(mixed_ref[...], wout_ref[...]) + bout_ref[...].astype(F32)
     xhat, rstd = norm_rows(x.astype(F32) + attended)
     xh1_ref[...] = xhat
     rs1_ref[...] = jnp.broadcast_to(rstd, (ROW, 128))
+    keep(xh1_ref, xh1_hbm)
+    keep(rs1_ref, rs1_hbm)
     first = xhat * g1_ref[...].astype(F32) + s1_ref[...].astype(F32)
     first_low = first.astype(BF16)
     branch = bdown_ref[...].astype(F32) + first
     step = 512
+    for copy in copies[12:]:
+        copy.wait()
     for c in range(FF // step):
         cols = slice(c * step, (c + 1) * step)
         inner = mm(first_low, wup_ref[:, cols]) + bup_ref[:, cols].astype(F32)
@@ -179,10 +239,14 @@
         act = (inner * gate).astype(BF16)
         act_ref[:, cols] = act
         slope_ref[:, cols] = (gate + inner * bell).astype(BF16)
+        keep(act_ref.at[:, cols], act_hbm.at[:, cols])
+        keep(slope_ref.at[:, cols], slope_hbm.at[:, cols])
         branch = branch + mm(act, wdown_ref[cols, :])
     xhat, rstd = norm_rows(branch)
     xh2_ref[...] = xhat
     rs2_ref[...] = jnp.broadcast_to(rstd, (ROW, 128))
+    keep(xh2_ref, xh2_hbm)
+    keep(rs2_ref, rs2_hbm)
     second = xhat * g2_ref[...].astype(F32) + s2_ref[...].astype(F32)
     vec_ref[:ROW, :] = mm(second.astype(BF16), wproj_ref[...]).astype(BF16)
     line = iota((EXT, PROJ), 0)
@@ -192,6 +256,8 @@
         tag = jnp.where(line == k, label >> 6, tag)
         tag = jnp.where(line == k + 8, label & 63, tag)
     vec_ref[ROW:, :] = tag.astype(F32).astype(BF16)
+    for copy in kept:
+        copy.wait()
 
 
 def prefix_norms(values, axis):
@@ -428,10 +494,11 @@
 
 
 def feed_back(
-    where_ref, dq_ref, dd_ref, got_ref, xh2_ref, rs2_ref, g2_ref, s2_ref, xh1_ref, g1_ref, s1_ref,
-    act_ref, slope_ref, wproj_ref, wdown_ref, wup_ref,
+    where_ref, dq_ref, dd_ref, got_ref, xh2_ref, rs2_ref, affine_ref, wproj_ref, wdown_ref,
+    slope_ref, act_ref, wup_ref, xh1_ref,
     down_keep, down_send, up_keep, up_send, dfirst_ref, gproj_ref, small_ref, dinner_ref,
 ):
+    g1, s1, g2, s2 = [affine_ref[k : k + 1, :] for k in range(4)]
     is_query, docs_there = where_ref[1] == 0, where_ref[4] == 0
     places = (where_ref[5], where_ref[6], where_ref[7])
     got = got_ref[...].astype(F32)
@@ -442,8 +509,8 @@
     )
     d_proj = d_vec.astype(BF16)
     xhat = xh2_ref[...]
-    gain = g2_ref[...].astype(F32)
-    second = (xhat * gain + s2_ref[...].astype(F32)).astype(BF16)
+    gain = g2
+    second = (xhat * gain + s2).astype(BF16)
     gproj_ref[...] = mm_tn(second, d_proj)
     d_second = mm_nt(d_proj, wproj_ref[...])
     small_ref[...] = jnp.zeros_like(small_ref)
@@ -472,7 +539,7 @@
             )
         d_first = d_first + mm_nt(d_inner, wup_ref[:, cols])
     dfirst_ref[...] = d_first
-    first = (xh1_ref[...] * g1_ref[...].astype(F32) + s1_ref[...].astype(F32)).astype(BF16)
+    first = (xh1_ref[...] * g1 + s1).astype(BF16)
     for c in range(FF // step):
         cols = slice(c * step, (c + 1) * step)
         grad = mm_tn(first, dinner_ref[:, cols]).astype(BF16)
@@ -486,14 +553,14 @@
 
 
 def attend_back(
-    where_ref, dfirst_ref, xh1_ref, rs1_ref, g1_ref, mixed_ref, wout_ref, qkv_ref, probs_ref,
-    rope_ref, x_ref, wqkv_ref, gproj_ref, small_ref,
+    where_ref, dfirst_ref, gproj_ref, small_ref, xh1_ref, rs1_ref, affine_ref, mixed_ref, wout_ref,
+    qkv_ref, probs_ref, rope_ref, x_ref, wqkv_ref,
     keep_one, send_one, keep_two, send_two, tokens_ref, djoined_ref, rest_ref,
 ):
     core, near_place, far_place = where_ref[5], where_ref[6], where_ref[7]
     d_first = dfirst_ref[...]
     xhat = xh1_ref[...]
-    gain = g1_ref[...].astype(F32)
+    gain = affine_ref[0:1, :]
     gain_grad = col_sum(d_first * xhat)
     shift_grad = col_sum(d_first)
     d_sum = norm_back(d_first, xhat, rs1_ref[:, :1], gain)
@@ -612,12 +679,17 @@
     return jax.ShapeDtypeStruct(tuple(shape), dtype)
 
 
-def call(kernel, args, specs, outs, scratch=(), room=24):
+def call(kernel, args, specs, outs, scratch=(), room=24, out_specs=None):
+    spaces = {id(HBM): pltpu.HBM, id(HELD): pltpu.VMEM}
+    args = [
+        pltpu.with_memory_space_constraint(arg, spaces[id(spec)]) if id(spec) in spaces else arg
+        for arg, spec in zip(args, specs)
+    ]
     return pl.pallas_call(
         kernel,
         out_shape=outs,
         in_specs=specs,
-        out_specs=[VMEM] * len(outs),
+        out_specs=out_specs or [VMEM] * len(outs),
         scratch_shapes=list(scratch),
         compiler_params=pltpu.CompilerParams(vmem_limit_bytes=room * MIB),
         cost_estimate=pl.CostEstimate(flops=10**9, bytes_accessed=10**7, transcendentals=0),
@@ -734,27 +806,27 @@
     ).astype(jnp.int32)
     scale = log_scale.reshape(1)
 
-    vec, qkv, rope, probs, mixed, xh1, rs1, act, slope, xh2, rs2 = call(
+    vec, qkv, rope, probs, mixed, xh1, rs1, act, slope, xh2, rs2, affine = call(
         encoder_forward,
         (
             where, doc_lengths, labels, jnp.asarray(rope_table()), tokens[0], qkv_weight[0], qkv_bias,
             out_weight[0], out_bias, first_gain, first_shift, up_weight[0], up_bias,
             down_weight[0], down_bias, second_gain, second_shift, proj_weight[0],
         ),
-        [SMEM] * 3 + [VMEM] * 15,
-        [
-            shape_of((ROW + EXT, PROJ), BF16),
-            shape_of((ROW, 3 * D), BF16),
-            shape_of((ROW, 256)),
-            shape_of((HEADS, ROW, ROW), BF16),
-            shape_of((ROW, D), BF16),
-            shape_of((ROW, D)),
-            shape_of((ROW, 128)),
-            shape_of((ROW, FF), BF16),
-            shape_of((ROW, FF), BF16),
-            shape_of((ROW, D)),
-            shape_of((ROW, 128)),
-        ],
+        [SMEM] * 3 + [HBM] * 15,
+        [shape_of((ROW + EXT, PROJ), BF16)] + [pltpu.HBM(*kind) for kind in KEPT],
+        [pltpu.VMEM(*kind) for kind in KEPT]
+        + [pltpu.SemaphoreType.DMA((len(KEPT) + 6,))]
+        + [
+            pltpu.VMEM(shape, BF16)
+            for shape in (
+                (ROW, 512), (ROW, D), (D, 3 * D), (1, 3 * D), (D, D), (1, D), (1, D), (1, D), (D, FF),
+                (1, FF), (FF, D), (1, D), (1, D), (1, D), (D, PROJ),
+            )
+        ]
+        + [pltpu.SemaphoreType.DMA((15,))],
+        room=40,
+        out_specs=[VMEM] + [HBM] * len(KEPT),
     )
 
     other = swapped(vec, 1, "stream")
@@ -820,25 +892,30 @@
     down_keep, down_send, up_keep, up_send, d_first, gproj, small = call(
         feed_back,
         (
-            where, dq, dd, got, xh2, rs2, second_gain, second_shift, xh1, first_gain, first_shift,
-            act, slope, proj_weight[0], down_weight[0], up_weight[0],
+            where, dq, dd, got, xh2, rs2, affine, proj_weight[0], down_weight[0], slope, act,
+            up_weight[0], xh1,
         ),
-        [SMEM] + [VMEM] * 15,
+        [SMEM] + [VMEM] * 3 + [HELD] * 9,
         [shape_of((blocks // 2, FF // blocks, D), BF16)] * 4
         + [shape_of((ROW, D)), shape_of((D, PROJ)), shape_of((8, D))],
-        [pltpu.VMEM((ROW, FF), BF16)],
+        [
+            pltpu.VMEM((ROW, FF), BF16),
+        ],
     )
     keep_one, send_one, keep_two, send_two, tokens_grad = call(
         attend_back,
         (
-            where, d_first, xh1, rs1, first_gain, mixed, out_weight[0], qkv, probs, rope,
-            tokens[0], qkv_weight[0], gproj, small,
+            where, d_first, gproj, small, xh1, rs1, affine, mixed, out_weight[0], qkv, probs, rope,
+            tokens[0], qkv_weight[0],
         ),
-        [SMEM] + [VMEM] * 13,
+        [SMEM] + [VMEM] * 3 + [HELD] * 10,
         [shape_of((blocks // 2, 3 * D // blocks, D), BF16)] * 2
         + [shape_of((blocks // 2, (REST - 3 * D) // blocks, D), BF16)] * 2
         + [shape_of((ROW, D))],
-        [pltpu.VMEM((ROW, 3 * D), BF16), pltpu.VMEM((REST, D), F32)],
+        [
+            pltpu.VMEM((ROW, 3 * D), BF16),
+            pltpu.VMEM((REST, D), F32),
+        ],
     )
     pieces = [
         Summed(keep, send, masks, others)

time: 185 us -> 166 us (0.90)
  local copies, waits for them, and re-layouts: 21.6 us -> 2.56 us
    unnamed x95 -> x49, local copies, waits for them, and re-layouts: 20.8 us -> 1.72 us
  transfers between devices with their start and end apart: 47 -> 47, of which waited for: 25 -> 25; matrix products, arithmetic and copies ran while one was open for 2% -> 2% of each run, Pallas kernels for 3% -> 4%
where the time goes in v3:
time: 166 us
  waiting for transfers between devices  74.1 us (45%)
  starting transfers between devices  49.1 us (30%)
  Pallas kernels  36.2 us (22%)
  local copies, waits for them, and re-layouts  2.56 us (2%)
  between operations  2.05 us (1%)
  other arithmetic  1.92 us (1%)
    ppermute x32, waiting for transfers between devices, swapped_by_core(): lax.ppermute(value, 'dp', [(k, k ^ masks[k & 1]) for k in range(size)])  51.2 us
    pallas_call x8, Pallas kernels, call(): pl.pallas_call(kernel, out_shape=outs, in_specs=specs, out_specs=out_spec...  36.2 us
    ppermute x32, starting transfers between devices, swapped_by_core(): lax.ppermute(value, 'dp', [(k, k ^ masks[k & 1]) for k in range(size)])  27.6 us
    ppermute x15, waiting for transfers between devices, swapped(): return lax.ppermute(value, axis, [(k, k ^ mask) for k in range(size)])  22.9 us
    ppermute x15, starting transfers between devices, swapped(): return lax.ppermute(value, axis, [(k, k ^ mask) for k in range(size)])  21.5 us
  transfers between devices with their start and end apart: 47, of which 25 were waited for; matrix products, arithmetic and copies ran while one was open for 2% of the time, Pallas kernels for 4%

profile of v3, /device:TPU:0, one launch (start us, length us, event | category | flops | bytes accessed | tf_op | source)
XLA Modules:
  0.0 165.9 jit_solution(7167452847387978640)
XLA Ops:
  2.2 8.9 %shard_map.297 = (bf16[272,128]{1,0:T(8,128)(2,1)S(1)}, bf16[256,1536]{1,0:T(8,128)(2,1)}, f32[256,256]{1,0:T(8,128)}, bf16[8,256,256]{2,1,0:T(8,128)(2,1)}, bf1...) custom-call(s32[8]{0:T(128)S(1)} %stack.39.where_ref, ...), custom_call_target="tpu_custom_call" | custom-call | flops 1000000000 | bytes 10000000 | tf_op jit(solution)/shard_map/pallas_call | solution.py:688
  11.1 3.0 %collective-permute-start = (bf16[272,128]{1,0:T(8,128)(2,1)S(1)}, bf16[272,128]{1,0:T(8,128)(2,1)S(1)}, u32[]{:S(2)}, u32[]{:S(2)}) collective-permute-start(bf16[272,128]{1,0:T(8,128)(2,1)S(1)} %get-tuple-element.132), channel_id=1, source_target_pairs={{0,16},{16,0},{1,17},{17,1},{2,18},{18,2},{3,19},{19,3},{4,20},{20... | collective-permute-start | bytes 208904 | tf_op jit(solution)/shard_map/ppermute | solution.py:717
  14.1 2.3 %collective-permute-done = bf16[272,128]{1,0:T(8,128)(2,1)S(1)} collective-permute-done((bf16[272,128]{1,0:T(8,128)(2,1)S(1)}, bf16[272,128]{1,0:T(8,128)(2,1)S(1)}, u32[]{:S(2)}, u32[]{:S(2)}) %collective-permute-start) | collective-permute-done | bytes 69664 | tf_op jit(solution)/shard_map/ppermute | solution.py:717
  16.4 2.1 %collective-permute-start.1 = (bf16[272,128]{1,0:T(8,128)(2,1)S(1)}, bf16[272,128]{1,0:T(8,128)(2,1)S(1)}, u32[]{:S(2)}, u32[]{:S(2)}) collective-permute-start(bf16[272,128]{1,0:T(8,128)(2,1)S(1)} %broadcast_select_fusion), channel_id=1, source_target_pairs={{0,2},{1,3},{2,0},{3,1},{4,6},{5,7},{6,4},{7,5},{8,10},{9,11},{10,... | collective-permute-start | bytes 208904 | tf_op jit(solution)/shard_map/ppermute | solution.py:717
  18.6 2.7 %collective-permute-start.3 = (bf16[256,128]{1,0:T(8,128)(2,1)S(1)}, bf16[256,128]{1,0:T(8,128)(2,1)S(1)}, u32[]{:S(2)}, u32[]{:S(2)}) collective-permute-start(bf16[256,128]{1,0:T(8,128)(2,1)S(1)} %slice_select_fusion), channel_id=1, source_target_pairs={{0,8},{1,9},{2,10},{3,11},{4,12},{5,13},{6,14},{7,15},{8,0},{9,1},... | collective-permute-start | bytes 196616 | tf_op jit(solution)/shard_map/ppermute | solution.py:717
  21.3 2.5 %collective-permute-done.3 = bf16[256,128]{1,0:T(8,128)(2,1)S(1)} collective-permute-done((bf16[256,128]{1,0:T(8,128)(2,1)S(1)}, bf16[256,128]{1,0:T(8,128)(2,1)S(1)}, u32[]{:S(2)}, u32[]{:S(2)}) %collective-permute-start.3) | collective-permute-done | bytes 65568 | tf_op jit(solution)/shard_map/ppermute | solution.py:717
  23.8 1.6 collective-permute-start.4
  26.1 2.0 %collective-permute-done.4.refs_1_ = bf16[256,128]{1,0:T(8,128)(2,1)S(1)} collective-permute-done((bf16[256,128]{1,0:T(8,128)(2,1)S(1)}, bf16[256,128]{1,0:T(8,128)(2,1)S(1)}, u32[]{:S(2)}, u32[]{:S(2)}) %collective-permute-start.4) | collective-permute-done | bytes 65568 | tf_op jit(solution)/shard_map/ppermute | solution.py:717
  28.2 2.9 %shard_map.298 = (f32[1024,128]{1,0:T(8,128)S(1)}, f32[32,128]{1,0:T(8,128)S(1)}, f32[32,128]{1,0:T(8,128)S(1)}, f32[32,128]{1,0:T(8,128)S(1)}) custom-call(s32[8]{0:T(128)S(1)} %stack.39.where_ref, f32[1]{0:T(128)} %bitcast.23.scale_ref, s32[16,5]{1,0:T(8,128)S(1)} %copy.36.lens_ref, bf16[544,128]{1,0:T(8,128)(2,1)S(1)} %pad_maximum_fusion.near_ref, ...), custom_call_target="tpu_custom_call" | custom-call | flops 1000000000 | bytes 10000000 | tf_op jit(solution)/shard_map/pallas_call | solution.py:688
  32.5 3.6 %collective-permute-done.6 = f32[32,128]{1,0:T(8,128)S(1)} collective-permute-done((f32[32,128]{1,0:T(8,128)S(1)}, f32[32,128]{1,0:T(8,128)S(1)}, u32[]{:S(2)}, u32[]{:S(2)}) %collective-permute-start.6) | collective-permute-done | bytes 16416 | tf_op jit(solution)/shard_map/ppermute | solution.py:717
  36.1 1.5 collective-permute-start.7
  37.6 2.2 %collective-permute-done.7 = f32[32,128]{1,0:T(8,128)S(1)} collective-permute-done((f32[32,128]{1,0:T(8,128)S(1)}, f32[32,128]{1,0:T(8,128)S(1)}, u32[]{:S(2)}, u32[]{:S(2)}) %collective-permute-start.7) | collective-permute-done | bytes 16416 | tf_op jit(solution)/shard_map/ppermute | solution.py:717
  39.9 5.2 %shard_map.299 = (bf16[1024,128]{1,0:T(8,128)(2,1)S(1)}, bf16[512,128]{1,0:T(8,128)(2,1)S(1)}, f32[8,128]{1,0:T(8,128)S(1)}) custom-call(s32[8]{0:T(128)S(1)} %stack.39.where_ref, f32[1]{0:T(128)} %bitcast.24.scale_ref, s32[16,5]{1,0:T(8,128)S(1)} %copy.36.lens_ref, bf16[544,128]{1,0:T(8,128)(2,1)S(1)} %pad_maximum_fusion.near_ref, ...), custom_call_target="tpu_custom_call" | custom-call | flops 1000000000 | bytes 10000000 | tf_op jit(solution)/shard_map/pallas_call | solution.py:688
  45.1 1.6 collective-permute-start.10
  46.8 2.6 %collective-permute-done.10 = bf16[256,128]{1,0:T(8,128)(2,1)S(1)} collective-permute-done((bf16[256,128]{1,0:T(8,128)(2,1)S(1)}, bf16[256,128]{1,0:T(8,128)(2,1)S(1)}, u32[]{:S(2)}, u32[]{:S(2)}) %collective-permute-start.10) | collective-permute-done | bytes 65568 | tf_op jit(solution)/shard_map/ppermute | solution.py:717
  49.4 3.2 %collective-permute-start.11 = (bf16[256,128]{1,0:T(8,128)(2,1)S(1)}, bf16[256,128]{1,0:T(8,128)(2,1)S(1)}, u32[]{:S(2)}, u32[]{:S(2)}) collective-permute-start(bf16[256,128]{1,0:T(8,128)(2,1)S(1)} %add_convert_fusion.27), channel_id=1, source_target_pairs={{0,8},{1,9},{2,10},{3,11},{4,12},{5,13},{6,14},{7,15},{8,0},{9,1},... | collective-permute-start | bytes 196616 | tf_op jit(solution)/shard_map/ppermute | solution.py:717
  53.3 1.6 collective-permute-done.11
  54.9 2.1 %collective-permute-done.9 = bf16[256,128]{1,0:T(8,128)(2,1)S(1)} collective-permute-done((bf16[256,128]{1,0:T(8,128)(2,1)S(1)}, bf16[256,128]{1,0:T(8,128)(2,1)S(1)}, u32[]{:S(2)}, u32[]{:S(2)}) %collective-permute-start.9) | collective-permute-done | bytes 65568 | tf_op jit(solution)/shard_map/ppermute | solution.py:717
  57.1 1.6 collective-permute-start.12
  58.6 2.8 %collective-permute-done.12.got_ref = bf16[256,128]{1,0:T(8,128)(2,1)S(1)} collective-permute-done((bf16[256,128]{1,0:T(8,128)(2,1)S(1)}, bf16[256,128]{1,0:T(8,128)(2,1)S(1)}, u32[]{:S(2)}, u32[]{:S(2)}) %collective-permute-start.12) | collective-permute-done | bytes 65568 | tf_op jit(solution)/shard_map/ppermute | solution.py:717
  61.6 5.1 %shard_map.300 = (bf16[8,128,512]{2,1,0:T(8,128)(2,1)S(1)}, bf16[8,128,512]{2,1,0:T(8,128)(2,1)S(1)}, bf16[8,128,512]{2,1,0:T(8,128)(2,1)S(1)}, bf16[8,128,512]{...) custom-call(s32[8]{0:T(128)S(1)} %stack.39.where_ref, ...), custom_call_target="tpu_custom_call" | custom-call | flops 1000000000 | bytes 10000000 | tf_op jit(solution)/shard_map/pallas_call | solution.py:688
  66.8 5.2 %shard_map.301 = (bf16[8,96,512]{2,1,0:T(8,128)(2,1)S(1)}, bf16[8,96,512]{2,1,0:T(8,128)(2,1)S(1)}, bf16[8,48,512]{2,1,0:T(8,128)(2,1)S(1)}, bf16[8,48,512]{2,1,0:T(8,128)(2,1)S(1)}, f32[256,512]{1,0:T(8,128)}) custom-call(s32[8]{0:T(128)S(1)} %stack.39.where_ref, f32[256,512]{1,0:T(8,128)S(1)} %get-tuple-element.146.dfirst_ref, ...), custom_call_target="tpu_custom_call" | custom-call | flops 1000000000 | bytes 10000000 | tf_op jit(solution)/shard_map/pallas_call | solution.py:688
  73.0 1.6 collective-permute-start.20
  75.5 2.4 %collective-permute-done.17 = bf16[8,48,512]{2,1,0:T(8,128)(2,1)S(1)} collective-permute-done((bf16[8,48,512]{2,1,0:T(8,128)(2,1)S(1)}, bf16[8,48,512]{2,1,0:T(8,128)(2,1)S(1)}, u32[]{:S(2)}, u32[]{:S(2)}) %collective-permute-start.17) | collective-permute-done | bytes 393248 | tf_op jit(solution)/shard_map/ppermute | solution.py:733
  78.9 1.6 collective-permute-start.25
  81.4 1.4 collective-permute-done.14
  82.8 1.3 collective-permute-start.18
  86.2 4.5 %collective-permute-done.18 = bf16[2,96,512]{2,1,0:T(8,128)(2,1)S(1)} collective-permute-done((bf16[2,96,512]{2,1,0:T(8,128)(2,1)S(1)}, bf16[2,96,512]{2,1,0:T(8,128)(2,1)S(1)}, u32[]{:S(2)}, u32[]{:S(2)}) %collective-permute-start.18) | collective-permute-done | bytes 196640 | tf_op jit(solution)/shard_map/ppermute | solution.py:733
  90.8 1.4 collective-permute-start.24
  92.2 1.6 collective-permute-start.30
  95.4 1.3 collective-permute-start.29
  97.2 1.7 %collective-permute-start.28 = (bf16[1,96,512]{2,1,0:T(8,128)(2,1)S(1)}, bf16[1,96,512]{2,1,0:T(8,128)(2,1)S(1)}, u32[]{:S(2)}, u32[]{:S(2)}) collective-permute-start(bf16[1,96,512]{2,1,0:T(8,128)(2,1)S(1)} %add_convert_fusion.21), channel_id=1, source_target_pairs={{0,8},{1,9},{2,10},{3,11},{4,12},{5,13},{6,14},{7,15},{8,0},{9,1},... | collective-permute-start | bytes 294920 | tf_op jit(solution)/shard_map/ppermute | solution.py:733
  98.9 3.1 %collective-permute-done.23 = bf16[4,128,512]{2,1,0:T(8,128)(2,1)S(1)} collective-permute-done((bf16[4,128,512]{2,1,0:T(8,128)(2,1)S(1)}, bf16[4,128,512]{2,1,0:T(8,128)(2,1)S(1)}, u32[]{:S(2)}, u32[]{:S(2)}) %collective-permute-start.23) | collective-permute-done | bytes 524320 | tf_op jit(solution)/shard_map/ppermute | solution.py:733
  103.5 1.4 collective-permute-start.26
  106.5 4.2 %collective-permute-done.27 = bf16[2,128,512]{2,1,0:T(8,128)(2,1)S(1)} collective-permute-done((bf16[2,128,512]{2,1,0:T(8,128)(2,1)S(1)}, bf16[2,128,512]{2,1,0:T(8,128)(2,1)S(1)}, u32[]{:S(2)}, u32[]{:S(2)}) %collective-permute-start.27) | collective-permute-done | bytes 262176 | tf_op jit(solution)/shard_map/ppermute | solution.py:733
  111.6 1.5 collective-permute-start.33
  113.1 1.5 collective-permute-start.35
  115.3 10.9 %collective-permute-done.35 = bf16[1,128,512]{2,1,0:T(8,128)(2,1)S(1)} collective-permute-done((bf16[1,128,512]{2,1,0:T(8,128)(2,1)S(1)}, bf16[1,128,512]{2,1,0:T(8,128)(2,1)S(1)}, u32[]{:S(2)}, u32[]{:S(2)}) %collective-permute-start.35) | collective-permute-done | bytes 131104 | tf_op jit(solution)/shard_map/ppermute | solution.py:733
  126.5 2.9 %collective-permute-start.39 = (bf16[1,128,512]{2,1,0:T(8,128)(2,1)S(1)}, bf16[1,128,512]{2,1,0:T(8,128)(2,1)S(1)}, u32[]{:S(2)}, u32[]{:S(2)}) collective-permute-start(bf16[1,128,512]{2,1,0:T(8,128)(2,1)S(1)} %add_convert_fusion.14), channel_id=1, source_target_pairs={{0,8},{1,9},{2,10},{3,11},{4,12},{5,13},{6,14},{7,15},{8,0},{9,1},... | collective-permute-start | bytes 393224 | tf_op jit(solution)/shard_map/ppermute | solution.py:733
  130.5 7.5 %collective-permute-done.37 = bf16[1,128,512]{2,1,0:T(8,128)(2,1)S(1)} collective-permute-done((bf16[1,128,512]{2,1,0:T(8,128)(2,1)S(1)}, bf16[1,128,512]{2,1,0:T(8,128)(2,1)S(1)}, u32[]{:S(2)}, u32[]{:S(2)}) %collective-permute-start.37) | collective-permute-done | bytes 131104 | tf_op jit(solution)/shard_map/ppermute | solution.py:733
  138.2 2.6 %collective-permute-done.39 = bf16[1,128,512]{2,1,0:T(8,128)(2,1)S(1)} collective-permute-done((bf16[1,128,512]{2,1,0:T(8,128)(2,1)S(1)}, bf16[1,128,512]{2,1,0:T(8,128)(2,1)S(1)}, u32[]{:S(2)}, u32[]{:S(2)}) %collective-permute-start.39) | collective-permute-done | bytes 131104 | tf_op jit(solution)/shard_map/ppermute | solution.py:733
  141.1 3.5 %collective-permute-done.41 = bf16[2,128,512]{2,1,0:T(8,128)(2,1)S(1)} collective-permute-done((bf16[2,128,512]{2,1,0:T(8,128)(2,1)S(1)}, bf16[2,128,512]{2,1,0:T(8,128)(2,1)S(1)}, u32[]{:S(2)}, u32[]{:S(2)}) %collective-permute-start.41) | collective-permute-done | bytes 262176 | tf_op jit(solution)/shard_map/ppermute | solution.py:733
  144.6 1.6 collective-permute-start.44
  146.2 3.0 %shard_map.302 = (f32[512,1536]{1,0:T(8,128)}, f32[512,512]{1,0:T(8,128)}, f32[512,128]{1,0:T(8,128)}, f32[1,1536]{1,0:T(1,128)}, f32[1,512]{1,0:T(1,128)}, /*in...) custom-call(s32[8]{0:T(128)S(1)} %stack.39.where_ref, ...), custom_call_target="tpu_custom_call" | custom-call | flops 1000000000 | bytes 10000000 | tf_op jit(solution)/shard_map/pallas_call | solution.py:688
  150.0 3.8 %collective-permute-done.44 = bf16[4,128,512]{2,1,0:T(8,128)(2,1)S(1)} collective-permute-done((bf16[4,128,512]{2,1,0:T(8,128)(2,1)S(1)}, bf16[4,128,512]{2,1,0:T(8,128)(2,1)S(1)}, u32[]{:S(2)}, u32[]{:S(2)}) %collective-permute-start.44) | collective-permute-done | bytes 524320 | tf_op jit(solution)/shard_map/ppermute | solution.py:733
  154.0 5.5 %collective-permute-done.43 = bf16[4,128,512]{2,1,0:T(8,128)(2,1)S(1)} collective-permute-done((bf16[4,128,512]{2,1,0:T(8,128)(2,1)S(1)}, bf16[4,128,512]{2,1,0:T(8,128)(2,1)S(1)}, u32[]{:S(2)}, u32[]{:S(2)}) %collective-permute-start.43) | collective-permute-done | bytes 524320 | tf_op jit(solution)/shard_map/ppermute | solution.py:733
  160.1 2.9 %shard_map.303 = f32[2048,512]{1,0:T(8,128)} custom-call(s32[8]{0:T(128)S(1)} %stack.39.where_ref, bf16[8,128,512]{2,1,0:T(8,128)(2,1)S(1)} %constant_dynamic-update-slice_fusion.20.near_ref, bf16[8,128,512]{2,1,0:T(8,128)(2,1)S(1)} %collective-permute-done.46.far_ref), custom_call_target="tpu_custom_call" | custom-call | flops 1000000000 | bytes 10000000 | tf_op jit(solution)/shard_map/pallas_call | solution.py:688
  163.0 2.9 %shard_map.304 = f32[512,2048]{1,0:T(8,128)} custom-call(s32[8]{0:T(128)S(1)} %stack.39.where_ref, bf16[8,128,512]{2,1,0:T(8,128)(2,1)S(1)} %constant_dynamic-update-slice_fusion.22.near_ref, bf16[8,128,512]{2,1,0:T(8,128)(2,1)S(1)} %collective-permute-done.45.far_ref), custom_call_target="tpu_custom_call" | custom-call | flops 1000000000 | bytes 10000000 | tf_op jit(solution)/shard_map/pallas_call | solution.py:688
  (148 shorter events, 19.9 us)
Async XLA Ops:
  11.1 5.3 %collective-permute-start = (bf16[272,128]{1,0:T(8,128)(2,1)S(1)}, bf16[272,128]{1,0:T(8,128)(2,1)S(1)}, u32[]{:S(2)}, u32[]{:S(2)}) collective-permute-start(bf16[272,128]{1,0:T(8,128)(2,1)S(1)} %get-tuple-element.132), channel_id=1, source_target_pairs={{0,16},{16,0},{1,17},{17,1},{2,18},{18,2},{3,19},{19,3},{4,20},{20... | collective-permute-start | bytes 208904 | tf_op jit(solution)/shard_map/ppermute | solution.py:717
  16.4 4.8 %collective-permute-start.1 = (bf16[272,128]{1,0:T(8,128)(2,1)S(1)}, bf16[272,128]{1,0:T(8,128)(2,1)S(1)}, u32[]{:S(2)}, u32[]{:S(2)}) collective-permute-start(bf16[272,128]{1,0:T(8,128)(2,1)S(1)} %broadcast_select_fusion), channel_id=1, source_target_pairs={{0,2},{1,3},{2,0},{3,1},{4,6},{5,7},{6,4},{7,5},{8,10},{9,11},{10,... | collective-permute-start | bytes 208904 | tf_op jit(solution)/shard_map/ppermute | solution.py:717
  18.6 5.2 %collective-permute-start.3 = (bf16[256,128]{1,0:T(8,128)(2,1)S(1)}, bf16[256,128]{1,0:T(8,128)(2,1)S(1)}, u32[]{:S(2)}, u32[]{:S(2)}) collective-permute-start(bf16[256,128]{1,0:T(8,128)(2,1)S(1)} %slice_select_fusion), channel_id=1, source_target_pairs={{0,8},{1,9},{2,10},{3,11},{4,12},{5,13},{6,14},{7,15},{8,0},{9,1},... | collective-permute-start | bytes 196616 | tf_op jit(solution)/shard_map/ppermute | solution.py:717
  21.3 6.9 %collective-permute-start.2 = (bf16[544,128]{1,0:T(8,128)(2,1)S(1)}, bf16[544,128]{1,0:T(8,128)(2,1)S(1)}, u32[]{:S(2)}, u32[]{:S(2)}) collective-permute-start(bf16[544,128]{1,0:T(8,128)(2,1)S(1)} %pad_maximum_fusion.near_ref), channel_id=1, source_target_pairs={{0,1},{1,0},{2,3},{3,2},{4,5},{5,4},{6,7},{7,6},{8,9},{9,8},{10,11... | collective-permute-start | bytes 417800 | tf_op jit(solution)/shard_map/ppermute | solution.py:717
  23.8 4.3 %collective-permute-start.4 = (bf16[256,128]{1,0:T(8,128)(2,1)S(1)}, bf16[256,128]{1,0:T(8,128)(2,1)S(1)}, u32[]{:S(2)}, u32[]{:S(2)}) collective-permute-start(bf16[256,128]{1,0:T(8,128)(2,1)S(1)} %broadcast_select_fusion.2.refs_0_), channel_id=1, source_target_pairs={{0,4},{1,5},{2,6},{3,7},{4,0},{5,1},{6,2},{7,3},{8,12},{9,13},{10,... | collective-permute-start | bytes 196616 | tf_op jit(solution)/shard_map/ppermute | solution.py:717
  28.2 33.2 %copy-start.14 = (f32[256,128]{1,0:T(8,128)S(1)}, f32[256,128]{1,0:T(8,128)}, u32[]{:S(2)}) copy-start(f32[256,128]{1,0:T(8,128)} %get-tuple-element.141.rs2_ref) | copy-start | bytes 393220
  31.1 1.2 collective-permute-start.5
  32.4 3.7 %collective-permute-start.6 = (f32[32,128]{1,0:T(8,128)S(1)}, f32[32,128]{1,0:T(8,128)S(1)}, u32[]{:S(2)}, u32[]{:S(2)}) collective-permute-start(f32[32,128]{1,0:T(8,128)S(1)} %add.115), channel_id=1, source_target_pairs={{0,2},{1,3},{2,0},{3,1},{4,6},{5,7},{6,4},{7,5},{8,10},{9,11},{10,... | collective-permute-start | bytes 49160 | tf_op jit(solution)/shard_map/ppermute | solution.py:717
  36.1 3.7 %collective-permute-start.7 = (f32[32,128]{1,0:T(8,128)S(1)}, f32[32,128]{1,0:T(8,128)S(1)}, u32[]{:S(2)}, u32[]{:S(2)}) collective-permute-start(f32[32,128]{1,0:T(8,128)S(1)} %add.116), channel_id=1, source_target_pairs={{0,16},{16,0},{1,17},{17,1},{2,18},{18,2},{3,19},{19,3},{4,20},{20... | collective-permute-start | bytes 49160 | tf_op jit(solution)/shard_map/ppermute | solution.py:717
  45.1 4.3 %collective-permute-start.10 = (bf16[256,128]{1,0:T(8,128)(2,1)S(1)}, bf16[256,128]{1,0:T(8,128)(2,1)S(1)}, u32[]{:S(2)}, u32[]{:S(2)}) collective-permute-start(bf16[256,128]{1,0:T(8,128)(2,1)S(1)} %slice.177), channel_id=1, source_target_pairs={{0,4},{1,5},{2,6},{3,7},{4,0},{5,1},{6,2},{7,3},{8,12},{9,13},{10,... | collective-permute-start | bytes 196616 | tf_op jit(solution)/shard_map/ppermute | solution.py:717
  46.7 5.9 %collective-permute-start.8 = (bf16[512,128]{1,0:T(8,128)(2,1)S(1)}, bf16[512,128]{1,0:T(8,128)(2,1)S(1)}, u32[]{:S(2)}, u32[]{:S(2)}) collective-permute-start(bf16[512,128]{1,0:T(8,128)(2,1)S(1)} %slice.173), channel_id=1, source_target_pairs={{0,1},{1,0},{2,3},{3,2},{4,5},{5,4},{6,7},{7,6},{8,9},{9,8},{10,11... | collective-permute-start | bytes 393224 | tf_op jit(solution)/shard_map/ppermute | solution.py:717
  49.4 5.5 %collective-permute-start.11 = (bf16[256,128]{1,0:T(8,128)(2,1)S(1)}, bf16[256,128]{1,0:T(8,128)(2,1)S(1)}, u32[]{:S(2)}, u32[]{:S(2)}) collective-permute-start(bf16[256,128]{1,0:T(8,128)(2,1)S(1)} %add_convert_fusion.27), channel_id=1, source_target_pairs={{0,8},{1,9},{2,10},{3,11},{4,12},{5,13},{6,14},{7,15},{8,0},{9,1},... | collective-permute-start | bytes 196616 | tf_op jit(solution)/shard_map/ppermute | solution.py:717
  52.7 4.3 %collective-permute-start.9 = (bf16[256,128]{1,0:T(8,128)(2,1)S(1)}, bf16[256,128]{1,0:T(8,128)(2,1)S(1)}, u32[]{:S(2)}, u32[]{:S(2)}) collective-permute-start(bf16[256,128]{1,0:T(8,128)(2,1)S(1)} %slice.231), channel_id=1, source_target_pairs={{0,2},{1,3},{2,0},{3,1},{4,6},{5,7},{6,4},{7,5},{8,10},{9,11},{10,... | collective-permute-start | bytes 196616 | tf_op jit(solution)/shard_map/ppermute | solution.py:717
  57.1 4.3 %collective-permute-start.12 = (bf16[256,128]{1,0:T(8,128)(2,1)S(1)}, bf16[256,128]{1,0:T(8,128)(2,1)S(1)}, u32[]{:S(2)}, u32[]{:S(2)}) collective-permute-start(bf16[256,128]{1,0:T(8,128)(2,1)S(1)} %get-tuple-element.248), channel_id=1, source_target_pairs={{0,16},{16,0},{1,17},{17,1},{2,18},{18,2},{3,19},{19,3},{4,20},{20... | collective-permute-start | bytes 196616 | tf_op jit(solution)/shard_map/ppermute | solution.py:717
  72.0 2.7 %collective-permute-start.13 = (bf16[8,96,512]{2,1,0:T(8,128)(2,1)S(1)}, bf16[8,96,512]{2,1,0:T(8,128)(2,1)S(1)}, u32[]{:S(2)}, u32[]{:S(2)}) collective-permute-start(bf16[8,96,512]{2,1,0:T(8,128)(2,1)S(1)} %get-tuple-element.155), channel_id=1, source_target_pairs={{0,1},{1,0},{2,3},{3,2},{4,5},{5,4},{6,7},{7,6},{8,9},{9,8},{10,11... | collective-permute-start | bytes 2359304 | tf_op jit(solution)/shard_map/ppermute | solution.py:733
  72.0 6.6 %collective-permute-start.16 = (bf16[8,128,512]{2,1,0:T(8,128)(2,1)S(1)}, bf16[8,128,512]{2,1,0:T(8,128)(2,1)S(1)}, u32[]{:S(2)}, u32[]{:S(2)}) collective-permute-start(bf16[8,128,512]{2,1,0:T(8,128)(2,1)S(1)} %get-tuple-element.161), channel_id=1, source_target_pairs={{0,1},{1,0},{2,3},{3,2},{4,5},{5,4},{6,7},{7,6},{8,9},{9,8},{10,11... | collective-permute-start | bytes 3145736 | tf_op jit(solution)/shard_map/ppermute | solution.py:733
  72.5 7.9 %collective-permute-start.15 = (bf16[8,128,512]{2,1,0:T(8,128)(2,1)S(1)}, bf16[8,128,512]{2,1,0:T(8,128)(2,1)S(1)}, u32[]{:S(2)}, u32[]{:S(2)}) collective-permute-start(bf16[8,128,512]{2,1,0:T(8,128)(2,1)S(1)} %get-tuple-element.159), channel_id=1, source_target_pairs={{0,1},{1,0},{2,3},{3,2},{4,5},{5,4},{6,7},{7,6},{8,9},{9,8},{10,11... | collective-permute-start | bytes 3145736 | tf_op jit(solution)/shard_map/ppermute | solution.py:733
  72.5 5.3 %collective-permute-start.17 = (bf16[8,48,512]{2,1,0:T(8,128)(2,1)S(1)}, bf16[8,48,512]{2,1,0:T(8,128)(2,1)S(1)}, u32[]{:S(2)}, u32[]{:S(2)}) collective-permute-start(bf16[8,48,512]{2,1,0:T(8,128)(2,1)S(1)} %get-tuple-element.163), channel_id=1, source_target_pairs={{0,1},{1,0},{2,3},{3,2},{4,5},{5,4},{6,7},{7,6},{8,9},{9,8},{10,11... | collective-permute-start | bytes 1179656 | tf_op jit(solution)/shard_map/ppermute | solution.py:733
  73.0 19.2 %collective-permute-start.20 = (f32[8,128]{1,0:T(8,128)S(1)}, f32[8,128]{1,0:T(8,128)S(1)}, u32[]{:S(2)}, u32[]{:S(2)}) collective-permute-start(f32[8,128]{1,0:T(8,128)S(1)} %get-tuple-element.176), channel_id=1, source_target_pairs={{0,4},{1,5},{2,6},{3,7},{4,0},{5,1},{6,2},{7,3},{8,12},{9,13},{10,... | collective-permute-start | bytes 12296 | tf_op jit(solution)/shard_map/ppermute | solution.py:717
  74.9 7.8 %collective-permute-start.14 = (bf16[4,96,512]{2,1,0:T(8,128)(2,1)S(1)}, bf16[4,96,512]{2,1,0:T(8,128)(2,1)S(1)}, u32[]{:S(2)}, u32[]{:S(2)}) collective-permute-start(bf16[4,96,512]{2,1,0:T(8,128)(2,1)S(1)} %get-tuple-element.255), channel_id=1, source_target_pairs={{0,2},{1,5},{2,0},{3,7},{4,6},{5,1},{6,4},{7,3},{8,10},{9,13},{10,... | collective-permute-start | bytes 1179656 | tf_op jit(solution)/shard_map/ppermute | solution.py:733
  77.9 7.1 %collective-permute-start.19 = (bf16[4,48,512]{2,1,0:T(8,128)(2,1)S(1)}, bf16[4,48,512]{2,1,0:T(8,128)(2,1)S(1)}, u32[]{:S(2)}, u32[]{:S(2)}) collective-permute-start(bf16[4,48,512]{2,1,0:T(8,128)(2,1)S(1)} %get-tuple-element.262), channel_id=1, source_target_pairs={{0,2},{1,5},{2,0},{3,7},{4,6},{5,1},{6,4},{7,3},{8,10},{9,13},{10,... | collective-permute-start | bytes 589832 | tf_op jit(solution)/shard_map/ppermute | solution.py:733
  78.9 16.3 %collective-permute-start.25 = (bf16[4,128,512]{2,1,0:T(8,128)(2,1)S(1)}, bf16[4,128,512]{2,1,0:T(8,128)(2,1)S(1)}, u32[]{:S(2)}, u32[]{:S(2)}) collective-permute-start(bf16[4,128,512]{2,1,0:T(8,128)(2,1)S(1)} %get-tuple-element.252), channel_id=1, source_target_pairs={{0,2},{1,5},{2,0},{3,7},{4,6},{5,1},{6,4},{7,3},{8,10},{9,13},{10,... | collective-permute-start | bytes 1572872 | tf_op jit(solution)/shard_map/ppermute | solution.py:733
  80.8 21.3 %collective-permute-start.23 = (bf16[4,128,512]{2,1,0:T(8,128)(2,1)S(1)}, bf16[4,128,512]{2,1,0:T(8,128)(2,1)S(1)}, u32[]{:S(2)}, u32[]{:S(2)}) collective-permute-start(bf16[4,128,512]{2,1,0:T(8,128)(2,1)S(1)} %get-tuple-element.254), channel_id=1, source_target_pairs={{0,2},{1,5},{2,0},{3,7},{4,6},{5,1},{6,4},{7,3},{8,10},{9,13},{10,... | collective-permute-start | bytes 1572872 | tf_op jit(solution)/shard_map/ppermute | solution.py:733
  82.8 7.9 %collective-permute-start.18 = (bf16[2,96,512]{2,1,0:T(8,128)(2,1)S(1)}, bf16[2,96,512]{2,1,0:T(8,128)(2,1)S(1)}, u32[]{:S(2)}, u32[]{:S(2)}) collective-permute-start(bf16[2,96,512]{2,1,0:T(8,128)(2,1)S(1)} %get-tuple-element.263), channel_id=1, source_target_pairs={{0,4},{1,3},{2,6},{3,1},{4,0},{5,7},{6,2},{7,5},{8,12},{9,11},{10,... | collective-permute-start | bytes 589832 | tf_op jit(solution)/shard_map/ppermute | solution.py:733
  85.1 8.8 %collective-permute-start.21 = (bf16[2,48,512]{2,1,0:T(8,128)(2,1)S(1)}, bf16[2,48,512]{2,1,0:T(8,128)(2,1)S(1)}, u32[]{:S(2)}, u32[]{:S(2)}) collective-permute-start(bf16[2,48,512]{2,1,0:T(8,128)(2,1)S(1)} %get-tuple-element.272), channel_id=1, source_target_pairs={{0,4},{1,3},{2,6},{3,1},{4,0},{5,7},{6,2},{7,5},{8,12},{9,11},{10,... | collective-permute-start | bytes 294920 | tf_op jit(solution)/shard_map/ppermute | solution.py:733
  90.8 6.4 %collective-permute-start.24 = (bf16[1,96,512]{2,1,0:T(8,128)(2,1)S(1)}, bf16[1,96,512]{2,1,0:T(8,128)(2,1)S(1)}, u32[]{:S(2)}, u32[]{:S(2)}) collective-permute-start(bf16[1,96,512]{2,1,0:T(8,128)(2,1)S(1)} %get-tuple-element.270), channel_id=1, source_target_pairs={{0,8},{1,9},{2,10},{3,11},{4,12},{5,13},{6,14},{7,15},{8,0},{9,1},... | collective-permute-start | bytes 294920 | tf_op jit(solution)/shard_map/ppermute | solution.py:733
  92.2 22.4 %collective-permute-start.30 = (f32[8,128]{1,0:T(8,128)S(1)}, f32[8,128]{1,0:T(8,128)S(1)}, u32[]{:S(2)}, u32[]{:S(2)}) collective-permute-start(f32[8,128]{1,0:T(8,128)S(1)} %add.132), channel_id=1, source_target_pairs={{0,8},{1,9},{2,10},{3,11},{4,12},{5,13},{6,14},{7,15},{8,0},{9,1},... | collective-permute-start | bytes 12296 | tf_op jit(solution)/shard_map/ppermute | solution.py:717
  94.0 9.5 %collective-permute-start.22 = (bf16[1,48,512]{2,1,0:T(8,128)(2,1)S(1)}, bf16[1,48,512]{2,1,0:T(8,128)(2,1)S(1)}, u32[]{:S(2)}, u32[]{:S(2)}) collective-permute-start(bf16[1,48,512]{2,1,0:T(8,128)(2,1)S(1)} %get-tuple-element.273), channel_id=1, source_target_pairs={{0,8},{1,9},{2,10},{3,11},{4,12},{5,13},{6,14},{7,15},{8,0},{9,1},... | collective-permute-start | bytes 147464 | tf_op jit(solution)/shard_map/ppermute | solution.py:733
  95.4 9.8 %collective-permute-start.29 = (bf16[2,128,512]{2,1,0:T(8,128)(2,1)S(1)}, bf16[2,128,512]{2,1,0:T(8,128)(2,1)S(1)}, u32[]{:S(2)}, u32[]{:S(2)}) collective-permute-start(bf16[2,128,512]{2,1,0:T(8,128)(2,1)S(1)} %get-tuple-element.258), channel_id=1, source_target_pairs={{0,4},{1,3},{2,6},{3,1},{4,0},{5,7},{6,2},{7,5},{8,12},{9,11},{10,... | collective-permute-start | bytes 786440 | tf_op jit(solution)/shard_map/ppermute | solution.py:733
  97.2 8.0 %collective-permute-start.28 = (bf16[1,96,512]{2,1,0:T(8,128)(2,1)S(1)}, bf16[1,96,512]{2,1,0:T(8,128)(2,1)S(1)}, u32[]{:S(2)}, u32[]{:S(2)}) collective-permute-start(bf16[1,96,512]{2,1,0:T(8,128)(2,1)S(1)} %add_convert_fusion.21), channel_id=1, source_target_pairs={{0,8},{1,9},{2,10},{3,11},{4,12},{5,13},{6,14},{7,15},{8,0},{9,1},... | collective-permute-start | bytes 294920 | tf_op jit(solution)/shard_map/ppermute | solution.py:733
  102.2 8.5 %collective-permute-start.27 = (bf16[2,128,512]{2,1,0:T(8,128)(2,1)S(1)}, bf16[2,128,512]{2,1,0:T(8,128)(2,1)S(1)}, u32[]{:S(2)}, u32[]{:S(2)}) collective-permute-start(bf16[2,128,512]{2,1,0:T(8,128)(2,1)S(1)} %get-tuple-element.260), channel_id=1, source_target_pairs={{0,4},{1,3},{2,6},{3,1},{4,0},{5,7},{6,2},{7,5},{8,12},{9,11},{10,... | collective-permute-start | bytes 786440 | tf_op jit(solution)/shard_map/ppermute | solution.py:733
  103.5 7.3 %collective-permute-start.26 = (bf16[1,48,512]{2,1,0:T(8,128)(2,1)S(1)}, bf16[1,48,512]{2,1,0:T(8,128)(2,1)S(1)}, u32[]{:S(2)}, u32[]{:S(2)}) collective-permute-start(bf16[1,48,512]{2,1,0:T(8,128)(2,1)S(1)} %add_convert_fusion.29), channel_id=1, source_target_pairs={{0,8},{1,9},{2,10},{3,11},{4,12},{5,13},{6,14},{7,15},{8,0},{9,1},... | collective-permute-start | bytes 147464 | tf_op jit(solution)/shard_map/ppermute | solution.py:733
  105.2 9.3 %collective-permute-start.31 = (bf16[2,96,512]{2,1,0:T(8,128)(2,1)S(1)}, bf16[2,96,512]{2,1,0:T(8,128)(2,1)S(1)}, u32[]{:S(2)}, u32[]{:S(2)}) collective-permute-start(bf16[2,96,512]{2,1,0:T(8,128)(2,1)S(1)} %constant_dynamic-update-slice_fusion), channel_id=1, source_target_pairs={{0,4},{1,3},{2,6},{3,1},{4,0},{5,7},{6,2},{7,5},{8,12},{9,11},{10,... | collective-permute-start | bytes 589832 | tf_op jit(solution)/shard_map/ppermute | solution.py:733
  110.8 15.4 %collective-permute-start.34 = (bf16[2,48,512]{2,1,0:T(8,128)(2,1)S(1)}, bf16[2,48,512]{2,1,0:T(8,128)(2,1)S(1)}, u32[]{:S(2)}, u32[]{:S(2)}) collective-permute-start(bf16[2,48,512]{2,1,0:T(8,128)(2,1)S(1)} %constant_dynamic-update-slice_fusion.2), channel_id=1, source_target_pairs={{0,4},{1,3},{2,6},{3,1},{4,0},{5,7},{6,2},{7,5},{8,12},{9,11},{10,... | collective-permute-start | bytes 294920 | tf_op jit(solution)/shard_map/ppermute | solution.py:733
  111.6 14.6 %collective-permute-start.33 = (bf16[1,128,512]{2,1,0:T(8,128)(2,1)S(1)}, bf16[1,128,512]{2,1,0:T(8,128)(2,1)S(1)}, u32[]{:S(2)}, u32[]{:S(2)}) collective-permute-start(bf16[1,128,512]{2,1,0:T(8,128)(2,1)S(1)} %get-tuple-element.268), channel_id=1, source_target_pairs={{0,8},{1,9},{2,10},{3,11},{4,12},{5,13},{6,14},{7,15},{8,0},{9,1},... | collective-permute-start | bytes 393224 | tf_op jit(solution)/shard_map/ppermute | solution.py:733
  113.1 13.1 %collective-permute-start.35 = (bf16[1,128,512]{2,1,0:T(8,128)(2,1)S(1)}, bf16[1,128,512]{2,1,0:T(8,128)(2,1)S(1)}, u32[]{:S(2)}, u32[]{:S(2)}) collective-permute-start(bf16[1,128,512]{2,1,0:T(8,128)(2,1)S(1)} %get-tuple-element.266), channel_id=1, source_target_pairs={{0,8},{1,9},{2,10},{3,11},{4,12},{5,13},{6,14},{7,15},{8,0},{9,1},... | collective-permute-start | bytes 393224 | tf_op jit(solution)/shard_map/ppermute | solution.py:733
  114.6 11.7 %collective-permute-start.32 = (bf16[4,96,512]{2,1,0:T(8,128)(2,1)S(1)}, bf16[4,96,512]{2,1,0:T(8,128)(2,1)S(1)}, u32[]{:S(2)}, u32[]{:S(2)}) collective-permute-start(bf16[4,96,512]{2,1,0:T(8,128)(2,1)S(1)} %constant_dynamic-update-slice_fusion.4), channel_id=1, source_target_pairs={{0,2},{1,5},{2,0},{3,7},{4,6},{5,1},{6,4},{7,3},{8,10},{9,13},{10,... | collective-permute-start | bytes 1179656 | tf_op jit(solution)/shard_map/ppermute | solution.py:733
  126.4 11.8 %collective-permute-start.36 = (bf16[8,96,512]{2,1,0:T(8,128)(2,1)S(1)}, bf16[8,96,512]{2,1,0:T(8,128)(2,1)S(1)}, u32[]{:S(2)}, u32[]{:S(2)}) collective-permute-start(bf16[8,96,512]{2,1,0:T(8,128)(2,1)S(1)} %constant_dynamic-update-slice_fusion.8.near_one), channel_id=1, source_target_pairs={{0,1},{1,0},{2,3},{3,2},{4,5},{5,4},{6,7},{7,6},{8,9},{9,8},{10,11... | collective-permute-start | bytes 2359304 | tf_op jit(solution)/shard_map/ppermute | solution.py:733
  126.5 11.6 %collective-permute-start.37 = (bf16[1,128,512]{2,1,0:T(8,128)(2,1)S(1)}, bf16[1,128,512]{2,1,0:T(8,128)(2,1)S(1)}, u32[]{:S(2)}, u32[]{:S(2)}) collective-permute-start(bf16[1,128,512]{2,1,0:T(8,128)(2,1)S(1)} %add_convert_fusion.15), channel_id=1, source_target_pairs={{0,8},{1,9},{2,10},{3,11},{4,12},{5,13},{6,14},{7,15},{8,0},{9,1},... | collective-permute-start | bytes 393224 | tf_op jit(solution)/shard_map/ppermute | solution.py:733
  126.5 14.3 %collective-permute-start.39 = (bf16[1,128,512]{2,1,0:T(8,128)(2,1)S(1)}, bf16[1,128,512]{2,1,0:T(8,128)(2,1)S(1)}, u32[]{:S(2)}, u32[]{:S(2)}) collective-permute-start(bf16[1,128,512]{2,1,0:T(8,128)(2,1)S(1)} %add_convert_fusion.14), channel_id=1, source_target_pairs={{0,8},{1,9},{2,10},{3,11},{4,12},{5,13},{6,14},{7,15},{8,0},{9,1},... | collective-permute-start | bytes 393224 | tf_op jit(solution)/shard_map/ppermute | solution.py:733
  129.5 11.4 %collective-permute-start.38 = (bf16[4,48,512]{2,1,0:T(8,128)(2,1)S(1)}, bf16[4,48,512]{2,1,0:T(8,128)(2,1)S(1)}, u32[]{:S(2)}, u32[]{:S(2)}) collective-permute-start(bf16[4,48,512]{2,1,0:T(8,128)(2,1)S(1)} %constant_dynamic-update-slice_fusion.6), channel_id=1, source_target_pairs={{0,2},{1,5},{2,0},{3,7},{4,6},{5,1},{6,4},{7,3},{8,10},{9,13},{10,... | collective-permute-start | bytes 589832 | tf_op jit(solution)/shard_map/ppermute | solution.py:733
  138.1 6.4 %collective-permute-start.41 = (bf16[2,128,512]{2,1,0:T(8,128)(2,1)S(1)}, bf16[2,128,512]{2,1,0:T(8,128)(2,1)S(1)}, u32[]{:S(2)}, u32[]{:S(2)}) collective-permute-start(bf16[2,128,512]{2,1,0:T(8,128)(2,1)S(1)} %constant_dynamic-update-slice_fusion.10), channel_id=1, source_target_pairs={{0,4},{1,3},{2,6},{3,1},{4,0},{5,7},{6,2},{7,5},{8,12},{9,11},{10,... | collective-permute-start | bytes 786440 | tf_op jit(solution)/shard_map/ppermute | solution.py:733
  140.9 5.3 %collective-permute-start.40 = (bf16[8,48,512]{2,1,0:T(8,128)(2,1)S(1)}, bf16[8,48,512]{2,1,0:T(8,128)(2,1)S(1)}, u32[]{:S(2)}, u32[]{:S(2)}) collective-permute-start(bf16[8,48,512]{2,1,0:T(8,128)(2,1)S(1)} %constant_dynamic-update-slice_fusion.14.near_two), channel_id=1, source_target_pairs={{0,1},{1,0},{2,3},{3,2},{4,5},{5,4},{6,7},{7,6},{8,9},{9,8},{10,11... | collective-permute-start | bytes 1179656 | tf_op jit(solution)/shard_map/ppermute | solution.py:733
  141.0 8.2 %collective-permute-start.42 = (bf16[2,128,512]{2,1,0:T(8,128)(2,1)S(1)}, bf16[2,128,512]{2,1,0:T(8,128)(2,1)S(1)}, u32[]{:S(2)}, u32[]{:S(2)}) collective-permute-start(bf16[2,128,512]{2,1,0:T(8,128)(2,1)S(1)} %constant_dynamic-update-slice_fusion.12), channel_id=1, source_target_pairs={{0,4},{1,3},{2,6},{3,1},{4,0},{5,7},{6,2},{7,5},{8,12},{9,11},{10,... | collective-permute-start | bytes 786440 | tf_op jit(solution)/shard_map/ppermute | solution.py:733
  144.6 9.2 %collective-permute-start.44 = (bf16[4,128,512]{2,1,0:T(8,128)(2,1)S(1)}, bf16[4,128,512]{2,1,0:T(8,128)(2,1)S(1)}, u32[]{:S(2)}, u32[]{:S(2)}) collective-permute-start(bf16[4,128,512]{2,1,0:T(8,128)(2,1)S(1)} %constant_dynamic-update-slice_fusion.16), channel_id=1, source_target_pairs={{0,2},{1,5},{2,0},{3,7},{4,6},{5,1},{6,4},{7,3},{8,10},{9,13},{10,... | collective-permute-start | bytes 1572872 | tf_op jit(solution)/shard_map/ppermute | solution.py:733
  149.3 10.1 %collective-permute-start.43 = (bf16[4,128,512]{2,1,0:T(8,128)(2,1)S(1)}, bf16[4,128,512]{2,1,0:T(8,128)(2,1)S(1)}, u32[]{:S(2)}, u32[]{:S(2)}) collective-permute-start(bf16[4,128,512]{2,1,0:T(8,128)(2,1)S(1)} %constant_dynamic-update-slice_fusion.18), channel_id=1, source_target_pairs={{0,2},{1,5},{2,0},{3,7},{4,6},{5,1},{6,4},{7,3},{8,10},{9,13},{10,... | collective-permute-start | bytes 1572872 | tf_op jit(solution)/shard_map/ppermute | solution.py:733
  153.9 6.2 %collective-permute-start.46 = (bf16[8,128,512]{2,1,0:T(8,128)(2,1)S(1)}, bf16[8,128,512]{2,1,0:T(8,128)(2,1)S(1)}, u32[]{:S(2)}, u32[]{:S(2)}) collective-permute-start(bf16[8,128,512]{2,1,0:T(8,128)(2,1)S(1)} %constant_dynamic-update-slice_fusion.20.near_ref), channel_id=1, source_target_pairs={{0,1},{1,0},{2,3},{3,2},{4,5},{5,4},{6,7},{7,6},{8,9},{9,8},{10,11... | collective-permute-start | bytes 3145736 | tf_op jit(solution)/shard_map/ppermute | solution.py:733
  159.5 3.5 %collective-permute-start.45 = (bf16[8,128,512]{2,1,0:T(8,128)(2,1)S(1)}, bf16[8,128,512]{2,1,0:T(8,128)(2,1)S(1)}, u32[]{:S(2)}, u32[]{:S(2)}) collective-permute-start(bf16[8,128,512]{2,1,0:T(8,128)(2,1)S(1)} %constant_dynamic-update-slice_fusion.22.near_ref), channel_id=1, source_target_pairs={{0,1},{1,0},{2,3},{3,2},{4,5},{5,4},{6,7},{7,6},{8,9},{9,8},{10,11... | collective-permute-start | bytes 3145736 | tf_op jit(solution)/shard_map/ppermute | solution.py:733
  (17 other events, 291.2 us)

commit v4 on v3

--- a/solution.py
+++ b/solution.py
@@ -28,8 +28,22 @@
 F32 = jnp.float32
 BF16 = jnp.bfloat16
 REST = 2304
-FINAL = ((0,), (1,), (2, 3))
-ORDER = [4, 2, 3, 0, 1, 2, 3, 2, 4, 3, 0, 2, 1, 3, 0, 2, 1, 3, 4, 2, 0, 3, 1, 2, 0, 2, 1, 3, 0, 3, 12, 1, 0, 1, 0, 10, 1, 11]
+SHARE = 32
+DOWN = FF // 16
+HEAD = 80
+TAIL = DOWN - HEAD
+FIRST = DOWN + HEAD
+SECOND = REST // 16 + TAIL
+CIRCLE = (0, 2, 4, 6, 7, 5, 3, 1)
+RING = len(CIRCLE)
+GROUPS = ((0, 1, 2, 6, 7), (3, 4, 5))
+STEP_COST = 3 * 10**7
+ROUND = (("step", 0), ("step", 1))
+ORDER = (
+    (("open", 0), ("open", 1), ("total", 0), ("total", 1)) + ROUND * 6
+    + (("share0", 0), ("share0", 1), ("near", 0)) + ROUND + (("far", 0),) + ROUND
+    + (("share1", 0), ("share1", 1), ("near", 1), ("far", 1))
+)
 MIB = 1024 * 1024
 
 VMEM = pl.BlockSpec(memory_space=pltpu.VMEM)
@@ -400,8 +414,8 @@
     masks, lanes, total_queries, where_ref, scale_ref, lens_ref, near_ref, far_ref, totals_ref,
     el_ref, hot_ref, stats_ref, *refs
 ):
-    doc_refs = refs[:-8]
-    dq_ref, dd_ref, loss_ref, turn_ref, unit_ref, qt_ref, dot_ref, dt_ref = refs[-8:]
+    doc_refs = refs[:-9]
+    dq_ref, send_ref, keep_ref, loss_ref, turn_ref, unit_ref, qt_ref, dot_ref, dt_ref = refs[-9:]
     base, near_at = where_ref[2], where_ref[3]
     temper = SHARPNESS * LOG2E
     queries = load_queries(near_ref, far_ref)
@@ -439,11 +453,12 @@
         loss = loss + (jnp.log(whole) - picked)
         moved = moved + (weighted / whole - picked)
     line = iota((8, 128), 0)
-    loss_ref[...] = jnp.where(
+    loss = jnp.where(
         line == 0,
         jnp.sum(loss, axis=0, keepdims=True) * (1.0 / total_queries),
         jnp.where(line == 1, jnp.sum(moved, axis=0, keepdims=True) * (1.0 / total_queries), 0.0),
     )
+    loss_ref[...] = loss
     scale = jnp.exp(jnp.full((8, lanes), scale_ref[0], F32))[:1]
     coeff = (el_ref[...] / sums - hot_ref[...]) * (scale * (1.0 / (QLEN * total_queries)))
     coeff = jnp.broadcast_to(coeff[:, None, :], (groups * 8, QLEN, lanes)).reshape(count, lanes)
@@ -475,32 +490,77 @@
         along = jnp.sum(grad * unit, axis=0, keepdims=True)
         total = total + inv_d[m] * (grad - unit * along)
     for p in range(doc_rows):
-        dd_ref[p * ROW : (p + 1) * ROW, :] = total[:, p * ROW : (p + 1) * ROW].T.astype(BF16)
-
-
-def store_block(refs, block, places, value):
-    keep_ref, send_ref = refs
-    core, near_place, far_place = places
-    half = keep_ref.shape[0]
-    mine = core == block // half
+        ref, at = (keep_ref, p) if p < doc_rows // 2 else (send_ref, p - doc_rows // 2)
+        ref[at * ROW : (at + 1) * ROW, :] = total[:, p * ROW : (p + 1) * ROW].T.astype(BF16)
+    send_ref[doc_rows // 2 * ROW :, :] = packed_loss(loss)
+
+
+def packed_loss(loss):
+    high = loss.astype(BF16)
+    rest = loss - high.astype(F32)
+    middle = rest.astype(BF16)
+    low = rest - middle.astype(F32)
+    lane = iota(loss.shape, 1)
+    packed = jnp.where(lane == 0, high.astype(F32), jnp.where(lane == 1, middle.astype(F32), low))
+    return jnp.concatenate([packed, jnp.zeros_like(packed)], axis=0).astype(BF16)
+
+
+def loss_of(packed):
+    lines = packed.astype(F32)[:8, :]
+    return jnp.sum(jnp.where(iota(lines.shape, 1) < 3, lines, 0.0), axis=1, keepdims=True)
+
+
+def fold_docs(keep_ref, got_ref, loss_ref, *outs):
+    rows = keep_ref.shape[0]
+    loss = loss_ref[...] + loss_of(got_ref[rows:, :])
+    total = (keep_ref[...].astype(F32) + got_ref[:rows, :].astype(F32)).astype(BF16)
+    outs[-1][...] = loss
+    if rows > ROW:
+        outs[0][: rows // 2, :] = total[rows // 2 :, :]
+        outs[0][rows // 2 :, :] = packed_loss(loss)
+        outs[1][...] = total[: rows // 2, :]
+    else:
+        outs[0][:rows, :] = total
+        outs[0][rows:, :] = packed_loss(loss)
+
+
+def last_docs(where_ref, near_ref, got_ref, loss_ref, dq_ref, dd_ref, send_ref, sum_ref):
+    sum_ref[...] = loss_ref[...] + loss_of(got_ref[ROW:, :])
+    total = (near_ref[:ROW, :].astype(F32) + got_ref[:ROW, :].astype(F32)).astype(BF16)
+    dd_ref[...] = total
+    send_ref[...] = jnp.where(where_ref[1] == 0, total, dq_ref[...])
+
+
+def turn(core, place, block):
+    return jnp.where(core == 0, place - block, block - place) & (RING - 1)
+
+
+def block_at(core, place, distance):
+    return jnp.where(core == 0, place - distance, place + distance) & (RING - 1)
+
+
+def store_block(keep_ref, send_ref, rows, block, places, value):
+    core, place = places
+    mine = core == block // RING
+    at = turn(block // RING, place, block % RING)
 
     @pl.when(mine)
     def _():
-        keep_ref[(block % half) ^ near_place] = value
+        keep_ref[at, rows, :] = value
 
     @pl.when(jnp.logical_not(mine))
     def _():
-        send_ref[(block % half) ^ far_place] = value
+        send_ref[at, rows, :] = value
 
 
 def feed_back(
     where_ref, dq_ref, dd_ref, got_ref, xh2_ref, rs2_ref, affine_ref, wproj_ref, wdown_ref,
     slope_ref, act_ref, wup_ref, xh1_ref,
-    down_keep, down_send, up_keep, up_send, dfirst_ref, gproj_ref, small_ref, dinner_ref,
+    keep_ref, send_ref, tail_keep, tail_send, dfirst_ref, gproj_ref, small_ref, dinner_ref,
 ):
     g1, s1, g2, s2 = [affine_ref[k : k + 1, :] for k in range(4)]
     is_query, docs_there = where_ref[1] == 0, where_ref[4] == 0
-    places = (where_ref[5], where_ref[6], where_ref[7])
+    places = (where_ref[5], where_ref[6])
     got = got_ref[...].astype(F32)
     d_vec = jnp.where(
         is_query,
@@ -520,8 +580,6 @@
     d_branch = d_sum.astype(BF16)
     small_ref[4:5, :] = col_sum(d_branch.astype(F32))
     step = 512
-    blocks = 2 * down_keep.shape[0]
-    size = down_keep.shape[1]
     d_first = d_sum
     for c in range(FF // step):
         cols = slice(c * step, (c + 1) * step)
@@ -530,12 +588,10 @@
         dinner_ref[:, cols] = d_inner
         small_ref[c : c + 1, :] = col_sum(d_inner.astype(F32))
         grad = mm_tn(act_ref[:, cols], d_branch).astype(BF16)
-        for k in range(step // size):
+        for k in range(step // DOWN):
             store_block(
-                (down_keep, down_send),
-                c * (step // size) + k,
-                places,
-                grad[k * size : (k + 1) * size, :],
+                keep_ref, send_ref, slice(0, DOWN), c * (step // DOWN) + k, places,
+                grad[k * DOWN : (k + 1) * DOWN, :],
             )
         d_first = d_first + mm_nt(d_inner, wup_ref[:, cols])
     dfirst_ref[...] = d_first
@@ -543,21 +599,24 @@
     for c in range(FF // step):
         cols = slice(c * step, (c + 1) * step)
         grad = mm_tn(first, dinner_ref[:, cols]).astype(BF16)
-        for k in range(D // size):
+        for k in range(D // DOWN):
+            block = c * (D // DOWN) + k
+            start = k * DOWN
             store_block(
-                (up_keep, up_send),
-                c * (D // size) + k,
-                places,
-                grad[k * size : (k + 1) * size, :],
+                keep_ref, send_ref, slice(DOWN, FIRST), block, places, grad[start : start + HEAD, :]
             )
+            store_block(
+                tail_keep, tail_send, slice(0, TAIL), block, places,
+                grad[start + HEAD : start + DOWN, :],
+            )
 
 
 def attend_back(
-    where_ref, dfirst_ref, gproj_ref, small_ref, xh1_ref, rs1_ref, affine_ref, mixed_ref, wout_ref,
+    where_ref, dfirst_ref, gproj_ref, small_ref, tail_keep, tail_send, xh1_ref, rs1_ref, affine_ref, mixed_ref, wout_ref,
     qkv_ref, probs_ref, rope_ref, x_ref, wqkv_ref,
-    keep_one, send_one, keep_two, send_two, tokens_ref, djoined_ref, rest_ref,
+    keep_ref, send_ref, tokens_ref, djoined_ref, rest_ref,
 ):
-    core, near_place, far_place = where_ref[5], where_ref[6], where_ref[7]
+    core, place = where_ref[5], where_ref[6]
     d_first = dfirst_ref[...]
     xhat = xh1_ref[...]
     gain = affine_ref[0:1, :]
@@ -601,7 +660,7 @@
         djoined_ref[:, 2 * D + g * 128 : 2 * D + (g + 1) * 128] = d_v.astype(BF16)
     x = x_ref[...]
     tokens = d_sum
-    rest_ref[4 * D + 128 :, :] = jnp.zeros((REST - 4 * D - 128, D), F32)
+    rest_ref[4 * D :, :] = jnp.zeros((8 * 2 * RING, D), F32)
     smalls = []
     for c in range(3):
         cols = slice(c * D, (c + 1) * D)
@@ -610,76 +669,121 @@
         smalls.append(col_sum(d_part.astype(F32)))
         tokens = tokens + mm_nt(d_part, wqkv_ref[:, cols])
     tokens_ref[...] = tokens
-    for k in range(4):
-        rest_ref[4 * D : 4 * D + 128, k * 128 : (k + 1) * 128] = gproj_ref[
-            k * 128 : (k + 1) * 128, :
-        ]
     smalls += [bias_out, gain_grad, shift_grad] + [small_ref[k : k + 1, :] for k in range(7)]
-    smalls += [jnp.zeros((EXT - len(smalls), D), F32)]
-    rest_ref[4 * D + 128 : 4 * D + 128 + EXT, :] = jnp.concatenate(smalls, axis=0)
-    first = 0
-    for keep_ref, send_ref in ((keep_one, send_one), (keep_two, send_two)):
-        half, size = keep_ref.shape[0], keep_ref.shape[1]
-        for p in range(half):
-            for ref, owner, place in ((keep_ref, core, near_place), (send_ref, 1 - core, far_place)):
-                block = owner * half + (p ^ place)
-                start = pl.multiple_of(first + block * size, 8)
-                ref[p] = rest_ref[pl.ds(start, size), :].astype(BF16)
-        first += 2 * half * size
-
-
-def spread_out(columns, where_ref, near_ref, far_ref, out_ref):
-    core, near_place, far_place = where_ref[5], where_ref[6], where_ref[7]
-    half, size, width = near_ref.shape
-    per_column = 2 * half // columns
-    for p in range(half):
-        for ref, owner, place in ((near_ref, core, near_place), (far_ref, 1 - core, far_place)):
-            block = owner * half + (p ^ place)
-            start = pl.multiple_of((block % per_column) * size, 8)
-            left = pl.multiple_of((block // per_column) * width, 128)
-            out_ref[pl.ds(start, size), pl.ds(left, width)] = ref[p].astype(F32)
-
-
-def spread_rest(
-    where_ref, near_one, far_one, near_two, far_two, qkv_ref, out_ref, proj_ref, bqkv_ref, bout_ref,
-    g1_ref, s1_ref, bup_ref, bdown_ref, g2_ref, s2_ref, rest_ref,
-):
-    core, near_place, far_place = where_ref[5], where_ref[6], where_ref[7]
-    first = 0
-    for near_ref, far_ref in ((near_one, far_one), (near_two, far_two)):
-        half, size = near_ref.shape[0], near_ref.shape[1]
-        for p in range(half):
-            for ref, owner, place in ((near_ref, core, near_place), (far_ref, 1 - core, far_place)):
-                block = owner * half + (p ^ place)
-                start = pl.multiple_of(first + block * size, 8)
-                rest_ref[pl.ds(start, size), :] = ref[p].astype(F32)
-        first += 2 * half * size
-    for c in range(3):
-        qkv_ref[:, c * D : (c + 1) * D] = rest_ref[c * D : (c + 1) * D, :]
-    out_ref[...] = rest_ref[3 * D : 4 * D, :]
-    for k in range(4):
-        proj_ref[k * 128 : (k + 1) * 128, :] = rest_ref[
-            4 * D : 4 * D + 128, k * 128 : (k + 1) * 128
-        ]
-    small = rest_ref[4 * D + 128 : 4 * D + 128 + EXT, :]
-    row = [small[k : k + 1, :] for k in range(13)]
-    for c in range(3):
-        bqkv_ref[:, c * D : (c + 1) * D] = row[c]
-    bout_ref[...] = row[3]
-    g1_ref[...] = row[4]
-    s1_ref[...] = row[5]
-    for c in range(4):
-        bup_ref[:, c * D : (c + 1) * D] = row[6 + c]
-    bdown_ref[...] = row[10]
-    g2_ref[...] = row[11]
-    s2_ref[...] = row[12]
+    for k, row in enumerate(smalls):
+        rest_ref[4 * D + 8 * k : 4 * D + 8 * k + 1, :] = row
+    for k in range(RING):
+        for ref, tail_ref, owner in (
+            (keep_ref, tail_keep, core), (send_ref, tail_send, 1 - core)
+        ):
+            block = owner * RING + block_at(owner, place, k)
+            parts = []
+            for c in range(4):
+                start = pl.multiple_of(c * D + block * SHARE, SHARE)
+                parts.append(rest_ref[pl.ds(start, SHARE), :])
+            row = pl.multiple_of(block * SHARE, SHARE)
+            parts.append(
+                jnp.concatenate(
+                    [gproj_ref[pl.ds(row + 8 * j, 8), :] for j in range(SHARE // 8)], axis=1
+                )
+            )
+            parts.append(rest_ref[pl.ds(pl.multiple_of(4 * D + block * 8, 8), 8), :])
+            ref[k, : REST // 16, :] = jnp.concatenate(parts, axis=0).astype(BF16)
+            ref[k, REST // 16 :, :] = tail_ref[k]
+
+
+def spread(mine, group, last, where_ref, *refs):
+    core, place = where_ref[5], where_ref[6]
+    owner = core if mine else 1 - core
+    one_ref, two_ref = refs[:2]
+    wide_one, wide_two, wide_proj, small_ref, sems = refs[-5:]
+    outs = refs[-18:-5] if last else refs[-10:-5]
+    down_hbm, up_hbm, qkv_hbm, out_hbm, proj_hbm = outs[:5]
+    copies = []
+
+    def move(src, dst):
+        copy = pltpu.make_async_copy(src, dst, sems.at[len(copies)])
+        copy.start()
+        copies.append(copy)
+
+    for p, distance in enumerate(GROUPS[group]):
+        block = owner * RING + block_at(owner, place, distance)
+        wide_one[p] = one_ref[p].astype(F32)
+        rows = pl.ds(pl.multiple_of(block * DOWN, DOWN), DOWN)
+        move(wide_one.at[p, :DOWN, :], down_hbm.at[rows, :])
+        wide = two_ref[p].astype(F32)
+        wide_two[p, : 4 * SHARE, :] = wide[: 4 * SHARE, :]
+        wide_two[p, 4 * SHARE :, :] = wide[REST // 16 :, :]
+        start = (block % (D // DOWN)) * DOWN
+        columns = pl.ds(pl.multiple_of((block // (D // DOWN)) * D, D), D)
+        rows = pl.ds(pl.multiple_of(start, DOWN), HEAD)
+        move(wide_one.at[p, DOWN:, :], up_hbm.at[rows, columns])
+        rows = pl.ds(pl.multiple_of(start + HEAD, 16), TAIL)
+        move(wide_two.at[p, 4 * SHARE :, :], up_hbm.at[rows, columns])
+        rows = pl.ds(pl.multiple_of(block * SHARE, SHARE), SHARE)
+        for c in range(3):
+            move(
+                wide_two.at[p, c * SHARE : (c + 1) * SHARE, :],
+                qkv_hbm.at[rows, c * D : (c + 1) * D],
+            )
+        move(wide_two.at[p, 3 * SHARE : 4 * SHARE, :], out_hbm.at[rows, :])
+        for j in range(SHARE // 8):
+            wide_proj[p, 8 * j : 8 * j + 8, :] = wide[
+                4 * SHARE : 4 * SHARE + 8, j * PROJ : (j + 1) * PROJ
+            ]
+        move(wide_proj.at[p], proj_hbm.at[rows, :])
+    if last:
+        sources = ((refs[2], core, 0), (refs[3], core, 1), (refs[4], 1 - core, 0), (two_ref, 1 - core, 1))
+        for ref, at, one_group in sources:
+            for p, distance in enumerate(GROUPS[one_group]):
+                block = at * RING + block_at(at, place, distance)
+                line = ref[p, 4 * SHARE : 4 * SHARE + 16, :].astype(F32)[8:, :]
+                small_ref[pl.ds(pl.multiple_of(block * 8, 8), 8), :] = line
+        rows = [small_ref[8 * k : 8 * k + 1, :] for k in range(13)]
+        bqkv_ref, bout_ref, g1_ref, s1_ref, bup_ref, bdown_ref, g2_ref, s2_ref = outs[5:]
+        for c in range(3):
+            bqkv_ref[:, c * D : (c + 1) * D] = rows[c]
+        bout_ref[...] = rows[3]
+        g1_ref[...] = rows[4]
+        s1_ref[...] = rows[5]
+        for c in range(4):
+            bup_ref[:, c * D : (c + 1) * D] = rows[6 + c]
+        bdown_ref[...] = rows[10]
+        g2_ref[...] = rows[11]
+        s2_ref[...] = rows[12]
+    for copy in copies:
+        copy.wait()
+
+
+def spread_call(mine, group, where, one, two, outs, others):
+    last = len(others) > 0
+    shapes = ((FF, D), (D, FF), (D, 3 * D), (D, D), (D, PROJ))
+    widths = (3 * D, D, D, D, FF, D, D, D) if last else ()
+    args = [where, one, two, *others, *outs]
+    half = len(GROUPS[group])
+    return call(
+        partial(spread, mine, group, last),
+        args,
+        [SMEM] + [VMEM] * (2 + len(others)) + [HBM] * len(outs),
+        [pltpu.HBM(shape, F32) for shape in shapes] + [shape_of((1, width)) for width in widths],
+        [
+            pltpu.VMEM((half, FIRST, D), F32),
+            pltpu.VMEM((half, 4 * SHARE + TAIL, D), F32),
+            pltpu.VMEM((half, SHARE, PROJ), F32),
+            pltpu.VMEM((16 * RING, D), F32),
+            pltpu.SemaphoreType.DMA((8 * half,)),
+        ],
+        out_specs=[HBM] * 5 + [VMEM] * len(widths),
+        aliases={3 + len(others) + k: k for k in range(len(outs))},
+        room=14,
+    )
 
 
 def shape_of(shape, dtype=F32):
     return jax.ShapeDtypeStruct(tuple(shape), dtype)
 
 
-def call(kernel, args, specs, outs, scratch=(), room=24, out_specs=None):
+def call(kernel, args, specs, outs, scratch=(), room=24, out_specs=None, aliases={}, cost=10**7):
     spaces = {id(HBM): pltpu.HBM, id(HELD): pltpu.VMEM}
     args = [
         pltpu.with_memory_space_constraint(arg, spaces[id(spec)]) if id(spec) in spaces else arg
@@ -691,25 +795,36 @@
         in_specs=specs,
         out_specs=out_specs or [VMEM] * len(outs),
         scratch_shapes=list(scratch),
+        input_output_aliases=aliases,
         compiler_params=pltpu.CompilerParams(vmem_limit_bytes=room * MIB),
-        cost_estimate=pl.CostEstimate(flops=10**9, bytes_accessed=10**7, transcendentals=0),
+        cost_estimate=pl.CostEstimate(
+            flops=10**8, bytes_accessed=cost, transcendentals=0
+        ),
     )(*args)
 
 
-def spread_call(kind, where, halves):
-    if kind < 2:
-        columns = (1, 4)[kind]
-        kernel, outs, scratch = (
-            partial(spread_out, columns), [shape_of((FF // columns, D * columns))], []
-        )
-    else:
-        kernel, scratch = spread_rest, [pltpu.VMEM((REST, D), F32)]
-        outs = [
-            shape_of((D, 3 * D)), shape_of((D, D)), shape_of((D, PROJ)), shape_of((1, 3 * D)),
-            shape_of((1, D)), shape_of((1, D)), shape_of((1, D)), shape_of((1, FF)),
-            shape_of((1, D)), shape_of((1, D)), shape_of((1, D)),
-        ]
-    return call(kernel, (where, *halves), [SMEM] + [VMEM] * len(halves), outs, scratch)
+def spread_half_call(where, halves, near=None, outs=()):
+    mine = near is None
+    args = [where, *halves] + ([] if mine else [near, *outs])
+    specs = [SMEM] + [VMEM] * (3 if mine else 4) + [HBM] * len(outs)
+    shapes = ((FF, D), (D, FF), (D, 3 * D), (D, D), (D, PROJ))
+    widths = () if mine else (3 * D, D, D, D, FF, D, D, D)
+    return call(
+        partial(spread_half, mine),
+        args,
+        specs,
+        [pltpu.HBM(shape, F32) for shape in shapes] + [shape_of((1, width)) for width in widths],
+        [
+            pltpu.VMEM((RING, FF // (2 * RING), D), F32),
+            pltpu.VMEM((RING, FF // (2 * RING), D), F32),
+            pltpu.VMEM((RING, 4 * SHARE, D), F32),
+            pltpu.VMEM((RING, SHARE, PROJ), F32),
+            pltpu.SemaphoreType.DMA((7 * RING,)),
+        ],
+        out_specs=[HBM] * 5 + [VMEM] * len(widths),
+        aliases={} if mine else {5 + k: k for k in range(5)},
+        room=14,
+    )
 
 
 def swapped(value, mask, axis="dp"):
@@ -721,63 +836,94 @@
     return (a.astype(F32) + b.astype(F32)).astype(BF16)
 
 
-def block_place(me, order):
-    place = jnp.int32(0)
-    for k, mask in enumerate(order):
-        place = place | jnp.where((me & mask) != 0, 1 << (len(order) - 1 - k), 0)
-    return place
-
-
-def swapped_by_core(value, masks):
+def join_blocks(*refs):
+    for k, ref in enumerate(refs[:-1]):
+        refs[-1][k] = ref[0]
+
+
+def ring_swap(value, onward):
     size = lax.axis_size("dp")
-    return lax.ppermute(value, "dp", [(k, k ^ masks[k & 1]) for k in range(size)])
+    pairs = []
+    for k in range(size):
+        at = CIRCLE.index((k >> 1) % RING)
+        to = CIRCLE[(at + (1 if (k % 2 == 0) == onward else -1)) % RING]
+        pairs.append((k, (k & ~(2 * RING - 1)) | (to << 1) | (k & 1)))
+    return lax.ppermute(value, "dp", pairs)
+
+
+def add_blocks(places, *refs):
+    count = len(places)
+    held_ref = refs[count] if any(place is not None for place in places) else None
+    for k, place in enumerate(places):
+        value = refs[k][...]
+        if place is not None:
+            value = (value.astype(F32) + held_ref[place : place + 1].astype(F32)).astype(BF16)
+        refs[-count + k][...] = value
 
 
 class Summed:
-    def __init__(self, keep, send, masks, others):
-        self.keep, self.masks, self.others, self.at = keep, masks, others, 0
-        self.got = swapped_by_core(send, masks[0])
+    def __init__(self, keep, send, others):
+        self.keep, self.others, self.hop = keep, others, 0
+        self.pair = swapped(send, 1)
+        self.got, self.blocks, self.near, self.far = [], {}, [], []
+
+    def blocks_call(self, blocks, places, held):
+        return call(
+            partial(add_blocks, places),
+            (*blocks, *held),
+            [VMEM] * (len(blocks) + len(held)),
+            [shape_of(block.shape, BF16) for block in blocks],
+            room=8,
+            cost=STEP_COST,
+        )
+
+    def open(self, after):
+        keep, pair, _ = lax.optimization_barrier((self.keep, self.pair, after))
+        half = RING // 2
+        first = added(keep[half : half + 1], pair[half : half + 1])
+        second = added(keep[half - 1 : half], pair[half - 1 : half])
+        self.got = [ring_swap(first, True), ring_swap(second, False)]
+        return second
+
+    def total(self, after):
+        keep, _ = lax.optimization_barrier((self.keep, after))
+        self.keep = added(keep, self.pair)
+        return self.keep
 
     def step(self, after):
-        keep, got = self.keep, self.got
-        if after is not None:
-            keep, got, _ = lax.optimization_barrier((keep, got, after))
-        self.at += 1
-        last = len(self.masks)
-        if self.at < last:
-            half = keep.shape[0] // 2
-            send = added(keep[half:], got[half:])
-            self.keep = added(keep[:half], got[:half])
-            self.got = swapped_by_core(send, self.masks[self.at])
-            return send
-        if self.at == last:
-            keep = added(keep, got)
+        half = RING // 2
+        self.hop += 1
+        hop = self.hop
+        *got, _ = lax.optimization_barrier((*self.got, after))
+        if hop < half:
+            out = self.blocks_call(got, (half + hop, half - 1 - hop), [self.keep])
+            self.part = out[1]
+        elif hop == half:
+            (own,) = self.blocks_call(got, (0,), [self.part])
             for mask in self.others:
-                keep = added(keep, swapped(keep, mask))
-        elif self.at < 2 * last:
-            keep = jnp.concatenate([keep, got], axis=0)
+                own = added(own, swapped(own, mask))
+            self.blocks[0] = own
+            out = [own, own]
         else:
-            self.keep, self.got = keep, got
-            return got
-        self.keep = keep
-        self.got = swapped_by_core(keep, self.masks[2 * last - 1 - self.at])
-        return keep
-
-
-class Doubled:
-    def __init__(self, value, masks):
-        self.value, self.masks, self.got = value, list(masks), None
-
-    def step(self, after):
-        value, got = self.value, self.got
-        if after is not None:
-            value, _ = lax.optimization_barrier((value, after))
-        if got is not None:
-            value = value + got
-        self.value, self.got = value, None
-        if self.masks:
-            self.got = swapped(value, self.masks.pop(0))
-        return value
+            out = self.blocks_call(got, (None,) * len(got), [])
+            hop -= half
+            self.blocks[hop] = out[0]
+            if hop < half:
+                self.blocks[RING - hop] = out[1]
+        if hop == half - 1:
+            self.got = [ring_swap(out[0], True)]
+        elif self.hop < 2 * half:
+            self.got = [ring_swap(out[0], True), ring_swap(out[1], False)]
+        return out[0]
+
+    def share(self, group, after):
+        *blocks, _ = lax.optimization_barrier((*[self.blocks[k] for k in GROUPS[group]], after))
+        shape = (len(blocks), *blocks[0].shape[1:])
+        self.near += call(
+            join_blocks, blocks, [VMEM] * len(blocks), [shape_of(shape, BF16)], room=8, cost=STEP_COST
+        )
+        self.far.append(swapped(self.near[-1], 1))
+        return self.near[-1]
 
 
 def per_device(
@@ -789,9 +935,7 @@
     bits = [1 << k for k in range(size.bit_length() - 1)]
     near_masks, doc_masks = bits[:2], bits[2:]
     top_mask, doc_masks = doc_masks[-1], doc_masks[:-1]
-    masks = [(bits[0], bits[0]), (bits[1], bits[2]), (bits[2], bits[1]), (bits[3], bits[3])]
     others = bits[4:]
-    blocks = 16
     me = lax.axis_index("dp")
     stream = lax.axis_index("stream")
     is_query = stream == 0
@@ -799,10 +943,12 @@
     base = jnp.where(is_query, me & ~top_mask, me | top_mask)
     near_at = jnp.where((me & near_masks[1]) != 0, 1, 0) + jnp.where((me & near_masks[0]) != 0, 2, 0)
     core = me & 1
-    places = [block_place(me, [pair[k] for pair in masks[1:]]) for k in range(2)]
+    chip = (me >> 1) % RING
+    place = jnp.int32(0)
+    for k, one in enumerate(CIRCLE):
+        place = jnp.where(chip == one, k, place)
     where = jnp.stack(
-        [me, stream, base, near_at, has_top.astype(jnp.int32), core]
-        + [jnp.where(core == 0, *places), jnp.where(core == 0, *places[::-1])]
+        [me, stream, base, near_at, has_top.astype(jnp.int32), core, place, place]
     ).astype(jnp.int32)
     scale = log_scale.reshape(1)
 
@@ -866,11 +1012,14 @@
     stats = stats + swapped(stats, near_masks[0])
     stats = stats + swapped(stats, near_masks[1])
     stats = stats + swapped(stats, 1, "stream")
-    dq, dd, loss = call(
+    dq, send, keep, loss = call(
         partial(matching_back, doc_masks, lanes, total_queries),
         (where, scale, doc_lengths, near, far, totals, el, hot, stats, *pieces),
         [SMEM] * 3 + [VMEM] * (6 + len(pieces)),
-        [shape_of((tokens_q, PROJ), BF16), shape_of((tokens_d, PROJ), BF16), shape_of((8, 128))],
+        [
+            shape_of((tokens_q, PROJ), BF16), shape_of((tokens_d // 2 + EXT, PROJ), BF16),
+            shape_of((tokens_d // 2, PROJ), BF16), shape_of((8, 128)),
+        ],
         [
             pltpu.VMEM((PROJ, tokens_d), F32),
             pltpu.VMEM((3, PROJ, tokens_d), BF16),
@@ -881,66 +1030,76 @@
         room=room,
     )
     for mask in reversed(doc_masks):
-        half = dd.shape[0] // 2
-        dd = added(dd[:half], swapped(dd[half:], mask))
+        got, rows = swapped(send, mask), keep.shape[0]
+        outs = [shape_of((rows // 2 + EXT, PROJ), BF16), shape_of((rows // 2, PROJ), BF16)]
+        if rows == ROW:
+            outs = [shape_of((ROW + EXT, PROJ), BF16)]
+        send, *keep, loss = call(
+            fold_docs, (keep, got, loss), [VMEM] * 3, outs + [shape_of((8, 128))], room=8
+        )
+        keep = keep[0] if keep else None
     for mask in near_masks:
         half = dq.shape[0] // 2
         dq = added(dq[:half], swapped(dq[half:], mask))
-    dd = added(dd, swapped(dd, top_mask))
-    got = swapped(jnp.where(is_query, dd, dq), 1, "stream")
-
-    down_keep, down_send, up_keep, up_send, d_first, gproj, small = call(
+    dd, send, loss = call(
+        last_docs,
+        (where, send, swapped(send, top_mask), loss, dq),
+        [SMEM] + [VMEM] * 4,
+        [shape_of((ROW, PROJ), BF16), shape_of((ROW, PROJ), BF16), shape_of((8, 128))],
+        room=8,
+    )
+    got = swapped(send, 1, "stream")
+
+    one_keep, one_send, tail_keep, tail_send, d_first, gproj, small = call(
         feed_back,
         (
             where, dq, dd, got, xh2, rs2, affine, proj_weight[0], down_weight[0], slope, act,
             up_weight[0], xh1,
         ),
         [SMEM] + [VMEM] * 3 + [HELD] * 9,
-        [shape_of((blocks // 2, FF // blocks, D), BF16)] * 4
+        [shape_of((RING, FIRST, D), BF16)] * 2
+        + [shape_of((RING, TAIL, D), BF16)] * 2
         + [shape_of((ROW, D)), shape_of((D, PROJ)), shape_of((8, D))],
-        [
-            pltpu.VMEM((ROW, FF), BF16),
-        ],
-    )
-    keep_one, send_one, keep_two, send_two, tokens_grad = call(
+        [pltpu.VMEM((ROW, FF), BF16)],
+        room=24,
+    )
+    two_keep, two_send, tokens_grad = call(
         attend_back,
         (
-            where, d_first, gproj, small, xh1, rs1, affine, mixed, out_weight[0], qkv, probs, rope,
+            where, d_first, gproj, small, tail_keep, tail_send, xh1, rs1, affine, mixed, out_weight[0], qkv, probs, rope,
             tokens[0], qkv_weight[0],
         ),
-        [SMEM] + [VMEM] * 3 + [HELD] * 10,
-        [shape_of((blocks // 2, 3 * D // blocks, D), BF16)] * 2
-        + [shape_of((blocks // 2, (REST - 3 * D) // blocks, D), BF16)] * 2
-        + [shape_of((ROW, D))],
+        [SMEM] + [VMEM] * 5 + [HELD] * 10,
+        [shape_of((RING, SECOND, D), BF16)] * 2 + [shape_of((ROW, D))],
         [
             pltpu.VMEM((ROW, 3 * D), BF16),
-            pltpu.VMEM((REST, D), F32),
+            pltpu.VMEM((4 * D + 16 * RING, D), F32),
         ],
-    )
-    pieces = [
-        Summed(keep, send, masks, others)
-        for keep, send in (
-            (down_keep, down_send), (up_keep, up_send), (keep_one, send_one), (keep_two, send_two)
-        )
-    ] + [Doubled(loss, doc_masks + [top_mask])]
-    token, spread = None, {}
-    for k in ORDER:
-        if k >= 10:
-            ready = [pieces[j] for j in FINAL[k - 10]]
-            halves = [half for piece in ready for half in (piece.keep, piece.got)]
+        room=24,
+    )
+    one, two = [
+        Summed(keep, send, others) for keep, send in ((one_keep, one_send), (two_keep, two_send))
+    ]
+    token, outs = tokens_grad, ()
+    for event in ORDER:
+        kind, k = event
+        if kind in ("near", "far"):
+            mine = kind == "near"
+            halves = [piece.near[k] if mine else piece.far[k] for piece in (one, two)]
             *halves, _ = lax.optimization_barrier((*halves, token))
-            spread[k - 10] = spread_call(k - 10, where, halves)
-            token = spread[k - 10][0]
+            rest = [*two.near, two.far[0]] if (kind, k) == ("far", 1) else []
+            outs = spread_call(mine, k, where, *halves, outs[:5], rest)
+            token = outs[0]
+            continue
+        piece = (one, two)[k]
+        if kind in ("share0", "share1"):
+            token = piece.share(int(kind[-1]), token)
         else:
-            token = pieces[k].step(token)
-    grad_down, grad_up = spread[0][0], spread[1][0]
+            token = getattr(piece, kind)(token)
+    grad_down, grad_up, grad_qkv, grad_out, grad_proj = outs[:5]
     (
-        grad_qkv, grad_out, grad_proj, grad_bqkv, grad_bout, grad_g1, grad_s1, grad_bup,
-        grad_bdown, grad_g2, grad_s2,
-    ) = spread[2]
-    while pieces[-1].got is not None:
-        pieces[-1].step(None)
-    loss = pieces[-1].value
+        grad_bqkv, grad_bout, grad_g1, grad_s1, grad_bup, grad_bdown, grad_g2, grad_s2,
+    ) = outs[5:]
     return (
         loss[0, 0],
         tokens_grad[None],

time: 166 us -> 160 us (0.964)
  waiting for transfers between devices: 74.1 us -> 58.5 us
  Pallas kernels: 36.2 us -> 40 us
  local copies, waits for them, and re-layouts: 2.56 us -> 6.14 us
  starting transfers between devices: 49.1 us -> 51.6 us
    ppermute x32 -> x28, waiting for transfers between devices: 51.2 us -> 33.5 us  [ring_swap(): return lax.ppermute(value, 'dp', pairs)]
    ppermute x32 -> x28, starting transfers between devices: 27.6 us -> 31.8 us  [ring_swap(): return lax.ppermute(value, 'dp', pairs)]
    unnamed x49 -> x37, local copies, waits for them, and re-layouts: 1.72 us -> 5.52 us
    pallas_call x8 -> x31, Pallas kernels: 36.2 us -> 40 us  [call(): pl.pallas_call(kernel, out_shape=outs, in_specs=specs, out_specs=out_spec...]
    ppermute x15 -> x19, waiting for transfers between devices: 22.9 us -> 25 us  [swapped(): return lax.ppermute(value, axis, [(k, k ^ mask) for k in range(size)])]
    ppermute x15 -> x19, starting transfers between devices: 21.5 us -> 19.8 us  [swapped(): return lax.ppermute(value, axis, [(k, k ^ mask) for k in range(size)])]
  transfers between devices with their start and end apart: 47 -> 47, of which waited for: 25 -> 31; matrix products, arithmetic and copies ran while one was open for 2% -> 1% of each run, Pallas kernels for 4% -> 9%
where the time goes in v4:
time: 160 us
  waiting for transfers between devices  58.5 us (37%)
  starting transfers between devices  51.6 us (32%)
  Pallas kernels  40 us (25%)
  local copies, waits for them, and re-layouts  6.14 us (4%)
  between operations  2.03 us (1%)
    pallas_call x31, Pallas kernels, call(): pl.pallas_call(kernel, out_shape=outs, in_specs=specs, out_specs=out_spec...  40 us
    ppermute x28, waiting for transfers between devices, ring_swap(): return lax.ppermute(value, 'dp', pairs)  33.5 us
    ppermute x28, starting transfers between devices, ring_swap(): return lax.ppermute(value, 'dp', pairs)  31.8 us
    ppermute x19, waiting for transfers between devices, swapped(): return lax.ppermute(value, axis, [(k, k ^ mask) for k in range(size)])  25 us
    ppermute x19, starting transfers between devices, swapped(): return lax.ppermute(value, axis, [(k, k ^ mask) for k in range(size)])  19.8 us
    unnamed x37, local copies, waits for them, and re-layouts  5.52 us
  transfers between devices with their start and end apart: 47, of which 31 were waited for; matrix products, arithmetic and copies ran while one was open for 1% of the time, Pallas kernels for 9%

profile of v4, /device:TPU:0, one launch (start us, length us, event | category | flops | bytes accessed | tf_op | source)
XLA Modules:
  0.0 159.7 jit_solution(15896290197786447141)
XLA Ops:
  2.2 8.9 %shard_map.297 = (bf16[272,128]{1,0:T(8,128)(2,1)S(1)}, bf16[256,1536]{1,0:T(8,128)(2,1)}, f32[256,256]{1,0:T(8,128)}, bf16[8,256,256]{2,1,0:T(8,128)(2,1)}, bf1...) custom-call(s32[8]{0:T(128)S(1)} %stack.36.where_ref, ...), custom_call_target="tpu_custom_call" | custom-call | flops 100000000 | bytes 10000000 | tf_op jit(solution)/shard_map/pallas_call | solution.py:792
  11.1 3.0 %collective-permute-start = (bf16[272,128]{1,0:T(8,128)(2,1)S(1)}, bf16[272,128]{1,0:T(8,128)(2,1)S(1)}, u32[]{:S(2)}, u32[]{:S(2)}) collective-permute-start(bf16[272,128]{1,0:T(8,128)(2,1)S(1)} %get-tuple-element.161), channel_id=1, source_target_pairs={{0,16},{16,0},{1,17},{17,1},{2,18},{18,2},{3,19},{19,3},{4,20},{20... | collective-permute-start | bytes 208904 | tf_op jit(solution)/shard_map/ppermute | solution.py:832
  14.1 2.3 %collective-permute-done = bf16[272,128]{1,0:T(8,128)(2,1)S(1)} collective-permute-done((bf16[272,128]{1,0:T(8,128)(2,1)S(1)}, bf16[272,128]{1,0:T(8,128)(2,1)S(1)}, u32[]{:S(2)}, u32[]{:S(2)}) %collective-permute-start) | collective-permute-done | bytes 69664 | tf_op jit(solution)/shard_map/ppermute | solution.py:832
  16.5 2.1 %collective-permute-start.1 = (bf16[272,128]{1,0:T(8,128)(2,1)S(1)}, bf16[272,128]{1,0:T(8,128)(2,1)S(1)}, u32[]{:S(2)}, u32[]{:S(2)}) collective-permute-start(bf16[272,128]{1,0:T(8,128)(2,1)S(1)} %broadcast_select_fusion), channel_id=1, source_target_pairs={{0,2},{1,3},{2,0},{3,1},{4,6},{5,7},{6,4},{7,5},{8,10},{9,11},{10,... | collective-permute-start | bytes 208904 | tf_op jit(solution)/shard_map/ppermute | solution.py:832
  18.6 2.7 %collective-permute-start.3 = (bf16[256,128]{1,0:T(8,128)(2,1)S(1)}, bf16[256,128]{1,0:T(8,128)(2,1)S(1)}, u32[]{:S(2)}, u32[]{:S(2)}) collective-permute-start(bf16[256,128]{1,0:T(8,128)(2,1)S(1)} %slice_select_fusion), channel_id=1, source_target_pairs={{0,8},{1,9},{2,10},{3,11},{4,12},{5,13},{6,14},{7,15},{8,0},{9,1},... | collective-permute-start | bytes 196616 | tf_op jit(solution)/shard_map/ppermute | solution.py:832
  21.3 2.5 %collective-permute-done.3 = bf16[256,128]{1,0:T(8,128)(2,1)S(1)} collective-permute-done((bf16[256,128]{1,0:T(8,128)(2,1)S(1)}, bf16[256,128]{1,0:T(8,128)(2,1)S(1)}, u32[]{:S(2)}, u32[]{:S(2)}) %collective-permute-start.3) | collective-permute-done | bytes 65568 | tf_op jit(solution)/shard_map/ppermute | solution.py:832
  23.9 1.6 %collective-permute-start.4 = (bf16[256,128]{1,0:T(8,128)(2,1)S(1)}, bf16[256,128]{1,0:T(8,128)(2,1)S(1)}, u32[]{:S(2)}, u32[]{:S(2)}) collective-permute-start(bf16[256,128]{1,0:T(8,128)(2,1)S(1)} %broadcast_select_fusion.1.refs_0_), channel_id=1, source_target_pairs={{0,4},{1,5},{2,6},{3,7},{4,0},{5,1},{6,2},{7,3},{8,12},{9,13},{10,... | collective-permute-start | bytes 196616 | tf_op jit(solution)/shard_map/ppermute | solution.py:832
  26.2 2.0 %collective-permute-done.4.refs_1_ = bf16[256,128]{1,0:T(8,128)(2,1)S(1)} collective-permute-done((bf16[256,128]{1,0:T(8,128)(2,1)S(1)}, bf16[256,128]{1,0:T(8,128)(2,1)S(1)}, u32[]{:S(2)}, u32[]{:S(2)}) %collective-permute-start.4) | collective-permute-done | bytes 65568 | tf_op jit(solution)/shard_map/ppermute | solution.py:832
  28.2 2.9 %shard_map.298 = (f32[1024,128]{1,0:T(8,128)S(1)}, f32[32,128]{1,0:T(8,128)S(1)}, f32[32,128]{1,0:T(8,128)S(1)}, f32[32,128]{1,0:T(8,128)S(1)}) custom-call(s32[8]{0:T(128)S(1)} %stack.36.where_ref, f32[1]{0:T(128)} %bitcast.22.scale_ref, s32[16,5]{1,0:T(8,128)S(1)} %copy.51.lens_ref, bf16[544,128]{1,0:T(8,128)(2,1)S(1)} %pad_maximum_fusion.near_ref, ...), custom_call_target="tpu_custom_call" | custom-call | flops 100000000 | bytes 10000000 | tf_op jit(solution)/shard_map/pallas_call | solution.py:792
  32.5 3.6 %collective-permute-done.6 = f32[32,128]{1,0:T(8,128)S(1)} collective-permute-done((f32[32,128]{1,0:T(8,128)S(1)}, f32[32,128]{1,0:T(8,128)S(1)}, u32[]{:S(2)}, u32[]{:S(2)}) %collective-permute-start.6) | collective-permute-done | bytes 16416 | tf_op jit(solution)/shard_map/ppermute | solution.py:832
  36.1 1.5 collective-permute-start.7
  37.6 2.2 %collective-permute-done.7 = f32[32,128]{1,0:T(8,128)S(1)} collective-permute-done((f32[32,128]{1,0:T(8,128)S(1)}, f32[32,128]{1,0:T(8,128)S(1)}, u32[]{:S(2)}, u32[]{:S(2)}) %collective-permute-start.7) | collective-permute-done | bytes 16416 | tf_op jit(solution)/shard_map/ppermute | solution.py:832
  39.8 5.2 %shard_map.299 = (bf16[1024,128]{1,0:T(8,128)(2,1)S(1)}, bf16[272,128]{1,0:T(8,128)(2,1)S(1)}, bf16[256,128]{1,0:T(8,128)(2,1)S(1)}, f32[8,128]{1,0:T(8,128)S(1)}) custom-call(s32[8]{0:T(128)S(1)} %stack.36.where_ref, f32[1]{0:T(128)} %bitcast.23.scale_ref, s32[16,5]{1,0:T(8,128)S(1)} %copy.51.lens_ref, bf16[544,128]{1,0:T(8,128)(2,1)S(1)} %pad_maximum_fusion.near_ref, ...), custom_call_target="tpu_custom_call" | custom-call | flops 100000000 | bytes 10000000 | tf_op jit(solution)/shard_map/pallas_call | solution.py:792
  45.1 1.6 %collective-permute-start.8 = (bf16[272,128]{1,0:T(8,128)(2,1)S(1)}, bf16[272,128]{1,0:T(8,128)(2,1)S(1)}, u32[]{:S(2)}, u32[]{:S(2)}) collective-permute-start(bf16[272,128]{1,0:T(8,128)(2,1)S(1)} %get-tuple-element.167), channel_id=1, source_target_pairs={{0,4},{1,5},{2,6},{3,7},{4,0},{5,1},{6,2},{7,3},{8,12},{9,13},{10,... | collective-permute-start | bytes 208904 | tf_op jit(solution)/shard_map/ppermute | solution.py:832
  47.4 2.3 %collective-permute-done.8.got_ref = bf16[272,128]{1,0:T(8,128)(2,1)S(1)} collective-permute-done((bf16[272,128]{1,0:T(8,128)(2,1)S(1)}, bf16[272,128]{1,0:T(8,128)(2,1)S(1)}, u32[]{:S(2)}, u32[]{:S(2)}) %collective-permute-start.8) | collective-permute-done | bytes 69664 | tf_op jit(solution)/shard_map/ppermute | solution.py:832
  49.8 3.0 %collective-permute-start.9 = (bf16[272,128]{1,0:T(8,128)(2,1)S(1)}, bf16[272,128]{1,0:T(8,128)(2,1)S(1)}, u32[]{:S(2)}, u32[]{:S(2)}) collective-permute-start(bf16[272,128]{1,0:T(8,128)(2,1)S(1)} %get-tuple-element.169.near_ref), channel_id=1, source_target_pairs={{0,8},{1,9},{2,10},{3,11},{4,12},{5,13},{6,14},{7,15},{8,0},{9,1},... | collective-permute-start | bytes 208904 | tf_op jit(solution)/shard_map/ppermute | solution.py:832
  52.8 3.8 %collective-permute-done.9.got_ref = bf16[272,128]{1,0:T(8,128)(2,1)S(1)} collective-permute-done((bf16[272,128]{1,0:T(8,128)(2,1)S(1)}, bf16[272,128]{1,0:T(8,128)(2,1)S(1)}, u32[]{:S(2)}, u32[]{:S(2)}) %collective-permute-start.9) | collective-permute-done | bytes 69664 | tf_op jit(solution)/shard_map/ppermute | solution.py:832
  57.2 1.5 collective-permute-start.12
  58.7 2.8 %collective-permute-done.12.got_ref = bf16[256,128]{1,0:T(8,128)(2,1)S(1)} collective-permute-done((bf16[256,128]{1,0:T(8,128)(2,1)S(1)}, bf16[256,128]{1,0:T(8,128)(2,1)S(1)}, u32[]{:S(2)}, u32[]{:S(2)}) %collective-permute-start.12) | collective-permute-done | bytes 65568 | tf_op jit(solution)/shard_map/ppermute | solution.py:832
  61.6 1.6 copy-done.1
  65.6 5.2 %shard_map.302 = (bf16[8,208,512]{2,1,0:T(8,128)(2,1)S(1)}, bf16[8,208,512]{2,1,0:T(8,128)(2,1)S(1)}, bf16[8,48,512]{2,1,0:T(8,128)(2,1)S(1)}, bf16[8,48,512]{2,...) custom-call(s32[8]{0:T(128)S(1)} %stack.36.where_ref, ...), custom_call_target="tpu_custom_call" | custom-call | flops 100000000 | bytes 10000000 | tf_op jit(solution)/shard_map/pallas_call | solution.py:792
  71.1 5.2 %shard_map.303 = (bf16[8,192,512]{2,1,0:T(8,128)(2,1)S(1)}, bf16[8,192,512]{2,1,0:T(8,128)(2,1)S(1)}, f32[256,512]{1,0:T(8,128)}) custom-call(s32[8]{0:T(128)S(1)} %stack.36.where_ref, f32[256,512]{1,0:T(8,128)S(1)} %get-tuple-element.181.dfirst_ref, f32[512,128]{1,0:T(8,128)S(1)} %get-tuple-element.182.gproj_ref, ...), custom_call_target="tpu_custom_call" | custom-call | flops 100000000 | bytes 10000000 | tf_op jit(solution)/shard_map/pallas_call | solution.py:792
  77.4 2.4 %collective-permute-done.16 = bf16[8,192,512]{2,1,0:T(8,128)(2,1)S(1)} collective-permute-done((bf16[8,192,512]{2,1,0:T(8,128)(2,1)S(1)}, bf16[8,192,512]{2,1,0:T(8,128)(2,1)S(1)}, u32[]{:S(2)}, u32[]{:S(2)}) %collective-permute-start.16) | collective-permute-done | bytes 1572896 | tf_op jit(solution)/shard_map/ppermute | solution.py:832
  80.5 1.5 collective-permute-start.14
  83.7 3.6 %collective-permute-done.14.refs_0_ = bf16[1,208,512]{2,1,0:T(8,128)(2,1)S(1)} collective-permute-done((bf16[1,208,512]{2,1,0:T(8,128)(2,1)S(1)}, bf16[1,208,512]{2,1,0:T(8,128)(2,1)S(1)}, u32[]{:S(2)}, u32[]{:S(2)}) %collective-permute-start.14) | collective-permute-done | bytes 213024 | tf_op jit(solution)/shard_map/ppermute | solution.py:851
  88.0 1.5 collective-permute-start.17
  90.2 1.5 collective-permute-start.23
  91.7 3.6 %collective-permute-done.18.refs_1_ = bf16[1,208,512]{2,1,0:T(8,128)(2,1)S(1)} collective-permute-done((bf16[1,208,512]{2,1,0:T(8,128)(2,1)S(1)}, bf16[1,208,512]{2,1,0:T(8,128)(2,1)S(1)}, u32[]{:S(2)}, u32[]{:S(2)}) %collective-permute-start.18) | collective-permute-done | bytes 213024 | tf_op jit(solution)/shard_map/ppermute | solution.py:851
  101.8 2.2 %collective-permute-done.22.refs_1_ = bf16[1,208,512]{2,1,0:T(8,128)(2,1)S(1)} collective-permute-done((bf16[1,208,512]{2,1,0:T(8,128)(2,1)S(1)}, bf16[1,208,512]{2,1,0:T(8,128)(2,1)S(1)}, u32[]{:S(2)}, u32[]{:S(2)}) %collective-permute-start.22) | collective-permute-done | bytes 213024 | tf_op jit(solution)/shard_map/ppermute | solution.py:851
  105.1 1.5 collective-permute-start.25
  106.6 1.6 %collective-permute-done.27.refs_1_ = bf16[1,192,512]{2,1,0:T(8,128)(2,1)S(1)} collective-permute-done((bf16[1,192,512]{2,1,0:T(8,128)(2,1)S(1)}, bf16[1,192,512]{2,1,0:T(8,128)(2,1)S(1)}, u32[]{:S(2)}, u32[]{:S(2)}) %collective-permute-start.27) | collective-permute-done | bytes 196640 | tf_op jit(solution)/shard_map/ppermute | solution.py:851
  108.4 1.6 %collective-permute-start.30 = (bf16[1,192,512]{2,1,0:T(8,128)(2,1)S(1)}, bf16[1,192,512]{2,1,0:T(8,128)(2,1)S(1)}, u32[]{:S(2)}, u32[]{:S(2)}) collective-permute-start(bf16[1,192,512]{2,1,0:T(8,128)(2,1)S(1)} %get-tuple-element.223), channel_id=1, source_target_pairs={{0,4},{1,3},{2,0},{3,7},{4,8},{5,1},{6,2},{7,11},{8,12},{9,5},{10,... | collective-permute-start | bytes 589832 | tf_op jit(solution)/shard_map/ppermute | solution.py:851
  114.5 2.3 %collective-permute-start.34 = (bf16[1,192,512]{2,1,0:T(8,128)(2,1)S(1)}, bf16[1,192,512]{2,1,0:T(8,128)(2,1)S(1)}, u32[]{:S(2)}, u32[]{:S(2)}) collective-permute-start(bf16[1,192,512]{2,1,0:T(8,128)(2,1)S(1)} %shard_map.311.refs_0_), channel_id=1, source_target_pairs={{0,2},{1,5},{2,6},{3,1},{4,0},{5,9},{6,10},{7,3},{8,4},{9,13},{10,... | collective-permute-start | bytes 589832 | tf_op jit(solution)/shard_map/ppermute | solution.py:851
  116.8 2.2 %collective-permute-done.29.refs_1_ = bf16[1,208,512]{2,1,0:T(8,128)(2,1)S(1)} collective-permute-done((bf16[1,208,512]{2,1,0:T(8,128)(2,1)S(1)}, bf16[1,208,512]{2,1,0:T(8,128)(2,1)S(1)}, u32[]{:S(2)}, u32[]{:S(2)}) %collective-permute-start.29) | collective-permute-done | bytes 213024 | tf_op jit(solution)/shard_map/ppermute | solution.py:851
  118.9 1.5 collective-permute-done.28.refs_0_
  120.5 1.7 %collective-permute-start.32 = (bf16[1,208,512]{2,1,0:T(8,128)(2,1)S(1)}, bf16[1,208,512]{2,1,0:T(8,128)(2,1)S(1)}, u32[]{:S(2)}, u32[]{:S(2)}) collective-permute-start(bf16[1,208,512]{2,1,0:T(8,128)(2,1)S(1)} %get-tuple-element.247.refs_4_), channel_id=1, source_target_pairs={{0,2},{1,5},{2,6},{3,1},{4,0},{5,9},{6,10},{7,3},{8,4},{9,13},{10,... | collective-permute-start | bytes 638984 | tf_op jit(solution)/shard_map/ppermute | solution.py:851
  123.4 3.4 %collective-permute-start.38 = (bf16[1,192,512]{2,1,0:T(8,128)(2,1)S(1)}, bf16[1,192,512]{2,1,0:T(8,128)(2,1)S(1)}, u32[]{:S(2)}, u32[]{:S(2)}) collective-permute-start(bf16[1,192,512]{2,1,0:T(8,128)(2,1)S(1)} %get-tuple-element.253.refs_4_), channel_id=1, source_target_pairs={{0,2},{1,5},{2,6},{3,1},{4,0},{5,9},{6,10},{7,3},{8,4},{9,13},{10,... | collective-permute-start | bytes 589832 | tf_op jit(solution)/shard_map/ppermute | solution.py:851
  126.8 1.9 %collective-permute-done.32.refs_1_ = bf16[1,208,512]{2,1,0:T(8,128)(2,1)S(1)} collective-permute-done((bf16[1,208,512]{2,1,0:T(8,128)(2,1)S(1)}, bf16[1,208,512]{2,1,0:T(8,128)(2,1)S(1)}, u32[]{:S(2)}, u32[]{:S(2)}) %collective-permute-start.32) | collective-permute-done | bytes 213024 | tf_op jit(solution)/shard_map/ppermute | solution.py:851
  128.7 1.3 collective-permute-done.31.refs_0_
  130.0 2.2 %collective-permute-done.38.refs_1_ = bf16[1,192,512]{2,1,0:T(8,128)(2,1)S(1)} collective-permute-done((bf16[1,192,512]{2,1,0:T(8,128)(2,1)S(1)}, bf16[1,192,512]{2,1,0:T(8,128)(2,1)S(1)}, u32[]{:S(2)}, u32[]{:S(2)}) %collective-permute-start.38) | collective-permute-done | bytes 196640 | tf_op jit(solution)/shard_map/ppermute | solution.py:851
  133.3 1.7 %collective-permute-start.36 = (bf16[1,208,512]{2,1,0:T(8,128)(2,1)S(1)}, bf16[1,208,512]{2,1,0:T(8,128)(2,1)S(1)}, u32[]{:S(2)}, u32[]{:S(2)}) collective-permute-start(bf16[1,208,512]{2,1,0:T(8,128)(2,1)S(1)} %get-tuple-element.246.refs_3_), channel_id=1, source_target_pairs={{0,2},{1,5},{2,6},{3,1},{4,0},{5,9},{6,10},{7,3},{8,4},{9,13},{10,... | collective-permute-start | bytes 638984 | tf_op jit(solution)/shard_map/ppermute | solution.py:851
  135.3 1.7 %collective-permute-start.43 = (bf16[1,192,512]{2,1,0:T(8,128)(2,1)S(1)}, bf16[1,192,512]{2,1,0:T(8,128)(2,1)S(1)}, u32[]{:S(2)}, u32[]{:S(2)}) collective-permute-start(bf16[1,192,512]{2,1,0:T(8,128)(2,1)S(1)} %get-tuple-element.252.refs_3_), channel_id=1, source_target_pairs={{0,2},{1,5},{2,6},{3,1},{4,0},{5,9},{6,10},{7,3},{8,4},{9,13},{10,... | collective-permute-start | bytes 589832 | tf_op jit(solution)/shard_map/ppermute | solution.py:851
  137.1 4.3 %collective-permute-done.36.refs_1_ = bf16[1,208,512]{2,1,0:T(8,128)(2,1)S(1)} collective-permute-done((bf16[1,208,512]{2,1,0:T(8,128)(2,1)S(1)}, bf16[1,208,512]{2,1,0:T(8,128)(2,1)S(1)}, u32[]{:S(2)}, u32[]{:S(2)}) %collective-permute-start.36) | collective-permute-done | bytes 213024 | tf_op jit(solution)/shard_map/ppermute | solution.py:851
  142.3 2.8 %shard_map.318 = (f32[2048,512]{1,0:T(8,128)}, f32[512,2048]{1,0:T(8,128)}, f32[512,1536]{1,0:T(8,128)}, f32[512,512]{1,0:T(8,128)}, f32[512,128]{1,0:T(8,128)}) custom-call(s32[8]{0:T(128)S(1)} %stack.36.where_ref, bf16[5,208,512]{2,1,0:T(8,128)(2,1)S(1)} %shard_map.316.refs_0_, bf16[5,192,512]{2,1,0:T(8,128)(2,1)S(1)} %shard_map.317.refs_1_.refs_2_), custom_call_target="tpu_custom_call" | custom-call | flops 100000000 | bytes 10000000 | tf_op jit(solution)/shard_map/pallas_call | solution.py:792
  148.3 2.8 %shard_map.321 = (f32[2048,512]{1,0:T(8,128)}, f32[512,2048]{1,0:T(8,128)}, f32[512,1536]{1,0:T(8,128)}, f32[512,512]{1,0:T(8,128)}, f32[512,128]{1,0:T(8,128)}) custom-call(s32[8]{0:T(128)S(1)} %stack.36.where_ref, ...), custom_call_target="tpu_custom_call", output_to_operand_aliasing={{0}: (3, {}), {1}: (4, {}), {2}: (5, {}), {3}: (6, {}), {4}... | custom-call | flops 100000000 | bytes 10000000 | tf_op jit(solution)/shard_map/pallas_call | solution.py:792
  151.2 2.0 %collective-permute-done.44.refs_0_ = bf16[1,192,512]{2,1,0:T(8,128)(2,1)S(1)} collective-permute-done((bf16[1,192,512]{2,1,0:T(8,128)(2,1)S(1)}, bf16[1,192,512]{2,1,0:T(8,128)(2,1)S(1)}, u32[]{:S(2)}, u32[]{:S(2)}) %collective-permute-start.44) | collective-permute-done | bytes 196640 | tf_op jit(solution)/shard_map/ppermute | solution.py:851
  154.5 2.2 %shard_map.326 = (f32[2048,512]{1,0:T(8,128)}, f32[512,2048]{1,0:T(8,128)}, f32[512,1536]{1,0:T(8,128)}, f32[512,512]{1,0:T(8,128)}, f32[512,128]{1,0:T(8,128)}) custom-call(s32[8]{0:T(128)S(1)} %stack.36.where_ref, bf16[3,208,512]{2,1,0:T(8,128)(2,1)S(1)} %shard_map.324.refs_0_, ...), custom_call_target="tpu_custom_call", output_to_operand_aliasing={{0}: (3, {}), {1}: (4, {}), {2}: (5, {}), {3}: (6, {}), {4}... | custom-call | flops 100000000 | bytes 10000000 | tf_op jit(solution)/shard_map/pallas_call | solution.py:792
  156.7 2.8 %shard_map.327 = (f32[2048,512]{1,0:T(8,128)}, f32[512,2048]{1,0:T(8,128)}, f32[512,1536]{1,0:T(8,128)}, f32[512,512]{1,0:T(8,128)}, f32[512,128]{1,0:T(8,128)},...) custom-call(s32[8]{0:T(128)S(1)} %stack.36.where_ref, ...), custom_call_target="tpu_custom_call", output_to_operand_aliasing={{0}: (6, {}), {1}: (7, {}), {2}: (8, {}), {3}: (9, {}), {4}... | custom-call | flops 100000000 | bytes 10000000 | tf_op jit(solution)/shard_map/pallas_call | solution.py:792
  (131 shorter events, 32.0 us)
Async XLA Ops:
  11.1 5.3 %collective-permute-start = (bf16[272,128]{1,0:T(8,128)(2,1)S(1)}, bf16[272,128]{1,0:T(8,128)(2,1)S(1)}, u32[]{:S(2)}, u32[]{:S(2)}) collective-permute-start(bf16[272,128]{1,0:T(8,128)(2,1)S(1)} %get-tuple-element.161), channel_id=1, source_target_pairs={{0,16},{16,0},{1,17},{17,1},{2,18},{18,2},{3,19},{19,3},{4,20},{20... | collective-permute-start | bytes 208904 | tf_op jit(solution)/shard_map/ppermute | solution.py:832
  16.5 4.8 %collective-permute-start.1 = (bf16[272,128]{1,0:T(8,128)(2,1)S(1)}, bf16[272,128]{1,0:T(8,128)(2,1)S(1)}, u32[]{:S(2)}, u32[]{:S(2)}) collective-permute-start(bf16[272,128]{1,0:T(8,128)(2,1)S(1)} %broadcast_select_fusion), channel_id=1, source_target_pairs={{0,2},{1,3},{2,0},{3,1},{4,6},{5,7},{6,4},{7,5},{8,10},{9,11},{10,... | collective-permute-start | bytes 208904 | tf_op jit(solution)/shard_map/ppermute | solution.py:832
  18.6 5.2 %collective-permute-start.3 = (bf16[256,128]{1,0:T(8,128)(2,1)S(1)}, bf16[256,128]{1,0:T(8,128)(2,1)S(1)}, u32[]{:S(2)}, u32[]{:S(2)}) collective-permute-start(bf16[256,128]{1,0:T(8,128)(2,1)S(1)} %slice_select_fusion), channel_id=1, source_target_pairs={{0,8},{1,9},{2,10},{3,11},{4,12},{5,13},{6,14},{7,15},{8,0},{9,1},... | collective-permute-start | bytes 196616 | tf_op jit(solution)/shard_map/ppermute | solution.py:832
  21.3 6.9 %collective-permute-start.2 = (bf16[544,128]{1,0:T(8,128)(2,1)S(1)}, bf16[544,128]{1,0:T(8,128)(2,1)S(1)}, u32[]{:S(2)}, u32[]{:S(2)}) collective-permute-start(bf16[544,128]{1,0:T(8,128)(2,1)S(1)} %pad_maximum_fusion.near_ref), channel_id=1, source_target_pairs={{0,1},{1,0},{2,3},{3,2},{4,5},{5,4},{6,7},{7,6},{8,9},{9,8},{10,11... | collective-permute-start | bytes 417800 | tf_op jit(solution)/shard_map/ppermute | solution.py:832
  23.8 37.7 %copy-start.14 = (f32[256,128]{1,0:T(8,128)S(1)}, f32[256,128]{1,0:T(8,128)}, u32[]{:S(2)}) copy-start(f32[256,128]{1,0:T(8,128)} %get-tuple-element.176.rs2_ref) | copy-start | bytes 393220
  23.9 4.3 %collective-permute-start.4 = (bf16[256,128]{1,0:T(8,128)(2,1)S(1)}, bf16[256,128]{1,0:T(8,128)(2,1)S(1)}, u32[]{:S(2)}, u32[]{:S(2)}) collective-permute-start(bf16[256,128]{1,0:T(8,128)(2,1)S(1)} %broadcast_select_fusion.1.refs_0_), channel_id=1, source_target_pairs={{0,4},{1,5},{2,6},{3,7},{4,0},{5,1},{6,2},{7,3},{8,12},{9,13},{10,... | collective-permute-start | bytes 196616 | tf_op jit(solution)/shard_map/ppermute | solution.py:832
  31.1 1.2 collective-permute-start.5
  32.3 3.7 %collective-permute-start.6 = (f32[32,128]{1,0:T(8,128)S(1)}, f32[32,128]{1,0:T(8,128)S(1)}, u32[]{:S(2)}, u32[]{:S(2)}) collective-permute-start(f32[32,128]{1,0:T(8,128)S(1)} %add.42), channel_id=1, source_target_pairs={{0,2},{1,3},{2,0},{3,1},{4,6},{5,7},{6,4},{7,5},{8,10},{9,11},{10,... | collective-permute-start | bytes 49160 | tf_op jit(solution)/shard_map/ppermute | solution.py:832
  36.1 3.7 %collective-permute-start.7 = (f32[32,128]{1,0:T(8,128)S(1)}, f32[32,128]{1,0:T(8,128)S(1)}, u32[]{:S(2)}, u32[]{:S(2)}) collective-permute-start(f32[32,128]{1,0:T(8,128)S(1)} %add.43), channel_id=1, source_target_pairs={{0,16},{16,0},{1,17},{17,1},{2,18},{18,2},{3,19},{19,3},{4,20},{20... | collective-permute-start | bytes 49160 | tf_op jit(solution)/shard_map/ppermute | solution.py:832
  45.0 1.7 %collective-permute-start.10 = (bf16[512,128]{1,0:T(8,128)(2,1)S(1)}, bf16[512,128]{1,0:T(8,128)(2,1)S(1)}, u32[]{:S(2)}, u32[]{:S(2)}) collective-permute-start(bf16[512,128]{1,0:T(8,128)(2,1)S(1)} %slice.47), channel_id=1, source_target_pairs={{0,1},{1,0},{2,3},{3,2},{4,5},{5,4},{6,7},{7,6},{8,9},{9,8},{10,11... | collective-permute-start | bytes 393224 | tf_op jit(solution)/shard_map/ppermute | solution.py:832
  45.1 4.6 %collective-permute-start.8 = (bf16[272,128]{1,0:T(8,128)(2,1)S(1)}, bf16[272,128]{1,0:T(8,128)(2,1)S(1)}, u32[]{:S(2)}, u32[]{:S(2)}) collective-permute-start(bf16[272,128]{1,0:T(8,128)(2,1)S(1)} %get-tuple-element.167), channel_id=1, source_target_pairs={{0,4},{1,5},{2,6},{3,7},{4,0},{5,1},{6,2},{7,3},{8,12},{9,13},{10,... | collective-permute-start | bytes 208904 | tf_op jit(solution)/shard_map/ppermute | solution.py:832
  46.8 6.0 %collective-permute-start.11 = (bf16[256,128]{1,0:T(8,128)(2,1)S(1)}, bf16[256,128]{1,0:T(8,128)(2,1)S(1)}, u32[]{:S(2)}, u32[]{:S(2)}) collective-permute-start(bf16[256,128]{1,0:T(8,128)(2,1)S(1)} %slice.63), channel_id=1, source_target_pairs={{0,2},{1,3},{2,0},{3,1},{4,6},{5,7},{6,4},{7,5},{8,10},{9,11},{10,... | collective-permute-start | bytes 196616 | tf_op jit(solution)/shard_map/ppermute | solution.py:832
  49.8 6.8 %collective-permute-start.9 = (bf16[272,128]{1,0:T(8,128)(2,1)S(1)}, bf16[272,128]{1,0:T(8,128)(2,1)S(1)}, u32[]{:S(2)}, u32[]{:S(2)}) collective-permute-start(bf16[272,128]{1,0:T(8,128)(2,1)S(1)} %get-tuple-element.169.near_ref), channel_id=1, source_target_pairs={{0,8},{1,9},{2,10},{3,11},{4,12},{5,13},{6,14},{7,15},{8,0},{9,1},... | collective-permute-start | bytes 208904 | tf_op jit(solution)/shard_map/ppermute | solution.py:832
  57.2 4.3 %collective-permute-start.12 = (bf16[256,128]{1,0:T(8,128)(2,1)S(1)}, bf16[256,128]{1,0:T(8,128)(2,1)S(1)}, u32[]{:S(2)}, u32[]{:S(2)}) collective-permute-start(bf16[256,128]{1,0:T(8,128)(2,1)S(1)} %get-tuple-element.174), channel_id=1, source_target_pairs={{0,16},{16,0},{1,17},{17,1},{2,18},{18,2},{3,19},{19,3},{4,20},{20... | collective-permute-start | bytes 196616 | tf_op jit(solution)/shard_map/ppermute | solution.py:832
  70.9 5.9 %collective-permute-start.13 = (bf16[8,208,512]{2,1,0:T(8,128)(2,1)S(1)}, bf16[8,208,512]{2,1,0:T(8,128)(2,1)S(1)}, u32[]{:S(2)}, u32[]{:S(2)}) collective-permute-start(bf16[8,208,512]{2,1,0:T(8,128)(2,1)S(1)} %get-tuple-element.193), channel_id=1, source_target_pairs={{0,1},{1,0},{2,3},{3,2},{4,5},{5,4},{6,7},{7,6},{8,9},{9,8},{10,11... | collective-permute-start | bytes 5111816 | tf_op jit(solution)/shard_map/ppermute | solution.py:832
  76.3 3.5 %collective-permute-start.16 = (bf16[8,192,512]{2,1,0:T(8,128)(2,1)S(1)}, bf16[8,192,512]{2,1,0:T(8,128)(2,1)S(1)}, u32[]{:S(2)}, u32[]{:S(2)}) collective-permute-start(bf16[8,192,512]{2,1,0:T(8,128)(2,1)S(1)} %get-tuple-element.197), channel_id=1, source_target_pairs={{0,1},{1,0},{2,3},{3,2},{4,5},{5,4},{6,7},{7,6},{8,9},{9,8},{10,11... | collective-permute-start | bytes 4718600 | tf_op jit(solution)/shard_map/ppermute | solution.py:832
  76.9 10.4 %collective-permute-start.15 = (bf16[1,208,512]{2,1,0:T(8,128)(2,1)S(1)}, bf16[1,208,512]{2,1,0:T(8,128)(2,1)S(1)}, u32[]{:S(2)}, u32[]{:S(2)}) collective-permute-start(bf16[1,208,512]{2,1,0:T(8,128)(2,1)S(1)} %get-tuple-element.306), channel_id=1, source_target_pairs={{0,2},{1,5},{2,6},{3,1},{4,0},{5,9},{6,10},{7,3},{8,4},{9,13},{10,... | collective-permute-start | bytes 638984 | tf_op jit(solution)/shard_map/ppermute | solution.py:851
  79.9 9.6 %collective-permute-start.20 = (bf16[1,192,512]{2,1,0:T(8,128)(2,1)S(1)}, bf16[1,192,512]{2,1,0:T(8,128)(2,1)S(1)}, u32[]{:S(2)}, u32[]{:S(2)}) collective-permute-start(bf16[1,192,512]{2,1,0:T(8,128)(2,1)S(1)} %get-tuple-element.309), channel_id=1, source_target_pairs={{0,2},{1,5},{2,6},{3,1},{4,0},{5,9},{6,10},{7,3},{8,4},{9,13},{10,... | collective-permute-start | bytes 589832 | tf_op jit(solution)/shard_map/ppermute | solution.py:851
  80.5 6.8 %collective-permute-start.14 = (bf16[1,208,512]{2,1,0:T(8,128)(2,1)S(1)}, bf16[1,208,512]{2,1,0:T(8,128)(2,1)S(1)}, u32[]{:S(2)}, u32[]{:S(2)}) collective-permute-start(bf16[1,208,512]{2,1,0:T(8,128)(2,1)S(1)} %get-tuple-element.307), channel_id=1, source_target_pairs={{0,4},{1,3},{2,0},{3,7},{4,8},{5,1},{6,2},{7,11},{8,12},{9,5},{10,... | collective-permute-start | bytes 638984 | tf_op jit(solution)/shard_map/ppermute | solution.py:851
  82.5 7.0 %collective-permute-start.19 = (bf16[1,192,512]{2,1,0:T(8,128)(2,1)S(1)}, bf16[1,192,512]{2,1,0:T(8,128)(2,1)S(1)}, u32[]{:S(2)}, u32[]{:S(2)}) collective-permute-start(bf16[1,192,512]{2,1,0:T(8,128)(2,1)S(1)} %get-tuple-element.308), channel_id=1, source_target_pairs={{0,4},{1,3},{2,0},{3,7},{4,8},{5,1},{6,2},{7,11},{8,12},{9,5},{10,... | collective-permute-start | bytes 589832 | tf_op jit(solution)/shard_map/ppermute | solution.py:851
  87.4 7.9 %collective-permute-start.18 = (bf16[1,208,512]{2,1,0:T(8,128)(2,1)S(1)}, bf16[1,208,512]{2,1,0:T(8,128)(2,1)S(1)}, u32[]{:S(2)}, u32[]{:S(2)}) collective-permute-start(bf16[1,208,512]{2,1,0:T(8,128)(2,1)S(1)} %get-tuple-element.205), channel_id=1, source_target_pairs={{0,2},{1,5},{2,6},{3,1},{4,0},{5,9},{6,10},{7,3},{8,4},{9,13},{10,... | collective-permute-start | bytes 638984 | tf_op jit(solution)/shard_map/ppermute | solution.py:851
  88.0 8.1 %collective-permute-start.17 = (bf16[1,208,512]{2,1,0:T(8,128)(2,1)S(1)}, bf16[1,208,512]{2,1,0:T(8,128)(2,1)S(1)}, u32[]{:S(2)}, u32[]{:S(2)}) collective-permute-start(bf16[1,208,512]{2,1,0:T(8,128)(2,1)S(1)} %get-tuple-element.204), channel_id=1, source_target_pairs={{0,4},{1,3},{2,0},{3,7},{4,8},{5,1},{6,2},{7,11},{8,12},{9,5},{10,... | collective-permute-start | bytes 638984 | tf_op jit(solution)/shard_map/ppermute | solution.py:851
  89.6 9.9 %collective-permute-start.24 = (bf16[1,192,512]{2,1,0:T(8,128)(2,1)S(1)}, bf16[1,192,512]{2,1,0:T(8,128)(2,1)S(1)}, u32[]{:S(2)}, u32[]{:S(2)}) collective-permute-start(bf16[1,192,512]{2,1,0:T(8,128)(2,1)S(1)} %get-tuple-element.213), channel_id=1, source_target_pairs={{0,2},{1,5},{2,6},{3,1},{4,0},{5,9},{6,10},{7,3},{8,4},{9,13},{10,... | collective-permute-start | bytes 589832 | tf_op jit(solution)/shard_map/ppermute | solution.py:851
  90.2 9.5 %collective-permute-start.23 = (bf16[1,192,512]{2,1,0:T(8,128)(2,1)S(1)}, bf16[1,192,512]{2,1,0:T(8,128)(2,1)S(1)}, u32[]{:S(2)}, u32[]{:S(2)}) collective-permute-start(bf16[1,192,512]{2,1,0:T(8,128)(2,1)S(1)} %get-tuple-element.208), channel_id=1, source_target_pairs={{0,4},{1,3},{2,0},{3,7},{4,8},{5,1},{6,2},{7,11},{8,12},{9,5},{10,... | collective-permute-start | bytes 589832 | tf_op jit(solution)/shard_map/ppermute | solution.py:851
  96.2 7.8 %collective-permute-start.22 = (bf16[1,208,512]{2,1,0:T(8,128)(2,1)S(1)}, bf16[1,208,512]{2,1,0:T(8,128)(2,1)S(1)}, u32[]{:S(2)}, u32[]{:S(2)}) collective-permute-start(bf16[1,208,512]{2,1,0:T(8,128)(2,1)S(1)} %get-tuple-element.212), channel_id=1, source_target_pairs={{0,2},{1,5},{2,6},{3,1},{4,0},{5,9},{6,10},{7,3},{8,4},{9,13},{10,... | collective-permute-start | bytes 638984 | tf_op jit(solution)/shard_map/ppermute | solution.py:851
  97.3 7.7 %collective-permute-start.21 = (bf16[1,208,512]{2,1,0:T(8,128)(2,1)S(1)}, bf16[1,208,512]{2,1,0:T(8,128)(2,1)S(1)}, u32[]{:S(2)}, u32[]{:S(2)}) collective-permute-start(bf16[1,208,512]{2,1,0:T(8,128)(2,1)S(1)} %get-tuple-element.211), channel_id=1, source_target_pairs={{0,4},{1,3},{2,0},{3,7},{4,8},{5,1},{6,2},{7,11},{8,12},{9,5},{10,... | collective-permute-start | bytes 638984 | tf_op jit(solution)/shard_map/ppermute | solution.py:851
  99.7 8.6 %collective-permute-start.27 = (bf16[1,192,512]{2,1,0:T(8,128)(2,1)S(1)}, bf16[1,192,512]{2,1,0:T(8,128)(2,1)S(1)}, u32[]{:S(2)}, u32[]{:S(2)}) collective-permute-start(bf16[1,192,512]{2,1,0:T(8,128)(2,1)S(1)} %get-tuple-element.220), channel_id=1, source_target_pairs={{0,2},{1,5},{2,6},{3,1},{4,0},{5,9},{6,10},{7,3},{8,4},{9,13},{10,... | collective-permute-start | bytes 589832 | tf_op jit(solution)/shard_map/ppermute | solution.py:851
  100.6 7.7 %collective-permute-start.26 = (bf16[1,192,512]{2,1,0:T(8,128)(2,1)S(1)}, bf16[1,192,512]{2,1,0:T(8,128)(2,1)S(1)}, u32[]{:S(2)}, u32[]{:S(2)}) collective-permute-start(bf16[1,192,512]{2,1,0:T(8,128)(2,1)S(1)} %get-tuple-element.216), channel_id=1, source_target_pairs={{0,4},{1,3},{2,0},{3,7},{4,8},{5,1},{6,2},{7,11},{8,12},{9,5},{10,... | collective-permute-start | bytes 589832 | tf_op jit(solution)/shard_map/ppermute | solution.py:851
  105.1 5.9 %collective-permute-start.25 = (bf16[1,208,512]{2,1,0:T(8,128)(2,1)S(1)}, bf16[1,208,512]{2,1,0:T(8,128)(2,1)S(1)}, u32[]{:S(2)}, u32[]{:S(2)}) collective-permute-start(bf16[1,208,512]{2,1,0:T(8,128)(2,1)S(1)} %get-tuple-element.219), channel_id=1, source_target_pairs={{0,4},{1,3},{2,0},{3,7},{4,8},{5,1},{6,2},{7,11},{8,12},{9,5},{10,... | collective-permute-start | bytes 638984 | tf_op jit(solution)/shard_map/ppermute | solution.py:851
  108.4 6.0 %collective-permute-start.30 = (bf16[1,192,512]{2,1,0:T(8,128)(2,1)S(1)}, bf16[1,192,512]{2,1,0:T(8,128)(2,1)S(1)}, u32[]{:S(2)}, u32[]{:S(2)}) collective-permute-start(bf16[1,192,512]{2,1,0:T(8,128)(2,1)S(1)} %get-tuple-element.223), channel_id=1, source_target_pairs={{0,4},{1,3},{2,0},{3,7},{4,8},{5,1},{6,2},{7,11},{8,12},{9,5},{10,... | collective-permute-start | bytes 589832 | tf_op jit(solution)/shard_map/ppermute | solution.py:851
  111.1 7.9 %collective-permute-start.29 = (bf16[1,208,512]{2,1,0:T(8,128)(2,1)S(1)}, bf16[1,208,512]{2,1,0:T(8,128)(2,1)S(1)}, u32[]{:S(2)}, u32[]{:S(2)}) collective-permute-start(bf16[1,208,512]{2,1,0:T(8,128)(2,1)S(1)} %shard_map.310.refs_0_), channel_id=1, source_target_pairs={{0,2},{1,5},{2,6},{3,1},{4,0},{5,9},{6,10},{7,3},{8,4},{9,13},{10,... | collective-permute-start | bytes 638984 | tf_op jit(solution)/shard_map/ppermute | solution.py:851
  112.2 8.2 %collective-permute-start.28 = (bf16[1,208,512]{2,1,0:T(8,128)(2,1)S(1)}, bf16[1,208,512]{2,1,0:T(8,128)(2,1)S(1)}, u32[]{:S(2)}, u32[]{:S(2)}) collective-permute-start(bf16[1,208,512]{2,1,0:T(8,128)(2,1)S(1)} %shard_map.310.refs_0_), channel_id=1, source_target_pairs={{0,4},{1,3},{2,0},{3,7},{4,8},{5,1},{6,2},{7,11},{8,12},{9,5},{10,... | collective-permute-start | bytes 638984 | tf_op jit(solution)/shard_map/ppermute | solution.py:851
  114.5 8.7 %collective-permute-start.34 = (bf16[1,192,512]{2,1,0:T(8,128)(2,1)S(1)}, bf16[1,192,512]{2,1,0:T(8,128)(2,1)S(1)}, u32[]{:S(2)}, u32[]{:S(2)}) collective-permute-start(bf16[1,192,512]{2,1,0:T(8,128)(2,1)S(1)} %shard_map.311.refs_0_), channel_id=1, source_target_pairs={{0,2},{1,5},{2,6},{3,1},{4,0},{5,9},{6,10},{7,3},{8,4},{9,13},{10,... | collective-permute-start | bytes 589832 | tf_op jit(solution)/shard_map/ppermute | solution.py:851
  116.7 6.6 %collective-permute-start.33 = (bf16[1,192,512]{2,1,0:T(8,128)(2,1)S(1)}, bf16[1,192,512]{2,1,0:T(8,128)(2,1)S(1)}, u32[]{:S(2)}, u32[]{:S(2)}) collective-permute-start(bf16[1,192,512]{2,1,0:T(8,128)(2,1)S(1)} %shard_map.311.refs_0_), channel_id=1, source_target_pairs={{0,4},{1,3},{2,0},{3,7},{4,8},{5,1},{6,2},{7,11},{8,12},{9,5},{10,... | collective-permute-start | bytes 589832 | tf_op jit(solution)/shard_map/ppermute | solution.py:851
  120.5 8.2 %collective-permute-start.32 = (bf16[1,208,512]{2,1,0:T(8,128)(2,1)S(1)}, bf16[1,208,512]{2,1,0:T(8,128)(2,1)S(1)}, u32[]{:S(2)}, u32[]{:S(2)}) collective-permute-start(bf16[1,208,512]{2,1,0:T(8,128)(2,1)S(1)} %get-tuple-element.247.refs_4_), channel_id=1, source_target_pairs={{0,2},{1,5},{2,6},{3,1},{4,0},{5,9},{6,10},{7,3},{8,4},{9,13},{10,... | collective-permute-start | bytes 638984 | tf_op jit(solution)/shard_map/ppermute | solution.py:851
  122.2 7.8 %collective-permute-start.31 = (bf16[1,208,512]{2,1,0:T(8,128)(2,1)S(1)}, bf16[1,208,512]{2,1,0:T(8,128)(2,1)S(1)}, u32[]{:S(2)}, u32[]{:S(2)}) collective-permute-start(bf16[1,208,512]{2,1,0:T(8,128)(2,1)S(1)} %get-tuple-element.244.refs_1_), channel_id=1, source_target_pairs={{0,4},{1,3},{2,0},{3,7},{4,8},{5,1},{6,2},{7,11},{8,12},{9,5},{10,... | collective-permute-start | bytes 638984 | tf_op jit(solution)/shard_map/ppermute | solution.py:851
  123.4 8.9 %collective-permute-start.38 = (bf16[1,192,512]{2,1,0:T(8,128)(2,1)S(1)}, bf16[1,192,512]{2,1,0:T(8,128)(2,1)S(1)}, u32[]{:S(2)}, u32[]{:S(2)}) collective-permute-start(bf16[1,192,512]{2,1,0:T(8,128)(2,1)S(1)} %get-tuple-element.253.refs_4_), channel_id=1, source_target_pairs={{0,2},{1,5},{2,6},{3,1},{4,0},{5,9},{6,10},{7,3},{8,4},{9,13},{10,... | collective-permute-start | bytes 589832 | tf_op jit(solution)/shard_map/ppermute | solution.py:851
  126.8 5.7 %collective-permute-start.37 = (bf16[1,192,512]{2,1,0:T(8,128)(2,1)S(1)}, bf16[1,192,512]{2,1,0:T(8,128)(2,1)S(1)}, u32[]{:S(2)}, u32[]{:S(2)}) collective-permute-start(bf16[1,192,512]{2,1,0:T(8,128)(2,1)S(1)} %get-tuple-element.250.refs_1_), channel_id=1, source_target_pairs={{0,4},{1,3},{2,0},{3,7},{4,8},{5,1},{6,2},{7,11},{8,12},{9,5},{10,... | collective-permute-start | bytes 589832 | tf_op jit(solution)/shard_map/ppermute | solution.py:851
  132.6 15.8 %collective-permute-start.40 = (bf16[5,208,512]{2,1,0:T(8,128)(2,1)S(1)}, bf16[5,208,512]{2,1,0:T(8,128)(2,1)S(1)}, u32[]{:S(2)}, u32[]{:S(2)}) collective-permute-start(bf16[5,208,512]{2,1,0:T(8,128)(2,1)S(1)} %shard_map.316.refs_0_), channel_id=1, source_target_pairs={{0,1},{1,0},{2,3},{3,2},{4,5},{5,4},{6,7},{7,6},{8,9},{9,8},{10,11... | collective-permute-start | bytes 3194888 | tf_op jit(solution)/shard_map/ppermute | solution.py:832
  132.7 15.6 %collective-permute-start.41 = (bf16[5,192,512]{2,1,0:T(8,128)(2,1)S(1)}, bf16[5,192,512]{2,1,0:T(8,128)(2,1)S(1)}, u32[]{:S(2)}, u32[]{:S(2)}) collective-permute-start(bf16[5,192,512]{2,1,0:T(8,128)(2,1)S(1)} %shard_map.317.refs_1_.refs_2_), channel_id=1, source_target_pairs={{0,1},{1,0},{2,3},{3,2},{4,5},{5,4},{6,7},{7,6},{8,9},{9,8},{10,11... | collective-permute-start | bytes 2949128 | tf_op jit(solution)/shard_map/ppermute | solution.py:832
  133.3 8.1 %collective-permute-start.36 = (bf16[1,208,512]{2,1,0:T(8,128)(2,1)S(1)}, bf16[1,208,512]{2,1,0:T(8,128)(2,1)S(1)}, u32[]{:S(2)}, u32[]{:S(2)}) collective-permute-start(bf16[1,208,512]{2,1,0:T(8,128)(2,1)S(1)} %get-tuple-element.246.refs_3_), channel_id=1, source_target_pairs={{0,2},{1,5},{2,6},{3,1},{4,0},{5,9},{6,10},{7,3},{8,4},{9,13},{10,... | collective-permute-start | bytes 638984 | tf_op jit(solution)/shard_map/ppermute | solution.py:851
  135.0 10.1 %collective-permute-start.35 = (bf16[1,208,512]{2,1,0:T(8,128)(2,1)S(1)}, bf16[1,208,512]{2,1,0:T(8,128)(2,1)S(1)}, u32[]{:S(2)}, u32[]{:S(2)}) collective-permute-start(bf16[1,208,512]{2,1,0:T(8,128)(2,1)S(1)} %get-tuple-element.245.refs_2_), channel_id=1, source_target_pairs={{0,4},{1,3},{2,0},{3,7},{4,8},{5,1},{6,2},{7,11},{8,12},{9,5},{10,... | collective-permute-start | bytes 638984 | tf_op jit(solution)/shard_map/ppermute | solution.py:851
  135.3 11.1 %collective-permute-start.43 = (bf16[1,192,512]{2,1,0:T(8,128)(2,1)S(1)}, bf16[1,192,512]{2,1,0:T(8,128)(2,1)S(1)}, u32[]{:S(2)}, u32[]{:S(2)}) collective-permute-start(bf16[1,192,512]{2,1,0:T(8,128)(2,1)S(1)} %get-tuple-element.252.refs_3_), channel_id=1, source_target_pairs={{0,2},{1,5},{2,6},{3,1},{4,0},{5,9},{6,10},{7,3},{8,4},{9,13},{10,... | collective-permute-start | bytes 589832 | tf_op jit(solution)/shard_map/ppermute | solution.py:851
  141.4 5.7 %collective-permute-start.42 = (bf16[1,192,512]{2,1,0:T(8,128)(2,1)S(1)}, bf16[1,192,512]{2,1,0:T(8,128)(2,1)S(1)}, u32[]{:S(2)}, u32[]{:S(2)}) collective-permute-start(bf16[1,192,512]{2,1,0:T(8,128)(2,1)S(1)} %get-tuple-element.251.refs_2_), channel_id=1, source_target_pairs={{0,4},{1,3},{2,0},{3,7},{4,8},{5,1},{6,2},{7,11},{8,12},{9,5},{10,... | collective-permute-start | bytes 589832 | tf_op jit(solution)/shard_map/ppermute | solution.py:851
  145.2 6.0 %collective-permute-start.39 = (bf16[1,208,512]{2,1,0:T(8,128)(2,1)S(1)}, bf16[1,208,512]{2,1,0:T(8,128)(2,1)S(1)}, u32[]{:S(2)}, u32[]{:S(2)}) collective-permute-start(bf16[1,208,512]{2,1,0:T(8,128)(2,1)S(1)} %get-tuple-element.273.refs_0_), channel_id=1, source_target_pairs={{0,4},{1,3},{2,0},{3,7},{4,8},{5,1},{6,2},{7,11},{8,12},{9,5},{10,... | collective-permute-start | bytes 638984 | tf_op jit(solution)/shard_map/ppermute | solution.py:851
  147.1 6.1 %collective-permute-start.44 = (bf16[1,192,512]{2,1,0:T(8,128)(2,1)S(1)}, bf16[1,192,512]{2,1,0:T(8,128)(2,1)S(1)}, u32[]{:S(2)}, u32[]{:S(2)}) collective-permute-start(bf16[1,192,512]{2,1,0:T(8,128)(2,1)S(1)} %get-tuple-element.277.refs_0_), channel_id=1, source_target_pairs={{0,4},{1,3},{2,0},{3,7},{4,8},{5,1},{6,2},{7,11},{8,12},{9,5},{10,... | collective-permute-start | bytes 589832 | tf_op jit(solution)/shard_map/ppermute | solution.py:851
  153.3 3.4 %collective-permute-start.45 = (bf16[3,208,512]{2,1,0:T(8,128)(2,1)S(1)}, bf16[3,208,512]{2,1,0:T(8,128)(2,1)S(1)}, u32[]{:S(2)}, u32[]{:S(2)}) collective-permute-start(bf16[3,208,512]{2,1,0:T(8,128)(2,1)S(1)} %shard_map.324.refs_0_), channel_id=1, source_target_pairs={{0,1},{1,0},{2,3},{3,2},{4,5},{5,4},{6,7},{7,6},{8,9},{9,8},{10,11... | collective-permute-start | bytes 1916936 | tf_op jit(solution)/shard_map/ppermute | solution.py:832
  153.4 3.3 %collective-permute-start.46 = (bf16[3,192,512]{2,1,0:T(8,128)(2,1)S(1)}, bf16[3,192,512]{2,1,0:T(8,128)(2,1)S(1)}, u32[]{:S(2)}, u32[]{:S(2)}) collective-permute-start(bf16[3,192,512]{2,1,0:T(8,128)(2,1)S(1)} %shard_map.325.refs_1_.refs_3_), channel_id=1, source_target_pairs={{0,1},{1,0},{2,3},{3,2},{4,5},{5,4},{6,7},{7,6},{8,9},{9,8},{10,11... | collective-permute-start | bytes 1769480 | tf_op jit(solution)/shard_map/ppermute | solution.py:832
  (17 other events, 234.0 us)

commit v5 on v4

--- a/solution.py
+++ b/solution.py
@@ -36,13 +36,14 @@
 SECOND = REST // 16 + TAIL
 CIRCLE = (0, 2, 4, 6, 7, 5, 3, 1)
 RING = len(CIRCLE)
-GROUPS = ((0, 1, 2, 6, 7), (3, 4, 5))
+GROUPS = ((0, 1, 2, 3, 5, 6, 7), (4,))
 STEP_COST = 3 * 10**7
+SPREAD_COST = 0
 ROUND = (("step", 0), ("step", 1))
 ORDER = (
-    (("open", 0), ("open", 1), ("total", 0), ("total", 1)) + ROUND * 6
-    + (("share0", 0), ("share0", 1), ("near", 0)) + ROUND + (("far", 0),) + ROUND
-    + (("share1", 0), ("share1", 1), ("near", 1), ("far", 1))
+    (("open", 0), ("open", 1), ("total", 0), ("total", 1)) + ROUND * 7
+    + (("share", 0, 0), ("share", 1, 0), ("spread", ((True, 0),))) + ROUND
+    + (("share", 0, 1), ("share", 1, 1), ("spread", ((False, 0),)), ("spread", ((True, 1), (False, 1))))
 )
 MIB = 1024 * 1024
 
@@ -249,7 +250,7 @@
         cols = slice(c * step, (c + 1) * step)
         inner = mm(first_low, wup_ref[:, cols]) + bup_ref[:, cols].astype(F32)
         gate = 0.5 + 0.5 * lax.erf(inner * math.sqrt(0.5))
-        bell = jnp.exp(inner * inner * -0.5) * (1.0 / math.sqrt(2.0 * math.pi))
+        bell = jnp.exp2(inner * inner * (-0.5 * LOG2E)) * (1.0 / math.sqrt(2.0 * math.pi))
         act = (inner * gate).astype(BF16)
         act_ref[:, cols] = act
         slope_ref[:, cols] = (gate + inner * bell).astype(BF16)
@@ -411,26 +412,27 @@
 
 
 def matching_back(
-    masks, lanes, total_queries, where_ref, scale_ref, lens_ref, near_ref, far_ref, totals_ref,
-    el_ref, hot_ref, stats_ref, *refs
+    masks, lanes, total_queries, where_ref, scale_ref, lens_ref, totals_ref, el_ref, hot_ref,
+    own_ref, over_y, over_x, over_both, unitq_ref, qt_ref, invq_ref, unit_ref, invd_ref, *refs
 ):
-    doc_refs = refs[:-9]
-    dq_ref, send_ref, keep_ref, loss_ref, turn_ref, unit_ref, qt_ref, dot_ref, dt_ref = refs[-9:]
+    dq_ref, far_ref, keep_ref, send_ref, loss_ref, dot_ref, dt_ref, stats_ref = refs[-8:]
     base, near_at = where_ref[2], where_ref[3]
     temper = SHARPNESS * LOG2E
-    queries = load_queries(near_ref, far_ref)
-    count = queries.shape[0]
-    unit_q, inv_q = unit_queries(queries, temper)
-    unit_q = [u.astype(BF16) for u in unit_q]
-    unit_d, inv_d = unit_docs(doc_refs, turn_ref)
-    for m in range(len(RANGES)):
-        unit_ref[m] = unit_d[m].astype(BF16)
-        qt_ref[m] = unit_q[m].astype(F32).T.astype(BF16)
-    doc_rows = turn_ref.shape[1] // ROW
+    count = unitq_ref.shape[1]
+    inv_q = [invq_ref[:, m : m + 1] for m in range(len(RANGES))]
+    inv_d = [invd_ref[m : m + 1, :] for m in range(len(RANGES))]
+    unit_q = [unitq_ref[m] for m in range(len(RANGES))]
+    doc_rows = unit_ref.shape[2] // ROW
     docs = doc_rows * DOCS_ROW
     ids = row_ids(base, masks, doc_rows)
     marks = doc_marks(lens_ref, ids, lanes, True)
     groups = count // ROW
+    odd_y, odd_x = (near_at & 1) == 1, where_ref[1] == 1
+    parts = [own_ref[...], over_y[...], over_x[...], over_both[...]]
+    parts = [jnp.where(odd_y, a, b) for a, b in ((parts[1], parts[0]), (parts[0], parts[1]),
+                                                  (parts[3], parts[2]), (parts[2], parts[3]))]
+    parts = [jnp.where(odd_x, parts[(k + 2) % 4], parts[k]) for k in range(4)]
+    stats_ref[...] = (parts[0] + parts[1]) + (parts[2] + parts[3])
     rows = []
     for a in range(groups):
         at = pl.multiple_of((near_at ^ a) * 8, 8)
@@ -471,7 +473,10 @@
         for p in range(doc_rows):
             block = unit_ref[m, :, p * ROW : (p + 1) * ROW]
             mark = marks[p][m]
-            exps = jnp.exp2(mm(unit_q[m], block))
+            if len(refs) > 8:
+                exps = refs[0][m, :, p * ROW : (p + 1) * ROW].astype(F32)
+            else:
+                exps = jnp.exp2(mm(unit_q[m], block))
             d_sims = (exps * mm(ratio, jnp.concatenate([mark, mark], axis=0))).astype(BF16)
             grad = grad + mm_nt(d_sims, block)
             dt_ref[m, :, p * ROW : (p + 1) * ROW] = mm(qt_ref[m], d_sims)
@@ -482,8 +487,9 @@
             dot_ref[...] = part
         else:
             dot_ref[...] += part
-    dq_ref[...] = dot_ref[...].astype(BF16)
-    total = jnp.zeros(turn_ref.shape, F32)
+    dq_ref[...] = dot_ref[: count // 2, :].astype(BF16)
+    far_ref[...] = dot_ref[count // 2 :, :].astype(BF16)
+    total = jnp.zeros(unit_ref.shape[1:], F32)
     for m in range(len(RANGES)):
         grad = dt_ref[m] * (1.0 / temper)
         unit = unit_ref[m].astype(F32)
@@ -492,43 +498,57 @@
     for p in range(doc_rows):
         ref, at = (keep_ref, p) if p < doc_rows // 2 else (send_ref, p - doc_rows // 2)
         ref[at * ROW : (at + 1) * ROW, :] = total[:, p * ROW : (p + 1) * ROW].T.astype(BF16)
-    send_ref[doc_rows // 2 * ROW :, :] = packed_loss(loss)
-
-
-def packed_loss(loss):
-    high = loss.astype(BF16)
-    rest = loss - high.astype(F32)
-    middle = rest.astype(BF16)
-    low = rest - middle.astype(F32)
-    lane = iota(loss.shape, 1)
-    packed = jnp.where(lane == 0, high.astype(F32), jnp.where(lane == 1, middle.astype(F32), low))
-    return jnp.concatenate([packed, jnp.zeros_like(packed)], axis=0).astype(BF16)
-
-
-def loss_of(packed):
-    lines = packed.astype(F32)[:8, :]
-    return jnp.sum(jnp.where(iota(lines.shape, 1) < 3, lines, 0.0), axis=1, keepdims=True)
-
-
-def fold_docs(keep_ref, got_ref, loss_ref, *outs):
-    rows = keep_ref.shape[0]
-    loss = loss_ref[...] + loss_of(got_ref[rows:, :])
-    total = (keep_ref[...].astype(F32) + got_ref[:rows, :].astype(F32)).astype(BF16)
-    outs[-1][...] = loss
-    if rows > ROW:
-        outs[0][: rows // 2, :] = total[rows // 2 :, :]
-        outs[0][rows // 2 :, :] = packed_loss(loss)
-        outs[1][...] = total[: rows // 2, :]
-    else:
-        outs[0][:rows, :] = total
-        outs[0][rows:, :] = packed_loss(loss)
-
-
-def last_docs(where_ref, near_ref, got_ref, loss_ref, dq_ref, dd_ref, send_ref, sum_ref):
-    sum_ref[...] = loss_ref[...] + loss_of(got_ref[ROW:, :])
-    total = (near_ref[:ROW, :].astype(F32) + got_ref[:ROW, :].astype(F32)).astype(BF16)
-    dd_ref[...] = total
-    send_ref[...] = jnp.where(where_ref[1] == 0, total, dq_ref[...])
+
+
+def matching_ready(near_ref, far_ref, *refs):
+    doc_refs = refs[:-6] if refs[-2].shape[0] != len(RANGES) else refs[:-7]
+    unitq_ref, qt_ref, invq_ref, unit_ref, invd_ref = refs[len(doc_refs) : len(doc_refs) + 5]
+    turn_ref = refs[-1]
+    queries = load_queries(near_ref, far_ref)
+    unit_q, inv_q = unit_queries(queries, SHARPNESS * LOG2E)
+    unit_d, inv_d = unit_docs(doc_refs, turn_ref)
+    lane = iota(invq_ref.shape, 1)
+    columns = jnp.zeros(invq_ref.shape, F32)
+    invd_ref[...] = jnp.zeros_like(invd_ref)
+    for m in range(len(RANGES)):
+        unitq_ref[m] = unit_q[m].astype(BF16)
+        unit_ref[m] = unit_d[m].astype(BF16)
+        qt_ref[m] = unit_q[m].T.astype(BF16)
+        columns = jnp.where(lane == m, inv_q[m], columns)
+        invd_ref[m : m + 1, :] = inv_d[m]
+        if len(refs) - len(doc_refs) > 6:
+            refs[-2][m] = jnp.exp2(mm(unitq_ref[m], unit_ref[m])).astype(BF16)
+    invq_ref[...] = columns
+
+
+def two_sums(dq_ref, got_ref, dd_ref, got_dd_ref, sum_dq, sum_dd):
+    sum_dq[...] = (dq_ref[...].astype(F32) + got_ref[...].astype(F32)).astype(BF16)
+    sum_dd[...] = (dd_ref[...].astype(F32) + got_dd_ref[...].astype(F32)).astype(BF16)
+
+
+DIGITS = 10
+POINT = 20
+
+
+def digits_of(value):
+    fixed = (value * float(1 << POINT)).astype(jnp.int32)
+    size = jnp.abs(fixed)
+    lane = iota(value.shape, 1)
+    digits = jnp.zeros(value.shape, jnp.int32)
+    for k in range(DIGITS):
+        digits = jnp.where(lane == k, (size >> (3 * k)) & 7, digits)
+    return jnp.where(fixed < 0, -digits, digits).astype(F32)
+
+
+def value_of(digits):
+    lane = iota(digits.shape, 1)
+    half = DIGITS // 2
+    weight = jnp.zeros(digits.shape, F32)
+    for k in range(half):
+        weight = jnp.where(jnp.logical_or(lane == k, lane == k + half), float(8**k), weight)
+    low = jnp.sum(jnp.where(lane < half, digits * weight, 0.0))
+    high = jnp.sum(jnp.where(jnp.logical_and(lane >= half, lane < DIGITS), digits * weight, 0.0))
+    return (high * float(8**half) + low) * (1.0 / (1 << POINT))
 
 
 def turn(core, place, block):
@@ -554,10 +574,25 @@
 
 
 def feed_back(
-    where_ref, dq_ref, dd_ref, got_ref, xh2_ref, rs2_ref, affine_ref, wproj_ref, wdown_ref,
-    slope_ref, act_ref, wup_ref, xh1_ref,
-    keep_ref, send_ref, tail_keep, tail_send, dfirst_ref, gproj_ref, small_ref, dinner_ref,
+    where_ref, dq_ref, dd_ref, got_ref, xh2_ref, rs2_ref, affine_ref, wproj_ref, wup_ref, xh1_ref,
+    wdown_hbm, slope_hbm, act_hbm,
+    keep_ref, send_ref, tail_keep, tail_send, dfirst_ref, gproj_ref, small_ref,
+    dinner_ref, wdown_ref, slope_ref, act_ref, sems,
 ):
+    step = 512
+    spans = [slice(c * step, (c + 1) * step) for c in range(FF // step)]
+    copies = fetch(
+        [
+            pair
+            for span in spans
+            for pair in (
+                (wdown_hbm.at[span, :], wdown_ref.at[span, :]),
+                (slope_hbm.at[:, span], slope_ref.at[:, span]),
+                (act_hbm.at[:, span], act_ref.at[:, span]),
+            )
+        ],
+        sems,
+    )
     g1, s1, g2, s2 = [affine_ref[k : k + 1, :] for k in range(4)]
     is_query, docs_there = where_ref[1] == 0, where_ref[4] == 0
     places = (where_ref[5], where_ref[6])
@@ -579,10 +614,11 @@
     d_sum = norm_back(d_second, xhat, rs2_ref[:, :1], gain)
     d_branch = d_sum.astype(BF16)
     small_ref[4:5, :] = col_sum(d_branch.astype(F32))
-    step = 512
     d_first = d_sum
     for c in range(FF // step):
-        cols = slice(c * step, (c + 1) * step)
+        cols = spans[c]
+        for copy in copies[3 * c : 3 * c + 3]:
+            copy.wait()
         d_act = mm_nt(d_branch, wdown_ref[cols, :])
         d_inner = (d_act * slope_ref[:, cols].astype(F32)).astype(BF16)
         dinner_ref[:, cols] = d_inner
@@ -612,7 +648,7 @@
 
 
 def attend_back(
-    where_ref, dfirst_ref, gproj_ref, small_ref, tail_keep, tail_send, xh1_ref, rs1_ref, affine_ref, mixed_ref, wout_ref,
+    where_ref, dfirst_ref, gproj_ref, small_ref, loss_ref, tail_keep, tail_send, xh1_ref, rs1_ref, affine_ref, mixed_ref, wout_ref,
     qkv_ref, probs_ref, rope_ref, x_ref, wqkv_ref,
     keep_ref, send_ref, tokens_ref, djoined_ref, rest_ref,
 ):
@@ -670,6 +706,9 @@
         tokens = tokens + mm_nt(d_part, wqkv_ref[:, cols])
     tokens_ref[...] = tokens
     smalls += [bias_out, gain_grad, shift_grad] + [small_ref[k : k + 1, :] for k in range(7)]
+    counted = jnp.where((where_ref[0] & 3) == 0, 1.0, 0.0)
+    lines = [digits_of(loss_ref[k : k + 1, :]) * counted for k in range(2)]
+    smalls.append(jnp.concatenate(lines + [jnp.zeros((1, D - 256), F32)], axis=1))
     for k, row in enumerate(smalls):
         rest_ref[4 * D + 8 * k : 4 * D + 8 * k + 1, :] = row
     for k in range(RING):
@@ -692,12 +731,11 @@
             ref[k, REST // 16 :, :] = tail_ref[k]
 
 
-def spread(mine, group, last, where_ref, *refs):
+def spread(jobs, last, where_ref, *refs):
     core, place = where_ref[5], where_ref[6]
-    owner = core if mine else 1 - core
-    one_ref, two_ref = refs[:2]
-    wide_one, wide_two, wide_proj, small_ref, sems = refs[-5:]
-    outs = refs[-18:-5] if last else refs[-10:-5]
+    halves = refs[: 2 * len(jobs)]
+    wide_one, wide_two, wide_qkv, wide_proj, small_ref, sems = refs[-6:]
+    outs = refs[-21:-6] if last else refs[-11:-6]
     down_hbm, up_hbm, qkv_hbm, out_hbm, proj_hbm = outs[:5]
     copies = []
 
@@ -706,41 +744,47 @@
         copy.start()
         copies.append(copy)
 
-    for p, distance in enumerate(GROUPS[group]):
-        block = owner * RING + block_at(owner, place, distance)
-        wide_one[p] = one_ref[p].astype(F32)
-        rows = pl.ds(pl.multiple_of(block * DOWN, DOWN), DOWN)
-        move(wide_one.at[p, :DOWN, :], down_hbm.at[rows, :])
-        wide = two_ref[p].astype(F32)
-        wide_two[p, : 4 * SHARE, :] = wide[: 4 * SHARE, :]
-        wide_two[p, 4 * SHARE :, :] = wide[REST // 16 :, :]
-        start = (block % (D // DOWN)) * DOWN
-        columns = pl.ds(pl.multiple_of((block // (D // DOWN)) * D, D), D)
-        rows = pl.ds(pl.multiple_of(start, DOWN), HEAD)
-        move(wide_one.at[p, DOWN:, :], up_hbm.at[rows, columns])
-        rows = pl.ds(pl.multiple_of(start + HEAD, 16), TAIL)
-        move(wide_two.at[p, 4 * SHARE :, :], up_hbm.at[rows, columns])
-        rows = pl.ds(pl.multiple_of(block * SHARE, SHARE), SHARE)
-        for c in range(3):
-            move(
-                wide_two.at[p, c * SHARE : (c + 1) * SHARE, :],
-                qkv_hbm.at[rows, c * D : (c + 1) * D],
-            )
-        move(wide_two.at[p, 3 * SHARE : 4 * SHARE, :], out_hbm.at[rows, :])
-        for j in range(SHARE // 8):
-            wide_proj[p, 8 * j : 8 * j + 8, :] = wide[
-                4 * SHARE : 4 * SHARE + 8, j * PROJ : (j + 1) * PROJ
-            ]
-        move(wide_proj.at[p], proj_hbm.at[rows, :])
+    at = 0
+    for job, (mine, group) in enumerate(jobs):
+        owner = core if mine else 1 - core
+        one_ref, two_ref = halves[2 * job : 2 * job + 2]
+        for p, distance in enumerate(GROUPS[group]):
+            block = owner * RING + block_at(owner, place, distance)
+            wide_one[at] = one_ref[p].astype(F32)
+            rows = pl.ds(pl.multiple_of(block * DOWN, DOWN), DOWN)
+            move(wide_one.at[at, :DOWN, :], down_hbm.at[rows, :])
+            start = (block % (D // DOWN)) * DOWN
+            columns = pl.ds(pl.multiple_of((block // (D // DOWN)) * D, D), D)
+            rows = pl.ds(pl.multiple_of(start, DOWN), HEAD)
+            move(wide_one.at[at, DOWN:, :], up_hbm.at[rows, columns])
+            wide = two_ref[p].astype(F32)
+            wide_two[at, :SHARE, :] = wide[3 * SHARE : 4 * SHARE, :]
+            wide_two[at, SHARE:, :] = wide[REST // 16 :, :]
+            rows = pl.ds(pl.multiple_of(start + HEAD, 16), TAIL)
+            move(wide_two.at[at, SHARE:, :], up_hbm.at[rows, columns])
+            rows = pl.ds(pl.multiple_of(block * SHARE, SHARE), SHARE)
+            for c in range(3):
+                wide_qkv[at, :, c * D : (c + 1) * D] = wide[c * SHARE : (c + 1) * SHARE, :]
+            move(wide_qkv.at[at], qkv_hbm.at[rows, :])
+            move(wide_two.at[at, :SHARE, :], out_hbm.at[rows, :])
+            for j in range(SHARE // 8):
+                wide_proj[at, 8 * j : 8 * j + 8, :] = wide[
+                    4 * SHARE : 4 * SHARE + 8, j * PROJ : (j + 1) * PROJ
+                ]
+            move(wide_proj.at[at], proj_hbm.at[rows, :])
+            at += 1
     if last:
-        sources = ((refs[2], core, 0), (refs[3], core, 1), (refs[4], 1 - core, 0), (two_ref, 1 - core, 1))
-        for ref, at, one_group in sources:
-            for p, distance in enumerate(GROUPS[one_group]):
-                block = at * RING + block_at(at, place, distance)
+        sources = refs[2 * len(jobs) : 2 * len(jobs) + 2 * len(GROUPS)]
+        for k, ref in enumerate(sources):
+            owner = core if k < len(GROUPS) else 1 - core
+            for p, distance in enumerate(GROUPS[k % len(GROUPS)]):
+                block = owner * RING + block_at(owner, place, distance)
                 line = ref[p, 4 * SHARE : 4 * SHARE + 16, :].astype(F32)[8:, :]
                 small_ref[pl.ds(pl.multiple_of(block * 8, 8), 8), :] = line
-        rows = [small_ref[8 * k : 8 * k + 1, :] for k in range(13)]
-        bqkv_ref, bout_ref, g1_ref, s1_ref, bup_ref, bdown_ref, g2_ref, s2_ref = outs[5:]
+        rows = [small_ref[8 * k : 8 * k + 1, :] for k in range(14)]
+        bqkv_ref, bout_ref, g1_ref, s1_ref, bup_ref, bdown_ref, g2_ref, s2_ref = outs[5:13]
+        for k, ref in enumerate(outs[13:]):
+            ref[0] = value_of(rows[13][:, k * 128 : (k + 1) * 128])
         for c in range(3):
             bqkv_ref[:, c * D : (c + 1) * D] = rows[c]
         bout_ref[...] = rows[3]
@@ -755,26 +799,31 @@
         copy.wait()
 
 
-def spread_call(mine, group, where, one, two, outs, others):
+def spread_call(jobs, where, halves, outs, others):
     last = len(others) > 0
     shapes = ((FF, D), (D, FF), (D, 3 * D), (D, D), (D, PROJ))
     widths = (3 * D, D, D, D, FF, D, D, D) if last else ()
-    args = [where, one, two, *others, *outs]
-    half = len(GROUPS[group])
+    args = [where, *halves, *others, *outs]
+    count = sum(len(GROUPS[group]) for _, group in jobs)
+    before = 1 + len(halves) + len(others)
     return call(
-        partial(spread, mine, group, last),
+        partial(spread, jobs, last),
         args,
-        [SMEM] + [VMEM] * (2 + len(others)) + [HBM] * len(outs),
-        [pltpu.HBM(shape, F32) for shape in shapes] + [shape_of((1, width)) for width in widths],
+        [SMEM] + [VMEM] * (before - 1) + [HBM] * len(outs),
+        [pltpu.HBM(shape, F32) for shape in shapes]
+        + [shape_of((1, width)) for width in widths]
+        + [shape_of((1,))] * (2 * last),
         [
-            pltpu.VMEM((half, FIRST, D), F32),
-            pltpu.VMEM((half, 4 * SHARE + TAIL, D), F32),
-            pltpu.VMEM((half, SHARE, PROJ), F32),
+            pltpu.VMEM((count, FIRST, D), F32),
+            pltpu.VMEM((count, SHARE + TAIL, D), F32),
+            pltpu.VMEM((count, SHARE, 3 * D), F32),
+            pltpu.VMEM((count, SHARE, PROJ), F32),
             pltpu.VMEM((16 * RING, D), F32),
-            pltpu.SemaphoreType.DMA((8 * half,)),
+            pltpu.SemaphoreType.DMA((6 * count,)),
         ],
-        out_specs=[HBM] * 5 + [VMEM] * len(widths),
-        aliases={3 + len(others) + k: k for k in range(len(outs))},
+        out_specs=[HBM] * 5 + [VMEM] * len(widths) + [SMEM] * (2 * last),
+        aliases={before + k: k for k in range(len(outs))},
+        cost=SPREAD_COST,
         room=14,
     )
 
@@ -798,7 +847,7 @@
         input_output_aliases=aliases,
         compiler_params=pltpu.CompilerParams(vmem_limit_bytes=room * MIB),
         cost_estimate=pl.CostEstimate(
-            flops=10**8, bytes_accessed=cost, transcendentals=0
+            flops=10 * cost, bytes_accessed=cost, transcendentals=0
         ),
     )(*args)
 
@@ -821,7 +870,7 @@
             pltpu.VMEM((RING, SHARE, PROJ), F32),
             pltpu.SemaphoreType.DMA((7 * RING,)),
         ],
-        out_specs=[HBM] * 5 + [VMEM] * len(widths),
+        out_specs=[HBM] * 5 + [VMEM] * len(widths) + [SMEM] * (2 * last),
         aliases={} if mine else {5 + k: k for k in range(5)},
         room=14,
     )
@@ -861,11 +910,16 @@
         refs[-count + k][...] = value
 
 
+def first_blocks(places, keep_ref, pair_ref, *outs):
+    for ref, k in zip(outs, places):
+        ref[0] = (keep_ref[k].astype(F32) + pair_ref[k].astype(F32)).astype(BF16)
+
+
 class Summed:
     def __init__(self, keep, send, others):
         self.keep, self.others, self.hop = keep, others, 0
         self.pair = swapped(send, 1)
-        self.got, self.blocks, self.near, self.far = [], {}, [], []
+        self.sent, self.blocks, self.near, self.far = [], {}, [], []
 
     def blocks_call(self, blocks, places, held):
         return call(
@@ -880,9 +934,16 @@
     def open(self, after):
         keep, pair, _ = lax.optimization_barrier((self.keep, self.pair, after))
         half = RING // 2
-        first = added(keep[half : half + 1], pair[half : half + 1])
-        second = added(keep[half - 1 : half], pair[half - 1 : half])
-        self.got = [ring_swap(first, True), ring_swap(second, False)]
+        shape = (1, *keep.shape[1:])
+        first, second = call(
+            partial(first_blocks, (half, half - 1)),
+            (keep, pair),
+            [VMEM] * 2,
+            [shape_of(shape, BF16)] * 2,
+            room=8,
+            cost=STEP_COST,
+        )
+        self.sent = [(first, True), (second, False)]
         return second
 
     def total(self, after):
@@ -894,7 +955,7 @@
         half = RING // 2
         self.hop += 1
         hop = self.hop
-        *got, _ = lax.optimization_barrier((*self.got, after))
+        *got, _ = lax.optimization_barrier((*[ring_swap(*one) for one in self.sent], after))
         if hop < half:
             out = self.blocks_call(got, (half + hop, half - 1 - hop), [self.keep])
             self.part = out[1]
@@ -911,16 +972,16 @@
             if hop < half:
                 self.blocks[RING - hop] = out[1]
         if hop == half - 1:
-            self.got = [ring_swap(out[0], True)]
+            self.sent = [(out[0], True)]
         elif self.hop < 2 * half:
-            self.got = [ring_swap(out[0], True), ring_swap(out[1], False)]
+            self.sent = [(out[0], True), (out[1], False)]
         return out[0]
 
     def share(self, group, after):
         *blocks, _ = lax.optimization_barrier((*[self.blocks[k] for k in GROUPS[group]], after))
         shape = (len(blocks), *blocks[0].shape[1:])
         self.near += call(
-            join_blocks, blocks, [VMEM] * len(blocks), [shape_of(shape, BF16)], room=8, cost=STEP_COST
+            join_blocks, blocks, [VMEM] * len(blocks), [shape_of(shape, BF16)], room=8, cost=0
         )
         self.far.append(swapped(self.near[-1], 1))
         return self.near[-1]
@@ -975,11 +1036,12 @@
         out_specs=[VMEM] + [HBM] * len(KEPT),
     )
 
+    every, other_y = range(size), near_masks[1]
     other = swapped(vec, 1, "stream")
     near = jnp.where(is_query, vec, other)
     rows = jnp.where(is_query, other, vec)[:ROW]
     moved = swapped(rows, top_mask)
-    near = jnp.concatenate([near, swapped(near, near_masks[1])], axis=0)
+    near = jnp.concatenate([near, swapped(near, other_y)], axis=0)
     rows = jnp.where(has_top == is_query, moved, rows)
     far = swapped(near, near_masks[0])
     pieces = []
@@ -1009,67 +1071,83 @@
         [pltpu.VMEM((PROJ, tokens_d), F32), pltpu.VMEM((3, PROJ, tokens_d), BF16)],
         room=room,
     )
+    small_enough = doc_rows <= 4
+    ready = call(
+        matching_ready,
+        (near, far, *pieces),
+        [VMEM] * (2 + len(pieces)),
+        [
+            shape_of((3, tokens_q, PROJ), BF16),
+            shape_of((3, PROJ, tokens_q), BF16),
+            shape_of((tokens_q, 128)),
+            shape_of((3, PROJ, tokens_d), BF16),
+            shape_of((8, tokens_d)),
+        ]
+        + [shape_of((3, tokens_q, tokens_d), BF16)] * small_enough,
+        [pltpu.VMEM((PROJ, tokens_d), F32)],
+        room=room,
+    )
     stats = stats + swapped(stats, near_masks[0])
-    stats = stats + swapped(stats, near_masks[1])
-    stats = stats + swapped(stats, 1, "stream")
-    dq, send, keep, loss = call(
+    over_y = swapped(stats, other_y)
+    over_x = swapped(stats, 1, "stream")
+    pairs = [(k * size + r, (1 - k) * size + (r ^ other_y)) for k in range(2) for r in every]
+    over_both = lax.ppermute(stats, ("stream", "dp"), pairs)
+    dq, dq_send, keep, send, loss = call(
         partial(matching_back, doc_masks, lanes, total_queries),
-        (where, scale, doc_lengths, near, far, totals, el, hot, stats, *pieces),
-        [SMEM] * 3 + [VMEM] * (6 + len(pieces)),
+        (where, scale, doc_lengths, totals, el, hot, stats, over_y, over_x, over_both, *ready),
+        [SMEM] * 3 + [VMEM] * (7 + len(ready)),
+        [shape_of((tokens_q // 2, PROJ), BF16)] * 2
+        + [shape_of((tokens_d // 2, PROJ), BF16)] * 2
+        + [shape_of((8, 128))],
         [
-            shape_of((tokens_q, PROJ), BF16), shape_of((tokens_d // 2 + EXT, PROJ), BF16),
-            shape_of((tokens_d // 2, PROJ), BF16), shape_of((8, 128)),
-        ],
-        [
-            pltpu.VMEM((PROJ, tokens_d), F32),
-            pltpu.VMEM((3, PROJ, tokens_d), BF16),
-            pltpu.VMEM((3, PROJ, tokens_q), BF16),
             pltpu.VMEM((tokens_q, PROJ), F32),
             pltpu.VMEM((3, PROJ, tokens_d), F32),
+            pltpu.VMEM((tokens_q // QLEN, 128), F32),
         ],
         room=room,
     )
-    for mask in reversed(doc_masks):
-        got, rows = swapped(send, mask), keep.shape[0]
-        outs = [shape_of((rows // 2 + EXT, PROJ), BF16), shape_of((rows // 2, PROJ), BF16)]
-        if rows == ROW:
-            outs = [shape_of((ROW + EXT, PROJ), BF16)]
-        send, *keep, loss = call(
-            fold_docs, (keep, got, loss), [VMEM] * 3, outs + [shape_of((8, 128))], room=8
-        )
-        keep = keep[0] if keep else None
-    for mask in near_masks:
-        half = dq.shape[0] // 2
-        dq = added(dq[:half], swapped(dq[half:], mask))
-    dd, send, loss = call(
-        last_docs,
-        (where, send, swapped(send, top_mask), loss, dq),
-        [SMEM] + [VMEM] * 4,
-        [shape_of((ROW, PROJ), BF16), shape_of((ROW, PROJ), BF16), shape_of((8, 128))],
+    got_dq = swapped(dq_send, near_masks[0])
+    for mask in reversed(doc_masks[1:]):
+        total, half = added(keep, swapped(send, mask)), keep.shape[0] // 2
+        keep, send = total[:half], total[half:]
+    got_dd = swapped(send, doc_masks[0])
+    dq, dd = call(
+        two_sums,
+        (dq, got_dq, keep, got_dd),
+        [VMEM] * 4,
+        [shape_of((2 * ROW, PROJ), BF16), shape_of((ROW, PROJ), BF16)],
         room=8,
     )
-    got = swapped(send, 1, "stream")
+    dq = added(dq[:ROW], swapped(dq[ROW:], other_y))
+    dd = added(dd, swapped(dd, top_mask))
+    got = swapped(jnp.where(is_query, dd, dq), 1, "stream")
 
     one_keep, one_send, tail_keep, tail_send, d_first, gproj, small = call(
         feed_back,
         (
-            where, dq, dd, got, xh2, rs2, affine, proj_weight[0], down_weight[0], slope, act,
-            up_weight[0], xh1,
+            where, dq, dd, got, xh2, rs2, affine, proj_weight[0], up_weight[0], xh1,
+            down_weight[0], slope, act,
         ),
-        [SMEM] + [VMEM] * 3 + [HELD] * 9,
+        [SMEM] + [VMEM] * 3 + [HELD] * 6 + [HBM] * 3,
         [shape_of((RING, FIRST, D), BF16)] * 2
         + [shape_of((RING, TAIL, D), BF16)] * 2
         + [shape_of((ROW, D)), shape_of((D, PROJ)), shape_of((8, D))],
-        [pltpu.VMEM((ROW, FF), BF16)],
+        [
+            pltpu.VMEM((ROW, FF), BF16),
+            pltpu.VMEM((FF, D), BF16),
+            pltpu.VMEM((ROW, FF), BF16),
+            pltpu.VMEM((ROW, FF), BF16),
+            pltpu.SemaphoreType.DMA((12,)),
+        ],
         room=24,
     )
     two_keep, two_send, tokens_grad = call(
         attend_back,
         (
-            where, d_first, gproj, small, tail_keep, tail_send, xh1, rs1, affine, mixed, out_weight[0], qkv, probs, rope,
+            where, d_first, gproj, small, loss, tail_keep, tail_send, xh1, rs1, affine, mixed, out_weight[0], qkv, probs, rope,
             tokens[0], qkv_weight[0],
         ),
-        [SMEM] + [VMEM] * 5 + [HELD] * 10,
+        [SMEM] + [VMEM] * 6 + [HELD] * 10,
         [shape_of((RING, SECOND, D), BF16)] * 2 + [shape_of((ROW, D))],
         [
             pltpu.VMEM((ROW, 3 * D), BF16),
@@ -1082,26 +1160,26 @@
     ]
     token, outs = tokens_grad, ()
     for event in ORDER:
-        kind, k = event
-        if kind in ("near", "far"):
-            mine = kind == "near"
-            halves = [piece.near[k] if mine else piece.far[k] for piece in (one, two)]
+        kind, k, *group = event
+        if kind == "spread":
+            jobs = event[1]
+            halves = [
+                (piece.near if mine else piece.far)[group] for mine, group in jobs for piece in (one, two)
+            ]
             *halves, _ = lax.optimization_barrier((*halves, token))
-            rest = [*two.near, two.far[0]] if (kind, k) == ("far", 1) else []
-            outs = spread_call(mine, k, where, *halves, outs[:5], rest)
+            others = [*two.near, *two.far] if event == ORDER[-1] else []
+            outs = spread_call(jobs, where, halves, outs[:5], others)
             token = outs[0]
             continue
         piece = (one, two)[k]
-        if kind in ("share0", "share1"):
-            token = piece.share(int(kind[-1]), token)
-        else:
-            token = getattr(piece, kind)(token)
+        token = getattr(piece, kind)(*group, token)
     grad_down, grad_up, grad_qkv, grad_out, grad_proj = outs[:5]
     (
-        grad_bqkv, grad_bout, grad_g1, grad_s1, grad_bup, grad_bdown, grad_g2, grad_s2,
+        grad_bqkv, grad_bout, grad_g1, grad_s1, grad_bup, grad_bdown, grad_g2, grad_s2, loss,
+        scale_grad,
     ) = outs[5:]
     return (
-        loss[0, 0],
+        loss.reshape(()),
         tokens_grad[None],
         grad_qkv[None],
         grad_bqkv,
@@ -1116,7 +1194,7 @@
         grad_g2,
         grad_s2,
         grad_proj[None],
-        loss[1, 0],
+        scale_grad.reshape(()),
     )
 
 

time: 160 us -> 152 us (0.950)
  local copies, waits for them, and re-layouts: 6.14 us -> 1.58 us
  waiting for transfers between devices: 58.5 us -> 54.6 us
  starting transfers between devices: 51.6 us -> 53.4 us
    ppermute x19, waiting for transfers between devices: 25 us -> 19.1 us  [swapped(): return lax.ppermute(value, axis, [(k, k ^ mask) for k in range(size)])]
    unnamed x37 -> x31, local copies, waits for them, and re-layouts: 5.52 us -> 1.49 us
    ppermute x28, waiting for transfers between devices: 33.5 us -> 35.5 us  [ring_swap(): return lax.ppermute(value, 'dp', pairs)]
    ppermute x19, starting transfers between devices: 19.8 us -> 21.8 us  [swapped(): return lax.ppermute(value, axis, [(k, k ^ mask) for k in range(size)])]
    pallas_call x31 -> x32, Pallas kernels: 40 us -> 39.6 us  [call(): pl.pallas_call(kernel, out_shape=outs, in_specs=specs, out_specs=out_spec...]
  transfers between devices with their start and end apart: 47 -> 48, of which waited for: 31 -> 35; matrix products, arithmetic and copies ran while one was open for 1% -> 1% of each run, Pallas kernels for 9% -> 10%
where the time goes in v5:
time: 152 us
  waiting for transfers between devices  54.6 us (36%)
  starting transfers between devices  53.4 us (35%)
  Pallas kernels  39.6 us (26%)
  between operations  2 us (1%)
  local copies, waits for them, and re-layouts  1.58 us (1%)
    pallas_call x32, Pallas kernels, call(): pl.pallas_call(kernel, out_shape=outs, in_specs=specs, out_specs=out_spec...  39.6 us
    ppermute x28, waiting for transfers between devices, ring_swap(): return lax.ppermute(value, 'dp', pairs)  35.5 us
    ppermute x28, starting transfers between devices, ring_swap(): return lax.ppermute(value, 'dp', pairs)  30.2 us
    ppermute x19, starting transfers between devices, swapped(): return lax.ppermute(value, axis, [(k, k ^ mask) for k in range(size)])  21.8 us
    ppermute x19, waiting for transfers between devices, swapped(): return lax.ppermute(value, axis, [(k, k ^ mask) for k in range(size)])  19.1 us
  transfers between devices with their start and end apart: 48, of which 35 were waited for; matrix products, arithmetic and copies ran while one was open for 1% of the time, Pallas kernels for 10%

profile of v5, /device:TPU:0, one launch (start us, length us, event | category | flops | bytes accessed | tf_op | source)
XLA Modules:
  0.0 152.2 jit_solution(16149601110690413007)
XLA Ops:
  2.2 8.9 %shard_map.297 = (bf16[272,128]{1,0:T(8,128)(2,1)S(1)}, bf16[256,1536]{1,0:T(8,128)(2,1)}, f32[256,256]{1,0:T(8,128)}, bf16[8,256,256]{2,1,0:T(8,128)(2,1)}, bf1...) custom-call(s32[8]{0:T(128)S(1)} %stack.36.where_ref, ...), custom_call_target="tpu_custom_call" | custom-call | flops 100000000 | bytes 10000000 | tf_op jit(solution)/shard_map/pallas_call | solution.py:841
  11.1 3.0 %collective-permute-start = (bf16[272,128]{1,0:T(8,128)(2,1)S(1)}, bf16[272,128]{1,0:T(8,128)(2,1)S(1)}, u32[]{:S(2)}, u32[]{:S(2)}) collective-permute-start(bf16[272,128]{1,0:T(8,128)(2,1)S(1)} %get-tuple-element.166), channel_id=1, source_target_pairs={{0,16},{16,0},{1,17},{17,1},{2,18},{18,2},{3,19},{19,3},{4,20},{20... | collective-permute-start | bytes 208904 | tf_op jit(solution)/shard_map/ppermute | solution.py:881
  14.1 2.3 %collective-permute-done = bf16[272,128]{1,0:T(8,128)(2,1)S(1)} collective-permute-done((bf16[272,128]{1,0:T(8,128)(2,1)S(1)}, bf16[272,128]{1,0:T(8,128)(2,1)S(1)}, u32[]{:S(2)}, u32[]{:S(2)}) %collective-permute-start) | collective-permute-done | bytes 69664 | tf_op jit(solution)/shard_map/ppermute | solution.py:881
  16.4 2.1 %collective-permute-start.1 = (bf16[272,128]{1,0:T(8,128)(2,1)S(1)}, bf16[272,128]{1,0:T(8,128)(2,1)S(1)}, u32[]{:S(2)}, u32[]{:S(2)}) collective-permute-start(bf16[272,128]{1,0:T(8,128)(2,1)S(1)} %broadcast_select_fusion), channel_id=1, source_target_pairs={{0,2},{1,3},{2,0},{3,1},{4,6},{5,7},{6,4},{7,5},{8,10},{9,11},{10,... | collective-permute-start | bytes 208904 | tf_op jit(solution)/shard_map/ppermute | solution.py:881
  18.5 2.7 %collective-permute-start.3 = (bf16[256,128]{1,0:T(8,128)(2,1)S(1)}, bf16[256,128]{1,0:T(8,128)(2,1)S(1)}, u32[]{:S(2)}, u32[]{:S(2)}) collective-permute-start(bf16[256,128]{1,0:T(8,128)(2,1)S(1)} %slice_select_fusion), channel_id=1, source_target_pairs={{0,8},{1,9},{2,10},{3,11},{4,12},{5,13},{6,14},{7,15},{8,0},{9,1},... | collective-permute-start | bytes 196616 | tf_op jit(solution)/shard_map/ppermute | solution.py:881
  21.2 2.5 %collective-permute-done.3 = bf16[256,128]{1,0:T(8,128)(2,1)S(1)} collective-permute-done((bf16[256,128]{1,0:T(8,128)(2,1)S(1)}, bf16[256,128]{1,0:T(8,128)(2,1)S(1)}, u32[]{:S(2)}, u32[]{:S(2)}) %collective-permute-start.3) | collective-permute-done | bytes 65568 | tf_op jit(solution)/shard_map/ppermute | solution.py:881
  23.7 1.6 %collective-permute-start.4 = (bf16[256,128]{1,0:T(8,128)(2,1)S(1)}, bf16[256,128]{1,0:T(8,128)(2,1)S(1)}, u32[]{:S(2)}, u32[]{:S(2)}) collective-permute-start(bf16[256,128]{1,0:T(8,128)(2,1)S(1)} %broadcast_select_fusion.2.refs_0_), channel_id=1, source_target_pairs={{0,4},{1,5},{2,6},{3,7},{4,0},{5,1},{6,2},{7,3},{8,12},{9,13},{10,... | collective-permute-start | bytes 196616 | tf_op jit(solution)/shard_map/ppermute | solution.py:881
  26.0 2.0 %collective-permute-done.4.refs_1_ = bf16[256,128]{1,0:T(8,128)(2,1)S(1)} collective-permute-done((bf16[256,128]{1,0:T(8,128)(2,1)S(1)}, bf16[256,128]{1,0:T(8,128)(2,1)S(1)}, u32[]{:S(2)}, u32[]{:S(2)}) %collective-permute-start.4) | collective-permute-done | bytes 65568 | tf_op jit(solution)/shard_map/ppermute | solution.py:881
  28.1 2.9 %shard_map.298 = (f32[1024,128]{1,0:T(8,128)S(1)}, f32[32,128]{1,0:T(8,128)S(1)}, f32[32,128]{1,0:T(8,128)S(1)}, f32[32,128]{1,0:T(8,128)S(1)}) custom-call(s32[8]{0:T(128)S(1)} %stack.36.where_ref, f32[1]{0:T(128)} %bitcast.22.scale_ref, s32[16,5]{1,0:T(8,128)S(1)} %copy.46.lens_ref, bf16[544,128]{1,0:T(8,128)(2,1)S(1)} %pad_maximum_fusion.near_ref, ...), custom_call_target="tpu_custom_call" | custom-call | flops 100000000 | bytes 10000000 | tf_op jit(solution)/shard_map/pallas_call | solution.py:841
  33.8 1.9 %collective-permute-start.6 = (f32[32,128]{1,0:T(8,128)S(1)}, f32[32,128]{1,0:T(8,128)S(1)}, u32[]{:S(2)}, u32[]{:S(2)}) collective-permute-start(f32[32,128]{1,0:T(8,128)S(1)} %add.24.own_ref), channel_id=1, source_target_pairs={{0,2},{1,3},{2,0},{3,1},{4,6},{5,7},{6,4},{7,5},{8,10},{9,11},{10,... | collective-permute-start | bytes 49160 | tf_op jit(solution)/shard_map/ppermute | solution.py:881
  35.7 1.5 shard_map.299
  37.6 3.9 %shard_map.300 = (bf16[512,128]{1,0:T(8,128)(2,1)S(1)}, bf16[512,128]{1,0:T(8,128)(2,1)S(1)}, bf16[256,128]{1,0:T(8,128)(2,1)S(1)}, bf16[256,128]{1,0:T(8,128)(2,1)S(1)}, f32[8,128]{1,0:T(8,128)S(1)}) custom-call(s32[8]{0:T(128)S(1)} %stack.36.where_ref, f32[1]{0:T(128)} %bitcast.23.scale_ref, s32[16,5]{1,0:T(8,128)S(1)} %copy.46.lens_ref, ...), custom_call_target="tpu_custom_call" | custom-call | flops 100000000 | bytes 10000000 | tf_op jit(solution)/shard_map/pallas_call | solution.py:841
  41.6 2.0 %collective-permute-start.10 = (bf16[256,128]{1,0:T(8,128)(2,1)S(1)}, bf16[256,128]{1,0:T(8,128)(2,1)S(1)}, u32[]{:S(2)}, u32[]{:S(2)}) collective-permute-start(bf16[256,128]{1,0:T(8,128)(2,1)S(1)} %get-tuple-element.180), channel_id=1, source_target_pairs={{0,4},{1,5},{2,6},{3,7},{4,0},{5,1},{6,2},{7,3},{8,12},{9,13},{10,... | collective-permute-start | bytes 196616 | tf_op jit(solution)/shard_map/ppermute | solution.py:881
  43.5 2.7 %collective-permute-done.10.got_dd_ref = bf16[256,128]{1,0:T(8,128)(2,1)S(1)} collective-permute-done((bf16[256,128]{1,0:T(8,128)(2,1)S(1)}, bf16[256,128]{1,0:T(8,128)(2,1)S(1)}, u32[]{:S(2)}, u32[]{:S(2)}) %collective-permute-start.10) | collective-permute-done | bytes 65568 | tf_op jit(solution)/shard_map/ppermute | solution.py:881
  46.3 1.8 %collective-permute-start.11 = (bf16[256,128]{1,0:T(8,128)(2,1)S(1)}, bf16[256,128]{1,0:T(8,128)(2,1)S(1)}, u32[]{:S(2)}, u32[]{:S(2)}) collective-permute-start(bf16[256,128]{1,0:T(8,128)(2,1)S(1)} %slice.11), channel_id=1, source_target_pairs={{0,2},{1,3},{2,0},{3,1},{4,6},{5,7},{6,4},{7,5},{8,10},{9,11},{10,... | collective-permute-start | bytes 196616 | tf_op jit(solution)/shard_map/ppermute | solution.py:881
  48.1 3.0 %collective-permute-start.12 = (bf16[256,128]{1,0:T(8,128)(2,1)S(1)}, bf16[256,128]{1,0:T(8,128)(2,1)S(1)}, u32[]{:S(2)}, u32[]{:S(2)}) collective-permute-start(bf16[256,128]{1,0:T(8,128)(2,1)S(1)} %get-tuple-element.182), channel_id=1, source_target_pairs={{0,8},{1,9},{2,10},{3,11},{4,12},{5,13},{6,14},{7,15},{8,0},{9,1},... | collective-permute-start | bytes 196616 | tf_op jit(solution)/shard_map/ppermute | solution.py:881
  51.1 2.8 %collective-permute-done.12 = bf16[256,128]{1,0:T(8,128)(2,1)S(1)} collective-permute-done((bf16[256,128]{1,0:T(8,128)(2,1)S(1)}, bf16[256,128]{1,0:T(8,128)(2,1)S(1)}, u32[]{:S(2)}, u32[]{:S(2)}) %collective-permute-start.12) | collective-permute-done | bytes 65568 | tf_op jit(solution)/shard_map/ppermute | solution.py:881
  53.9 1.5 %collective-permute-start.13 = (bf16[256,128]{1,0:T(8,128)(2,1)S(1)}, bf16[256,128]{1,0:T(8,128)(2,1)S(1)}, u32[]{:S(2)}, u32[]{:S(2)}) collective-permute-start(bf16[256,128]{1,0:T(8,128)(2,1)S(1)} %get-tuple-element.316), channel_id=1, source_target_pairs={{0,16},{16,0},{1,17},{17,1},{2,18},{18,2},{3,19},{19,3},{4,20},{20... | collective-permute-start | bytes 196616 | tf_op jit(solution)/shard_map/ppermute | solution.py:881
  55.5 2.8 %collective-permute-done.13.got_ref = bf16[256,128]{1,0:T(8,128)(2,1)S(1)} collective-permute-done((bf16[256,128]{1,0:T(8,128)(2,1)S(1)}, bf16[256,128]{1,0:T(8,128)(2,1)S(1)}, u32[]{:S(2)}, u32[]{:S(2)}) %collective-permute-start.13) | collective-permute-done | bytes 65568 | tf_op jit(solution)/shard_map/ppermute | solution.py:881
  58.4 6.7 %shard_map.302 = (bf16[8,208,512]{2,1,0:T(8,128)(2,1)S(1)}, bf16[8,208,512]{2,1,0:T(8,128)(2,1)S(1)}, bf16[8,48,512]{2,1,0:T(8,128)(2,1)S(1)}, bf16[8,48,512]{2,...) custom-call(s32[8]{0:T(128)S(1)} %stack.36.where_ref, ...), custom_call_target="tpu_custom_call" | custom-call | flops 100000000 | bytes 10000000 | tf_op jit(solution)/shard_map/pallas_call | solution.py:841
  65.3 5.3 %shard_map.303 = (bf16[8,192,512]{2,1,0:T(8,128)(2,1)S(1)}, bf16[8,192,512]{2,1,0:T(8,128)(2,1)S(1)}, f32[256,512]{1,0:T(8,128)}) custom-call(s32[8]{0:T(128)S(1)} %stack.36.where_ref, f32[256,512]{1,0:T(8,128)S(1)} %get-tuple-element.191.dfirst_ref, f32[512,128]{1,0:T(8,128)S(1)} %get-tuple-element.192.gproj_ref, ...), custom_call_target="tpu_custom_call" | custom-call | flops 100000000 | bytes 10000000 | tf_op jit(solution)/shard_map/pallas_call | solution.py:841
  71.7 2.4 %collective-permute-done.17.pair_ref = bf16[8,192,512]{2,1,0:T(8,128)(2,1)S(1)} collective-permute-done((bf16[8,192,512]{2,1,0:T(8,128)(2,1)S(1)}, bf16[8,192,512]{2,1,0:T(8,128)(2,1)S(1)}, u32[]{:S(2)}, u32[]{:S(2)}) %collective-permute-start.17) | collective-permute-done | bytes 1572896 | tf_op jit(solution)/shard_map/ppermute | solution.py:881
  74.7 1.5 collective-permute-start.15
  78.6 3.0 %collective-permute-done.15.refs_0_ = bf16[1,208,512]{2,1,0:T(8,128)(2,1)S(1)} collective-permute-done((bf16[1,208,512]{2,1,0:T(8,128)(2,1)S(1)}, bf16[1,208,512]{2,1,0:T(8,128)(2,1)S(1)}, u32[]{:S(2)}, u32[]{:S(2)}) %collective-permute-start.15) | collective-permute-done | bytes 213024 | tf_op jit(solution)/shard_map/ppermute | solution.py:900
  82.2 1.5 collective-permute-start.18
  84.4 1.5 collective-permute-start.24
  85.9 3.2 %collective-permute-done.19.refs_1_ = bf16[1,208,512]{2,1,0:T(8,128)(2,1)S(1)} collective-permute-done((bf16[1,208,512]{2,1,0:T(8,128)(2,1)S(1)}, bf16[1,208,512]{2,1,0:T(8,128)(2,1)S(1)}, u32[]{:S(2)}, u32[]{:S(2)}) %collective-permute-start.19) | collective-permute-done | bytes 213024 | tf_op jit(solution)/shard_map/ppermute | solution.py:900
  90.4 1.7 %collective-permute-start.23 = (bf16[1,208,512]{2,1,0:T(8,128)(2,1)S(1)}, bf16[1,208,512]{2,1,0:T(8,128)(2,1)S(1)}, u32[]{:S(2)}, u32[]{:S(2)}) collective-permute-start(bf16[1,208,512]{2,1,0:T(8,128)(2,1)S(1)} %get-tuple-element.225), channel_id=1, source_target_pairs={{0,2},{1,5},{2,6},{3,1},{4,0},{5,9},{6,10},{7,3},{8,4},{9,13},{10,... | collective-permute-start | bytes 638984 | tf_op jit(solution)/shard_map/ppermute | solution.py:900
  94.5 1.7 %collective-permute-start.27 = (bf16[1,192,512]{2,1,0:T(8,128)(2,1)S(1)}, bf16[1,192,512]{2,1,0:T(8,128)(2,1)S(1)}, u32[]{:S(2)}, u32[]{:S(2)}) collective-permute-start(bf16[1,192,512]{2,1,0:T(8,128)(2,1)S(1)} %get-tuple-element.229), channel_id=1, source_target_pairs={{0,4},{1,3},{2,0},{3,7},{4,8},{5,1},{6,2},{7,11},{8,12},{9,5},{10,... | collective-permute-start | bytes 589832 | tf_op jit(solution)/shard_map/ppermute | solution.py:900
  96.2 1.5 collective-permute-done.23.refs_1_
  97.7 2.1 %collective-permute-done.22.refs_0_ = bf16[1,208,512]{2,1,0:T(8,128)(2,1)S(1)} collective-permute-done((bf16[1,208,512]{2,1,0:T(8,128)(2,1)S(1)}, bf16[1,208,512]{2,1,0:T(8,128)(2,1)S(1)}, u32[]{:S(2)}, u32[]{:S(2)}) %collective-permute-start.22) | collective-permute-done | bytes 213024 | tf_op jit(solution)/shard_map/ppermute | solution.py:900
  102.6 1.5 collective-permute-start.31
  104.2 1.6 %collective-permute-done.26.refs_0_ = bf16[1,208,512]{2,1,0:T(8,128)(2,1)S(1)} collective-permute-done((bf16[1,208,512]{2,1,0:T(8,128)(2,1)S(1)}, bf16[1,208,512]{2,1,0:T(8,128)(2,1)S(1)}, u32[]{:S(2)}, u32[]{:S(2)}) %collective-permute-start.26) | collective-permute-done | bytes 213024 | tf_op jit(solution)/shard_map/ppermute | solution.py:900
  105.8 1.7 %collective-permute-start.30 = (bf16[1,208,512]{2,1,0:T(8,128)(2,1)S(1)}, bf16[1,208,512]{2,1,0:T(8,128)(2,1)S(1)}, u32[]{:S(2)}, u32[]{:S(2)}) collective-permute-start(bf16[1,208,512]{2,1,0:T(8,128)(2,1)S(1)} %shard_map.312.refs_0_), channel_id=1, source_target_pairs={{0,2},{1,5},{2,6},{3,1},{4,0},{5,9},{6,10},{7,3},{8,4},{9,13},{10,... | collective-permute-start | bytes 638984 | tf_op jit(solution)/shard_map/ppermute | solution.py:900
  108.8 2.5 %collective-permute-start.35 = (bf16[1,192,512]{2,1,0:T(8,128)(2,1)S(1)}, bf16[1,192,512]{2,1,0:T(8,128)(2,1)S(1)}, u32[]{:S(2)}, u32[]{:S(2)}) collective-permute-start(bf16[1,192,512]{2,1,0:T(8,128)(2,1)S(1)} %shard_map.313.refs_0_), channel_id=1, source_target_pairs={{0,2},{1,5},{2,6},{3,1},{4,0},{5,9},{6,10},{7,3},{8,4},{9,13},{10,... | collective-permute-start | bytes 589832 | tf_op jit(solution)/shard_map/ppermute | solution.py:900
  111.3 2.7 %collective-permute-done.30.refs_1_ = bf16[1,208,512]{2,1,0:T(8,128)(2,1)S(1)} collective-permute-done((bf16[1,208,512]{2,1,0:T(8,128)(2,1)S(1)}, bf16[1,208,512]{2,1,0:T(8,128)(2,1)S(1)}, u32[]{:S(2)}, u32[]{:S(2)}) %collective-permute-start.30) | collective-permute-done | bytes 213024 | tf_op jit(solution)/shard_map/ppermute | solution.py:900
  115.1 2.1 %collective-permute-start.33 = (bf16[1,208,512]{2,1,0:T(8,128)(2,1)S(1)}, bf16[1,208,512]{2,1,0:T(8,128)(2,1)S(1)}, u32[]{:S(2)}, u32[]{:S(2)}) collective-permute-start(bf16[1,208,512]{2,1,0:T(8,128)(2,1)S(1)} %get-tuple-element.270.refs_6_), channel_id=1, source_target_pairs={{0,2},{1,5},{2,6},{3,1},{4,0},{5,9},{6,10},{7,3},{8,4},{9,13},{10,... | collective-permute-start | bytes 638984 | tf_op jit(solution)/shard_map/ppermute | solution.py:900
  118.4 3.2 %collective-permute-start.39 = (bf16[1,192,512]{2,1,0:T(8,128)(2,1)S(1)}, bf16[1,192,512]{2,1,0:T(8,128)(2,1)S(1)}, u32[]{:S(2)}, u32[]{:S(2)}) collective-permute-start(bf16[1,192,512]{2,1,0:T(8,128)(2,1)S(1)} %get-tuple-element.278.refs_6_), channel_id=1, source_target_pairs={{0,2},{1,5},{2,6},{3,1},{4,0},{5,9},{6,10},{7,3},{8,4},{9,13},{10,... | collective-permute-start | bytes 589832 | tf_op jit(solution)/shard_map/ppermute | solution.py:900
  121.6 1.7 %collective-permute-done.33.refs_1_ = bf16[1,208,512]{2,1,0:T(8,128)(2,1)S(1)} collective-permute-done((bf16[1,208,512]{2,1,0:T(8,128)(2,1)S(1)}, bf16[1,208,512]{2,1,0:T(8,128)(2,1)S(1)}, u32[]{:S(2)}, u32[]{:S(2)}) %collective-permute-start.33) | collective-permute-done | bytes 213024 | tf_op jit(solution)/shard_map/ppermute | solution.py:900
  123.3 1.8 %collective-permute-done.32.refs_0_ = bf16[1,208,512]{2,1,0:T(8,128)(2,1)S(1)} collective-permute-done((bf16[1,208,512]{2,1,0:T(8,128)(2,1)S(1)}, bf16[1,208,512]{2,1,0:T(8,128)(2,1)S(1)}, u32[]{:S(2)}, u32[]{:S(2)}) %collective-permute-start.32) | collective-permute-done | bytes 213024 | tf_op jit(solution)/shard_map/ppermute | solution.py:900
  127.5 1.9 %collective-permute-done.38.refs_0_ = bf16[1,192,512]{2,1,0:T(8,128)(2,1)S(1)} collective-permute-done((bf16[1,192,512]{2,1,0:T(8,128)(2,1)S(1)}, bf16[1,192,512]{2,1,0:T(8,128)(2,1)S(1)}, u32[]{:S(2)}, u32[]{:S(2)}) %collective-permute-start.38) | collective-permute-done | bytes 196640 | tf_op jit(solution)/shard_map/ppermute | solution.py:900
  129.4 1.6 %collective-permute-start.42 = (bf16[1,192,512]{2,1,0:T(8,128)(2,1)S(1)}, bf16[1,192,512]{2,1,0:T(8,128)(2,1)S(1)}, u32[]{:S(2)}, u32[]{:S(2)}) collective-permute-start(bf16[1,192,512]{2,1,0:T(8,128)(2,1)S(1)} %get-tuple-element.277.refs_5_), channel_id=1, source_target_pairs={{0,2},{1,5},{2,6},{3,1},{4,0},{5,9},{6,10},{7,3},{8,4},{9,13},{10,... | collective-permute-start | bytes 589832 | tf_op jit(solution)/shard_map/ppermute | solution.py:900
  131.4 1.5 collective-permute-done.37.refs_1_
  133.6 1.9 %collective-permute-done.42.refs_1_ = bf16[1,192,512]{2,1,0:T(8,128)(2,1)S(1)} collective-permute-done((bf16[1,192,512]{2,1,0:T(8,128)(2,1)S(1)}, bf16[1,192,512]{2,1,0:T(8,128)(2,1)S(1)}, u32[]{:S(2)}, u32[]{:S(2)}) %collective-permute-start.42) | collective-permute-done | bytes 196640 | tf_op jit(solution)/shard_map/ppermute | solution.py:900
  139.0 3.3 %shard_map.322 = (f32[2048,512]{1,0:T(8,128)}, f32[512,2048]{1,0:T(8,128)}, f32[512,1536]{1,0:T(8,128)}, f32[512,512]{1,0:T(8,128)}, f32[512,128]{1,0:T(8,128)}) custom-call(s32[8]{0:T(128)S(1)} %stack.36.where_ref, bf16[7,208,512]{2,1,0:T(8,128)(2,1)S(1)} %shard_map.320.refs_0_, bf16[7,192,512]{2,1,0:T(8,128)(2,1)S(1)} %shard_map.321.refs_1_.refs_4_), custom_call_target="tpu_custom_call" | custom-call | tf_op jit(solution)/shard_map/pallas_call | solution.py:841
  143.4 2.1 %collective-permute-done.43.refs_0_ = bf16[1,192,512]{2,1,0:T(8,128)(2,1)S(1)} collective-permute-done((bf16[1,192,512]{2,1,0:T(8,128)(2,1)S(1)}, bf16[1,192,512]{2,1,0:T(8,128)(2,1)S(1)}, u32[]{:S(2)}, u32[]{:S(2)}) %collective-permute-start.43) | collective-permute-done | bytes 196640 | tf_op jit(solution)/shard_map/ppermute | solution.py:900
  146.2 3.3 %shard_map.327 = (f32[2048,512]{1,0:T(8,128)}, f32[512,2048]{1,0:T(8,128)}, f32[512,1536]{1,0:T(8,128)}, f32[512,512]{1,0:T(8,128)}, f32[512,128]{1,0:T(8,128)}) custom-call(s32[8]{0:T(128)S(1)} %stack.36.where_ref, ...), custom_call_target="tpu_custom_call", output_to_operand_aliasing={{0}: (3, {}), {1}: (4, {}), {2}: (5, {}), {3}: (6, {}), {4}... | custom-call | tf_op jit(solution)/shard_map/pallas_call | solution.py:841
  149.5 2.5 %shard_map.328 = (f32[2048,512]{1,0:T(8,128)}, f32[512,2048]{1,0:T(8,128)}, f32[512,1536]{1,0:T(8,128)}, f32[512,512]{1,0:T(8,128)}, f32[512,128]{1,0:T(8,128)},...) custom-call(s32[8]{0:T(128)S(1)} %stack.36.where_ref, ...), custom_call_target="tpu_custom_call", output_to_operand_aliasing={{0}: (9, {}), {1}: (10, {}), {2}: (11, {}), {3}: (12, {}), ... | custom-call | tf_op jit(solution)/shard_map/pallas_call | solution.py:841
  (121 shorter events, 29.7 us)
Async XLA Ops:
  11.1 5.3 %collective-permute-start = (bf16[272,128]{1,0:T(8,128)(2,1)S(1)}, bf16[272,128]{1,0:T(8,128)(2,1)S(1)}, u32[]{:S(2)}, u32[]{:S(2)}) collective-permute-start(bf16[272,128]{1,0:T(8,128)(2,1)S(1)} %get-tuple-element.166), channel_id=1, source_target_pairs={{0,16},{16,0},{1,17},{17,1},{2,18},{18,2},{3,19},{19,3},{4,20},{20... | collective-permute-start | bytes 208904 | tf_op jit(solution)/shard_map/ppermute | solution.py:881
  16.4 4.8 %collective-permute-start.1 = (bf16[272,128]{1,0:T(8,128)(2,1)S(1)}, bf16[272,128]{1,0:T(8,128)(2,1)S(1)}, u32[]{:S(2)}, u32[]{:S(2)}) collective-permute-start(bf16[272,128]{1,0:T(8,128)(2,1)S(1)} %broadcast_select_fusion), channel_id=1, source_target_pairs={{0,2},{1,3},{2,0},{3,1},{4,6},{5,7},{6,4},{7,5},{8,10},{9,11},{10,... | collective-permute-start | bytes 208904 | tf_op jit(solution)/shard_map/ppermute | solution.py:881
  18.5 5.2 %collective-permute-start.3 = (bf16[256,128]{1,0:T(8,128)(2,1)S(1)}, bf16[256,128]{1,0:T(8,128)(2,1)S(1)}, u32[]{:S(2)}, u32[]{:S(2)}) collective-permute-start(bf16[256,128]{1,0:T(8,128)(2,1)S(1)} %slice_select_fusion), channel_id=1, source_target_pairs={{0,8},{1,9},{2,10},{3,11},{4,12},{5,13},{6,14},{7,15},{8,0},{9,1},... | collective-permute-start | bytes 196616 | tf_op jit(solution)/shard_map/ppermute | solution.py:881
  21.2 6.9 %collective-permute-start.2 = (bf16[544,128]{1,0:T(8,128)(2,1)S(1)}, bf16[544,128]{1,0:T(8,128)(2,1)S(1)}, u32[]{:S(2)}, u32[]{:S(2)}) collective-permute-start(bf16[544,128]{1,0:T(8,128)(2,1)S(1)} %pad_maximum_fusion.near_ref), channel_id=1, source_target_pairs={{0,1},{1,0},{2,3},{3,2},{4,5},{5,4},{6,7},{7,6},{8,9},{9,8},{10,11... | collective-permute-start | bytes 417800 | tf_op jit(solution)/shard_map/ppermute | solution.py:881
  23.7 4.3 %collective-permute-start.4 = (bf16[256,128]{1,0:T(8,128)(2,1)S(1)}, bf16[256,128]{1,0:T(8,128)(2,1)S(1)}, u32[]{:S(2)}, u32[]{:S(2)}) collective-permute-start(bf16[256,128]{1,0:T(8,128)(2,1)S(1)} %broadcast_select_fusion.2.refs_0_), channel_id=1, source_target_pairs={{0,4},{1,5},{2,6},{3,7},{4,0},{5,1},{6,2},{7,3},{8,12},{9,13},{10,... | collective-permute-start | bytes 196616 | tf_op jit(solution)/shard_map/ppermute | solution.py:881
  30.9 1.2 collective-permute-start.5
  32.2 5.0 %collective-permute-start.8 = (f32[32,128]{1,0:T(8,128)S(1)}, f32[32,128]{1,0:T(8,128)S(1)}, u32[]{:S(2)}, u32[]{:S(2)}) collective-permute-start(f32[32,128]{1,0:T(8,128)S(1)} %add.24.own_ref), channel_id=1, source_target_pairs={{0,18},{1,19},{2,16},{3,17},{4,22},{5,23},{6,20},{7,21},{8,26},{9,... | collective-permute-start | bytes 49160 | tf_op jit(solution)/shard_map/ppermute | solution.py:1094
  33.6 3.7 %collective-permute-start.7 = (f32[32,128]{1,0:T(8,128)S(1)}, f32[32,128]{1,0:T(8,128)S(1)}, u32[]{:S(2)}, u32[]{:S(2)}) collective-permute-start(f32[32,128]{1,0:T(8,128)S(1)} %add.24.own_ref), channel_id=1, source_target_pairs={{0,16},{16,0},{1,17},{17,1},{2,18},{18,2},{3,19},{19,3},{4,20},{20... | collective-permute-start | bytes 49160 | tf_op jit(solution)/shard_map/ppermute | solution.py:881
  33.8 3.7 %collective-permute-start.6 = (f32[32,128]{1,0:T(8,128)S(1)}, f32[32,128]{1,0:T(8,128)S(1)}, u32[]{:S(2)}, u32[]{:S(2)}) collective-permute-start(f32[32,128]{1,0:T(8,128)S(1)} %add.24.own_ref), channel_id=1, source_target_pairs={{0,2},{1,3},{2,0},{3,1},{4,6},{5,7},{6,4},{7,5},{8,10},{9,11},{10,... | collective-permute-start | bytes 49160 | tf_op jit(solution)/shard_map/ppermute | solution.py:881
  41.5 4.7 %collective-permute-start.9 = (bf16[512,128]{1,0:T(8,128)(2,1)S(1)}, bf16[512,128]{1,0:T(8,128)(2,1)S(1)}, u32[]{:S(2)}, u32[]{:S(2)}) collective-permute-start(bf16[512,128]{1,0:T(8,128)(2,1)S(1)} %get-tuple-element.178), channel_id=1, source_target_pairs={{0,1},{1,0},{2,3},{3,2},{4,5},{5,4},{6,7},{7,6},{8,9},{9,8},{10,11... | collective-permute-start | bytes 393224 | tf_op jit(solution)/shard_map/ppermute | solution.py:881
  41.6 4.7 %collective-permute-start.10 = (bf16[256,128]{1,0:T(8,128)(2,1)S(1)}, bf16[256,128]{1,0:T(8,128)(2,1)S(1)}, u32[]{:S(2)}, u32[]{:S(2)}) collective-permute-start(bf16[256,128]{1,0:T(8,128)(2,1)S(1)} %get-tuple-element.180), channel_id=1, source_target_pairs={{0,4},{1,5},{2,6},{3,7},{4,0},{5,1},{6,2},{7,3},{8,12},{9,13},{10,... | collective-permute-start | bytes 196616 | tf_op jit(solution)/shard_map/ppermute | solution.py:881
  46.3 4.8 %collective-permute-start.11 = (bf16[256,128]{1,0:T(8,128)(2,1)S(1)}, bf16[256,128]{1,0:T(8,128)(2,1)S(1)}, u32[]{:S(2)}, u32[]{:S(2)}) collective-permute-start(bf16[256,128]{1,0:T(8,128)(2,1)S(1)} %slice.11), channel_id=1, source_target_pairs={{0,2},{1,3},{2,0},{3,1},{4,6},{5,7},{6,4},{7,5},{8,10},{9,11},{10,... | collective-permute-start | bytes 196616 | tf_op jit(solution)/shard_map/ppermute | solution.py:881
  48.1 5.8 %collective-permute-start.12 = (bf16[256,128]{1,0:T(8,128)(2,1)S(1)}, bf16[256,128]{1,0:T(8,128)(2,1)S(1)}, u32[]{:S(2)}, u32[]{:S(2)}) collective-permute-start(bf16[256,128]{1,0:T(8,128)(2,1)S(1)} %get-tuple-element.182), channel_id=1, source_target_pairs={{0,8},{1,9},{2,10},{3,11},{4,12},{5,13},{6,14},{7,15},{8,0},{9,1},... | collective-permute-start | bytes 196616 | tf_op jit(solution)/shard_map/ppermute | solution.py:881
  53.9 4.3 %collective-permute-start.13 = (bf16[256,128]{1,0:T(8,128)(2,1)S(1)}, bf16[256,128]{1,0:T(8,128)(2,1)S(1)}, u32[]{:S(2)}, u32[]{:S(2)}) collective-permute-start(bf16[256,128]{1,0:T(8,128)(2,1)S(1)} %get-tuple-element.316), channel_id=1, source_target_pairs={{0,16},{16,0},{1,17},{17,1},{2,18},{18,2},{3,19},{19,3},{4,20},{20... | collective-permute-start | bytes 196616 | tf_op jit(solution)/shard_map/ppermute | solution.py:881
  65.1 5.9 %collective-permute-start.14 = (bf16[8,208,512]{2,1,0:T(8,128)(2,1)S(1)}, bf16[8,208,512]{2,1,0:T(8,128)(2,1)S(1)}, u32[]{:S(2)}, u32[]{:S(2)}) collective-permute-start(bf16[8,208,512]{2,1,0:T(8,128)(2,1)S(1)} %get-tuple-element.190), channel_id=1, source_target_pairs={{0,1},{1,0},{2,3},{3,2},{4,5},{5,4},{6,7},{7,6},{8,9},{9,8},{10,11... | collective-permute-start | bytes 5111816 | tf_op jit(solution)/shard_map/ppermute | solution.py:881
  70.5 3.5 %collective-permute-start.17 = (bf16[8,192,512]{2,1,0:T(8,128)(2,1)S(1)}, bf16[8,192,512]{2,1,0:T(8,128)(2,1)S(1)}, u32[]{:S(2)}, u32[]{:S(2)}) collective-permute-start(bf16[8,192,512]{2,1,0:T(8,128)(2,1)S(1)} %get-tuple-element.208), channel_id=1, source_target_pairs={{0,1},{1,0},{2,3},{3,2},{4,5},{5,4},{6,7},{7,6},{8,9},{9,8},{10,11... | collective-permute-start | bytes 4718600 | tf_op jit(solution)/shard_map/ppermute | solution.py:881
  71.1 10.4 %collective-permute-start.16 = (bf16[1,208,512]{2,1,0:T(8,128)(2,1)S(1)}, bf16[1,208,512]{2,1,0:T(8,128)(2,1)S(1)}, u32[]{:S(2)}, u32[]{:S(2)}) collective-permute-start(bf16[1,208,512]{2,1,0:T(8,128)(2,1)S(1)} %get-tuple-element.206), channel_id=1, source_target_pairs={{0,2},{1,5},{2,6},{3,1},{4,0},{5,9},{6,10},{7,3},{8,4},{9,13},{10,... | collective-permute-start | bytes 638984 | tf_op jit(solution)/shard_map/ppermute | solution.py:900
  74.1 9.6 %collective-permute-start.21 = (bf16[1,192,512]{2,1,0:T(8,128)(2,1)S(1)}, bf16[1,192,512]{2,1,0:T(8,128)(2,1)S(1)}, u32[]{:S(2)}, u32[]{:S(2)}) collective-permute-start(bf16[1,192,512]{2,1,0:T(8,128)(2,1)S(1)} %get-tuple-element.211), channel_id=1, source_target_pairs={{0,2},{1,5},{2,6},{3,1},{4,0},{5,9},{6,10},{7,3},{8,4},{9,13},{10,... | collective-permute-start | bytes 589832 | tf_op jit(solution)/shard_map/ppermute | solution.py:900
  74.7 6.8 %collective-permute-start.15 = (bf16[1,208,512]{2,1,0:T(8,128)(2,1)S(1)}, bf16[1,208,512]{2,1,0:T(8,128)(2,1)S(1)}, u32[]{:S(2)}, u32[]{:S(2)}) collective-permute-start(bf16[1,208,512]{2,1,0:T(8,128)(2,1)S(1)} %get-tuple-element.205), channel_id=1, source_target_pairs={{0,4},{1,3},{2,0},{3,7},{4,8},{5,1},{6,2},{7,11},{8,12},{9,5},{10,... | collective-permute-start | bytes 638984 | tf_op jit(solution)/shard_map/ppermute | solution.py:900
  76.8 7.0 %collective-permute-start.20 = (bf16[1,192,512]{2,1,0:T(8,128)(2,1)S(1)}, bf16[1,192,512]{2,1,0:T(8,128)(2,1)S(1)}, u32[]{:S(2)}, u32[]{:S(2)}) collective-permute-start(bf16[1,192,512]{2,1,0:T(8,128)(2,1)S(1)} %get-tuple-element.218), channel_id=1, source_target_pairs={{0,4},{1,3},{2,0},{3,7},{4,8},{5,1},{6,2},{7,11},{8,12},{9,5},{10,... | collective-permute-start | bytes 589832 | tf_op jit(solution)/shard_map/ppermute | solution.py:900
  81.6 7.4 %collective-permute-start.19 = (bf16[1,208,512]{2,1,0:T(8,128)(2,1)S(1)}, bf16[1,208,512]{2,1,0:T(8,128)(2,1)S(1)}, u32[]{:S(2)}, u32[]{:S(2)}) collective-permute-start(bf16[1,208,512]{2,1,0:T(8,128)(2,1)S(1)} %get-tuple-element.217), channel_id=1, source_target_pairs={{0,2},{1,5},{2,6},{3,1},{4,0},{5,9},{6,10},{7,3},{8,4},{9,13},{10,... | collective-permute-start | bytes 638984 | tf_op jit(solution)/shard_map/ppermute | solution.py:900
  82.2 8.1 %collective-permute-start.18 = (bf16[1,208,512]{2,1,0:T(8,128)(2,1)S(1)}, bf16[1,208,512]{2,1,0:T(8,128)(2,1)S(1)}, u32[]{:S(2)}, u32[]{:S(2)}) collective-permute-start(bf16[1,208,512]{2,1,0:T(8,128)(2,1)S(1)} %get-tuple-element.216), channel_id=1, source_target_pairs={{0,4},{1,3},{2,0},{3,7},{4,8},{5,1},{6,2},{7,11},{8,12},{9,5},{10,... | collective-permute-start | bytes 638984 | tf_op jit(solution)/shard_map/ppermute | solution.py:900
  83.8 9.5 %collective-permute-start.25 = (bf16[1,192,512]{2,1,0:T(8,128)(2,1)S(1)}, bf16[1,192,512]{2,1,0:T(8,128)(2,1)S(1)}, u32[]{:S(2)}, u32[]{:S(2)}) collective-permute-start(bf16[1,192,512]{2,1,0:T(8,128)(2,1)S(1)} %get-tuple-element.226), channel_id=1, source_target_pairs={{0,2},{1,5},{2,6},{3,1},{4,0},{5,9},{6,10},{7,3},{8,4},{9,13},{10,... | collective-permute-start | bytes 589832 | tf_op jit(solution)/shard_map/ppermute | solution.py:900
  84.4 9.7 %collective-permute-start.24 = (bf16[1,192,512]{2,1,0:T(8,128)(2,1)S(1)}, bf16[1,192,512]{2,1,0:T(8,128)(2,1)S(1)}, u32[]{:S(2)}, u32[]{:S(2)}) collective-permute-start(bf16[1,192,512]{2,1,0:T(8,128)(2,1)S(1)} %get-tuple-element.221), channel_id=1, source_target_pairs={{0,4},{1,3},{2,0},{3,7},{4,8},{5,1},{6,2},{7,11},{8,12},{9,5},{10,... | collective-permute-start | bytes 589832 | tf_op jit(solution)/shard_map/ppermute | solution.py:900
  90.4 7.3 %collective-permute-start.23 = (bf16[1,208,512]{2,1,0:T(8,128)(2,1)S(1)}, bf16[1,208,512]{2,1,0:T(8,128)(2,1)S(1)}, u32[]{:S(2)}, u32[]{:S(2)}) collective-permute-start(bf16[1,208,512]{2,1,0:T(8,128)(2,1)S(1)} %get-tuple-element.225), channel_id=1, source_target_pairs={{0,2},{1,5},{2,6},{3,1},{4,0},{5,9},{6,10},{7,3},{8,4},{9,13},{10,... | collective-permute-start | bytes 638984 | tf_op jit(solution)/shard_map/ppermute | solution.py:900
  92.1 7.7 %collective-permute-start.22 = (bf16[1,208,512]{2,1,0:T(8,128)(2,1)S(1)}, bf16[1,208,512]{2,1,0:T(8,128)(2,1)S(1)}, u32[]{:S(2)}, u32[]{:S(2)}) collective-permute-start(bf16[1,208,512]{2,1,0:T(8,128)(2,1)S(1)} %get-tuple-element.224), channel_id=1, source_target_pairs={{0,4},{1,3},{2,0},{3,7},{4,8},{5,1},{6,2},{7,11},{8,12},{9,5},{10,... | collective-permute-start | bytes 638984 | tf_op jit(solution)/shard_map/ppermute | solution.py:900
  94.1 7.9 %collective-permute-start.28 = (bf16[1,192,512]{2,1,0:T(8,128)(2,1)S(1)}, bf16[1,192,512]{2,1,0:T(8,128)(2,1)S(1)}, u32[]{:S(2)}, u32[]{:S(2)}) collective-permute-start(bf16[1,192,512]{2,1,0:T(8,128)(2,1)S(1)} %get-tuple-element.233), channel_id=1, source_target_pairs={{0,2},{1,5},{2,6},{3,1},{4,0},{5,9},{6,10},{7,3},{8,4},{9,13},{10,... | collective-permute-start | bytes 589832 | tf_op jit(solution)/shard_map/ppermute | solution.py:900
  94.5 8.1 %collective-permute-start.27 = (bf16[1,192,512]{2,1,0:T(8,128)(2,1)S(1)}, bf16[1,192,512]{2,1,0:T(8,128)(2,1)S(1)}, u32[]{:S(2)}, u32[]{:S(2)}) collective-permute-start(bf16[1,192,512]{2,1,0:T(8,128)(2,1)S(1)} %get-tuple-element.229), channel_id=1, source_target_pairs={{0,4},{1,3},{2,0},{3,7},{4,8},{5,1},{6,2},{7,11},{8,12},{9,5},{10,... | collective-permute-start | bytes 589832 | tf_op jit(solution)/shard_map/ppermute | solution.py:900
  99.9 5.9 %collective-permute-start.26 = (bf16[1,208,512]{2,1,0:T(8,128)(2,1)S(1)}, bf16[1,208,512]{2,1,0:T(8,128)(2,1)S(1)}, u32[]{:S(2)}, u32[]{:S(2)}) collective-permute-start(bf16[1,208,512]{2,1,0:T(8,128)(2,1)S(1)} %get-tuple-element.232), channel_id=1, source_target_pairs={{0,4},{1,3},{2,0},{3,7},{4,8},{5,1},{6,2},{7,11},{8,12},{9,5},{10,... | collective-permute-start | bytes 638984 | tf_op jit(solution)/shard_map/ppermute | solution.py:900
  102.6 6.1 %collective-permute-start.31 = (bf16[1,192,512]{2,1,0:T(8,128)(2,1)S(1)}, bf16[1,192,512]{2,1,0:T(8,128)(2,1)S(1)}, u32[]{:S(2)}, u32[]{:S(2)}) collective-permute-start(bf16[1,192,512]{2,1,0:T(8,128)(2,1)S(1)} %get-tuple-element.236), channel_id=1, source_target_pairs={{0,4},{1,3},{2,0},{3,7},{4,8},{5,1},{6,2},{7,11},{8,12},{9,5},{10,... | collective-permute-start | bytes 589832 | tf_op jit(solution)/shard_map/ppermute | solution.py:900
  105.8 8.2 %collective-permute-start.30 = (bf16[1,208,512]{2,1,0:T(8,128)(2,1)S(1)}, bf16[1,208,512]{2,1,0:T(8,128)(2,1)S(1)}, u32[]{:S(2)}, u32[]{:S(2)}) collective-permute-start(bf16[1,208,512]{2,1,0:T(8,128)(2,1)S(1)} %shard_map.312.refs_0_), channel_id=1, source_target_pairs={{0,2},{1,5},{2,6},{3,1},{4,0},{5,9},{6,10},{7,3},{8,4},{9,13},{10,... | collective-permute-start | bytes 638984 | tf_op jit(solution)/shard_map/ppermute | solution.py:900
  107.6 7.5 %collective-permute-start.29 = (bf16[1,208,512]{2,1,0:T(8,128)(2,1)S(1)}, bf16[1,208,512]{2,1,0:T(8,128)(2,1)S(1)}, u32[]{:S(2)}, u32[]{:S(2)}) collective-permute-start(bf16[1,208,512]{2,1,0:T(8,128)(2,1)S(1)} %shard_map.312.refs_0_), channel_id=1, source_target_pairs={{0,4},{1,3},{2,0},{3,7},{4,8},{5,1},{6,2},{7,11},{8,12},{9,5},{10,... | collective-permute-start | bytes 638984 | tf_op jit(solution)/shard_map/ppermute | solution.py:900
  108.8 9.3 %collective-permute-start.35 = (bf16[1,192,512]{2,1,0:T(8,128)(2,1)S(1)}, bf16[1,192,512]{2,1,0:T(8,128)(2,1)S(1)}, u32[]{:S(2)}, u32[]{:S(2)}) collective-permute-start(bf16[1,192,512]{2,1,0:T(8,128)(2,1)S(1)} %shard_map.313.refs_0_), channel_id=1, source_target_pairs={{0,2},{1,5},{2,6},{3,1},{4,0},{5,9},{6,10},{7,3},{8,4},{9,13},{10,... | collective-permute-start | bytes 589832 | tf_op jit(solution)/shard_map/ppermute | solution.py:900
  111.3 7.1 %collective-permute-start.34 = (bf16[1,192,512]{2,1,0:T(8,128)(2,1)S(1)}, bf16[1,192,512]{2,1,0:T(8,128)(2,1)S(1)}, u32[]{:S(2)}, u32[]{:S(2)}) collective-permute-start(bf16[1,192,512]{2,1,0:T(8,128)(2,1)S(1)} %shard_map.313.refs_0_), channel_id=1, source_target_pairs={{0,4},{1,3},{2,0},{3,7},{4,8},{5,1},{6,2},{7,11},{8,12},{9,5},{10,... | collective-permute-start | bytes 589832 | tf_op jit(solution)/shard_map/ppermute | solution.py:900
  115.1 8.2 %collective-permute-start.33 = (bf16[1,208,512]{2,1,0:T(8,128)(2,1)S(1)}, bf16[1,208,512]{2,1,0:T(8,128)(2,1)S(1)}, u32[]{:S(2)}, u32[]{:S(2)}) collective-permute-start(bf16[1,208,512]{2,1,0:T(8,128)(2,1)S(1)} %get-tuple-element.270.refs_6_), channel_id=1, source_target_pairs={{0,2},{1,5},{2,6},{3,1},{4,0},{5,9},{6,10},{7,3},{8,4},{9,13},{10,... | collective-permute-start | bytes 638984 | tf_op jit(solution)/shard_map/ppermute | solution.py:900
  117.2 7.9 %collective-permute-start.32 = (bf16[1,208,512]{2,1,0:T(8,128)(2,1)S(1)}, bf16[1,208,512]{2,1,0:T(8,128)(2,1)S(1)}, u32[]{:S(2)}, u32[]{:S(2)}) collective-permute-start(bf16[1,208,512]{2,1,0:T(8,128)(2,1)S(1)} %get-tuple-element.265.refs_1_), channel_id=1, source_target_pairs={{0,4},{1,3},{2,0},{3,7},{4,8},{5,1},{6,2},{7,11},{8,12},{9,5},{10,... | collective-permute-start | bytes 638984 | tf_op jit(solution)/shard_map/ppermute | solution.py:900
  118.4 9.1 %collective-permute-start.39 = (bf16[1,192,512]{2,1,0:T(8,128)(2,1)S(1)}, bf16[1,192,512]{2,1,0:T(8,128)(2,1)S(1)}, u32[]{:S(2)}, u32[]{:S(2)}) collective-permute-start(bf16[1,192,512]{2,1,0:T(8,128)(2,1)S(1)} %get-tuple-element.278.refs_6_), channel_id=1, source_target_pairs={{0,2},{1,5},{2,6},{3,1},{4,0},{5,9},{6,10},{7,3},{8,4},{9,13},{10,... | collective-permute-start | bytes 589832 | tf_op jit(solution)/shard_map/ppermute | solution.py:900
  121.6 7.8 %collective-permute-start.38 = (bf16[1,192,512]{2,1,0:T(8,128)(2,1)S(1)}, bf16[1,192,512]{2,1,0:T(8,128)(2,1)S(1)}, u32[]{:S(2)}, u32[]{:S(2)}) collective-permute-start(bf16[1,192,512]{2,1,0:T(8,128)(2,1)S(1)} %get-tuple-element.273.refs_1_), channel_id=1, source_target_pairs={{0,4},{1,3},{2,0},{3,7},{4,8},{5,1},{6,2},{7,11},{8,12},{9,5},{10,... | collective-permute-start | bytes 589832 | tf_op jit(solution)/shard_map/ppermute | solution.py:900
  125.1 7.9 %collective-permute-start.37 = (bf16[1,208,512]{2,1,0:T(8,128)(2,1)S(1)}, bf16[1,208,512]{2,1,0:T(8,128)(2,1)S(1)}, u32[]{:S(2)}, u32[]{:S(2)}) collective-permute-start(bf16[1,208,512]{2,1,0:T(8,128)(2,1)S(1)} %get-tuple-element.269.refs_5_), channel_id=1, source_target_pairs={{0,2},{1,5},{2,6},{3,1},{4,0},{5,9},{6,10},{7,3},{8,4},{9,13},{10,... | collective-permute-start | bytes 638984 | tf_op jit(solution)/shard_map/ppermute | solution.py:900
  126.5 7.1 %collective-permute-start.36 = (bf16[1,208,512]{2,1,0:T(8,128)(2,1)S(1)}, bf16[1,208,512]{2,1,0:T(8,128)(2,1)S(1)}, u32[]{:S(2)}, u32[]{:S(2)}) collective-permute-start(bf16[1,208,512]{2,1,0:T(8,128)(2,1)S(1)} %get-tuple-element.266.refs_2_), channel_id=1, source_target_pairs={{0,4},{1,3},{2,0},{3,7},{4,8},{5,1},{6,2},{7,11},{8,12},{9,5},{10,... | collective-permute-start | bytes 638984 | tf_op jit(solution)/shard_map/ppermute | solution.py:900
  129.4 6.1 %collective-permute-start.42 = (bf16[1,192,512]{2,1,0:T(8,128)(2,1)S(1)}, bf16[1,192,512]{2,1,0:T(8,128)(2,1)S(1)}, u32[]{:S(2)}, u32[]{:S(2)}) collective-permute-start(bf16[1,192,512]{2,1,0:T(8,128)(2,1)S(1)} %get-tuple-element.277.refs_5_), channel_id=1, source_target_pairs={{0,2},{1,5},{2,6},{3,1},{4,0},{5,9},{6,10},{7,3},{8,4},{9,13},{10,... | collective-permute-start | bytes 589832 | tf_op jit(solution)/shard_map/ppermute | solution.py:900
  131.0 5.7 %collective-permute-start.41 = (bf16[1,192,512]{2,1,0:T(8,128)(2,1)S(1)}, bf16[1,192,512]{2,1,0:T(8,128)(2,1)S(1)}, u32[]{:S(2)}, u32[]{:S(2)}) collective-permute-start(bf16[1,192,512]{2,1,0:T(8,128)(2,1)S(1)} %get-tuple-element.274.refs_2_), channel_id=1, source_target_pairs={{0,4},{1,3},{2,0},{3,7},{4,8},{5,1},{6,2},{7,11},{8,12},{9,5},{10,... | collective-permute-start | bytes 589832 | tf_op jit(solution)/shard_map/ppermute | solution.py:900
  136.8 9.4 %collective-permute-start.46 = (bf16[7,208,512]{2,1,0:T(8,128)(2,1)S(1)}, bf16[7,208,512]{2,1,0:T(8,128)(2,1)S(1)}, u32[]{:S(2)}, u32[]{:S(2)}) collective-permute-start(bf16[7,208,512]{2,1,0:T(8,128)(2,1)S(1)} %shard_map.320.refs_0_), channel_id=1, source_target_pairs={{0,1},{1,0},{2,3},{3,2},{4,5},{5,4},{6,7},{7,6},{8,9},{9,8},{10,11... | collective-permute-start | bytes 4472840 | tf_op jit(solution)/shard_map/ppermute | solution.py:881
  136.9 9.2 %collective-permute-start.47 = (bf16[7,192,512]{2,1,0:T(8,128)(2,1)S(1)}, bf16[7,192,512]{2,1,0:T(8,128)(2,1)S(1)}, u32[]{:S(2)}, u32[]{:S(2)}) collective-permute-start(bf16[7,192,512]{2,1,0:T(8,128)(2,1)S(1)} %shard_map.321.refs_1_.refs_4_), channel_id=1, source_target_pairs={{0,1},{1,0},{2,3},{3,2},{4,5},{5,4},{6,7},{7,6},{8,9},{9,8},{10,11... | collective-permute-start | bytes 4128776 | tf_op jit(solution)/shard_map/ppermute | solution.py:881
  137.5 5.8 %collective-permute-start.40 = (bf16[1,208,512]{2,1,0:T(8,128)(2,1)S(1)}, bf16[1,208,512]{2,1,0:T(8,128)(2,1)S(1)}, u32[]{:S(2)}, u32[]{:S(2)}) collective-permute-start(bf16[1,208,512]{2,1,0:T(8,128)(2,1)S(1)} %get-tuple-element.267.refs_3_), channel_id=1, source_target_pairs={{0,4},{1,3},{2,0},{3,7},{4,8},{5,1},{6,2},{7,11},{8,12},{9,5},{10,... | collective-permute-start | bytes 638984 | tf_op jit(solution)/shard_map/ppermute | solution.py:900
  138.0 7.5 %collective-permute-start.43 = (bf16[1,192,512]{2,1,0:T(8,128)(2,1)S(1)}, bf16[1,192,512]{2,1,0:T(8,128)(2,1)S(1)}, u32[]{:S(2)}, u32[]{:S(2)}) collective-permute-start(bf16[1,192,512]{2,1,0:T(8,128)(2,1)S(1)} %get-tuple-element.275.refs_3_), channel_id=1, source_target_pairs={{0,4},{1,3},{2,0},{3,7},{4,8},{5,1},{6,2},{7,11},{8,12},{9,5},{10,... | collective-permute-start | bytes 589832 | tf_op jit(solution)/shard_map/ppermute | solution.py:900
  145.5 4.0 %collective-permute-start.44 = (bf16[1,208,512]{2,1,0:T(8,128)(2,1)S(1)}, bf16[1,208,512]{2,1,0:T(8,128)(2,1)S(1)}, u32[]{:S(2)}, u32[]{:S(2)}) collective-permute-start(bf16[1,208,512]{2,1,0:T(8,128)(2,1)S(1)} %shard_map.325.refs_0_), channel_id=1, source_target_pairs={{0,1},{1,0},{2,3},{3,2},{4,5},{5,4},{6,7},{7,6},{8,9},{9,8},{10,11... | collective-permute-start | bytes 638984 | tf_op jit(solution)/shard_map/ppermute | solution.py:881
  145.6 3.9 %collective-permute-start.45 = (bf16[1,192,512]{2,1,0:T(8,128)(2,1)S(1)}, bf16[1,192,512]{2,1,0:T(8,128)(2,1)S(1)}, u32[]{:S(2)}, u32[]{:S(2)}) collective-permute-start(bf16[1,192,512]{2,1,0:T(8,128)(2,1)S(1)} %shard_map.326.refs_1_.refs_5_), channel_id=1, source_target_pairs={{0,1},{1,0},{2,3},{3,2},{4,5},{5,4},{6,7},{7,6},{8,9},{9,8},{10,11... | collective-permute-start | bytes 589832 | tf_op jit(solution)/shard_map/ppermute | solution.py:881
  (15 other events, 179.8 us)

commit v6 on v5

--- a/solution.py
+++ b/solution.py
@@ -36,14 +36,16 @@
 SECOND = REST // 16 + TAIL
 CIRCLE = (0, 2, 4, 6, 7, 5, 3, 1)
 RING = len(CIRCLE)
+AHEAD = (RING // 2, RING // 2 - 1)
+LATER = tuple(k for k in range(RING) if k not in AHEAD)
 GROUPS = ((0, 1, 2, 3, 5, 6, 7), (4,))
 STEP_COST = 3 * 10**7
 SPREAD_COST = 0
 ROUND = (("step", 0), ("step", 1))
 ORDER = (
     (("open", 0), ("open", 1), ("total", 0), ("total", 1)) + ROUND * 7
-    + (("share", 0, 0), ("share", 1, 0), ("spread", ((True, 0),))) + ROUND
-    + (("share", 0, 1), ("share", 1, 1), ("spread", ((False, 0),)), ("spread", ((True, 1), (False, 1))))
+    + (("share", 0, 0), ("share", 1, 0), ("spread", ((True, 0),)), ("spread", ((False, 0),))) + ROUND
+    + (("share", 0, 1), ("share", 1, 1), ("spread", ((True, 1), (False, 1))))
 )
 MIB = 1024 * 1024
 
@@ -93,7 +95,7 @@
 def bounds_of(lens_ref, row):
     ends, total = [], jnp.int32(0)
     for k in range(DOCS_ROW):
-        total = total + lens_ref[row, k]
+        total = total + lens_ref[k, row]
         ends.append(total)
     return ends
 
@@ -122,6 +124,19 @@
 
 def col_sum(values):
     return jnp.sum(values, axis=0, keepdims=True)
+
+
+def here(size):
+    me, stream = lax.axis_index("dp"), lax.axis_index("stream")
+    top = size // 2
+    has_top = jnp.where((me & top) != 0, 1, 0)
+    base = jnp.where(stream == 0, me & ~top, me | top)
+    near_at = jnp.where((me & 2) != 0, 1, 0) + jnp.where((me & 1) != 0, 2, 0)
+    chip = (me >> 1) % RING
+    place = jnp.int32(0)
+    for k, one in enumerate(CIRCLE):
+        place = jnp.where(chip == one, k, place)
+    return me, stream, base, near_at, has_top, me & 1, place
 
 
 def fetch(pairs, sems):
@@ -147,15 +162,18 @@
 
 
 def encoder_forward(
-    where_ref, lens_ref, labels_ref, table_hbm, x_hbm, wqkv_hbm, bqkv_hbm, wout_hbm, bout_hbm,
+    size, lens_hbm, labels_hbm, table_hbm, x_hbm, wqkv_hbm, bqkv_hbm, wout_hbm, bout_hbm,
     g1_hbm, s1_hbm, wup_hbm, bup_hbm, wdown_hbm, bdown_hbm, g2_hbm, s2_hbm, wproj_hbm,
     vec_ref, qkv_hbm, rope_hbm, probs_hbm, mixed_hbm, xh1_hbm, rs1_hbm, act_hbm, slope_hbm,
     xh2_hbm, rs2_hbm, affine_hbm,
     qkv_ref, rope_ref, probs_ref, mixed_ref, xh1_ref, rs1_ref, act_ref, slope_ref,
     xh2_ref, rs2_ref, affine_ref, out_sems,
     table_ref, x_ref, wqkv_ref, bqkv_ref, wout_ref, bout_ref, g1_ref, s1_ref, wup_ref, bup_ref,
-    wdown_ref, bdown_ref, g2_ref, s2_ref, wproj_ref, sems,
+    wdown_ref, bdown_ref, g2_ref, s2_ref, wproj_ref, lens_ref, labels_ref, sems,
 ):
+    me, stream = here(size)[:2]
+    is_query = stream == 0
+    scalars = fetch(((lens_hbm, lens_ref), (labels_hbm, labels_ref)), sems.at[pl.ds(15, 2)])
     copies = fetch(
         (
             (table_hbm, table_ref), (x_hbm, x_ref), (wqkv_hbm, wqkv_ref), (bqkv_hbm, bqkv_ref),
@@ -172,7 +190,8 @@
         copy.start()
         kept.append(copy)
 
-    me, is_query = where_ref[0], where_ref[1] == 0
+    for copy in scalars:
+        copy.wait()
     ends = bounds_of(lens_ref, me)
 
     def layout(spot):
@@ -343,11 +362,12 @@
 
 
 def matching_stats(
-    masks, lanes, where_ref, scale_ref, lens_ref, near_ref, far_ref, *refs
+    size, masks, lanes, scale_ref, lens_hbm, near_ref, far_ref, *refs
 ):
-    doc_refs = refs[:-6]
-    totals_ref, el_ref, hot_ref, stats_ref, turn_ref, unit_ref = refs[-6:]
-    base, near_at = where_ref[2], where_ref[3]
+    doc_refs = refs[:-8]
+    totals_ref, el_ref, hot_ref, stats_ref, turn_ref, unit_ref, lens_ref, sems = refs[-8:]
+    scalars = fetch(((lens_hbm, lens_ref),), sems)
+    base, near_at = here(size)[2:4]
     span = ROW + EXT
     queries = load_queries(near_ref, far_ref)
     count = queries.shape[0]
@@ -359,6 +379,8 @@
     doc_rows = turn_ref.shape[1] // ROW
     docs = doc_rows * DOCS_ROW
     ids = row_ids(base, masks, doc_rows)
+    for copy in scalars:
+        copy.wait()
     marks = doc_marks(lens_ref, ids, lanes, False)
     totals = jnp.zeros((count, lanes), F32)
     for p in range(doc_rows):
@@ -377,7 +399,7 @@
             own = jnp.zeros(shape, jnp.bool_)
             for m in range(len(RANGES)):
                 own = jnp.logical_or(own, lane == m * docs + p * DOCS_ROW + k)
-            length = jnp.where(own, lens_ref[ids[p], k], length)
+            length = jnp.where(own, lens_ref[k, ids[p]], length)
             name = jnp.where(own, ids[p] * DOCS_ROW + k, name)
     log_length = jnp.log(length.astype(F32))
     matched = (jnp.log(totals) - log_length[:1]) * (1.0 / SHARPNESS)
@@ -412,11 +434,13 @@
 
 
 def matching_back(
-    masks, lanes, total_queries, where_ref, scale_ref, lens_ref, totals_ref, el_ref, hot_ref,
-    own_ref, over_y, over_x, over_both, unitq_ref, qt_ref, invq_ref, unit_ref, invd_ref, *refs
+    size, masks, lanes, scale_ref, lens_hbm, totals_ref, el_ref, hot_ref, own_ref, over_y, over_x, over_both, unitq_ref, qt_ref, invq_ref, unit_ref, invd_ref, *refs
 ):
-    dq_ref, far_ref, keep_ref, send_ref, loss_ref, dot_ref, dt_ref, stats_ref = refs[-8:]
-    base, near_at = where_ref[2], where_ref[3]
+    dq_ref, far_ref, keep_ref, send_ref, loss_ref = refs[-10:-5]
+    dot_ref, dt_ref, stats_ref, lens_ref, sems = refs[-5:]
+    scalars = fetch(((lens_hbm, lens_ref),), sems)
+    _, stream, base, near_at = here(size)[:4]
+    total_queries = size * (ROW // QLEN)
     temper = SHARPNESS * LOG2E
     count = unitq_ref.shape[1]
     inv_q = [invq_ref[:, m : m + 1] for m in range(len(RANGES))]
@@ -425,9 +449,8 @@
     doc_rows = unit_ref.shape[2] // ROW
     docs = doc_rows * DOCS_ROW
     ids = row_ids(base, masks, doc_rows)
-    marks = doc_marks(lens_ref, ids, lanes, True)
     groups = count // ROW
-    odd_y, odd_x = (near_at & 1) == 1, where_ref[1] == 1
+    odd_y, odd_x = (near_at & 1) == 1, stream == 1
     parts = [own_ref[...], over_y[...], over_x[...], over_both[...]]
     parts = [jnp.where(odd_y, a, b) for a, b in ((parts[1], parts[0]), (parts[0], parts[1]),
                                                   (parts[3], parts[2]), (parts[2], parts[3]))]
@@ -461,6 +484,9 @@
         jnp.where(line == 1, jnp.sum(moved, axis=0, keepdims=True) * (1.0 / total_queries), 0.0),
     )
     loss_ref[...] = loss
+    for copy in scalars:
+        copy.wait()
+    marks = doc_marks(lens_ref, ids, lanes, True)
     scale = jnp.exp(jnp.full((8, lanes), scale_ref[0], F32))[:1]
     coeff = (el_ref[...] / sums - hot_ref[...]) * (scale * (1.0 / (QLEN * total_queries)))
     coeff = jnp.broadcast_to(coeff[:, None, :], (groups * 8, QLEN, lanes)).reshape(count, lanes)
@@ -473,7 +499,7 @@
         for p in range(doc_rows):
             block = unit_ref[m, :, p * ROW : (p + 1) * ROW]
             mark = marks[p][m]
-            if len(refs) > 8:
+            if len(refs) > 10:
                 exps = refs[0][m, :, p * ROW : (p + 1) * ROW].astype(F32)
             else:
                 exps = jnp.exp2(mm(unit_q[m], block))
@@ -574,28 +600,17 @@
 
 
 def feed_back(
-    where_ref, dq_ref, dd_ref, got_ref, xh2_ref, rs2_ref, affine_ref, wproj_ref, wup_ref, xh1_ref,
-    wdown_hbm, slope_hbm, act_hbm,
+    size, dq_ref, dd_ref, got_ref, xh2_ref, rs2_ref, affine_ref, wproj_ref, slope_ref, act_ref,
+    xh1_ref, wup_ref, wdown_hbm,
     keep_ref, send_ref, tail_keep, tail_send, dfirst_ref, gproj_ref, small_ref,
-    dinner_ref, wdown_ref, slope_ref, act_ref, sems,
+    dinner_ref, wdown_ref, sems,
 ):
     step = 512
     spans = [slice(c * step, (c + 1) * step) for c in range(FF // step)]
-    copies = fetch(
-        [
-            pair
-            for span in spans
-            for pair in (
-                (wdown_hbm.at[span, :], wdown_ref.at[span, :]),
-                (slope_hbm.at[:, span], slope_ref.at[:, span]),
-                (act_hbm.at[:, span], act_ref.at[:, span]),
-            )
-        ],
-        sems,
-    )
+    copies = fetch([(wdown_hbm.at[span, :], wdown_ref.at[span, :]) for span in spans], sems)
     g1, s1, g2, s2 = [affine_ref[k : k + 1, :] for k in range(4)]
-    is_query, docs_there = where_ref[1] == 0, where_ref[4] == 0
-    places = (where_ref[5], where_ref[6])
+    _, stream, _, _, has_top, *places = here(size)
+    is_query, docs_there = stream == 0, has_top == 0
     got = got_ref[...].astype(F32)
     d_vec = jnp.where(
         is_query,
@@ -617,8 +632,7 @@
     d_first = d_sum
     for c in range(FF // step):
         cols = spans[c]
-        for copy in copies[3 * c : 3 * c + 3]:
-            copy.wait()
+        copies[c].wait()
         d_act = mm_nt(d_branch, wdown_ref[cols, :])
         d_inner = (d_act * slope_ref[:, cols].astype(F32)).astype(BF16)
         dinner_ref[:, cols] = d_inner
@@ -648,11 +662,11 @@
 
 
 def attend_back(
-    where_ref, dfirst_ref, gproj_ref, small_ref, loss_ref, tail_keep, tail_send, xh1_ref, rs1_ref, affine_ref, mixed_ref, wout_ref,
+    size, dfirst_ref, gproj_ref, small_ref, loss_ref, tail_keep, tail_send, xh1_ref, rs1_ref, affine_ref, mixed_ref, wout_ref,
     qkv_ref, probs_ref, rope_ref, x_ref, wqkv_ref,
-    keep_ref, send_ref, tokens_ref, djoined_ref, rest_ref,
+    keep_ref, ahead_ref, send_ref, tokens_ref, djoined_ref, rest_ref,
 ):
-    core, place = where_ref[5], where_ref[6]
+    me, *_, core, place = here(size)
     d_first = dfirst_ref[...]
     xhat = xh1_ref[...]
     gain = affine_ref[0:1, :]
@@ -706,14 +720,15 @@
         tokens = tokens + mm_nt(d_part, wqkv_ref[:, cols])
     tokens_ref[...] = tokens
     smalls += [bias_out, gain_grad, shift_grad] + [small_ref[k : k + 1, :] for k in range(7)]
-    counted = jnp.where((where_ref[0] & 3) == 0, 1.0, 0.0)
+    counted = jnp.where((me & 3) == 0, 1.0, 0.0)
     lines = [digits_of(loss_ref[k : k + 1, :]) * counted for k in range(2)]
     smalls.append(jnp.concatenate(lines + [jnp.zeros((1, D - 256), F32)], axis=1))
     for k, row in enumerate(smalls):
         rest_ref[4 * D + 8 * k : 4 * D + 8 * k + 1, :] = row
     for k in range(RING):
-        for ref, tail_ref, owner in (
-            (keep_ref, tail_keep, core), (send_ref, tail_send, 1 - core)
+        sent, at = (ahead_ref, AHEAD.index(k)) if k in AHEAD else (send_ref, LATER.index(k))
+        for ref, index, tail_ref, owner in (
+            (keep_ref, k, tail_keep, core), (sent, at, tail_send, 1 - core)
         ):
             block = owner * RING + block_at(owner, place, k)
             parts = []
@@ -727,12 +742,12 @@
                 )
             )
             parts.append(rest_ref[pl.ds(pl.multiple_of(4 * D + block * 8, 8), 8), :])
-            ref[k, : REST // 16, :] = jnp.concatenate(parts, axis=0).astype(BF16)
-            ref[k, REST // 16 :, :] = tail_ref[k]
-
-
-def spread(jobs, last, where_ref, *refs):
-    core, place = where_ref[5], where_ref[6]
+            ref[index, : REST // 16, :] = jnp.concatenate(parts, axis=0).astype(BF16)
+            ref[index, REST // 16 :, :] = tail_ref[k]
+
+
+def spread(size, jobs, last, *refs):
+    core, place = here(size)[-2:]
     halves = refs[: 2 * len(jobs)]
     wide_one, wide_two, wide_qkv, wide_proj, small_ref, sems = refs[-6:]
     outs = refs[-21:-6] if last else refs[-11:-6]
@@ -799,17 +814,17 @@
         copy.wait()
 
 
-def spread_call(jobs, where, halves, outs, others):
+def spread_call(size, jobs, halves, outs, others):
     last = len(others) > 0
     shapes = ((FF, D), (D, FF), (D, 3 * D), (D, D), (D, PROJ))
     widths = (3 * D, D, D, D, FF, D, D, D) if last else ()
-    args = [where, *halves, *others, *outs]
+    args = [*halves, *others, *outs]
     count = sum(len(GROUPS[group]) for _, group in jobs)
-    before = 1 + len(halves) + len(others)
+    before = len(halves) + len(others)
     return call(
-        partial(spread, jobs, last),
+        partial(spread, size, jobs, last),
         args,
-        [SMEM] + [VMEM] * (before - 1) + [HBM] * len(outs),
+        [VMEM] * before + [HBM] * len(outs),
         [pltpu.HBM(shape, F32) for shape in shapes]
         + [shape_of((1, width)) for width in widths]
         + [shape_of((1,))] * (2 * last),
@@ -852,30 +867,6 @@
     )(*args)
 
 
-def spread_half_call(where, halves, near=None, outs=()):
-    mine = near is None
-    args = [where, *halves] + ([] if mine else [near, *outs])
-    specs = [SMEM] + [VMEM] * (3 if mine else 4) + [HBM] * len(outs)
-    shapes = ((FF, D), (D, FF), (D, 3 * D), (D, D), (D, PROJ))
-    widths = () if mine else (3 * D, D, D, D, FF, D, D, D)
-    return call(
-        partial(spread_half, mine),
-        args,
-        specs,
-        [pltpu.HBM(shape, F32) for shape in shapes] + [shape_of((1, width)) for width in widths],
-        [
-            pltpu.VMEM((RING, FF // (2 * RING), D), F32),
-            pltpu.VMEM((RING, FF // (2 * RING), D), F32),
-            pltpu.VMEM((RING, 4 * SHARE, D), F32),
-            pltpu.VMEM((RING, SHARE, PROJ), F32),
-            pltpu.SemaphoreType.DMA((7 * RING,)),
-        ],
-        out_specs=[HBM] * 5 + [VMEM] * len(widths) + [SMEM] * (2 * last),
-        aliases={} if mine else {5 + k: k for k in range(5)},
-        room=14,
-    )
-
-
 def swapped(value, mask, axis="dp"):
     size = lax.axis_size(axis)
     return lax.ppermute(value, axis, [(k, k ^ mask) for k in range(size)])
@@ -911,14 +902,21 @@
 
 
 def first_blocks(places, keep_ref, pair_ref, *outs):
-    for ref, k in zip(outs, places):
-        ref[0] = (keep_ref[k].astype(F32) + pair_ref[k].astype(F32)).astype(BF16)
+    for ref, (k, j) in zip(outs, places):
+        ref[0] = (keep_ref[k].astype(F32) + pair_ref[j].astype(F32)).astype(BF16)
+
+
+def later_blocks(places, keep_ref, pair_ref, out_ref):
+    for k in AHEAD:
+        out_ref[k] = jnp.zeros(out_ref.shape[1:], BF16)
+    for k, j in places:
+        out_ref[k] = (keep_ref[k].astype(F32) + pair_ref[j].astype(F32)).astype(BF16)
 
 
 class Summed:
-    def __init__(self, keep, send, others):
+    def __init__(self, keep, sends, others):
         self.keep, self.others, self.hop = keep, others, 0
-        self.pair = swapped(send, 1)
+        self.pairs = [swapped(send, 1) for send in sends]
         self.sent, self.blocks, self.near, self.far = [], {}, [], []
 
     def blocks_call(self, blocks, places, held):
@@ -932,11 +930,11 @@
         )
 
     def open(self, after):
-        keep, pair, _ = lax.optimization_barrier((self.keep, self.pair, after))
-        half = RING // 2
+        keep, pair, _ = lax.optimization_barrier((self.keep, self.pairs[0], after))
         shape = (1, *keep.shape[1:])
+        places = [(k, AHEAD.index(k) if len(self.pairs) > 1 else k) for k in AHEAD]
         first, second = call(
-            partial(first_blocks, (half, half - 1)),
+            partial(first_blocks, places),
             (keep, pair),
             [VMEM] * 2,
             [shape_of(shape, BF16)] * 2,
@@ -948,7 +946,15 @@
 
     def total(self, after):
         keep, _ = lax.optimization_barrier((self.keep, after))
-        self.keep = added(keep, self.pair)
+        later = [(k, LATER.index(k) if len(self.pairs) > 1 else k) for k in LATER]
+        (self.keep,) = call(
+            partial(later_blocks, later),
+            (keep, self.pairs[-1]),
+            [VMEM] * 2,
+            [shape_of(keep.shape, BF16)],
+            room=8,
+            cost=STEP_COST,
+        )
         return self.keep
 
     def step(self, after):
@@ -1001,26 +1007,17 @@
     stream = lax.axis_index("stream")
     is_query = stream == 0
     has_top = (me & top_mask) != 0
-    base = jnp.where(is_query, me & ~top_mask, me | top_mask)
-    near_at = jnp.where((me & near_masks[1]) != 0, 1, 0) + jnp.where((me & near_masks[0]) != 0, 2, 0)
-    core = me & 1
-    chip = (me >> 1) % RING
-    place = jnp.int32(0)
-    for k, one in enumerate(CIRCLE):
-        place = jnp.where(chip == one, k, place)
-    where = jnp.stack(
-        [me, stream, base, near_at, has_top.astype(jnp.int32), core, place, place]
-    ).astype(jnp.int32)
+    lens = doc_lengths.T
     scale = log_scale.reshape(1)
 
     vec, qkv, rope, probs, mixed, xh1, rs1, act, slope, xh2, rs2, affine = call(
-        encoder_forward,
+        partial(encoder_forward, size),
         (
-            where, doc_lengths, labels, jnp.asarray(rope_table()), tokens[0], qkv_weight[0], qkv_bias,
+            lens, labels, jnp.asarray(rope_table()), tokens[0], qkv_weight[0], qkv_bias,
             out_weight[0], out_bias, first_gain, first_shift, up_weight[0], up_bias,
             down_weight[0], down_bias, second_gain, second_shift, proj_weight[0],
         ),
-        [SMEM] * 3 + [HBM] * 15,
+        [HBM] * 17,
         [shape_of((ROW + EXT, PROJ), BF16)] + [pltpu.HBM(*kind) for kind in KEPT],
         [pltpu.VMEM(*kind) for kind in KEPT]
         + [pltpu.SemaphoreType.DMA((len(KEPT) + 6,))]
@@ -1031,7 +1028,11 @@
                 (1, FF), (FF, D), (1, D), (1, D), (1, D), (D, PROJ),
             )
         ]
-        + [pltpu.SemaphoreType.DMA((15,))],
+        + [
+            pltpu.SMEM(lens.shape, jnp.int32),
+            pltpu.SMEM(labels.shape, jnp.int32),
+            pltpu.SemaphoreType.DMA((17,)),
+        ],
         room=40,
         out_specs=[VMEM] + [HBM] * len(KEPT),
     )
@@ -1056,19 +1057,19 @@
     tokens_d = doc_rows * ROW
     tokens_q = 4 * ROW
     lanes = -(-3 * doc_rows * DOCS_ROW // 128) * 128
-    total_queries = size * (ROW // QLEN)
     room = 20 if doc_rows <= 4 else 56
+    scalars = [pltpu.SMEM(lens.shape, jnp.int32), pltpu.SemaphoreType.DMA((1,))]
     totals, el, hot, stats = call(
-        partial(matching_stats, doc_masks, lanes),
-        (where, scale, doc_lengths, near, far, *pieces),
-        [SMEM] * 3 + [VMEM] * (2 + len(pieces)),
+        partial(matching_stats, size, doc_masks, lanes),
+        (scale, lens, near, far, *pieces),
+        [SMEM, HBM] + [VMEM] * (2 + len(pieces)),
         [
             shape_of((tokens_q, lanes)),
             shape_of((tokens_q // QLEN, lanes)),
             shape_of((tokens_q // QLEN, lanes)),
             shape_of((tokens_q // QLEN, 128)),
         ],
-        [pltpu.VMEM((PROJ, tokens_d), F32), pltpu.VMEM((3, PROJ, tokens_d), BF16)],
+        [pltpu.VMEM((PROJ, tokens_d), F32), pltpu.VMEM((3, PROJ, tokens_d), BF16), *scalars],
         room=room,
     )
     small_enough = doc_rows <= 4
@@ -1093,9 +1094,9 @@
     pairs = [(k * size + r, (1 - k) * size + (r ^ other_y)) for k in range(2) for r in every]
     over_both = lax.ppermute(stats, ("stream", "dp"), pairs)
     dq, dq_send, keep, send, loss = call(
-        partial(matching_back, doc_masks, lanes, total_queries),
-        (where, scale, doc_lengths, totals, el, hot, stats, over_y, over_x, over_both, *ready),
-        [SMEM] * 3 + [VMEM] * (7 + len(ready)),
+        partial(matching_back, size, doc_masks, lanes),
+        (scale, lens, totals, el, hot, stats, over_y, over_x, over_both, *ready),
+        [SMEM, HBM] + [VMEM] * (7 + len(ready)),
         [shape_of((tokens_q // 2, PROJ), BF16)] * 2
         + [shape_of((tokens_d // 2, PROJ), BF16)] * 2
         + [shape_of((8, 128))],
@@ -1103,6 +1104,7 @@
             pltpu.VMEM((tokens_q, PROJ), F32),
             pltpu.VMEM((3, PROJ, tokens_d), F32),
             pltpu.VMEM((tokens_q // QLEN, 128), F32),
+            *scalars,
         ],
         room=room,
     )
@@ -1123,32 +1125,31 @@
     got = swapped(jnp.where(is_query, dd, dq), 1, "stream")
 
     one_keep, one_send, tail_keep, tail_send, d_first, gproj, small = call(
-        feed_back,
+        partial(feed_back, size),
         (
-            where, dq, dd, got, xh2, rs2, affine, proj_weight[0], up_weight[0], xh1,
-            down_weight[0], slope, act,
+            dq, dd, got, xh2, rs2, affine, proj_weight[0], slope, act, xh1, up_weight[0],
+            down_weight[0],
         ),
-        [SMEM] + [VMEM] * 3 + [HELD] * 6 + [HBM] * 3,
+        [VMEM] * 3 + [HELD] * 8 + [HBM],
         [shape_of((RING, FIRST, D), BF16)] * 2
         + [shape_of((RING, TAIL, D), BF16)] * 2
         + [shape_of((ROW, D)), shape_of((D, PROJ)), shape_of((8, D))],
         [
             pltpu.VMEM((ROW, FF), BF16),
             pltpu.VMEM((FF, D), BF16),
-            pltpu.VMEM((ROW, FF), BF16),
-            pltpu.VMEM((ROW, FF), BF16),
-            pltpu.SemaphoreType.DMA((12,)),
+            pltpu.SemaphoreType.DMA((4,)),
         ],
         room=24,
     )
-    two_keep, two_send, tokens_grad = call(
-        attend_back,
+    two_keep, two_ahead, two_send, tokens_grad = call(
+        partial(attend_back, size),
         (
-            where, d_first, gproj, small, loss, tail_keep, tail_send, xh1, rs1, affine, mixed, out_weight[0], qkv, probs, rope,
+            d_first, gproj, small, loss, tail_keep, tail_send, xh1, rs1, affine, mixed, out_weight[0], qkv, probs, rope,
             tokens[0], qkv_weight[0],
         ),
-        [SMEM] + [VMEM] * 6 + [HELD] * 10,
-        [shape_of((RING, SECOND, D), BF16)] * 2 + [shape_of((ROW, D))],
+        [VMEM] * 6 + [HELD] * 10,
+        [shape_of((count, SECOND, D), BF16) for count in (RING, len(AHEAD), len(LATER))]
+        + [shape_of((ROW, D))],
         [
             pltpu.VMEM((ROW, 3 * D), BF16),
             pltpu.VMEM((4 * D + 16 * RING, D), F32),
@@ -1156,7 +1157,8 @@
         room=24,
     )
     one, two = [
-        Summed(keep, send, others) for keep, send in ((one_keep, one_send), (two_keep, two_send))
+        Summed(keep, sends, others)
+        for keep, *sends in ((one_keep, one_send), (two_keep, two_ahead, two_send))
     ]
     token, outs = tokens_grad, ()
     for event in ORDER:
@@ -1168,7 +1170,7 @@
             ]
             *halves, _ = lax.optimization_barrier((*halves, token))
             others = [*two.near, *two.far] if event == ORDER[-1] else []
-            outs = spread_call(jobs, where, halves, outs[:5], others)
+            outs = spread_call(size, jobs, halves, outs[:5], others)
             token = outs[0]
             continue
         piece = (one, two)[k]

time: 152 us -> 145 us (0.954)
  Pallas kernels: 39.6 us -> 36.7 us
    pallas_call x32 -> x34, Pallas kernels: 39.6 us -> 36.7 us  [call(): pl.pallas_call(kernel, out_shape=outs, in_specs=specs, out_specs=out_spec...]
    ppermute x19 -> x20, waiting for transfers between devices: 19.1 us -> 19.1 us  [swapped(): return lax.ppermute(value, axis, [(k, k ^ mask) for k in range(size)])]
    ppermute x19 -> x20, starting transfers between devices: 21.8 us -> 21.8 us  [swapped(): return lax.ppermute(value, axis, [(k, k ^ mask) for k in range(size)])]
  transfers between devices with their start and end apart: 48 -> 49, of which waited for: 35 -> 35; matrix products, arithmetic and copies ran while one was open for 1% -> 0% of each run, Pallas kernels for 10% -> 9%
where the time goes in v6:
time: 145 us
  waiting for transfers between devices  53.8 us (37%)
  starting transfers between devices  52.4 us (36%)
  Pallas kernels  36.7 us (25%)
  between operations  1.98 us (1%)
    pallas_call x34, Pallas kernels, call(): pl.pallas_call(kernel, out_shape=outs, in_specs=specs, out_specs=out_spec...  36.7 us
    ppermute x28, waiting for transfers between devices, ring_swap(): return lax.ppermute(value, 'dp', pairs)  34.7 us
    ppermute x28, starting transfers between devices, ring_swap(): return lax.ppermute(value, 'dp', pairs)  29.1 us
    ppermute x20, starting transfers between devices, swapped(): return lax.ppermute(value, axis, [(k, k ^ mask) for k in range(size)])  21.8 us
    ppermute x20, waiting for transfers between devices, swapped(): return lax.ppermute(value, axis, [(k, k ^ mask) for k in range(size)])  19.1 us
  transfers between devices with their start and end apart: 49, of which 35 were waited for; matrix products, arithmetic and copies ran while one was open for 0% of the time, Pallas kernels for 9%

profile of v6, /device:TPU:0, one launch (start us, length us, event | category | flops | bytes accessed | tf_op | source)
XLA Modules:
  0.0 145.1 jit_solution(10416945497913522816)
XLA Ops:
  0.6 8.2 %shard_map.297 = (bf16[272,128]{1,0:T(8,128)(2,1)S(1)}, bf16[256,1536]{1,0:T(8,128)(2,1)}, f32[256,256]{1,0:T(8,128)}, bf16[8,256,256]{2,1,0:T(8,128)(2,1)}, bf1...) custom-call(s32[5,16]{1,0:T(8,128)} %bitcast.35, ...), custom_call_target="tpu_custom_call" | custom-call | flops 100000000 | bytes 10000000 | tf_op jit(solution)/shard_map/pallas_call | solution.py:856
  8.9 3.0 %collective-permute-start = (bf16[272,128]{1,0:T(8,128)(2,1)S(1)}, bf16[272,128]{1,0:T(8,128)(2,1)S(1)}, u32[]{:S(2)}, u32[]{:S(2)}) collective-permute-start(bf16[272,128]{1,0:T(8,128)(2,1)S(1)} %get-tuple-element.167), channel_id=1, source_target_pairs={{0,16},{16,0},{1,17},{17,1},{2,18},{18,2},{3,19},{19,3},{4,20},{20... | collective-permute-start | bytes 208904 | tf_op jit(solution)/shard_map/ppermute | solution.py:872
  11.9 2.3 %collective-permute-done = bf16[272,128]{1,0:T(8,128)(2,1)S(1)} collective-permute-done((bf16[272,128]{1,0:T(8,128)(2,1)S(1)}, bf16[272,128]{1,0:T(8,128)(2,1)S(1)}, u32[]{:S(2)}, u32[]{:S(2)}) %collective-permute-start) | collective-permute-done | bytes 69664 | tf_op jit(solution)/shard_map/ppermute | solution.py:872
  14.2 2.1 %collective-permute-start.1 = (bf16[272,128]{1,0:T(8,128)(2,1)S(1)}, bf16[272,128]{1,0:T(8,128)(2,1)S(1)}, u32[]{:S(2)}, u32[]{:S(2)}) collective-permute-start(bf16[272,128]{1,0:T(8,128)(2,1)S(1)} %broadcast_select_fusion), channel_id=1, source_target_pairs={{0,2},{1,3},{2,0},{3,1},{4,6},{5,7},{6,4},{7,5},{8,10},{9,11},{10,... | collective-permute-start | bytes 208904 | tf_op jit(solution)/shard_map/ppermute | solution.py:872
  16.3 2.7 %collective-permute-start.3 = (bf16[256,128]{1,0:T(8,128)(2,1)S(1)}, bf16[256,128]{1,0:T(8,128)(2,1)S(1)}, u32[]{:S(2)}, u32[]{:S(2)}) collective-permute-start(bf16[256,128]{1,0:T(8,128)(2,1)S(1)} %slice_select_fusion), channel_id=1, source_target_pairs={{0,8},{1,9},{2,10},{3,11},{4,12},{5,13},{6,14},{7,15},{8,0},{9,1},... | collective-permute-start | bytes 196616 | tf_op jit(solution)/shard_map/ppermute | solution.py:872
  19.1 2.5 %collective-permute-done.3 = bf16[256,128]{1,0:T(8,128)(2,1)S(1)} collective-permute-done((bf16[256,128]{1,0:T(8,128)(2,1)S(1)}, bf16[256,128]{1,0:T(8,128)(2,1)S(1)}, u32[]{:S(2)}, u32[]{:S(2)}) %collective-permute-start.3) | collective-permute-done | bytes 65568 | tf_op jit(solution)/shard_map/ppermute | solution.py:872
  21.6 1.6 %collective-permute-start.4 = (bf16[256,128]{1,0:T(8,128)(2,1)S(1)}, bf16[256,128]{1,0:T(8,128)(2,1)S(1)}, u32[]{:S(2)}, u32[]{:S(2)}) collective-permute-start(bf16[256,128]{1,0:T(8,128)(2,1)S(1)} %broadcast_select_fusion.2.refs_0_), channel_id=1, source_target_pairs={{0,4},{1,5},{2,6},{3,7},{4,0},{5,1},{6,2},{7,3},{8,12},{9,13},{10,... | collective-permute-start | bytes 196616 | tf_op jit(solution)/shard_map/ppermute | solution.py:872
  23.9 2.0 %collective-permute-done.4.refs_1_ = bf16[256,128]{1,0:T(8,128)(2,1)S(1)} collective-permute-done((bf16[256,128]{1,0:T(8,128)(2,1)S(1)}, bf16[256,128]{1,0:T(8,128)(2,1)S(1)}, u32[]{:S(2)}, u32[]{:S(2)}) %collective-permute-start.4) | collective-permute-done | bytes 65568 | tf_op jit(solution)/shard_map/ppermute | solution.py:872
  25.9 3.2 %shard_map.298 = (f32[1024,128]{1,0:T(8,128)S(1)}, f32[32,128]{1,0:T(8,128)S(1)}, f32[32,128]{1,0:T(8,128)S(1)}, f32[32,128]{1,0:T(8,128)S(1)}) custom-call(f32[1]{0:T(128)} %bitcast.16.scale_ref, s32[5,16]{1,0:T(8,128)} %bitcast.36, bf16[544,128]{1,0:T(8,128)(2,1)S(1)} %pad_maximum_fusion.near_ref, bf16[544,128]{1,0:T(8,128)(2,1)S(1)} %collective-permute-done.2.far_ref, ...), custom_call_target="tpu_custom_call" | custom-call | flops 100000000 | bytes 10000000 | tf_op jit(solution)/shard_map/pallas_call | solution.py:856
  30.4 1.4 collective-permute-start.8
  32.0 1.9 %collective-permute-start.6 = (f32[32,128]{1,0:T(8,128)S(1)}, f32[32,128]{1,0:T(8,128)S(1)}, u32[]{:S(2)}, u32[]{:S(2)}) collective-permute-start(f32[32,128]{1,0:T(8,128)S(1)} %add.9.own_ref), channel_id=1, source_target_pairs={{0,2},{1,3},{2,0},{3,1},{4,6},{5,7},{6,4},{7,5},{8,10},{9,11},{10,... | collective-permute-start | bytes 49160 | tf_op jit(solution)/shard_map/ppermute | solution.py:872
  33.8 1.4 shard_map.299
  35.8 3.9 %shard_map.300 = (bf16[512,128]{1,0:T(8,128)(2,1)S(1)}, bf16[512,128]{1,0:T(8,128)(2,1)S(1)}, bf16[256,128]{1,0:T(8,128)(2,1)S(1)}, bf16[256,128]{1,0:T(8,128)(2,1)S(1)}, f32[8,128]{1,0:T(8,128)S(1)}) custom-call(f32[1]{0:T(128)} %bitcast.17.scale_ref, s32[5,16]{1,0:T(8,128)} %bitcast.37, f32[1024,128]{1,0:T(8,128)S(1)} %get-tuple-element.168.totals_ref, ...), custom_call_target="tpu_custom_call" | custom-call | flops 100000000 | bytes 10000000 | tf_op jit(solution)/shard_map/pallas_call | solution.py:856
  39.7 2.0 %collective-permute-start.10 = (bf16[256,128]{1,0:T(8,128)(2,1)S(1)}, bf16[256,128]{1,0:T(8,128)(2,1)S(1)}, u32[]{:S(2)}, u32[]{:S(2)}) collective-permute-start(bf16[256,128]{1,0:T(8,128)(2,1)S(1)} %get-tuple-element.181), channel_id=1, source_target_pairs={{0,4},{1,5},{2,6},{3,7},{4,0},{5,1},{6,2},{7,3},{8,12},{9,13},{10,... | collective-permute-start | bytes 196616 | tf_op jit(solution)/shard_map/ppermute | solution.py:872
  41.7 2.7 %collective-permute-done.10.got_dd_ref = bf16[256,128]{1,0:T(8,128)(2,1)S(1)} collective-permute-done((bf16[256,128]{1,0:T(8,128)(2,1)S(1)}, bf16[256,128]{1,0:T(8,128)(2,1)S(1)}, u32[]{:S(2)}, u32[]{:S(2)}) %collective-permute-start.10) | collective-permute-done | bytes 65568 | tf_op jit(solution)/shard_map/ppermute | solution.py:872
  44.5 1.8 %collective-permute-start.11 = (bf16[256,128]{1,0:T(8,128)(2,1)S(1)}, bf16[256,128]{1,0:T(8,128)(2,1)S(1)}, u32[]{:S(2)}, u32[]{:S(2)}) collective-permute-start(bf16[256,128]{1,0:T(8,128)(2,1)S(1)} %slice.11), channel_id=1, source_target_pairs={{0,2},{1,3},{2,0},{3,1},{4,6},{5,7},{6,4},{7,5},{8,10},{9,11},{10,... | collective-permute-start | bytes 196616 | tf_op jit(solution)/shard_map/ppermute | solution.py:872
  46.2 3.0 %collective-permute-start.12 = (bf16[256,128]{1,0:T(8,128)(2,1)S(1)}, bf16[256,128]{1,0:T(8,128)(2,1)S(1)}, u32[]{:S(2)}, u32[]{:S(2)}) collective-permute-start(bf16[256,128]{1,0:T(8,128)(2,1)S(1)} %get-tuple-element.183), channel_id=1, source_target_pairs={{0,8},{1,9},{2,10},{3,11},{4,12},{5,13},{6,14},{7,15},{8,0},{9,1},... | collective-permute-start | bytes 196616 | tf_op jit(solution)/shard_map/ppermute | solution.py:872
  49.2 2.8 %collective-permute-done.12 = bf16[256,128]{1,0:T(8,128)(2,1)S(1)} collective-permute-done((bf16[256,128]{1,0:T(8,128)(2,1)S(1)}, bf16[256,128]{1,0:T(8,128)(2,1)S(1)}, u32[]{:S(2)}, u32[]{:S(2)}) %collective-permute-start.12) | collective-permute-done | bytes 65568 | tf_op jit(solution)/shard_map/ppermute | solution.py:872
  52.1 1.5 %collective-permute-start.13 = (bf16[256,128]{1,0:T(8,128)(2,1)S(1)}, bf16[256,128]{1,0:T(8,128)(2,1)S(1)}, u32[]{:S(2)}, u32[]{:S(2)}) collective-permute-start(bf16[256,128]{1,0:T(8,128)(2,1)S(1)} %get-tuple-element.318), channel_id=1, source_target_pairs={{0,16},{16,0},{1,17},{17,1},{2,18},{18,2},{3,19},{19,3},{4,20},{20... | collective-permute-start | bytes 196616 | tf_op jit(solution)/shard_map/ppermute | solution.py:872
  53.7 2.8 %collective-permute-done.13.got_ref = bf16[256,128]{1,0:T(8,128)(2,1)S(1)} collective-permute-done((bf16[256,128]{1,0:T(8,128)(2,1)S(1)}, bf16[256,128]{1,0:T(8,128)(2,1)S(1)}, u32[]{:S(2)}, u32[]{:S(2)}) %collective-permute-start.13) | collective-permute-done | bytes 65568 | tf_op jit(solution)/shard_map/ppermute | solution.py:872
  56.6 5.8 %shard_map.302 = (bf16[8,208,512]{2,1,0:T(8,128)(2,1)S(1)}, bf16[8,208,512]{2,1,0:T(8,128)(2,1)S(1)}, bf16[8,48,512]{2,1,0:T(8,128)(2,1)S(1)}, bf16[8,48,512]{2,...) custom-call(bf16[256,128]{1,0:T(8,128)(2,1)S(1)} %get-tuple-element.320.dq_ref, ...), custom_call_target="tpu_custom_call" | custom-call | flops 100000000 | bytes 10000000 | tf_op jit(solution)/shard_map/pallas_call | solution.py:856
  62.6 4.6 %shard_map.303 = (bf16[8,192,512]{2,1,0:T(8,128)(2,1)S(1)}, bf16[2,192,512]{2,1,0:T(8,128)(2,1)S(1)}, bf16[6,192,512]{2,1,0:T(8,128)(2,1)S(1)}, f32[256,512]{1,0:T(8,128)}) custom-call(f32[256,512]{1,0:T(8,128)S(1)} %get-tuple-element.192.dfirst_ref, f32[512,128]{1,0:T(8,128)S(1)} %get-tuple-element.193.gproj_ref, ...), custom_call_target="tpu_custom_call" | custom-call | flops 100000000 | bytes 10000000 | tf_op jit(solution)/shard_map/pallas_call | solution.py:856
  73.6 2.5 %collective-permute-done.15.refs_0_ = bf16[1,208,512]{2,1,0:T(8,128)(2,1)S(1)} collective-permute-done((bf16[1,208,512]{2,1,0:T(8,128)(2,1)S(1)}, bf16[1,208,512]{2,1,0:T(8,128)(2,1)S(1)}, u32[]{:S(2)}, u32[]{:S(2)}) %collective-permute-start.15) | collective-permute-done | bytes 213024 | tf_op jit(solution)/shard_map/ppermute | solution.py:891
  77.9 1.5 %collective-permute-start.19 = (bf16[1,208,512]{2,1,0:T(8,128)(2,1)S(1)}, bf16[1,208,512]{2,1,0:T(8,128)(2,1)S(1)}, u32[]{:S(2)}, u32[]{:S(2)}) collective-permute-start(bf16[1,208,512]{2,1,0:T(8,128)(2,1)S(1)} %get-tuple-element.218), channel_id=1, source_target_pairs={{0,4},{1,3},{2,0},{3,7},{4,8},{5,1},{6,2},{7,11},{8,12},{9,5},{10,... | collective-permute-start | bytes 638984 | tf_op jit(solution)/shard_map/ppermute | solution.py:891
  80.5 1.9 %collective-permute-start.25 = (bf16[1,192,512]{2,1,0:T(8,128)(2,1)S(1)}, bf16[1,192,512]{2,1,0:T(8,128)(2,1)S(1)}, u32[]{:S(2)}, u32[]{:S(2)}) collective-permute-start(bf16[1,192,512]{2,1,0:T(8,128)(2,1)S(1)} %get-tuple-element.223), channel_id=1, source_target_pairs={{0,4},{1,3},{2,0},{3,7},{4,8},{5,1},{6,2},{7,11},{8,12},{9,5},{10,... | collective-permute-start | bytes 589832 | tf_op jit(solution)/shard_map/ppermute | solution.py:891
  82.4 2.3 %collective-permute-done.20.refs_1_ = bf16[1,208,512]{2,1,0:T(8,128)(2,1)S(1)} collective-permute-done((bf16[1,208,512]{2,1,0:T(8,128)(2,1)S(1)}, bf16[1,208,512]{2,1,0:T(8,128)(2,1)S(1)}, u32[]{:S(2)}, u32[]{:S(2)}) %collective-permute-start.20) | collective-permute-done | bytes 213024 | tf_op jit(solution)/shard_map/ppermute | solution.py:891
  84.7 1.4 collective-permute-done.19.refs_0_
  88.9 1.4 collective-permute-done.25.refs_0_
  92.5 1.6 %collective-permute-done.24.refs_1_ = bf16[1,208,512]{2,1,0:T(8,128)(2,1)S(1)} collective-permute-done((bf16[1,208,512]{2,1,0:T(8,128)(2,1)S(1)}, bf16[1,208,512]{2,1,0:T(8,128)(2,1)S(1)}, u32[]{:S(2)}, u32[]{:S(2)}) %collective-permute-start.24) | collective-permute-done | bytes 213024 | tf_op jit(solution)/shard_map/ppermute | solution.py:891
  96.6 1.7 %collective-permute-done.29.refs_1_ = bf16[1,192,512]{2,1,0:T(8,128)(2,1)S(1)} collective-permute-done((bf16[1,192,512]{2,1,0:T(8,128)(2,1)S(1)}, bf16[1,192,512]{2,1,0:T(8,128)(2,1)S(1)}, u32[]{:S(2)}, u32[]{:S(2)}) %collective-permute-start.29) | collective-permute-done | bytes 196640 | tf_op jit(solution)/shard_map/ppermute | solution.py:891
  98.4 1.5 %collective-permute-start.32 = (bf16[1,192,512]{2,1,0:T(8,128)(2,1)S(1)}, bf16[1,192,512]{2,1,0:T(8,128)(2,1)S(1)}, u32[]{:S(2)}, u32[]{:S(2)}) collective-permute-start(bf16[1,192,512]{2,1,0:T(8,128)(2,1)S(1)} %get-tuple-element.238), channel_id=1, source_target_pairs={{0,4},{1,3},{2,0},{3,7},{4,8},{5,1},{6,2},{7,11},{8,12},{9,5},{10,... | collective-permute-start | bytes 589832 | tf_op jit(solution)/shard_map/ppermute | solution.py:891
  99.9 1.4 collective-permute-done.27.refs_0_
  103.4 2.4 %collective-permute-done.32.refs_0_ = bf16[1,192,512]{2,1,0:T(8,128)(2,1)S(1)} collective-permute-done((bf16[1,192,512]{2,1,0:T(8,128)(2,1)S(1)}, bf16[1,192,512]{2,1,0:T(8,128)(2,1)S(1)}, u32[]{:S(2)}, u32[]{:S(2)}) %collective-permute-start.32) | collective-permute-done | bytes 196640 | tf_op jit(solution)/shard_map/ppermute | solution.py:891
  108.0 1.6 %collective-permute-done.31.refs_1_ = bf16[1,208,512]{2,1,0:T(8,128)(2,1)S(1)} collective-permute-done((bf16[1,208,512]{2,1,0:T(8,128)(2,1)S(1)}, bf16[1,208,512]{2,1,0:T(8,128)(2,1)S(1)}, u32[]{:S(2)}, u32[]{:S(2)}) %collective-permute-start.31) | collective-permute-done | bytes 213024 | tf_op jit(solution)/shard_map/ppermute | solution.py:891
  110.5 1.7 %collective-permute-start.34 = (bf16[1,208,512]{2,1,0:T(8,128)(2,1)S(1)}, bf16[1,208,512]{2,1,0:T(8,128)(2,1)S(1)}, u32[]{:S(2)}, u32[]{:S(2)}) collective-permute-start(bf16[1,208,512]{2,1,0:T(8,128)(2,1)S(1)} %get-tuple-element.272.refs_6_), channel_id=1, source_target_pairs={{0,2},{1,5},{2,6},{3,1},{4,0},{5,9},{6,10},{7,3},{8,4},{9,13},{10,... | collective-permute-start | bytes 638984 | tf_op jit(solution)/shard_map/ppermute | solution.py:891
  112.7 2.2 %collective-permute-done.35.refs_0_ = bf16[1,192,512]{2,1,0:T(8,128)(2,1)S(1)} collective-permute-done((bf16[1,192,512]{2,1,0:T(8,128)(2,1)S(1)}, bf16[1,192,512]{2,1,0:T(8,128)(2,1)S(1)}, u32[]{:S(2)}, u32[]{:S(2)}) %collective-permute-start.35) | collective-permute-done | bytes 196640 | tf_op jit(solution)/shard_map/ppermute | solution.py:891
  114.9 1.5 %collective-permute-start.40 = (bf16[1,192,512]{2,1,0:T(8,128)(2,1)S(1)}, bf16[1,192,512]{2,1,0:T(8,128)(2,1)S(1)}, u32[]{:S(2)}, u32[]{:S(2)}) collective-permute-start(bf16[1,192,512]{2,1,0:T(8,128)(2,1)S(1)} %get-tuple-element.280.refs_6_), channel_id=1, source_target_pairs={{0,2},{1,5},{2,6},{3,1},{4,0},{5,9},{6,10},{7,3},{8,4},{9,13},{10,... | collective-permute-start | bytes 589832 | tf_op jit(solution)/shard_map/ppermute | solution.py:891
  117.0 1.4 collective-permute-done.34.refs_1_
  118.4 2.1 %collective-permute-done.33.refs_0_ = bf16[1,208,512]{2,1,0:T(8,128)(2,1)S(1)} collective-permute-done((bf16[1,208,512]{2,1,0:T(8,128)(2,1)S(1)}, bf16[1,208,512]{2,1,0:T(8,128)(2,1)S(1)}, u32[]{:S(2)}, u32[]{:S(2)}) %collective-permute-start.33) | collective-permute-done | bytes 213024 | tf_op jit(solution)/shard_map/ppermute | solution.py:891
  120.5 1.8 %collective-permute-start.38 = (bf16[1,208,512]{2,1,0:T(8,128)(2,1)S(1)}, bf16[1,208,512]{2,1,0:T(8,128)(2,1)S(1)}, u32[]{:S(2)}, u32[]{:S(2)}) collective-permute-start(bf16[1,208,512]{2,1,0:T(8,128)(2,1)S(1)} %get-tuple-element.271.refs_5_), channel_id=1, source_target_pairs={{0,2},{1,5},{2,6},{3,1},{4,0},{5,9},{6,10},{7,3},{8,4},{9,13},{10,... | collective-permute-start | bytes 638984 | tf_op jit(solution)/shard_map/ppermute | solution.py:891
  122.6 2.1 %collective-permute-done.39.refs_0_ = bf16[1,192,512]{2,1,0:T(8,128)(2,1)S(1)} collective-permute-done((bf16[1,192,512]{2,1,0:T(8,128)(2,1)S(1)}, bf16[1,192,512]{2,1,0:T(8,128)(2,1)S(1)}, u32[]{:S(2)}, u32[]{:S(2)}) %collective-permute-start.39) | collective-permute-done | bytes 196640 | tf_op jit(solution)/shard_map/ppermute | solution.py:891
  124.7 1.8 %collective-permute-start.43 = (bf16[1,192,512]{2,1,0:T(8,128)(2,1)S(1)}, bf16[1,192,512]{2,1,0:T(8,128)(2,1)S(1)}, u32[]{:S(2)}, u32[]{:S(2)}) collective-permute-start(bf16[1,192,512]{2,1,0:T(8,128)(2,1)S(1)} %get-tuple-element.279.refs_5_), channel_id=1, source_target_pairs={{0,2},{1,5},{2,6},{3,1},{4,0},{5,9},{6,10},{7,3},{8,4},{9,13},{10,... | collective-permute-start | bytes 589832 | tf_op jit(solution)/shard_map/ppermute | solution.py:891
  126.8 1.7 %collective-permute-done.38.refs_1_ = bf16[1,208,512]{2,1,0:T(8,128)(2,1)S(1)} collective-permute-done((bf16[1,208,512]{2,1,0:T(8,128)(2,1)S(1)}, bf16[1,208,512]{2,1,0:T(8,128)(2,1)S(1)}, u32[]{:S(2)}, u32[]{:S(2)}) %collective-permute-start.38) | collective-permute-done | bytes 213024 | tf_op jit(solution)/shard_map/ppermute | solution.py:891
  128.5 2.1 %collective-permute-done.43.refs_1_ = bf16[1,192,512]{2,1,0:T(8,128)(2,1)S(1)} collective-permute-done((bf16[1,192,512]{2,1,0:T(8,128)(2,1)S(1)}, bf16[1,192,512]{2,1,0:T(8,128)(2,1)S(1)}, u32[]{:S(2)}, u32[]{:S(2)}) %collective-permute-start.43) | collective-permute-done | bytes 196640 | tf_op jit(solution)/shard_map/ppermute | solution.py:891
  130.6 1.6 %collective-permute-done.42.refs_0_ = bf16[1,192,512]{2,1,0:T(8,128)(2,1)S(1)} collective-permute-done((bf16[1,192,512]{2,1,0:T(8,128)(2,1)S(1)}, bf16[1,192,512]{2,1,0:T(8,128)(2,1)S(1)}, u32[]{:S(2)}, u32[]{:S(2)}) %collective-permute-start.42) | collective-permute-done | bytes 196640 | tf_op jit(solution)/shard_map/ppermute | solution.py:891
  134.5 2.8 %shard_map.324 = (f32[2048,512]{1,0:T(8,128)}, f32[512,2048]{1,0:T(8,128)}, f32[512,1536]{1,0:T(8,128)}, f32[512,512]{1,0:T(8,128)}, f32[512,128]{1,0:T(8,128)}) custom-call(bf16[7,208,512]{2,1,0:T(8,128)(2,1)S(1)} %shard_map.322.refs_0_, bf16[7,192,512]{2,1,0:T(8,128)(2,1)S(1)} %shard_map.323.refs_1_.refs_4_), custom_call_target="tpu_custom_call" | custom-call | tf_op jit(solution)/shard_map/pallas_call | solution.py:856
  137.7 2.8 %shard_map.325 = (f32[2048,512]{1,0:T(8,128)}, f32[512,2048]{1,0:T(8,128)}, f32[512,1536]{1,0:T(8,128)}, f32[512,512]{1,0:T(8,128)}, f32[512,128]{1,0:T(8,128)}) custom-call(bf16[7,208,512]{2,1,0:T(8,128)(2,1)S(1)} %collective-permute-done.44.refs_0_, ...), custom_call_target="tpu_custom_call", output_to_operand_aliasing={{0}: (2, {}), {1}: (3, {}), {2}: (4, {}), {3}: (5, {}), {4}... | custom-call | tf_op jit(solution)/shard_map/pallas_call | solution.py:856
  143.0 1.9 %shard_map.330 = (f32[2048,512]{1,0:T(8,128)}, f32[512,2048]{1,0:T(8,128)}, f32[512,1536]{1,0:T(8,128)}, f32[512,512]{1,0:T(8,128)}, f32[512,128]{1,0:T(8,128)},...) custom-call(bf16[1,208,512]{2,1,0:T(8,128)(2,1)S(1)} %shard_map.328., ...), custom_call_target="tpu_custom_call", output_to_operand_aliasing={{0}: (8, {}), {1}: (9, {}), {2}: (10, {}), {3}: (11, {}), {... | custom-call | tf_op jit(solution)/shard_map/pallas_call | solution.py:856
  (123 shorter events, 31.1 us)
Async XLA Ops:
  8.9 5.3 %collective-permute-start = (bf16[272,128]{1,0:T(8,128)(2,1)S(1)}, bf16[272,128]{1,0:T(8,128)(2,1)S(1)}, u32[]{:S(2)}, u32[]{:S(2)}) collective-permute-start(bf16[272,128]{1,0:T(8,128)(2,1)S(1)} %get-tuple-element.167), channel_id=1, source_target_pairs={{0,16},{16,0},{1,17},{17,1},{2,18},{18,2},{3,19},{19,3},{4,20},{20... | collective-permute-start | bytes 208904 | tf_op jit(solution)/shard_map/ppermute | solution.py:872
  14.2 4.8 %collective-permute-start.1 = (bf16[272,128]{1,0:T(8,128)(2,1)S(1)}, bf16[272,128]{1,0:T(8,128)(2,1)S(1)}, u32[]{:S(2)}, u32[]{:S(2)}) collective-permute-start(bf16[272,128]{1,0:T(8,128)(2,1)S(1)} %broadcast_select_fusion), channel_id=1, source_target_pairs={{0,2},{1,3},{2,0},{3,1},{4,6},{5,7},{6,4},{7,5},{8,10},{9,11},{10,... | collective-permute-start | bytes 208904 | tf_op jit(solution)/shard_map/ppermute | solution.py:872
  16.3 5.2 %collective-permute-start.3 = (bf16[256,128]{1,0:T(8,128)(2,1)S(1)}, bf16[256,128]{1,0:T(8,128)(2,1)S(1)}, u32[]{:S(2)}, u32[]{:S(2)}) collective-permute-start(bf16[256,128]{1,0:T(8,128)(2,1)S(1)} %slice_select_fusion), channel_id=1, source_target_pairs={{0,8},{1,9},{2,10},{3,11},{4,12},{5,13},{6,14},{7,15},{8,0},{9,1},... | collective-permute-start | bytes 196616 | tf_op jit(solution)/shard_map/ppermute | solution.py:872
  19.0 6.9 %collective-permute-start.2 = (bf16[544,128]{1,0:T(8,128)(2,1)S(1)}, bf16[544,128]{1,0:T(8,128)(2,1)S(1)}, u32[]{:S(2)}, u32[]{:S(2)}) collective-permute-start(bf16[544,128]{1,0:T(8,128)(2,1)S(1)} %pad_maximum_fusion.near_ref), channel_id=1, source_target_pairs={{0,1},{1,0},{2,3},{3,2},{4,5},{5,4},{6,7},{7,6},{8,9},{9,8},{10,11... | collective-permute-start | bytes 417800 | tf_op jit(solution)/shard_map/ppermute | solution.py:872
  21.6 4.3 %collective-permute-start.4 = (bf16[256,128]{1,0:T(8,128)(2,1)S(1)}, bf16[256,128]{1,0:T(8,128)(2,1)S(1)}, u32[]{:S(2)}, u32[]{:S(2)}) collective-permute-start(bf16[256,128]{1,0:T(8,128)(2,1)S(1)} %broadcast_select_fusion.2.refs_0_), channel_id=1, source_target_pairs={{0,4},{1,5},{2,6},{3,7},{4,0},{5,1},{6,2},{7,3},{8,12},{9,13},{10,... | collective-permute-start | bytes 196616 | tf_op jit(solution)/shard_map/ppermute | solution.py:872
  30.4 4.9 %collective-permute-start.8 = (f32[32,128]{1,0:T(8,128)S(1)}, f32[32,128]{1,0:T(8,128)S(1)}, u32[]{:S(2)}, u32[]{:S(2)}) collective-permute-start(f32[32,128]{1,0:T(8,128)S(1)} %add.9.own_ref), channel_id=1, source_target_pairs={{0,18},{1,19},{2,16},{3,17},{4,22},{5,23},{6,20},{7,21},{8,26},{9,... | collective-permute-start | bytes 49160 | tf_op jit(solution)/shard_map/ppermute | solution.py:1095
  31.8 3.7 %collective-permute-start.7 = (f32[32,128]{1,0:T(8,128)S(1)}, f32[32,128]{1,0:T(8,128)S(1)}, u32[]{:S(2)}, u32[]{:S(2)}) collective-permute-start(f32[32,128]{1,0:T(8,128)S(1)} %add.9.own_ref), channel_id=1, source_target_pairs={{0,16},{16,0},{1,17},{17,1},{2,18},{18,2},{3,19},{19,3},{4,20},{20... | collective-permute-start | bytes 49160 | tf_op jit(solution)/shard_map/ppermute | solution.py:872
  32.0 3.7 %collective-permute-start.6 = (f32[32,128]{1,0:T(8,128)S(1)}, f32[32,128]{1,0:T(8,128)S(1)}, u32[]{:S(2)}, u32[]{:S(2)}) collective-permute-start(f32[32,128]{1,0:T(8,128)S(1)} %add.9.own_ref), channel_id=1, source_target_pairs={{0,2},{1,3},{2,0},{3,1},{4,6},{5,7},{6,4},{7,5},{8,10},{9,11},{10,... | collective-permute-start | bytes 49160 | tf_op jit(solution)/shard_map/ppermute | solution.py:872
  39.6 4.7 %collective-permute-start.9 = (bf16[512,128]{1,0:T(8,128)(2,1)S(1)}, bf16[512,128]{1,0:T(8,128)(2,1)S(1)}, u32[]{:S(2)}, u32[]{:S(2)}) collective-permute-start(bf16[512,128]{1,0:T(8,128)(2,1)S(1)} %get-tuple-element.179), channel_id=1, source_target_pairs={{0,1},{1,0},{2,3},{3,2},{4,5},{5,4},{6,7},{7,6},{8,9},{9,8},{10,11... | collective-permute-start | bytes 393224 | tf_op jit(solution)/shard_map/ppermute | solution.py:872
  39.7 4.7 %collective-permute-start.10 = (bf16[256,128]{1,0:T(8,128)(2,1)S(1)}, bf16[256,128]{1,0:T(8,128)(2,1)S(1)}, u32[]{:S(2)}, u32[]{:S(2)}) collective-permute-start(bf16[256,128]{1,0:T(8,128)(2,1)S(1)} %get-tuple-element.181), channel_id=1, source_target_pairs={{0,4},{1,5},{2,6},{3,7},{4,0},{5,1},{6,2},{7,3},{8,12},{9,13},{10,... | collective-permute-start | bytes 196616 | tf_op jit(solution)/shard_map/ppermute | solution.py:872
  44.5 4.8 %collective-permute-start.11 = (bf16[256,128]{1,0:T(8,128)(2,1)S(1)}, bf16[256,128]{1,0:T(8,128)(2,1)S(1)}, u32[]{:S(2)}, u32[]{:S(2)}) collective-permute-start(bf16[256,128]{1,0:T(8,128)(2,1)S(1)} %slice.11), channel_id=1, source_target_pairs={{0,2},{1,3},{2,0},{3,1},{4,6},{5,7},{6,4},{7,5},{8,10},{9,11},{10,... | collective-permute-start | bytes 196616 | tf_op jit(solution)/shard_map/ppermute | solution.py:872
  46.2 5.8 %collective-permute-start.12 = (bf16[256,128]{1,0:T(8,128)(2,1)S(1)}, bf16[256,128]{1,0:T(8,128)(2,1)S(1)}, u32[]{:S(2)}, u32[]{:S(2)}) collective-permute-start(bf16[256,128]{1,0:T(8,128)(2,1)S(1)} %get-tuple-element.183), channel_id=1, source_target_pairs={{0,8},{1,9},{2,10},{3,11},{4,12},{5,13},{6,14},{7,15},{8,0},{9,1},... | collective-permute-start | bytes 196616 | tf_op jit(solution)/shard_map/ppermute | solution.py:872
  52.1 4.3 %collective-permute-start.13 = (bf16[256,128]{1,0:T(8,128)(2,1)S(1)}, bf16[256,128]{1,0:T(8,128)(2,1)S(1)}, u32[]{:S(2)}, u32[]{:S(2)}) collective-permute-start(bf16[256,128]{1,0:T(8,128)(2,1)S(1)} %get-tuple-element.318), channel_id=1, source_target_pairs={{0,16},{16,0},{1,17},{17,1},{2,18},{18,2},{3,19},{19,3},{4,20},{20... | collective-permute-start | bytes 196616 | tf_op jit(solution)/shard_map/ppermute | solution.py:872
  62.4 5.3 %collective-permute-start.14 = (bf16[8,208,512]{2,1,0:T(8,128)(2,1)S(1)}, bf16[8,208,512]{2,1,0:T(8,128)(2,1)S(1)}, u32[]{:S(2)}, u32[]{:S(2)}) collective-permute-start(bf16[8,208,512]{2,1,0:T(8,128)(2,1)S(1)} %get-tuple-element.191), channel_id=1, source_target_pairs={{0,1},{1,0},{2,3},{3,2},{4,5},{5,4},{6,7},{7,6},{8,9},{9,8},{10,11... | collective-permute-start | bytes 5111816 | tf_op jit(solution)/shard_map/ppermute | solution.py:872
  67.2 6.0 %collective-permute-start.18 = (bf16[6,192,512]{2,1,0:T(8,128)(2,1)S(1)}, bf16[6,192,512]{2,1,0:T(8,128)(2,1)S(1)}, u32[]{:S(2)}, u32[]{:S(2)}) collective-permute-start(bf16[6,192,512]{2,1,0:T(8,128)(2,1)S(1)} %get-tuple-element.215), channel_id=1, source_target_pairs={{0,1},{1,0},{2,3},{3,2},{4,5},{5,4},{6,7},{7,6},{8,9},{9,8},{10,11... | collective-permute-start | bytes 3538952 | tf_op jit(solution)/shard_map/ppermute | solution.py:872
  67.7 3.0 %collective-permute-start.17 = (bf16[2,192,512]{2,1,0:T(8,128)(2,1)S(1)}, bf16[2,192,512]{2,1,0:T(8,128)(2,1)S(1)}, u32[]{:S(2)}, u32[]{:S(2)}) collective-permute-start(bf16[2,192,512]{2,1,0:T(8,128)(2,1)S(1)} %get-tuple-element.209), channel_id=1, source_target_pairs={{0,1},{1,0},{2,3},{3,2},{4,5},{5,4},{6,7},{7,6},{8,9},{9,8},{10,11... | collective-permute-start | bytes 1179656 | tf_op jit(solution)/shard_map/ppermute | solution.py:872
  67.9 8.2 %collective-permute-start.15 = (bf16[1,208,512]{2,1,0:T(8,128)(2,1)S(1)}, bf16[1,208,512]{2,1,0:T(8,128)(2,1)S(1)}, u32[]{:S(2)}, u32[]{:S(2)}) collective-permute-start(bf16[1,208,512]{2,1,0:T(8,128)(2,1)S(1)} %get-tuple-element.206), channel_id=1, source_target_pairs={{0,4},{1,3},{2,0},{3,7},{4,8},{5,1},{6,2},{7,11},{8,12},{9,5},{10,... | collective-permute-start | bytes 638984 | tf_op jit(solution)/shard_map/ppermute | solution.py:891
  69.2 8.0 %collective-permute-start.16 = (bf16[1,208,512]{2,1,0:T(8,128)(2,1)S(1)}, bf16[1,208,512]{2,1,0:T(8,128)(2,1)S(1)}, u32[]{:S(2)}, u32[]{:S(2)}) collective-permute-start(bf16[1,208,512]{2,1,0:T(8,128)(2,1)S(1)} %get-tuple-element.207), channel_id=1, source_target_pairs={{0,2},{1,5},{2,6},{3,1},{4,0},{5,9},{6,10},{7,3},{8,4},{9,13},{10,... | collective-permute-start | bytes 638984 | tf_op jit(solution)/shard_map/ppermute | solution.py:891
  70.8 9.4 %collective-permute-start.21 = (bf16[1,192,512]{2,1,0:T(8,128)(2,1)S(1)}, bf16[1,192,512]{2,1,0:T(8,128)(2,1)S(1)}, u32[]{:S(2)}, u32[]{:S(2)}) collective-permute-start(bf16[1,192,512]{2,1,0:T(8,128)(2,1)S(1)} %get-tuple-element.220), channel_id=1, source_target_pairs={{0,4},{1,3},{2,0},{3,7},{4,8},{5,1},{6,2},{7,11},{8,12},{9,5},{10,... | collective-permute-start | bytes 589832 | tf_op jit(solution)/shard_map/ppermute | solution.py:891
  72.2 8.1 %collective-permute-start.22 = (bf16[1,192,512]{2,1,0:T(8,128)(2,1)S(1)}, bf16[1,192,512]{2,1,0:T(8,128)(2,1)S(1)}, u32[]{:S(2)}, u32[]{:S(2)}) collective-permute-start(bf16[1,192,512]{2,1,0:T(8,128)(2,1)S(1)} %get-tuple-element.212), channel_id=1, source_target_pairs={{0,2},{1,5},{2,6},{3,1},{4,0},{5,9},{6,10},{7,3},{8,4},{9,13},{10,... | collective-permute-start | bytes 589832 | tf_op jit(solution)/shard_map/ppermute | solution.py:891
  77.3 7.4 %collective-permute-start.20 = (bf16[1,208,512]{2,1,0:T(8,128)(2,1)S(1)}, bf16[1,208,512]{2,1,0:T(8,128)(2,1)S(1)}, u32[]{:S(2)}, u32[]{:S(2)}) collective-permute-start(bf16[1,208,512]{2,1,0:T(8,128)(2,1)S(1)} %get-tuple-element.219), channel_id=1, source_target_pairs={{0,2},{1,5},{2,6},{3,1},{4,0},{5,9},{6,10},{7,3},{8,4},{9,13},{10,... | collective-permute-start | bytes 638984 | tf_op jit(solution)/shard_map/ppermute | solution.py:891
  77.9 8.2 %collective-permute-start.19 = (bf16[1,208,512]{2,1,0:T(8,128)(2,1)S(1)}, bf16[1,208,512]{2,1,0:T(8,128)(2,1)S(1)}, u32[]{:S(2)}, u32[]{:S(2)}) collective-permute-start(bf16[1,208,512]{2,1,0:T(8,128)(2,1)S(1)} %get-tuple-element.218), channel_id=1, source_target_pairs={{0,4},{1,3},{2,0},{3,7},{4,8},{5,1},{6,2},{7,11},{8,12},{9,5},{10,... | collective-permute-start | bytes 638984 | tf_op jit(solution)/shard_map/ppermute | solution.py:891
  80.4 8.6 %collective-permute-start.26 = (bf16[1,192,512]{2,1,0:T(8,128)(2,1)S(1)}, bf16[1,192,512]{2,1,0:T(8,128)(2,1)S(1)}, u32[]{:S(2)}, u32[]{:S(2)}) collective-permute-start(bf16[1,192,512]{2,1,0:T(8,128)(2,1)S(1)} %get-tuple-element.228), channel_id=1, source_target_pairs={{0,2},{1,5},{2,6},{3,1},{4,0},{5,9},{6,10},{7,3},{8,4},{9,13},{10,... | collective-permute-start | bytes 589832 | tf_op jit(solution)/shard_map/ppermute | solution.py:891
  80.5 9.8 %collective-permute-start.25 = (bf16[1,192,512]{2,1,0:T(8,128)(2,1)S(1)}, bf16[1,192,512]{2,1,0:T(8,128)(2,1)S(1)}, u32[]{:S(2)}, u32[]{:S(2)}) collective-permute-start(bf16[1,192,512]{2,1,0:T(8,128)(2,1)S(1)} %get-tuple-element.223), channel_id=1, source_target_pairs={{0,4},{1,3},{2,0},{3,7},{4,8},{5,1},{6,2},{7,11},{8,12},{9,5},{10,... | collective-permute-start | bytes 589832 | tf_op jit(solution)/shard_map/ppermute | solution.py:891
  86.2 7.9 %collective-permute-start.24 = (bf16[1,208,512]{2,1,0:T(8,128)(2,1)S(1)}, bf16[1,208,512]{2,1,0:T(8,128)(2,1)S(1)}, u32[]{:S(2)}, u32[]{:S(2)}) collective-permute-start(bf16[1,208,512]{2,1,0:T(8,128)(2,1)S(1)} %get-tuple-element.227), channel_id=1, source_target_pairs={{0,2},{1,5},{2,6},{3,1},{4,0},{5,9},{6,10},{7,3},{8,4},{9,13},{10,... | collective-permute-start | bytes 638984 | tf_op jit(solution)/shard_map/ppermute | solution.py:891
  87.1 8.2 %collective-permute-start.23 = (bf16[1,208,512]{2,1,0:T(8,128)(2,1)S(1)}, bf16[1,208,512]{2,1,0:T(8,128)(2,1)S(1)}, u32[]{:S(2)}, u32[]{:S(2)}) collective-permute-start(bf16[1,208,512]{2,1,0:T(8,128)(2,1)S(1)} %get-tuple-element.226), channel_id=1, source_target_pairs={{0,4},{1,3},{2,0},{3,7},{4,8},{5,1},{6,2},{7,11},{8,12},{9,5},{10,... | collective-permute-start | bytes 638984 | tf_op jit(solution)/shard_map/ppermute | solution.py:891
  90.4 7.9 %collective-permute-start.29 = (bf16[1,192,512]{2,1,0:T(8,128)(2,1)S(1)}, bf16[1,192,512]{2,1,0:T(8,128)(2,1)S(1)}, u32[]{:S(2)}, u32[]{:S(2)}) collective-permute-start(bf16[1,192,512]{2,1,0:T(8,128)(2,1)S(1)} %get-tuple-element.235), channel_id=1, source_target_pairs={{0,2},{1,5},{2,6},{3,1},{4,0},{5,9},{6,10},{7,3},{8,4},{9,13},{10,... | collective-permute-start | bytes 589832 | tf_op jit(solution)/shard_map/ppermute | solution.py:891
  91.3 7.0 %collective-permute-start.28 = (bf16[1,192,512]{2,1,0:T(8,128)(2,1)S(1)}, bf16[1,192,512]{2,1,0:T(8,128)(2,1)S(1)}, u32[]{:S(2)}, u32[]{:S(2)}) collective-permute-start(bf16[1,192,512]{2,1,0:T(8,128)(2,1)S(1)} %get-tuple-element.231), channel_id=1, source_target_pairs={{0,4},{1,3},{2,0},{3,7},{4,8},{5,1},{6,2},{7,11},{8,12},{9,5},{10,... | collective-permute-start | bytes 589832 | tf_op jit(solution)/shard_map/ppermute | solution.py:891
  95.4 5.9 %collective-permute-start.27 = (bf16[1,208,512]{2,1,0:T(8,128)(2,1)S(1)}, bf16[1,208,512]{2,1,0:T(8,128)(2,1)S(1)}, u32[]{:S(2)}, u32[]{:S(2)}) collective-permute-start(bf16[1,208,512]{2,1,0:T(8,128)(2,1)S(1)} %get-tuple-element.234), channel_id=1, source_target_pairs={{0,4},{1,3},{2,0},{3,7},{4,8},{5,1},{6,2},{7,11},{8,12},{9,5},{10,... | collective-permute-start | bytes 638984 | tf_op jit(solution)/shard_map/ppermute | solution.py:891
  98.4 7.4 %collective-permute-start.32 = (bf16[1,192,512]{2,1,0:T(8,128)(2,1)S(1)}, bf16[1,192,512]{2,1,0:T(8,128)(2,1)S(1)}, u32[]{:S(2)}, u32[]{:S(2)}) collective-permute-start(bf16[1,192,512]{2,1,0:T(8,128)(2,1)S(1)} %get-tuple-element.238), channel_id=1, source_target_pairs={{0,4},{1,3},{2,0},{3,7},{4,8},{5,1},{6,2},{7,11},{8,12},{9,5},{10,... | collective-permute-start | bytes 589832 | tf_op jit(solution)/shard_map/ppermute | solution.py:891
  101.4 8.2 %collective-permute-start.31 = (bf16[1,208,512]{2,1,0:T(8,128)(2,1)S(1)}, bf16[1,208,512]{2,1,0:T(8,128)(2,1)S(1)}, u32[]{:S(2)}, u32[]{:S(2)}) collective-permute-start(bf16[1,208,512]{2,1,0:T(8,128)(2,1)S(1)} %shard_map.314.refs_0_), channel_id=1, source_target_pairs={{0,2},{1,5},{2,6},{3,1},{4,0},{5,9},{6,10},{7,3},{8,4},{9,13},{10,... | collective-permute-start | bytes 638984 | tf_op jit(solution)/shard_map/ppermute | solution.py:891
  102.3 8.2 %collective-permute-start.30 = (bf16[1,208,512]{2,1,0:T(8,128)(2,1)S(1)}, bf16[1,208,512]{2,1,0:T(8,128)(2,1)S(1)}, u32[]{:S(2)}, u32[]{:S(2)}) collective-permute-start(bf16[1,208,512]{2,1,0:T(8,128)(2,1)S(1)} %shard_map.314.refs_0_), channel_id=1, source_target_pairs={{0,4},{1,3},{2,0},{3,7},{4,8},{5,1},{6,2},{7,11},{8,12},{9,5},{10,... | collective-permute-start | bytes 638984 | tf_op jit(solution)/shard_map/ppermute | solution.py:891
  105.9 6.9 %collective-permute-start.36 = (bf16[1,192,512]{2,1,0:T(8,128)(2,1)S(1)}, bf16[1,192,512]{2,1,0:T(8,128)(2,1)S(1)}, u32[]{:S(2)}, u32[]{:S(2)}) collective-permute-start(bf16[1,192,512]{2,1,0:T(8,128)(2,1)S(1)} %shard_map.315.refs_0_), channel_id=1, source_target_pairs={{0,2},{1,5},{2,6},{3,1},{4,0},{5,9},{6,10},{7,3},{8,4},{9,13},{10,... | collective-permute-start | bytes 589832 | tf_op jit(solution)/shard_map/ppermute | solution.py:891
  107.1 7.8 %collective-permute-start.35 = (bf16[1,192,512]{2,1,0:T(8,128)(2,1)S(1)}, bf16[1,192,512]{2,1,0:T(8,128)(2,1)S(1)}, u32[]{:S(2)}, u32[]{:S(2)}) collective-permute-start(bf16[1,192,512]{2,1,0:T(8,128)(2,1)S(1)} %shard_map.315.refs_0_), channel_id=1, source_target_pairs={{0,4},{1,3},{2,0},{3,7},{4,8},{5,1},{6,2},{7,11},{8,12},{9,5},{10,... | collective-permute-start | bytes 589832 | tf_op jit(solution)/shard_map/ppermute | solution.py:891
  110.5 7.8 %collective-permute-start.34 = (bf16[1,208,512]{2,1,0:T(8,128)(2,1)S(1)}, bf16[1,208,512]{2,1,0:T(8,128)(2,1)S(1)}, u32[]{:S(2)}, u32[]{:S(2)}) collective-permute-start(bf16[1,208,512]{2,1,0:T(8,128)(2,1)S(1)} %get-tuple-element.272.refs_6_), channel_id=1, source_target_pairs={{0,2},{1,5},{2,6},{3,1},{4,0},{5,9},{6,10},{7,3},{8,4},{9,13},{10,... | collective-permute-start | bytes 638984 | tf_op jit(solution)/shard_map/ppermute | solution.py:891
  112.3 8.2 %collective-permute-start.33 = (bf16[1,208,512]{2,1,0:T(8,128)(2,1)S(1)}, bf16[1,208,512]{2,1,0:T(8,128)(2,1)S(1)}, u32[]{:S(2)}, u32[]{:S(2)}) collective-permute-start(bf16[1,208,512]{2,1,0:T(8,128)(2,1)S(1)} %get-tuple-element.267.refs_1_), channel_id=1, source_target_pairs={{0,4},{1,3},{2,0},{3,7},{4,8},{5,1},{6,2},{7,11},{8,12},{9,5},{10,... | collective-permute-start | bytes 638984 | tf_op jit(solution)/shard_map/ppermute | solution.py:891
  114.9 7.7 %collective-permute-start.40 = (bf16[1,192,512]{2,1,0:T(8,128)(2,1)S(1)}, bf16[1,192,512]{2,1,0:T(8,128)(2,1)S(1)}, u32[]{:S(2)}, u32[]{:S(2)}) collective-permute-start(bf16[1,192,512]{2,1,0:T(8,128)(2,1)S(1)} %get-tuple-element.280.refs_6_), channel_id=1, source_target_pairs={{0,2},{1,5},{2,6},{3,1},{4,0},{5,9},{6,10},{7,3},{8,4},{9,13},{10,... | collective-permute-start | bytes 589832 | tf_op jit(solution)/shard_map/ppermute | solution.py:891
  116.5 8.2 %collective-permute-start.39 = (bf16[1,192,512]{2,1,0:T(8,128)(2,1)S(1)}, bf16[1,192,512]{2,1,0:T(8,128)(2,1)S(1)}, u32[]{:S(2)}, u32[]{:S(2)}) collective-permute-start(bf16[1,192,512]{2,1,0:T(8,128)(2,1)S(1)} %get-tuple-element.275.refs_1_), channel_id=1, source_target_pairs={{0,4},{1,3},{2,0},{3,7},{4,8},{5,1},{6,2},{7,11},{8,12},{9,5},{10,... | collective-permute-start | bytes 589832 | tf_op jit(solution)/shard_map/ppermute | solution.py:891
  120.5 8.0 %collective-permute-start.38 = (bf16[1,208,512]{2,1,0:T(8,128)(2,1)S(1)}, bf16[1,208,512]{2,1,0:T(8,128)(2,1)S(1)}, u32[]{:S(2)}, u32[]{:S(2)}) collective-permute-start(bf16[1,208,512]{2,1,0:T(8,128)(2,1)S(1)} %get-tuple-element.271.refs_5_), channel_id=1, source_target_pairs={{0,2},{1,5},{2,6},{3,1},{4,0},{5,9},{6,10},{7,3},{8,4},{9,13},{10,... | collective-permute-start | bytes 638984 | tf_op jit(solution)/shard_map/ppermute | solution.py:891
  122.3 6.2 %collective-permute-start.37 = (bf16[1,208,512]{2,1,0:T(8,128)(2,1)S(1)}, bf16[1,208,512]{2,1,0:T(8,128)(2,1)S(1)}, u32[]{:S(2)}, u32[]{:S(2)}) collective-permute-start(bf16[1,208,512]{2,1,0:T(8,128)(2,1)S(1)} %get-tuple-element.268.refs_2_), channel_id=1, source_target_pairs={{0,4},{1,3},{2,0},{3,7},{4,8},{5,1},{6,2},{7,11},{8,12},{9,5},{10,... | collective-permute-start | bytes 638984 | tf_op jit(solution)/shard_map/ppermute | solution.py:891
  124.7 5.9 %collective-permute-start.43 = (bf16[1,192,512]{2,1,0:T(8,128)(2,1)S(1)}, bf16[1,192,512]{2,1,0:T(8,128)(2,1)S(1)}, u32[]{:S(2)}, u32[]{:S(2)}) collective-permute-start(bf16[1,192,512]{2,1,0:T(8,128)(2,1)S(1)} %get-tuple-element.279.refs_5_), channel_id=1, source_target_pairs={{0,2},{1,5},{2,6},{3,1},{4,0},{5,9},{6,10},{7,3},{8,4},{9,13},{10,... | collective-permute-start | bytes 589832 | tf_op jit(solution)/shard_map/ppermute | solution.py:891
  126.5 5.7 %collective-permute-start.42 = (bf16[1,192,512]{2,1,0:T(8,128)(2,1)S(1)}, bf16[1,192,512]{2,1,0:T(8,128)(2,1)S(1)}, u32[]{:S(2)}, u32[]{:S(2)}) collective-permute-start(bf16[1,192,512]{2,1,0:T(8,128)(2,1)S(1)} %get-tuple-element.276.refs_2_), channel_id=1, source_target_pairs={{0,4},{1,3},{2,0},{3,7},{4,8},{5,1},{6,2},{7,11},{8,12},{9,5},{10,... | collective-permute-start | bytes 589832 | tf_op jit(solution)/shard_map/ppermute | solution.py:891
  132.3 5.3 %collective-permute-start.44 = (bf16[7,208,512]{2,1,0:T(8,128)(2,1)S(1)}, bf16[7,208,512]{2,1,0:T(8,128)(2,1)S(1)}, u32[]{:S(2)}, u32[]{:S(2)}) collective-permute-start(bf16[7,208,512]{2,1,0:T(8,128)(2,1)S(1)} %shard_map.322.refs_0_), channel_id=1, source_target_pairs={{0,1},{1,0},{2,3},{3,2},{4,5},{5,4},{6,7},{7,6},{8,9},{9,8},{10,11... | collective-permute-start | bytes 4472840 | tf_op jit(solution)/shard_map/ppermute | solution.py:872
  132.5 5.1 %collective-permute-start.45 = (bf16[7,192,512]{2,1,0:T(8,128)(2,1)S(1)}, bf16[7,192,512]{2,1,0:T(8,128)(2,1)S(1)}, u32[]{:S(2)}, u32[]{:S(2)}) collective-permute-start(bf16[7,192,512]{2,1,0:T(8,128)(2,1)S(1)} %shard_map.323.refs_1_.refs_4_), channel_id=1, source_target_pairs={{0,1},{1,0},{2,3},{3,2},{4,5},{5,4},{6,7},{7,6},{8,9},{9,8},{10,11... | collective-permute-start | bytes 4128776 | tf_op jit(solution)/shard_map/ppermute | solution.py:872
  133.1 7.4 %collective-permute-start.41 = (bf16[1,208,512]{2,1,0:T(8,128)(2,1)S(1)}, bf16[1,208,512]{2,1,0:T(8,128)(2,1)S(1)}, u32[]{:S(2)}, u32[]{:S(2)}) collective-permute-start(bf16[1,208,512]{2,1,0:T(8,128)(2,1)S(1)} %get-tuple-element.269.refs_3_), channel_id=1, source_target_pairs={{0,4},{1,3},{2,0},{3,7},{4,8},{5,1},{6,2},{7,11},{8,12},{9,5},{10,... | collective-permute-start | bytes 638984 | tf_op jit(solution)/shard_map/ppermute | solution.py:891
  133.3 7.7 %collective-permute-start.46 = (bf16[1,192,512]{2,1,0:T(8,128)(2,1)S(1)}, bf16[1,192,512]{2,1,0:T(8,128)(2,1)S(1)}, u32[]{:S(2)}, u32[]{:S(2)}) collective-permute-start(bf16[1,192,512]{2,1,0:T(8,128)(2,1)S(1)} %get-tuple-element.277.refs_3_), channel_id=1, source_target_pairs={{0,4},{1,3},{2,0},{3,7},{4,8},{5,1},{6,2},{7,11},{8,12},{9,5},{10,... | collective-permute-start | bytes 589832 | tf_op jit(solution)/shard_map/ppermute | solution.py:891
  141.1 1.9 %collective-permute-start.47 = (bf16[1,208,512]{2,1,0:T(8,128)(2,1)S(1)}, bf16[1,208,512]{2,1,0:T(8,128)(2,1)S(1)}, u32[]{:S(2)}, u32[]{:S(2)}) collective-permute-start(bf16[1,208,512]{2,1,0:T(8,128)(2,1)S(1)} %shard_map.328.refs_0_), channel_id=1, source_target_pairs={{0,1},{1,0},{2,3},{3,2},{4,5},{5,4},{6,7},{7,6},{8,9},{9,8},{10,11... | collective-permute-start | bytes 638984 | tf_op jit(solution)/shard_map/ppermute | solution.py:872
  141.5 1.5 %collective-permute-start.48 = (bf16[1,192,512]{2,1,0:T(8,128)(2,1)S(1)}, bf16[1,192,512]{2,1,0:T(8,128)(2,1)S(1)}, u32[]{:S(2)}, u32[]{:S(2)}) collective-permute-start(bf16[1,192,512]{2,1,0:T(8,128)(2,1)S(1)} %shard_map.329.refs_1_.refs_5_), channel_id=1, source_target_pairs={{0,1},{1,0},{2,3},{3,2},{4,5},{5,4},{6,7},{7,6},{8,9},{9,8},{10,11... | collective-permute-start | bytes 589832 | tf_op jit(solution)/shard_map/ppermute | solution.py:872
  (17 other events, 215.0 us)

commit v7 on v6

--- a/solution.py
+++ b/solution.py
@@ -43,7 +43,7 @@
 SPREAD_COST = 0
 ROUND = (("step", 0), ("step", 1))
 ORDER = (
-    (("open", 0), ("open", 1), ("total", 0), ("total", 1)) + ROUND * 7
+    (("open", 0), ("open", 1), ("total", 0), ("total", 1), ("tokens", 0)) + ROUND * 7
     + (("share", 0, 0), ("share", 1, 0), ("spread", ((True, 0),)), ("spread", ((False, 0),))) + ROUND
     + (("share", 0, 1), ("share", 1, 1), ("spread", ((True, 1), (False, 1))))
 )
@@ -153,21 +153,23 @@
     ((ROW, D), BF16),
     ((ROW, D), F32),
     ((ROW, 128), F32),
-    ((ROW, FF), BF16),
-    ((ROW, FF), BF16),
-    ((ROW, D), F32),
-    ((ROW, 128), F32),
     ((8, D), F32),
 )
+MOVED = (((ROW, FF), BF16), ((ROW, FF), BF16), ((ROW, D), F32), ((ROW, 128), F32))
+
+
+def move_kept(*refs):
+    count = len(MOVED)
+    for copy in fetch([*zip(refs[:count], refs[count:-1])], refs[-1]):
+        copy.wait()
 
 
 def encoder_forward(
     size, lens_hbm, labels_hbm, table_hbm, x_hbm, wqkv_hbm, bqkv_hbm, wout_hbm, bout_hbm,
     g1_hbm, s1_hbm, wup_hbm, bup_hbm, wdown_hbm, bdown_hbm, g2_hbm, s2_hbm, wproj_hbm,
-    vec_ref, qkv_hbm, rope_hbm, probs_hbm, mixed_hbm, xh1_hbm, rs1_hbm, act_hbm, slope_hbm,
-    xh2_hbm, rs2_hbm, affine_hbm,
-    qkv_ref, rope_ref, probs_ref, mixed_ref, xh1_ref, rs1_ref, act_ref, slope_ref,
-    xh2_ref, rs2_ref, affine_ref, out_sems,
+    vec_ref, act_ref, slope_ref, xh2_ref, rs2_ref, qkv_hbm, rope_hbm, probs_hbm, mixed_hbm, xh1_hbm,
+    rs1_hbm, affine_hbm,
+    qkv_ref, rope_ref, probs_ref, mixed_ref, xh1_ref, rs1_ref, affine_ref, out_sems,
     table_ref, x_ref, wqkv_ref, bqkv_ref, wout_ref, bout_ref, g1_ref, s1_ref, wup_ref, bup_ref,
     wdown_ref, bdown_ref, g2_ref, s2_ref, wproj_ref, lens_ref, labels_ref, sems,
 ):
@@ -273,14 +275,10 @@
         act = (inner * gate).astype(BF16)
         act_ref[:, cols] = act
         slope_ref[:, cols] = (gate + inner * bell).astype(BF16)
-        keep(act_ref.at[:, cols], act_hbm.at[:, cols])
-        keep(slope_ref.at[:, cols], slope_hbm.at[:, cols])
         branch = branch + mm(act, wdown_ref[cols, :])
     xhat, rstd = norm_rows(branch)
     xh2_ref[...] = xhat
     rs2_ref[...] = jnp.broadcast_to(rstd, (ROW, 128))
-    keep(xh2_ref, xh2_hbm)
-    keep(rs2_ref, rs2_hbm)
     second = xhat * g2_ref[...].astype(F32) + s2_ref[...].astype(F32)
     vec_ref[:ROW, :] = mm(second.astype(BF16), wproj_ref[...]).astype(BF16)
     line = iota((EXT, PROJ), 0)
@@ -362,11 +360,10 @@
 
 
 def matching_stats(
-    size, masks, lanes, scale_ref, lens_hbm, near_ref, far_ref, *refs
+    size, masks, lanes, scale_ref, lens_ref, near_ref, far_ref, *refs
 ):
-    doc_refs = refs[:-8]
-    totals_ref, el_ref, hot_ref, stats_ref, turn_ref, unit_ref, lens_ref, sems = refs[-8:]
-    scalars = fetch(((lens_hbm, lens_ref),), sems)
+    doc_refs = refs[:-6]
+    totals_ref, el_ref, hot_ref, stats_ref, turn_ref, unit_ref = refs[-6:]
     base, near_at = here(size)[2:4]
     span = ROW + EXT
     queries = load_queries(near_ref, far_ref)
@@ -379,8 +376,6 @@
     doc_rows = turn_ref.shape[1] // ROW
     docs = doc_rows * DOCS_ROW
     ids = row_ids(base, masks, doc_rows)
-    for copy in scalars:
-        copy.wait()
     marks = doc_marks(lens_ref, ids, lanes, False)
     totals = jnp.zeros((count, lanes), F32)
     for p in range(doc_rows):
@@ -434,11 +429,9 @@
 
 
 def matching_back(
-    size, masks, lanes, scale_ref, lens_hbm, totals_ref, el_ref, hot_ref, own_ref, over_y, over_x, over_both, unitq_ref, qt_ref, invq_ref, unit_ref, invd_ref, *refs
+    size, masks, lanes, scale_ref, lens_ref, totals_ref, el_ref, hot_ref, own_ref, over_y, over_x, over_both, unitq_ref, qt_ref, invq_ref, unit_ref, invd_ref, *refs
 ):
-    dq_ref, far_ref, keep_ref, send_ref, loss_ref = refs[-10:-5]
-    dot_ref, dt_ref, stats_ref, lens_ref, sems = refs[-5:]
-    scalars = fetch(((lens_hbm, lens_ref),), sems)
+    dq_ref, far_ref, keep_ref, send_ref, loss_ref, dot_ref, dt_ref, stats_ref = refs[-8:]
     _, stream, base, near_at = here(size)[:4]
     total_queries = size * (ROW // QLEN)
     temper = SHARPNESS * LOG2E
@@ -484,8 +477,6 @@
         jnp.where(line == 1, jnp.sum(moved, axis=0, keepdims=True) * (1.0 / total_queries), 0.0),
     )
     loss_ref[...] = loss
-    for copy in scalars:
-        copy.wait()
     marks = doc_marks(lens_ref, ids, lanes, True)
     scale = jnp.exp(jnp.full((8, lanes), scale_ref[0], F32))[:1]
     coeff = (el_ref[...] / sums - hot_ref[...]) * (scale * (1.0 / (QLEN * total_queries)))
@@ -499,7 +490,7 @@
         for p in range(doc_rows):
             block = unit_ref[m, :, p * ROW : (p + 1) * ROW]
             mark = marks[p][m]
-            if len(refs) > 10:
+            if len(refs) > 8:
                 exps = refs[0][m, :, p * ROW : (p + 1) * ROW].astype(F32)
             else:
                 exps = jnp.exp2(mm(unit_q[m], block))
@@ -547,9 +538,13 @@
     invq_ref[...] = columns
 
 
-def two_sums(dq_ref, got_ref, dd_ref, got_dd_ref, sum_dq, sum_dd):
-    sum_dq[...] = (dq_ref[...].astype(F32) + got_ref[...].astype(F32)).astype(BF16)
-    sum_dd[...] = (dd_ref[...].astype(F32) + got_dd_ref[...].astype(F32)).astype(BF16)
+def pick_rows(size, here_ref, there_ref, rows_ref):
+    _, stream, _, _, has_top = here(size)[:5]
+    rows_ref[...] = jnp.where(has_top == stream, here_ref[...], there_ref[...])
+
+
+def add_rows(rows_ref, got_ref, sum_ref):
+    sum_ref[...] = (rows_ref[...].astype(F32) + got_ref[...].astype(F32)).astype(BF16)
 
 
 DIGITS = 10
@@ -663,8 +658,8 @@
 
 def attend_back(
     size, dfirst_ref, gproj_ref, small_ref, loss_ref, tail_keep, tail_send, xh1_ref, rs1_ref, affine_ref, mixed_ref, wout_ref,
-    qkv_ref, probs_ref, rope_ref, x_ref, wqkv_ref,
-    keep_ref, ahead_ref, send_ref, tokens_ref, djoined_ref, rest_ref,
+    qkv_ref, probs_ref, rope_ref, x_ref,
+    keep_ref, ahead_ref, send_ref, dsum_ref, djoined_ref, rest_ref,
 ):
     me, *_, core, place = here(size)
     d_first = dfirst_ref[...]
@@ -709,7 +704,7 @@
         djoined_ref[:, D + g * 128 : D + (g + 1) * 128] = unrotate(d_k)
         djoined_ref[:, 2 * D + g * 128 : 2 * D + (g + 1) * 128] = d_v.astype(BF16)
     x = x_ref[...]
-    tokens = d_sum
+    dsum_ref[...] = d_sum
     rest_ref[4 * D :, :] = jnp.zeros((8 * 2 * RING, D), F32)
     smalls = []
     for c in range(3):
@@ -717,8 +712,6 @@
         d_part = djoined_ref[:, cols]
         rest_ref[c * D : (c + 1) * D, :] = mm_tn(x, d_part)
         smalls.append(col_sum(d_part.astype(F32)))
-        tokens = tokens + mm_nt(d_part, wqkv_ref[:, cols])
-    tokens_ref[...] = tokens
     smalls += [bias_out, gain_grad, shift_grad] + [small_ref[k : k + 1, :] for k in range(7)]
     counted = jnp.where((me & 3) == 0, 1.0, 0.0)
     lines = [digits_of(loss_ref[k : k + 1, :]) * counted for k in range(2)]
@@ -744,6 +737,14 @@
             parts.append(rest_ref[pl.ds(pl.multiple_of(4 * D + block * 8, 8), 8), :])
             ref[index, : REST // 16, :] = jnp.concatenate(parts, axis=0).astype(BF16)
             ref[index, REST // 16 :, :] = tail_ref[k]
+
+
+def tokens_back(dsum_ref, djoined_ref, wqkv_ref, tokens_ref):
+    tokens = dsum_ref[...]
+    for c in range(3):
+        cols = slice(c * D, (c + 1) * D)
+        tokens = tokens + mm_nt(djoined_ref[:, cols], wqkv_ref[:, cols])
+    tokens_ref[...] = tokens
 
 
 def spread(size, jobs, last, *refs):
@@ -1010,7 +1011,7 @@
     lens = doc_lengths.T
     scale = log_scale.reshape(1)
 
-    vec, qkv, rope, probs, mixed, xh1, rs1, act, slope, xh2, rs2, affine = call(
+    vec, *moved, qkv, rope, probs, mixed, xh1, rs1, affine = call(
         partial(encoder_forward, size),
         (
             lens, labels, jnp.asarray(rope_table()), tokens[0], qkv_weight[0], qkv_bias,
@@ -1018,9 +1019,11 @@
             down_weight[0], down_bias, second_gain, second_shift, proj_weight[0],
         ),
         [HBM] * 17,
-        [shape_of((ROW + EXT, PROJ), BF16)] + [pltpu.HBM(*kind) for kind in KEPT],
+        [shape_of((ROW + EXT, PROJ), BF16)]
+        + [shape_of(*kind) for kind in MOVED]
+        + [pltpu.HBM(*kind) for kind in KEPT],
         [pltpu.VMEM(*kind) for kind in KEPT]
-        + [pltpu.SemaphoreType.DMA((len(KEPT) + 6,))]
+        + [pltpu.SemaphoreType.DMA((len(KEPT),))]
         + [
             pltpu.VMEM(shape, BF16)
             for shape in (
@@ -1034,16 +1037,34 @@
             pltpu.SemaphoreType.DMA((17,)),
         ],
         room=40,
-        out_specs=[VMEM] + [HBM] * len(KEPT),
+        out_specs=[VMEM] * (1 + len(MOVED)) + [HBM] * len(KEPT),
+    )
+    act, slope, xh2, rs2 = call(
+        move_kept,
+        moved,
+        [VMEM] * len(MOVED),
+        [pltpu.HBM(*kind) for kind in MOVED],
+        [pltpu.SemaphoreType.DMA((len(MOVED),))],
+        room=8,
+        out_specs=[HBM] * len(MOVED),
+        cost=STEP_COST,
     )
 
     every, other_y = range(size), near_masks[1]
-    other = swapped(vec, 1, "stream")
+    other, _ = lax.optimization_barrier((swapped(vec, 1, "stream"), rs2))
     near = jnp.where(is_query, vec, other)
     rows = jnp.where(is_query, other, vec)[:ROW]
     moved = swapped(rows, top_mask)
-    near = jnp.concatenate([near, swapped(near, other_y)], axis=0)
-    rows = jnp.where(has_top == is_query, moved, rows)
+    (rows,) = call(
+        partial(pick_rows, size),
+        (rows, moved),
+        [VMEM] * 2,
+        [shape_of((ROW, PROJ), BF16)],
+        room=8,
+        cost=STEP_COST,
+    )
+    got_y, _ = lax.optimization_barrier((swapped(near, other_y), rows))
+    near = jnp.concatenate([near, got_y], axis=0)
     far = swapped(near, near_masks[0])
     pieces = []
     for k, mask in enumerate(doc_masks):
@@ -1058,18 +1079,17 @@
     tokens_q = 4 * ROW
     lanes = -(-3 * doc_rows * DOCS_ROW // 128) * 128
     room = 20 if doc_rows <= 4 else 56
-    scalars = [pltpu.SMEM(lens.shape, jnp.int32), pltpu.SemaphoreType.DMA((1,))]
     totals, el, hot, stats = call(
         partial(matching_stats, size, doc_masks, lanes),
         (scale, lens, near, far, *pieces),
-        [SMEM, HBM] + [VMEM] * (2 + len(pieces)),
+        [SMEM] * 2 + [VMEM] * (2 + len(pieces)),
         [
             shape_of((tokens_q, lanes)),
             shape_of((tokens_q // QLEN, lanes)),
             shape_of((tokens_q // QLEN, lanes)),
             shape_of((tokens_q // QLEN, 128)),
         ],
-        [pltpu.VMEM((PROJ, tokens_d), F32), pltpu.VMEM((3, PROJ, tokens_d), BF16), *scalars],
+        [pltpu.VMEM((PROJ, tokens_d), F32), pltpu.VMEM((3, PROJ, tokens_d), BF16)],
         room=room,
     )
     small_enough = doc_rows <= 4
@@ -1096,7 +1116,7 @@
     dq, dq_send, keep, send, loss = call(
         partial(matching_back, size, doc_masks, lanes),
         (scale, lens, totals, el, hot, stats, over_y, over_x, over_both, *ready),
-        [SMEM, HBM] + [VMEM] * (7 + len(ready)),
+        [SMEM] * 2 + [VMEM] * (7 + len(ready)),
         [shape_of((tokens_q // 2, PROJ), BF16)] * 2
         + [shape_of((tokens_d // 2, PROJ), BF16)] * 2
         + [shape_of((8, 128))],
@@ -1104,7 +1124,6 @@
             pltpu.VMEM((tokens_q, PROJ), F32),
             pltpu.VMEM((3, PROJ, tokens_d), F32),
             pltpu.VMEM((tokens_q // QLEN, 128), F32),
-            *scalars,
         ],
         room=room,
     )
@@ -1113,15 +1132,17 @@
         total, half = added(keep, swapped(send, mask)), keep.shape[0] // 2
         keep, send = total[:half], total[half:]
     got_dd = swapped(send, doc_masks[0])
-    dq, dd = call(
-        two_sums,
-        (dq, got_dq, keep, got_dd),
-        [VMEM] * 4,
-        [shape_of((2 * ROW, PROJ), BF16), shape_of((ROW, PROJ), BF16)],
-        room=8,
-    )
-    dq = added(dq[:ROW], swapped(dq[ROW:], other_y))
-    dd = added(dd, swapped(dd, top_mask))
+    def summed(rows, got, after=None):
+        if after is not None:
+            got, _ = lax.optimization_barrier((got, after))
+        return call(
+            add_rows, (rows, got), [VMEM] * 2, [shape_of(rows.shape, BF16)], room=8, cost=STEP_COST
+        )[0]
+
+    dq = summed(dq, got_dq)
+    dd = summed(keep, got_dd, dq)
+    dd = summed(dd, swapped(dd, top_mask))
+    dq = summed(dq[:ROW], swapped(dq[ROW:], other_y), dd)
     got = swapped(jnp.where(is_query, dd, dq), 1, "stream")
 
     one_keep, one_send, tail_keep, tail_send, d_first, gproj, small = call(
@@ -1141,28 +1162,37 @@
         ],
         room=24,
     )
-    two_keep, two_ahead, two_send, tokens_grad = call(
+    two_keep, two_ahead, two_send, d_sum, d_joined = call(
         partial(attend_back, size),
         (
             d_first, gproj, small, loss, tail_keep, tail_send, xh1, rs1, affine, mixed, out_weight[0], qkv, probs, rope,
-            tokens[0], qkv_weight[0],
+            tokens[0],
         ),
-        [VMEM] * 6 + [HELD] * 10,
+        [VMEM] * 6 + [HELD] * 9,
         [shape_of((count, SECOND, D), BF16) for count in (RING, len(AHEAD), len(LATER))]
-        + [shape_of((ROW, D))],
-        [
-            pltpu.VMEM((ROW, 3 * D), BF16),
-            pltpu.VMEM((4 * D + 16 * RING, D), F32),
-        ],
+        + [shape_of((ROW, D)), shape_of((ROW, 3 * D), BF16)],
+        [pltpu.VMEM((4 * D + 16 * RING, D), F32)],
         room=24,
     )
     one, two = [
         Summed(keep, sends, others)
         for keep, *sends in ((one_keep, one_send), (two_keep, two_ahead, two_send))
     ]
-    token, outs = tokens_grad, ()
+    token, outs = d_sum, ()
     for event in ORDER:
         kind, k, *group = event
+        if kind == "tokens":
+            d_sum, _ = lax.optimization_barrier((d_sum, token))
+            (tokens_grad,) = call(
+                tokens_back,
+                (d_sum, d_joined, qkv_weight[0]),
+                [VMEM] * 3,
+                [shape_of((ROW, D))],
+                room=8,
+                cost=STEP_COST,
+            )
+            token = tokens_grad
+            continue
         if kind == "spread":
             jobs = event[1]
             halves = [

time: 145 us -> 142 us (0.979)
  waiting for transfers between devices: 53.8 us -> 49.8 us
    ppermute x28, waiting for transfers between devices: 34.7 us -> 29.8 us  [ring_swap(): return lax.ppermute(value, 'dp', pairs)]
    ppermute x20, starting transfers between devices: 21.8 us -> 17.9 us  [swapped(): return lax.ppermute(value, axis, [(k, k ^ mask) for k in range(size)])]
    ppermute x28, starting transfers between devices: 29.1 us -> 30.7 us  [ring_swap(): return lax.ppermute(value, 'dp', pairs)]
    pallas_call x34 -> x40, Pallas kernels: 36.7 us -> 37.5 us  [call(): pl.pallas_call(kernel, out_shape=outs, in_specs=specs, out_specs=out_spec...]
  transfers between devices with their start and end apart: 49 -> 49, of which waited for: 35 -> 36; matrix products, arithmetic and copies ran while one was open for 0% -> 0% of each run, Pallas kernels for 9% -> 11%
where the time goes in v7:
time: 142 us
  starting transfers between devices  51 us (36%)
  waiting for transfers between devices  49.8 us (35%)
  Pallas kernels  37.5 us (26%)
  between operations  2.01 us (1%)
    pallas_call x40, Pallas kernels, call(): pl.pallas_call(kernel, out_shape=outs, in_specs=specs, out_specs=out_spec...  37.5 us
    ppermute x28, starting transfers between devices, ring_swap(): return lax.ppermute(value, 'dp', pairs)  30.7 us
    ppermute x28, waiting for transfers between devices, ring_swap(): return lax.ppermute(value, 'dp', pairs)  29.8 us
    ppermute x20, waiting for transfers between devices, swapped(): return lax.ppermute(value, axis, [(k, k ^ mask) for k in range(size)])  19.9 us
    ppermute x20, starting transfers between devices, swapped(): return lax.ppermute(value, axis, [(k, k ^ mask) for k in range(size)])  17.9 us
  transfers between devices with their start and end apart: 49, of which 36 were waited for; matrix products, arithmetic and copies ran while one was open for 0% of the time, Pallas kernels for 11%

profile of v7, /device:TPU:0, one launch (start us, length us, event | category | flops | bytes accessed | tf_op | source)
XLA Modules:
  0.0 141.5 jit_solution(5190896244119945634)
XLA Ops:
  0.7 7.5 %shard_map.297 = (bf16[272,128]{1,0:T(8,128)(2,1)S(1)}, bf16[256,2048]{1,0:T(8,128)(2,1)S(1)}, bf16[256,2048]{1,0:T(8,128)(2,1)S(1)}, f32[256,512]{1,0:T(8,128)S...) custom-call(s32[5,16]{1,0:T(8,128)} %bitcast.28, ...), custom_call_target="tpu_custom_call" | custom-call | flops 100000000 | bytes 10000000 | tf_op jit(solution)/shard_map/pallas_call | solution.py:857
  8.1 3.0 %collective-permute-start = (bf16[272,128]{1,0:T(8,128)(2,1)S(1)}, bf16[272,128]{1,0:T(8,128)(2,1)S(1)}, u32[]{:S(2)}, u32[]{:S(2)}) collective-permute-start(bf16[272,128]{1,0:T(8,128)(2,1)S(1)} %get-tuple-element.175), channel_id=1, source_target_pairs={{0,16},{16,0},{1,17},{17,1},{2,18},{18,2},{3,19},{19,3},{4,20},{20... | collective-permute-start | bytes 208904 | tf_op jit(solution)/shard_map/ppermute | solution.py:873
  11.1 1.5 %shard_map.298 = (bf16[256,2048]{1,0:T(8,128)(2,1)}, bf16[256,2048]{1,0:T(8,128)(2,1)}, f32[256,512]{1,0:T(8,128)}, f32[256,128]{1,0:T(8,128)}) custom-call(bf16[256,2048]{1,0:T(8,128)(2,1)S(1)} %get-tuple-element.176.refs_0_, bf16[256,2048]{1,0:T(8,128)(2,1)S(1)} %get-tuple-element.177.refs_1_, f32[256,512]{1,0:T(8,128)S(1)} %get-tuple-element.178.refs_2_, ...), custom_call_target="tpu_custom_call" | custom-call | flops 300000000 | bytes 30000000 | tf_op jit(solution)/shard_map/pallas_call | solution.py:857
  13.4 3.2 %collective-permute-start.2 = (bf16[256,128]{1,0:T(8,128)(2,1)S(1)}, bf16[256,128]{1,0:T(8,128)(2,1)S(1)}, u32[]{:S(2)}, u32[]{:S(2)}) collective-permute-start(bf16[256,128]{1,0:T(8,128)(2,1)S(1)} %slice_select_fusion.here_ref), channel_id=1, source_target_pairs={{0,8},{1,9},{2,10},{3,11},{4,12},{5,13},{6,14},{7,15},{8,0},{9,1},... | collective-permute-start | bytes 196616 | tf_op jit(solution)/shard_map/ppermute | solution.py:873
  16.6 1.6 %collective-permute-start.1 = (bf16[272,128]{1,0:T(8,128)(2,1)S(1)}, bf16[272,128]{1,0:T(8,128)(2,1)S(1)}, u32[]{:S(2)}, u32[]{:S(2)}) collective-permute-start(bf16[272,128]{1,0:T(8,128)(2,1)S(1)} %broadcast_select_fusion), channel_id=1, source_target_pairs={{0,2},{1,3},{2,0},{3,1},{4,6},{5,7},{6,4},{7,5},{8,10},{9,11},{10,... | collective-permute-start | bytes 208904 | tf_op jit(solution)/shard_map/ppermute | solution.py:873
  18.9 2.1 %collective-permute-done.1 = bf16[272,128]{1,0:T(8,128)(2,1)S(1)} collective-permute-done((bf16[272,128]{1,0:T(8,128)(2,1)S(1)}, bf16[272,128]{1,0:T(8,128)(2,1)S(1)}, u32[]{:S(2)}, u32[]{:S(2)}) %collective-permute-start.1) | collective-permute-done | bytes 69664 | tf_op jit(solution)/shard_map/ppermute | solution.py:873
  21.1 1.6 %collective-permute-start.4 = (bf16[256,128]{1,0:T(8,128)(2,1)S(1)}, bf16[256,128]{1,0:T(8,128)(2,1)S(1)}, u32[]{:S(2)}, u32[]{:S(2)}) collective-permute-start(bf16[256,128]{1,0:T(8,128)(2,1)S(1)} %shard_map.299.refs_0_), channel_id=1, source_target_pairs={{0,4},{1,5},{2,6},{3,7},{4,0},{5,1},{6,2},{7,3},{8,12},{9,13},{10,... | collective-permute-start | bytes 196616 | tf_op jit(solution)/shard_map/ppermute | solution.py:873
  23.4 2.2 %collective-permute-done.4.refs_1_ = bf16[256,128]{1,0:T(8,128)(2,1)S(1)} collective-permute-done((bf16[256,128]{1,0:T(8,128)(2,1)S(1)}, bf16[256,128]{1,0:T(8,128)(2,1)S(1)}, u32[]{:S(2)}, u32[]{:S(2)}) %collective-permute-start.4) | collective-permute-done | bytes 65568 | tf_op jit(solution)/shard_map/ppermute | solution.py:873
  25.6 2.8 %shard_map.300 = (f32[1024,128]{1,0:T(8,128)S(1)}, f32[32,128]{1,0:T(8,128)S(1)}, f32[32,128]{1,0:T(8,128)S(1)}, f32[32,128]{1,0:T(8,128)S(1)}) custom-call(f32[1]{0:T(128)} %bitcast.16.scale_ref, s32[5,16]{1,0:T(8,128)S(1)} %bitcast.29, bf16[544,128]{1,0:T(8,128)(2,1)S(1)} %pad_maximum_fusion.near_ref, bf16[544,128]{1,0:T(8,128)(2,1)S(1)} %collective-permute-done.3.far_ref, ...), custom_call_target="tpu_custom_call" | custom-call | flops 100000000 | bytes 10000000 | tf_op jit(solution)/shard_map/pallas_call | solution.py:857
  29.7 2.5 %collective-permute-start.8 = (f32[32,128]{1,0:T(8,128)S(1)}, f32[32,128]{1,0:T(8,128)S(1)}, u32[]{:S(2)}, u32[]{:S(2)}) collective-permute-start(f32[32,128]{1,0:T(8,128)S(1)} %add.3.own_ref), channel_id=1, source_target_pairs={{0,18},{1,19},{2,16},{3,17},{4,22},{5,23},{6,20},{7,21},{8,26},{9,... | collective-permute-start | bytes 49160 | tf_op jit(solution)/shard_map/ppermute | solution.py:1115
  33.1 1.5 %shard_map.301 = (bf16[3,1024,128]{2,1,0:T(8,128)(2,1)S(1)}, bf16[3,128,1024]{2,1,0:T(8,128)(2,1)S(1)}, f32[1024,128]{1,0:T(8,128)S(1)}, bf16[3,128,512]{2,1,0:T...) custom-call(bf16[544,128]{1,0:T(8,128)(2,1)S(1)} %pad_maximum_fusion.near_ref, ...), custom_call_target="tpu_custom_call" | custom-call | flops 100000000 | bytes 10000000 | tf_op jit(solution)/shard_map/pallas_call | solution.py:857
  36.4 3.6 %shard_map.302 = (bf16[512,128]{1,0:T(8,128)(2,1)S(1)}, bf16[512,128]{1,0:T(8,128)(2,1)S(1)}, bf16[256,128]{1,0:T(8,128)(2,1)S(1)}, bf16[256,128]{1,0:T(8,128)(2,1)S(1)}, f32[8,128]{1,0:T(8,128)S(1)}) custom-call(f32[1]{0:T(128)} %bitcast.17.scale_ref, s32[5,16]{1,0:T(8,128)S(1)} %bitcast.30, f32[1024,128]{1,0:T(8,128)S(1)} %get-tuple-element.183.totals_ref, ...), custom_call_target="tpu_custom_call" | custom-call | flops 100000000 | bytes 10000000 | tf_op jit(solution)/shard_map/pallas_call | solution.py:857
  40.2 1.6 %collective-permute-start.11 = (bf16[256,128]{1,0:T(8,128)(2,1)S(1)}, bf16[256,128]{1,0:T(8,128)(2,1)S(1)}, u32[]{:S(2)}, u32[]{:S(2)}) collective-permute-start(bf16[256,128]{1,0:T(8,128)(2,1)S(1)} %get-tuple-element.196), channel_id=1, source_target_pairs={{0,4},{1,5},{2,6},{3,7},{4,0},{5,1},{6,2},{7,3},{8,12},{9,13},{10,... | collective-permute-start | bytes 196616 | tf_op jit(solution)/shard_map/ppermute | solution.py:873
  41.9 2.8 %collective-permute-done.11.got_ref = bf16[256,128]{1,0:T(8,128)(2,1)S(1)} collective-permute-done((bf16[256,128]{1,0:T(8,128)(2,1)S(1)}, bf16[256,128]{1,0:T(8,128)(2,1)S(1)}, u32[]{:S(2)}, u32[]{:S(2)}) %collective-permute-start.11) | collective-permute-done | bytes 65568 | tf_op jit(solution)/shard_map/ppermute | solution.py:873
  44.8 1.3 collective-permute-start.12
  46.7 3.8 %collective-permute-done.12.got_ref = bf16[256,128]{1,0:T(8,128)(2,1)S(1)} collective-permute-done((bf16[256,128]{1,0:T(8,128)(2,1)S(1)}, bf16[256,128]{1,0:T(8,128)(2,1)S(1)}, u32[]{:S(2)}, u32[]{:S(2)}) %collective-permute-start.12) | collective-permute-done | bytes 65568 | tf_op jit(solution)/shard_map/ppermute | solution.py:873
  50.5 1.6 %collective-permute-start.13 = (bf16[256,128]{1,0:T(8,128)(2,1)S(1)}, bf16[256,128]{1,0:T(8,128)(2,1)S(1)}, u32[]{:S(2)}, u32[]{:S(2)}) collective-permute-start(bf16[256,128]{1,0:T(8,128)(2,1)S(1)} %broadcast_select_fusion.1), channel_id=1, source_target_pairs={{0,16},{16,0},{1,17},{17,1},{2,18},{18,2},{3,19},{19,3},{4,20},{20... | collective-permute-start | bytes 196616 | tf_op jit(solution)/shard_map/ppermute | solution.py:873
  52.1 2.8 %collective-permute-done.13.got_ref = bf16[256,128]{1,0:T(8,128)(2,1)S(1)} collective-permute-done((bf16[256,128]{1,0:T(8,128)(2,1)S(1)}, bf16[256,128]{1,0:T(8,128)(2,1)S(1)}, u32[]{:S(2)}, u32[]{:S(2)}) %collective-permute-start.13) | collective-permute-done | bytes 65568 | tf_op jit(solution)/shard_map/ppermute | solution.py:873
  55.0 5.8 %shard_map.307 = (bf16[8,208,512]{2,1,0:T(8,128)(2,1)S(1)}, bf16[8,208,512]{2,1,0:T(8,128)(2,1)S(1)}, bf16[8,48,512]{2,1,0:T(8,128)(2,1)S(1)}, bf16[8,48,512]{2,...) custom-call(bf16[256,128]{1,0:T(8,128)(2,1)S(1)} %shard_map.306.dq_ref, ...), custom_call_target="tpu_custom_call" | custom-call | flops 100000000 | bytes 10000000 | tf_op jit(solution)/shard_map/pallas_call | solution.py:857
  61.0 3.8 %shard_map.308 = (bf16[8,192,512]{2,1,0:T(8,128)(2,1)S(1)}, bf16[2,192,512]{2,1,0:T(8,128)(2,1)S(1)}, bf16[6,192,512]{2,1,0:T(8,128)(2,1)S(1)}, f32[256,512]{1,0:T(8,128)S(1)}, bf16[256,1536]{1,0:T(8,128)(2,1)S(1)}) custom-call(f32[256,512]{1,0:T(8,128)S(1)} %get-tuple-element.206.dfirst_ref, f32[512,128]{1,0:T(8,128)S(1)} %get-tuple-element.207.gproj_ref, ...), custom_call_target="tpu_custom_call" | custom-call | flops 100000000 | bytes 10000000 | tf_op jit(solution)/shard_map/pallas_call | solution.py:857
  65.5 1.8 %collective-permute-start.15 = (bf16[1,208,512]{2,1,0:T(8,128)(2,1)S(1)}, bf16[1,208,512]{2,1,0:T(8,128)(2,1)S(1)}, u32[]{:S(2)}, u32[]{:S(2)}) collective-permute-start(bf16[1,208,512]{2,1,0:T(8,128)(2,1)S(1)} %get-tuple-element.220), channel_id=1, source_target_pairs={{0,4},{1,3},{2,0},{3,7},{4,8},{5,1},{6,2},{7,11},{8,12},{9,5},{10,... | collective-permute-start | bytes 638984 | tf_op jit(solution)/shard_map/ppermute | solution.py:892
  69.1 1.5 %collective-permute-start.21 = (bf16[1,192,512]{2,1,0:T(8,128)(2,1)S(1)}, bf16[1,192,512]{2,1,0:T(8,128)(2,1)S(1)}, u32[]{:S(2)}, u32[]{:S(2)}) collective-permute-start(bf16[1,192,512]{2,1,0:T(8,128)(2,1)S(1)} %get-tuple-element.236), channel_id=1, source_target_pairs={{0,4},{1,3},{2,0},{3,7},{4,8},{5,1},{6,2},{7,11},{8,12},{9,5},{10,... | collective-permute-start | bytes 589832 | tf_op jit(solution)/shard_map/ppermute | solution.py:892
  72.3 1.4 shard_map.313
  74.4 1.8 %collective-permute-start.19 = (bf16[1,208,512]{2,1,0:T(8,128)(2,1)S(1)}, bf16[1,208,512]{2,1,0:T(8,128)(2,1)S(1)}, u32[]{:S(2)}, u32[]{:S(2)}) collective-permute-start(bf16[1,208,512]{2,1,0:T(8,128)(2,1)S(1)} %get-tuple-element.234), channel_id=1, source_target_pairs={{0,4},{1,3},{2,0},{3,7},{4,8},{5,1},{6,2},{7,11},{8,12},{9,5},{10,... | collective-permute-start | bytes 638984 | tf_op jit(solution)/shard_map/ppermute | solution.py:892
  76.2 1.8 %collective-permute-done.21.refs_0_ = bf16[1,192,512]{2,1,0:T(8,128)(2,1)S(1)} collective-permute-done((bf16[1,192,512]{2,1,0:T(8,128)(2,1)S(1)}, bf16[1,192,512]{2,1,0:T(8,128)(2,1)S(1)}, u32[]{:S(2)}, u32[]{:S(2)}) %collective-permute-start.21) | collective-permute-done | bytes 196640 | tf_op jit(solution)/shard_map/ppermute | solution.py:892
  78.8 1.3 collective-permute-start.25
  80.1 2.0 %collective-permute-done.20.refs_1_ = bf16[1,208,512]{2,1,0:T(8,128)(2,1)S(1)} collective-permute-done((bf16[1,208,512]{2,1,0:T(8,128)(2,1)S(1)}, bf16[1,208,512]{2,1,0:T(8,128)(2,1)S(1)}, u32[]{:S(2)}, u32[]{:S(2)}) %collective-permute-start.20) | collective-permute-done | bytes 213024 | tf_op jit(solution)/shard_map/ppermute | solution.py:892
  82.6 2.1 %collective-permute-start.24 = (bf16[1,208,512]{2,1,0:T(8,128)(2,1)S(1)}, bf16[1,208,512]{2,1,0:T(8,128)(2,1)S(1)}, u32[]{:S(2)}, u32[]{:S(2)}) collective-permute-start(bf16[1,208,512]{2,1,0:T(8,128)(2,1)S(1)} %get-tuple-element.243), channel_id=1, source_target_pairs={{0,2},{1,5},{2,6},{3,1},{4,0},{5,9},{6,10},{7,3},{8,4},{9,13},{10,... | collective-permute-start | bytes 638984 | tf_op jit(solution)/shard_map/ppermute | solution.py:892
  84.7 1.6 %collective-permute-done.26.refs_1_ = bf16[1,192,512]{2,1,0:T(8,128)(2,1)S(1)} collective-permute-done((bf16[1,192,512]{2,1,0:T(8,128)(2,1)S(1)}, bf16[1,192,512]{2,1,0:T(8,128)(2,1)S(1)}, u32[]{:S(2)}, u32[]{:S(2)}) %collective-permute-start.26) | collective-permute-done | bytes 196640 | tf_op jit(solution)/shard_map/ppermute | solution.py:892
  86.8 2.1 %collective-permute-start.29 = (bf16[1,192,512]{2,1,0:T(8,128)(2,1)S(1)}, bf16[1,192,512]{2,1,0:T(8,128)(2,1)S(1)}, u32[]{:S(2)}, u32[]{:S(2)}) collective-permute-start(bf16[1,192,512]{2,1,0:T(8,128)(2,1)S(1)} %get-tuple-element.251), channel_id=1, source_target_pairs={{0,2},{1,5},{2,6},{3,1},{4,0},{5,9},{6,10},{7,3},{8,4},{9,13},{10,... | collective-permute-start | bytes 589832 | tf_op jit(solution)/shard_map/ppermute | solution.py:892
  88.9 2.0 %collective-permute-done.24.refs_1_ = bf16[1,208,512]{2,1,0:T(8,128)(2,1)S(1)} collective-permute-done((bf16[1,208,512]{2,1,0:T(8,128)(2,1)S(1)}, bf16[1,208,512]{2,1,0:T(8,128)(2,1)S(1)}, u32[]{:S(2)}, u32[]{:S(2)}) %collective-permute-start.24) | collective-permute-done | bytes 213024 | tf_op jit(solution)/shard_map/ppermute | solution.py:892
  90.9 1.7 %collective-permute-done.23.refs_0_ = bf16[1,208,512]{2,1,0:T(8,128)(2,1)S(1)} collective-permute-done((bf16[1,208,512]{2,1,0:T(8,128)(2,1)S(1)}, bf16[1,208,512]{2,1,0:T(8,128)(2,1)S(1)}, u32[]{:S(2)}, u32[]{:S(2)}) %collective-permute-start.23) | collective-permute-done | bytes 213024 | tf_op jit(solution)/shard_map/ppermute | solution.py:892
  93.3 1.8 %collective-permute-done.29.refs_1_ = bf16[1,192,512]{2,1,0:T(8,128)(2,1)S(1)} collective-permute-done((bf16[1,192,512]{2,1,0:T(8,128)(2,1)S(1)}, bf16[1,192,512]{2,1,0:T(8,128)(2,1)S(1)}, u32[]{:S(2)}, u32[]{:S(2)}) %collective-permute-start.29) | collective-permute-done | bytes 196640 | tf_op jit(solution)/shard_map/ppermute | solution.py:892
  95.3 2.1 %collective-permute-start.32 = (bf16[1,192,512]{2,1,0:T(8,128)(2,1)S(1)}, bf16[1,192,512]{2,1,0:T(8,128)(2,1)S(1)}, u32[]{:S(2)}, u32[]{:S(2)}) collective-permute-start(bf16[1,192,512]{2,1,0:T(8,128)(2,1)S(1)} %get-tuple-element.254), channel_id=1, source_target_pairs={{0,4},{1,3},{2,0},{3,7},{4,8},{5,1},{6,2},{7,11},{8,12},{9,5},{10,... | collective-permute-start | bytes 589832 | tf_op jit(solution)/shard_map/ppermute | solution.py:892
  99.5 1.3 collective-permute-start.30
  101.9 2.9 %collective-permute-start.36 = (bf16[1,192,512]{2,1,0:T(8,128)(2,1)S(1)}, bf16[1,192,512]{2,1,0:T(8,128)(2,1)S(1)}, u32[]{:S(2)}, u32[]{:S(2)}) collective-permute-start(bf16[1,192,512]{2,1,0:T(8,128)(2,1)S(1)} %shard_map.321.refs_0_), channel_id=1, source_target_pairs={{0,2},{1,5},{2,6},{3,1},{4,0},{5,9},{6,10},{7,3},{8,4},{9,13},{10,... | collective-permute-start | bytes 589832 | tf_op jit(solution)/shard_map/ppermute | solution.py:892
  104.8 2.0 %collective-permute-done.31.refs_1_ = bf16[1,208,512]{2,1,0:T(8,128)(2,1)S(1)} collective-permute-done((bf16[1,208,512]{2,1,0:T(8,128)(2,1)S(1)}, bf16[1,208,512]{2,1,0:T(8,128)(2,1)S(1)}, u32[]{:S(2)}, u32[]{:S(2)}) %collective-permute-start.31) | collective-permute-done | bytes 213024 | tf_op jit(solution)/shard_map/ppermute | solution.py:892
  107.7 1.9 %collective-permute-start.34 = (bf16[1,208,512]{2,1,0:T(8,128)(2,1)S(1)}, bf16[1,208,512]{2,1,0:T(8,128)(2,1)S(1)}, u32[]{:S(2)}, u32[]{:S(2)}) collective-permute-start(bf16[1,208,512]{2,1,0:T(8,128)(2,1)S(1)} %get-tuple-element.288.refs_6_), channel_id=1, source_target_pairs={{0,2},{1,5},{2,6},{3,1},{4,0},{5,9},{6,10},{7,3},{8,4},{9,13},{10,... | collective-permute-start | bytes 638984 | tf_op jit(solution)/shard_map/ppermute | solution.py:892
  111.0 1.5 %collective-permute-done.35.refs_0_ = bf16[1,192,512]{2,1,0:T(8,128)(2,1)S(1)} collective-permute-done((bf16[1,192,512]{2,1,0:T(8,128)(2,1)S(1)}, bf16[1,192,512]{2,1,0:T(8,128)(2,1)S(1)}, u32[]{:S(2)}, u32[]{:S(2)}) %collective-permute-start.35) | collective-permute-done | bytes 196640 | tf_op jit(solution)/shard_map/ppermute | solution.py:892
  114.7 1.3 collective-permute-done.34.refs_1_
  117.2 1.6 %collective-permute-start.38 = (bf16[1,208,512]{2,1,0:T(8,128)(2,1)S(1)}, bf16[1,208,512]{2,1,0:T(8,128)(2,1)S(1)}, u32[]{:S(2)}, u32[]{:S(2)}) collective-permute-start(bf16[1,208,512]{2,1,0:T(8,128)(2,1)S(1)} %get-tuple-element.287.refs_5_), channel_id=1, source_target_pairs={{0,2},{1,5},{2,6},{3,1},{4,0},{5,9},{6,10},{7,3},{8,4},{9,13},{10,... | collective-permute-start | bytes 638984 | tf_op jit(solution)/shard_map/ppermute | solution.py:892
  121.5 1.5 %collective-permute-start.43 = (bf16[1,192,512]{2,1,0:T(8,128)(2,1)S(1)}, bf16[1,192,512]{2,1,0:T(8,128)(2,1)S(1)}, u32[]{:S(2)}, u32[]{:S(2)}) collective-permute-start(bf16[1,192,512]{2,1,0:T(8,128)(2,1)S(1)} %get-tuple-element.295.refs_5_), channel_id=1, source_target_pairs={{0,2},{1,5},{2,6},{3,1},{4,0},{5,9},{6,10},{7,3},{8,4},{9,13},{10,... | collective-permute-start | bytes 589832 | tf_op jit(solution)/shard_map/ppermute | solution.py:892
  123.6 1.8 %collective-permute-done.38.refs_1_ = bf16[1,208,512]{2,1,0:T(8,128)(2,1)S(1)} collective-permute-done((bf16[1,208,512]{2,1,0:T(8,128)(2,1)S(1)}, bf16[1,208,512]{2,1,0:T(8,128)(2,1)S(1)}, u32[]{:S(2)}, u32[]{:S(2)}) %collective-permute-start.38) | collective-permute-done | bytes 213024 | tf_op jit(solution)/shard_map/ppermute | solution.py:892
  125.7 2.1 %collective-permute-done.43.refs_1_ = bf16[1,192,512]{2,1,0:T(8,128)(2,1)S(1)} collective-permute-done((bf16[1,192,512]{2,1,0:T(8,128)(2,1)S(1)}, bf16[1,192,512]{2,1,0:T(8,128)(2,1)S(1)}, u32[]{:S(2)}, u32[]{:S(2)}) %collective-permute-start.43) | collective-permute-done | bytes 196640 | tf_op jit(solution)/shard_map/ppermute | solution.py:892
  130.3 1.3 collective-permute-start.46
  131.5 2.8 %shard_map.330 = (f32[2048,512]{1,0:T(8,128)}, f32[512,2048]{1,0:T(8,128)}, f32[512,1536]{1,0:T(8,128)}, f32[512,512]{1,0:T(8,128)}, f32[512,128]{1,0:T(8,128)}) custom-call(bf16[7,208,512]{2,1,0:T(8,128)(2,1)S(1)} %shard_map.328.refs_0_, bf16[7,192,512]{2,1,0:T(8,128)(2,1)S(1)} %shard_map.329.refs_1_.refs_4_), custom_call_target="tpu_custom_call" | custom-call | tf_op jit(solution)/shard_map/pallas_call | solution.py:857
  134.4 2.8 %shard_map.331 = (f32[2048,512]{1,0:T(8,128)}, f32[512,2048]{1,0:T(8,128)}, f32[512,1536]{1,0:T(8,128)}, f32[512,512]{1,0:T(8,128)}, f32[512,128]{1,0:T(8,128)}) custom-call(bf16[7,208,512]{2,1,0:T(8,128)(2,1)S(1)} %collective-permute-done.44.refs_0_, ...), custom_call_target="tpu_custom_call", output_to_operand_aliasing={{0}: (2, {}), {1}: (3, {}), {2}: (4, {}), {3}: (5, {}), {4}... | custom-call | tf_op jit(solution)/shard_map/pallas_call | solution.py:857
  139.4 1.9 %shard_map.336 = (f32[2048,512]{1,0:T(8,128)}, f32[512,2048]{1,0:T(8,128)}, f32[512,1536]{1,0:T(8,128)}, f32[512,512]{1,0:T(8,128)}, f32[512,128]{1,0:T(8,128)},...) custom-call(bf16[1,208,512]{2,1,0:T(8,128)(2,1)S(1)} %shard_map.334., ...), custom_call_target="tpu_custom_call", output_to_operand_aliasing={{0}: (8, {}), {1}: (9, {}), {2}: (10, {}), {3}: (11, {}), {... | custom-call | tf_op jit(solution)/shard_map/pallas_call | solution.py:857
  (130 shorter events, 31.0 us)
Async XLA Ops:
  8.1 5.3 %collective-permute-start = (bf16[272,128]{1,0:T(8,128)(2,1)S(1)}, bf16[272,128]{1,0:T(8,128)(2,1)S(1)}, u32[]{:S(2)}, u32[]{:S(2)}) collective-permute-start(bf16[272,128]{1,0:T(8,128)(2,1)S(1)} %get-tuple-element.175), channel_id=1, source_target_pairs={{0,16},{16,0},{1,17},{17,1},{2,18},{18,2},{3,19},{19,3},{4,20},{20... | collective-permute-start | bytes 208904 | tf_op jit(solution)/shard_map/ppermute | solution.py:873
  13.4 5.4 %collective-permute-start.2 = (bf16[256,128]{1,0:T(8,128)(2,1)S(1)}, bf16[256,128]{1,0:T(8,128)(2,1)S(1)}, u32[]{:S(2)}, u32[]{:S(2)}) collective-permute-start(bf16[256,128]{1,0:T(8,128)(2,1)S(1)} %slice_select_fusion.here_ref), channel_id=1, source_target_pairs={{0,8},{1,9},{2,10},{3,11},{4,12},{5,13},{6,14},{7,15},{8,0},{9,1},... | collective-permute-start | bytes 196616 | tf_op jit(solution)/shard_map/ppermute | solution.py:873
  16.6 4.4 %collective-permute-start.1 = (bf16[272,128]{1,0:T(8,128)(2,1)S(1)}, bf16[272,128]{1,0:T(8,128)(2,1)S(1)}, u32[]{:S(2)}, u32[]{:S(2)}) collective-permute-start(bf16[272,128]{1,0:T(8,128)(2,1)S(1)} %broadcast_select_fusion), channel_id=1, source_target_pairs={{0,2},{1,3},{2,0},{3,1},{4,6},{5,7},{6,4},{7,5},{8,10},{9,11},{10,... | collective-permute-start | bytes 208904 | tf_op jit(solution)/shard_map/ppermute | solution.py:873
  21.0 4.6 %collective-permute-start.3 = (bf16[544,128]{1,0:T(8,128)(2,1)S(1)}, bf16[544,128]{1,0:T(8,128)(2,1)S(1)}, u32[]{:S(2)}, u32[]{:S(2)}) collective-permute-start(bf16[544,128]{1,0:T(8,128)(2,1)S(1)} %pad_maximum_fusion.near_ref), channel_id=1, source_target_pairs={{0,1},{1,0},{2,3},{3,2},{4,5},{5,4},{6,7},{7,6},{8,9},{9,8},{10,11... | collective-permute-start | bytes 417800 | tf_op jit(solution)/shard_map/ppermute | solution.py:873
  21.1 4.5 %collective-permute-start.4 = (bf16[256,128]{1,0:T(8,128)(2,1)S(1)}, bf16[256,128]{1,0:T(8,128)(2,1)S(1)}, u32[]{:S(2)}, u32[]{:S(2)}) collective-permute-start(bf16[256,128]{1,0:T(8,128)(2,1)S(1)} %shard_map.299.refs_0_), channel_id=1, source_target_pairs={{0,4},{1,5},{2,6},{3,7},{4,0},{5,1},{6,2},{7,3},{8,12},{9,13},{10,... | collective-permute-start | bytes 196616 | tf_op jit(solution)/shard_map/ppermute | solution.py:873
  29.7 5.0 %collective-permute-start.8 = (f32[32,128]{1,0:T(8,128)S(1)}, f32[32,128]{1,0:T(8,128)S(1)}, u32[]{:S(2)}, u32[]{:S(2)}) collective-permute-start(f32[32,128]{1,0:T(8,128)S(1)} %add.3.own_ref), channel_id=1, source_target_pairs={{0,18},{1,19},{2,16},{3,17},{4,22},{5,23},{6,20},{7,21},{8,26},{9,... | collective-permute-start | bytes 49160 | tf_op jit(solution)/shard_map/ppermute | solution.py:1115
  32.1 3.7 %collective-permute-start.7 = (f32[32,128]{1,0:T(8,128)S(1)}, f32[32,128]{1,0:T(8,128)S(1)}, u32[]{:S(2)}, u32[]{:S(2)}) collective-permute-start(f32[32,128]{1,0:T(8,128)S(1)} %add.3.own_ref), channel_id=1, source_target_pairs={{0,16},{16,0},{1,17},{17,1},{2,18},{18,2},{3,19},{19,3},{4,20},{20... | collective-permute-start | bytes 49160 | tf_op jit(solution)/shard_map/ppermute | solution.py:873
  32.6 3.7 %collective-permute-start.6 = (f32[32,128]{1,0:T(8,128)S(1)}, f32[32,128]{1,0:T(8,128)S(1)}, u32[]{:S(2)}, u32[]{:S(2)}) collective-permute-start(f32[32,128]{1,0:T(8,128)S(1)} %add.3.own_ref), channel_id=1, source_target_pairs={{0,2},{1,3},{2,0},{3,1},{4,6},{5,7},{6,4},{7,5},{8,10},{9,11},{10,... | collective-permute-start | bytes 49160 | tf_op jit(solution)/shard_map/ppermute | solution.py:873
  40.0 1.9 %collective-permute-start.9 = (bf16[512,128]{1,0:T(8,128)(2,1)S(1)}, bf16[512,128]{1,0:T(8,128)(2,1)S(1)}, u32[]{:S(2)}, u32[]{:S(2)}) collective-permute-start(bf16[512,128]{1,0:T(8,128)(2,1)S(1)} %get-tuple-element.194), channel_id=1, source_target_pairs={{0,1},{1,0},{2,3},{3,2},{4,5},{5,4},{6,7},{7,6},{8,9},{9,8},{10,11... | collective-permute-start | bytes 393224 | tf_op jit(solution)/shard_map/ppermute | solution.py:873
  40.2 4.5 %collective-permute-start.11 = (bf16[256,128]{1,0:T(8,128)(2,1)S(1)}, bf16[256,128]{1,0:T(8,128)(2,1)S(1)}, u32[]{:S(2)}, u32[]{:S(2)}) collective-permute-start(bf16[256,128]{1,0:T(8,128)(2,1)S(1)} %get-tuple-element.196), channel_id=1, source_target_pairs={{0,4},{1,5},{2,6},{3,7},{4,0},{5,1},{6,2},{7,3},{8,12},{9,13},{10,... | collective-permute-start | bytes 196616 | tf_op jit(solution)/shard_map/ppermute | solution.py:873
  44.8 5.6 %collective-permute-start.12 = (bf16[256,128]{1,0:T(8,128)(2,1)S(1)}, bf16[256,128]{1,0:T(8,128)(2,1)S(1)}, u32[]{:S(2)}, u32[]{:S(2)}) collective-permute-start(bf16[256,128]{1,0:T(8,128)(2,1)S(1)} %shard_map.304.rows_ref), channel_id=1, source_target_pairs={{0,8},{1,9},{2,10},{3,11},{4,12},{5,13},{6,14},{7,15},{8,0},{9,1},... | collective-permute-start | bytes 196616 | tf_op jit(solution)/shard_map/ppermute | solution.py:873
  46.1 4.4 %collective-permute-start.10 = (bf16[256,128]{1,0:T(8,128)(2,1)S(1)}, bf16[256,128]{1,0:T(8,128)(2,1)S(1)}, u32[]{:S(2)}, u32[]{:S(2)}) collective-permute-start(bf16[256,128]{1,0:T(8,128)(2,1)S(1)} %get-tuple-element.334), channel_id=1, source_target_pairs={{0,2},{1,3},{2,0},{3,1},{4,6},{5,7},{6,4},{7,5},{8,10},{9,11},{10,... | collective-permute-start | bytes 196616 | tf_op jit(solution)/shard_map/ppermute | solution.py:873
  50.5 4.3 %collective-permute-start.13 = (bf16[256,128]{1,0:T(8,128)(2,1)S(1)}, bf16[256,128]{1,0:T(8,128)(2,1)S(1)}, u32[]{:S(2)}, u32[]{:S(2)}) collective-permute-start(bf16[256,128]{1,0:T(8,128)(2,1)S(1)} %broadcast_select_fusion.1), channel_id=1, source_target_pairs={{0,16},{16,0},{1,17},{17,1},{2,18},{18,2},{3,19},{19,3},{4,20},{20... | collective-permute-start | bytes 196616 | tf_op jit(solution)/shard_map/ppermute | solution.py:873
  60.8 4.6 %collective-permute-start.14 = (bf16[8,208,512]{2,1,0:T(8,128)(2,1)S(1)}, bf16[8,208,512]{2,1,0:T(8,128)(2,1)S(1)}, u32[]{:S(2)}, u32[]{:S(2)}) collective-permute-start(bf16[8,208,512]{2,1,0:T(8,128)(2,1)S(1)} %get-tuple-element.205), channel_id=1, source_target_pairs={{0,1},{1,0},{2,3},{3,2},{4,5},{5,4},{6,7},{7,6},{8,9},{9,8},{10,11... | collective-permute-start | bytes 5111816 | tf_op jit(solution)/shard_map/ppermute | solution.py:873
  64.8 6.1 %collective-permute-start.18 = (bf16[6,192,512]{2,1,0:T(8,128)(2,1)S(1)}, bf16[6,192,512]{2,1,0:T(8,128)(2,1)S(1)}, u32[]{:S(2)}, u32[]{:S(2)}) collective-permute-start(bf16[6,192,512]{2,1,0:T(8,128)(2,1)S(1)} %get-tuple-element.229), channel_id=1, source_target_pairs={{0,1},{1,0},{2,3},{3,2},{4,5},{5,4},{6,7},{7,6},{8,9},{9,8},{10,11... | collective-permute-start | bytes 3538952 | tf_op jit(solution)/shard_map/ppermute | solution.py:873
  65.4 3.0 %collective-permute-start.17 = (bf16[2,192,512]{2,1,0:T(8,128)(2,1)S(1)}, bf16[2,192,512]{2,1,0:T(8,128)(2,1)S(1)}, u32[]{:S(2)}, u32[]{:S(2)}) collective-permute-start(bf16[2,192,512]{2,1,0:T(8,128)(2,1)S(1)} %get-tuple-element.223), channel_id=1, source_target_pairs={{0,1},{1,0},{2,3},{3,2},{4,5},{5,4},{6,7},{7,6},{8,9},{9,8},{10,11... | collective-permute-start | bytes 1179656 | tf_op jit(solution)/shard_map/ppermute | solution.py:873
  65.5 8.2 %collective-permute-start.15 = (bf16[1,208,512]{2,1,0:T(8,128)(2,1)S(1)}, bf16[1,208,512]{2,1,0:T(8,128)(2,1)S(1)}, u32[]{:S(2)}, u32[]{:S(2)}) collective-permute-start(bf16[1,208,512]{2,1,0:T(8,128)(2,1)S(1)} %get-tuple-element.220), channel_id=1, source_target_pairs={{0,4},{1,3},{2,0},{3,7},{4,8},{5,1},{6,2},{7,11},{8,12},{9,5},{10,... | collective-permute-start | bytes 638984 | tf_op jit(solution)/shard_map/ppermute | solution.py:892
  67.3 6.4 %collective-permute-start.16 = (bf16[1,208,512]{2,1,0:T(8,128)(2,1)S(1)}, bf16[1,208,512]{2,1,0:T(8,128)(2,1)S(1)}, u32[]{:S(2)}, u32[]{:S(2)}) collective-permute-start(bf16[1,208,512]{2,1,0:T(8,128)(2,1)S(1)} %get-tuple-element.221), channel_id=1, source_target_pairs={{0,2},{1,5},{2,6},{3,1},{4,0},{5,9},{6,10},{7,3},{8,4},{9,13},{10,... | collective-permute-start | bytes 638984 | tf_op jit(solution)/shard_map/ppermute | solution.py:892
  68.5 9.4 %collective-permute-start.22 = (bf16[1,192,512]{2,1,0:T(8,128)(2,1)S(1)}, bf16[1,192,512]{2,1,0:T(8,128)(2,1)S(1)}, u32[]{:S(2)}, u32[]{:S(2)}) collective-permute-start(bf16[1,192,512]{2,1,0:T(8,128)(2,1)S(1)} %get-tuple-element.226), channel_id=1, source_target_pairs={{0,2},{1,5},{2,6},{3,1},{4,0},{5,9},{6,10},{7,3},{8,4},{9,13},{10,... | collective-permute-start | bytes 589832 | tf_op jit(solution)/shard_map/ppermute | solution.py:892
  69.1 8.9 %collective-permute-start.21 = (bf16[1,192,512]{2,1,0:T(8,128)(2,1)S(1)}, bf16[1,192,512]{2,1,0:T(8,128)(2,1)S(1)}, u32[]{:S(2)}, u32[]{:S(2)}) collective-permute-start(bf16[1,192,512]{2,1,0:T(8,128)(2,1)S(1)} %get-tuple-element.236), channel_id=1, source_target_pairs={{0,4},{1,3},{2,0},{3,7},{4,8},{5,1},{6,2},{7,11},{8,12},{9,5},{10,... | collective-permute-start | bytes 589832 | tf_op jit(solution)/shard_map/ppermute | solution.py:892
  73.8 8.3 %collective-permute-start.20 = (bf16[1,208,512]{2,1,0:T(8,128)(2,1)S(1)}, bf16[1,208,512]{2,1,0:T(8,128)(2,1)S(1)}, u32[]{:S(2)}, u32[]{:S(2)}) collective-permute-start(bf16[1,208,512]{2,1,0:T(8,128)(2,1)S(1)} %get-tuple-element.235), channel_id=1, source_target_pairs={{0,2},{1,5},{2,6},{3,1},{4,0},{5,9},{6,10},{7,3},{8,4},{9,13},{10,... | collective-permute-start | bytes 638984 | tf_op jit(solution)/shard_map/ppermute | solution.py:892
  74.4 8.1 %collective-permute-start.19 = (bf16[1,208,512]{2,1,0:T(8,128)(2,1)S(1)}, bf16[1,208,512]{2,1,0:T(8,128)(2,1)S(1)}, u32[]{:S(2)}, u32[]{:S(2)}) collective-permute-start(bf16[1,208,512]{2,1,0:T(8,128)(2,1)S(1)} %get-tuple-element.234), channel_id=1, source_target_pairs={{0,4},{1,3},{2,0},{3,7},{4,8},{5,1},{6,2},{7,11},{8,12},{9,5},{10,... | collective-permute-start | bytes 638984 | tf_op jit(solution)/shard_map/ppermute | solution.py:892
  78.0 8.3 %collective-permute-start.26 = (bf16[1,192,512]{2,1,0:T(8,128)(2,1)S(1)}, bf16[1,192,512]{2,1,0:T(8,128)(2,1)S(1)}, u32[]{:S(2)}, u32[]{:S(2)}) collective-permute-start(bf16[1,192,512]{2,1,0:T(8,128)(2,1)S(1)} %get-tuple-element.244), channel_id=1, source_target_pairs={{0,2},{1,5},{2,6},{3,1},{4,0},{5,9},{6,10},{7,3},{8,4},{9,13},{10,... | collective-permute-start | bytes 589832 | tf_op jit(solution)/shard_map/ppermute | solution.py:892
  78.8 7.9 %collective-permute-start.25 = (bf16[1,192,512]{2,1,0:T(8,128)(2,1)S(1)}, bf16[1,192,512]{2,1,0:T(8,128)(2,1)S(1)}, u32[]{:S(2)}, u32[]{:S(2)}) collective-permute-start(bf16[1,192,512]{2,1,0:T(8,128)(2,1)S(1)} %get-tuple-element.239), channel_id=1, source_target_pairs={{0,4},{1,3},{2,0},{3,7},{4,8},{5,1},{6,2},{7,11},{8,12},{9,5},{10,... | collective-permute-start | bytes 589832 | tf_op jit(solution)/shard_map/ppermute | solution.py:892
  82.6 8.3 %collective-permute-start.24 = (bf16[1,208,512]{2,1,0:T(8,128)(2,1)S(1)}, bf16[1,208,512]{2,1,0:T(8,128)(2,1)S(1)}, u32[]{:S(2)}, u32[]{:S(2)}) collective-permute-start(bf16[1,208,512]{2,1,0:T(8,128)(2,1)S(1)} %get-tuple-element.243), channel_id=1, source_target_pairs={{0,2},{1,5},{2,6},{3,1},{4,0},{5,9},{6,10},{7,3},{8,4},{9,13},{10,... | collective-permute-start | bytes 638984 | tf_op jit(solution)/shard_map/ppermute | solution.py:892
  84.7 7.9 %collective-permute-start.23 = (bf16[1,208,512]{2,1,0:T(8,128)(2,1)S(1)}, bf16[1,208,512]{2,1,0:T(8,128)(2,1)S(1)}, u32[]{:S(2)}, u32[]{:S(2)}) collective-permute-start(bf16[1,208,512]{2,1,0:T(8,128)(2,1)S(1)} %get-tuple-element.242), channel_id=1, source_target_pairs={{0,4},{1,3},{2,0},{3,7},{4,8},{5,1},{6,2},{7,11},{8,12},{9,5},{10,... | collective-permute-start | bytes 638984 | tf_op jit(solution)/shard_map/ppermute | solution.py:892
  86.8 8.3 %collective-permute-start.29 = (bf16[1,192,512]{2,1,0:T(8,128)(2,1)S(1)}, bf16[1,192,512]{2,1,0:T(8,128)(2,1)S(1)}, u32[]{:S(2)}, u32[]{:S(2)}) collective-permute-start(bf16[1,192,512]{2,1,0:T(8,128)(2,1)S(1)} %get-tuple-element.251), channel_id=1, source_target_pairs={{0,2},{1,5},{2,6},{3,1},{4,0},{5,9},{6,10},{7,3},{8,4},{9,13},{10,... | collective-permute-start | bytes 589832 | tf_op jit(solution)/shard_map/ppermute | solution.py:892
  88.9 6.2 %collective-permute-start.28 = (bf16[1,192,512]{2,1,0:T(8,128)(2,1)S(1)}, bf16[1,192,512]{2,1,0:T(8,128)(2,1)S(1)}, u32[]{:S(2)}, u32[]{:S(2)}) collective-permute-start(bf16[1,192,512]{2,1,0:T(8,128)(2,1)S(1)} %get-tuple-element.247), channel_id=1, source_target_pairs={{0,4},{1,3},{2,0},{3,7},{4,8},{5,1},{6,2},{7,11},{8,12},{9,5},{10,... | collective-permute-start | bytes 589832 | tf_op jit(solution)/shard_map/ppermute | solution.py:892
  92.7 5.9 %collective-permute-start.27 = (bf16[1,208,512]{2,1,0:T(8,128)(2,1)S(1)}, bf16[1,208,512]{2,1,0:T(8,128)(2,1)S(1)}, u32[]{:S(2)}, u32[]{:S(2)}) collective-permute-start(bf16[1,208,512]{2,1,0:T(8,128)(2,1)S(1)} %get-tuple-element.250), channel_id=1, source_target_pairs={{0,4},{1,3},{2,0},{3,7},{4,8},{5,1},{6,2},{7,11},{8,12},{9,5},{10,... | collective-permute-start | bytes 638984 | tf_op jit(solution)/shard_map/ppermute | solution.py:892
  95.3 6.6 %collective-permute-start.32 = (bf16[1,192,512]{2,1,0:T(8,128)(2,1)S(1)}, bf16[1,192,512]{2,1,0:T(8,128)(2,1)S(1)}, u32[]{:S(2)}, u32[]{:S(2)}) collective-permute-start(bf16[1,192,512]{2,1,0:T(8,128)(2,1)S(1)} %get-tuple-element.254), channel_id=1, source_target_pairs={{0,4},{1,3},{2,0},{3,7},{4,8},{5,1},{6,2},{7,11},{8,12},{9,5},{10,... | collective-permute-start | bytes 589832 | tf_op jit(solution)/shard_map/ppermute | solution.py:892
  98.7 8.1 %collective-permute-start.31 = (bf16[1,208,512]{2,1,0:T(8,128)(2,1)S(1)}, bf16[1,208,512]{2,1,0:T(8,128)(2,1)S(1)}, u32[]{:S(2)}, u32[]{:S(2)}) collective-permute-start(bf16[1,208,512]{2,1,0:T(8,128)(2,1)S(1)} %shard_map.320.refs_0_), channel_id=1, source_target_pairs={{0,2},{1,5},{2,6},{3,1},{4,0},{5,9},{6,10},{7,3},{8,4},{9,13},{10,... | collective-permute-start | bytes 638984 | tf_op jit(solution)/shard_map/ppermute | solution.py:892
  99.5 8.2 %collective-permute-start.30 = (bf16[1,208,512]{2,1,0:T(8,128)(2,1)S(1)}, bf16[1,208,512]{2,1,0:T(8,128)(2,1)S(1)}, u32[]{:S(2)}, u32[]{:S(2)}) collective-permute-start(bf16[1,208,512]{2,1,0:T(8,128)(2,1)S(1)} %shard_map.320.refs_0_), channel_id=1, source_target_pairs={{0,4},{1,3},{2,0},{3,7},{4,8},{5,1},{6,2},{7,11},{8,12},{9,5},{10,... | collective-permute-start | bytes 638984 | tf_op jit(solution)/shard_map/ppermute | solution.py:892
  101.9 9.1 %collective-permute-start.36 = (bf16[1,192,512]{2,1,0:T(8,128)(2,1)S(1)}, bf16[1,192,512]{2,1,0:T(8,128)(2,1)S(1)}, u32[]{:S(2)}, u32[]{:S(2)}) collective-permute-start(bf16[1,192,512]{2,1,0:T(8,128)(2,1)S(1)} %shard_map.321.refs_0_), channel_id=1, source_target_pairs={{0,2},{1,5},{2,6},{3,1},{4,0},{5,9},{6,10},{7,3},{8,4},{9,13},{10,... | collective-permute-start | bytes 589832 | tf_op jit(solution)/shard_map/ppermute | solution.py:892
  104.8 7.8 %collective-permute-start.35 = (bf16[1,192,512]{2,1,0:T(8,128)(2,1)S(1)}, bf16[1,192,512]{2,1,0:T(8,128)(2,1)S(1)}, u32[]{:S(2)}, u32[]{:S(2)}) collective-permute-start(bf16[1,192,512]{2,1,0:T(8,128)(2,1)S(1)} %shard_map.321.refs_0_), channel_id=1, source_target_pairs={{0,4},{1,3},{2,0},{3,7},{4,8},{5,1},{6,2},{7,11},{8,12},{9,5},{10,... | collective-permute-start | bytes 589832 | tf_op jit(solution)/shard_map/ppermute | solution.py:892
  107.7 8.2 %collective-permute-start.34 = (bf16[1,208,512]{2,1,0:T(8,128)(2,1)S(1)}, bf16[1,208,512]{2,1,0:T(8,128)(2,1)S(1)}, u32[]{:S(2)}, u32[]{:S(2)}) collective-permute-start(bf16[1,208,512]{2,1,0:T(8,128)(2,1)S(1)} %get-tuple-element.288.refs_6_), channel_id=1, source_target_pairs={{0,2},{1,5},{2,6},{3,1},{4,0},{5,9},{6,10},{7,3},{8,4},{9,13},{10,... | collective-permute-start | bytes 638984 | tf_op jit(solution)/shard_map/ppermute | solution.py:892
  109.6 7.6 %collective-permute-start.33 = (bf16[1,208,512]{2,1,0:T(8,128)(2,1)S(1)}, bf16[1,208,512]{2,1,0:T(8,128)(2,1)S(1)}, u32[]{:S(2)}, u32[]{:S(2)}) collective-permute-start(bf16[1,208,512]{2,1,0:T(8,128)(2,1)S(1)} %get-tuple-element.283.refs_1_), channel_id=1, source_target_pairs={{0,4},{1,3},{2,0},{3,7},{4,8},{5,1},{6,2},{7,11},{8,12},{9,5},{10,... | collective-permute-start | bytes 638984 | tf_op jit(solution)/shard_map/ppermute | solution.py:892
  112.6 7.9 %collective-permute-start.40 = (bf16[1,192,512]{2,1,0:T(8,128)(2,1)S(1)}, bf16[1,192,512]{2,1,0:T(8,128)(2,1)S(1)}, u32[]{:S(2)}, u32[]{:S(2)}) collective-permute-start(bf16[1,192,512]{2,1,0:T(8,128)(2,1)S(1)} %get-tuple-element.296.refs_6_), channel_id=1, source_target_pairs={{0,2},{1,5},{2,6},{3,1},{4,0},{5,9},{6,10},{7,3},{8,4},{9,13},{10,... | collective-permute-start | bytes 589832 | tf_op jit(solution)/shard_map/ppermute | solution.py:892
  113.8 7.7 %collective-permute-start.39 = (bf16[1,192,512]{2,1,0:T(8,128)(2,1)S(1)}, bf16[1,192,512]{2,1,0:T(8,128)(2,1)S(1)}, u32[]{:S(2)}, u32[]{:S(2)}) collective-permute-start(bf16[1,192,512]{2,1,0:T(8,128)(2,1)S(1)} %get-tuple-element.291.refs_1_), channel_id=1, source_target_pairs={{0,4},{1,3},{2,0},{3,7},{4,8},{5,1},{6,2},{7,11},{8,12},{9,5},{10,... | collective-permute-start | bytes 589832 | tf_op jit(solution)/shard_map/ppermute | solution.py:892
  117.2 8.2 %collective-permute-start.38 = (bf16[1,208,512]{2,1,0:T(8,128)(2,1)S(1)}, bf16[1,208,512]{2,1,0:T(8,128)(2,1)S(1)}, u32[]{:S(2)}, u32[]{:S(2)}) collective-permute-start(bf16[1,208,512]{2,1,0:T(8,128)(2,1)S(1)} %get-tuple-element.287.refs_5_), channel_id=1, source_target_pairs={{0,2},{1,5},{2,6},{3,1},{4,0},{5,9},{6,10},{7,3},{8,4},{9,13},{10,... | collective-permute-start | bytes 638984 | tf_op jit(solution)/shard_map/ppermute | solution.py:892
  118.8 6.8 %collective-permute-start.37 = (bf16[1,208,512]{2,1,0:T(8,128)(2,1)S(1)}, bf16[1,208,512]{2,1,0:T(8,128)(2,1)S(1)}, u32[]{:S(2)}, u32[]{:S(2)}) collective-permute-start(bf16[1,208,512]{2,1,0:T(8,128)(2,1)S(1)} %get-tuple-element.284.refs_2_), channel_id=1, source_target_pairs={{0,4},{1,3},{2,0},{3,7},{4,8},{5,1},{6,2},{7,11},{8,12},{9,5},{10,... | collective-permute-start | bytes 638984 | tf_op jit(solution)/shard_map/ppermute | solution.py:892
  121.5 6.3 %collective-permute-start.43 = (bf16[1,192,512]{2,1,0:T(8,128)(2,1)S(1)}, bf16[1,192,512]{2,1,0:T(8,128)(2,1)S(1)}, u32[]{:S(2)}, u32[]{:S(2)}) collective-permute-start(bf16[1,192,512]{2,1,0:T(8,128)(2,1)S(1)} %get-tuple-element.295.refs_5_), channel_id=1, source_target_pairs={{0,2},{1,5},{2,6},{3,1},{4,0},{5,9},{6,10},{7,3},{8,4},{9,13},{10,... | collective-permute-start | bytes 589832 | tf_op jit(solution)/shard_map/ppermute | solution.py:892
  123.0 5.7 %collective-permute-start.42 = (bf16[1,192,512]{2,1,0:T(8,128)(2,1)S(1)}, bf16[1,192,512]{2,1,0:T(8,128)(2,1)S(1)}, u32[]{:S(2)}, u32[]{:S(2)}) collective-permute-start(bf16[1,192,512]{2,1,0:T(8,128)(2,1)S(1)} %get-tuple-element.292.refs_2_), channel_id=1, source_target_pairs={{0,4},{1,3},{2,0},{3,7},{4,8},{5,1},{6,2},{7,11},{8,12},{9,5},{10,... | collective-permute-start | bytes 589832 | tf_op jit(solution)/shard_map/ppermute | solution.py:892
  128.8 5.5 %collective-permute-start.44 = (bf16[7,208,512]{2,1,0:T(8,128)(2,1)S(1)}, bf16[7,208,512]{2,1,0:T(8,128)(2,1)S(1)}, u32[]{:S(2)}, u32[]{:S(2)}) collective-permute-start(bf16[7,208,512]{2,1,0:T(8,128)(2,1)S(1)} %shard_map.328.refs_0_), channel_id=1, source_target_pairs={{0,1},{1,0},{2,3},{3,2},{4,5},{5,4},{6,7},{7,6},{8,9},{9,8},{10,11... | collective-permute-start | bytes 4472840 | tf_op jit(solution)/shard_map/ppermute | solution.py:873
  129.0 5.3 %collective-permute-start.45 = (bf16[7,192,512]{2,1,0:T(8,128)(2,1)S(1)}, bf16[7,192,512]{2,1,0:T(8,128)(2,1)S(1)}, u32[]{:S(2)}, u32[]{:S(2)}) collective-permute-start(bf16[7,192,512]{2,1,0:T(8,128)(2,1)S(1)} %shard_map.329.refs_1_.refs_4_), channel_id=1, source_target_pairs={{0,1},{1,0},{2,3},{3,2},{4,5},{5,4},{6,7},{7,6},{8,9},{9,8},{10,11... | collective-permute-start | bytes 4128776 | tf_op jit(solution)/shard_map/ppermute | solution.py:873
  129.6 7.6 %collective-permute-start.41 = (bf16[1,208,512]{2,1,0:T(8,128)(2,1)S(1)}, bf16[1,208,512]{2,1,0:T(8,128)(2,1)S(1)}, u32[]{:S(2)}, u32[]{:S(2)}) collective-permute-start(bf16[1,208,512]{2,1,0:T(8,128)(2,1)S(1)} %get-tuple-element.285.refs_3_), channel_id=1, source_target_pairs={{0,4},{1,3},{2,0},{3,7},{4,8},{5,1},{6,2},{7,11},{8,12},{9,5},{10,... | collective-permute-start | bytes 638984 | tf_op jit(solution)/shard_map/ppermute | solution.py:892
  130.3 7.3 %collective-permute-start.46 = (bf16[1,192,512]{2,1,0:T(8,128)(2,1)S(1)}, bf16[1,192,512]{2,1,0:T(8,128)(2,1)S(1)}, u32[]{:S(2)}, u32[]{:S(2)}) collective-permute-start(bf16[1,192,512]{2,1,0:T(8,128)(2,1)S(1)} %get-tuple-element.293.refs_3_), channel_id=1, source_target_pairs={{0,4},{1,3},{2,0},{3,7},{4,8},{5,1},{6,2},{7,11},{8,12},{9,5},{10,... | collective-permute-start | bytes 589832 | tf_op jit(solution)/shard_map/ppermute | solution.py:892
  137.6 1.8 %collective-permute-start.47 = (bf16[1,208,512]{2,1,0:T(8,128)(2,1)S(1)}, bf16[1,208,512]{2,1,0:T(8,128)(2,1)S(1)}, u32[]{:S(2)}, u32[]{:S(2)}) collective-permute-start(bf16[1,208,512]{2,1,0:T(8,128)(2,1)S(1)} %shard_map.334.refs_0_), channel_id=1, source_target_pairs={{0,1},{1,0},{2,3},{3,2},{4,5},{5,4},{6,7},{7,6},{8,9},{9,8},{10,11... | collective-permute-start | bytes 638984 | tf_op jit(solution)/shard_map/ppermute | solution.py:873
  137.7 1.7 %collective-permute-start.48 = (bf16[1,192,512]{2,1,0:T(8,128)(2,1)S(1)}, bf16[1,192,512]{2,1,0:T(8,128)(2,1)S(1)}, u32[]{:S(2)}, u32[]{:S(2)}) collective-permute-start(bf16[1,192,512]{2,1,0:T(8,128)(2,1)S(1)} %shard_map.335.refs_1_.refs_5_), channel_id=1, source_target_pairs={{0,1},{1,0},{2,3},{3,2},{4,5},{5,4},{6,7},{7,6},{8,9},{9,8},{10,11... | collective-permute-start | bytes 589832 | tf_op jit(solution)/shard_map/ppermute | solution.py:873
  (18 other events, 162.6 us)

commit v8 on v7

--- a/solution.py
+++ b/solution.py
@@ -87,9 +87,9 @@
     return np.concatenate(parts, axis=1)
 
 
-def swap_halves(block):
-    lane = iota(block.shape, 1)
-    return jnp.where(lane % HD < HD // 2, pltpu.roll(block, 96, 1), pltpu.roll(block, 32, 1))
+def swapping():
+    shape = (128, 128)
+    return (iota(shape, 0) == (iota(shape, 1) ^ (HD // 2))).astype(F32).astype(BF16)
 
 
 def bounds_of(lens_ref, row):
@@ -222,11 +222,14 @@
 
     x = x_ref[...]
     joined = mm(x, wqkv_ref[...]) + bqkv_ref[...].astype(F32)
+    swap = swapping()
+    swap = jnp.concatenate([swap, swap], axis=0)
     for g in range(2 * D // 128):
         block = joined[:, g * 128 : (g + 1) * 128]
-        qkv_ref[:, g * 128 : (g + 1) * 128] = (
-            block * cosine + swap_halves(block) * sine
-        ).astype(BF16)
+        high = block.astype(BF16)
+        low = (block - high.astype(F32)).astype(BF16)
+        other = mm(jnp.concatenate([high, low], axis=1), swap)
+        qkv_ref[:, g * 128 : (g + 1) * 128] = (block * cosine + other * sine).astype(BF16)
     qkv_ref[:, 2 * D :] = joined[:, 2 * D :].astype(BF16)
     keep(qkv_ref, qkv_hbm)
 
@@ -235,16 +238,18 @@
         q_g = qkv_ref[:, g * 128 : (g + 1) * 128]
         k_g = qkv_ref[:, D + g * 128 : D + (g + 1) * 128]
         v_g = qkv_ref[:, 2 * D + g * 128 : 2 * D + (g + 1) * 128]
+        v_ones = jnp.concatenate([v_g, jnp.ones((ROW, 128), BF16)], axis=1)
         outs = []
         for h in range(2):
             pick = low_half if h == 0 else jnp.logical_not(low_half)
-            scores = mm_nt(jnp.where(pick, q_g, jnp.zeros_like(q_g)), k_g) * (1.0 / math.sqrt(HD))
-            scores = jnp.where(same, scores, -1e30)
+            scores = mm_nt(jnp.where(pick, q_g, jnp.zeros_like(q_g)), k_g)
+            scores = jnp.where(same, scores * (LOG2E / math.sqrt(HD)), -1e30)
             top = jnp.max(scores, axis=1, keepdims=True)
-            exps = jnp.exp(scores - top)
-            probs = (exps / jnp.sum(exps, axis=1, keepdims=True)).astype(BF16)
-            probs_ref[2 * g + h] = probs
-            outs.append(mm(probs, v_g))
+            exps = jnp.exp2(scores - top)
+            both = mm(exps.astype(BF16), v_ones)
+            inverse = 1.0 / both[:, 128:]
+            probs_ref[2 * g + h] = (exps * jnp.concatenate([inverse, inverse], axis=1)).astype(BF16)
+            outs.append(both[:, :128] * inverse)
         mixed_ref[:, g * 128 : (g + 1) * 128] = jnp.where(low_half, outs[0], outs[1]).astype(BF16)
 
     keep(probs_ref, probs_hbm)
@@ -596,13 +601,13 @@
 
 def feed_back(
     size, dq_ref, dd_ref, got_ref, xh2_ref, rs2_ref, affine_ref, wproj_ref, slope_ref, act_ref,
-    xh1_ref, wup_ref, wdown_hbm,
+    xh1_ref, wdown_ref, wup_hbm,
     keep_ref, send_ref, tail_keep, tail_send, dfirst_ref, gproj_ref, small_ref,
-    dinner_ref, wdown_ref, sems,
+    dinner_ref, wup_ref, sems,
 ):
     step = 512
     spans = [slice(c * step, (c + 1) * step) for c in range(FF // step)]
-    copies = fetch([(wdown_hbm.at[span, :], wdown_ref.at[span, :]) for span in spans], sems)
+    copies = fetch([(wup_hbm, wup_ref)], sems)
     g1, s1, g2, s2 = [affine_ref[k : k + 1, :] for k in range(4)]
     _, stream, _, _, has_top, *places = here(size)
     is_query, docs_there = stream == 0, has_top == 0
@@ -627,7 +632,6 @@
     d_first = d_sum
     for c in range(FF // step):
         cols = spans[c]
-        copies[c].wait()
         d_act = mm_nt(d_branch, wdown_ref[cols, :])
         d_inner = (d_act * slope_ref[:, cols].astype(F32)).astype(BF16)
         dinner_ref[:, cols] = d_inner
@@ -638,11 +642,11 @@
                 keep_ref, send_ref, slice(0, DOWN), c * (step // DOWN) + k, places,
                 grad[k * DOWN : (k + 1) * DOWN, :],
             )
-        d_first = d_first + mm_nt(d_inner, wup_ref[:, cols])
-    dfirst_ref[...] = d_first
+    copies[0].wait()
     first = (xh1_ref[...] * g1 + s1).astype(BF16)
     for c in range(FF // step):
         cols = slice(c * step, (c + 1) * step)
+        d_first = d_first + mm_nt(dinner_ref[:, cols], wup_ref[:, cols])
         grad = mm_tn(first, dinner_ref[:, cols]).astype(BF16)
         for k in range(D // DOWN):
             block = c * (D // DOWN) + k
@@ -654,6 +658,7 @@
                 tail_keep, tail_send, slice(0, TAIL), block, places,
                 grad[start + HEAD : start + DOWN, :],
             )
+    dfirst_ref[...] = d_first
 
 
 def attend_back(
@@ -675,9 +680,12 @@
     cosine, sine = rope_ref[:, :128], rope_ref[:, 128:]
     low_half = iota((ROW, 128), 1) < HD
 
-    def unrotate(values):
-        values = values * (1.0 / math.sqrt(HD))
-        return (values * cosine - swap_halves(values) * sine).astype(BF16)
+    scale = 1.0 / math.sqrt(HD)
+    cosine, sine = cosine * scale, sine * scale
+    swap = swapping()
+
+    def unrotate(both):
+        return (both[:, :128] * cosine - both[:, 128:] * sine).astype(BF16)
 
     for g in range(HEADS // 2):
         span = slice(g * 128, (g + 1) * 128)
@@ -685,10 +693,13 @@
         k_g = qkv_ref[:, D + g * 128 : D + (g + 1) * 128]
         v_g = qkv_ref[:, 2 * D + g * 128 : 2 * D + (g + 1) * 128]
         m_g = d_mixed[:, span]
-        d_q = jnp.zeros((ROW, 128), F32)
-        d_k = jnp.zeros((ROW, 128), F32)
+        q_both = jnp.concatenate([q_g, mm(q_g, swap).astype(BF16)], axis=1)
+        k_both = jnp.concatenate([k_g, mm(k_g, swap).astype(BF16)], axis=1)
+        d_q = jnp.zeros((ROW, 256), F32)
+        d_k = jnp.zeros((ROW, 256), F32)
         d_v = jnp.zeros((ROW, 128), F32)
         zero = jnp.zeros((ROW, 128), BF16)
+        zero_both = jnp.zeros((ROW, 256), BF16)
         for h in range(2):
             pick = low_half if h == 0 else jnp.logical_not(low_half)
             probs_low = probs_ref[2 * g + h]
@@ -698,8 +709,9 @@
             d_v = d_v + mm_tn(probs_low, m_h)
             inner = jnp.sum(d_probs * probs, axis=1, keepdims=True)
             d_scores = (probs * (d_probs - inner)).astype(BF16)
-            d_q = d_q + mm(d_scores, jnp.where(pick, k_g, zero))
-            d_k = d_k + mm_tn(d_scores, jnp.where(pick, q_g, zero))
+            pick_both = jnp.concatenate([pick, pick], axis=1)
+            d_q = d_q + mm(d_scores, jnp.where(pick_both, k_both, zero_both))
+            d_k = d_k + mm_tn(d_scores, jnp.where(pick_both, q_both, zero_both))
         djoined_ref[:, g * 128 : (g + 1) * 128] = unrotate(d_q)
         djoined_ref[:, D + g * 128 : D + (g + 1) * 128] = unrotate(d_k)
         djoined_ref[:, 2 * D + g * 128 : 2 * D + (g + 1) * 128] = d_v.astype(BF16)
@@ -1148,8 +1160,8 @@
     one_keep, one_send, tail_keep, tail_send, d_first, gproj, small = call(
         partial(feed_back, size),
         (
-            dq, dd, got, xh2, rs2, affine, proj_weight[0], slope, act, xh1, up_weight[0],
-            down_weight[0],
+            dq, dd, got, xh2, rs2, affine, proj_weight[0], slope, act, xh1, down_weight[0],
+            up_weight[0],
         ),
         [VMEM] * 3 + [HELD] * 8 + [HBM],
         [shape_of((RING, FIRST, D), BF16)] * 2
@@ -1157,8 +1169,8 @@
         + [shape_of((ROW, D)), shape_of((D, PROJ)), shape_of((8, D))],
         [
             pltpu.VMEM((ROW, FF), BF16),
-            pltpu.VMEM((FF, D), BF16),
-            pltpu.SemaphoreType.DMA((4,)),
+            pltpu.VMEM((D, FF), BF16),
+            pltpu.SemaphoreType.DMA((1,)),
         ],
         room=24,
     )

time: 142 us -> 140 us (0.986)
  Pallas kernels: 37.5 us -> 35.5 us
    pallas_call x40, Pallas kernels: 37.5 us -> 35.5 us  [call(): pl.pallas_call(kernel, out_shape=outs, in_specs=specs, out_specs=out_spec...]
  transfers between devices with their start and end apart: 49 -> 49, of which waited for: 36 -> 35; matrix products, arithmetic and copies ran while one was open for 0% -> 0% of each run, Pallas kernels for 11% -> 11%
where the time goes in v8:
time: 140 us
  starting transfers between devices  50.5 us (36%)
  waiting for transfers between devices  50.1 us (36%)
  Pallas kernels  35.5 us (25%)
  between operations  2.18 us (2%)
    pallas_call x40, Pallas kernels, call(): pl.pallas_call(kernel, out_shape=outs, in_specs=specs, out_specs=out_spec...  35.5 us
    ppermute x28, starting transfers between devices, ring_swap(): return lax.ppermute(value, 'dp', pairs)  30.4 us
    ppermute x28, waiting for transfers between devices, ring_swap(): return lax.ppermute(value, 'dp', pairs)  30.2 us
    ppermute x20, waiting for transfers between devices, swapped(): return lax.ppermute(value, axis, [(k, k ^ mask) for k in range(size)])  19.9 us
    ppermute x20, starting transfers between devices, swapped(): return lax.ppermute(value, axis, [(k, k ^ mask) for k in range(size)])  17.7 us
  transfers between devices with their start and end apart: 49, of which 35 were waited for; matrix products, arithmetic and copies ran while one was open for 0% of the time, Pallas kernels for 11%

profile of v8, /device:TPU:0, one launch (start us, length us, event | category | flops | bytes accessed | tf_op | source)
XLA Modules:
  0.0 139.5 jit_solution(17134012073714237784)
XLA Ops:
  0.7 6.6 %shard_map.297 = (bf16[272,128]{1,0:T(8,128)(2,1)S(1)}, bf16[256,2048]{1,0:T(8,128)(2,1)S(1)}, bf16[256,2048]{1,0:T(8,128)(2,1)S(1)}, f32[256,512]{1,0:T(8,128)S...) custom-call(s32[5,16]{1,0:T(8,128)} %bitcast.28, ...), custom_call_target="tpu_custom_call" | custom-call | flops 100000000 | bytes 10000000 | tf_op jit(solution)/shard_map/pallas_call | solution.py:869
  7.3 3.0 %collective-permute-start = (bf16[272,128]{1,0:T(8,128)(2,1)S(1)}, bf16[272,128]{1,0:T(8,128)(2,1)S(1)}, u32[]{:S(2)}, u32[]{:S(2)}) collective-permute-start(bf16[272,128]{1,0:T(8,128)(2,1)S(1)} %get-tuple-element.175), channel_id=1, source_target_pairs={{0,16},{16,0},{1,17},{17,1},{2,18},{18,2},{3,19},{19,3},{4,20},{20... | collective-permute-start | bytes 208904 | tf_op jit(solution)/shard_map/ppermute | solution.py:885
  10.3 1.5 %shard_map.298 = (bf16[256,2048]{1,0:T(8,128)(2,1)}, bf16[256,2048]{1,0:T(8,128)(2,1)}, f32[256,512]{1,0:T(8,128)}, f32[256,128]{1,0:T(8,128)}) custom-call(bf16[256,2048]{1,0:T(8,128)(2,1)S(1)} %get-tuple-element.176.refs_0_, bf16[256,2048]{1,0:T(8,128)(2,1)S(1)} %get-tuple-element.177.refs_1_, f32[256,512]{1,0:T(8,128)S(1)} %get-tuple-element.178.refs_2_, ...), custom_call_target="tpu_custom_call" | custom-call | flops 300000000 | bytes 30000000 | tf_op jit(solution)/shard_map/pallas_call | solution.py:869
  12.6 3.2 %collective-permute-start.2 = (bf16[256,128]{1,0:T(8,128)(2,1)S(1)}, bf16[256,128]{1,0:T(8,128)(2,1)S(1)}, u32[]{:S(2)}, u32[]{:S(2)}) collective-permute-start(bf16[256,128]{1,0:T(8,128)(2,1)S(1)} %slice_select_fusion.here_ref), channel_id=1, source_target_pairs={{0,8},{1,9},{2,10},{3,11},{4,12},{5,13},{6,14},{7,15},{8,0},{9,1},... | collective-permute-start | bytes 196616 | tf_op jit(solution)/shard_map/ppermute | solution.py:885
  15.8 1.6 %collective-permute-start.1 = (bf16[272,128]{1,0:T(8,128)(2,1)S(1)}, bf16[272,128]{1,0:T(8,128)(2,1)S(1)}, u32[]{:S(2)}, u32[]{:S(2)}) collective-permute-start(bf16[272,128]{1,0:T(8,128)(2,1)S(1)} %broadcast_select_fusion), channel_id=1, source_target_pairs={{0,2},{1,3},{2,0},{3,1},{4,6},{5,7},{6,4},{7,5},{8,10},{9,11},{10,... | collective-permute-start | bytes 208904 | tf_op jit(solution)/shard_map/ppermute | solution.py:885
  18.1 2.1 %collective-permute-done.1 = bf16[272,128]{1,0:T(8,128)(2,1)S(1)} collective-permute-done((bf16[272,128]{1,0:T(8,128)(2,1)S(1)}, bf16[272,128]{1,0:T(8,128)(2,1)S(1)}, u32[]{:S(2)}, u32[]{:S(2)}) %collective-permute-start.1) | collective-permute-done | bytes 69664 | tf_op jit(solution)/shard_map/ppermute | solution.py:885
  20.3 1.6 %collective-permute-start.4 = (bf16[256,128]{1,0:T(8,128)(2,1)S(1)}, bf16[256,128]{1,0:T(8,128)(2,1)S(1)}, u32[]{:S(2)}, u32[]{:S(2)}) collective-permute-start(bf16[256,128]{1,0:T(8,128)(2,1)S(1)} %shard_map.299.refs_0_), channel_id=1, source_target_pairs={{0,4},{1,5},{2,6},{3,7},{4,0},{5,1},{6,2},{7,3},{8,12},{9,13},{10,... | collective-permute-start | bytes 196616 | tf_op jit(solution)/shard_map/ppermute | solution.py:885
  22.6 2.2 %collective-permute-done.4.refs_1_ = bf16[256,128]{1,0:T(8,128)(2,1)S(1)} collective-permute-done((bf16[256,128]{1,0:T(8,128)(2,1)S(1)}, bf16[256,128]{1,0:T(8,128)(2,1)S(1)}, u32[]{:S(2)}, u32[]{:S(2)}) %collective-permute-start.4) | collective-permute-done | bytes 65568 | tf_op jit(solution)/shard_map/ppermute | solution.py:885
  24.8 2.8 %shard_map.300 = (f32[1024,128]{1,0:T(8,128)S(1)}, f32[32,128]{1,0:T(8,128)S(1)}, f32[32,128]{1,0:T(8,128)S(1)}, f32[32,128]{1,0:T(8,128)S(1)}) custom-call(f32[1]{0:T(128)} %bitcast.16.scale_ref, s32[5,16]{1,0:T(8,128)S(1)} %bitcast.29, bf16[544,128]{1,0:T(8,128)(2,1)S(1)} %pad_maximum_fusion.near_ref, bf16[544,128]{1,0:T(8,128)(2,1)S(1)} %collective-permute-done.3.far_ref, ...), custom_call_target="tpu_custom_call" | custom-call | flops 100000000 | bytes 10000000 | tf_op jit(solution)/shard_map/pallas_call | solution.py:869
  28.8 2.4 %collective-permute-start.8 = (f32[32,128]{1,0:T(8,128)S(1)}, f32[32,128]{1,0:T(8,128)S(1)}, u32[]{:S(2)}, u32[]{:S(2)}) collective-permute-start(f32[32,128]{1,0:T(8,128)S(1)} %add.3.own_ref), channel_id=1, source_target_pairs={{0,18},{1,19},{2,16},{3,17},{4,22},{5,23},{6,20},{7,21},{8,26},{9,... | collective-permute-start | bytes 49160 | tf_op jit(solution)/shard_map/ppermute | solution.py:1127
  32.3 1.5 %shard_map.301 = (bf16[3,1024,128]{2,1,0:T(8,128)(2,1)S(1)}, bf16[3,128,1024]{2,1,0:T(8,128)(2,1)S(1)}, f32[1024,128]{1,0:T(8,128)S(1)}, bf16[3,128,512]{2,1,0:T...) custom-call(bf16[544,128]{1,0:T(8,128)(2,1)S(1)} %pad_maximum_fusion.near_ref, ...), custom_call_target="tpu_custom_call" | custom-call | flops 100000000 | bytes 10000000 | tf_op jit(solution)/shard_map/pallas_call | solution.py:869
  35.6 3.6 %shard_map.302 = (bf16[512,128]{1,0:T(8,128)(2,1)S(1)}, bf16[512,128]{1,0:T(8,128)(2,1)S(1)}, bf16[256,128]{1,0:T(8,128)(2,1)S(1)}, bf16[256,128]{1,0:T(8,128)(2,1)S(1)}, f32[8,128]{1,0:T(8,128)S(1)}) custom-call(f32[1]{0:T(128)} %bitcast.17.scale_ref, s32[5,16]{1,0:T(8,128)S(1)} %bitcast.30, f32[1024,128]{1,0:T(8,128)S(1)} %get-tuple-element.183.totals_ref, ...), custom_call_target="tpu_custom_call" | custom-call | flops 100000000 | bytes 10000000 | tf_op jit(solution)/shard_map/pallas_call | solution.py:869
  39.2 1.6 %collective-permute-start.11 = (bf16[256,128]{1,0:T(8,128)(2,1)S(1)}, bf16[256,128]{1,0:T(8,128)(2,1)S(1)}, u32[]{:S(2)}, u32[]{:S(2)}) collective-permute-start(bf16[256,128]{1,0:T(8,128)(2,1)S(1)} %get-tuple-element.196), channel_id=1, source_target_pairs={{0,4},{1,5},{2,6},{3,7},{4,0},{5,1},{6,2},{7,3},{8,12},{9,13},{10,... | collective-permute-start | bytes 196616 | tf_op jit(solution)/shard_map/ppermute | solution.py:885
  40.9 2.8 %collective-permute-done.11.got_ref = bf16[256,128]{1,0:T(8,128)(2,1)S(1)} collective-permute-done((bf16[256,128]{1,0:T(8,128)(2,1)S(1)}, bf16[256,128]{1,0:T(8,128)(2,1)S(1)}, u32[]{:S(2)}, u32[]{:S(2)}) %collective-permute-start.11) | collective-permute-done | bytes 65568 | tf_op jit(solution)/shard_map/ppermute | solution.py:885
  43.8 1.3 collective-permute-start.12
  45.7 3.8 %collective-permute-done.12.got_ref = bf16[256,128]{1,0:T(8,128)(2,1)S(1)} collective-permute-done((bf16[256,128]{1,0:T(8,128)(2,1)S(1)}, bf16[256,128]{1,0:T(8,128)(2,1)S(1)}, u32[]{:S(2)}, u32[]{:S(2)}) %collective-permute-start.12) | collective-permute-done | bytes 65568 | tf_op jit(solution)/shard_map/ppermute | solution.py:885
  49.5 1.6 %collective-permute-start.13 = (bf16[256,128]{1,0:T(8,128)(2,1)S(1)}, bf16[256,128]{1,0:T(8,128)(2,1)S(1)}, u32[]{:S(2)}, u32[]{:S(2)}) collective-permute-start(bf16[256,128]{1,0:T(8,128)(2,1)S(1)} %broadcast_select_fusion.1), channel_id=1, source_target_pairs={{0,16},{16,0},{1,17},{17,1},{2,18},{18,2},{3,19},{19,3},{4,20},{20... | collective-permute-start | bytes 196616 | tf_op jit(solution)/shard_map/ppermute | solution.py:885
  51.1 2.8 %collective-permute-done.13.got_ref = bf16[256,128]{1,0:T(8,128)(2,1)S(1)} collective-permute-done((bf16[256,128]{1,0:T(8,128)(2,1)S(1)}, bf16[256,128]{1,0:T(8,128)(2,1)S(1)}, u32[]{:S(2)}, u32[]{:S(2)}) %collective-permute-start.13) | collective-permute-done | bytes 65568 | tf_op jit(solution)/shard_map/ppermute | solution.py:885
  54.2 4.8 %shard_map.307 = (bf16[8,208,512]{2,1,0:T(8,128)(2,1)S(1)}, bf16[8,208,512]{2,1,0:T(8,128)(2,1)S(1)}, bf16[8,48,512]{2,1,0:T(8,128)(2,1)S(1)}, bf16[8,48,512]{2,...) custom-call(bf16[256,128]{1,0:T(8,128)(2,1)S(1)} %shard_map.306.dq_ref, ...), custom_call_target="tpu_custom_call" | custom-call | flops 100000000 | bytes 10000000 | tf_op jit(solution)/shard_map/pallas_call | solution.py:869
  59.1 3.7 %shard_map.308 = (bf16[8,192,512]{2,1,0:T(8,128)(2,1)S(1)}, bf16[2,192,512]{2,1,0:T(8,128)(2,1)S(1)}, bf16[6,192,512]{2,1,0:T(8,128)(2,1)S(1)}, f32[256,512]{1,0:T(8,128)S(1)}, bf16[256,1536]{1,0:T(8,128)(2,1)S(1)}) custom-call(f32[256,512]{1,0:T(8,128)S(1)} %get-tuple-element.206.dfirst_ref, f32[512,128]{1,0:T(8,128)S(1)} %get-tuple-element.207.gproj_ref, ...), custom_call_target="tpu_custom_call" | custom-call | flops 100000000 | bytes 10000000 | tf_op jit(solution)/shard_map/pallas_call | solution.py:869
  63.6 1.8 %collective-permute-start.15 = (bf16[1,208,512]{2,1,0:T(8,128)(2,1)S(1)}, bf16[1,208,512]{2,1,0:T(8,128)(2,1)S(1)}, u32[]{:S(2)}, u32[]{:S(2)}) collective-permute-start(bf16[1,208,512]{2,1,0:T(8,128)(2,1)S(1)} %get-tuple-element.220), channel_id=1, source_target_pairs={{0,4},{1,3},{2,0},{3,7},{4,8},{5,1},{6,2},{7,11},{8,12},{9,5},{10,... | collective-permute-start | bytes 638984 | tf_op jit(solution)/shard_map/ppermute | solution.py:904
  67.1 1.5 %collective-permute-start.21 = (bf16[1,192,512]{2,1,0:T(8,128)(2,1)S(1)}, bf16[1,192,512]{2,1,0:T(8,128)(2,1)S(1)}, u32[]{:S(2)}, u32[]{:S(2)}) collective-permute-start(bf16[1,192,512]{2,1,0:T(8,128)(2,1)S(1)} %get-tuple-element.236), channel_id=1, source_target_pairs={{0,4},{1,3},{2,0},{3,7},{4,8},{5,1},{6,2},{7,11},{8,12},{9,5},{10,... | collective-permute-start | bytes 589832 | tf_op jit(solution)/shard_map/ppermute | solution.py:904
  70.3 1.4 %shard_map.313 = f32[256,512]{1,0:T(8,128)} custom-call(f32[256,512]{1,0:T(8,128)S(1)} %get-tuple-element.230.dsum_ref, bf16[256,1536]{1,0:T(8,128)(2,1)S(1)} %get-tuple-element.231.djoined_ref, bf16[512,1536]{1,0:T(8,128)(2,1)S(1)} %bitcast.21), custom_call_target="tpu_custom_call" | custom-call | flops 300000000 | bytes 30000000 | tf_op jit(solution)/shard_map/pallas_call | solution.py:869
  72.4 1.8 %collective-permute-start.19 = (bf16[1,208,512]{2,1,0:T(8,128)(2,1)S(1)}, bf16[1,208,512]{2,1,0:T(8,128)(2,1)S(1)}, u32[]{:S(2)}, u32[]{:S(2)}) collective-permute-start(bf16[1,208,512]{2,1,0:T(8,128)(2,1)S(1)} %get-tuple-element.234), channel_id=1, source_target_pairs={{0,4},{1,3},{2,0},{3,7},{4,8},{5,1},{6,2},{7,11},{8,12},{9,5},{10,... | collective-permute-start | bytes 638984 | tf_op jit(solution)/shard_map/ppermute | solution.py:904
  74.2 1.8 %collective-permute-done.21.refs_0_ = bf16[1,192,512]{2,1,0:T(8,128)(2,1)S(1)} collective-permute-done((bf16[1,192,512]{2,1,0:T(8,128)(2,1)S(1)}, bf16[1,192,512]{2,1,0:T(8,128)(2,1)S(1)}, u32[]{:S(2)}, u32[]{:S(2)}) %collective-permute-start.21) | collective-permute-done | bytes 196640 | tf_op jit(solution)/shard_map/ppermute | solution.py:904
  76.8 1.4 collective-permute-start.25
  78.1 2.0 %collective-permute-done.20.refs_1_ = bf16[1,208,512]{2,1,0:T(8,128)(2,1)S(1)} collective-permute-done((bf16[1,208,512]{2,1,0:T(8,128)(2,1)S(1)}, bf16[1,208,512]{2,1,0:T(8,128)(2,1)S(1)}, u32[]{:S(2)}, u32[]{:S(2)}) %collective-permute-start.20) | collective-permute-done | bytes 213024 | tf_op jit(solution)/shard_map/ppermute | solution.py:904
  80.7 2.1 %collective-permute-start.24 = (bf16[1,208,512]{2,1,0:T(8,128)(2,1)S(1)}, bf16[1,208,512]{2,1,0:T(8,128)(2,1)S(1)}, u32[]{:S(2)}, u32[]{:S(2)}) collective-permute-start(bf16[1,208,512]{2,1,0:T(8,128)(2,1)S(1)} %get-tuple-element.243), channel_id=1, source_target_pairs={{0,2},{1,5},{2,6},{3,1},{4,0},{5,9},{6,10},{7,3},{8,4},{9,13},{10,... | collective-permute-start | bytes 638984 | tf_op jit(solution)/shard_map/ppermute | solution.py:904
  82.8 1.6 %collective-permute-done.26.refs_1_ = bf16[1,192,512]{2,1,0:T(8,128)(2,1)S(1)} collective-permute-done((bf16[1,192,512]{2,1,0:T(8,128)(2,1)S(1)}, bf16[1,192,512]{2,1,0:T(8,128)(2,1)S(1)}, u32[]{:S(2)}, u32[]{:S(2)}) %collective-permute-start.26) | collective-permute-done | bytes 196640 | tf_op jit(solution)/shard_map/ppermute | solution.py:904
  84.9 2.1 %collective-permute-start.29 = (bf16[1,192,512]{2,1,0:T(8,128)(2,1)S(1)}, bf16[1,192,512]{2,1,0:T(8,128)(2,1)S(1)}, u32[]{:S(2)}, u32[]{:S(2)}) collective-permute-start(bf16[1,192,512]{2,1,0:T(8,128)(2,1)S(1)} %get-tuple-element.251), channel_id=1, source_target_pairs={{0,2},{1,5},{2,6},{3,1},{4,0},{5,9},{6,10},{7,3},{8,4},{9,13},{10,... | collective-permute-start | bytes 589832 | tf_op jit(solution)/shard_map/ppermute | solution.py:904
  87.0 2.0 %collective-permute-done.24.refs_1_ = bf16[1,208,512]{2,1,0:T(8,128)(2,1)S(1)} collective-permute-done((bf16[1,208,512]{2,1,0:T(8,128)(2,1)S(1)}, bf16[1,208,512]{2,1,0:T(8,128)(2,1)S(1)}, u32[]{:S(2)}, u32[]{:S(2)}) %collective-permute-start.24) | collective-permute-done | bytes 213024 | tf_op jit(solution)/shard_map/ppermute | solution.py:904
  89.0 1.7 %collective-permute-done.23.refs_0_ = bf16[1,208,512]{2,1,0:T(8,128)(2,1)S(1)} collective-permute-done((bf16[1,208,512]{2,1,0:T(8,128)(2,1)S(1)}, bf16[1,208,512]{2,1,0:T(8,128)(2,1)S(1)}, u32[]{:S(2)}, u32[]{:S(2)}) %collective-permute-start.23) | collective-permute-done | bytes 213024 | tf_op jit(solution)/shard_map/ppermute | solution.py:904
  91.3 1.9 %collective-permute-done.29.refs_1_ = bf16[1,192,512]{2,1,0:T(8,128)(2,1)S(1)} collective-permute-done((bf16[1,192,512]{2,1,0:T(8,128)(2,1)S(1)}, bf16[1,192,512]{2,1,0:T(8,128)(2,1)S(1)}, u32[]{:S(2)}, u32[]{:S(2)}) %collective-permute-start.29) | collective-permute-done | bytes 196640 | tf_op jit(solution)/shard_map/ppermute | solution.py:904
  93.3 2.1 %collective-permute-start.32 = (bf16[1,192,512]{2,1,0:T(8,128)(2,1)S(1)}, bf16[1,192,512]{2,1,0:T(8,128)(2,1)S(1)}, u32[]{:S(2)}, u32[]{:S(2)}) collective-permute-start(bf16[1,192,512]{2,1,0:T(8,128)(2,1)S(1)} %get-tuple-element.254), channel_id=1, source_target_pairs={{0,4},{1,3},{2,0},{3,7},{4,8},{5,1},{6,2},{7,11},{8,12},{9,5},{10,... | collective-permute-start | bytes 589832 | tf_op jit(solution)/shard_map/ppermute | solution.py:904
  97.5 1.3 collective-permute-start.30
  99.9 2.7 %collective-permute-start.36 = (bf16[1,192,512]{2,1,0:T(8,128)(2,1)S(1)}, bf16[1,192,512]{2,1,0:T(8,128)(2,1)S(1)}, u32[]{:S(2)}, u32[]{:S(2)}) collective-permute-start(bf16[1,192,512]{2,1,0:T(8,128)(2,1)S(1)} %shard_map.321.refs_0_), channel_id=1, source_target_pairs={{0,2},{1,5},{2,6},{3,1},{4,0},{5,9},{6,10},{7,3},{8,4},{9,13},{10,... | collective-permute-start | bytes 589832 | tf_op jit(solution)/shard_map/ppermute | solution.py:904
  102.6 2.3 %collective-permute-done.31.refs_1_ = bf16[1,208,512]{2,1,0:T(8,128)(2,1)S(1)} collective-permute-done((bf16[1,208,512]{2,1,0:T(8,128)(2,1)S(1)}, bf16[1,208,512]{2,1,0:T(8,128)(2,1)S(1)}, u32[]{:S(2)}, u32[]{:S(2)}) %collective-permute-start.31) | collective-permute-done | bytes 213024 | tf_op jit(solution)/shard_map/ppermute | solution.py:904
  105.7 1.8 %collective-permute-start.34 = (bf16[1,208,512]{2,1,0:T(8,128)(2,1)S(1)}, bf16[1,208,512]{2,1,0:T(8,128)(2,1)S(1)}, u32[]{:S(2)}, u32[]{:S(2)}) collective-permute-start(bf16[1,208,512]{2,1,0:T(8,128)(2,1)S(1)} %get-tuple-element.288.refs_6_), channel_id=1, source_target_pairs={{0,2},{1,5},{2,6},{3,1},{4,0},{5,9},{6,10},{7,3},{8,4},{9,13},{10,... | collective-permute-start | bytes 638984 | tf_op jit(solution)/shard_map/ppermute | solution.py:904
  109.1 1.3 collective-permute-done.35.refs_0_
  110.4 1.4 collective-permute-start.40
  112.5 1.5 %collective-permute-done.34.refs_1_ = bf16[1,208,512]{2,1,0:T(8,128)(2,1)S(1)} collective-permute-done((bf16[1,208,512]{2,1,0:T(8,128)(2,1)S(1)}, bf16[1,208,512]{2,1,0:T(8,128)(2,1)S(1)}, u32[]{:S(2)}, u32[]{:S(2)}) %collective-permute-start.34) | collective-permute-done | bytes 213024 | tf_op jit(solution)/shard_map/ppermute | solution.py:904
  115.1 1.7 %collective-permute-start.38 = (bf16[1,208,512]{2,1,0:T(8,128)(2,1)S(1)}, bf16[1,208,512]{2,1,0:T(8,128)(2,1)S(1)}, u32[]{:S(2)}, u32[]{:S(2)}) collective-permute-start(bf16[1,208,512]{2,1,0:T(8,128)(2,1)S(1)} %get-tuple-element.287.refs_5_), channel_id=1, source_target_pairs={{0,2},{1,5},{2,6},{3,1},{4,0},{5,9},{6,10},{7,3},{8,4},{9,13},{10,... | collective-permute-start | bytes 638984 | tf_op jit(solution)/shard_map/ppermute | solution.py:904
  119.5 1.5 %collective-permute-start.43 = (bf16[1,192,512]{2,1,0:T(8,128)(2,1)S(1)}, bf16[1,192,512]{2,1,0:T(8,128)(2,1)S(1)}, u32[]{:S(2)}, u32[]{:S(2)}) collective-permute-start(bf16[1,192,512]{2,1,0:T(8,128)(2,1)S(1)} %get-tuple-element.295.refs_5_), channel_id=1, source_target_pairs={{0,2},{1,5},{2,6},{3,1},{4,0},{5,9},{6,10},{7,3},{8,4},{9,13},{10,... | collective-permute-start | bytes 589832 | tf_op jit(solution)/shard_map/ppermute | solution.py:904
  121.6 1.7 %collective-permute-done.38.refs_1_ = bf16[1,208,512]{2,1,0:T(8,128)(2,1)S(1)} collective-permute-done((bf16[1,208,512]{2,1,0:T(8,128)(2,1)S(1)}, bf16[1,208,512]{2,1,0:T(8,128)(2,1)S(1)}, u32[]{:S(2)}, u32[]{:S(2)}) %collective-permute-start.38) | collective-permute-done | bytes 213024 | tf_op jit(solution)/shard_map/ppermute | solution.py:904
  123.7 2.2 %collective-permute-done.43.refs_1_ = bf16[1,192,512]{2,1,0:T(8,128)(2,1)S(1)} collective-permute-done((bf16[1,192,512]{2,1,0:T(8,128)(2,1)S(1)}, bf16[1,192,512]{2,1,0:T(8,128)(2,1)S(1)}, u32[]{:S(2)}, u32[]{:S(2)}) %collective-permute-start.43) | collective-permute-done | bytes 196640 | tf_op jit(solution)/shard_map/ppermute | solution.py:904
  129.6 2.8 %shard_map.330 = (f32[2048,512]{1,0:T(8,128)}, f32[512,2048]{1,0:T(8,128)}, f32[512,1536]{1,0:T(8,128)}, f32[512,512]{1,0:T(8,128)}, f32[512,128]{1,0:T(8,128)}) custom-call(bf16[7,208,512]{2,1,0:T(8,128)(2,1)S(1)} %shard_map.328.refs_0_, bf16[7,192,512]{2,1,0:T(8,128)(2,1)S(1)} %shard_map.329.refs_1_.refs_4_), custom_call_target="tpu_custom_call" | custom-call | tf_op jit(solution)/shard_map/pallas_call | solution.py:869
  132.4 2.8 %shard_map.331 = (f32[2048,512]{1,0:T(8,128)}, f32[512,2048]{1,0:T(8,128)}, f32[512,1536]{1,0:T(8,128)}, f32[512,512]{1,0:T(8,128)}, f32[512,128]{1,0:T(8,128)}) custom-call(bf16[7,208,512]{2,1,0:T(8,128)(2,1)S(1)} %collective-permute-done.44.refs_0_, ...), custom_call_target="tpu_custom_call", output_to_operand_aliasing={{0}: (2, {}), {1}: (3, {}), {2}: (4, {}), {3}: (5, {}), {4}... | custom-call | tf_op jit(solution)/shard_map/pallas_call | solution.py:869
  137.4 1.9 %shard_map.336 = (f32[2048,512]{1,0:T(8,128)}, f32[512,2048]{1,0:T(8,128)}, f32[512,1536]{1,0:T(8,128)}, f32[512,512]{1,0:T(8,128)}, f32[512,128]{1,0:T(8,128)},...) custom-call(bf16[1,208,512]{2,1,0:T(8,128)(2,1)S(1)} %shard_map.334., ...), custom_call_target="tpu_custom_call", output_to_operand_aliasing={{0}: (8, {}), {1}: (9, {}), {2}: (10, {}), {3}: (11, {}), {... | custom-call | tf_op jit(solution)/shard_map/pallas_call | solution.py:869
  (130 shorter events, 30.8 us)
Async XLA Ops:
  7.3 5.3 %collective-permute-start = (bf16[272,128]{1,0:T(8,128)(2,1)S(1)}, bf16[272,128]{1,0:T(8,128)(2,1)S(1)}, u32[]{:S(2)}, u32[]{:S(2)}) collective-permute-start(bf16[272,128]{1,0:T(8,128)(2,1)S(1)} %get-tuple-element.175), channel_id=1, source_target_pairs={{0,16},{16,0},{1,17},{17,1},{2,18},{18,2},{3,19},{19,3},{4,20},{20... | collective-permute-start | bytes 208904 | tf_op jit(solution)/shard_map/ppermute | solution.py:885
  12.6 5.4 %collective-permute-start.2 = (bf16[256,128]{1,0:T(8,128)(2,1)S(1)}, bf16[256,128]{1,0:T(8,128)(2,1)S(1)}, u32[]{:S(2)}, u32[]{:S(2)}) collective-permute-start(bf16[256,128]{1,0:T(8,128)(2,1)S(1)} %slice_select_fusion.here_ref), channel_id=1, source_target_pairs={{0,8},{1,9},{2,10},{3,11},{4,12},{5,13},{6,14},{7,15},{8,0},{9,1},... | collective-permute-start | bytes 196616 | tf_op jit(solution)/shard_map/ppermute | solution.py:885
  15.8 4.4 %collective-permute-start.1 = (bf16[272,128]{1,0:T(8,128)(2,1)S(1)}, bf16[272,128]{1,0:T(8,128)(2,1)S(1)}, u32[]{:S(2)}, u32[]{:S(2)}) collective-permute-start(bf16[272,128]{1,0:T(8,128)(2,1)S(1)} %broadcast_select_fusion), channel_id=1, source_target_pairs={{0,2},{1,3},{2,0},{3,1},{4,6},{5,7},{6,4},{7,5},{8,10},{9,11},{10,... | collective-permute-start | bytes 208904 | tf_op jit(solution)/shard_map/ppermute | solution.py:885
  20.2 4.6 %collective-permute-start.3 = (bf16[544,128]{1,0:T(8,128)(2,1)S(1)}, bf16[544,128]{1,0:T(8,128)(2,1)S(1)}, u32[]{:S(2)}, u32[]{:S(2)}) collective-permute-start(bf16[544,128]{1,0:T(8,128)(2,1)S(1)} %pad_maximum_fusion.near_ref), channel_id=1, source_target_pairs={{0,1},{1,0},{2,3},{3,2},{4,5},{5,4},{6,7},{7,6},{8,9},{9,8},{10,11... | collective-permute-start | bytes 417800 | tf_op jit(solution)/shard_map/ppermute | solution.py:885
  20.3 4.5 %collective-permute-start.4 = (bf16[256,128]{1,0:T(8,128)(2,1)S(1)}, bf16[256,128]{1,0:T(8,128)(2,1)S(1)}, u32[]{:S(2)}, u32[]{:S(2)}) collective-permute-start(bf16[256,128]{1,0:T(8,128)(2,1)S(1)} %shard_map.299.refs_0_), channel_id=1, source_target_pairs={{0,4},{1,5},{2,6},{3,7},{4,0},{5,1},{6,2},{7,3},{8,12},{9,13},{10,... | collective-permute-start | bytes 196616 | tf_op jit(solution)/shard_map/ppermute | solution.py:885
  28.8 5.0 %collective-permute-start.8 = (f32[32,128]{1,0:T(8,128)S(1)}, f32[32,128]{1,0:T(8,128)S(1)}, u32[]{:S(2)}, u32[]{:S(2)}) collective-permute-start(f32[32,128]{1,0:T(8,128)S(1)} %add.3.own_ref), channel_id=1, source_target_pairs={{0,18},{1,19},{2,16},{3,17},{4,22},{5,23},{6,20},{7,21},{8,26},{9,... | collective-permute-start | bytes 49160 | tf_op jit(solution)/shard_map/ppermute | solution.py:1127
  31.3 3.7 %collective-permute-start.7 = (f32[32,128]{1,0:T(8,128)S(1)}, f32[32,128]{1,0:T(8,128)S(1)}, u32[]{:S(2)}, u32[]{:S(2)}) collective-permute-start(f32[32,128]{1,0:T(8,128)S(1)} %add.3.own_ref), channel_id=1, source_target_pairs={{0,16},{16,0},{1,17},{17,1},{2,18},{18,2},{3,19},{19,3},{4,20},{20... | collective-permute-start | bytes 49160 | tf_op jit(solution)/shard_map/ppermute | solution.py:885
  31.8 3.7 %collective-permute-start.6 = (f32[32,128]{1,0:T(8,128)S(1)}, f32[32,128]{1,0:T(8,128)S(1)}, u32[]{:S(2)}, u32[]{:S(2)}) collective-permute-start(f32[32,128]{1,0:T(8,128)S(1)} %add.3.own_ref), channel_id=1, source_target_pairs={{0,2},{1,3},{2,0},{3,1},{4,6},{5,7},{6,4},{7,5},{8,10},{9,11},{10,... | collective-permute-start | bytes 49160 | tf_op jit(solution)/shard_map/ppermute | solution.py:885
  39.2 1.7 %collective-permute-start.9 = (bf16[512,128]{1,0:T(8,128)(2,1)S(1)}, bf16[512,128]{1,0:T(8,128)(2,1)S(1)}, u32[]{:S(2)}, u32[]{:S(2)}) collective-permute-start(bf16[512,128]{1,0:T(8,128)(2,1)S(1)} %get-tuple-element.194), channel_id=1, source_target_pairs={{0,1},{1,0},{2,3},{3,2},{4,5},{5,4},{6,7},{7,6},{8,9},{9,8},{10,11... | collective-permute-start | bytes 393224 | tf_op jit(solution)/shard_map/ppermute | solution.py:885
  39.2 4.5 %collective-permute-start.11 = (bf16[256,128]{1,0:T(8,128)(2,1)S(1)}, bf16[256,128]{1,0:T(8,128)(2,1)S(1)}, u32[]{:S(2)}, u32[]{:S(2)}) collective-permute-start(bf16[256,128]{1,0:T(8,128)(2,1)S(1)} %get-tuple-element.196), channel_id=1, source_target_pairs={{0,4},{1,5},{2,6},{3,7},{4,0},{5,1},{6,2},{7,3},{8,12},{9,13},{10,... | collective-permute-start | bytes 196616 | tf_op jit(solution)/shard_map/ppermute | solution.py:885
  43.8 5.6 %collective-permute-start.12 = (bf16[256,128]{1,0:T(8,128)(2,1)S(1)}, bf16[256,128]{1,0:T(8,128)(2,1)S(1)}, u32[]{:S(2)}, u32[]{:S(2)}) collective-permute-start(bf16[256,128]{1,0:T(8,128)(2,1)S(1)} %shard_map.304.rows_ref), channel_id=1, source_target_pairs={{0,8},{1,9},{2,10},{3,11},{4,12},{5,13},{6,14},{7,15},{8,0},{9,1},... | collective-permute-start | bytes 196616 | tf_op jit(solution)/shard_map/ppermute | solution.py:885
  45.1 4.4 %collective-permute-start.10 = (bf16[256,128]{1,0:T(8,128)(2,1)S(1)}, bf16[256,128]{1,0:T(8,128)(2,1)S(1)}, u32[]{:S(2)}, u32[]{:S(2)}) collective-permute-start(bf16[256,128]{1,0:T(8,128)(2,1)S(1)} %get-tuple-element.334), channel_id=1, source_target_pairs={{0,2},{1,3},{2,0},{3,1},{4,6},{5,7},{6,4},{7,5},{8,10},{9,11},{10,... | collective-permute-start | bytes 196616 | tf_op jit(solution)/shard_map/ppermute | solution.py:885
  49.5 4.3 %collective-permute-start.13 = (bf16[256,128]{1,0:T(8,128)(2,1)S(1)}, bf16[256,128]{1,0:T(8,128)(2,1)S(1)}, u32[]{:S(2)}, u32[]{:S(2)}) collective-permute-start(bf16[256,128]{1,0:T(8,128)(2,1)S(1)} %broadcast_select_fusion.1), channel_id=1, source_target_pairs={{0,16},{16,0},{1,17},{17,1},{2,18},{18,2},{3,19},{19,3},{4,20},{20... | collective-permute-start | bytes 196616 | tf_op jit(solution)/shard_map/ppermute | solution.py:885
  59.0 4.5 %collective-permute-start.14 = (bf16[8,208,512]{2,1,0:T(8,128)(2,1)S(1)}, bf16[8,208,512]{2,1,0:T(8,128)(2,1)S(1)}, u32[]{:S(2)}, u32[]{:S(2)}) collective-permute-start(bf16[8,208,512]{2,1,0:T(8,128)(2,1)S(1)} %get-tuple-element.205), channel_id=1, source_target_pairs={{0,1},{1,0},{2,3},{3,2},{4,5},{5,4},{6,7},{7,6},{8,9},{9,8},{10,11... | collective-permute-start | bytes 5111816 | tf_op jit(solution)/shard_map/ppermute | solution.py:885
  62.8 6.1 %collective-permute-start.18 = (bf16[6,192,512]{2,1,0:T(8,128)(2,1)S(1)}, bf16[6,192,512]{2,1,0:T(8,128)(2,1)S(1)}, u32[]{:S(2)}, u32[]{:S(2)}) collective-permute-start(bf16[6,192,512]{2,1,0:T(8,128)(2,1)S(1)} %get-tuple-element.229), channel_id=1, source_target_pairs={{0,1},{1,0},{2,3},{3,2},{4,5},{5,4},{6,7},{7,6},{8,9},{9,8},{10,11... | collective-permute-start | bytes 3538952 | tf_op jit(solution)/shard_map/ppermute | solution.py:885
  63.4 3.0 %collective-permute-start.17 = (bf16[2,192,512]{2,1,0:T(8,128)(2,1)S(1)}, bf16[2,192,512]{2,1,0:T(8,128)(2,1)S(1)}, u32[]{:S(2)}, u32[]{:S(2)}) collective-permute-start(bf16[2,192,512]{2,1,0:T(8,128)(2,1)S(1)} %get-tuple-element.223), channel_id=1, source_target_pairs={{0,1},{1,0},{2,3},{3,2},{4,5},{5,4},{6,7},{7,6},{8,9},{9,8},{10,11... | collective-permute-start | bytes 1179656 | tf_op jit(solution)/shard_map/ppermute | solution.py:885
  63.6 8.2 %collective-permute-start.15 = (bf16[1,208,512]{2,1,0:T(8,128)(2,1)S(1)}, bf16[1,208,512]{2,1,0:T(8,128)(2,1)S(1)}, u32[]{:S(2)}, u32[]{:S(2)}) collective-permute-start(bf16[1,208,512]{2,1,0:T(8,128)(2,1)S(1)} %get-tuple-element.220), channel_id=1, source_target_pairs={{0,4},{1,3},{2,0},{3,7},{4,8},{5,1},{6,2},{7,11},{8,12},{9,5},{10,... | collective-permute-start | bytes 638984 | tf_op jit(solution)/shard_map/ppermute | solution.py:904
  65.3 6.4 %collective-permute-start.16 = (bf16[1,208,512]{2,1,0:T(8,128)(2,1)S(1)}, bf16[1,208,512]{2,1,0:T(8,128)(2,1)S(1)}, u32[]{:S(2)}, u32[]{:S(2)}) collective-permute-start(bf16[1,208,512]{2,1,0:T(8,128)(2,1)S(1)} %get-tuple-element.221), channel_id=1, source_target_pairs={{0,2},{1,5},{2,6},{3,1},{4,0},{5,9},{6,10},{7,3},{8,4},{9,13},{10,... | collective-permute-start | bytes 638984 | tf_op jit(solution)/shard_map/ppermute | solution.py:904
  66.5 9.4 %collective-permute-start.22 = (bf16[1,192,512]{2,1,0:T(8,128)(2,1)S(1)}, bf16[1,192,512]{2,1,0:T(8,128)(2,1)S(1)}, u32[]{:S(2)}, u32[]{:S(2)}) collective-permute-start(bf16[1,192,512]{2,1,0:T(8,128)(2,1)S(1)} %get-tuple-element.226), channel_id=1, source_target_pairs={{0,2},{1,5},{2,6},{3,1},{4,0},{5,9},{6,10},{7,3},{8,4},{9,13},{10,... | collective-permute-start | bytes 589832 | tf_op jit(solution)/shard_map/ppermute | solution.py:904
  67.1 8.9 %collective-permute-start.21 = (bf16[1,192,512]{2,1,0:T(8,128)(2,1)S(1)}, bf16[1,192,512]{2,1,0:T(8,128)(2,1)S(1)}, u32[]{:S(2)}, u32[]{:S(2)}) collective-permute-start(bf16[1,192,512]{2,1,0:T(8,128)(2,1)S(1)} %get-tuple-element.236), channel_id=1, source_target_pairs={{0,4},{1,3},{2,0},{3,7},{4,8},{5,1},{6,2},{7,11},{8,12},{9,5},{10,... | collective-permute-start | bytes 589832 | tf_op jit(solution)/shard_map/ppermute | solution.py:904
  71.8 8.3 %collective-permute-start.20 = (bf16[1,208,512]{2,1,0:T(8,128)(2,1)S(1)}, bf16[1,208,512]{2,1,0:T(8,128)(2,1)S(1)}, u32[]{:S(2)}, u32[]{:S(2)}) collective-permute-start(bf16[1,208,512]{2,1,0:T(8,128)(2,1)S(1)} %get-tuple-element.235), channel_id=1, source_target_pairs={{0,2},{1,5},{2,6},{3,1},{4,0},{5,9},{6,10},{7,3},{8,4},{9,13},{10,... | collective-permute-start | bytes 638984 | tf_op jit(solution)/shard_map/ppermute | solution.py:904
  72.4 8.2 %collective-permute-start.19 = (bf16[1,208,512]{2,1,0:T(8,128)(2,1)S(1)}, bf16[1,208,512]{2,1,0:T(8,128)(2,1)S(1)}, u32[]{:S(2)}, u32[]{:S(2)}) collective-permute-start(bf16[1,208,512]{2,1,0:T(8,128)(2,1)S(1)} %get-tuple-element.234), channel_id=1, source_target_pairs={{0,4},{1,3},{2,0},{3,7},{4,8},{5,1},{6,2},{7,11},{8,12},{9,5},{10,... | collective-permute-start | bytes 638984 | tf_op jit(solution)/shard_map/ppermute | solution.py:904
  76.0 8.3 %collective-permute-start.26 = (bf16[1,192,512]{2,1,0:T(8,128)(2,1)S(1)}, bf16[1,192,512]{2,1,0:T(8,128)(2,1)S(1)}, u32[]{:S(2)}, u32[]{:S(2)}) collective-permute-start(bf16[1,192,512]{2,1,0:T(8,128)(2,1)S(1)} %get-tuple-element.244), channel_id=1, source_target_pairs={{0,2},{1,5},{2,6},{3,1},{4,0},{5,9},{6,10},{7,3},{8,4},{9,13},{10,... | collective-permute-start | bytes 589832 | tf_op jit(solution)/shard_map/ppermute | solution.py:904
  76.8 8.0 %collective-permute-start.25 = (bf16[1,192,512]{2,1,0:T(8,128)(2,1)S(1)}, bf16[1,192,512]{2,1,0:T(8,128)(2,1)S(1)}, u32[]{:S(2)}, u32[]{:S(2)}) collective-permute-start(bf16[1,192,512]{2,1,0:T(8,128)(2,1)S(1)} %get-tuple-element.239), channel_id=1, source_target_pairs={{0,4},{1,3},{2,0},{3,7},{4,8},{5,1},{6,2},{7,11},{8,12},{9,5},{10,... | collective-permute-start | bytes 589832 | tf_op jit(solution)/shard_map/ppermute | solution.py:904
  80.7 8.3 %collective-permute-start.24 = (bf16[1,208,512]{2,1,0:T(8,128)(2,1)S(1)}, bf16[1,208,512]{2,1,0:T(8,128)(2,1)S(1)}, u32[]{:S(2)}, u32[]{:S(2)}) collective-permute-start(bf16[1,208,512]{2,1,0:T(8,128)(2,1)S(1)} %get-tuple-element.243), channel_id=1, source_target_pairs={{0,2},{1,5},{2,6},{3,1},{4,0},{5,9},{6,10},{7,3},{8,4},{9,13},{10,... | collective-permute-start | bytes 638984 | tf_op jit(solution)/shard_map/ppermute | solution.py:904
  82.8 7.9 %collective-permute-start.23 = (bf16[1,208,512]{2,1,0:T(8,128)(2,1)S(1)}, bf16[1,208,512]{2,1,0:T(8,128)(2,1)S(1)}, u32[]{:S(2)}, u32[]{:S(2)}) collective-permute-start(bf16[1,208,512]{2,1,0:T(8,128)(2,1)S(1)} %get-tuple-element.242), channel_id=1, source_target_pairs={{0,4},{1,3},{2,0},{3,7},{4,8},{5,1},{6,2},{7,11},{8,12},{9,5},{10,... | collective-permute-start | bytes 638984 | tf_op jit(solution)/shard_map/ppermute | solution.py:904
  84.9 8.3 %collective-permute-start.29 = (bf16[1,192,512]{2,1,0:T(8,128)(2,1)S(1)}, bf16[1,192,512]{2,1,0:T(8,128)(2,1)S(1)}, u32[]{:S(2)}, u32[]{:S(2)}) collective-permute-start(bf16[1,192,512]{2,1,0:T(8,128)(2,1)S(1)} %get-tuple-element.251), channel_id=1, source_target_pairs={{0,2},{1,5},{2,6},{3,1},{4,0},{5,9},{6,10},{7,3},{8,4},{9,13},{10,... | collective-permute-start | bytes 589832 | tf_op jit(solution)/shard_map/ppermute | solution.py:904
  87.0 6.2 %collective-permute-start.28 = (bf16[1,192,512]{2,1,0:T(8,128)(2,1)S(1)}, bf16[1,192,512]{2,1,0:T(8,128)(2,1)S(1)}, u32[]{:S(2)}, u32[]{:S(2)}) collective-permute-start(bf16[1,192,512]{2,1,0:T(8,128)(2,1)S(1)} %get-tuple-element.247), channel_id=1, source_target_pairs={{0,4},{1,3},{2,0},{3,7},{4,8},{5,1},{6,2},{7,11},{8,12},{9,5},{10,... | collective-permute-start | bytes 589832 | tf_op jit(solution)/shard_map/ppermute | solution.py:904
  90.8 5.9 %collective-permute-start.27 = (bf16[1,208,512]{2,1,0:T(8,128)(2,1)S(1)}, bf16[1,208,512]{2,1,0:T(8,128)(2,1)S(1)}, u32[]{:S(2)}, u32[]{:S(2)}) collective-permute-start(bf16[1,208,512]{2,1,0:T(8,128)(2,1)S(1)} %get-tuple-element.250), channel_id=1, source_target_pairs={{0,4},{1,3},{2,0},{3,7},{4,8},{5,1},{6,2},{7,11},{8,12},{9,5},{10,... | collective-permute-start | bytes 638984 | tf_op jit(solution)/shard_map/ppermute | solution.py:904
  93.3 6.6 %collective-permute-start.32 = (bf16[1,192,512]{2,1,0:T(8,128)(2,1)S(1)}, bf16[1,192,512]{2,1,0:T(8,128)(2,1)S(1)}, u32[]{:S(2)}, u32[]{:S(2)}) collective-permute-start(bf16[1,192,512]{2,1,0:T(8,128)(2,1)S(1)} %get-tuple-element.254), channel_id=1, source_target_pairs={{0,4},{1,3},{2,0},{3,7},{4,8},{5,1},{6,2},{7,11},{8,12},{9,5},{10,... | collective-permute-start | bytes 589832 | tf_op jit(solution)/shard_map/ppermute | solution.py:904
  96.7 8.1 %collective-permute-start.31 = (bf16[1,208,512]{2,1,0:T(8,128)(2,1)S(1)}, bf16[1,208,512]{2,1,0:T(8,128)(2,1)S(1)}, u32[]{:S(2)}, u32[]{:S(2)}) collective-permute-start(bf16[1,208,512]{2,1,0:T(8,128)(2,1)S(1)} %shard_map.320.refs_0_), channel_id=1, source_target_pairs={{0,2},{1,5},{2,6},{3,1},{4,0},{5,9},{6,10},{7,3},{8,4},{9,13},{10,... | collective-permute-start | bytes 638984 | tf_op jit(solution)/shard_map/ppermute | solution.py:904
  97.5 8.2 %collective-permute-start.30 = (bf16[1,208,512]{2,1,0:T(8,128)(2,1)S(1)}, bf16[1,208,512]{2,1,0:T(8,128)(2,1)S(1)}, u32[]{:S(2)}, u32[]{:S(2)}) collective-permute-start(bf16[1,208,512]{2,1,0:T(8,128)(2,1)S(1)} %shard_map.320.refs_0_), channel_id=1, source_target_pairs={{0,4},{1,3},{2,0},{3,7},{4,8},{5,1},{6,2},{7,11},{8,12},{9,5},{10,... | collective-permute-start | bytes 638984 | tf_op jit(solution)/shard_map/ppermute | solution.py:904
  99.9 9.1 %collective-permute-start.36 = (bf16[1,192,512]{2,1,0:T(8,128)(2,1)S(1)}, bf16[1,192,512]{2,1,0:T(8,128)(2,1)S(1)}, u32[]{:S(2)}, u32[]{:S(2)}) collective-permute-start(bf16[1,192,512]{2,1,0:T(8,128)(2,1)S(1)} %shard_map.321.refs_0_), channel_id=1, source_target_pairs={{0,2},{1,5},{2,6},{3,1},{4,0},{5,9},{6,10},{7,3},{8,4},{9,13},{10,... | collective-permute-start | bytes 589832 | tf_op jit(solution)/shard_map/ppermute | solution.py:904
  102.6 7.8 %collective-permute-start.35 = (bf16[1,192,512]{2,1,0:T(8,128)(2,1)S(1)}, bf16[1,192,512]{2,1,0:T(8,128)(2,1)S(1)}, u32[]{:S(2)}, u32[]{:S(2)}) collective-permute-start(bf16[1,192,512]{2,1,0:T(8,128)(2,1)S(1)} %shard_map.321.refs_0_), channel_id=1, source_target_pairs={{0,4},{1,3},{2,0},{3,7},{4,8},{5,1},{6,2},{7,11},{8,12},{9,5},{10,... | collective-permute-start | bytes 589832 | tf_op jit(solution)/shard_map/ppermute | solution.py:904
  105.7 8.2 %collective-permute-start.34 = (bf16[1,208,512]{2,1,0:T(8,128)(2,1)S(1)}, bf16[1,208,512]{2,1,0:T(8,128)(2,1)S(1)}, u32[]{:S(2)}, u32[]{:S(2)}) collective-permute-start(bf16[1,208,512]{2,1,0:T(8,128)(2,1)S(1)} %get-tuple-element.288.refs_6_), channel_id=1, source_target_pairs={{0,2},{1,5},{2,6},{3,1},{4,0},{5,9},{6,10},{7,3},{8,4},{9,13},{10,... | collective-permute-start | bytes 638984 | tf_op jit(solution)/shard_map/ppermute | solution.py:904
  107.6 7.5 %collective-permute-start.33 = (bf16[1,208,512]{2,1,0:T(8,128)(2,1)S(1)}, bf16[1,208,512]{2,1,0:T(8,128)(2,1)S(1)}, u32[]{:S(2)}, u32[]{:S(2)}) collective-permute-start(bf16[1,208,512]{2,1,0:T(8,128)(2,1)S(1)} %get-tuple-element.283.refs_1_), channel_id=1, source_target_pairs={{0,4},{1,3},{2,0},{3,7},{4,8},{5,1},{6,2},{7,11},{8,12},{9,5},{10,... | collective-permute-start | bytes 638984 | tf_op jit(solution)/shard_map/ppermute | solution.py:904
  110.4 7.9 %collective-permute-start.40 = (bf16[1,192,512]{2,1,0:T(8,128)(2,1)S(1)}, bf16[1,192,512]{2,1,0:T(8,128)(2,1)S(1)}, u32[]{:S(2)}, u32[]{:S(2)}) collective-permute-start(bf16[1,192,512]{2,1,0:T(8,128)(2,1)S(1)} %get-tuple-element.296.refs_6_), channel_id=1, source_target_pairs={{0,2},{1,5},{2,6},{3,1},{4,0},{5,9},{6,10},{7,3},{8,4},{9,13},{10,... | collective-permute-start | bytes 589832 | tf_op jit(solution)/shard_map/ppermute | solution.py:904
  111.8 7.7 %collective-permute-start.39 = (bf16[1,192,512]{2,1,0:T(8,128)(2,1)S(1)}, bf16[1,192,512]{2,1,0:T(8,128)(2,1)S(1)}, u32[]{:S(2)}, u32[]{:S(2)}) collective-permute-start(bf16[1,192,512]{2,1,0:T(8,128)(2,1)S(1)} %get-tuple-element.291.refs_1_), channel_id=1, source_target_pairs={{0,4},{1,3},{2,0},{3,7},{4,8},{5,1},{6,2},{7,11},{8,12},{9,5},{10,... | collective-permute-start | bytes 589832 | tf_op jit(solution)/shard_map/ppermute | solution.py:904
  115.1 8.2 %collective-permute-start.38 = (bf16[1,208,512]{2,1,0:T(8,128)(2,1)S(1)}, bf16[1,208,512]{2,1,0:T(8,128)(2,1)S(1)}, u32[]{:S(2)}, u32[]{:S(2)}) collective-permute-start(bf16[1,208,512]{2,1,0:T(8,128)(2,1)S(1)} %get-tuple-element.287.refs_5_), channel_id=1, source_target_pairs={{0,2},{1,5},{2,6},{3,1},{4,0},{5,9},{6,10},{7,3},{8,4},{9,13},{10,... | collective-permute-start | bytes 638984 | tf_op jit(solution)/shard_map/ppermute | solution.py:904
  116.8 6.8 %collective-permute-start.37 = (bf16[1,208,512]{2,1,0:T(8,128)(2,1)S(1)}, bf16[1,208,512]{2,1,0:T(8,128)(2,1)S(1)}, u32[]{:S(2)}, u32[]{:S(2)}) collective-permute-start(bf16[1,208,512]{2,1,0:T(8,128)(2,1)S(1)} %get-tuple-element.284.refs_2_), channel_id=1, source_target_pairs={{0,4},{1,3},{2,0},{3,7},{4,8},{5,1},{6,2},{7,11},{8,12},{9,5},{10,... | collective-permute-start | bytes 638984 | tf_op jit(solution)/shard_map/ppermute | solution.py:904
  119.5 6.3 %collective-permute-start.43 = (bf16[1,192,512]{2,1,0:T(8,128)(2,1)S(1)}, bf16[1,192,512]{2,1,0:T(8,128)(2,1)S(1)}, u32[]{:S(2)}, u32[]{:S(2)}) collective-permute-start(bf16[1,192,512]{2,1,0:T(8,128)(2,1)S(1)} %get-tuple-element.295.refs_5_), channel_id=1, source_target_pairs={{0,2},{1,5},{2,6},{3,1},{4,0},{5,9},{6,10},{7,3},{8,4},{9,13},{10,... | collective-permute-start | bytes 589832 | tf_op jit(solution)/shard_map/ppermute | solution.py:904
  121.0 5.7 %collective-permute-start.42 = (bf16[1,192,512]{2,1,0:T(8,128)(2,1)S(1)}, bf16[1,192,512]{2,1,0:T(8,128)(2,1)S(1)}, u32[]{:S(2)}, u32[]{:S(2)}) collective-permute-start(bf16[1,192,512]{2,1,0:T(8,128)(2,1)S(1)} %get-tuple-element.292.refs_2_), channel_id=1, source_target_pairs={{0,4},{1,3},{2,0},{3,7},{4,8},{5,1},{6,2},{7,11},{8,12},{9,5},{10,... | collective-permute-start | bytes 589832 | tf_op jit(solution)/shard_map/ppermute | solution.py:904
  126.9 5.5 %collective-permute-start.44 = (bf16[7,208,512]{2,1,0:T(8,128)(2,1)S(1)}, bf16[7,208,512]{2,1,0:T(8,128)(2,1)S(1)}, u32[]{:S(2)}, u32[]{:S(2)}) collective-permute-start(bf16[7,208,512]{2,1,0:T(8,128)(2,1)S(1)} %shard_map.328.refs_0_), channel_id=1, source_target_pairs={{0,1},{1,0},{2,3},{3,2},{4,5},{5,4},{6,7},{7,6},{8,9},{9,8},{10,11... | collective-permute-start | bytes 4472840 | tf_op jit(solution)/shard_map/ppermute | solution.py:885
  127.0 5.3 %collective-permute-start.45 = (bf16[7,192,512]{2,1,0:T(8,128)(2,1)S(1)}, bf16[7,192,512]{2,1,0:T(8,128)(2,1)S(1)}, u32[]{:S(2)}, u32[]{:S(2)}) collective-permute-start(bf16[7,192,512]{2,1,0:T(8,128)(2,1)S(1)} %shard_map.329.refs_1_.refs_4_), channel_id=1, source_target_pairs={{0,1},{1,0},{2,3},{3,2},{4,5},{5,4},{6,7},{7,6},{8,9},{9,8},{10,11... | collective-permute-start | bytes 4128776 | tf_op jit(solution)/shard_map/ppermute | solution.py:885
  127.6 7.6 %collective-permute-start.41 = (bf16[1,208,512]{2,1,0:T(8,128)(2,1)S(1)}, bf16[1,208,512]{2,1,0:T(8,128)(2,1)S(1)}, u32[]{:S(2)}, u32[]{:S(2)}) collective-permute-start(bf16[1,208,512]{2,1,0:T(8,128)(2,1)S(1)} %get-tuple-element.285.refs_3_), channel_id=1, source_target_pairs={{0,4},{1,3},{2,0},{3,7},{4,8},{5,1},{6,2},{7,11},{8,12},{9,5},{10,... | collective-permute-start | bytes 638984 | tf_op jit(solution)/shard_map/ppermute | solution.py:904
  128.3 7.3 %collective-permute-start.46 = (bf16[1,192,512]{2,1,0:T(8,128)(2,1)S(1)}, bf16[1,192,512]{2,1,0:T(8,128)(2,1)S(1)}, u32[]{:S(2)}, u32[]{:S(2)}) collective-permute-start(bf16[1,192,512]{2,1,0:T(8,128)(2,1)S(1)} %get-tuple-element.293.refs_3_), channel_id=1, source_target_pairs={{0,4},{1,3},{2,0},{3,7},{4,8},{5,1},{6,2},{7,11},{8,12},{9,5},{10,... | collective-permute-start | bytes 589832 | tf_op jit(solution)/shard_map/ppermute | solution.py:904
  135.6 1.8 %collective-permute-start.47 = (bf16[1,208,512]{2,1,0:T(8,128)(2,1)S(1)}, bf16[1,208,512]{2,1,0:T(8,128)(2,1)S(1)}, u32[]{:S(2)}, u32[]{:S(2)}) collective-permute-start(bf16[1,208,512]{2,1,0:T(8,128)(2,1)S(1)} %shard_map.334.refs_0_), channel_id=1, source_target_pairs={{0,1},{1,0},{2,3},{3,2},{4,5},{5,4},{6,7},{7,6},{8,9},{9,8},{10,11... | collective-permute-start | bytes 638984 | tf_op jit(solution)/shard_map/ppermute | solution.py:885
  135.7 1.7 %collective-permute-start.48 = (bf16[1,192,512]{2,1,0:T(8,128)(2,1)S(1)}, bf16[1,192,512]{2,1,0:T(8,128)(2,1)S(1)}, u32[]{:S(2)}, u32[]{:S(2)}) collective-permute-start(bf16[1,192,512]{2,1,0:T(8,128)(2,1)S(1)} %shard_map.335.refs_1_.refs_5_), channel_id=1, source_target_pairs={{0,1},{1,0},{2,3},{3,2},{4,5},{5,4},{6,7},{7,6},{8,9},{9,8},{10,11... | collective-permute-start | bytes 589832 | tf_op jit(solution)/shard_map/ppermute | solution.py:885
  (18 other events, 155.1 us)

commit v9 on v8

--- a/solution.py
+++ b/solution.py
@@ -45,7 +45,7 @@
 ORDER = (
     (("open", 0), ("open", 1), ("total", 0), ("total", 1), ("tokens", 0)) + ROUND * 7
     + (("share", 0, 0), ("share", 1, 0), ("spread", ((True, 0),)), ("spread", ((False, 0),))) + ROUND
-    + (("share", 0, 1), ("share", 1, 1), ("spread", ((True, 1), (False, 1))))
+    + (("share", 0, 1), ("share", 1, 1), ("spread", ((True, 1),)), ("spread", ((False, 1),)))
 )
 MIB = 1024 * 1024
 
@@ -270,8 +270,7 @@
     first_low = first.astype(BF16)
     branch = bdown_ref[...].astype(F32) + first
     step = 512
-    for copy in copies[12:]:
-        copy.wait()
+    copies[12].wait()
     for c in range(FF // step):
         cols = slice(c * step, (c + 1) * step)
         inner = mm(first_low, wup_ref[:, cols]) + bup_ref[:, cols].astype(F32)
@@ -280,11 +279,14 @@
         act = (inner * gate).astype(BF16)
         act_ref[:, cols] = act
         slope_ref[:, cols] = (gate + inner * bell).astype(BF16)
+        if c == 0:
+            copies[13].wait()
         branch = branch + mm(act, wdown_ref[cols, :])
     xhat, rstd = norm_rows(branch)
     xh2_ref[...] = xhat
     rs2_ref[...] = jnp.broadcast_to(rstd, (ROW, 128))
     second = xhat * g2_ref[...].astype(F32) + s2_ref[...].astype(F32)
+    copies[14].wait()
     vec_ref[:ROW, :] = mm(second.astype(BF16), wproj_ref[...]).astype(BF16)
     line = iota((EXT, PROJ), 0)
     tag = jnp.zeros((EXT, PROJ), jnp.int32)

time: 140 us -> 140 us (level)
    pallas_call x40 -> x41, Pallas kernels: 35.5 us -> 36.3 us  [call(): pl.pallas_call(kernel, out_shape=outs, in_specs=specs, out_specs=out_spec...]
  transfers between devices with their start and end apart: 49 -> 49, of which waited for: 35 -> 35; matrix products, arithmetic and copies ran while one was open for 0% -> 0% of each run, Pallas kernels for 11% -> 12%
where the time goes in v9:
time: 140 us; the launch traced here: 139 us
  starting transfers between devices  50.8 us (36%)
  waiting for transfers between devices  49 us (35%)
  Pallas kernels  36.3 us (26%)
  between operations  2.03 us (1%)
    pallas_call x41, Pallas kernels, call(): pl.pallas_call(kernel, out_shape=outs, in_specs=specs, out_specs=out_spec...  36.3 us
    ppermute x28, starting transfers between devices, ring_swap(): return lax.ppermute(value, 'dp', pairs)  30.5 us
    ppermute x28, waiting for transfers between devices, ring_swap(): return lax.ppermute(value, 'dp', pairs)  30 us
    ppermute x20, waiting for transfers between devices, swapped(): return lax.ppermute(value, axis, [(k, k ^ mask) for k in range(size)])  18.9 us
    ppermute x20, starting transfers between devices, swapped(): return lax.ppermute(value, axis, [(k, k ^ mask) for k in range(size)])  17.9 us
  transfers between devices with their start and end apart: 49, of which 35 were waited for; matrix products, arithmetic and copies ran while one was open for 0% of the time, Pallas kernels for 12%

profile of v9, /device:TPU:0, one launch (start us, length us, event | category | flops | bytes accessed | tf_op | source)
XLA Modules:
  0.0 139.4 jit_solution(9119750309635870942)
XLA Ops:
  0.7 6.8 %shard_map.297 = (bf16[272,128]{1,0:T(8,128)(2,1)S(1)}, bf16[256,2048]{1,0:T(8,128)(2,1)S(1)}, bf16[256,2048]{1,0:T(8,128)(2,1)S(1)}, f32[256,512]{1,0:T(8,128)S...) custom-call(s32[5,16]{1,0:T(8,128)} %bitcast.28, ...), custom_call_target="tpu_custom_call" | custom-call | flops 100000000 | bytes 10000000 | tf_op jit(solution)/shard_map/pallas_call | solution.py:871
  7.5 3.0 %collective-permute-start = (bf16[272,128]{1,0:T(8,128)(2,1)S(1)}, bf16[272,128]{1,0:T(8,128)(2,1)S(1)}, u32[]{:S(2)}, u32[]{:S(2)}) collective-permute-start(bf16[272,128]{1,0:T(8,128)(2,1)S(1)} %get-tuple-element.180), channel_id=1, source_target_pairs={{0,16},{16,0},{1,17},{17,1},{2,18},{18,2},{3,19},{19,3},{4,20},{20... | collective-permute-start | bytes 208904 | tf_op jit(solution)/shard_map/ppermute | solution.py:887
  10.5 1.5 %shard_map.298 = (bf16[256,2048]{1,0:T(8,128)(2,1)}, bf16[256,2048]{1,0:T(8,128)(2,1)}, f32[256,512]{1,0:T(8,128)}, f32[256,128]{1,0:T(8,128)}) custom-call(bf16[256,2048]{1,0:T(8,128)(2,1)S(1)} %get-tuple-element.181.refs_0_, bf16[256,2048]{1,0:T(8,128)(2,1)S(1)} %get-tuple-element.182.refs_1_, f32[256,512]{1,0:T(8,128)S(1)} %get-tuple-element.183.refs_2_, ...), custom_call_target="tpu_custom_call" | custom-call | flops 300000000 | bytes 30000000 | tf_op jit(solution)/shard_map/pallas_call | solution.py:871
  12.8 3.2 %collective-permute-start.2 = (bf16[256,128]{1,0:T(8,128)(2,1)S(1)}, bf16[256,128]{1,0:T(8,128)(2,1)S(1)}, u32[]{:S(2)}, u32[]{:S(2)}) collective-permute-start(bf16[256,128]{1,0:T(8,128)(2,1)S(1)} %slice_select_fusion.here_ref), channel_id=1, source_target_pairs={{0,8},{1,9},{2,10},{3,11},{4,12},{5,13},{6,14},{7,15},{8,0},{9,1},... | collective-permute-start | bytes 196616 | tf_op jit(solution)/shard_map/ppermute | solution.py:887
  16.0 1.6 %collective-permute-start.1 = (bf16[272,128]{1,0:T(8,128)(2,1)S(1)}, bf16[272,128]{1,0:T(8,128)(2,1)S(1)}, u32[]{:S(2)}, u32[]{:S(2)}) collective-permute-start(bf16[272,128]{1,0:T(8,128)(2,1)S(1)} %broadcast_select_fusion), channel_id=1, source_target_pairs={{0,2},{1,3},{2,0},{3,1},{4,6},{5,7},{6,4},{7,5},{8,10},{9,11},{10,... | collective-permute-start | bytes 208904 | tf_op jit(solution)/shard_map/ppermute | solution.py:887
  18.3 2.1 %collective-permute-done.1 = bf16[272,128]{1,0:T(8,128)(2,1)S(1)} collective-permute-done((bf16[272,128]{1,0:T(8,128)(2,1)S(1)}, bf16[272,128]{1,0:T(8,128)(2,1)S(1)}, u32[]{:S(2)}, u32[]{:S(2)}) %collective-permute-start.1) | collective-permute-done | bytes 69664 | tf_op jit(solution)/shard_map/ppermute | solution.py:887
  20.5 1.6 %collective-permute-start.4 = (bf16[256,128]{1,0:T(8,128)(2,1)S(1)}, bf16[256,128]{1,0:T(8,128)(2,1)S(1)}, u32[]{:S(2)}, u32[]{:S(2)}) collective-permute-start(bf16[256,128]{1,0:T(8,128)(2,1)S(1)} %shard_map.299.refs_0_), channel_id=1, source_target_pairs={{0,4},{1,5},{2,6},{3,7},{4,0},{5,1},{6,2},{7,3},{8,12},{9,13},{10,... | collective-permute-start | bytes 196616 | tf_op jit(solution)/shard_map/ppermute | solution.py:887
  22.8 2.2 %collective-permute-done.4.refs_1_ = bf16[256,128]{1,0:T(8,128)(2,1)S(1)} collective-permute-done((bf16[256,128]{1,0:T(8,128)(2,1)S(1)}, bf16[256,128]{1,0:T(8,128)(2,1)S(1)}, u32[]{:S(2)}, u32[]{:S(2)}) %collective-permute-start.4) | collective-permute-done | bytes 65568 | tf_op jit(solution)/shard_map/ppermute | solution.py:887
  25.0 2.8 %shard_map.300 = (f32[1024,128]{1,0:T(8,128)S(1)}, f32[32,128]{1,0:T(8,128)S(1)}, f32[32,128]{1,0:T(8,128)S(1)}, f32[32,128]{1,0:T(8,128)S(1)}) custom-call(f32[1]{0:T(128)} %bitcast.16.scale_ref, s32[5,16]{1,0:T(8,128)S(1)} %bitcast.29, bf16[544,128]{1,0:T(8,128)(2,1)S(1)} %pad_maximum_fusion.near_ref, bf16[544,128]{1,0:T(8,128)(2,1)S(1)} %collective-permute-done.3.far_ref, ...), custom_call_target="tpu_custom_call" | custom-call | flops 100000000 | bytes 10000000 | tf_op jit(solution)/shard_map/pallas_call | solution.py:871
  29.0 2.4 %collective-permute-start.8 = (f32[32,128]{1,0:T(8,128)S(1)}, f32[32,128]{1,0:T(8,128)S(1)}, u32[]{:S(2)}, u32[]{:S(2)}) collective-permute-start(f32[32,128]{1,0:T(8,128)S(1)} %add.3.own_ref), channel_id=1, source_target_pairs={{0,18},{1,19},{2,16},{3,17},{4,22},{5,23},{6,20},{7,21},{8,26},{9,... | collective-permute-start | bytes 49160 | tf_op jit(solution)/shard_map/ppermute | solution.py:1129
  32.5 1.5 %shard_map.301 = (bf16[3,1024,128]{2,1,0:T(8,128)(2,1)S(1)}, bf16[3,128,1024]{2,1,0:T(8,128)(2,1)S(1)}, f32[1024,128]{1,0:T(8,128)S(1)}, bf16[3,128,512]{2,1,0:T...) custom-call(bf16[544,128]{1,0:T(8,128)(2,1)S(1)} %pad_maximum_fusion.near_ref, ...), custom_call_target="tpu_custom_call" | custom-call | flops 100000000 | bytes 10000000 | tf_op jit(solution)/shard_map/pallas_call | solution.py:871
  35.8 3.6 %shard_map.302 = (bf16[512,128]{1,0:T(8,128)(2,1)S(1)}, bf16[512,128]{1,0:T(8,128)(2,1)S(1)}, bf16[256,128]{1,0:T(8,128)(2,1)S(1)}, bf16[256,128]{1,0:T(8,128)(2,1)S(1)}, f32[8,128]{1,0:T(8,128)S(1)}) custom-call(f32[1]{0:T(128)} %bitcast.17.scale_ref, s32[5,16]{1,0:T(8,128)S(1)} %bitcast.30, f32[1024,128]{1,0:T(8,128)S(1)} %get-tuple-element.188.totals_ref, ...), custom_call_target="tpu_custom_call" | custom-call | flops 100000000 | bytes 10000000 | tf_op jit(solution)/shard_map/pallas_call | solution.py:871
  39.4 1.6 %collective-permute-start.11 = (bf16[256,128]{1,0:T(8,128)(2,1)S(1)}, bf16[256,128]{1,0:T(8,128)(2,1)S(1)}, u32[]{:S(2)}, u32[]{:S(2)}) collective-permute-start(bf16[256,128]{1,0:T(8,128)(2,1)S(1)} %get-tuple-element.201), channel_id=1, source_target_pairs={{0,4},{1,5},{2,6},{3,7},{4,0},{5,1},{6,2},{7,3},{8,12},{9,13},{10,... | collective-permute-start | bytes 196616 | tf_op jit(solution)/shard_map/ppermute | solution.py:887
  41.2 2.8 %collective-permute-done.11.got_ref = bf16[256,128]{1,0:T(8,128)(2,1)S(1)} collective-permute-done((bf16[256,128]{1,0:T(8,128)(2,1)S(1)}, bf16[256,128]{1,0:T(8,128)(2,1)S(1)}, u32[]{:S(2)}, u32[]{:S(2)}) %collective-permute-start.11) | collective-permute-done | bytes 65568 | tf_op jit(solution)/shard_map/ppermute | solution.py:887
  44.0 1.3 collective-permute-start.12
  45.8 3.8 %collective-permute-done.12.got_ref = bf16[256,128]{1,0:T(8,128)(2,1)S(1)} collective-permute-done((bf16[256,128]{1,0:T(8,128)(2,1)S(1)}, bf16[256,128]{1,0:T(8,128)(2,1)S(1)}, u32[]{:S(2)}, u32[]{:S(2)}) %collective-permute-start.12) | collective-permute-done | bytes 65568 | tf_op jit(solution)/shard_map/ppermute | solution.py:887
  49.7 1.7 %collective-permute-start.13 = (bf16[256,128]{1,0:T(8,128)(2,1)S(1)}, bf16[256,128]{1,0:T(8,128)(2,1)S(1)}, u32[]{:S(2)}, u32[]{:S(2)}) collective-permute-start(bf16[256,128]{1,0:T(8,128)(2,1)S(1)} %broadcast_select_fusion.1), channel_id=1, source_target_pairs={{0,16},{16,0},{1,17},{17,1},{2,18},{18,2},{3,19},{19,3},{4,20},{20... | collective-permute-start | bytes 196616 | tf_op jit(solution)/shard_map/ppermute | solution.py:887
  51.4 2.8 %collective-permute-done.13.got_ref = bf16[256,128]{1,0:T(8,128)(2,1)S(1)} collective-permute-done((bf16[256,128]{1,0:T(8,128)(2,1)S(1)}, bf16[256,128]{1,0:T(8,128)(2,1)S(1)}, u32[]{:S(2)}, u32[]{:S(2)}) %collective-permute-start.13) | collective-permute-done | bytes 65568 | tf_op jit(solution)/shard_map/ppermute | solution.py:887
  54.3 4.8 %shard_map.307 = (bf16[8,208,512]{2,1,0:T(8,128)(2,1)S(1)}, bf16[8,208,512]{2,1,0:T(8,128)(2,1)S(1)}, bf16[8,48,512]{2,1,0:T(8,128)(2,1)S(1)}, bf16[8,48,512]{2,...) custom-call(bf16[256,128]{1,0:T(8,128)(2,1)S(1)} %shard_map.306.dq_ref, ...), custom_call_target="tpu_custom_call" | custom-call | flops 100000000 | bytes 10000000 | tf_op jit(solution)/shard_map/pallas_call | solution.py:871
  59.3 3.7 %shard_map.308 = (bf16[8,192,512]{2,1,0:T(8,128)(2,1)S(1)}, bf16[2,192,512]{2,1,0:T(8,128)(2,1)S(1)}, bf16[6,192,512]{2,1,0:T(8,128)(2,1)S(1)}, f32[256,512]{1,0:T(8,128)S(1)}, bf16[256,1536]{1,0:T(8,128)(2,1)S(1)}) custom-call(f32[256,512]{1,0:T(8,128)S(1)} %get-tuple-element.211.dfirst_ref, f32[512,128]{1,0:T(8,128)S(1)} %get-tuple-element.212.gproj_ref, ...), custom_call_target="tpu_custom_call" | custom-call | flops 100000000 | bytes 10000000 | tf_op jit(solution)/shard_map/pallas_call | solution.py:871
  63.7 1.8 %collective-permute-start.15 = (bf16[1,208,512]{2,1,0:T(8,128)(2,1)S(1)}, bf16[1,208,512]{2,1,0:T(8,128)(2,1)S(1)}, u32[]{:S(2)}, u32[]{:S(2)}) collective-permute-start(bf16[1,208,512]{2,1,0:T(8,128)(2,1)S(1)} %get-tuple-element.225), channel_id=1, source_target_pairs={{0,4},{1,3},{2,0},{3,7},{4,8},{5,1},{6,2},{7,11},{8,12},{9,5},{10,... | collective-permute-start | bytes 638984 | tf_op jit(solution)/shard_map/ppermute | solution.py:906
  67.2 1.5 %collective-permute-start.21 = (bf16[1,192,512]{2,1,0:T(8,128)(2,1)S(1)}, bf16[1,192,512]{2,1,0:T(8,128)(2,1)S(1)}, u32[]{:S(2)}, u32[]{:S(2)}) collective-permute-start(bf16[1,192,512]{2,1,0:T(8,128)(2,1)S(1)} %get-tuple-element.241), channel_id=1, source_target_pairs={{0,4},{1,3},{2,0},{3,7},{4,8},{5,1},{6,2},{7,11},{8,12},{9,5},{10,... | collective-permute-start | bytes 589832 | tf_op jit(solution)/shard_map/ppermute | solution.py:906
  70.5 1.4 %shard_map.313 = f32[256,512]{1,0:T(8,128)} custom-call(f32[256,512]{1,0:T(8,128)S(1)} %get-tuple-element.235.dsum_ref, bf16[256,1536]{1,0:T(8,128)(2,1)S(1)} %get-tuple-element.236.djoined_ref, bf16[512,1536]{1,0:T(8,128)(2,1)S(1)} %bitcast.21), custom_call_target="tpu_custom_call" | custom-call | flops 300000000 | bytes 30000000 | tf_op jit(solution)/shard_map/pallas_call | solution.py:871
  72.5 1.8 %collective-permute-start.19 = (bf16[1,208,512]{2,1,0:T(8,128)(2,1)S(1)}, bf16[1,208,512]{2,1,0:T(8,128)(2,1)S(1)}, u32[]{:S(2)}, u32[]{:S(2)}) collective-permute-start(bf16[1,208,512]{2,1,0:T(8,128)(2,1)S(1)} %get-tuple-element.239), channel_id=1, source_target_pairs={{0,4},{1,3},{2,0},{3,7},{4,8},{5,1},{6,2},{7,11},{8,12},{9,5},{10,... | collective-permute-start | bytes 638984 | tf_op jit(solution)/shard_map/ppermute | solution.py:906
  74.4 1.8 %collective-permute-done.21.refs_0_ = bf16[1,192,512]{2,1,0:T(8,128)(2,1)S(1)} collective-permute-done((bf16[1,192,512]{2,1,0:T(8,128)(2,1)S(1)}, bf16[1,192,512]{2,1,0:T(8,128)(2,1)S(1)}, u32[]{:S(2)}, u32[]{:S(2)}) %collective-permute-start.21) | collective-permute-done | bytes 196640 | tf_op jit(solution)/shard_map/ppermute | solution.py:906
  76.9 1.4 collective-permute-start.25
  78.3 2.1 %collective-permute-done.20.refs_1_ = bf16[1,208,512]{2,1,0:T(8,128)(2,1)S(1)} collective-permute-done((bf16[1,208,512]{2,1,0:T(8,128)(2,1)S(1)}, bf16[1,208,512]{2,1,0:T(8,128)(2,1)S(1)}, u32[]{:S(2)}, u32[]{:S(2)}) %collective-permute-start.20) | collective-permute-done | bytes 213024 | tf_op jit(solution)/shard_map/ppermute | solution.py:906
  80.8 2.1 %collective-permute-start.24 = (bf16[1,208,512]{2,1,0:T(8,128)(2,1)S(1)}, bf16[1,208,512]{2,1,0:T(8,128)(2,1)S(1)}, u32[]{:S(2)}, u32[]{:S(2)}) collective-permute-start(bf16[1,208,512]{2,1,0:T(8,128)(2,1)S(1)} %get-tuple-element.248), channel_id=1, source_target_pairs={{0,2},{1,5},{2,6},{3,1},{4,0},{5,9},{6,10},{7,3},{8,4},{9,13},{10,... | collective-permute-start | bytes 638984 | tf_op jit(solution)/shard_map/ppermute | solution.py:906
  82.9 1.6 %collective-permute-done.26.refs_1_ = bf16[1,192,512]{2,1,0:T(8,128)(2,1)S(1)} collective-permute-done((bf16[1,192,512]{2,1,0:T(8,128)(2,1)S(1)}, bf16[1,192,512]{2,1,0:T(8,128)(2,1)S(1)}, u32[]{:S(2)}, u32[]{:S(2)}) %collective-permute-start.26) | collective-permute-done | bytes 196640 | tf_op jit(solution)/shard_map/ppermute | solution.py:906
  85.0 2.1 %collective-permute-start.29 = (bf16[1,192,512]{2,1,0:T(8,128)(2,1)S(1)}, bf16[1,192,512]{2,1,0:T(8,128)(2,1)S(1)}, u32[]{:S(2)}, u32[]{:S(2)}) collective-permute-start(bf16[1,192,512]{2,1,0:T(8,128)(2,1)S(1)} %get-tuple-element.256), channel_id=1, source_target_pairs={{0,2},{1,5},{2,6},{3,1},{4,0},{5,9},{6,10},{7,3},{8,4},{9,13},{10,... | collective-permute-start | bytes 589832 | tf_op jit(solution)/shard_map/ppermute | solution.py:906
  87.1 2.0 %collective-permute-done.24.refs_1_ = bf16[1,208,512]{2,1,0:T(8,128)(2,1)S(1)} collective-permute-done((bf16[1,208,512]{2,1,0:T(8,128)(2,1)S(1)}, bf16[1,208,512]{2,1,0:T(8,128)(2,1)S(1)}, u32[]{:S(2)}, u32[]{:S(2)}) %collective-permute-start.24) | collective-permute-done | bytes 213024 | tf_op jit(solution)/shard_map/ppermute | solution.py:906
  89.1 1.7 %collective-permute-done.23.refs_0_ = bf16[1,208,512]{2,1,0:T(8,128)(2,1)S(1)} collective-permute-done((bf16[1,208,512]{2,1,0:T(8,128)(2,1)S(1)}, bf16[1,208,512]{2,1,0:T(8,128)(2,1)S(1)}, u32[]{:S(2)}, u32[]{:S(2)}) %collective-permute-start.23) | collective-permute-done | bytes 213024 | tf_op jit(solution)/shard_map/ppermute | solution.py:906
  91.5 1.9 %collective-permute-done.29.refs_1_ = bf16[1,192,512]{2,1,0:T(8,128)(2,1)S(1)} collective-permute-done((bf16[1,192,512]{2,1,0:T(8,128)(2,1)S(1)}, bf16[1,192,512]{2,1,0:T(8,128)(2,1)S(1)}, u32[]{:S(2)}, u32[]{:S(2)}) %collective-permute-start.29) | collective-permute-done | bytes 196640 | tf_op jit(solution)/shard_map/ppermute | solution.py:906
  93.5 2.1 %collective-permute-start.32 = (bf16[1,192,512]{2,1,0:T(8,128)(2,1)S(1)}, bf16[1,192,512]{2,1,0:T(8,128)(2,1)S(1)}, u32[]{:S(2)}, u32[]{:S(2)}) collective-permute-start(bf16[1,192,512]{2,1,0:T(8,128)(2,1)S(1)} %get-tuple-element.259), channel_id=1, source_target_pairs={{0,4},{1,3},{2,0},{3,7},{4,8},{5,1},{6,2},{7,11},{8,12},{9,5},{10,... | collective-permute-start | bytes 589832 | tf_op jit(solution)/shard_map/ppermute | solution.py:906
  100.1 2.6 %collective-permute-start.36 = (bf16[1,192,512]{2,1,0:T(8,128)(2,1)S(1)}, bf16[1,192,512]{2,1,0:T(8,128)(2,1)S(1)}, u32[]{:S(2)}, u32[]{:S(2)}) collective-permute-start(bf16[1,192,512]{2,1,0:T(8,128)(2,1)S(1)} %shard_map.321.refs_0_), channel_id=1, source_target_pairs={{0,2},{1,5},{2,6},{3,1},{4,0},{5,9},{6,10},{7,3},{8,4},{9,13},{10,... | collective-permute-start | bytes 589832 | tf_op jit(solution)/shard_map/ppermute | solution.py:906
  102.7 2.3 %collective-permute-done.31.refs_1_ = bf16[1,208,512]{2,1,0:T(8,128)(2,1)S(1)} collective-permute-done((bf16[1,208,512]{2,1,0:T(8,128)(2,1)S(1)}, bf16[1,208,512]{2,1,0:T(8,128)(2,1)S(1)}, u32[]{:S(2)}, u32[]{:S(2)}) %collective-permute-start.31) | collective-permute-done | bytes 213024 | tf_op jit(solution)/shard_map/ppermute | solution.py:906
  105.9 1.9 %collective-permute-start.34 = (bf16[1,208,512]{2,1,0:T(8,128)(2,1)S(1)}, bf16[1,208,512]{2,1,0:T(8,128)(2,1)S(1)}, u32[]{:S(2)}, u32[]{:S(2)}) collective-permute-start(bf16[1,208,512]{2,1,0:T(8,128)(2,1)S(1)} %get-tuple-element.293.refs_6_), channel_id=1, source_target_pairs={{0,2},{1,5},{2,6},{3,1},{4,0},{5,9},{6,10},{7,3},{8,4},{9,13},{10,... | collective-permute-start | bytes 638984 | tf_op jit(solution)/shard_map/ppermute | solution.py:906
  110.5 1.4 %collective-permute-start.40 = (bf16[1,192,512]{2,1,0:T(8,128)(2,1)S(1)}, bf16[1,192,512]{2,1,0:T(8,128)(2,1)S(1)}, u32[]{:S(2)}, u32[]{:S(2)}) collective-permute-start(bf16[1,192,512]{2,1,0:T(8,128)(2,1)S(1)} %get-tuple-element.301.refs_6_), channel_id=1, source_target_pairs={{0,2},{1,5},{2,6},{3,1},{4,0},{5,9},{6,10},{7,3},{8,4},{9,13},{10,... | collective-permute-start | bytes 589832 | tf_op jit(solution)/shard_map/ppermute | solution.py:906
  112.6 1.5 %collective-permute-done.34.refs_1_ = bf16[1,208,512]{2,1,0:T(8,128)(2,1)S(1)} collective-permute-done((bf16[1,208,512]{2,1,0:T(8,128)(2,1)S(1)}, bf16[1,208,512]{2,1,0:T(8,128)(2,1)S(1)}, u32[]{:S(2)}, u32[]{:S(2)}) %collective-permute-start.34) | collective-permute-done | bytes 213024 | tf_op jit(solution)/shard_map/ppermute | solution.py:906
  115.3 1.7 %collective-permute-start.38 = (bf16[1,208,512]{2,1,0:T(8,128)(2,1)S(1)}, bf16[1,208,512]{2,1,0:T(8,128)(2,1)S(1)}, u32[]{:S(2)}, u32[]{:S(2)}) collective-permute-start(bf16[1,208,512]{2,1,0:T(8,128)(2,1)S(1)} %get-tuple-element.292.refs_5_), channel_id=1, source_target_pairs={{0,2},{1,5},{2,6},{3,1},{4,0},{5,9},{6,10},{7,3},{8,4},{9,13},{10,... | collective-permute-start | bytes 638984 | tf_op jit(solution)/shard_map/ppermute | solution.py:906
  118.4 1.3 collective-permute-done.39.refs_0_
  119.7 1.5 %collective-permute-start.43 = (bf16[1,192,512]{2,1,0:T(8,128)(2,1)S(1)}, bf16[1,192,512]{2,1,0:T(8,128)(2,1)S(1)}, u32[]{:S(2)}, u32[]{:S(2)}) collective-permute-start(bf16[1,192,512]{2,1,0:T(8,128)(2,1)S(1)} %get-tuple-element.300.refs_5_), channel_id=1, source_target_pairs={{0,2},{1,5},{2,6},{3,1},{4,0},{5,9},{6,10},{7,3},{8,4},{9,13},{10,... | collective-permute-start | bytes 589832 | tf_op jit(solution)/shard_map/ppermute | solution.py:906
  121.8 1.8 %collective-permute-done.38.refs_1_ = bf16[1,208,512]{2,1,0:T(8,128)(2,1)S(1)} collective-permute-done((bf16[1,208,512]{2,1,0:T(8,128)(2,1)S(1)}, bf16[1,208,512]{2,1,0:T(8,128)(2,1)S(1)}, u32[]{:S(2)}, u32[]{:S(2)}) %collective-permute-start.38) | collective-permute-done | bytes 213024 | tf_op jit(solution)/shard_map/ppermute | solution.py:906
  123.9 2.1 %collective-permute-done.43.refs_1_ = bf16[1,192,512]{2,1,0:T(8,128)(2,1)S(1)} collective-permute-done((bf16[1,192,512]{2,1,0:T(8,128)(2,1)S(1)}, bf16[1,192,512]{2,1,0:T(8,128)(2,1)S(1)}, u32[]{:S(2)}, u32[]{:S(2)}) %collective-permute-start.43) | collective-permute-done | bytes 196640 | tf_op jit(solution)/shard_map/ppermute | solution.py:906
  128.5 1.3 collective-permute-start.46
  129.7 2.8 %shard_map.330 = (f32[2048,512]{1,0:T(8,128)}, f32[512,2048]{1,0:T(8,128)}, f32[512,1536]{1,0:T(8,128)}, f32[512,512]{1,0:T(8,128)}, f32[512,128]{1,0:T(8,128)}) custom-call(bf16[7,208,512]{2,1,0:T(8,128)(2,1)S(1)} %shard_map.328.refs_0_, bf16[7,192,512]{2,1,0:T(8,128)(2,1)S(1)} %shard_map.329.refs_1_.refs_2_), custom_call_target="tpu_custom_call" | custom-call | tf_op jit(solution)/shard_map/pallas_call | solution.py:871
  132.6 2.8 %shard_map.331 = (f32[2048,512]{1,0:T(8,128)}, f32[512,2048]{1,0:T(8,128)}, f32[512,1536]{1,0:T(8,128)}, f32[512,512]{1,0:T(8,128)}, f32[512,128]{1,0:T(8,128)}) custom-call(bf16[7,208,512]{2,1,0:T(8,128)(2,1)S(1)} %collective-permute-done.44.refs_0_, ...), custom_call_target="tpu_custom_call", output_to_operand_aliasing={{0}: (2, {}), {1}: (3, {}), {2}: (4, {}), {3}: (5, {}), {4}... | custom-call | tf_op jit(solution)/shard_map/pallas_call | solution.py:871
  137.6 1.6 %shard_map.337 = (f32[2048,512]{1,0:T(8,128)}, f32[512,2048]{1,0:T(8,128)}, f32[512,1536]{1,0:T(8,128)}, f32[512,512]{1,0:T(8,128)}, f32[512,128]{1,0:T(8,128)},...) custom-call(bf16[1,208,512]{2,1,0:T(8,128)(2,1)S(1)} %collective-per, ...), custom_call_target="tpu_custom_call", output_to_operand_aliasing={{0}: (6, {}), {1}: (7, {}), {2}: (8, {}), {3}: (9, {}), {4}... | custom-call | tf_op jit(solution)/shard_map/pallas_call | solution.py:871
  (131 shorter events, 30.6 us)
Async XLA Ops:
  7.5 5.3 %collective-permute-start = (bf16[272,128]{1,0:T(8,128)(2,1)S(1)}, bf16[272,128]{1,0:T(8,128)(2,1)S(1)}, u32[]{:S(2)}, u32[]{:S(2)}) collective-permute-start(bf16[272,128]{1,0:T(8,128)(2,1)S(1)} %get-tuple-element.180), channel_id=1, source_target_pairs={{0,16},{16,0},{1,17},{17,1},{2,18},{18,2},{3,19},{19,3},{4,20},{20... | collective-permute-start | bytes 208904 | tf_op jit(solution)/shard_map/ppermute | solution.py:887
  12.8 5.4 %collective-permute-start.2 = (bf16[256,128]{1,0:T(8,128)(2,1)S(1)}, bf16[256,128]{1,0:T(8,128)(2,1)S(1)}, u32[]{:S(2)}, u32[]{:S(2)}) collective-permute-start(bf16[256,128]{1,0:T(8,128)(2,1)S(1)} %slice_select_fusion.here_ref), channel_id=1, source_target_pairs={{0,8},{1,9},{2,10},{3,11},{4,12},{5,13},{6,14},{7,15},{8,0},{9,1},... | collective-permute-start | bytes 196616 | tf_op jit(solution)/shard_map/ppermute | solution.py:887
  16.0 4.4 %collective-permute-start.1 = (bf16[272,128]{1,0:T(8,128)(2,1)S(1)}, bf16[272,128]{1,0:T(8,128)(2,1)S(1)}, u32[]{:S(2)}, u32[]{:S(2)}) collective-permute-start(bf16[272,128]{1,0:T(8,128)(2,1)S(1)} %broadcast_select_fusion), channel_id=1, source_target_pairs={{0,2},{1,3},{2,0},{3,1},{4,6},{5,7},{6,4},{7,5},{8,10},{9,11},{10,... | collective-permute-start | bytes 208904 | tf_op jit(solution)/shard_map/ppermute | solution.py:887
  20.4 4.6 %collective-permute-start.3 = (bf16[544,128]{1,0:T(8,128)(2,1)S(1)}, bf16[544,128]{1,0:T(8,128)(2,1)S(1)}, u32[]{:S(2)}, u32[]{:S(2)}) collective-permute-start(bf16[544,128]{1,0:T(8,128)(2,1)S(1)} %pad_maximum_fusion.near_ref), channel_id=1, source_target_pairs={{0,1},{1,0},{2,3},{3,2},{4,5},{5,4},{6,7},{7,6},{8,9},{9,8},{10,11... | collective-permute-start | bytes 417800 | tf_op jit(solution)/shard_map/ppermute | solution.py:887
  20.5 4.5 %collective-permute-start.4 = (bf16[256,128]{1,0:T(8,128)(2,1)S(1)}, bf16[256,128]{1,0:T(8,128)(2,1)S(1)}, u32[]{:S(2)}, u32[]{:S(2)}) collective-permute-start(bf16[256,128]{1,0:T(8,128)(2,1)S(1)} %shard_map.299.refs_0_), channel_id=1, source_target_pairs={{0,4},{1,5},{2,6},{3,7},{4,0},{5,1},{6,2},{7,3},{8,12},{9,13},{10,... | collective-permute-start | bytes 196616 | tf_op jit(solution)/shard_map/ppermute | solution.py:887
  29.0 5.0 %collective-permute-start.8 = (f32[32,128]{1,0:T(8,128)S(1)}, f32[32,128]{1,0:T(8,128)S(1)}, u32[]{:S(2)}, u32[]{:S(2)}) collective-permute-start(f32[32,128]{1,0:T(8,128)S(1)} %add.3.own_ref), channel_id=1, source_target_pairs={{0,18},{1,19},{2,16},{3,17},{4,22},{5,23},{6,20},{7,21},{8,26},{9,... | collective-permute-start | bytes 49160 | tf_op jit(solution)/shard_map/ppermute | solution.py:1129
  31.5 3.7 %collective-permute-start.7 = (f32[32,128]{1,0:T(8,128)S(1)}, f32[32,128]{1,0:T(8,128)S(1)}, u32[]{:S(2)}, u32[]{:S(2)}) collective-permute-start(f32[32,128]{1,0:T(8,128)S(1)} %add.3.own_ref), channel_id=1, source_target_pairs={{0,16},{16,0},{1,17},{17,1},{2,18},{18,2},{3,19},{19,3},{4,20},{20... | collective-permute-start | bytes 49160 | tf_op jit(solution)/shard_map/ppermute | solution.py:887
  32.0 3.7 %collective-permute-start.6 = (f32[32,128]{1,0:T(8,128)S(1)}, f32[32,128]{1,0:T(8,128)S(1)}, u32[]{:S(2)}, u32[]{:S(2)}) collective-permute-start(f32[32,128]{1,0:T(8,128)S(1)} %add.3.own_ref), channel_id=1, source_target_pairs={{0,2},{1,3},{2,0},{3,1},{4,6},{5,7},{6,4},{7,5},{8,10},{9,11},{10,... | collective-permute-start | bytes 49160 | tf_op jit(solution)/shard_map/ppermute | solution.py:887
  39.4 1.7 %collective-permute-start.9 = (bf16[512,128]{1,0:T(8,128)(2,1)S(1)}, bf16[512,128]{1,0:T(8,128)(2,1)S(1)}, u32[]{:S(2)}, u32[]{:S(2)}) collective-permute-start(bf16[512,128]{1,0:T(8,128)(2,1)S(1)} %get-tuple-element.199), channel_id=1, source_target_pairs={{0,1},{1,0},{2,3},{3,2},{4,5},{5,4},{6,7},{7,6},{8,9},{9,8},{10,11... | collective-permute-start | bytes 393224 | tf_op jit(solution)/shard_map/ppermute | solution.py:887
  39.4 4.5 %collective-permute-start.11 = (bf16[256,128]{1,0:T(8,128)(2,1)S(1)}, bf16[256,128]{1,0:T(8,128)(2,1)S(1)}, u32[]{:S(2)}, u32[]{:S(2)}) collective-permute-start(bf16[256,128]{1,0:T(8,128)(2,1)S(1)} %get-tuple-element.201), channel_id=1, source_target_pairs={{0,4},{1,5},{2,6},{3,7},{4,0},{5,1},{6,2},{7,3},{8,12},{9,13},{10,... | collective-permute-start | bytes 196616 | tf_op jit(solution)/shard_map/ppermute | solution.py:887
  44.0 5.6 %collective-permute-start.12 = (bf16[256,128]{1,0:T(8,128)(2,1)S(1)}, bf16[256,128]{1,0:T(8,128)(2,1)S(1)}, u32[]{:S(2)}, u32[]{:S(2)}) collective-permute-start(bf16[256,128]{1,0:T(8,128)(2,1)S(1)} %shard_map.304.rows_ref), channel_id=1, source_target_pairs={{0,8},{1,9},{2,10},{3,11},{4,12},{5,13},{6,14},{7,15},{8,0},{9,1},... | collective-permute-start | bytes 196616 | tf_op jit(solution)/shard_map/ppermute | solution.py:887
  45.3 4.4 %collective-permute-start.10 = (bf16[256,128]{1,0:T(8,128)(2,1)S(1)}, bf16[256,128]{1,0:T(8,128)(2,1)S(1)}, u32[]{:S(2)}, u32[]{:S(2)}) collective-permute-start(bf16[256,128]{1,0:T(8,128)(2,1)S(1)} %get-tuple-element.344), channel_id=1, source_target_pairs={{0,2},{1,3},{2,0},{3,1},{4,6},{5,7},{6,4},{7,5},{8,10},{9,11},{10,... | collective-permute-start | bytes 196616 | tf_op jit(solution)/shard_map/ppermute | solution.py:887
  49.7 4.5 %collective-permute-start.13 = (bf16[256,128]{1,0:T(8,128)(2,1)S(1)}, bf16[256,128]{1,0:T(8,128)(2,1)S(1)}, u32[]{:S(2)}, u32[]{:S(2)}) collective-permute-start(bf16[256,128]{1,0:T(8,128)(2,1)S(1)} %broadcast_select_fusion.1), channel_id=1, source_target_pairs={{0,16},{16,0},{1,17},{17,1},{2,18},{18,2},{3,19},{19,3},{4,20},{20... | collective-permute-start | bytes 196616 | tf_op jit(solution)/shard_map/ppermute | solution.py:887
  59.1 4.5 %collective-permute-start.14 = (bf16[8,208,512]{2,1,0:T(8,128)(2,1)S(1)}, bf16[8,208,512]{2,1,0:T(8,128)(2,1)S(1)}, u32[]{:S(2)}, u32[]{:S(2)}) collective-permute-start(bf16[8,208,512]{2,1,0:T(8,128)(2,1)S(1)} %get-tuple-element.210), channel_id=1, source_target_pairs={{0,1},{1,0},{2,3},{3,2},{4,5},{5,4},{6,7},{7,6},{8,9},{9,8},{10,11... | collective-permute-start | bytes 5111816 | tf_op jit(solution)/shard_map/ppermute | solution.py:887
  63.0 6.1 %collective-permute-start.18 = (bf16[6,192,512]{2,1,0:T(8,128)(2,1)S(1)}, bf16[6,192,512]{2,1,0:T(8,128)(2,1)S(1)}, u32[]{:S(2)}, u32[]{:S(2)}) collective-permute-start(bf16[6,192,512]{2,1,0:T(8,128)(2,1)S(1)} %get-tuple-element.234), channel_id=1, source_target_pairs={{0,1},{1,0},{2,3},{3,2},{4,5},{5,4},{6,7},{7,6},{8,9},{9,8},{10,11... | collective-permute-start | bytes 3538952 | tf_op jit(solution)/shard_map/ppermute | solution.py:887
  63.5 3.0 %collective-permute-start.17 = (bf16[2,192,512]{2,1,0:T(8,128)(2,1)S(1)}, bf16[2,192,512]{2,1,0:T(8,128)(2,1)S(1)}, u32[]{:S(2)}, u32[]{:S(2)}) collective-permute-start(bf16[2,192,512]{2,1,0:T(8,128)(2,1)S(1)} %get-tuple-element.228), channel_id=1, source_target_pairs={{0,1},{1,0},{2,3},{3,2},{4,5},{5,4},{6,7},{7,6},{8,9},{9,8},{10,11... | collective-permute-start | bytes 1179656 | tf_op jit(solution)/shard_map/ppermute | solution.py:887
  63.7 8.2 %collective-permute-start.15 = (bf16[1,208,512]{2,1,0:T(8,128)(2,1)S(1)}, bf16[1,208,512]{2,1,0:T(8,128)(2,1)S(1)}, u32[]{:S(2)}, u32[]{:S(2)}) collective-permute-start(bf16[1,208,512]{2,1,0:T(8,128)(2,1)S(1)} %get-tuple-element.225), channel_id=1, source_target_pairs={{0,4},{1,3},{2,0},{3,7},{4,8},{5,1},{6,2},{7,11},{8,12},{9,5},{10,... | collective-permute-start | bytes 638984 | tf_op jit(solution)/shard_map/ppermute | solution.py:906
  65.5 6.4 %collective-permute-start.16 = (bf16[1,208,512]{2,1,0:T(8,128)(2,1)S(1)}, bf16[1,208,512]{2,1,0:T(8,128)(2,1)S(1)}, u32[]{:S(2)}, u32[]{:S(2)}) collective-permute-start(bf16[1,208,512]{2,1,0:T(8,128)(2,1)S(1)} %get-tuple-element.226), channel_id=1, source_target_pairs={{0,2},{1,5},{2,6},{3,1},{4,0},{5,9},{6,10},{7,3},{8,4},{9,13},{10,... | collective-permute-start | bytes 638984 | tf_op jit(solution)/shard_map/ppermute | solution.py:906
  66.7 9.4 %collective-permute-start.22 = (bf16[1,192,512]{2,1,0:T(8,128)(2,1)S(1)}, bf16[1,192,512]{2,1,0:T(8,128)(2,1)S(1)}, u32[]{:S(2)}, u32[]{:S(2)}) collective-permute-start(bf16[1,192,512]{2,1,0:T(8,128)(2,1)S(1)} %get-tuple-element.231), channel_id=1, source_target_pairs={{0,2},{1,5},{2,6},{3,1},{4,0},{5,9},{6,10},{7,3},{8,4},{9,13},{10,... | collective-permute-start | bytes 589832 | tf_op jit(solution)/shard_map/ppermute | solution.py:906
  67.2 8.9 %collective-permute-start.21 = (bf16[1,192,512]{2,1,0:T(8,128)(2,1)S(1)}, bf16[1,192,512]{2,1,0:T(8,128)(2,1)S(1)}, u32[]{:S(2)}, u32[]{:S(2)}) collective-permute-start(bf16[1,192,512]{2,1,0:T(8,128)(2,1)S(1)} %get-tuple-element.241), channel_id=1, source_target_pairs={{0,4},{1,3},{2,0},{3,7},{4,8},{5,1},{6,2},{7,11},{8,12},{9,5},{10,... | collective-permute-start | bytes 589832 | tf_op jit(solution)/shard_map/ppermute | solution.py:906
  72.0 8.3 %collective-permute-start.20 = (bf16[1,208,512]{2,1,0:T(8,128)(2,1)S(1)}, bf16[1,208,512]{2,1,0:T(8,128)(2,1)S(1)}, u32[]{:S(2)}, u32[]{:S(2)}) collective-permute-start(bf16[1,208,512]{2,1,0:T(8,128)(2,1)S(1)} %get-tuple-element.240), channel_id=1, source_target_pairs={{0,2},{1,5},{2,6},{3,1},{4,0},{5,9},{6,10},{7,3},{8,4},{9,13},{10,... | collective-permute-start | bytes 638984 | tf_op jit(solution)/shard_map/ppermute | solution.py:906
  72.5 8.1 %collective-permute-start.19 = (bf16[1,208,512]{2,1,0:T(8,128)(2,1)S(1)}, bf16[1,208,512]{2,1,0:T(8,128)(2,1)S(1)}, u32[]{:S(2)}, u32[]{:S(2)}) collective-permute-start(bf16[1,208,512]{2,1,0:T(8,128)(2,1)S(1)} %get-tuple-element.239), channel_id=1, source_target_pairs={{0,4},{1,3},{2,0},{3,7},{4,8},{5,1},{6,2},{7,11},{8,12},{9,5},{10,... | collective-permute-start | bytes 638984 | tf_op jit(solution)/shard_map/ppermute | solution.py:906
  76.2 8.3 %collective-permute-start.26 = (bf16[1,192,512]{2,1,0:T(8,128)(2,1)S(1)}, bf16[1,192,512]{2,1,0:T(8,128)(2,1)S(1)}, u32[]{:S(2)}, u32[]{:S(2)}) collective-permute-start(bf16[1,192,512]{2,1,0:T(8,128)(2,1)S(1)} %get-tuple-element.249), channel_id=1, source_target_pairs={{0,2},{1,5},{2,6},{3,1},{4,0},{5,9},{6,10},{7,3},{8,4},{9,13},{10,... | collective-permute-start | bytes 589832 | tf_op jit(solution)/shard_map/ppermute | solution.py:906
  76.9 8.0 %collective-permute-start.25 = (bf16[1,192,512]{2,1,0:T(8,128)(2,1)S(1)}, bf16[1,192,512]{2,1,0:T(8,128)(2,1)S(1)}, u32[]{:S(2)}, u32[]{:S(2)}) collective-permute-start(bf16[1,192,512]{2,1,0:T(8,128)(2,1)S(1)} %get-tuple-element.244), channel_id=1, source_target_pairs={{0,4},{1,3},{2,0},{3,7},{4,8},{5,1},{6,2},{7,11},{8,12},{9,5},{10,... | collective-permute-start | bytes 589832 | tf_op jit(solution)/shard_map/ppermute | solution.py:906
  80.8 8.3 %collective-permute-start.24 = (bf16[1,208,512]{2,1,0:T(8,128)(2,1)S(1)}, bf16[1,208,512]{2,1,0:T(8,128)(2,1)S(1)}, u32[]{:S(2)}, u32[]{:S(2)}) collective-permute-start(bf16[1,208,512]{2,1,0:T(8,128)(2,1)S(1)} %get-tuple-element.248), channel_id=1, source_target_pairs={{0,2},{1,5},{2,6},{3,1},{4,0},{5,9},{6,10},{7,3},{8,4},{9,13},{10,... | collective-permute-start | bytes 638984 | tf_op jit(solution)/shard_map/ppermute | solution.py:906
  82.9 7.9 %collective-permute-start.23 = (bf16[1,208,512]{2,1,0:T(8,128)(2,1)S(1)}, bf16[1,208,512]{2,1,0:T(8,128)(2,1)S(1)}, u32[]{:S(2)}, u32[]{:S(2)}) collective-permute-start(bf16[1,208,512]{2,1,0:T(8,128)(2,1)S(1)} %get-tuple-element.247), channel_id=1, source_target_pairs={{0,4},{1,3},{2,0},{3,7},{4,8},{5,1},{6,2},{7,11},{8,12},{9,5},{10,... | collective-permute-start | bytes 638984 | tf_op jit(solution)/shard_map/ppermute | solution.py:906
  85.0 8.4 %collective-permute-start.29 = (bf16[1,192,512]{2,1,0:T(8,128)(2,1)S(1)}, bf16[1,192,512]{2,1,0:T(8,128)(2,1)S(1)}, u32[]{:S(2)}, u32[]{:S(2)}) collective-permute-start(bf16[1,192,512]{2,1,0:T(8,128)(2,1)S(1)} %get-tuple-element.256), channel_id=1, source_target_pairs={{0,2},{1,5},{2,6},{3,1},{4,0},{5,9},{6,10},{7,3},{8,4},{9,13},{10,... | collective-permute-start | bytes 589832 | tf_op jit(solution)/shard_map/ppermute | solution.py:906
  87.1 6.2 %collective-permute-start.28 = (bf16[1,192,512]{2,1,0:T(8,128)(2,1)S(1)}, bf16[1,192,512]{2,1,0:T(8,128)(2,1)S(1)}, u32[]{:S(2)}, u32[]{:S(2)}) collective-permute-start(bf16[1,192,512]{2,1,0:T(8,128)(2,1)S(1)} %get-tuple-element.252), channel_id=1, source_target_pairs={{0,4},{1,3},{2,0},{3,7},{4,8},{5,1},{6,2},{7,11},{8,12},{9,5},{10,... | collective-permute-start | bytes 589832 | tf_op jit(solution)/shard_map/ppermute | solution.py:906
  90.9 5.9 %collective-permute-start.27 = (bf16[1,208,512]{2,1,0:T(8,128)(2,1)S(1)}, bf16[1,208,512]{2,1,0:T(8,128)(2,1)S(1)}, u32[]{:S(2)}, u32[]{:S(2)}) collective-permute-start(bf16[1,208,512]{2,1,0:T(8,128)(2,1)S(1)} %get-tuple-element.255), channel_id=1, source_target_pairs={{0,4},{1,3},{2,0},{3,7},{4,8},{5,1},{6,2},{7,11},{8,12},{9,5},{10,... | collective-permute-start | bytes 638984 | tf_op jit(solution)/shard_map/ppermute | solution.py:906
  93.5 6.6 %collective-permute-start.32 = (bf16[1,192,512]{2,1,0:T(8,128)(2,1)S(1)}, bf16[1,192,512]{2,1,0:T(8,128)(2,1)S(1)}, u32[]{:S(2)}, u32[]{:S(2)}) collective-permute-start(bf16[1,192,512]{2,1,0:T(8,128)(2,1)S(1)} %get-tuple-element.259), channel_id=1, source_target_pairs={{0,4},{1,3},{2,0},{3,7},{4,8},{5,1},{6,2},{7,11},{8,12},{9,5},{10,... | collective-permute-start | bytes 589832 | tf_op jit(solution)/shard_map/ppermute | solution.py:906
  96.8 8.1 %collective-permute-start.31 = (bf16[1,208,512]{2,1,0:T(8,128)(2,1)S(1)}, bf16[1,208,512]{2,1,0:T(8,128)(2,1)S(1)}, u32[]{:S(2)}, u32[]{:S(2)}) collective-permute-start(bf16[1,208,512]{2,1,0:T(8,128)(2,1)S(1)} %shard_map.320.refs_0_), channel_id=1, source_target_pairs={{0,2},{1,5},{2,6},{3,1},{4,0},{5,9},{6,10},{7,3},{8,4},{9,13},{10,... | collective-permute-start | bytes 638984 | tf_op jit(solution)/shard_map/ppermute | solution.py:906
  97.6 8.2 %collective-permute-start.30 = (bf16[1,208,512]{2,1,0:T(8,128)(2,1)S(1)}, bf16[1,208,512]{2,1,0:T(8,128)(2,1)S(1)}, u32[]{:S(2)}, u32[]{:S(2)}) collective-permute-start(bf16[1,208,512]{2,1,0:T(8,128)(2,1)S(1)} %shard_map.320.refs_0_), channel_id=1, source_target_pairs={{0,4},{1,3},{2,0},{3,7},{4,8},{5,1},{6,2},{7,11},{8,12},{9,5},{10,... | collective-permute-start | bytes 638984 | tf_op jit(solution)/shard_map/ppermute | solution.py:906
  100.1 9.1 %collective-permute-start.36 = (bf16[1,192,512]{2,1,0:T(8,128)(2,1)S(1)}, bf16[1,192,512]{2,1,0:T(8,128)(2,1)S(1)}, u32[]{:S(2)}, u32[]{:S(2)}) collective-permute-start(bf16[1,192,512]{2,1,0:T(8,128)(2,1)S(1)} %shard_map.321.refs_0_), channel_id=1, source_target_pairs={{0,2},{1,5},{2,6},{3,1},{4,0},{5,9},{6,10},{7,3},{8,4},{9,13},{10,... | collective-permute-start | bytes 589832 | tf_op jit(solution)/shard_map/ppermute | solution.py:906
  102.7 7.8 %collective-permute-start.35 = (bf16[1,192,512]{2,1,0:T(8,128)(2,1)S(1)}, bf16[1,192,512]{2,1,0:T(8,128)(2,1)S(1)}, u32[]{:S(2)}, u32[]{:S(2)}) collective-permute-start(bf16[1,192,512]{2,1,0:T(8,128)(2,1)S(1)} %shard_map.321.refs_0_), channel_id=1, source_target_pairs={{0,4},{1,3},{2,0},{3,7},{4,8},{5,1},{6,2},{7,11},{8,12},{9,5},{10,... | collective-permute-start | bytes 589832 | tf_op jit(solution)/shard_map/ppermute | solution.py:906
  105.9 8.2 %collective-permute-start.34 = (bf16[1,208,512]{2,1,0:T(8,128)(2,1)S(1)}, bf16[1,208,512]{2,1,0:T(8,128)(2,1)S(1)}, u32[]{:S(2)}, u32[]{:S(2)}) collective-permute-start(bf16[1,208,512]{2,1,0:T(8,128)(2,1)S(1)} %get-tuple-element.293.refs_6_), channel_id=1, source_target_pairs={{0,2},{1,5},{2,6},{3,1},{4,0},{5,9},{6,10},{7,3},{8,4},{9,13},{10,... | collective-permute-start | bytes 638984 | tf_op jit(solution)/shard_map/ppermute | solution.py:906
  107.7 7.6 %collective-permute-start.33 = (bf16[1,208,512]{2,1,0:T(8,128)(2,1)S(1)}, bf16[1,208,512]{2,1,0:T(8,128)(2,1)S(1)}, u32[]{:S(2)}, u32[]{:S(2)}) collective-permute-start(bf16[1,208,512]{2,1,0:T(8,128)(2,1)S(1)} %get-tuple-element.288.refs_1_), channel_id=1, source_target_pairs={{0,4},{1,3},{2,0},{3,7},{4,8},{5,1},{6,2},{7,11},{8,12},{9,5},{10,... | collective-permute-start | bytes 638984 | tf_op jit(solution)/shard_map/ppermute | solution.py:906
  110.5 7.9 %collective-permute-start.40 = (bf16[1,192,512]{2,1,0:T(8,128)(2,1)S(1)}, bf16[1,192,512]{2,1,0:T(8,128)(2,1)S(1)}, u32[]{:S(2)}, u32[]{:S(2)}) collective-permute-start(bf16[1,192,512]{2,1,0:T(8,128)(2,1)S(1)} %get-tuple-element.301.refs_6_), channel_id=1, source_target_pairs={{0,2},{1,5},{2,6},{3,1},{4,0},{5,9},{6,10},{7,3},{8,4},{9,13},{10,... | collective-permute-start | bytes 589832 | tf_op jit(solution)/shard_map/ppermute | solution.py:906
  111.9 7.7 %collective-permute-start.39 = (bf16[1,192,512]{2,1,0:T(8,128)(2,1)S(1)}, bf16[1,192,512]{2,1,0:T(8,128)(2,1)S(1)}, u32[]{:S(2)}, u32[]{:S(2)}) collective-permute-start(bf16[1,192,512]{2,1,0:T(8,128)(2,1)S(1)} %get-tuple-element.296.refs_1_), channel_id=1, source_target_pairs={{0,4},{1,3},{2,0},{3,7},{4,8},{5,1},{6,2},{7,11},{8,12},{9,5},{10,... | collective-permute-start | bytes 589832 | tf_op jit(solution)/shard_map/ppermute | solution.py:906
  115.3 8.2 %collective-permute-start.38 = (bf16[1,208,512]{2,1,0:T(8,128)(2,1)S(1)}, bf16[1,208,512]{2,1,0:T(8,128)(2,1)S(1)}, u32[]{:S(2)}, u32[]{:S(2)}) collective-permute-start(bf16[1,208,512]{2,1,0:T(8,128)(2,1)S(1)} %get-tuple-element.292.refs_5_), channel_id=1, source_target_pairs={{0,2},{1,5},{2,6},{3,1},{4,0},{5,9},{6,10},{7,3},{8,4},{9,13},{10,... | collective-permute-start | bytes 638984 | tf_op jit(solution)/shard_map/ppermute | solution.py:906
  117.0 6.8 %collective-permute-start.37 = (bf16[1,208,512]{2,1,0:T(8,128)(2,1)S(1)}, bf16[1,208,512]{2,1,0:T(8,128)(2,1)S(1)}, u32[]{:S(2)}, u32[]{:S(2)}) collective-permute-start(bf16[1,208,512]{2,1,0:T(8,128)(2,1)S(1)} %get-tuple-element.289.refs_2_), channel_id=1, source_target_pairs={{0,4},{1,3},{2,0},{3,7},{4,8},{5,1},{6,2},{7,11},{8,12},{9,5},{10,... | collective-permute-start | bytes 638984 | tf_op jit(solution)/shard_map/ppermute | solution.py:906
  119.7 6.3 %collective-permute-start.43 = (bf16[1,192,512]{2,1,0:T(8,128)(2,1)S(1)}, bf16[1,192,512]{2,1,0:T(8,128)(2,1)S(1)}, u32[]{:S(2)}, u32[]{:S(2)}) collective-permute-start(bf16[1,192,512]{2,1,0:T(8,128)(2,1)S(1)} %get-tuple-element.300.refs_5_), channel_id=1, source_target_pairs={{0,2},{1,5},{2,6},{3,1},{4,0},{5,9},{6,10},{7,3},{8,4},{9,13},{10,... | collective-permute-start | bytes 589832 | tf_op jit(solution)/shard_map/ppermute | solution.py:906
  121.2 5.7 %collective-permute-start.42 = (bf16[1,192,512]{2,1,0:T(8,128)(2,1)S(1)}, bf16[1,192,512]{2,1,0:T(8,128)(2,1)S(1)}, u32[]{:S(2)}, u32[]{:S(2)}) collective-permute-start(bf16[1,192,512]{2,1,0:T(8,128)(2,1)S(1)} %get-tuple-element.297.refs_2_), channel_id=1, source_target_pairs={{0,4},{1,3},{2,0},{3,7},{4,8},{5,1},{6,2},{7,11},{8,12},{9,5},{10,... | collective-permute-start | bytes 589832 | tf_op jit(solution)/shard_map/ppermute | solution.py:906
  127.0 5.5 %collective-permute-start.44 = (bf16[7,208,512]{2,1,0:T(8,128)(2,1)S(1)}, bf16[7,208,512]{2,1,0:T(8,128)(2,1)S(1)}, u32[]{:S(2)}, u32[]{:S(2)}) collective-permute-start(bf16[7,208,512]{2,1,0:T(8,128)(2,1)S(1)} %shard_map.328.refs_0_), channel_id=1, source_target_pairs={{0,1},{1,0},{2,3},{3,2},{4,5},{5,4},{6,7},{7,6},{8,9},{9,8},{10,11... | collective-permute-start | bytes 4472840 | tf_op jit(solution)/shard_map/ppermute | solution.py:887
  127.2 5.4 %collective-permute-start.45 = (bf16[7,192,512]{2,1,0:T(8,128)(2,1)S(1)}, bf16[7,192,512]{2,1,0:T(8,128)(2,1)S(1)}, u32[]{:S(2)}, u32[]{:S(2)}) collective-permute-start(bf16[7,192,512]{2,1,0:T(8,128)(2,1)S(1)} %shard_map.329.refs_1_.refs_2_), channel_id=1, source_target_pairs={{0,1},{1,0},{2,3},{3,2},{4,5},{5,4},{6,7},{7,6},{8,9},{9,8},{10,11... | collective-permute-start | bytes 4128776 | tf_op jit(solution)/shard_map/ppermute | solution.py:887
  127.8 7.6 %collective-permute-start.41 = (bf16[1,208,512]{2,1,0:T(8,128)(2,1)S(1)}, bf16[1,208,512]{2,1,0:T(8,128)(2,1)S(1)}, u32[]{:S(2)}, u32[]{:S(2)}) collective-permute-start(bf16[1,208,512]{2,1,0:T(8,128)(2,1)S(1)} %get-tuple-element.290.refs_3_), channel_id=1, source_target_pairs={{0,4},{1,3},{2,0},{3,7},{4,8},{5,1},{6,2},{7,11},{8,12},{9,5},{10,... | collective-permute-start | bytes 638984 | tf_op jit(solution)/shard_map/ppermute | solution.py:906
  128.5 7.3 %collective-permute-start.46 = (bf16[1,192,512]{2,1,0:T(8,128)(2,1)S(1)}, bf16[1,192,512]{2,1,0:T(8,128)(2,1)S(1)}, u32[]{:S(2)}, u32[]{:S(2)}) collective-permute-start(bf16[1,192,512]{2,1,0:T(8,128)(2,1)S(1)} %get-tuple-element.298.refs_3_), channel_id=1, source_target_pairs={{0,4},{1,3},{2,0},{3,7},{4,8},{5,1},{6,2},{7,11},{8,12},{9,5},{10,... | collective-permute-start | bytes 589832 | tf_op jit(solution)/shard_map/ppermute | solution.py:906
  135.8 1.8 %collective-permute-start.47 = (bf16[1,208,512]{2,1,0:T(8,128)(2,1)S(1)}, bf16[1,208,512]{2,1,0:T(8,128)(2,1)S(1)}, u32[]{:S(2)}, u32[]{:S(2)}) collective-permute-start(bf16[1,208,512]{2,1,0:T(8,128)(2,1)S(1)} %shard_map.334.refs_0_), channel_id=1, source_target_pairs={{0,1},{1,0},{2,3},{3,2},{4,5},{5,4},{6,7},{7,6},{8,9},{9,8},{10,11... | collective-permute-start | bytes 638984 | tf_op jit(solution)/shard_map/ppermute | solution.py:887
  135.9 1.7 %collective-permute-start.48 = (bf16[1,192,512]{2,1,0:T(8,128)(2,1)S(1)}, bf16[1,192,512]{2,1,0:T(8,128)(2,1)S(1)}, u32[]{:S(2)}, u32[]{:S(2)}) collective-permute-start(bf16[1,192,512]{2,1,0:T(8,128)(2,1)S(1)} %shard_map.335.refs_1_.refs_3_), channel_id=1, source_target_pairs={{0,1},{1,0},{2,3},{3,2},{4,5},{5,4},{6,7},{7,6},{8,9},{9,8},{10,11... | collective-permute-start | bytes 589832 | tf_op jit(solution)/shard_map/ppermute | solution.py:887
  (18 other events, 167.4 us)

commit v10 on v9

--- a/solution.py
+++ b/solution.py
@@ -44,8 +44,8 @@
 ROUND = (("step", 0), ("step", 1))
 ORDER = (
     (("open", 0), ("open", 1), ("total", 0), ("total", 1), ("tokens", 0)) + ROUND * 7
-    + (("share", 0, 0), ("share", 1, 0), ("spread", ((True, 0),)), ("spread", ((False, 0),))) + ROUND
-    + (("share", 0, 1), ("share", 1, 1), ("spread", ((True, 1),)), ("spread", ((False, 1),)))
+    + (("share", 0), ("spread", ((True, 0),)), ("spread", ((False, 0),))) + ROUND
+    + (("share", 1), ("spread", ((True, 1),)), ("spread", ((False, 1),)))
 )
 MIB = 1024 * 1024
 
@@ -763,7 +763,7 @@
 
 def spread(size, jobs, last, *refs):
     core, place = here(size)[-2:]
-    halves = refs[: 2 * len(jobs)]
+    halves = refs[: len(jobs)]
     wide_one, wide_two, wide_qkv, wide_proj, small_ref, sems = refs[-6:]
     outs = refs[-21:-6] if last else refs[-11:-6]
     down_hbm, up_hbm, qkv_hbm, out_hbm, proj_hbm = outs[:5]
@@ -777,17 +777,17 @@
     at = 0
     for job, (mine, group) in enumerate(jobs):
         owner = core if mine else 1 - core
-        one_ref, two_ref = halves[2 * job : 2 * job + 2]
+        both_ref = halves[job]
         for p, distance in enumerate(GROUPS[group]):
             block = owner * RING + block_at(owner, place, distance)
-            wide_one[at] = one_ref[p].astype(F32)
+            wide_one[at] = both_ref[p, :FIRST, :].astype(F32)
             rows = pl.ds(pl.multiple_of(block * DOWN, DOWN), DOWN)
             move(wide_one.at[at, :DOWN, :], down_hbm.at[rows, :])
             start = (block % (D // DOWN)) * DOWN
             columns = pl.ds(pl.multiple_of((block // (D // DOWN)) * D, D), D)
             rows = pl.ds(pl.multiple_of(start, DOWN), HEAD)
             move(wide_one.at[at, DOWN:, :], up_hbm.at[rows, columns])
-            wide = two_ref[p].astype(F32)
+            wide = both_ref[p, FIRST:, :].astype(F32)
             wide_two[at, :SHARE, :] = wide[3 * SHARE : 4 * SHARE, :]
             wide_two[at, SHARE:, :] = wide[REST // 16 :, :]
             rows = pl.ds(pl.multiple_of(start + HEAD, 16), TAIL)
@@ -804,12 +804,13 @@
             move(wide_proj.at[at], proj_hbm.at[rows, :])
             at += 1
     if last:
-        sources = refs[2 * len(jobs) : 2 * len(jobs) + 2 * len(GROUPS)]
+        sources = refs[len(jobs) : len(jobs) + 2 * len(GROUPS)]
         for k, ref in enumerate(sources):
             owner = core if k < len(GROUPS) else 1 - core
             for p, distance in enumerate(GROUPS[k % len(GROUPS)]):
                 block = owner * RING + block_at(owner, place, distance)
-                line = ref[p, 4 * SHARE : 4 * SHARE + 16, :].astype(F32)[8:, :]
+                start = FIRST + 4 * SHARE
+                line = ref[p, start : start + 16, :].astype(F32)[8:, :]
                 small_ref[pl.ds(pl.multiple_of(block * 8, 8), 8), :] = line
         rows = [small_ref[8 * k : 8 * k + 1, :] for k in range(14)]
         bqkv_ref, bout_ref, g1_ref, s1_ref, bup_ref, bdown_ref, g2_ref, s2_ref = outs[5:13]
@@ -892,8 +893,10 @@
 
 
 def join_blocks(*refs):
-    for k, ref in enumerate(refs[:-1]):
-        refs[-1][k] = ref[0]
+    half = (len(refs) - 1) // 2
+    for k in range(half):
+        refs[-1][k, :FIRST, :] = refs[k][0]
+        refs[-1][k, FIRST:, :] = refs[half + k][0]
 
 
 def ring_swap(value, onward):
@@ -932,7 +935,7 @@
     def __init__(self, keep, sends, others):
         self.keep, self.others, self.hop = keep, others, 0
         self.pairs = [swapped(send, 1) for send in sends]
-        self.sent, self.blocks, self.near, self.far = [], {}, [], []
+        self.sent, self.blocks = [], {}
 
     def blocks_call(self, blocks, places, held):
         return call(
@@ -998,14 +1001,15 @@
             self.sent = [(out[0], True), (out[1], False)]
         return out[0]
 
-    def share(self, group, after):
-        *blocks, _ = lax.optimization_barrier((*[self.blocks[k] for k in GROUPS[group]], after))
-        shape = (len(blocks), *blocks[0].shape[1:])
-        self.near += call(
-            join_blocks, blocks, [VMEM] * len(blocks), [shape_of(shape, BF16)], room=8, cost=0
-        )
-        self.far.append(swapped(self.near[-1], 1))
-        return self.near[-1]
+
+def share(pieces, group, after):
+    blocks = [piece.blocks[k] for piece in pieces for k in GROUPS[group]]
+    *blocks, _ = lax.optimization_barrier((*blocks, after))
+    shape = (len(GROUPS[group]), FIRST + SECOND, D)
+    (near,) = call(
+        join_blocks, blocks, [VMEM] * len(blocks), [shape_of(shape, BF16)], room=8, cost=0
+    )
+    return near, swapped(near, 1)
 
 
 def per_device(
@@ -1192,7 +1196,7 @@
         Summed(keep, sends, others)
         for keep, *sends in ((one_keep, one_send), (two_keep, two_ahead, two_send))
     ]
-    token, outs = d_sum, ()
+    token, outs, shared = d_sum, (), []
     for event in ORDER:
         kind, k, *group = event
         if kind == "tokens":
@@ -1209,13 +1213,15 @@
             continue
         if kind == "spread":
             jobs = event[1]
-            halves = [
-                (piece.near if mine else piece.far)[group] for mine, group in jobs for piece in (one, two)
-            ]
+            halves = [shared[group][0 if mine else 1] for mine, group in jobs]
             *halves, _ = lax.optimization_barrier((*halves, token))
-            others = [*two.near, *two.far] if event == ORDER[-1] else []
+            others = [pair[j] for j in range(2) for pair in shared] if event == ORDER[-1] else []
             outs = spread_call(size, jobs, halves, outs[:5], others)
             token = outs[0]
+            continue
+        if kind == "share":
+            shared.append(share((one, two), k, token))
+            token = shared[-1][0]
             continue
         piece = (one, two)[k]
         token = getattr(piece, kind)(*group, token)

time: 140 us -> 139 us (level)
    ppermute x20 -> x18, starting transfers between devices: 17.9 us -> 17 us  [swapped(): return lax.ppermute(value, axis, [(k, k ^ mask) for k in range(size)])]
    ppermute x20 -> x18, waiting for transfers between devices: 18.9 us -> 19.7 us  [swapped(): return lax.ppermute(value, axis, [(k, k ^ mask) for k in range(size)])]
    pallas_call x41 -> x39, Pallas kernels: 36.3 us -> 36.3 us  [call(): pl.pallas_call(kernel, out_shape=outs, in_specs=specs, out_specs=out_spec...]
  transfers between devices with their start and end apart: 49 -> 47, of which waited for: 35 -> 35; matrix products, arithmetic and copies ran while one was open for 0% -> 0% of each run, Pallas kernels for 12% -> 12%
where the time goes in v10:
time: 139 us
  starting transfers between devices  50 us (36%)
  waiting for transfers between devices  49.5 us (36%)
  Pallas kernels  36.3 us (26%)
  between operations  2.03 us (1%)
    pallas_call x39, Pallas kernels, call(): pl.pallas_call(kernel, out_shape=outs, in_specs=specs, out_specs=out_spec...  36.3 us
    ppermute x28, starting transfers between devices, ring_swap(): return lax.ppermute(value, 'dp', pairs)  30.6 us
    ppermute x28, waiting for transfers between devices, ring_swap(): return lax.ppermute(value, 'dp', pairs)  29.8 us
    ppermute x18, waiting for transfers between devices, swapped(): return lax.ppermute(value, axis, [(k, k ^ mask) for k in range(size)])  19.7 us
    ppermute x18, starting transfers between devices, swapped(): return lax.ppermute(value, axis, [(k, k ^ mask) for k in range(size)])  17 us
  transfers between devices with their start and end apart: 47, of which 35 were waited for; matrix products, arithmetic and copies ran while one was open for 0% of the time, Pallas kernels for 12%

profile of v10, /device:TPU:0, one launch (start us, length us, event | category | flops | bytes accessed | tf_op | source)
XLA Modules:
  0.0 139.1 jit_solution(5451391786143299314)
XLA Ops:
  0.7 6.8 %shard_map.297 = (bf16[272,128]{1,0:T(8,128)(2,1)S(1)}, bf16[256,2048]{1,0:T(8,128)(2,1)S(1)}, bf16[256,2048]{1,0:T(8,128)(2,1)S(1)}, f32[256,512]{1,0:T(8,128)S...) custom-call(s32[5,16]{1,0:T(8,128)} %bitcast.28, ...), custom_call_target="tpu_custom_call" | custom-call | flops 100000000 | bytes 10000000 | tf_op jit(solution)/shard_map/pallas_call | solution.py:872
  7.5 3.0 %collective-permute-start = (bf16[272,128]{1,0:T(8,128)(2,1)S(1)}, bf16[272,128]{1,0:T(8,128)(2,1)S(1)}, u32[]{:S(2)}, u32[]{:S(2)}) collective-permute-start(bf16[272,128]{1,0:T(8,128)(2,1)S(1)} %get-tuple-element.176), channel_id=1, source_target_pairs={{0,16},{16,0},{1,17},{17,1},{2,18},{18,2},{3,19},{19,3},{4,20},{20... | collective-permute-start | bytes 208904 | tf_op jit(solution)/shard_map/ppermute | solution.py:888
  10.5 1.5 %shard_map.298 = (bf16[256,2048]{1,0:T(8,128)(2,1)}, bf16[256,2048]{1,0:T(8,128)(2,1)}, f32[256,512]{1,0:T(8,128)}, f32[256,128]{1,0:T(8,128)}) custom-call(bf16[256,2048]{1,0:T(8,128)(2,1)S(1)} %get-tuple-element.177.refs_0_, bf16[256,2048]{1,0:T(8,128)(2,1)S(1)} %get-tuple-element.178.refs_1_, f32[256,512]{1,0:T(8,128)S(1)} %get-tuple-element.179.refs_2_, ...), custom_call_target="tpu_custom_call" | custom-call | flops 300000000 | bytes 30000000 | tf_op jit(solution)/shard_map/pallas_call | solution.py:872
  12.8 3.2 %collective-permute-start.2 = (bf16[256,128]{1,0:T(8,128)(2,1)S(1)}, bf16[256,128]{1,0:T(8,128)(2,1)S(1)}, u32[]{:S(2)}, u32[]{:S(2)}) collective-permute-start(bf16[256,128]{1,0:T(8,128)(2,1)S(1)} %slice_select_fusion.here_ref), channel_id=1, source_target_pairs={{0,8},{1,9},{2,10},{3,11},{4,12},{5,13},{6,14},{7,15},{8,0},{9,1},... | collective-permute-start | bytes 196616 | tf_op jit(solution)/shard_map/ppermute | solution.py:888
  16.0 1.6 %collective-permute-start.1 = (bf16[272,128]{1,0:T(8,128)(2,1)S(1)}, bf16[272,128]{1,0:T(8,128)(2,1)S(1)}, u32[]{:S(2)}, u32[]{:S(2)}) collective-permute-start(bf16[272,128]{1,0:T(8,128)(2,1)S(1)} %broadcast_select_fusion), channel_id=1, source_target_pairs={{0,2},{1,3},{2,0},{3,1},{4,6},{5,7},{6,4},{7,5},{8,10},{9,11},{10,... | collective-permute-start | bytes 208904 | tf_op jit(solution)/shard_map/ppermute | solution.py:888
  18.3 2.1 %collective-permute-done.1 = bf16[272,128]{1,0:T(8,128)(2,1)S(1)} collective-permute-done((bf16[272,128]{1,0:T(8,128)(2,1)S(1)}, bf16[272,128]{1,0:T(8,128)(2,1)S(1)}, u32[]{:S(2)}, u32[]{:S(2)}) %collective-permute-start.1) | collective-permute-done | bytes 69664 | tf_op jit(solution)/shard_map/ppermute | solution.py:888
  20.5 1.6 %collective-permute-start.4 = (bf16[256,128]{1,0:T(8,128)(2,1)S(1)}, bf16[256,128]{1,0:T(8,128)(2,1)S(1)}, u32[]{:S(2)}, u32[]{:S(2)}) collective-permute-start(bf16[256,128]{1,0:T(8,128)(2,1)S(1)} %shard_map.299.refs_0_), channel_id=1, source_target_pairs={{0,4},{1,5},{2,6},{3,7},{4,0},{5,1},{6,2},{7,3},{8,12},{9,13},{10,... | collective-permute-start | bytes 196616 | tf_op jit(solution)/shard_map/ppermute | solution.py:888
  22.8 2.2 %collective-permute-done.4.refs_1_ = bf16[256,128]{1,0:T(8,128)(2,1)S(1)} collective-permute-done((bf16[256,128]{1,0:T(8,128)(2,1)S(1)}, bf16[256,128]{1,0:T(8,128)(2,1)S(1)}, u32[]{:S(2)}, u32[]{:S(2)}) %collective-permute-start.4) | collective-permute-done | bytes 65568 | tf_op jit(solution)/shard_map/ppermute | solution.py:888
  25.0 2.8 %shard_map.300 = (f32[1024,128]{1,0:T(8,128)S(1)}, f32[32,128]{1,0:T(8,128)S(1)}, f32[32,128]{1,0:T(8,128)S(1)}, f32[32,128]{1,0:T(8,128)S(1)}) custom-call(f32[1]{0:T(128)} %bitcast.16.scale_ref, s32[5,16]{1,0:T(8,128)S(1)} %bitcast.29, bf16[544,128]{1,0:T(8,128)(2,1)S(1)} %pad_maximum_fusion.near_ref, bf16[544,128]{1,0:T(8,128)(2,1)S(1)} %collective-permute-done.3.far_ref, ...), custom_call_target="tpu_custom_call" | custom-call | flops 100000000 | bytes 10000000 | tf_op jit(solution)/shard_map/pallas_call | solution.py:872
  29.0 2.4 %collective-permute-start.8 = (f32[32,128]{1,0:T(8,128)S(1)}, f32[32,128]{1,0:T(8,128)S(1)}, u32[]{:S(2)}, u32[]{:S(2)}) collective-permute-start(f32[32,128]{1,0:T(8,128)S(1)} %add.3.own_ref), channel_id=1, source_target_pairs={{0,18},{1,19},{2,16},{3,17},{4,22},{5,23},{6,20},{7,21},{8,26},{9,... | collective-permute-start | bytes 49160 | tf_op jit(solution)/shard_map/ppermute | solution.py:1133
  32.5 1.5 %shard_map.301 = (bf16[3,1024,128]{2,1,0:T(8,128)(2,1)S(1)}, bf16[3,128,1024]{2,1,0:T(8,128)(2,1)S(1)}, f32[1024,128]{1,0:T(8,128)S(1)}, bf16[3,128,512]{2,1,0:T...) custom-call(bf16[544,128]{1,0:T(8,128)(2,1)S(1)} %pad_maximum_fusion.near_ref, ...), custom_call_target="tpu_custom_call" | custom-call | flops 100000000 | bytes 10000000 | tf_op jit(solution)/shard_map/pallas_call | solution.py:872
  35.8 3.6 %shard_map.302 = (bf16[512,128]{1,0:T(8,128)(2,1)S(1)}, bf16[512,128]{1,0:T(8,128)(2,1)S(1)}, bf16[256,128]{1,0:T(8,128)(2,1)S(1)}, bf16[256,128]{1,0:T(8,128)(2,1)S(1)}, f32[8,128]{1,0:T(8,128)S(1)}) custom-call(f32[1]{0:T(128)} %bitcast.17.scale_ref, s32[5,16]{1,0:T(8,128)S(1)} %bitcast.30, f32[1024,128]{1,0:T(8,128)S(1)} %get-tuple-element.184.totals_ref, ...), custom_call_target="tpu_custom_call" | custom-call | flops 100000000 | bytes 10000000 | tf_op jit(solution)/shard_map/pallas_call | solution.py:872
  39.5 1.6 %collective-permute-start.11 = (bf16[256,128]{1,0:T(8,128)(2,1)S(1)}, bf16[256,128]{1,0:T(8,128)(2,1)S(1)}, u32[]{:S(2)}, u32[]{:S(2)}) collective-permute-start(bf16[256,128]{1,0:T(8,128)(2,1)S(1)} %get-tuple-element.197), channel_id=1, source_target_pairs={{0,4},{1,5},{2,6},{3,7},{4,0},{5,1},{6,2},{7,3},{8,12},{9,13},{10,... | collective-permute-start | bytes 196616 | tf_op jit(solution)/shard_map/ppermute | solution.py:888
  41.2 2.8 %collective-permute-done.11.got_ref = bf16[256,128]{1,0:T(8,128)(2,1)S(1)} collective-permute-done((bf16[256,128]{1,0:T(8,128)(2,1)S(1)}, bf16[256,128]{1,0:T(8,128)(2,1)S(1)}, u32[]{:S(2)}, u32[]{:S(2)}) %collective-permute-start.11) | collective-permute-done | bytes 65568 | tf_op jit(solution)/shard_map/ppermute | solution.py:888
  44.1 1.3 collective-permute-start.12
  45.9 3.8 %collective-permute-done.12.got_ref = bf16[256,128]{1,0:T(8,128)(2,1)S(1)} collective-permute-done((bf16[256,128]{1,0:T(8,128)(2,1)S(1)}, bf16[256,128]{1,0:T(8,128)(2,1)S(1)}, u32[]{:S(2)}, u32[]{:S(2)}) %collective-permute-start.12) | collective-permute-done | bytes 65568 | tf_op jit(solution)/shard_map/ppermute | solution.py:888
  49.8 1.7 %collective-permute-start.13 = (bf16[256,128]{1,0:T(8,128)(2,1)S(1)}, bf16[256,128]{1,0:T(8,128)(2,1)S(1)}, u32[]{:S(2)}, u32[]{:S(2)}) collective-permute-start(bf16[256,128]{1,0:T(8,128)(2,1)S(1)} %broadcast_select_fusion.1), channel_id=1, source_target_pairs={{0,16},{16,0},{1,17},{17,1},{2,18},{18,2},{3,19},{19,3},{4,20},{20... | collective-permute-start | bytes 196616 | tf_op jit(solution)/shard_map/ppermute | solution.py:888
  51.5 2.8 %collective-permute-done.13.got_ref = bf16[256,128]{1,0:T(8,128)(2,1)S(1)} collective-permute-done((bf16[256,128]{1,0:T(8,128)(2,1)S(1)}, bf16[256,128]{1,0:T(8,128)(2,1)S(1)}, u32[]{:S(2)}, u32[]{:S(2)}) %collective-permute-start.13) | collective-permute-done | bytes 65568 | tf_op jit(solution)/shard_map/ppermute | solution.py:888
  54.4 4.8 %shard_map.307 = (bf16[8,208,512]{2,1,0:T(8,128)(2,1)S(1)}, bf16[8,208,512]{2,1,0:T(8,128)(2,1)S(1)}, bf16[8,48,512]{2,1,0:T(8,128)(2,1)S(1)}, bf16[8,48,512]{2,...) custom-call(bf16[256,128]{1,0:T(8,128)(2,1)S(1)} %shard_map.306.dq_ref, ...), custom_call_target="tpu_custom_call" | custom-call | flops 100000000 | bytes 10000000 | tf_op jit(solution)/shard_map/pallas_call | solution.py:872
  59.4 3.7 %shard_map.308 = (bf16[8,192,512]{2,1,0:T(8,128)(2,1)S(1)}, bf16[2,192,512]{2,1,0:T(8,128)(2,1)S(1)}, bf16[6,192,512]{2,1,0:T(8,128)(2,1)S(1)}, f32[256,512]{1,0:T(8,128)S(1)}, bf16[256,1536]{1,0:T(8,128)(2,1)S(1)}) custom-call(f32[256,512]{1,0:T(8,128)S(1)} %get-tuple-element.207.dfirst_ref, f32[512,128]{1,0:T(8,128)S(1)} %get-tuple-element.208.gproj_ref, ...), custom_call_target="tpu_custom_call" | custom-call | flops 100000000 | bytes 10000000 | tf_op jit(solution)/shard_map/pallas_call | solution.py:872
  63.8 1.8 %collective-permute-start.15 = (bf16[1,208,512]{2,1,0:T(8,128)(2,1)S(1)}, bf16[1,208,512]{2,1,0:T(8,128)(2,1)S(1)}, u32[]{:S(2)}, u32[]{:S(2)}) collective-permute-start(bf16[1,208,512]{2,1,0:T(8,128)(2,1)S(1)} %get-tuple-element.221), channel_id=1, source_target_pairs={{0,4},{1,3},{2,0},{3,7},{4,8},{5,1},{6,2},{7,11},{8,12},{9,5},{10,... | collective-permute-start | bytes 638984 | tf_op jit(solution)/shard_map/ppermute | solution.py:909
  67.3 1.5 %collective-permute-start.21 = (bf16[1,192,512]{2,1,0:T(8,128)(2,1)S(1)}, bf16[1,192,512]{2,1,0:T(8,128)(2,1)S(1)}, u32[]{:S(2)}, u32[]{:S(2)}) collective-permute-start(bf16[1,192,512]{2,1,0:T(8,128)(2,1)S(1)} %get-tuple-element.237), channel_id=1, source_target_pairs={{0,4},{1,3},{2,0},{3,7},{4,8},{5,1},{6,2},{7,11},{8,12},{9,5},{10,... | collective-permute-start | bytes 589832 | tf_op jit(solution)/shard_map/ppermute | solution.py:909
  70.6 1.4 %shard_map.313 = f32[256,512]{1,0:T(8,128)} custom-call(f32[256,512]{1,0:T(8,128)S(1)} %get-tuple-element.231.dsum_ref, bf16[256,1536]{1,0:T(8,128)(2,1)S(1)} %get-tuple-element.232.djoined_ref, bf16[512,1536]{1,0:T(8,128)(2,1)S(1)} %bitcast.21), custom_call_target="tpu_custom_call" | custom-call | flops 300000000 | bytes 30000000 | tf_op jit(solution)/shard_map/pallas_call | solution.py:872
  72.6 1.8 %collective-permute-start.19 = (bf16[1,208,512]{2,1,0:T(8,128)(2,1)S(1)}, bf16[1,208,512]{2,1,0:T(8,128)(2,1)S(1)}, u32[]{:S(2)}, u32[]{:S(2)}) collective-permute-start(bf16[1,208,512]{2,1,0:T(8,128)(2,1)S(1)} %get-tuple-element.235), channel_id=1, source_target_pairs={{0,4},{1,3},{2,0},{3,7},{4,8},{5,1},{6,2},{7,11},{8,12},{9,5},{10,... | collective-permute-start | bytes 638984 | tf_op jit(solution)/shard_map/ppermute | solution.py:909
  74.4 1.8 %collective-permute-done.21.refs_0_ = bf16[1,192,512]{2,1,0:T(8,128)(2,1)S(1)} collective-permute-done((bf16[1,192,512]{2,1,0:T(8,128)(2,1)S(1)}, bf16[1,192,512]{2,1,0:T(8,128)(2,1)S(1)}, u32[]{:S(2)}, u32[]{:S(2)}) %collective-permute-start.21) | collective-permute-done | bytes 196640 | tf_op jit(solution)/shard_map/ppermute | solution.py:909
  77.0 1.4 collective-permute-start.25
  78.4 2.1 %collective-permute-done.20.refs_1_ = bf16[1,208,512]{2,1,0:T(8,128)(2,1)S(1)} collective-permute-done((bf16[1,208,512]{2,1,0:T(8,128)(2,1)S(1)}, bf16[1,208,512]{2,1,0:T(8,128)(2,1)S(1)}, u32[]{:S(2)}, u32[]{:S(2)}) %collective-permute-start.20) | collective-permute-done | bytes 213024 | tf_op jit(solution)/shard_map/ppermute | solution.py:909
  80.9 2.1 %collective-permute-start.24 = (bf16[1,208,512]{2,1,0:T(8,128)(2,1)S(1)}, bf16[1,208,512]{2,1,0:T(8,128)(2,1)S(1)}, u32[]{:S(2)}, u32[]{:S(2)}) collective-permute-start(bf16[1,208,512]{2,1,0:T(8,128)(2,1)S(1)} %get-tuple-element.244), channel_id=1, source_target_pairs={{0,2},{1,5},{2,6},{3,1},{4,0},{5,9},{6,10},{7,3},{8,4},{9,13},{10,... | collective-permute-start | bytes 638984 | tf_op jit(solution)/shard_map/ppermute | solution.py:909
  83.0 1.6 %collective-permute-done.26.refs_1_ = bf16[1,192,512]{2,1,0:T(8,128)(2,1)S(1)} collective-permute-done((bf16[1,192,512]{2,1,0:T(8,128)(2,1)S(1)}, bf16[1,192,512]{2,1,0:T(8,128)(2,1)S(1)}, u32[]{:S(2)}, u32[]{:S(2)}) %collective-permute-start.26) | collective-permute-done | bytes 196640 | tf_op jit(solution)/shard_map/ppermute | solution.py:909
  85.1 2.1 %collective-permute-start.29 = (bf16[1,192,512]{2,1,0:T(8,128)(2,1)S(1)}, bf16[1,192,512]{2,1,0:T(8,128)(2,1)S(1)}, u32[]{:S(2)}, u32[]{:S(2)}) collective-permute-start(bf16[1,192,512]{2,1,0:T(8,128)(2,1)S(1)} %get-tuple-element.252), channel_id=1, source_target_pairs={{0,2},{1,5},{2,6},{3,1},{4,0},{5,9},{6,10},{7,3},{8,4},{9,13},{10,... | collective-permute-start | bytes 589832 | tf_op jit(solution)/shard_map/ppermute | solution.py:909
  87.2 2.0 %collective-permute-done.24.refs_1_ = bf16[1,208,512]{2,1,0:T(8,128)(2,1)S(1)} collective-permute-done((bf16[1,208,512]{2,1,0:T(8,128)(2,1)S(1)}, bf16[1,208,512]{2,1,0:T(8,128)(2,1)S(1)}, u32[]{:S(2)}, u32[]{:S(2)}) %collective-permute-start.24) | collective-permute-done | bytes 213024 | tf_op jit(solution)/shard_map/ppermute | solution.py:909
  89.2 1.7 %collective-permute-done.23.refs_0_ = bf16[1,208,512]{2,1,0:T(8,128)(2,1)S(1)} collective-permute-done((bf16[1,208,512]{2,1,0:T(8,128)(2,1)S(1)}, bf16[1,208,512]{2,1,0:T(8,128)(2,1)S(1)}, u32[]{:S(2)}, u32[]{:S(2)}) %collective-permute-start.23) | collective-permute-done | bytes 213024 | tf_op jit(solution)/shard_map/ppermute | solution.py:909
  91.6 1.9 %collective-permute-done.29.refs_1_ = bf16[1,192,512]{2,1,0:T(8,128)(2,1)S(1)} collective-permute-done((bf16[1,192,512]{2,1,0:T(8,128)(2,1)S(1)}, bf16[1,192,512]{2,1,0:T(8,128)(2,1)S(1)}, u32[]{:S(2)}, u32[]{:S(2)}) %collective-permute-start.29) | collective-permute-done | bytes 196640 | tf_op jit(solution)/shard_map/ppermute | solution.py:909
  93.5 2.1 %collective-permute-start.32 = (bf16[1,192,512]{2,1,0:T(8,128)(2,1)S(1)}, bf16[1,192,512]{2,1,0:T(8,128)(2,1)S(1)}, u32[]{:S(2)}, u32[]{:S(2)}) collective-permute-start(bf16[1,192,512]{2,1,0:T(8,128)(2,1)S(1)} %get-tuple-element.255), channel_id=1, source_target_pairs={{0,4},{1,3},{2,0},{3,7},{4,8},{5,1},{6,2},{7,11},{8,12},{9,5},{10,... | collective-permute-start | bytes 589832 | tf_op jit(solution)/shard_map/ppermute | solution.py:909
  100.2 2.6 %collective-permute-start.36 = (bf16[1,192,512]{2,1,0:T(8,128)(2,1)S(1)}, bf16[1,192,512]{2,1,0:T(8,128)(2,1)S(1)}, u32[]{:S(2)}, u32[]{:S(2)}) collective-permute-start(bf16[1,192,512]{2,1,0:T(8,128)(2,1)S(1)} %shard_map.321.refs_7_), channel_id=1, source_target_pairs={{0,2},{1,5},{2,6},{3,1},{4,0},{5,9},{6,10},{7,3},{8,4},{9,13},{10,... | collective-permute-start | bytes 589832 | tf_op jit(solution)/shard_map/ppermute | solution.py:909
  102.8 2.3 %collective-permute-done.31.refs_1_ = bf16[1,208,512]{2,1,0:T(8,128)(2,1)S(1)} collective-permute-done((bf16[1,208,512]{2,1,0:T(8,128)(2,1)S(1)}, bf16[1,208,512]{2,1,0:T(8,128)(2,1)S(1)}, u32[]{:S(2)}, u32[]{:S(2)}) %collective-permute-start.31) | collective-permute-done | bytes 213024 | tf_op jit(solution)/shard_map/ppermute | solution.py:909
  106.0 1.9 %collective-permute-start.34 = (bf16[1,208,512]{2,1,0:T(8,128)(2,1)S(1)}, bf16[1,208,512]{2,1,0:T(8,128)(2,1)S(1)}, u32[]{:S(2)}, u32[]{:S(2)}) collective-permute-start(bf16[1,208,512]{2,1,0:T(8,128)(2,1)S(1)} %get-tuple-element.290.refs_6_), channel_id=1, source_target_pairs={{0,2},{1,5},{2,6},{3,1},{4,0},{5,9},{6,10},{7,3},{8,4},{9,13},{10,... | collective-permute-start | bytes 638984 | tf_op jit(solution)/shard_map/ppermute | solution.py:909
  110.6 1.5 %collective-permute-start.40 = (bf16[1,192,512]{2,1,0:T(8,128)(2,1)S(1)}, bf16[1,192,512]{2,1,0:T(8,128)(2,1)S(1)}, u32[]{:S(2)}, u32[]{:S(2)}) collective-permute-start(bf16[1,192,512]{2,1,0:T(8,128)(2,1)S(1)} %get-tuple-element.297.refs_13_), channel_id=1, source_target_pairs={{0,2},{1,5},{2,6},{3,1},{4,0},{5,9},{6,10},{7,3},{8,4},{9,13},{10,... | collective-permute-start | bytes 589832 | tf_op jit(solution)/shard_map/ppermute | solution.py:909
  112.7 1.5 %collective-permute-done.34.refs_1_ = bf16[1,208,512]{2,1,0:T(8,128)(2,1)S(1)} collective-permute-done((bf16[1,208,512]{2,1,0:T(8,128)(2,1)S(1)}, bf16[1,208,512]{2,1,0:T(8,128)(2,1)S(1)}, u32[]{:S(2)}, u32[]{:S(2)}) %collective-permute-start.34) | collective-permute-done | bytes 213024 | tf_op jit(solution)/shard_map/ppermute | solution.py:909
  115.4 1.7 %collective-permute-start.38 = (bf16[1,208,512]{2,1,0:T(8,128)(2,1)S(1)}, bf16[1,208,512]{2,1,0:T(8,128)(2,1)S(1)}, u32[]{:S(2)}, u32[]{:S(2)}) collective-permute-start(bf16[1,208,512]{2,1,0:T(8,128)(2,1)S(1)} %get-tuple-element.289.refs_5_), channel_id=1, source_target_pairs={{0,2},{1,5},{2,6},{3,1},{4,0},{5,9},{6,10},{7,3},{8,4},{9,13},{10,... | collective-permute-start | bytes 638984 | tf_op jit(solution)/shard_map/ppermute | solution.py:909
  118.5 1.3 collective-permute-done.39.refs_0_
  119.8 1.5 %collective-permute-start.43 = (bf16[1,192,512]{2,1,0:T(8,128)(2,1)S(1)}, bf16[1,192,512]{2,1,0:T(8,128)(2,1)S(1)}, u32[]{:S(2)}, u32[]{:S(2)}) collective-permute-start(bf16[1,192,512]{2,1,0:T(8,128)(2,1)S(1)} %get-tuple-element.296.refs_12_), channel_id=1, source_target_pairs={{0,2},{1,5},{2,6},{3,1},{4,0},{5,9},{6,10},{7,3},{8,4},{9,13},{10,... | collective-permute-start | bytes 589832 | tf_op jit(solution)/shard_map/ppermute | solution.py:909
  121.9 1.8 %collective-permute-done.38.refs_1_ = bf16[1,208,512]{2,1,0:T(8,128)(2,1)S(1)} collective-permute-done((bf16[1,208,512]{2,1,0:T(8,128)(2,1)S(1)}, bf16[1,208,512]{2,1,0:T(8,128)(2,1)S(1)}, u32[]{:S(2)}, u32[]{:S(2)}) %collective-permute-start.38) | collective-permute-done | bytes 213024 | tf_op jit(solution)/shard_map/ppermute | solution.py:909
  123.9 2.1 %collective-permute-done.43.refs_1_ = bf16[1,192,512]{2,1,0:T(8,128)(2,1)S(1)} collective-permute-done((bf16[1,192,512]{2,1,0:T(8,128)(2,1)S(1)}, bf16[1,192,512]{2,1,0:T(8,128)(2,1)S(1)}, u32[]{:S(2)}, u32[]{:S(2)}) %collective-permute-start.43) | collective-permute-done | bytes 196640 | tf_op jit(solution)/shard_map/ppermute | solution.py:909
  128.0 1.3 collective-permute-start.45
  129.3 2.8 %shard_map.329 = (f32[2048,512]{1,0:T(8,128)}, f32[512,2048]{1,0:T(8,128)}, f32[512,1536]{1,0:T(8,128)}, f32[512,512]{1,0:T(8,128)}, f32[512,128]{1,0:T(8,128)}) custom-call(bf16[7,400,512]{2,1,0:T(8,128)(2,1)S(1)} %shard_map.328.refs_0_.refs_1_), custom_call_target="tpu_custom_call" | custom-call | tf_op jit(solution)/shard_map/pallas_call | solution.py:872
  132.5 2.8 %shard_map.330 = (f32[2048,512]{1,0:T(8,128)}, f32[512,2048]{1,0:T(8,128)}, f32[512,1536]{1,0:T(8,128)}, f32[512,512]{1,0:T(8,128)}, f32[512,128]{1,0:T(8,128)}) custom-call(bf16[7,400,512]{2,1,0:T(8,128)(2,1)S(1)} %collective-permute-done.44.refs_0_.refs_3_, ...), custom_call_target="tpu_custom_call", output_to_operand_aliasing={{0}: (1, {}), {1}: (2, {}), {2}: (3, {}), {3}: (4, {}), {4}... | custom-call | tf_op jit(solution)/shard_map/pallas_call | solution.py:872
  137.3 1.6 %shard_map.335 = (f32[2048,512]{1,0:T(8,128)}, f32[512,2048]{1,0:T(8,128)}, f32[512,1536]{1,0:T(8,128)}, f32[512,512]{1,0:T(8,128)}, f32[512,128]{1,0:T(8,128)},...) custom-call(bf16[1,400,512]{2,1,0:T(8,128)(2,1)S(1)} %collective-per, ...), custom_call_target="tpu_custom_call", output_to_operand_aliasing={{0}: (5, {}), {1}: (6, {}), {2}: (7, {}), {3}: (8, {}), {4}... | custom-call | tf_op jit(solution)/shard_map/pallas_call | solution.py:872
  (125 shorter events, 30.2 us)
Async XLA Ops:
  7.5 5.3 %collective-permute-start = (bf16[272,128]{1,0:T(8,128)(2,1)S(1)}, bf16[272,128]{1,0:T(8,128)(2,1)S(1)}, u32[]{:S(2)}, u32[]{:S(2)}) collective-permute-start(bf16[272,128]{1,0:T(8,128)(2,1)S(1)} %get-tuple-element.176), channel_id=1, source_target_pairs={{0,16},{16,0},{1,17},{17,1},{2,18},{18,2},{3,19},{19,3},{4,20},{20... | collective-permute-start | bytes 208904 | tf_op jit(solution)/shard_map/ppermute | solution.py:888
  12.8 5.4 %collective-permute-start.2 = (bf16[256,128]{1,0:T(8,128)(2,1)S(1)}, bf16[256,128]{1,0:T(8,128)(2,1)S(1)}, u32[]{:S(2)}, u32[]{:S(2)}) collective-permute-start(bf16[256,128]{1,0:T(8,128)(2,1)S(1)} %slice_select_fusion.here_ref), channel_id=1, source_target_pairs={{0,8},{1,9},{2,10},{3,11},{4,12},{5,13},{6,14},{7,15},{8,0},{9,1},... | collective-permute-start | bytes 196616 | tf_op jit(solution)/shard_map/ppermute | solution.py:888
  16.0 4.4 %collective-permute-start.1 = (bf16[272,128]{1,0:T(8,128)(2,1)S(1)}, bf16[272,128]{1,0:T(8,128)(2,1)S(1)}, u32[]{:S(2)}, u32[]{:S(2)}) collective-permute-start(bf16[272,128]{1,0:T(8,128)(2,1)S(1)} %broadcast_select_fusion), channel_id=1, source_target_pairs={{0,2},{1,3},{2,0},{3,1},{4,6},{5,7},{6,4},{7,5},{8,10},{9,11},{10,... | collective-permute-start | bytes 208904 | tf_op jit(solution)/shard_map/ppermute | solution.py:888
  20.4 4.6 %collective-permute-start.3 = (bf16[544,128]{1,0:T(8,128)(2,1)S(1)}, bf16[544,128]{1,0:T(8,128)(2,1)S(1)}, u32[]{:S(2)}, u32[]{:S(2)}) collective-permute-start(bf16[544,128]{1,0:T(8,128)(2,1)S(1)} %pad_maximum_fusion.near_ref), channel_id=1, source_target_pairs={{0,1},{1,0},{2,3},{3,2},{4,5},{5,4},{6,7},{7,6},{8,9},{9,8},{10,11... | collective-permute-start | bytes 417800 | tf_op jit(solution)/shard_map/ppermute | solution.py:888
  20.5 4.5 %collective-permute-start.4 = (bf16[256,128]{1,0:T(8,128)(2,1)S(1)}, bf16[256,128]{1,0:T(8,128)(2,1)S(1)}, u32[]{:S(2)}, u32[]{:S(2)}) collective-permute-start(bf16[256,128]{1,0:T(8,128)(2,1)S(1)} %shard_map.299.refs_0_), channel_id=1, source_target_pairs={{0,4},{1,5},{2,6},{3,7},{4,0},{5,1},{6,2},{7,3},{8,12},{9,13},{10,... | collective-permute-start | bytes 196616 | tf_op jit(solution)/shard_map/ppermute | solution.py:888
  27.8 1.2 collective-permute-start.5
  29.0 5.0 %collective-permute-start.8 = (f32[32,128]{1,0:T(8,128)S(1)}, f32[32,128]{1,0:T(8,128)S(1)}, u32[]{:S(2)}, u32[]{:S(2)}) collective-permute-start(f32[32,128]{1,0:T(8,128)S(1)} %add.3.own_ref), channel_id=1, source_target_pairs={{0,18},{1,19},{2,16},{3,17},{4,22},{5,23},{6,20},{7,21},{8,26},{9,... | collective-permute-start | bytes 49160 | tf_op jit(solution)/shard_map/ppermute | solution.py:1133
  31.5 3.7 %collective-permute-start.7 = (f32[32,128]{1,0:T(8,128)S(1)}, f32[32,128]{1,0:T(8,128)S(1)}, u32[]{:S(2)}, u32[]{:S(2)}) collective-permute-start(f32[32,128]{1,0:T(8,128)S(1)} %add.3.own_ref), channel_id=1, source_target_pairs={{0,16},{16,0},{1,17},{17,1},{2,18},{18,2},{3,19},{19,3},{4,20},{20... | collective-permute-start | bytes 49160 | tf_op jit(solution)/shard_map/ppermute | solution.py:888
  32.0 3.7 %collective-permute-start.6 = (f32[32,128]{1,0:T(8,128)S(1)}, f32[32,128]{1,0:T(8,128)S(1)}, u32[]{:S(2)}, u32[]{:S(2)}) collective-permute-start(f32[32,128]{1,0:T(8,128)S(1)} %add.3.own_ref), channel_id=1, source_target_pairs={{0,2},{1,3},{2,0},{3,1},{4,6},{5,7},{6,4},{7,5},{8,10},{9,11},{10,... | collective-permute-start | bytes 49160 | tf_op jit(solution)/shard_map/ppermute | solution.py:888
  35.8 18.5 %copy-start.13 = (f32[256,128]{1,0:T(8,128)S(1)}, f32[256,128]{1,0:T(8,128)}, u32[]{:S(2)}) copy-start(f32[256,128]{1,0:T(8,128)} %get-tuple-element.181.rs2_ref) | copy-start | bytes 393220
  39.4 1.7 %collective-permute-start.9 = (bf16[512,128]{1,0:T(8,128)(2,1)S(1)}, bf16[512,128]{1,0:T(8,128)(2,1)S(1)}, u32[]{:S(2)}, u32[]{:S(2)}) collective-permute-start(bf16[512,128]{1,0:T(8,128)(2,1)S(1)} %get-tuple-element.195), channel_id=1, source_target_pairs={{0,1},{1,0},{2,3},{3,2},{4,5},{5,4},{6,7},{7,6},{8,9},{9,8},{10,11... | collective-permute-start | bytes 393224 | tf_op jit(solution)/shard_map/ppermute | solution.py:888
  39.5 4.5 %collective-permute-start.11 = (bf16[256,128]{1,0:T(8,128)(2,1)S(1)}, bf16[256,128]{1,0:T(8,128)(2,1)S(1)}, u32[]{:S(2)}, u32[]{:S(2)}) collective-permute-start(bf16[256,128]{1,0:T(8,128)(2,1)S(1)} %get-tuple-element.197), channel_id=1, source_target_pairs={{0,4},{1,5},{2,6},{3,7},{4,0},{5,1},{6,2},{7,3},{8,12},{9,13},{10,... | collective-permute-start | bytes 196616 | tf_op jit(solution)/shard_map/ppermute | solution.py:888
  44.1 5.6 %collective-permute-start.12 = (bf16[256,128]{1,0:T(8,128)(2,1)S(1)}, bf16[256,128]{1,0:T(8,128)(2,1)S(1)}, u32[]{:S(2)}, u32[]{:S(2)}) collective-permute-start(bf16[256,128]{1,0:T(8,128)(2,1)S(1)} %shard_map.304.rows_ref), channel_id=1, source_target_pairs={{0,8},{1,9},{2,10},{3,11},{4,12},{5,13},{6,14},{7,15},{8,0},{9,1},... | collective-permute-start | bytes 196616 | tf_op jit(solution)/shard_map/ppermute | solution.py:888
  45.4 4.4 %collective-permute-start.10 = (bf16[256,128]{1,0:T(8,128)(2,1)S(1)}, bf16[256,128]{1,0:T(8,128)(2,1)S(1)}, u32[]{:S(2)}, u32[]{:S(2)}) collective-permute-start(bf16[256,128]{1,0:T(8,128)(2,1)S(1)} %get-tuple-element.336), channel_id=1, source_target_pairs={{0,2},{1,3},{2,0},{3,1},{4,6},{5,7},{6,4},{7,5},{8,10},{9,11},{10,... | collective-permute-start | bytes 196616 | tf_op jit(solution)/shard_map/ppermute | solution.py:888
  49.8 4.5 %collective-permute-start.13 = (bf16[256,128]{1,0:T(8,128)(2,1)S(1)}, bf16[256,128]{1,0:T(8,128)(2,1)S(1)}, u32[]{:S(2)}, u32[]{:S(2)}) collective-permute-start(bf16[256,128]{1,0:T(8,128)(2,1)S(1)} %broadcast_select_fusion.1), channel_id=1, source_target_pairs={{0,16},{16,0},{1,17},{17,1},{2,18},{18,2},{3,19},{19,3},{4,20},{20... | collective-permute-start | bytes 196616 | tf_op jit(solution)/shard_map/ppermute | solution.py:888
  59.2 4.5 %collective-permute-start.14 = (bf16[8,208,512]{2,1,0:T(8,128)(2,1)S(1)}, bf16[8,208,512]{2,1,0:T(8,128)(2,1)S(1)}, u32[]{:S(2)}, u32[]{:S(2)}) collective-permute-start(bf16[8,208,512]{2,1,0:T(8,128)(2,1)S(1)} %get-tuple-element.206), channel_id=1, source_target_pairs={{0,1},{1,0},{2,3},{3,2},{4,5},{5,4},{6,7},{7,6},{8,9},{9,8},{10,11... | collective-permute-start | bytes 5111816 | tf_op jit(solution)/shard_map/ppermute | solution.py:888
  63.1 6.1 %collective-permute-start.18 = (bf16[6,192,512]{2,1,0:T(8,128)(2,1)S(1)}, bf16[6,192,512]{2,1,0:T(8,128)(2,1)S(1)}, u32[]{:S(2)}, u32[]{:S(2)}) collective-permute-start(bf16[6,192,512]{2,1,0:T(8,128)(2,1)S(1)} %get-tuple-element.230), channel_id=1, source_target_pairs={{0,1},{1,0},{2,3},{3,2},{4,5},{5,4},{6,7},{7,6},{8,9},{9,8},{10,11... | collective-permute-start | bytes 3538952 | tf_op jit(solution)/shard_map/ppermute | solution.py:888
  63.6 3.0 %collective-permute-start.17 = (bf16[2,192,512]{2,1,0:T(8,128)(2,1)S(1)}, bf16[2,192,512]{2,1,0:T(8,128)(2,1)S(1)}, u32[]{:S(2)}, u32[]{:S(2)}) collective-permute-start(bf16[2,192,512]{2,1,0:T(8,128)(2,1)S(1)} %get-tuple-element.224), channel_id=1, source_target_pairs={{0,1},{1,0},{2,3},{3,2},{4,5},{5,4},{6,7},{7,6},{8,9},{9,8},{10,11... | collective-permute-start | bytes 1179656 | tf_op jit(solution)/shard_map/ppermute | solution.py:888
  63.8 8.2 %collective-permute-start.15 = (bf16[1,208,512]{2,1,0:T(8,128)(2,1)S(1)}, bf16[1,208,512]{2,1,0:T(8,128)(2,1)S(1)}, u32[]{:S(2)}, u32[]{:S(2)}) collective-permute-start(bf16[1,208,512]{2,1,0:T(8,128)(2,1)S(1)} %get-tuple-element.221), channel_id=1, source_target_pairs={{0,4},{1,3},{2,0},{3,7},{4,8},{5,1},{6,2},{7,11},{8,12},{9,5},{10,... | collective-permute-start | bytes 638984 | tf_op jit(solution)/shard_map/ppermute | solution.py:909
  65.6 6.4 %collective-permute-start.16 = (bf16[1,208,512]{2,1,0:T(8,128)(2,1)S(1)}, bf16[1,208,512]{2,1,0:T(8,128)(2,1)S(1)}, u32[]{:S(2)}, u32[]{:S(2)}) collective-permute-start(bf16[1,208,512]{2,1,0:T(8,128)(2,1)S(1)} %get-tuple-element.222), channel_id=1, source_target_pairs={{0,2},{1,5},{2,6},{3,1},{4,0},{5,9},{6,10},{7,3},{8,4},{9,13},{10,... | collective-permute-start | bytes 638984 | tf_op jit(solution)/shard_map/ppermute | solution.py:909
  66.8 9.4 %collective-permute-start.22 = (bf16[1,192,512]{2,1,0:T(8,128)(2,1)S(1)}, bf16[1,192,512]{2,1,0:T(8,128)(2,1)S(1)}, u32[]{:S(2)}, u32[]{:S(2)}) collective-permute-start(bf16[1,192,512]{2,1,0:T(8,128)(2,1)S(1)} %get-tuple-element.227), channel_id=1, source_target_pairs={{0,2},{1,5},{2,6},{3,1},{4,0},{5,9},{6,10},{7,3},{8,4},{9,13},{10,... | collective-permute-start | bytes 589832 | tf_op jit(solution)/shard_map/ppermute | solution.py:909
  67.3 8.9 %collective-permute-start.21 = (bf16[1,192,512]{2,1,0:T(8,128)(2,1)S(1)}, bf16[1,192,512]{2,1,0:T(8,128)(2,1)S(1)}, u32[]{:S(2)}, u32[]{:S(2)}) collective-permute-start(bf16[1,192,512]{2,1,0:T(8,128)(2,1)S(1)} %get-tuple-element.237), channel_id=1, source_target_pairs={{0,4},{1,3},{2,0},{3,7},{4,8},{5,1},{6,2},{7,11},{8,12},{9,5},{10,... | collective-permute-start | bytes 589832 | tf_op jit(solution)/shard_map/ppermute | solution.py:909
  72.1 8.3 %collective-permute-start.20 = (bf16[1,208,512]{2,1,0:T(8,128)(2,1)S(1)}, bf16[1,208,512]{2,1,0:T(8,128)(2,1)S(1)}, u32[]{:S(2)}, u32[]{:S(2)}) collective-permute-start(bf16[1,208,512]{2,1,0:T(8,128)(2,1)S(1)} %get-tuple-element.236), channel_id=1, source_target_pairs={{0,2},{1,5},{2,6},{3,1},{4,0},{5,9},{6,10},{7,3},{8,4},{9,13},{10,... | collective-permute-start | bytes 638984 | tf_op jit(solution)/shard_map/ppermute | solution.py:909
  72.6 8.1 %collective-permute-start.19 = (bf16[1,208,512]{2,1,0:T(8,128)(2,1)S(1)}, bf16[1,208,512]{2,1,0:T(8,128)(2,1)S(1)}, u32[]{:S(2)}, u32[]{:S(2)}) collective-permute-start(bf16[1,208,512]{2,1,0:T(8,128)(2,1)S(1)} %get-tuple-element.235), channel_id=1, source_target_pairs={{0,4},{1,3},{2,0},{3,7},{4,8},{5,1},{6,2},{7,11},{8,12},{9,5},{10,... | collective-permute-start | bytes 638984 | tf_op jit(solution)/shard_map/ppermute | solution.py:909
  76.3 8.3 %collective-permute-start.26 = (bf16[1,192,512]{2,1,0:T(8,128)(2,1)S(1)}, bf16[1,192,512]{2,1,0:T(8,128)(2,1)S(1)}, u32[]{:S(2)}, u32[]{:S(2)}) collective-permute-start(bf16[1,192,512]{2,1,0:T(8,128)(2,1)S(1)} %get-tuple-element.245), channel_id=1, source_target_pairs={{0,2},{1,5},{2,6},{3,1},{4,0},{5,9},{6,10},{7,3},{8,4},{9,13},{10,... | collective-permute-start | bytes 589832 | tf_op jit(solution)/shard_map/ppermute | solution.py:909
  77.0 8.0 %collective-permute-start.25 = (bf16[1,192,512]{2,1,0:T(8,128)(2,1)S(1)}, bf16[1,192,512]{2,1,0:T(8,128)(2,1)S(1)}, u32[]{:S(2)}, u32[]{:S(2)}) collective-permute-start(bf16[1,192,512]{2,1,0:T(8,128)(2,1)S(1)} %get-tuple-element.240), channel_id=1, source_target_pairs={{0,4},{1,3},{2,0},{3,7},{4,8},{5,1},{6,2},{7,11},{8,12},{9,5},{10,... | collective-permute-start | bytes 589832 | tf_op jit(solution)/shard_map/ppermute | solution.py:909
  80.9 8.3 %collective-permute-start.24 = (bf16[1,208,512]{2,1,0:T(8,128)(2,1)S(1)}, bf16[1,208,512]{2,1,0:T(8,128)(2,1)S(1)}, u32[]{:S(2)}, u32[]{:S(2)}) collective-permute-start(bf16[1,208,512]{2,1,0:T(8,128)(2,1)S(1)} %get-tuple-element.244), channel_id=1, source_target_pairs={{0,2},{1,5},{2,6},{3,1},{4,0},{5,9},{6,10},{7,3},{8,4},{9,13},{10,... | collective-permute-start | bytes 638984 | tf_op jit(solution)/shard_map/ppermute | solution.py:909
  83.0 7.9 %collective-permute-start.23 = (bf16[1,208,512]{2,1,0:T(8,128)(2,1)S(1)}, bf16[1,208,512]{2,1,0:T(8,128)(2,1)S(1)}, u32[]{:S(2)}, u32[]{:S(2)}) collective-permute-start(bf16[1,208,512]{2,1,0:T(8,128)(2,1)S(1)} %get-tuple-element.243), channel_id=1, source_target_pairs={{0,4},{1,3},{2,0},{3,7},{4,8},{5,1},{6,2},{7,11},{8,12},{9,5},{10,... | collective-permute-start | bytes 638984 | tf_op jit(solution)/shard_map/ppermute | solution.py:909
  85.1 8.4 %collective-permute-start.29 = (bf16[1,192,512]{2,1,0:T(8,128)(2,1)S(1)}, bf16[1,192,512]{2,1,0:T(8,128)(2,1)S(1)}, u32[]{:S(2)}, u32[]{:S(2)}) collective-permute-start(bf16[1,192,512]{2,1,0:T(8,128)(2,1)S(1)} %get-tuple-element.252), channel_id=1, source_target_pairs={{0,2},{1,5},{2,6},{3,1},{4,0},{5,9},{6,10},{7,3},{8,4},{9,13},{10,... | collective-permute-start | bytes 589832 | tf_op jit(solution)/shard_map/ppermute | solution.py:909
  87.2 6.2 %collective-permute-start.28 = (bf16[1,192,512]{2,1,0:T(8,128)(2,1)S(1)}, bf16[1,192,512]{2,1,0:T(8,128)(2,1)S(1)}, u32[]{:S(2)}, u32[]{:S(2)}) collective-permute-start(bf16[1,192,512]{2,1,0:T(8,128)(2,1)S(1)} %get-tuple-element.248), channel_id=1, source_target_pairs={{0,4},{1,3},{2,0},{3,7},{4,8},{5,1},{6,2},{7,11},{8,12},{9,5},{10,... | collective-permute-start | bytes 589832 | tf_op jit(solution)/shard_map/ppermute | solution.py:909
  91.0 5.9 %collective-permute-start.27 = (bf16[1,208,512]{2,1,0:T(8,128)(2,1)S(1)}, bf16[1,208,512]{2,1,0:T(8,128)(2,1)S(1)}, u32[]{:S(2)}, u32[]{:S(2)}) collective-permute-start(bf16[1,208,512]{2,1,0:T(8,128)(2,1)S(1)} %get-tuple-element.251), channel_id=1, source_target_pairs={{0,4},{1,3},{2,0},{3,7},{4,8},{5,1},{6,2},{7,11},{8,12},{9,5},{10,... | collective-permute-start | bytes 638984 | tf_op jit(solution)/shard_map/ppermute | solution.py:909
  93.5 6.6 %collective-permute-start.32 = (bf16[1,192,512]{2,1,0:T(8,128)(2,1)S(1)}, bf16[1,192,512]{2,1,0:T(8,128)(2,1)S(1)}, u32[]{:S(2)}, u32[]{:S(2)}) collective-permute-start(bf16[1,192,512]{2,1,0:T(8,128)(2,1)S(1)} %get-tuple-element.255), channel_id=1, source_target_pairs={{0,4},{1,3},{2,0},{3,7},{4,8},{5,1},{6,2},{7,11},{8,12},{9,5},{10,... | collective-permute-start | bytes 589832 | tf_op jit(solution)/shard_map/ppermute | solution.py:909
  96.9 8.1 %collective-permute-start.31 = (bf16[1,208,512]{2,1,0:T(8,128)(2,1)S(1)}, bf16[1,208,512]{2,1,0:T(8,128)(2,1)S(1)}, u32[]{:S(2)}, u32[]{:S(2)}) collective-permute-start(bf16[1,208,512]{2,1,0:T(8,128)(2,1)S(1)} %shard_map.320.refs_0_), channel_id=1, source_target_pairs={{0,2},{1,5},{2,6},{3,1},{4,0},{5,9},{6,10},{7,3},{8,4},{9,13},{10,... | collective-permute-start | bytes 638984 | tf_op jit(solution)/shard_map/ppermute | solution.py:909
  97.7 8.2 %collective-permute-start.30 = (bf16[1,208,512]{2,1,0:T(8,128)(2,1)S(1)}, bf16[1,208,512]{2,1,0:T(8,128)(2,1)S(1)}, u32[]{:S(2)}, u32[]{:S(2)}) collective-permute-start(bf16[1,208,512]{2,1,0:T(8,128)(2,1)S(1)} %shard_map.320.refs_0_), channel_id=1, source_target_pairs={{0,4},{1,3},{2,0},{3,7},{4,8},{5,1},{6,2},{7,11},{8,12},{9,5},{10,... | collective-permute-start | bytes 638984 | tf_op jit(solution)/shard_map/ppermute | solution.py:909
  100.2 9.1 %collective-permute-start.36 = (bf16[1,192,512]{2,1,0:T(8,128)(2,1)S(1)}, bf16[1,192,512]{2,1,0:T(8,128)(2,1)S(1)}, u32[]{:S(2)}, u32[]{:S(2)}) collective-permute-start(bf16[1,192,512]{2,1,0:T(8,128)(2,1)S(1)} %shard_map.321.refs_7_), channel_id=1, source_target_pairs={{0,2},{1,5},{2,6},{3,1},{4,0},{5,9},{6,10},{7,3},{8,4},{9,13},{10,... | collective-permute-start | bytes 589832 | tf_op jit(solution)/shard_map/ppermute | solution.py:909
  102.8 7.8 %collective-permute-start.35 = (bf16[1,192,512]{2,1,0:T(8,128)(2,1)S(1)}, bf16[1,192,512]{2,1,0:T(8,128)(2,1)S(1)}, u32[]{:S(2)}, u32[]{:S(2)}) collective-permute-start(bf16[1,192,512]{2,1,0:T(8,128)(2,1)S(1)} %shard_map.321.refs_7_), channel_id=1, source_target_pairs={{0,4},{1,3},{2,0},{3,7},{4,8},{5,1},{6,2},{7,11},{8,12},{9,5},{10,... | collective-permute-start | bytes 589832 | tf_op jit(solution)/shard_map/ppermute | solution.py:909
  106.0 8.2 %collective-permute-start.34 = (bf16[1,208,512]{2,1,0:T(8,128)(2,1)S(1)}, bf16[1,208,512]{2,1,0:T(8,128)(2,1)S(1)}, u32[]{:S(2)}, u32[]{:S(2)}) collective-permute-start(bf16[1,208,512]{2,1,0:T(8,128)(2,1)S(1)} %get-tuple-element.290.refs_6_), channel_id=1, source_target_pairs={{0,2},{1,5},{2,6},{3,1},{4,0},{5,9},{6,10},{7,3},{8,4},{9,13},{10,... | collective-permute-start | bytes 638984 | tf_op jit(solution)/shard_map/ppermute | solution.py:909
  107.8 7.6 %collective-permute-start.33 = (bf16[1,208,512]{2,1,0:T(8,128)(2,1)S(1)}, bf16[1,208,512]{2,1,0:T(8,128)(2,1)S(1)}, u32[]{:S(2)}, u32[]{:S(2)}) collective-permute-start(bf16[1,208,512]{2,1,0:T(8,128)(2,1)S(1)} %get-tuple-element.285.refs_1_), channel_id=1, source_target_pairs={{0,4},{1,3},{2,0},{3,7},{4,8},{5,1},{6,2},{7,11},{8,12},{9,5},{10,... | collective-permute-start | bytes 638984 | tf_op jit(solution)/shard_map/ppermute | solution.py:909
  110.6 7.9 %collective-permute-start.40 = (bf16[1,192,512]{2,1,0:T(8,128)(2,1)S(1)}, bf16[1,192,512]{2,1,0:T(8,128)(2,1)S(1)}, u32[]{:S(2)}, u32[]{:S(2)}) collective-permute-start(bf16[1,192,512]{2,1,0:T(8,128)(2,1)S(1)} %get-tuple-element.297.refs_13_), channel_id=1, source_target_pairs={{0,2},{1,5},{2,6},{3,1},{4,0},{5,9},{6,10},{7,3},{8,4},{9,13},{10,... | collective-permute-start | bytes 589832 | tf_op jit(solution)/shard_map/ppermute | solution.py:909
  112.0 7.7 %collective-permute-start.39 = (bf16[1,192,512]{2,1,0:T(8,128)(2,1)S(1)}, bf16[1,192,512]{2,1,0:T(8,128)(2,1)S(1)}, u32[]{:S(2)}, u32[]{:S(2)}) collective-permute-start(bf16[1,192,512]{2,1,0:T(8,128)(2,1)S(1)} %get-tuple-element.292.refs_8_), channel_id=1, source_target_pairs={{0,4},{1,3},{2,0},{3,7},{4,8},{5,1},{6,2},{7,11},{8,12},{9,5},{10,... | collective-permute-start | bytes 589832 | tf_op jit(solution)/shard_map/ppermute | solution.py:909
  115.4 8.2 %collective-permute-start.38 = (bf16[1,208,512]{2,1,0:T(8,128)(2,1)S(1)}, bf16[1,208,512]{2,1,0:T(8,128)(2,1)S(1)}, u32[]{:S(2)}, u32[]{:S(2)}) collective-permute-start(bf16[1,208,512]{2,1,0:T(8,128)(2,1)S(1)} %get-tuple-element.289.refs_5_), channel_id=1, source_target_pairs={{0,2},{1,5},{2,6},{3,1},{4,0},{5,9},{6,10},{7,3},{8,4},{9,13},{10,... | collective-permute-start | bytes 638984 | tf_op jit(solution)/shard_map/ppermute | solution.py:909
  117.1 6.8 %collective-permute-start.37 = (bf16[1,208,512]{2,1,0:T(8,128)(2,1)S(1)}, bf16[1,208,512]{2,1,0:T(8,128)(2,1)S(1)}, u32[]{:S(2)}, u32[]{:S(2)}) collective-permute-start(bf16[1,208,512]{2,1,0:T(8,128)(2,1)S(1)} %get-tuple-element.286.refs_2_), channel_id=1, source_target_pairs={{0,4},{1,3},{2,0},{3,7},{4,8},{5,1},{6,2},{7,11},{8,12},{9,5},{10,... | collective-permute-start | bytes 638984 | tf_op jit(solution)/shard_map/ppermute | solution.py:909
  119.8 6.3 %collective-permute-start.43 = (bf16[1,192,512]{2,1,0:T(8,128)(2,1)S(1)}, bf16[1,192,512]{2,1,0:T(8,128)(2,1)S(1)}, u32[]{:S(2)}, u32[]{:S(2)}) collective-permute-start(bf16[1,192,512]{2,1,0:T(8,128)(2,1)S(1)} %get-tuple-element.296.refs_12_), channel_id=1, source_target_pairs={{0,2},{1,5},{2,6},{3,1},{4,0},{5,9},{6,10},{7,3},{8,4},{9,13},{10,... | collective-permute-start | bytes 589832 | tf_op jit(solution)/shard_map/ppermute | solution.py:909
  121.3 5.7 %collective-permute-start.42 = (bf16[1,192,512]{2,1,0:T(8,128)(2,1)S(1)}, bf16[1,192,512]{2,1,0:T(8,128)(2,1)S(1)}, u32[]{:S(2)}, u32[]{:S(2)}) collective-permute-start(bf16[1,192,512]{2,1,0:T(8,128)(2,1)S(1)} %get-tuple-element.293.refs_9_), channel_id=1, source_target_pairs={{0,4},{1,3},{2,0},{3,7},{4,8},{5,1},{6,2},{7,11},{8,12},{9,5},{10,... | collective-permute-start | bytes 589832 | tf_op jit(solution)/shard_map/ppermute | solution.py:909
  127.2 5.3 %collective-permute-start.44 = (bf16[7,400,512]{2,1,0:T(8,128)(2,1)S(1)}, bf16[7,400,512]{2,1,0:T(8,128)(2,1)S(1)}, u32[]{:S(2)}, u32[]{:S(2)}) collective-permute-start(bf16[7,400,512]{2,1,0:T(8,128)(2,1)S(1)} %shard_map.328.refs_0_.refs_1_), channel_id=1, source_target_pairs={{0,1},{1,0},{2,3},{3,2},{4,5},{5,4},{6,7},{7,6},{8,9},{9,8},{10,11... | collective-permute-start | bytes 8601608 | tf_op jit(solution)/shard_map/ppermute | solution.py:888
  127.3 8.1 %collective-permute-start.41 = (bf16[1,208,512]{2,1,0:T(8,128)(2,1)S(1)}, bf16[1,208,512]{2,1,0:T(8,128)(2,1)S(1)}, u32[]{:S(2)}, u32[]{:S(2)}) collective-permute-start(bf16[1,208,512]{2,1,0:T(8,128)(2,1)S(1)} %get-tuple-element.287.refs_3_), channel_id=1, source_target_pairs={{0,4},{1,3},{2,0},{3,7},{4,8},{5,1},{6,2},{7,11},{8,12},{9,5},{10,... | collective-permute-start | bytes 638984 | tf_op jit(solution)/shard_map/ppermute | solution.py:909
  128.0 7.4 %collective-permute-start.45 = (bf16[1,192,512]{2,1,0:T(8,128)(2,1)S(1)}, bf16[1,192,512]{2,1,0:T(8,128)(2,1)S(1)}, u32[]{:S(2)}, u32[]{:S(2)}) collective-permute-start(bf16[1,192,512]{2,1,0:T(8,128)(2,1)S(1)} %get-tuple-element.294.refs_10_), channel_id=1, source_target_pairs={{0,4},{1,3},{2,0},{3,7},{4,8},{5,1},{6,2},{7,11},{8,12},{9,5},{10,... | collective-permute-start | bytes 589832 | tf_op jit(solution)/shard_map/ppermute | solution.py:909
  135.5 1.8 %collective-permute-start.46 = (bf16[1,400,512]{2,1,0:T(8,128)(2,1)S(1)}, bf16[1,400,512]{2,1,0:T(8,128)(2,1)S(1)}, u32[]{:S(2)}, u32[]{:S(2)}) collective-permute-start(bf16[1,400,512]{2,1,0:T(8,128)(2,1)S(1)} %shard_map.333.refs_0_.refs_2_), channel_id=1, source_target_pairs={{0,1},{1,0},{2,3},{3,2},{4,5},{5,4},{6,7},{7,6},{8,9},{9,8},{10,11... | collective-permute-start | bytes 1228808 | tf_op jit(solution)/shard_map/ppermute | solution.py:888
  (16 other events, 161.6 us)

commit v11 on v10

--- a/solution.py
+++ b/solution.py
@@ -369,8 +369,8 @@
 def matching_stats(
     size, masks, lanes, scale_ref, lens_ref, near_ref, far_ref, *refs
 ):
-    doc_refs = refs[:-6]
-    totals_ref, el_ref, hot_ref, stats_ref, turn_ref, unit_ref = refs[-6:]
+    doc_refs = refs[:-7]
+    totals_ref, el_ref, hot_ref, factor_ref, stats_ref, turn_ref, unit_ref = refs[-7:]
     base, near_at = here(size)[2:4]
     span = ROW + EXT
     queries = load_queries(near_ref, far_ref)
@@ -406,7 +406,9 @@
     log_length = jnp.log(length.astype(F32))
     matched = (jnp.log(totals) - log_length[:1]) * (1.0 / SHARPNESS)
     per_query = jnp.sum(matched.reshape(count // QLEN, QLEN, lanes), axis=1)
-    scale = jnp.exp(jnp.full(shape, scale_ref[0], F32))[:1]
+    scale = jnp.exp(jnp.full(shape, scale_ref[0], F32))
+    factor_ref[...] = scale
+    scale = scale[:1]
     logits = per_query * (scale * (1.0 / QLEN))
     groups = count // ROW
     tags = []
@@ -436,7 +438,7 @@
 
 
 def matching_back(
-    size, masks, lanes, scale_ref, lens_ref, totals_ref, el_ref, hot_ref, own_ref, over_y, over_x, over_both, unitq_ref, qt_ref, invq_ref, unit_ref, invd_ref, *refs
+    size, masks, lanes, totals_ref, el_ref, hot_ref, factor_ref, own_ref, over_y, over_x, over_both, unitq_ref, qt_ref, invq_ref, unit_ref, invd_ref, marks_ref, *refs
 ):
     dq_ref, far_ref, keep_ref, send_ref, loss_ref, dot_ref, dt_ref, stats_ref = refs[-8:]
     _, stream, base, near_at = here(size)[:4]
@@ -448,7 +450,6 @@
     unit_q = [unitq_ref[m] for m in range(len(RANGES))]
     doc_rows = unit_ref.shape[2] // ROW
     docs = doc_rows * DOCS_ROW
-    ids = row_ids(base, masks, doc_rows)
     groups = count // ROW
     odd_y, odd_x = (near_at & 1) == 1, stream == 1
     parts = [own_ref[...], over_y[...], over_x[...], over_both[...]]
@@ -484,8 +485,7 @@
         jnp.where(line == 1, jnp.sum(moved, axis=0, keepdims=True) * (1.0 / total_queries), 0.0),
     )
     loss_ref[...] = loss
-    marks = doc_marks(lens_ref, ids, lanes, True)
-    scale = jnp.exp(jnp.full((8, lanes), scale_ref[0], F32))[:1]
+    scale = factor_ref[:1, :]
     coeff = (el_ref[...] / sums - hot_ref[...]) * (scale * (1.0 / (QLEN * total_queries)))
     coeff = jnp.broadcast_to(coeff[:, None, :], (groups * 8, QLEN, lanes)).reshape(count, lanes)
     ratio = coeff / totals_ref[...]
@@ -496,7 +496,7 @@
         grad = jnp.zeros((count, PROJ), F32)
         for p in range(doc_rows):
             block = unit_ref[m, :, p * ROW : (p + 1) * ROW]
-            mark = marks[p][m]
+            mark = marks_ref[p * len(RANGES) + m]
             if len(refs) > 8:
                 exps = refs[0][m, :, p * ROW : (p + 1) * ROW].astype(F32)
             else:
@@ -524,10 +524,14 @@
         ref[at * ROW : (at + 1) * ROW, :] = total[:, p * ROW : (p + 1) * ROW].T.astype(BF16)
 
 
-def matching_ready(near_ref, far_ref, *refs):
-    doc_refs = refs[:-6] if refs[-2].shape[0] != len(RANGES) else refs[:-7]
-    unitq_ref, qt_ref, invq_ref, unit_ref, invd_ref = refs[len(doc_refs) : len(doc_refs) + 5]
+def matching_ready(size, masks, lanes, lens_ref, near_ref, far_ref, *refs):
+    doc_refs = refs[:-7] if refs[-2].shape[0] != len(RANGES) else refs[:-8]
+    unitq_ref, qt_ref, invq_ref, unit_ref, invd_ref, marks_ref = refs[len(doc_refs) : len(doc_refs) + 6]
     turn_ref = refs[-1]
+    ids = row_ids(here(size)[2], masks, unit_ref.shape[2] // ROW)
+    for p, marks in enumerate(doc_marks(lens_ref, ids, lanes, True)):
+        for m, mark in enumerate(marks):
+            marks_ref[p * len(RANGES) + m] = mark
     queries = load_queries(near_ref, far_ref)
     unit_q, inv_q = unit_queries(queries, SHARPNESS * LOG2E)
     unit_d, inv_d = unit_docs(doc_refs, turn_ref)
@@ -540,7 +544,7 @@
         qt_ref[m] = unit_q[m].T.astype(BF16)
         columns = jnp.where(lane == m, inv_q[m], columns)
         invd_ref[m : m + 1, :] = inv_d[m]
-        if len(refs) - len(doc_refs) > 6:
+        if len(refs) - len(doc_refs) > 7:
             refs[-2][m] = jnp.exp2(mm(unitq_ref[m], unit_ref[m])).astype(BF16)
     invq_ref[...] = columns
 
@@ -1097,7 +1101,7 @@
     tokens_q = 4 * ROW
     lanes = -(-3 * doc_rows * DOCS_ROW // 128) * 128
     room = 20 if doc_rows <= 4 else 56
-    totals, el, hot, stats = call(
+    totals, el, hot, factor, stats = call(
         partial(matching_stats, size, doc_masks, lanes),
         (scale, lens, near, far, *pieces),
         [SMEM] * 2 + [VMEM] * (2 + len(pieces)),
@@ -1105,6 +1109,7 @@
             shape_of((tokens_q, lanes)),
             shape_of((tokens_q // QLEN, lanes)),
             shape_of((tokens_q // QLEN, lanes)),
+            shape_of((8, lanes)),
             shape_of((tokens_q // QLEN, 128)),
         ],
         [pltpu.VMEM((PROJ, tokens_d), F32), pltpu.VMEM((3, PROJ, tokens_d), BF16)],
@@ -1112,15 +1117,16 @@
     )
     small_enough = doc_rows <= 4
     ready = call(
-        matching_ready,
-        (near, far, *pieces),
-        [VMEM] * (2 + len(pieces)),
+        partial(matching_ready, size, doc_masks, lanes),
+        (lens, near, far, *pieces),
+        [SMEM] + [VMEM] * (2 + len(pieces)),
         [
             shape_of((3, tokens_q, PROJ), BF16),
             shape_of((3, PROJ, tokens_q), BF16),
             shape_of((tokens_q, 128)),
             shape_of((3, PROJ, tokens_d), BF16),
             shape_of((8, tokens_d)),
+            shape_of((3 * doc_rows, lanes, ROW), BF16),
         ]
         + [shape_of((3, tokens_q, tokens_d), BF16)] * small_enough,
         [pltpu.VMEM((PROJ, tokens_d), F32)],
@@ -1133,8 +1139,8 @@
     over_both = lax.ppermute(stats, ("stream", "dp"), pairs)
     dq, dq_send, keep, send, loss = call(
         partial(matching_back, size, doc_masks, lanes),
-        (scale, lens, totals, el, hot, stats, over_y, over_x, over_both, *ready),
-        [SMEM] * 2 + [VMEM] * (7 + len(ready)),
+        (totals, el, hot, factor, stats, over_y, over_x, over_both, *ready),
+        [VMEM] * (8 + len(ready)),
         [shape_of((tokens_q // 2, PROJ), BF16)] * 2
         + [shape_of((tokens_d // 2, PROJ), BF16)] * 2
         + [shape_of((8, 128))],

time: 139 us -> 139 us (level)
  transfers between devices with their start and end apart: 47 -> 47, of which waited for: 35 -> 37; matrix products, arithmetic and copies ran while one was open for 0% -> 0% of each run, Pallas kernels for 12% -> 12%
where the time goes in v11:
time: 139 us
  starting transfers between devices  50 us (36%)
  waiting for transfers between devices  48.8 us (35%)
  Pallas kernels  36.4 us (26%)
  between operations  2.02 us (1%)
    pallas_call x39, Pallas kernels, call(): pl.pallas_call(kernel, out_shape=outs, in_specs=specs, out_specs=out_spec...  36.4 us
    ppermute x28, starting transfers between devices, ring_swap(): return lax.ppermute(value, 'dp', pairs)  30.5 us
    ppermute x28, waiting for transfers between devices, ring_swap(): return lax.ppermute(value, 'dp', pairs)  29.8 us
    ppermute x18, waiting for transfers between devices, swapped(): return lax.ppermute(value, axis, [(k, k ^ mask) for k in range(size)])  19 us
    ppermute x18, starting transfers between devices, swapped(): return lax.ppermute(value, axis, [(k, k ^ mask) for k in range(size)])  17.1 us
  transfers between devices with their start and end apart: 47, of which 37 were waited for; matrix products, arithmetic and copies ran while one was open for 0% of the time, Pallas kernels for 12%

profile of v11, /device:TPU:0, one launch (start us, length us, event | category | flops | bytes accessed | tf_op | source)
XLA Modules:
  0.0 138.5 jit_solution(4917409283328371537)
XLA Ops:
  0.7 6.8 %shard_map.297 = (bf16[272,128]{1,0:T(8,128)(2,1)S(1)}, bf16[256,2048]{1,0:T(8,128)(2,1)S(1)}, bf16[256,2048]{1,0:T(8,128)(2,1)S(1)}, f32[256,512]{1,0:T(8,128)S...) custom-call(s32[5,16]{1,0:T(8,128)} %bitcast.27, ...), custom_call_target="tpu_custom_call" | custom-call | flops 100000000 | bytes 10000000 | tf_op jit(solution)/shard_map/pallas_call | solution.py:876
  7.5 3.0 %collective-permute-start = (bf16[272,128]{1,0:T(8,128)(2,1)S(1)}, bf16[272,128]{1,0:T(8,128)(2,1)S(1)}, u32[]{:S(2)}, u32[]{:S(2)}) collective-permute-start(bf16[272,128]{1,0:T(8,128)(2,1)S(1)} %get-tuple-element.178), channel_id=1, source_target_pairs={{0,16},{16,0},{1,17},{17,1},{2,18},{18,2},{3,19},{19,3},{4,20},{20... | collective-permute-start | bytes 208904 | tf_op jit(solution)/shard_map/ppermute | solution.py:892
  10.5 1.5 %shard_map.298 = (bf16[256,2048]{1,0:T(8,128)(2,1)}, bf16[256,2048]{1,0:T(8,128)(2,1)}, f32[256,512]{1,0:T(8,128)}, f32[256,128]{1,0:T(8,128)}) custom-call(bf16[256,2048]{1,0:T(8,128)(2,1)S(1)} %get-tuple-element.179.refs_0_, bf16[256,2048]{1,0:T(8,128)(2,1)S(1)} %get-tuple-element.180.refs_1_, f32[256,512]{1,0:T(8,128)S(1)} %get-tuple-element.181.refs_2_, ...), custom_call_target="tpu_custom_call" | custom-call | flops 300000000 | bytes 30000000 | tf_op jit(solution)/shard_map/pallas_call | solution.py:876
  12.8 3.2 %collective-permute-start.2 = (bf16[256,128]{1,0:T(8,128)(2,1)S(1)}, bf16[256,128]{1,0:T(8,128)(2,1)S(1)}, u32[]{:S(2)}, u32[]{:S(2)}) collective-permute-start(bf16[256,128]{1,0:T(8,128)(2,1)S(1)} %slice_select_fusion.here_ref), channel_id=1, source_target_pairs={{0,8},{1,9},{2,10},{3,11},{4,12},{5,13},{6,14},{7,15},{8,0},{9,1},... | collective-permute-start | bytes 196616 | tf_op jit(solution)/shard_map/ppermute | solution.py:892
  16.0 1.6 %collective-permute-start.1 = (bf16[272,128]{1,0:T(8,128)(2,1)S(1)}, bf16[272,128]{1,0:T(8,128)(2,1)S(1)}, u32[]{:S(2)}, u32[]{:S(2)}) collective-permute-start(bf16[272,128]{1,0:T(8,128)(2,1)S(1)} %broadcast_select_fusion), channel_id=1, source_target_pairs={{0,2},{1,3},{2,0},{3,1},{4,6},{5,7},{6,4},{7,5},{8,10},{9,11},{10,... | collective-permute-start | bytes 208904 | tf_op jit(solution)/shard_map/ppermute | solution.py:892
  18.3 2.1 %collective-permute-done.1 = bf16[272,128]{1,0:T(8,128)(2,1)S(1)} collective-permute-done((bf16[272,128]{1,0:T(8,128)(2,1)S(1)}, bf16[272,128]{1,0:T(8,128)(2,1)S(1)}, u32[]{:S(2)}, u32[]{:S(2)}) %collective-permute-start.1) | collective-permute-done | bytes 69664 | tf_op jit(solution)/shard_map/ppermute | solution.py:892
  20.5 1.6 %collective-permute-start.4 = (bf16[256,128]{1,0:T(8,128)(2,1)S(1)}, bf16[256,128]{1,0:T(8,128)(2,1)S(1)}, u32[]{:S(2)}, u32[]{:S(2)}) collective-permute-start(bf16[256,128]{1,0:T(8,128)(2,1)S(1)} %shard_map.299.refs_0_), channel_id=1, source_target_pairs={{0,4},{1,5},{2,6},{3,7},{4,0},{5,1},{6,2},{7,3},{8,12},{9,13},{10,... | collective-permute-start | bytes 196616 | tf_op jit(solution)/shard_map/ppermute | solution.py:892
  22.8 2.2 %collective-permute-done.4.refs_1_ = bf16[256,128]{1,0:T(8,128)(2,1)S(1)} collective-permute-done((bf16[256,128]{1,0:T(8,128)(2,1)S(1)}, bf16[256,128]{1,0:T(8,128)(2,1)S(1)}, u32[]{:S(2)}, u32[]{:S(2)}) %collective-permute-start.4) | collective-permute-done | bytes 65568 | tf_op jit(solution)/shard_map/ppermute | solution.py:892
  25.0 2.8 %shard_map.300 = (f32[1024,128]{1,0:T(8,128)S(1)}, f32[32,128]{1,0:T(8,128)S(1)}, f32[32,128]{1,0:T(8,128)S(1)}, f32[8,128]{1,0:T(8,128)S(1)}, f32[32,128]{1,0:T(8,128)S(1)}) custom-call(f32[1]{0:T(128)} %bitcast.16.scale_ref, s32[5,16]{1,0:T(8,128)S(1)} %bitcast.28, bf16[544,128]{1,0:T(8,128)(2,1)S(1)} %pad_maximum_fusion.near_ref, ...), custom_call_target="tpu_custom_call" | custom-call | flops 100000000 | bytes 10000000 | tf_op jit(solution)/shard_map/pallas_call | solution.py:876
  29.0 2.4 %collective-permute-start.8 = (f32[32,128]{1,0:T(8,128)S(1)}, f32[32,128]{1,0:T(8,128)S(1)}, u32[]{:S(2)}, u32[]{:S(2)}) collective-permute-start(f32[32,128]{1,0:T(8,128)S(1)} %add.3.own_ref), channel_id=1, source_target_pairs={{0,18},{1,19},{2,16},{3,17},{4,22},{5,23},{6,20},{7,21},{8,26},{9,... | collective-permute-start | bytes 49160 | tf_op jit(solution)/shard_map/ppermute | solution.py:1139
  32.5 2.2 %shard_map.301 = (bf16[3,1024,128]{2,1,0:T(8,128)(2,1)S(1)}, bf16[3,128,1024]{2,1,0:T(8,128)(2,1)S(1)}, f32[1024,128]{1,0:T(8,128)S(1)}, bf16[3,128,512]{2,1,0:T...) custom-call(s32[5,16]{1,0:T(8,128)S(1)} %bitcast.29, ...), custom_call_target="tpu_custom_call" | custom-call | flops 100000000 | bytes 10000000 | tf_op jit(solution)/shard_map/pallas_call | solution.py:876
  35.8 3.0 %shard_map.302 = (bf16[512,128]{1,0:T(8,128)(2,1)S(1)}, bf16[512,128]{1,0:T(8,128)(2,1)S(1)}, bf16[256,128]{1,0:T(8,128)(2,1)S(1)}, bf16[256,128]{1,0:T(8,128)(2,1)S(1)}, f32[8,128]{1,0:T(8,128)S(1)}) custom-call(f32[1024,128]{1,0:T(8,128)S(1)} %get-tuple-element.186.totals_ref, f32[32,128]{1,0:T(8,128)S(1)} %get-tuple-element.187.el_ref, ...), custom_call_target="tpu_custom_call" | custom-call | flops 100000000 | bytes 10000000 | tf_op jit(solution)/shard_map/pallas_call | solution.py:876
  38.9 1.6 %collective-permute-start.11 = (bf16[256,128]{1,0:T(8,128)(2,1)S(1)}, bf16[256,128]{1,0:T(8,128)(2,1)S(1)}, u32[]{:S(2)}, u32[]{:S(2)}) collective-permute-start(bf16[256,128]{1,0:T(8,128)(2,1)S(1)} %get-tuple-element.201), channel_id=1, source_target_pairs={{0,4},{1,5},{2,6},{3,7},{4,0},{5,1},{6,2},{7,3},{8,12},{9,13},{10,... | collective-permute-start | bytes 196616 | tf_op jit(solution)/shard_map/ppermute | solution.py:892
  40.6 2.8 %collective-permute-done.11.got_ref = bf16[256,128]{1,0:T(8,128)(2,1)S(1)} collective-permute-done((bf16[256,128]{1,0:T(8,128)(2,1)S(1)}, bf16[256,128]{1,0:T(8,128)(2,1)S(1)}, u32[]{:S(2)}, u32[]{:S(2)}) %collective-permute-start.11) | collective-permute-done | bytes 65568 | tf_op jit(solution)/shard_map/ppermute | solution.py:892
  43.4 1.3 collective-permute-start.12
  45.6 3.5 %collective-permute-done.12.got_ref = bf16[256,128]{1,0:T(8,128)(2,1)S(1)} collective-permute-done((bf16[256,128]{1,0:T(8,128)(2,1)S(1)}, bf16[256,128]{1,0:T(8,128)(2,1)S(1)}, u32[]{:S(2)}, u32[]{:S(2)}) %collective-permute-start.12) | collective-permute-done | bytes 65568 | tf_op jit(solution)/shard_map/ppermute | solution.py:892
  49.3 1.5 %collective-permute-start.13 = (bf16[256,128]{1,0:T(8,128)(2,1)S(1)}, bf16[256,128]{1,0:T(8,128)(2,1)S(1)}, u32[]{:S(2)}, u32[]{:S(2)}) collective-permute-start(bf16[256,128]{1,0:T(8,128)(2,1)S(1)} %broadcast_select_fusion.1), channel_id=1, source_target_pairs={{0,16},{16,0},{1,17},{17,1},{2,18},{18,2},{3,19},{19,3},{4,20},{20... | collective-permute-start | bytes 196616 | tf_op jit(solution)/shard_map/ppermute | solution.py:892
  50.8 2.8 %collective-permute-done.13.got_ref = bf16[256,128]{1,0:T(8,128)(2,1)S(1)} collective-permute-done((bf16[256,128]{1,0:T(8,128)(2,1)S(1)}, bf16[256,128]{1,0:T(8,128)(2,1)S(1)}, u32[]{:S(2)}, u32[]{:S(2)}) %collective-permute-start.13) | collective-permute-done | bytes 65568 | tf_op jit(solution)/shard_map/ppermute | solution.py:892
  53.8 4.8 %shard_map.307 = (bf16[8,208,512]{2,1,0:T(8,128)(2,1)S(1)}, bf16[8,208,512]{2,1,0:T(8,128)(2,1)S(1)}, bf16[8,48,512]{2,1,0:T(8,128)(2,1)S(1)}, bf16[8,48,512]{2,...) custom-call(bf16[256,128]{1,0:T(8,128)(2,1)S(1)} %shard_map.306.dq_ref, ...), custom_call_target="tpu_custom_call" | custom-call | flops 100000000 | bytes 10000000 | tf_op jit(solution)/shard_map/pallas_call | solution.py:876
  58.7 3.7 %shard_map.308 = (bf16[8,192,512]{2,1,0:T(8,128)(2,1)S(1)}, bf16[2,192,512]{2,1,0:T(8,128)(2,1)S(1)}, bf16[6,192,512]{2,1,0:T(8,128)(2,1)S(1)}, f32[256,512]{1,0:T(8,128)S(1)}, bf16[256,1536]{1,0:T(8,128)(2,1)S(1)}) custom-call(f32[256,512]{1,0:T(8,128)S(1)} %get-tuple-element.211.dfirst_ref, f32[512,128]{1,0:T(8,128)S(1)} %get-tuple-element.212.gproj_ref, ...), custom_call_target="tpu_custom_call" | custom-call | flops 100000000 | bytes 10000000 | tf_op jit(solution)/shard_map/pallas_call | solution.py:876
  63.2 1.8 %collective-permute-start.15 = (bf16[1,208,512]{2,1,0:T(8,128)(2,1)S(1)}, bf16[1,208,512]{2,1,0:T(8,128)(2,1)S(1)}, u32[]{:S(2)}, u32[]{:S(2)}) collective-permute-start(bf16[1,208,512]{2,1,0:T(8,128)(2,1)S(1)} %get-tuple-element.225), channel_id=1, source_target_pairs={{0,4},{1,3},{2,0},{3,7},{4,8},{5,1},{6,2},{7,11},{8,12},{9,5},{10,... | collective-permute-start | bytes 638984 | tf_op jit(solution)/shard_map/ppermute | solution.py:913
  66.7 1.5 %collective-permute-start.21 = (bf16[1,192,512]{2,1,0:T(8,128)(2,1)S(1)}, bf16[1,192,512]{2,1,0:T(8,128)(2,1)S(1)}, u32[]{:S(2)}, u32[]{:S(2)}) collective-permute-start(bf16[1,192,512]{2,1,0:T(8,128)(2,1)S(1)} %get-tuple-element.241), channel_id=1, source_target_pairs={{0,4},{1,3},{2,0},{3,7},{4,8},{5,1},{6,2},{7,11},{8,12},{9,5},{10,... | collective-permute-start | bytes 589832 | tf_op jit(solution)/shard_map/ppermute | solution.py:913
  69.9 1.4 %shard_map.313 = f32[256,512]{1,0:T(8,128)} custom-call(f32[256,512]{1,0:T(8,128)S(1)} %get-tuple-element.235.dsum_ref, bf16[256,1536]{1,0:T(8,128)(2,1)S(1)} %get-tuple-element.236.djoined_ref, bf16[512,1536]{1,0:T(8,128)(2,1)S(1)} %bitcast.20), custom_call_target="tpu_custom_call" | custom-call | flops 300000000 | bytes 30000000 | tf_op jit(solution)/shard_map/pallas_call | solution.py:876
  72.0 1.8 %collective-permute-start.19 = (bf16[1,208,512]{2,1,0:T(8,128)(2,1)S(1)}, bf16[1,208,512]{2,1,0:T(8,128)(2,1)S(1)}, u32[]{:S(2)}, u32[]{:S(2)}) collective-permute-start(bf16[1,208,512]{2,1,0:T(8,128)(2,1)S(1)} %get-tuple-element.239), channel_id=1, source_target_pairs={{0,4},{1,3},{2,0},{3,7},{4,8},{5,1},{6,2},{7,11},{8,12},{9,5},{10,... | collective-permute-start | bytes 638984 | tf_op jit(solution)/shard_map/ppermute | solution.py:913
  73.8 1.7 %collective-permute-done.21.refs_0_ = bf16[1,192,512]{2,1,0:T(8,128)(2,1)S(1)} collective-permute-done((bf16[1,192,512]{2,1,0:T(8,128)(2,1)S(1)}, bf16[1,192,512]{2,1,0:T(8,128)(2,1)S(1)}, u32[]{:S(2)}, u32[]{:S(2)}) %collective-permute-start.21) | collective-permute-done | bytes 196640 | tf_op jit(solution)/shard_map/ppermute | solution.py:913
  77.7 2.1 %collective-permute-done.20.refs_1_ = bf16[1,208,512]{2,1,0:T(8,128)(2,1)S(1)} collective-permute-done((bf16[1,208,512]{2,1,0:T(8,128)(2,1)S(1)}, bf16[1,208,512]{2,1,0:T(8,128)(2,1)S(1)}, u32[]{:S(2)}, u32[]{:S(2)}) %collective-permute-start.20) | collective-permute-done | bytes 213024 | tf_op jit(solution)/shard_map/ppermute | solution.py:913
  80.3 2.1 %collective-permute-start.24 = (bf16[1,208,512]{2,1,0:T(8,128)(2,1)S(1)}, bf16[1,208,512]{2,1,0:T(8,128)(2,1)S(1)}, u32[]{:S(2)}, u32[]{:S(2)}) collective-permute-start(bf16[1,208,512]{2,1,0:T(8,128)(2,1)S(1)} %get-tuple-element.248), channel_id=1, source_target_pairs={{0,2},{1,5},{2,6},{3,1},{4,0},{5,9},{6,10},{7,3},{8,4},{9,13},{10,... | collective-permute-start | bytes 638984 | tf_op jit(solution)/shard_map/ppermute | solution.py:913
  82.4 1.6 %collective-permute-done.26.refs_1_ = bf16[1,192,512]{2,1,0:T(8,128)(2,1)S(1)} collective-permute-done((bf16[1,192,512]{2,1,0:T(8,128)(2,1)S(1)}, bf16[1,192,512]{2,1,0:T(8,128)(2,1)S(1)}, u32[]{:S(2)}, u32[]{:S(2)}) %collective-permute-start.26) | collective-permute-done | bytes 196640 | tf_op jit(solution)/shard_map/ppermute | solution.py:913
  84.5 2.1 %collective-permute-start.29 = (bf16[1,192,512]{2,1,0:T(8,128)(2,1)S(1)}, bf16[1,192,512]{2,1,0:T(8,128)(2,1)S(1)}, u32[]{:S(2)}, u32[]{:S(2)}) collective-permute-start(bf16[1,192,512]{2,1,0:T(8,128)(2,1)S(1)} %get-tuple-element.256), channel_id=1, source_target_pairs={{0,2},{1,5},{2,6},{3,1},{4,0},{5,9},{6,10},{7,3},{8,4},{9,13},{10,... | collective-permute-start | bytes 589832 | tf_op jit(solution)/shard_map/ppermute | solution.py:913
  86.6 2.0 %collective-permute-done.24.refs_1_ = bf16[1,208,512]{2,1,0:T(8,128)(2,1)S(1)} collective-permute-done((bf16[1,208,512]{2,1,0:T(8,128)(2,1)S(1)}, bf16[1,208,512]{2,1,0:T(8,128)(2,1)S(1)}, u32[]{:S(2)}, u32[]{:S(2)}) %collective-permute-start.24) | collective-permute-done | bytes 213024 | tf_op jit(solution)/shard_map/ppermute | solution.py:913
  88.6 1.7 %collective-permute-done.23.refs_0_ = bf16[1,208,512]{2,1,0:T(8,128)(2,1)S(1)} collective-permute-done((bf16[1,208,512]{2,1,0:T(8,128)(2,1)S(1)}, bf16[1,208,512]{2,1,0:T(8,128)(2,1)S(1)}, u32[]{:S(2)}, u32[]{:S(2)}) %collective-permute-start.23) | collective-permute-done | bytes 213024 | tf_op jit(solution)/shard_map/ppermute | solution.py:913
  90.9 1.9 %collective-permute-done.29.refs_1_ = bf16[1,192,512]{2,1,0:T(8,128)(2,1)S(1)} collective-permute-done((bf16[1,192,512]{2,1,0:T(8,128)(2,1)S(1)}, bf16[1,192,512]{2,1,0:T(8,128)(2,1)S(1)}, u32[]{:S(2)}, u32[]{:S(2)}) %collective-permute-start.29) | collective-permute-done | bytes 196640 | tf_op jit(solution)/shard_map/ppermute | solution.py:913
  93.0 2.1 %collective-permute-start.32 = (bf16[1,192,512]{2,1,0:T(8,128)(2,1)S(1)}, bf16[1,192,512]{2,1,0:T(8,128)(2,1)S(1)}, u32[]{:S(2)}, u32[]{:S(2)}) collective-permute-start(bf16[1,192,512]{2,1,0:T(8,128)(2,1)S(1)} %get-tuple-element.259), channel_id=1, source_target_pairs={{0,4},{1,3},{2,0},{3,7},{4,8},{5,1},{6,2},{7,11},{8,12},{9,5},{10,... | collective-permute-start | bytes 589832 | tf_op jit(solution)/shard_map/ppermute | solution.py:913
  95.0 1.3 collective-permute-done.27.refs_0_
  97.1 1.3 collective-permute-start.30
  99.6 2.7 %collective-permute-start.36 = (bf16[1,192,512]{2,1,0:T(8,128)(2,1)S(1)}, bf16[1,192,512]{2,1,0:T(8,128)(2,1)S(1)}, u32[]{:S(2)}, u32[]{:S(2)}) collective-permute-start(bf16[1,192,512]{2,1,0:T(8,128)(2,1)S(1)} %shard_map.321.refs_7_), channel_id=1, source_target_pairs={{0,2},{1,5},{2,6},{3,1},{4,0},{5,9},{6,10},{7,3},{8,4},{9,13},{10,... | collective-permute-start | bytes 589832 | tf_op jit(solution)/shard_map/ppermute | solution.py:913
  102.4 2.1 %collective-permute-done.31.refs_1_ = bf16[1,208,512]{2,1,0:T(8,128)(2,1)S(1)} collective-permute-done((bf16[1,208,512]{2,1,0:T(8,128)(2,1)S(1)}, bf16[1,208,512]{2,1,0:T(8,128)(2,1)S(1)}, u32[]{:S(2)}, u32[]{:S(2)}) %collective-permute-start.31) | collective-permute-done | bytes 213024 | tf_op jit(solution)/shard_map/ppermute | solution.py:913
  105.4 1.9 %collective-permute-start.34 = (bf16[1,208,512]{2,1,0:T(8,128)(2,1)S(1)}, bf16[1,208,512]{2,1,0:T(8,128)(2,1)S(1)}, u32[]{:S(2)}, u32[]{:S(2)}) collective-permute-start(bf16[1,208,512]{2,1,0:T(8,128)(2,1)S(1)} %get-tuple-element.294.refs_6_), channel_id=1, source_target_pairs={{0,2},{1,5},{2,6},{3,1},{4,0},{5,9},{6,10},{7,3},{8,4},{9,13},{10,... | collective-permute-start | bytes 638984 | tf_op jit(solution)/shard_map/ppermute | solution.py:913
  107.4 1.3 collective-permute-done.36.refs_1_
  110.0 1.4 %collective-permute-start.40 = (bf16[1,192,512]{2,1,0:T(8,128)(2,1)S(1)}, bf16[1,192,512]{2,1,0:T(8,128)(2,1)S(1)}, u32[]{:S(2)}, u32[]{:S(2)}) collective-permute-start(bf16[1,192,512]{2,1,0:T(8,128)(2,1)S(1)} %get-tuple-element.301.refs_13_), channel_id=1, source_target_pairs={{0,2},{1,5},{2,6},{3,1},{4,0},{5,9},{6,10},{7,3},{8,4},{9,13},{10,... | collective-permute-start | bytes 589832 | tf_op jit(solution)/shard_map/ppermute | solution.py:913
  112.1 1.5 %collective-permute-done.34.refs_1_ = bf16[1,208,512]{2,1,0:T(8,128)(2,1)S(1)} collective-permute-done((bf16[1,208,512]{2,1,0:T(8,128)(2,1)S(1)}, bf16[1,208,512]{2,1,0:T(8,128)(2,1)S(1)}, u32[]{:S(2)}, u32[]{:S(2)}) %collective-permute-start.34) | collective-permute-done | bytes 213024 | tf_op jit(solution)/shard_map/ppermute | solution.py:913
  114.7 1.8 %collective-permute-start.38 = (bf16[1,208,512]{2,1,0:T(8,128)(2,1)S(1)}, bf16[1,208,512]{2,1,0:T(8,128)(2,1)S(1)}, u32[]{:S(2)}, u32[]{:S(2)}) collective-permute-start(bf16[1,208,512]{2,1,0:T(8,128)(2,1)S(1)} %get-tuple-element.293.refs_5_), channel_id=1, source_target_pairs={{0,2},{1,5},{2,6},{3,1},{4,0},{5,9},{6,10},{7,3},{8,4},{9,13},{10,... | collective-permute-start | bytes 638984 | tf_op jit(solution)/shard_map/ppermute | solution.py:913
  119.2 1.5 %collective-permute-start.43 = (bf16[1,192,512]{2,1,0:T(8,128)(2,1)S(1)}, bf16[1,192,512]{2,1,0:T(8,128)(2,1)S(1)}, u32[]{:S(2)}, u32[]{:S(2)}) collective-permute-start(bf16[1,192,512]{2,1,0:T(8,128)(2,1)S(1)} %get-tuple-element.300.refs_12_), channel_id=1, source_target_pairs={{0,2},{1,5},{2,6},{3,1},{4,0},{5,9},{6,10},{7,3},{8,4},{9,13},{10,... | collective-permute-start | bytes 589832 | tf_op jit(solution)/shard_map/ppermute | solution.py:913
  121.3 1.6 %collective-permute-done.38.refs_1_ = bf16[1,208,512]{2,1,0:T(8,128)(2,1)S(1)} collective-permute-done((bf16[1,208,512]{2,1,0:T(8,128)(2,1)S(1)}, bf16[1,208,512]{2,1,0:T(8,128)(2,1)S(1)}, u32[]{:S(2)}, u32[]{:S(2)}) %collective-permute-start.38) | collective-permute-done | bytes 213024 | tf_op jit(solution)/shard_map/ppermute | solution.py:913
  123.2 2.2 %collective-permute-done.43.refs_1_ = bf16[1,192,512]{2,1,0:T(8,128)(2,1)S(1)} collective-permute-done((bf16[1,192,512]{2,1,0:T(8,128)(2,1)S(1)}, bf16[1,192,512]{2,1,0:T(8,128)(2,1)S(1)}, u32[]{:S(2)}, u32[]{:S(2)}) %collective-permute-start.43) | collective-permute-done | bytes 196640 | tf_op jit(solution)/shard_map/ppermute | solution.py:913
  128.7 2.8 %shard_map.329 = (f32[2048,512]{1,0:T(8,128)}, f32[512,2048]{1,0:T(8,128)}, f32[512,1536]{1,0:T(8,128)}, f32[512,512]{1,0:T(8,128)}, f32[512,128]{1,0:T(8,128)}) custom-call(bf16[7,400,512]{2,1,0:T(8,128)(2,1)S(1)} %shard_map.328.refs_0_.refs_1_), custom_call_target="tpu_custom_call" | custom-call | tf_op jit(solution)/shard_map/pallas_call | solution.py:876
  132.0 2.8 %shard_map.330 = (f32[2048,512]{1,0:T(8,128)}, f32[512,2048]{1,0:T(8,128)}, f32[512,1536]{1,0:T(8,128)}, f32[512,512]{1,0:T(8,128)}, f32[512,128]{1,0:T(8,128)}) custom-call(bf16[7,400,512]{2,1,0:T(8,128)(2,1)S(1)} %collective-permute-done.44.refs_0_.refs_3_, ...), custom_call_target="tpu_custom_call", output_to_operand_aliasing={{0}: (1, {}), {1}: (2, {}), {2}: (3, {}), {3}: (4, {}), {4}... | custom-call | tf_op jit(solution)/shard_map/pallas_call | solution.py:876
  136.7 1.6 %shard_map.335 = (f32[2048,512]{1,0:T(8,128)}, f32[512,2048]{1,0:T(8,128)}, f32[512,1536]{1,0:T(8,128)}, f32[512,512]{1,0:T(8,128)}, f32[512,128]{1,0:T(8,128)},...) custom-call(bf16[1,400,512]{2,1,0:T(8,128)(2,1)S(1)} %collective-per, ...), custom_call_target="tpu_custom_call", output_to_operand_aliasing={{0}: (5, {}), {1}: (6, {}), {2}: (7, {}), {3}: (8, {}), {4}... | custom-call | tf_op jit(solution)/shard_map/pallas_call | solution.py:876
  (125 shorter events, 30.1 us)
Async XLA Ops:
  7.5 5.3 %collective-permute-start = (bf16[272,128]{1,0:T(8,128)(2,1)S(1)}, bf16[272,128]{1,0:T(8,128)(2,1)S(1)}, u32[]{:S(2)}, u32[]{:S(2)}) collective-permute-start(bf16[272,128]{1,0:T(8,128)(2,1)S(1)} %get-tuple-element.178), channel_id=1, source_target_pairs={{0,16},{16,0},{1,17},{17,1},{2,18},{18,2},{3,19},{19,3},{4,20},{20... | collective-permute-start | bytes 208904 | tf_op jit(solution)/shard_map/ppermute | solution.py:892
  12.8 5.4 %collective-permute-start.2 = (bf16[256,128]{1,0:T(8,128)(2,1)S(1)}, bf16[256,128]{1,0:T(8,128)(2,1)S(1)}, u32[]{:S(2)}, u32[]{:S(2)}) collective-permute-start(bf16[256,128]{1,0:T(8,128)(2,1)S(1)} %slice_select_fusion.here_ref), channel_id=1, source_target_pairs={{0,8},{1,9},{2,10},{3,11},{4,12},{5,13},{6,14},{7,15},{8,0},{9,1},... | collective-permute-start | bytes 196616 | tf_op jit(solution)/shard_map/ppermute | solution.py:892
  16.0 4.4 %collective-permute-start.1 = (bf16[272,128]{1,0:T(8,128)(2,1)S(1)}, bf16[272,128]{1,0:T(8,128)(2,1)S(1)}, u32[]{:S(2)}, u32[]{:S(2)}) collective-permute-start(bf16[272,128]{1,0:T(8,128)(2,1)S(1)} %broadcast_select_fusion), channel_id=1, source_target_pairs={{0,2},{1,3},{2,0},{3,1},{4,6},{5,7},{6,4},{7,5},{8,10},{9,11},{10,... | collective-permute-start | bytes 208904 | tf_op jit(solution)/shard_map/ppermute | solution.py:892
  20.4 4.6 %collective-permute-start.3 = (bf16[544,128]{1,0:T(8,128)(2,1)S(1)}, bf16[544,128]{1,0:T(8,128)(2,1)S(1)}, u32[]{:S(2)}, u32[]{:S(2)}) collective-permute-start(bf16[544,128]{1,0:T(8,128)(2,1)S(1)} %pad_maximum_fusion.near_ref), channel_id=1, source_target_pairs={{0,1},{1,0},{2,3},{3,2},{4,5},{5,4},{6,7},{7,6},{8,9},{9,8},{10,11... | collective-permute-start | bytes 417800 | tf_op jit(solution)/shard_map/ppermute | solution.py:892
  20.5 4.5 %collective-permute-start.4 = (bf16[256,128]{1,0:T(8,128)(2,1)S(1)}, bf16[256,128]{1,0:T(8,128)(2,1)S(1)}, u32[]{:S(2)}, u32[]{:S(2)}) collective-permute-start(bf16[256,128]{1,0:T(8,128)(2,1)S(1)} %shard_map.299.refs_0_), channel_id=1, source_target_pairs={{0,4},{1,5},{2,6},{3,7},{4,0},{5,1},{6,2},{7,3},{8,12},{9,13},{10,... | collective-permute-start | bytes 196616 | tf_op jit(solution)/shard_map/ppermute | solution.py:892
  27.8 1.2 collective-permute-start.5
  29.0 5.7 %collective-permute-start.8 = (f32[32,128]{1,0:T(8,128)S(1)}, f32[32,128]{1,0:T(8,128)S(1)}, u32[]{:S(2)}, u32[]{:S(2)}) collective-permute-start(f32[32,128]{1,0:T(8,128)S(1)} %add.3.own_ref), channel_id=1, source_target_pairs={{0,18},{1,19},{2,16},{3,17},{4,22},{5,23},{6,20},{7,21},{8,26},{9,... | collective-permute-start | bytes 49160 | tf_op jit(solution)/shard_map/ppermute | solution.py:1139
  31.5 3.7 %collective-permute-start.7 = (f32[32,128]{1,0:T(8,128)S(1)}, f32[32,128]{1,0:T(8,128)S(1)}, u32[]{:S(2)}, u32[]{:S(2)}) collective-permute-start(f32[32,128]{1,0:T(8,128)S(1)} %add.3.own_ref), channel_id=1, source_target_pairs={{0,16},{16,0},{1,17},{17,1},{2,18},{18,2},{3,19},{19,3},{4,20},{20... | collective-permute-start | bytes 49160 | tf_op jit(solution)/shard_map/ppermute | solution.py:892
  32.0 3.7 %collective-permute-start.6 = (f32[32,128]{1,0:T(8,128)S(1)}, f32[32,128]{1,0:T(8,128)S(1)}, u32[]{:S(2)}, u32[]{:S(2)}) collective-permute-start(f32[32,128]{1,0:T(8,128)S(1)} %add.3.own_ref), channel_id=1, source_target_pairs={{0,2},{1,3},{2,0},{3,1},{4,6},{5,7},{6,4},{7,5},{8,10},{9,11},{10,... | collective-permute-start | bytes 49160 | tf_op jit(solution)/shard_map/ppermute | solution.py:892
  35.8 17.9 %copy-start.13 = (f32[256,128]{1,0:T(8,128)S(1)}, f32[256,128]{1,0:T(8,128)}, u32[]{:S(2)}) copy-start(f32[256,128]{1,0:T(8,128)} %get-tuple-element.183.rs2_ref) | copy-start | bytes 393220
  38.8 1.7 %collective-permute-start.9 = (bf16[512,128]{1,0:T(8,128)(2,1)S(1)}, bf16[512,128]{1,0:T(8,128)(2,1)S(1)}, u32[]{:S(2)}, u32[]{:S(2)}) collective-permute-start(bf16[512,128]{1,0:T(8,128)(2,1)S(1)} %get-tuple-element.199), channel_id=1, source_target_pairs={{0,1},{1,0},{2,3},{3,2},{4,5},{5,4},{6,7},{7,6},{8,9},{9,8},{10,11... | collective-permute-start | bytes 393224 | tf_op jit(solution)/shard_map/ppermute | solution.py:892
  38.9 4.5 %collective-permute-start.11 = (bf16[256,128]{1,0:T(8,128)(2,1)S(1)}, bf16[256,128]{1,0:T(8,128)(2,1)S(1)}, u32[]{:S(2)}, u32[]{:S(2)}) collective-permute-start(bf16[256,128]{1,0:T(8,128)(2,1)S(1)} %get-tuple-element.201), channel_id=1, source_target_pairs={{0,4},{1,5},{2,6},{3,7},{4,0},{5,1},{6,2},{7,3},{8,12},{9,13},{10,... | collective-permute-start | bytes 196616 | tf_op jit(solution)/shard_map/ppermute | solution.py:892
  43.4 5.6 %collective-permute-start.12 = (bf16[256,128]{1,0:T(8,128)(2,1)S(1)}, bf16[256,128]{1,0:T(8,128)(2,1)S(1)}, u32[]{:S(2)}, u32[]{:S(2)}) collective-permute-start(bf16[256,128]{1,0:T(8,128)(2,1)S(1)} %shard_map.304.rows_ref), channel_id=1, source_target_pairs={{0,8},{1,9},{2,10},{3,11},{4,12},{5,13},{6,14},{7,15},{8,0},{9,1},... | collective-permute-start | bytes 196616 | tf_op jit(solution)/shard_map/ppermute | solution.py:892
  44.7 4.5 %collective-permute-start.10 = (bf16[256,128]{1,0:T(8,128)(2,1)S(1)}, bf16[256,128]{1,0:T(8,128)(2,1)S(1)}, u32[]{:S(2)}, u32[]{:S(2)}) collective-permute-start(bf16[256,128]{1,0:T(8,128)(2,1)S(1)} %get-tuple-element.340), channel_id=1, source_target_pairs={{0,2},{1,3},{2,0},{3,1},{4,6},{5,7},{6,4},{7,5},{8,10},{9,11},{10,... | collective-permute-start | bytes 196616 | tf_op jit(solution)/shard_map/ppermute | solution.py:892
  49.3 4.3 %collective-permute-start.13 = (bf16[256,128]{1,0:T(8,128)(2,1)S(1)}, bf16[256,128]{1,0:T(8,128)(2,1)S(1)}, u32[]{:S(2)}, u32[]{:S(2)}) collective-permute-start(bf16[256,128]{1,0:T(8,128)(2,1)S(1)} %broadcast_select_fusion.1), channel_id=1, source_target_pairs={{0,16},{16,0},{1,17},{17,1},{2,18},{18,2},{3,19},{19,3},{4,20},{20... | collective-permute-start | bytes 196616 | tf_op jit(solution)/shard_map/ppermute | solution.py:892
  58.6 4.5 %collective-permute-start.14 = (bf16[8,208,512]{2,1,0:T(8,128)(2,1)S(1)}, bf16[8,208,512]{2,1,0:T(8,128)(2,1)S(1)}, u32[]{:S(2)}, u32[]{:S(2)}) collective-permute-start(bf16[8,208,512]{2,1,0:T(8,128)(2,1)S(1)} %get-tuple-element.210), channel_id=1, source_target_pairs={{0,1},{1,0},{2,3},{3,2},{4,5},{5,4},{6,7},{7,6},{8,9},{9,8},{10,11... | collective-permute-start | bytes 5111816 | tf_op jit(solution)/shard_map/ppermute | solution.py:892
  62.4 6.1 %collective-permute-start.18 = (bf16[6,192,512]{2,1,0:T(8,128)(2,1)S(1)}, bf16[6,192,512]{2,1,0:T(8,128)(2,1)S(1)}, u32[]{:S(2)}, u32[]{:S(2)}) collective-permute-start(bf16[6,192,512]{2,1,0:T(8,128)(2,1)S(1)} %get-tuple-element.234), channel_id=1, source_target_pairs={{0,1},{1,0},{2,3},{3,2},{4,5},{5,4},{6,7},{7,6},{8,9},{9,8},{10,11... | collective-permute-start | bytes 3538952 | tf_op jit(solution)/shard_map/ppermute | solution.py:892
  63.0 3.0 %collective-permute-start.17 = (bf16[2,192,512]{2,1,0:T(8,128)(2,1)S(1)}, bf16[2,192,512]{2,1,0:T(8,128)(2,1)S(1)}, u32[]{:S(2)}, u32[]{:S(2)}) collective-permute-start(bf16[2,192,512]{2,1,0:T(8,128)(2,1)S(1)} %get-tuple-element.228), channel_id=1, source_target_pairs={{0,1},{1,0},{2,3},{3,2},{4,5},{5,4},{6,7},{7,6},{8,9},{9,8},{10,11... | collective-permute-start | bytes 1179656 | tf_op jit(solution)/shard_map/ppermute | solution.py:892
  63.2 8.2 %collective-permute-start.15 = (bf16[1,208,512]{2,1,0:T(8,128)(2,1)S(1)}, bf16[1,208,512]{2,1,0:T(8,128)(2,1)S(1)}, u32[]{:S(2)}, u32[]{:S(2)}) collective-permute-start(bf16[1,208,512]{2,1,0:T(8,128)(2,1)S(1)} %get-tuple-element.225), channel_id=1, source_target_pairs={{0,4},{1,3},{2,0},{3,7},{4,8},{5,1},{6,2},{7,11},{8,12},{9,5},{10,... | collective-permute-start | bytes 638984 | tf_op jit(solution)/shard_map/ppermute | solution.py:913
  65.0 6.4 %collective-permute-start.16 = (bf16[1,208,512]{2,1,0:T(8,128)(2,1)S(1)}, bf16[1,208,512]{2,1,0:T(8,128)(2,1)S(1)}, u32[]{:S(2)}, u32[]{:S(2)}) collective-permute-start(bf16[1,208,512]{2,1,0:T(8,128)(2,1)S(1)} %get-tuple-element.226), channel_id=1, source_target_pairs={{0,2},{1,5},{2,6},{3,1},{4,0},{5,9},{6,10},{7,3},{8,4},{9,13},{10,... | collective-permute-start | bytes 638984 | tf_op jit(solution)/shard_map/ppermute | solution.py:913
  66.1 9.4 %collective-permute-start.22 = (bf16[1,192,512]{2,1,0:T(8,128)(2,1)S(1)}, bf16[1,192,512]{2,1,0:T(8,128)(2,1)S(1)}, u32[]{:S(2)}, u32[]{:S(2)}) collective-permute-start(bf16[1,192,512]{2,1,0:T(8,128)(2,1)S(1)} %get-tuple-element.231), channel_id=1, source_target_pairs={{0,2},{1,5},{2,6},{3,1},{4,0},{5,9},{6,10},{7,3},{8,4},{9,13},{10,... | collective-permute-start | bytes 589832 | tf_op jit(solution)/shard_map/ppermute | solution.py:913
  66.7 8.8 %collective-permute-start.21 = (bf16[1,192,512]{2,1,0:T(8,128)(2,1)S(1)}, bf16[1,192,512]{2,1,0:T(8,128)(2,1)S(1)}, u32[]{:S(2)}, u32[]{:S(2)}) collective-permute-start(bf16[1,192,512]{2,1,0:T(8,128)(2,1)S(1)} %get-tuple-element.241), channel_id=1, source_target_pairs={{0,4},{1,3},{2,0},{3,7},{4,8},{5,1},{6,2},{7,11},{8,12},{9,5},{10,... | collective-permute-start | bytes 589832 | tf_op jit(solution)/shard_map/ppermute | solution.py:913
  71.5 8.4 %collective-permute-start.20 = (bf16[1,208,512]{2,1,0:T(8,128)(2,1)S(1)}, bf16[1,208,512]{2,1,0:T(8,128)(2,1)S(1)}, u32[]{:S(2)}, u32[]{:S(2)}) collective-permute-start(bf16[1,208,512]{2,1,0:T(8,128)(2,1)S(1)} %get-tuple-element.240), channel_id=1, source_target_pairs={{0,2},{1,5},{2,6},{3,1},{4,0},{5,9},{6,10},{7,3},{8,4},{9,13},{10,... | collective-permute-start | bytes 638984 | tf_op jit(solution)/shard_map/ppermute | solution.py:913
  72.0 8.2 %collective-permute-start.19 = (bf16[1,208,512]{2,1,0:T(8,128)(2,1)S(1)}, bf16[1,208,512]{2,1,0:T(8,128)(2,1)S(1)}, u32[]{:S(2)}, u32[]{:S(2)}) collective-permute-start(bf16[1,208,512]{2,1,0:T(8,128)(2,1)S(1)} %get-tuple-element.239), channel_id=1, source_target_pairs={{0,4},{1,3},{2,0},{3,7},{4,8},{5,1},{6,2},{7,11},{8,12},{9,5},{10,... | collective-permute-start | bytes 638984 | tf_op jit(solution)/shard_map/ppermute | solution.py:913
  75.7 8.4 %collective-permute-start.26 = (bf16[1,192,512]{2,1,0:T(8,128)(2,1)S(1)}, bf16[1,192,512]{2,1,0:T(8,128)(2,1)S(1)}, u32[]{:S(2)}, u32[]{:S(2)}) collective-permute-start(bf16[1,192,512]{2,1,0:T(8,128)(2,1)S(1)} %get-tuple-element.249), channel_id=1, source_target_pairs={{0,2},{1,5},{2,6},{3,1},{4,0},{5,9},{6,10},{7,3},{8,4},{9,13},{10,... | collective-permute-start | bytes 589832 | tf_op jit(solution)/shard_map/ppermute | solution.py:913
  76.5 8.0 %collective-permute-start.25 = (bf16[1,192,512]{2,1,0:T(8,128)(2,1)S(1)}, bf16[1,192,512]{2,1,0:T(8,128)(2,1)S(1)}, u32[]{:S(2)}, u32[]{:S(2)}) collective-permute-start(bf16[1,192,512]{2,1,0:T(8,128)(2,1)S(1)} %get-tuple-element.244), channel_id=1, source_target_pairs={{0,4},{1,3},{2,0},{3,7},{4,8},{5,1},{6,2},{7,11},{8,12},{9,5},{10,... | collective-permute-start | bytes 589832 | tf_op jit(solution)/shard_map/ppermute | solution.py:913
  80.3 8.3 %collective-permute-start.24 = (bf16[1,208,512]{2,1,0:T(8,128)(2,1)S(1)}, bf16[1,208,512]{2,1,0:T(8,128)(2,1)S(1)}, u32[]{:S(2)}, u32[]{:S(2)}) collective-permute-start(bf16[1,208,512]{2,1,0:T(8,128)(2,1)S(1)} %get-tuple-element.248), channel_id=1, source_target_pairs={{0,2},{1,5},{2,6},{3,1},{4,0},{5,9},{6,10},{7,3},{8,4},{9,13},{10,... | collective-permute-start | bytes 638984 | tf_op jit(solution)/shard_map/ppermute | solution.py:913
  82.4 7.9 %collective-permute-start.23 = (bf16[1,208,512]{2,1,0:T(8,128)(2,1)S(1)}, bf16[1,208,512]{2,1,0:T(8,128)(2,1)S(1)}, u32[]{:S(2)}, u32[]{:S(2)}) collective-permute-start(bf16[1,208,512]{2,1,0:T(8,128)(2,1)S(1)} %get-tuple-element.247), channel_id=1, source_target_pairs={{0,4},{1,3},{2,0},{3,7},{4,8},{5,1},{6,2},{7,11},{8,12},{9,5},{10,... | collective-permute-start | bytes 638984 | tf_op jit(solution)/shard_map/ppermute | solution.py:913
  84.5 8.3 %collective-permute-start.29 = (bf16[1,192,512]{2,1,0:T(8,128)(2,1)S(1)}, bf16[1,192,512]{2,1,0:T(8,128)(2,1)S(1)}, u32[]{:S(2)}, u32[]{:S(2)}) collective-permute-start(bf16[1,192,512]{2,1,0:T(8,128)(2,1)S(1)} %get-tuple-element.256), channel_id=1, source_target_pairs={{0,2},{1,5},{2,6},{3,1},{4,0},{5,9},{6,10},{7,3},{8,4},{9,13},{10,... | collective-permute-start | bytes 589832 | tf_op jit(solution)/shard_map/ppermute | solution.py:913
  86.6 6.3 %collective-permute-start.28 = (bf16[1,192,512]{2,1,0:T(8,128)(2,1)S(1)}, bf16[1,192,512]{2,1,0:T(8,128)(2,1)S(1)}, u32[]{:S(2)}, u32[]{:S(2)}) collective-permute-start(bf16[1,192,512]{2,1,0:T(8,128)(2,1)S(1)} %get-tuple-element.252), channel_id=1, source_target_pairs={{0,4},{1,3},{2,0},{3,7},{4,8},{5,1},{6,2},{7,11},{8,12},{9,5},{10,... | collective-permute-start | bytes 589832 | tf_op jit(solution)/shard_map/ppermute | solution.py:913
  90.4 5.9 %collective-permute-start.27 = (bf16[1,208,512]{2,1,0:T(8,128)(2,1)S(1)}, bf16[1,208,512]{2,1,0:T(8,128)(2,1)S(1)}, u32[]{:S(2)}, u32[]{:S(2)}) collective-permute-start(bf16[1,208,512]{2,1,0:T(8,128)(2,1)S(1)} %get-tuple-element.255), channel_id=1, source_target_pairs={{0,4},{1,3},{2,0},{3,7},{4,8},{5,1},{6,2},{7,11},{8,12},{9,5},{10,... | collective-permute-start | bytes 638984 | tf_op jit(solution)/shard_map/ppermute | solution.py:913
  93.0 6.6 %collective-permute-start.32 = (bf16[1,192,512]{2,1,0:T(8,128)(2,1)S(1)}, bf16[1,192,512]{2,1,0:T(8,128)(2,1)S(1)}, u32[]{:S(2)}, u32[]{:S(2)}) collective-permute-start(bf16[1,192,512]{2,1,0:T(8,128)(2,1)S(1)} %get-tuple-element.259), channel_id=1, source_target_pairs={{0,4},{1,3},{2,0},{3,7},{4,8},{5,1},{6,2},{7,11},{8,12},{9,5},{10,... | collective-permute-start | bytes 589832 | tf_op jit(solution)/shard_map/ppermute | solution.py:913
  96.4 8.2 %collective-permute-start.31 = (bf16[1,208,512]{2,1,0:T(8,128)(2,1)S(1)}, bf16[1,208,512]{2,1,0:T(8,128)(2,1)S(1)}, u32[]{:S(2)}, u32[]{:S(2)}) collective-permute-start(bf16[1,208,512]{2,1,0:T(8,128)(2,1)S(1)} %shard_map.320.refs_0_), channel_id=1, source_target_pairs={{0,2},{1,5},{2,6},{3,1},{4,0},{5,9},{6,10},{7,3},{8,4},{9,13},{10,... | collective-permute-start | bytes 638984 | tf_op jit(solution)/shard_map/ppermute | solution.py:913
  97.1 8.2 %collective-permute-start.30 = (bf16[1,208,512]{2,1,0:T(8,128)(2,1)S(1)}, bf16[1,208,512]{2,1,0:T(8,128)(2,1)S(1)}, u32[]{:S(2)}, u32[]{:S(2)}) collective-permute-start(bf16[1,208,512]{2,1,0:T(8,128)(2,1)S(1)} %shard_map.320.refs_0_), channel_id=1, source_target_pairs={{0,4},{1,3},{2,0},{3,7},{4,8},{5,1},{6,2},{7,11},{8,12},{9,5},{10,... | collective-permute-start | bytes 638984 | tf_op jit(solution)/shard_map/ppermute | solution.py:913
  99.6 9.2 %collective-permute-start.36 = (bf16[1,192,512]{2,1,0:T(8,128)(2,1)S(1)}, bf16[1,192,512]{2,1,0:T(8,128)(2,1)S(1)}, u32[]{:S(2)}, u32[]{:S(2)}) collective-permute-start(bf16[1,192,512]{2,1,0:T(8,128)(2,1)S(1)} %shard_map.321.refs_7_), channel_id=1, source_target_pairs={{0,2},{1,5},{2,6},{3,1},{4,0},{5,9},{6,10},{7,3},{8,4},{9,13},{10,... | collective-permute-start | bytes 589832 | tf_op jit(solution)/shard_map/ppermute | solution.py:913
  102.2 7.8 %collective-permute-start.35 = (bf16[1,192,512]{2,1,0:T(8,128)(2,1)S(1)}, bf16[1,192,512]{2,1,0:T(8,128)(2,1)S(1)}, u32[]{:S(2)}, u32[]{:S(2)}) collective-permute-start(bf16[1,192,512]{2,1,0:T(8,128)(2,1)S(1)} %shard_map.321.refs_7_), channel_id=1, source_target_pairs={{0,4},{1,3},{2,0},{3,7},{4,8},{5,1},{6,2},{7,11},{8,12},{9,5},{10,... | collective-permute-start | bytes 589832 | tf_op jit(solution)/shard_map/ppermute | solution.py:913
  105.4 8.2 %collective-permute-start.34 = (bf16[1,208,512]{2,1,0:T(8,128)(2,1)S(1)}, bf16[1,208,512]{2,1,0:T(8,128)(2,1)S(1)}, u32[]{:S(2)}, u32[]{:S(2)}) collective-permute-start(bf16[1,208,512]{2,1,0:T(8,128)(2,1)S(1)} %get-tuple-element.294.refs_6_), channel_id=1, source_target_pairs={{0,2},{1,5},{2,6},{3,1},{4,0},{5,9},{6,10},{7,3},{8,4},{9,13},{10,... | collective-permute-start | bytes 638984 | tf_op jit(solution)/shard_map/ppermute | solution.py:913
  107.2 7.4 %collective-permute-start.33 = (bf16[1,208,512]{2,1,0:T(8,128)(2,1)S(1)}, bf16[1,208,512]{2,1,0:T(8,128)(2,1)S(1)}, u32[]{:S(2)}, u32[]{:S(2)}) collective-permute-start(bf16[1,208,512]{2,1,0:T(8,128)(2,1)S(1)} %get-tuple-element.289.refs_1_), channel_id=1, source_target_pairs={{0,4},{1,3},{2,0},{3,7},{4,8},{5,1},{6,2},{7,11},{8,12},{9,5},{10,... | collective-permute-start | bytes 638984 | tf_op jit(solution)/shard_map/ppermute | solution.py:913
  110.0 7.9 %collective-permute-start.40 = (bf16[1,192,512]{2,1,0:T(8,128)(2,1)S(1)}, bf16[1,192,512]{2,1,0:T(8,128)(2,1)S(1)}, u32[]{:S(2)}, u32[]{:S(2)}) collective-permute-start(bf16[1,192,512]{2,1,0:T(8,128)(2,1)S(1)} %get-tuple-element.301.refs_13_), channel_id=1, source_target_pairs={{0,2},{1,5},{2,6},{3,1},{4,0},{5,9},{6,10},{7,3},{8,4},{9,13},{10,... | collective-permute-start | bytes 589832 | tf_op jit(solution)/shard_map/ppermute | solution.py:913
  111.5 7.8 %collective-permute-start.39 = (bf16[1,192,512]{2,1,0:T(8,128)(2,1)S(1)}, bf16[1,192,512]{2,1,0:T(8,128)(2,1)S(1)}, u32[]{:S(2)}, u32[]{:S(2)}) collective-permute-start(bf16[1,192,512]{2,1,0:T(8,128)(2,1)S(1)} %get-tuple-element.296.refs_8_), channel_id=1, source_target_pairs={{0,4},{1,3},{2,0},{3,7},{4,8},{5,1},{6,2},{7,11},{8,12},{9,5},{10,... | collective-permute-start | bytes 589832 | tf_op jit(solution)/shard_map/ppermute | solution.py:913
  114.7 8.2 %collective-permute-start.38 = (bf16[1,208,512]{2,1,0:T(8,128)(2,1)S(1)}, bf16[1,208,512]{2,1,0:T(8,128)(2,1)S(1)}, u32[]{:S(2)}, u32[]{:S(2)}) collective-permute-start(bf16[1,208,512]{2,1,0:T(8,128)(2,1)S(1)} %get-tuple-element.293.refs_5_), channel_id=1, source_target_pairs={{0,2},{1,5},{2,6},{3,1},{4,0},{5,9},{6,10},{7,3},{8,4},{9,13},{10,... | collective-permute-start | bytes 638984 | tf_op jit(solution)/shard_map/ppermute | solution.py:913
  116.5 6.7 %collective-permute-start.37 = (bf16[1,208,512]{2,1,0:T(8,128)(2,1)S(1)}, bf16[1,208,512]{2,1,0:T(8,128)(2,1)S(1)}, u32[]{:S(2)}, u32[]{:S(2)}) collective-permute-start(bf16[1,208,512]{2,1,0:T(8,128)(2,1)S(1)} %get-tuple-element.290.refs_2_), channel_id=1, source_target_pairs={{0,4},{1,3},{2,0},{3,7},{4,8},{5,1},{6,2},{7,11},{8,12},{9,5},{10,... | collective-permute-start | bytes 638984 | tf_op jit(solution)/shard_map/ppermute | solution.py:913
  119.2 6.2 %collective-permute-start.43 = (bf16[1,192,512]{2,1,0:T(8,128)(2,1)S(1)}, bf16[1,192,512]{2,1,0:T(8,128)(2,1)S(1)}, u32[]{:S(2)}, u32[]{:S(2)}) collective-permute-start(bf16[1,192,512]{2,1,0:T(8,128)(2,1)S(1)} %get-tuple-element.300.refs_12_), channel_id=1, source_target_pairs={{0,2},{1,5},{2,6},{3,1},{4,0},{5,9},{6,10},{7,3},{8,4},{9,13},{10,... | collective-permute-start | bytes 589832 | tf_op jit(solution)/shard_map/ppermute | solution.py:913
  120.7 5.7 %collective-permute-start.42 = (bf16[1,192,512]{2,1,0:T(8,128)(2,1)S(1)}, bf16[1,192,512]{2,1,0:T(8,128)(2,1)S(1)}, u32[]{:S(2)}, u32[]{:S(2)}) collective-permute-start(bf16[1,192,512]{2,1,0:T(8,128)(2,1)S(1)} %get-tuple-element.297.refs_9_), channel_id=1, source_target_pairs={{0,4},{1,3},{2,0},{3,7},{4,8},{5,1},{6,2},{7,11},{8,12},{9,5},{10,... | collective-permute-start | bytes 589832 | tf_op jit(solution)/shard_map/ppermute | solution.py:913
  126.6 5.3 %collective-permute-start.44 = (bf16[7,400,512]{2,1,0:T(8,128)(2,1)S(1)}, bf16[7,400,512]{2,1,0:T(8,128)(2,1)S(1)}, u32[]{:S(2)}, u32[]{:S(2)}) collective-permute-start(bf16[7,400,512]{2,1,0:T(8,128)(2,1)S(1)} %shard_map.328.refs_0_.refs_1_), channel_id=1, source_target_pairs={{0,1},{1,0},{2,3},{3,2},{4,5},{5,4},{6,7},{7,6},{8,9},{9,8},{10,11... | collective-permute-start | bytes 8601608 | tf_op jit(solution)/shard_map/ppermute | solution.py:892
  126.7 8.1 %collective-permute-start.41 = (bf16[1,208,512]{2,1,0:T(8,128)(2,1)S(1)}, bf16[1,208,512]{2,1,0:T(8,128)(2,1)S(1)}, u32[]{:S(2)}, u32[]{:S(2)}) collective-permute-start(bf16[1,208,512]{2,1,0:T(8,128)(2,1)S(1)} %get-tuple-element.291.refs_3_), channel_id=1, source_target_pairs={{0,4},{1,3},{2,0},{3,7},{4,8},{5,1},{6,2},{7,11},{8,12},{9,5},{10,... | collective-permute-start | bytes 638984 | tf_op jit(solution)/shard_map/ppermute | solution.py:913
  127.4 7.4 %collective-permute-start.45 = (bf16[1,192,512]{2,1,0:T(8,128)(2,1)S(1)}, bf16[1,192,512]{2,1,0:T(8,128)(2,1)S(1)}, u32[]{:S(2)}, u32[]{:S(2)}) collective-permute-start(bf16[1,192,512]{2,1,0:T(8,128)(2,1)S(1)} %get-tuple-element.298.refs_10_), channel_id=1, source_target_pairs={{0,4},{1,3},{2,0},{3,7},{4,8},{5,1},{6,2},{7,11},{8,12},{9,5},{10,... | collective-permute-start | bytes 589832 | tf_op jit(solution)/shard_map/ppermute | solution.py:913
  134.9 1.8 %collective-permute-start.46 = (bf16[1,400,512]{2,1,0:T(8,128)(2,1)S(1)}, bf16[1,400,512]{2,1,0:T(8,128)(2,1)S(1)}, u32[]{:S(2)}, u32[]{:S(2)}) collective-permute-start(bf16[1,400,512]{2,1,0:T(8,128)(2,1)S(1)} %shard_map.333.refs_0_.refs_2_), channel_id=1, source_target_pairs={{0,1},{1,0},{2,3},{3,2},{4,5},{5,4},{6,7},{7,6},{8,9},{9,8},{10,11... | collective-permute-start | bytes 1228808 | tf_op jit(solution)/shard_map/ppermute | solution.py:892
  (16 other events, 160.8 us)
